TPU v7x, 32 devices: a whole 2x2x4 slice. The times are simulated.
32 devices in a mesh: patch: 4 (over y, x), member: 8 (over z, core).
Axes of the slice: x: 2, y: 2, z: 4, core: 2. Of those that a mesh axis runs over, the one named last changes fastest.
Arguments:
- init_field: float32 [1024, 32, 256], P('member', 'patch'), may hold values from -6 to 6
- flow_fields: float32 [4, 32, 256], P(None, 'patch'), may hold values from -6 to 6, as said below
- emission: float32 [1024], P('member'), may hold values from 0.5 to 2
- observed_cell: int32 [32, 512], P(('patch', 'member')), may hold values from 0 to 767
- observed_count: int32 [32], P(('patch', 'member')), may hold values from 1 to 512, as said below
- observed_value: float32 [32, 512], P(('patch', 'member')), may hold values from -6 to 6
- observed_scale: float32 [32, 512], P(('patch', 'member')), may hold values from 0.1 to 10
Outputs:
- analysis: float32 [1024, 32, 256], P('member', 'patch')
Inputs may be any that keep to these rules, and one draw needn't show every extreme that they name: `observed_cell`: A position is (row offset + 1) * 256 + column with row offset -1, 0 or 1 from the region's row; slots from observed_count on are not read. `observed_count`: some region has 512 observations and some region has one. `flow_fields`: rows 0 and 1 lie in -0.5 to 0.5, row 2 in 0.02 to 0.5.
All inputs are finite; a program needn't handle non-finite values.
Results may differ from a plain program's by a relative error of at most 0.0012.
Values sent between devices are 32-bit elements; how exact they have to be, the bound alone decides.
No kernel may reach another device: no remote copies, remote signals or barrier semaphores. Data moves between devices by JAX's collectives and lax.ppermute only.
A program may use at most 64 MiB of HBM per device.

v0:
```python
import math

import jax
import jax.numpy as jnp
from jax import lax
from jax.sharding import PartitionSpec as P

SLOTS = 512
STEPS = 2


HIGH = lax.Precision.HIGHEST


def padded(cells, sides, width):
    for axis, dim in sides:
        count = lax.axis_size(axis)
        ends = count - 1
        head = lax.slice_in_dim(cells, 0, width, axis=dim)
        tail = lax.slice_in_dim(cells, cells.shape[dim] - width, cells.shape[dim], axis=dim)
        cells = jnp.concatenate(
            [
                lax.ppermute(tail, axis, [(i, (i + 1) % count) for i in range(ends)]),
                cells,
                lax.ppermute(head, axis, [((i + 1) % count, i) for i in range(ends)]),
            ],
            axis=dim,
        )
    return cells


def advance(extended, flow_piece, emission):
    field = extended[:, 1:-1, :]
    behind_rows = extended[:, :-2, :]
    ahead_rows = extended[:, 2:, :]
    behind_cols = jnp.roll(field, 1, axis=2)
    ahead_cols = jnp.roll(field, -1, axis=2)
    row_flow = flow_piece[0]
    col_flow = flow_piece[1]
    advected = (
        field
        - jnp.maximum(row_flow, 0.0) * (field - behind_rows)
        - jnp.minimum(row_flow, 0.0) * (ahead_rows - field)
        - jnp.maximum(col_flow, 0.0) * (field - behind_cols)
        - jnp.minimum(col_flow, 0.0) * (ahead_cols - field)
    )
    return (1.0 - flow_piece[2]) * advected + emission[:, None, None] * flow_piece[3]


def per_device(
    init_field, flow_fields, emission, observed_cell, observed_count, observed_value, observed_scale
):
    rows = init_field.shape[1]
    field = init_field
    extended = padded(field, (("patch", 1),), STEPS)
    flow_wide = padded(flow_fields, (("patch", 1),), STEPS - 1)
    for step_index in range(STEPS):
        margin = STEPS - 1 - step_index
        extended = advance(
            extended, flow_wide[:, step_index : step_index + rows + 2 * margin, :], emission
        )
    field = extended
    regrouped = lax.all_to_all(field, "member", split_axis=1, concat_axis=0, tiled=True)
    bordered = padded(regrouped, ((("patch", "member"), 1),), 1)
    window = bordered.reshape(bordered.shape[0], 3 * bordered.shape[2])
    members = window.shape[0]
    width = window.shape[1] // 3
    root = math.sqrt(members - 1)
    predicted = jnp.take(window, observed_cell[0], axis=1)
    active_slot = (jnp.arange(SLOTS, dtype=jnp.int32) < observed_count[0]).astype(jnp.float32)
    slot_weight = active_slot * observed_scale[0]
    predicted_mean = jnp.mean(predicted, axis=0)
    spread = (predicted - predicted_mean) * (slot_weight / root)
    innovation = slot_weight * (observed_value[0] - predicted_mean)
    own_row = window[:, width : 2 * width]
    mean_row = jnp.mean(own_row, axis=0)
    anomaly = own_row - mean_row
    forcing = jnp.dot(spread, innovation, precision=HIGH) / root
    inner = jnp.eye(SLOTS, dtype=jnp.float32) + jnp.dot(spread.T, spread, precision=HIGH)
    factor = jnp.linalg.cholesky(inner)
    projected = jnp.dot(spread.T, anomaly, precision=HIGH)
    solved = anomaly - jnp.dot(
        spread, jax.scipy.linalg.cho_solve((factor, True), projected), precision=HIGH
    )
    pushed = jnp.dot(spread.T, forcing, precision=HIGH)
    weights = forcing - jnp.dot(
        spread, jax.scipy.linalg.cho_solve((factor, True), pushed), precision=HIGH
    )
    offset_term = jnp.dot(weights, anomaly, precision=HIGH)
    analysed = mean_row + 0.5 * anomaly + 0.5 * solved + offset_term
    return lax.all_to_all(
        analysed.reshape(members, 1, width), "member", split_axis=0, concat_axis=1, tiled=True
    )


def solution(mesh):
    return jax.shard_map(
        per_device,
        mesh=mesh,
        in_specs=(
            P("member", "patch", None),
            P(None, "patch", None),
            P("member"),
            P(("patch", "member"), None),
            P(("patch", "member")),
            P(("patch", "member"), None),
            P(("patch", "member"), None),
        ),
        out_specs=P("member", "patch", None),
        check_vma=False,
    )
```

profile of v0, /device:TPU:2, one launch (start us, length us, event | category | flops | bytes accessed | tf_op | source)
XLA Modules:
  0.0 303.2 jit_solution(2639831300358718324)
XLA Ops:
  0.0 1.7 copy.20
  1.7 3.4 %collective-permute-start.2 = (f32[128,2,256]{2,0,1:T(8,128)S(1)}, f32[128,2,256]{2,0,1:T(8,128)S(1)}, u32[]{:S(2)}, u32[]{:S(2)}) collective-permute-start(f32[128,2,256]{2,0,1:T(8,128)S(1)} %get-tuple-element.34), channel_id=1, source_target_pairs={{0,8},{8,16},{16,24},{1,9},{9,17},{17,25},{2,10},{10,18},{18,26},{... | collective-permute-start | bytes 786440 | tf_op jit(solution)/shard_map/ppermute | solution.py:23
  5.1 2.5 collective-permute-start.3
  7.6 1.9 collective-permute-start.1
  9.5 4.8 %collective-permute-start = (f32[4,1,256]{2,1,0:T(1,128)S(1)}, f32[4,1,256]{2,1,0:T(1,128)S(1)}, u32[]{:S(2)}, u32[]{:S(2)}) collective-permute-start(f32[4,1,256]{2,1,0:T(1,128)S(1)} %get-tuple-element.57), channel_id=1, source_target_pairs={{0,8},{8,16},{16,24},{1,9},{9,17},{17,25},{2,10},{10,18},{18,26},{... | collective-permute-start | bytes 12296 | tf_op jit(solution)/shard_map/ppermute | solution.py:23
  14.4 4.0 %collective-permute-done.1 = f32[4,1,256]{2,1,0:T(1,128)S(1)} collective-permute-done((f32[4,1,256]{2,1,0:T(1,128)S(1)}, f32[4,1,256]{2,1,0:T(1,128)S(1)}, u32[]{:S(2)}, u32[]{:S(2)}) %collective-permute-start.1) | collective-permute-done | bytes 4128 | tf_op jit(solution)/shard_map/ppermute | solution.py:25
  19.9 1.1 fusion.14
  21.6 0.8 fusion.35
  22.4 31.3 %all_to_all.36 = f32[128,8,256]{2,0,1:T(8,128)S(1)} all-to-all(f32[128,8,256]{2,0,1:T(8,128)S(1)} %fusion.35), channel_id=1, replica_groups=mesh['patch'=4,'member'=8] {'member'}, dimensions={1} | all-to-all | bytes 2097152 | tf_op jit(solution)/shard_map/all_to_all | solution.py:63
  53.7 2.8 collective-permute-start.5
  56.5 1.9 collective-permute-start.4
  59.2 19.3 %collective-permute-done.5 = f32[1024,1,256]{2,0,1:T(8,128)S(1)} collective-permute-done((f32[1024,1,256]{2,0,1:T(8,128)S(1)}, f32[1024,1,256]{2,0,1:T(8,128)S(1)}, u32[]{:S(2)}, u32[]{:S(2)}) %collective-permute-start.5) | collective-permute-done | bytes 1048608 | tf_op jit(solution)/shard_map/ppermute | solution.py:25
  78.5 2.3 collective-permute-done.4
  80.8 1.8 pad_maximum_fusion
  82.7 2.4 copy.25
  85.1 1.0 slice_reduce_fusion
  86.1 2.8 gather_fusion
  89.0 1.7 copy.30
  91.4 0.9 copy-done.1
  92.6 4.5 %fusion.152 = f32[512,512]{1,0:T(8,128)} fusion(f32[512,1024]{1,0:T(8,128)S(1)} %subtract_multiply_fusion), kind=kOutput, calls=%fused_computation.244 | convolution fusion | flops 3221225472 | bytes 3145728 | tf_op jit(solution)/shard_map/dot_general | solution.py:79
  97.1 2.5 copy.27
  99.7 1.8 fusion.41
  101.4 1.0 copy-done.4
  102.4 11.7 %cholesky.104 = f32[128,128]{1,0:T(8,128)S(1)} custom-call(f32[128,128]{1,0:T(8,128)S(1)} %cholesky.266), custom_call_target="Cholesky" | custom-call | tf_op jit(solution)/shard_map/jit(cholesky)/cholesky | solution.py:80
  114.2 1.1 cholesky.224
  115.3 9.8 %custom-call.40 = f32[1,128,128]{1,2,0:T(8,128)S(1)} custom-call(f32[1,128,128]{2,1,0:T(8,128)S(1)} %get-tuple-element.44), custom_call_target="InvertDiagBlocksLowerTriangular" | custom-call | tf_op jit(solution)/shard_map/jit(cholesky)/cholesky | solution.py:80
  125.1 1.9 constant_dynamic-update-slice_fusion.6
  127.0 1.2 convolution_subtract_fusion.1
  128.3 12.1 %cholesky.217 = f32[128,128]{1,0:T(8,128)S(1)} custom-call(f32[128,128]{1,0:T(8,128)S(1)} %cholesky.270), custom_call_target="Cholesky" | custom-call | tf_op jit(solution)/shard_map/jit(cholesky)/cholesky | solution.py:80
  140.4 0.6 select_reduce_fusion.3
  141.0 9.8 %custom-call.41 = f32[1,128,128]{1,2,0:T(8,128)S(1)} custom-call(f32[1,128,128]{2,1,0:T(8,128)S(1)} %get-tuple-element.41), custom_call_target="InvertDiagBlocksLowerTriangular" | custom-call | tf_op jit(solution)/shard_map/jit(cholesky)/cholesky | solution.py:80
  150.8 0.9 convolution_dynamic-update-slice_fusion
  151.7 1.4 convolution_subtract_fusion.6
  153.2 11.7 %cholesky.238 = f32[128,128]{1,0:T(8,128)S(1)} custom-call(f32[128,128]{1,0:T(8,128)S(1)} %cholesky.275), custom_call_target="Cholesky" | custom-call | tf_op jit(solution)/shard_map/jit(cholesky)/cholesky | solution.py:80
  164.9 0.6 select_reduce_fusion.2
  165.5 9.9 %custom-call.42 = f32[1,128,128]{1,2,0:T(8,128)S(1)} custom-call(f32[1,128,128]{2,1,0:T(8,128)S(1)} %get-tuple-element.38), custom_call_target="InvertDiagBlocksLowerTriangular" | custom-call | tf_op jit(solution)/shard_map/jit(cholesky)/cholesky | solution.py:80
  175.5 0.8 convolution_dynamic-update-slice_fusion.1
  176.3 1.4 convolution_subtract_fusion.9
  177.7 11.7 %cholesky.255 = f32[128,128]{1,0:T(8,128)S(1)} custom-call(f32[128,128]{1,0:T(8,128)S(1)} %convolution_subtract_fusion.9), custom_call_target="Cholesky" | custom-call | tf_op jit(solution)/shard_map/jit(cholesky)/cholesky | solution.py:80
  189.4 0.6 select_reduce_fusion.1
  190.1 0.6 compare_reduce_fusion.1
  190.7 0.6 compare_reduce_fusion
  191.4 0.7 compare_reduce_fusion.2
  194.5 2.3 select_select_fusion
  196.8 13.6 %while.1 = (s32[]{:T(128)}, f32[512,512]{1,0:T(8,128)}, s32[4,2]{0,1:T(2,128)S(1)}, f32[4,128,128]{2,1,0:T(8,128)}, s32[]{:T(128)}) while((s32[]{:T(128)}, f32[512,512]{1,0:T(8,128)}, s32[4,2]{0,1:T(2,128)S(1)}, f32[4,128,128]{2,1,0:T(8,128)}, s32[]{:T(128)}) %tuple.45), condition=%wide.while_cond, body=%wide.while_body.sunk | while | flops 2 | bytes 132205 | solution.py:83
  196.9 0.5 fusion.181
  197.4 2.8 bitcast_dynamic-update-slice_fusion.2
  200.3 0.5 fusion.181
  200.9 2.8 bitcast_dynamic-update-slice_fusion.2
  203.7 0.5 fusion.181
  204.3 2.8 bitcast_dynamic-update-slice_fusion.2
  207.1 0.5 fusion.181
  207.7 2.7 bitcast_dynamic-update-slice_fusion.2
  210.4 40.1 %custom-call.43 = f32[4,128,128]{1,2,0:T(8,128)S(1)} custom-call(f32[4,128,128]{2,1,0:T(8,128)} %get-tuple-element.12), custom_call_target="InvertDiagBlocksLowerTriangular" | custom-call | tf_op jit(solution)/shard_map/jit(_cho_solve)/triangular_solve | solution.py:83
  250.6 1.8 fusion.42
  256.1 0.5 convolution_subtract_fusion.2
  256.9 1.2 fusion
  258.1 1.9 fusion.153
  262.9 1.2 fusion.2
  264.2 0.6 fusion.44
  264.7 3.7 %fusion.7 = f32[1024,1,256]{2,0,1:T(8,128)S(1)} fusion(f32[512,1024]{1,0:T(8,128)S(1)} %subtract_multiply_fusion, f32[1024,256]{1,0:T(8,128)S(1)} %copy.30, f32[128,256]{1,0:T(8,128)S(1)} %fusion.104, f32[128,256]{1,0:T(8,128)S(1)} %fusion.102, f32[128,256]{1,0:T(8,128)S(1)} %fusion.99, f32[128,256]{1,0:T(8,128)S(1)} %fusion.97, f32[256]{0:T(256)S(1)} %bitcast.250, ...), kind=kOutput, calls=%fused_computation.14 | convolution fusion | flops 1612840960 | bytes 4720640 | tf_op jit(solution)/shard_map/dot_general | solution.py:82
  268.5 1.1 copy.28
  269.5 31.9 %all_to_all.37 = f32[1024,1,256]{2,1,0:T(1,128)S(1)} all-to-all(f32[1024,1,256]{2,1,0:T(1,128)S(1)} %copy.28), channel_id=1, replica_groups=mesh['patch'=4,'member'=8] {'member'}, dimensions={0} | all-to-all | bytes 2097152 | tf_op jit(solution)/shard_map/all_to_all | solution.py:91
  301.4 1.6 copy.34
  (81 shorter events, 10.4 us)
Async XLA Ops:
  0.0 18.4 %copy-start.3 = (f32[128,8,256]{2,1,0:T(8,128)S(1)}, f32[128,8,256]{2,1,0:T(8,128)}, u32[]{:S(2)}) copy-start(f32[128,8,256]{2,1,0:T(8,128)} %param.7) | copy-start | bytes 3145732
  0.0 7.6 %copy-start.5 = (f32[4,8,256]{2,1,0:T(8,128)S(1)}, f32[4,8,256]{2,1,0:T(8,128)}, u32[]{:S(2)}) copy-start(f32[4,8,256]{2,1,0:T(8,128)} %param.8) | copy-start | bytes 98308
  1.7 16.7 %collective-permute-start.2 = (f32[128,2,256]{2,0,1:T(8,128)S(1)}, f32[128,2,256]{2,0,1:T(8,128)S(1)}, u32[]{:S(2)}, u32[]{:S(2)}) collective-permute-start(f32[128,2,256]{2,0,1:T(8,128)S(1)} %get-tuple-element.34), channel_id=1, source_target_pairs={{0,8},{8,16},{16,24},{1,9},{9,17},{17,25},{2,10},{10,18},{18,26},{... | collective-permute-start | bytes 786440 | tf_op jit(solution)/shard_map/ppermute | solution.py:23
  5.1 13.6 %collective-permute-start.3 = (f32[128,2,256]{2,0,1:T(8,128)S(1)}, f32[128,2,256]{2,0,1:T(8,128)S(1)}, u32[]{:S(2)}, u32[]{:S(2)}) collective-permute-start(f32[128,2,256]{2,0,1:T(8,128)S(1)} %get-tuple-element.33), channel_id=1, source_target_pairs={{8,0},{16,8},{24,16},{9,1},{17,9},{25,17},{10,2},{18,10},{26,18},{... | collective-permute-start | bytes 786440 | tf_op jit(solution)/shard_map/ppermute | solution.py:25
  7.6 10.7 %collective-permute-start.1 = (f32[4,1,256]{2,1,0:T(1,128)S(1)}, f32[4,1,256]{2,1,0:T(1,128)S(1)}, u32[]{:S(2)}, u32[]{:S(2)}) collective-permute-start(f32[4,1,256]{2,1,0:T(1,128)S(1)} %get-tuple-element.58), channel_id=1, source_target_pairs={{8,0},{16,8},{24,16},{9,1},{17,9},{25,17},{10,2},{18,10},{26,18},{... | collective-permute-start | bytes 12296 | tf_op jit(solution)/shard_map/ppermute | solution.py:25
  9.5 8.8 %collective-permute-start = (f32[4,1,256]{2,1,0:T(1,128)S(1)}, f32[4,1,256]{2,1,0:T(1,128)S(1)}, u32[]{:S(2)}, u32[]{:S(2)}) collective-permute-start(f32[4,1,256]{2,1,0:T(1,128)S(1)} %get-tuple-element.57), channel_id=1, source_target_pairs={{0,8},{8,16},{16,24},{1,9},{9,17},{17,25},{2,10},{10,18},{18,26},{... | collective-permute-start | bytes 12296 | tf_op jit(solution)/shard_map/ppermute | solution.py:23
  19.3 0.7 copy-start.9
  22.4 36.7 %copy-start.6 = (s32[1,512]{1,0:T(1,128)S(1)}, s32[1,512]{1,0:T(1,128)}, u32[]{:S(2)}) copy-start(s32[1,512]{1,0:T(1,128)} %param.10) | copy-start | bytes 6148
  22.4 36.7 %copy-start.7 = (f32[1,512]{1,0:T(1,128)S(1)}, f32[1,512]{1,0:T(1,128)}, u32[]{:S(2)}) copy-start(f32[1,512]{1,0:T(1,128)} %param.13) | copy-start | bytes 6148
  53.7 24.8 %collective-permute-start.5 = (f32[1024,1,256]{2,0,1:T(8,128)S(1)}, f32[1024,1,256]{2,0,1:T(8,128)S(1)}, u32[]{:S(2)}, u32[]{:S(2)}) collective-permute-start(f32[1024,1,256]{2,0,1:T(8,128)S(1)} %bitcast.228), channel_id=1, source_target_pairs={{1,0},{2,1},{3,2},{4,3},{5,4},{6,5},{7,6},{8,7},{9,8},{10,9},{11,1... | collective-permute-start | bytes 3145736 | tf_op jit(solution)/shard_map/ppermute | solution.py:25
  56.5 24.3 %collective-permute-start.4 = (f32[1024,1,256]{2,0,1:T(8,128)S(1)}, f32[1024,1,256]{2,0,1:T(8,128)S(1)}, u32[]{:S(2)}, u32[]{:S(2)}) collective-permute-start(f32[1024,1,256]{2,0,1:T(8,128)S(1)} %bitcast.229), channel_id=1, source_target_pairs={{0,1},{1,2},{2,3},{3,4},{4,5},{5,6},{6,7},{7,8},{8,9},{9,10},{10,1... | collective-permute-start | bytes 3145736 | tf_op jit(solution)/shard_map/ppermute | solution.py:23
  89.0 1.9 copy-start
  90.7 0.7 copy-start.8
  90.7 1.6 copy-start.1
  101.4 1.0 copy-start.4
  250.5 2.2 copy-start.2
where the time goes:
time: 309 us; the launch traced here: 303 us
  other arithmetic  130 us (42%)
  blocking collectives  63.1 us (20%)
  local copies, waits for them, and re-layouts  32.8 us (11%)
  matrix products  30 us (10%)
  waiting for transfers between devices  25.6 us (8%)
  starting transfers between devices  17.3 us (6%)
  between operations  3.87 us (1%)
    another operation x14, other arithmetic, per_device(): factor = jnp.linalg.cholesky(inner)  80.7 us
    another operation x3, other arithmetic, per_device(): jax.scipy.linalg.cho_solve((factor, True), projected)  42.5 us
    all_to_all x1, blocking collectives, per_device(): lax.all_to_all(analysed.reshape(members, 1, width), 'member', split_axis=...  31.9 us
    all_to_all x1, blocking collectives, per_device(): lax.all_to_all(field, 'member', split_axis=1, concat_axis=0, tiled=True)  31.3 us
    ppermute x3, waiting for transfers between devices, padded(): lax.ppermute(head, axis, [((i + 1) % count, i) for i in range(ends)])  23.3 us
    another operation x12, local copies, waits for them, and re-layouts  13.6 us
    ppermute x3, starting transfers between devices, padded(): lax.ppermute(tail, axis, [(i, (i + 1) % count) for i in range(ends)])  10.1 us
    another operation x6, matrix products, per_device(): factor = jnp.linalg.cholesky(inner)  7.76 us
  transfers between devices with their start and end apart: 6, of which 3 were waited for; matrix products, arithmetic and copies ran while one was open for 0% of the time, Pallas kernels for 0%

commit v1 on v0

v1 whole, which is shorter than its diff:
```python
import functools
import math

import jax
import jax.numpy as jnp
from jax import lax
from jax.experimental import pallas as pl
from jax.experimental.pallas import tpu as pltpu
from jax.sharding import PartitionSpec as P

STEPS = 2
COARSE = 0.06
DONE = 1e-4
LARGE = 2e4
F32 = jnp.float32
BF16 = jnp.bfloat16


def padded(cells, sides, width):
    for axis, dim in sides:
        count = lax.axis_size(axis)
        ends = count - 1
        head = lax.slice_in_dim(cells, 0, width, axis=dim)
        tail = lax.slice_in_dim(cells, cells.shape[dim] - width, cells.shape[dim], axis=dim)
        cells = jnp.concatenate(
            [
                lax.ppermute(tail, axis, [(i, (i + 1) % count) for i in range(ends)]),
                cells,
                lax.ppermute(head, axis, [((i + 1) % count, i) for i in range(ends)]),
            ],
            axis=dim,
        )
    return cells


def advance(extended, flow_piece, emission):
    field = extended[1:-1]
    behind_rows = extended[:-2]
    ahead_rows = extended[2:]
    behind_cols = jnp.roll(field, 1, axis=2)
    ahead_cols = jnp.roll(field, -1, axis=2)
    row_flow = flow_piece[0][:, None, :]
    col_flow = flow_piece[1][:, None, :]
    advected = (
        field
        - jnp.maximum(row_flow, 0.0) * (field - behind_rows)
        - jnp.minimum(row_flow, 0.0) * (ahead_rows - field)
        - jnp.maximum(col_flow, 0.0) * (field - behind_cols)
        - jnp.minimum(col_flow, 0.0) * (ahead_cols - field)
    )
    return (1.0 - flow_piece[2][:, None, :]) * advected + emission[None, :, None] * flow_piece[3][:, None, :]


def pieces(x, count):
    parts = []
    for _ in range(count - 1):
        part = x.astype(BF16)
        parts.append(part)
        x = x - part.astype(F32)
    return parts + [x.astype(BF16)]


def dot(a, b):
    return lax.dot_general(a, b, (((1,), (0,)), ((), ())), preferred_element_type=F32)


def dot_t(a, b):
    return lax.dot_general(a, b, (((0,), (0,)), ((), ())), preferred_element_type=F32)


def product(a, b):
    total = None
    for i, left in enumerate(a):
        for j, right in enumerate(b):
            if i + j < max(len(a), len(b)):
                term = dot(left, right)
                total = term if total is None else total + term
    return total


def region_kernel(
    up_ref, own_ref, down_ref, cells_ref, count_ref, values_ref, scales_ref, out_ref,
    high_ref, low_ref, spread_high, spread_low, factor, answer,
):
    members, width = own_ref.shape
    slots = cells_ref.shape[1]
    root = math.sqrt(members - 1)
    step = 256

    means = []
    for place, row in enumerate((up_ref, own_ref, down_ref)):
        mean = jnp.sum(row[...], axis=0, keepdims=True) * (1.0 / members)
        means.append(mean)
        for first in range(0, members, step):
            at = (pl.ds(first, step), pl.ds(place * width, width))
            high, low = pieces(row[pl.ds(first, step), :] - mean, 2)
            high_ref[at] = high
            low_ref[at] = low
    chosen = (
        lax.broadcasted_iota(jnp.int32, (3 * width, slots), 0) == cells_ref[...]
    ).astype(F32).astype(BF16)
    active = lax.broadcasted_iota(jnp.int32, (1, slots), 1) < count_ref[0]
    slot_weight = jnp.where(active, scales_ref[...], 0.0)
    scale = slot_weight * (1.0 / root)
    mean_parts = pieces(jnp.broadcast_to(jnp.concatenate(means, axis=1), (8, 3 * width)), 3)
    predicted_mean = (dot(mean_parts[0], chosen) + (dot(mean_parts[1], chosen) + dot(mean_parts[2], chosen)))[:1]
    innovation = slot_weight * (values_ref[...] - predicted_mean)
    for first in range(0, members, step):
        rows = pl.ds(first, step)
        spread = (dot(high_ref[rows, :], chosen) + dot(low_ref[rows, :], chosen)) * scale
        high, low = pieces(spread, 2)
        spread_high[rows, :] = high
        spread_low[rows, :] = low

    high, low = spread_high[...], spread_low[...]
    middle = pl.ds(width, width)
    eye = lax.broadcasted_iota(jnp.int32, (slots, slots), 0) == lax.broadcasted_iota(
        jnp.int32, (slots, slots), 1
    )
    cross = dot_t(high, low)
    matrix = dot_t(high, high) + (cross + cross.T) + jnp.where(eye, 1.0, 0.0)
    right = dot_t(high, high_ref[:, middle]) + (dot_t(high, low_ref[:, middle]) + dot_t(low, high_ref[:, middle]))

    norm = jnp.max(jnp.sum(jnp.abs(matrix), axis=0, keepdims=True))
    start = 2.0 / (1.0 + norm)
    factor[...] = matrix * start
    answer[...] = right * start

    def refine(bound, count):
        gain = 2.0 / (2.0 - bound * bound)
        parts = pieces(factor[...], count)
        answer[...] = gain * (2.0 * answer[...] - product(parts, pieces(answer[...], count)))
        factor[...] = gain * (2.0 * factor[...] - product(parts, parts))
        return bound * bound / (2.0 - bound * bound)

    def finish(bound):
        gain = 2.0 / (2.0 - bound * bound)
        rest = factor[...].astype(BF16)
        answer[...] = gain * (answer[...] + dot(rest, answer[...].astype(BF16)))
        factor[...] = gain * (dot(rest, rest) - jnp.where(eye, 0.5 * bound * bound, 0.0))
        return bound * bound / (2.0 - bound * bound)

    bound = 1.0 - start
    bound = lax.while_loop(
        lambda b: jnp.logical_and(b > COARSE, norm > LARGE), lambda b: refine(b, 3), bound
    )
    bound = lax.while_loop(lambda b: b > COARSE, lambda b: refine(b, 2), bound)
    factor[...] = jnp.where(eye, 1.0, 0.0) - factor[...]
    lax.while_loop(lambda b: b > DONE, finish, bound)

    solved = answer[...]
    solved_parts = pieces(solved, 2)
    innovation_parts = pieces(jnp.broadcast_to(innovation * (1.0 / root), (8, slots)), 3)
    shift = product(innovation_parts, pieces(solved, 3))[:1]
    half = [part * jnp.asarray(-0.5, BF16) for part in solved_parts]
    for first in range(0, members, step):
        rows = pl.ds(first, step)
        moved = product([spread_high[rows, :], spread_low[rows, :]], half)
        out_ref[rows, :] = own_ref[rows, :] + shift + moved


def analyse(up, own, down, cells, count, values, scales):
    members, width = own.shape
    slots = cells.shape[1]
    vmem = pl.BlockSpec(memory_space=pltpu.VMEM)
    return pl.pallas_call(
        region_kernel,
        out_shape=jax.ShapeDtypeStruct((members, width), F32),
        in_specs=[vmem] * 4 + [pl.BlockSpec(memory_space=pltpu.SMEM)] + [vmem] * 2,
        out_specs=vmem,
        scratch_shapes=[
            pltpu.VMEM((members, 3 * width), BF16),
            pltpu.VMEM((members, 3 * width), BF16),
            pltpu.VMEM((members, slots), BF16),
            pltpu.VMEM((members, slots), BF16),
            pltpu.VMEM((slots, slots), F32),
            pltpu.VMEM((slots, width), F32),
        ],
        compiler_params=pltpu.CompilerParams(vmem_limit_bytes=48 * 1024 * 1024),
        name="region",
    )(up, own, down, cells, count, values, scales)


def per_device(
    init_field, flow_fields, emission, observed_cell, observed_count, observed_value, observed_scale
):
    rows = init_field.shape[1]
    width = init_field.shape[2]
    field = jnp.transpose(init_field, (1, 0, 2))
    extended = padded(field, (("patch", 0),), STEPS)
    flow_wide = padded(flow_fields, (("patch", 1),), STEPS - 1)
    for step_index in range(STEPS):
        margin = STEPS - 1 - step_index
        extended = advance(
            extended, flow_wide[:, step_index : step_index + rows + 2 * margin, :], emission
        )
    regrouped = lax.all_to_all(extended, "member", split_axis=0, concat_axis=0, tiled=True)
    own = regrouped.reshape(-1, width)
    count = lax.axis_size("patch") * lax.axis_size("member")
    axes = ("patch", "member")
    up = lax.ppermute(own, axes, [(i, i + 1) for i in range(count - 1)])
    down = lax.ppermute(own, axes, [(i + 1, i) for i in range(count - 1)])
    analysed = analyse(up, own, down, observed_cell, observed_count, observed_value, observed_scale)
    returned = lax.all_to_all(
        analysed.reshape(rows, -1, width), "member", split_axis=0, concat_axis=0, tiled=True
    )
    return jnp.transpose(returned, (1, 0, 2))


def solution(mesh):
    return jax.shard_map(
        per_device,
        mesh=mesh,
        in_specs=(
            P("member", "patch", None),
            P(None, "patch", None),
            P("member"),
            P(("patch", "member"), None),
            P(("patch", "member")),
            P(("patch", "member"), None),
            P(("patch", "member"), None),
        ),
        out_specs=P("member", "patch", None),
        check_vma=False,
    )
```

time: 309 us -> 132 us (0.43); the launches traced: 303 us -> 132 us
  other arithmetic: 130 us -> 2.05 us
  matrix products: 30 us -> 0 us
  local copies, waits for them, and re-layouts: 32.8 us -> 4.87 us
  Pallas kernels: 0 us -> 18.1 us
    another operation x17 -> x0, other arithmetic: 123 us -> none  [the longest x14 80.7 us: per_device(): factor = jnp.linalg.cholesky(inner)]
    ppermute x3 -> x2, waiting for transfers between devices: 23.3 us -> 1.99 us  [padded(): lax.ppermute(head, axis, [((i + 1) % count, i) for i in range(ends)])]
    ppermute x0 -> x2, waiting for transfers between devices: none -> 20.4 us  [the longest x1 20.4 us: per_device(): up = lax.ppermute(own, axes, [(i, i + 1) for i in range(count - 1)])]
    pallas_call x0 -> x1, Pallas kernels: none -> 18.1 us  [analyse(): pl.pallas_call(region_kernel, out_shape=jax.ShapeDtypeStruct((members, wi...]
    another operation x34 -> x0, matrix products: 15.1 us -> none  [the longest x6 7.76 us: per_device(): factor = jnp.linalg.cholesky(inner)]
    dot_general x7 -> x0, matrix products: 14.9 us -> none  [the longest x1 4.5 us: per_device(): jnp.dot(spread.T, spread, precision=HIGH)]
    another operation x17 -> x0, local copies, waits for them, and re-layouts: 14.7 us -> none
    ppermute x0 -> x2, starting transfers between devices: none -> 8.25 us  [the longest x1 6.34 us: per_device(): down = lax.ppermute(own, axes, [(i + 1, i) for i in range(count - 1)])]
where the time goes in v1:
time: 132 us
  blocking collectives  60.4 us (46%)
  waiting for transfers between devices  25 us (19%)
  starting transfers between devices  20.3 us (15%)
  Pallas kernels  18.1 us (14%)
  local copies, waits for them, and re-layouts  4.87 us (4%)
  other arithmetic  2.05 us (2%)
    all_to_all x1, blocking collectives, per_device(): lax.all_to_all(extended, 'member', split_axis=0, concat_axis=0, tiled=True)  31.4 us
    all_to_all x1, blocking collectives, per_device(): lax.all_to_all(analysed.reshape(rows, -1, width), 'member', split_axis=0,...  29 us
    ppermute x1, waiting for transfers between devices, per_device(): up = lax.ppermute(own, axes, [(i, i + 1) for i in range(count - 1)])  20.4 us
    pallas_call x1, Pallas kernels, analyse(): pl.pallas_call(region_kernel, out_shape=jax.ShapeDtypeStruct((members, wi...  18.1 us
    ppermute x2, starting transfers between devices, padded(): lax.ppermute(tail, axis, [(i, (i + 1) % count) for i in range(ends)])  7.69 us
    ppermute x1, starting transfers between devices, per_device(): down = lax.ppermute(own, axes, [(i + 1, i) for i in range(count - 1)])  6.34 us
    ppermute x2, starting transfers between devices, padded(): lax.ppermute(head, axis, [((i + 1) % count, i) for i in range(ends)])  4.38 us
  transfers between devices with their start and end apart: 6, of which 3 were waited for; matrix products, arithmetic and copies ran while one was open for 0% of the time, Pallas kernels for 0%

profile of v1, /device:TPU:2, one launch (start us, length us, event | category | flops | bytes accessed | tf_op | source)
XLA Modules:
  0.0 131.5 jit_solution(16321690029499210653)
XLA Ops:
  0.0 0.0 copy-start.3
  0.0 1.6 %copy.13 = f32[128,8,256]{2,0,1:T(8,128)S(1)} copy(f32[128,8,256]{2,1,0:T(8,128)} %param.7) | data formatting | bytes 2097152 | tf_op args[0]
  1.6 3.4 %collective-permute-start.2 = (f32[2,128,256]{2,1,0:T(8,128)S(1)}, f32[2,128,256]{2,1,0:T(8,128)S(1)}, u32[]{:S(2)}, u32[]{:S(2)}) collective-permute-start(f32[2,128,256]{2,1,0:T(8,128)S(1)} %get-tuple-element.14), channel_id=1, source_target_pairs={{0,8},{8,16},{16,24},{1,9},{9,17},{17,25},{2,10},{10,18},{18,26},{... | collective-permute-start | bytes 786440 | tf_op jit(solution)/shard_map/ppermute | solution.py:27
  5.0 2.5 %collective-permute-start.3 = (f32[2,128,256]{2,1,0:T(8,128)S(1)}, f32[2,128,256]{2,1,0:T(8,128)S(1)}, u32[]{:S(2)}, u32[]{:S(2)}) collective-permute-start(f32[2,128,256]{2,1,0:T(8,128)S(1)} %get-tuple-element.13), channel_id=1, source_target_pairs={{8,0},{16,8},{24,16},{9,1},{17,9},{25,17},{10,2},{18,10},{26,18},{... | collective-permute-start | bytes 786440 | tf_op jit(solution)/shard_map/ppermute | solution.py:29
  7.5 0.0 copy-done.3
  7.5 4.3 %collective-permute-start = (f32[4,1,256]{2,1,0:T(1,128)S(1)}, f32[4,1,256]{2,1,0:T(1,128)S(1)}, u32[]{:S(2)}, u32[]{:S(2)}) collective-permute-start(f32[4,1,256]{2,1,0:T(1,128)S(1)} %get-tuple-element.27), channel_id=1, source_target_pairs={{0,8},{8,16},{16,24},{1,9},{9,17},{17,25},{2,10},{10,18},{18,26},{... | collective-permute-start | bytes 12296 | tf_op jit(solution)/shard_map/ppermute | solution.py:27
  11.8 1.9 %collective-permute-start.1 = (f32[4,1,256]{2,1,0:T(1,128)S(1)}, f32[4,1,256]{2,1,0:T(1,128)S(1)}, u32[]{:S(2)}, u32[]{:S(2)}) collective-permute-start(f32[4,1,256]{2,1,0:T(1,128)S(1)} %get-tuple-element.28), channel_id=1, source_target_pairs={{8,0},{16,8},{24,16},{9,1},{17,9},{25,17},{10,2},{18,10},{26,18},{... | collective-permute-start | bytes 12296 | tf_op jit(solution)/shard_map/ppermute | solution.py:29
  13.8 2.6 %collective-permute-done = f32[4,1,256]{2,1,0:T(1,128)S(1)} collective-permute-done((f32[4,1,256]{2,1,0:T(1,128)S(1)}, f32[4,1,256]{2,1,0:T(1,128)S(1)}, u32[]{:S(2)}, u32[]{:S(2)}) %collective-permute-start) | collective-permute-done | bytes 4128 | tf_op jit(solution)/shard_map/ppermute | solution.py:27
  16.3 2.0 %collective-permute-done.1 = f32[4,1,256]{2,1,0:T(1,128)S(1)} collective-permute-done((f32[4,1,256]{2,1,0:T(1,128)S(1)}, f32[4,1,256]{2,1,0:T(1,128)S(1)}, u32[]{:S(2)}, u32[]{:S(2)}) %collective-permute-start.1) | collective-permute-done | bytes 4128 | tf_op jit(solution)/shard_map/ppermute | solution.py:29
  18.3 0.0 collective-permute-done.2
  18.4 0.0 collective-permute-done.3
  18.4 0.1 pad_maximum_fusion
  18.5 0.4 fusion.21
  18.9 0.0 copy-start.4
  18.9 0.2 fusion.22
  19.2 0.4 copy-done.4
  19.6 1.1 fusion.6
  20.7 0.4 fusion.23
  21.0 0.2 fusion.24
  21.2 0.8 fusion.15
  22.1 0.0 copy-start
  22.1 0.0 copy-start.1
  22.1 0.0 copy-start.2
  22.1 31.4 %all_to_all.10 = f32[8,128,256]{2,1,0:T(8,128)S(1)} all-to-all(f32[8,128,256]{2,1,0:T(8,128)S(1)} %fusion.15), channel_id=1, replica_groups=mesh['patch'=4,'member'=8] {'member'}, dimensions={0} | all-to-all | bytes 2097152 | tf_op jit(solution)/shard_map/all_to_all | solution.py:197
  53.5 1.9 %collective-permute-start.4 = (f32[1024,256]{1,0:T(8,128)S(1)}, f32[1024,256]{1,0:T(8,128)S(1)}, u32[]{:S(2)}, u32[]{:S(2)}) collective-permute-start(f32[1024,256]{1,0:T(8,128)S(1)} %bitcast.30), channel_id=1, source_target_pairs={{0,1},{1,2},{2,3},{3,4},{4,5},{5,6},{6,7},{7,8},{8,9},{9,10},{10,1... | collective-permute-start | bytes 3145736 | tf_op jit(solution)/shard_map/ppermute | solution.py:201
  55.4 6.3 %collective-permute-start.5 = (f32[1024,256]{1,0:T(8,128)S(1)}, f32[1024,256]{1,0:T(8,128)S(1)}, u32[]{:S(2)}, u32[]{:S(2)}) collective-permute-start(f32[1024,256]{1,0:T(8,128)S(1)} %bitcast.31), channel_id=1, source_target_pairs={{1,0},{2,1},{3,2},{4,3},{5,4},{6,5},{7,6},{8,7},{9,8},{10,9},{11,1... | collective-permute-start | bytes 3145736 | tf_op jit(solution)/shard_map/ppermute | solution.py:202
  62.4 20.4 %collective-permute-done.4.up_ref = f32[1024,256]{1,0:T(8,128)S(1)} collective-permute-done((f32[1024,256]{1,0:T(8,128)S(1)}, f32[1024,256]{1,0:T(8,128)S(1)}, u32[]{:S(2)}, u32[]{:S(2)}) %collective-permute-start.4) | collective-permute-done | bytes 1048608 | tf_op jit(solution)/shard_map/ppermute | solution.py:201
  82.8 0.0 collective-permute-done.5.down_ref
  82.8 0.0 copy-done
  82.8 0.0 copy-done.1
  82.9 0.0 copy-done.2
  82.9 18.1 %region.1 = f32[1024,256]{1,0:T(8,128)S(1)} custom-call(f32[1024,256]{1,0:T(8,128)S(1)} %collective-permute-done.4.up_ref, f32[1024,256]{1,0:T(8,128)S(1)} %bitcast.32, f32[1024,256]{1,0:T(8,128)S(1)} %collective-permute-done.5.down_ref, s32[1,512]{1,0:T(1,128)S(1)} %copy-done, s32[1]{0:T(128)S(6)} %copy.14.count_ref, f32[1,512]{1,0:T(1,128)S(1)} %copy-done.1, ...), custom_call_target="tpu_custom_call" | custom-call | tf_op jit(solution)/shard_map/region/pallas_call | solution.py:166
  101.0 29.0 %all_to_all.11 = f32[8,128,256]{2,1,0:T(8,128)S(1)} all-to-all(f32[8,128,256]{2,1,0:T(8,128)S(1)} %bitcast.33), channel_id=1, replica_groups=mesh['patch'=4,'member'=8] {'member'}, dimensions={0} | all-to-all | bytes 2097152 | tf_op jit(solution)/shard_map/all_to_all | solution.py:204
  130.0 1.6 %copy.11 = f32[128,8,256]{2,1,0:T(8,128)} copy(f32[128,8,256]{2,0,1:T(8,128)S(1)} %bitcast.37) | data formatting | bytes 2097152 | tf_op jit(solution)/shard_map/transpose | solution.py:207
  (5 shorter events, 0.1 us)
Async XLA Ops:
  0.0 7.5 %copy-start.3 = (f32[4,8,256]{2,1,0:T(8,128)S(1)}, f32[4,8,256]{2,1,0:T(8,128)}, u32[]{:S(2)}) copy-start(f32[4,8,256]{2,1,0:T(8,128)} %param.8) | copy-start | bytes 98308
  1.6 16.7 %collective-permute-start.2 = (f32[2,128,256]{2,1,0:T(8,128)S(1)}, f32[2,128,256]{2,1,0:T(8,128)S(1)}, u32[]{:S(2)}, u32[]{:S(2)}) collective-permute-start(f32[2,128,256]{2,1,0:T(8,128)S(1)} %get-tuple-element.14), channel_id=1, source_target_pairs={{0,8},{8,16},{16,24},{1,9},{9,17},{17,25},{2,10},{10,18},{18,26},{... | collective-permute-start | bytes 786440 | tf_op jit(solution)/shard_map/ppermute | solution.py:27
  5.0 13.3 %collective-permute-start.3 = (f32[2,128,256]{2,1,0:T(8,128)S(1)}, f32[2,128,256]{2,1,0:T(8,128)S(1)}, u32[]{:S(2)}, u32[]{:S(2)}) collective-permute-start(f32[2,128,256]{2,1,0:T(8,128)S(1)} %get-tuple-element.13), channel_id=1, source_target_pairs={{8,0},{16,8},{24,16},{9,1},{17,9},{25,17},{10,2},{18,10},{26,18},{... | collective-permute-start | bytes 786440 | tf_op jit(solution)/shard_map/ppermute | solution.py:29
  7.5 8.8 %collective-permute-start = (f32[4,1,256]{2,1,0:T(1,128)S(1)}, f32[4,1,256]{2,1,0:T(1,128)S(1)}, u32[]{:S(2)}, u32[]{:S(2)}) collective-permute-start(f32[4,1,256]{2,1,0:T(1,128)S(1)} %get-tuple-element.27), channel_id=1, source_target_pairs={{0,8},{8,16},{16,24},{1,9},{9,17},{17,25},{2,10},{10,18},{18,26},{... | collective-permute-start | bytes 12296 | tf_op jit(solution)/shard_map/ppermute | solution.py:27
  11.8 6.5 %collective-permute-start.1 = (f32[4,1,256]{2,1,0:T(1,128)S(1)}, f32[4,1,256]{2,1,0:T(1,128)S(1)}, u32[]{:S(2)}, u32[]{:S(2)}) collective-permute-start(f32[4,1,256]{2,1,0:T(1,128)S(1)} %get-tuple-element.28), channel_id=1, source_target_pairs={{8,0},{16,8},{24,16},{9,1},{17,9},{25,17},{10,2},{18,10},{26,18},{... | collective-permute-start | bytes 12296 | tf_op jit(solution)/shard_map/ppermute | solution.py:29
  18.9 0.7 copy-start.4
  22.1 60.8 %copy-start = (s32[1,512]{1,0:T(1,128)S(1)}, s32[1,512]{1,0:T(1,128)}, u32[]{:S(2)}) copy-start(s32[1,512]{1,0:T(1,128)} %cells_ref.1) | copy-start | bytes 6148
  22.1 60.8 %copy-start.1 = (f32[1,512]{1,0:T(1,128)S(1)}, f32[1,512]{1,0:T(1,128)}, u32[]{:S(2)}) copy-start(f32[1,512]{1,0:T(1,128)} %values_ref.1) | copy-start | bytes 6148
  22.1 60.8 %copy-start.2 = (f32[1,512]{1,0:T(1,128)S(1)}, f32[1,512]{1,0:T(1,128)}, u32[]{:S(2)}) copy-start(f32[1,512]{1,0:T(1,128)} %scales_ref.1) | copy-start | bytes 6148
  53.5 29.3 %collective-permute-start.4 = (f32[1024,256]{1,0:T(8,128)S(1)}, f32[1024,256]{1,0:T(8,128)S(1)}, u32[]{:S(2)}, u32[]{:S(2)}) collective-permute-start(f32[1024,256]{1,0:T(8,128)S(1)} %bitcast.30), channel_id=1, source_target_pairs={{0,1},{1,2},{2,3},{3,4},{4,5},{5,6},{6,7},{7,8},{8,9},{9,10},{10,1... | collective-permute-start | bytes 3145736 | tf_op jit(solution)/shard_map/ppermute | solution.py:201
  55.4 27.4 %collective-permute-start.5 = (f32[1024,256]{1,0:T(8,128)S(1)}, f32[1024,256]{1,0:T(8,128)S(1)}, u32[]{:S(2)}, u32[]{:S(2)}) collective-permute-start(f32[1024,256]{1,0:T(8,128)S(1)} %bitcast.31), channel_id=1, source_target_pairs={{1,0},{2,1},{3,2},{4,3},{5,4},{6,5},{7,6},{8,7},{9,8},{10,9},{11,1... | collective-permute-start | bytes 3145736 | tf_op jit(solution)/shard_map/ppermute | solution.py:202

commit v2 on v1

v2 whole, which is shorter than its diff:
```python
import functools
import math

import jax
import jax.numpy as jnp
from jax import lax
from jax.experimental import pallas as pl
from jax.experimental.pallas import tpu as pltpu
from jax.sharding import PartitionSpec as P

STEPS = 2
COARSE = 0.06
DONE = 1e-4
LARGE = 2e4
PART = 256
F32 = jnp.float32
BF16 = jnp.bfloat16


def pack_kernel(field_ref, flow_ref, tail_ref, head_ref):
    members, rows, width = field_ref.shape
    for out_ref, first, edge in ((tail_ref, rows - STEPS, rows - 1), (head_ref, 0, 0)):
        for place in range(STEPS):
            out_ref[pl.ds(place * members, members), :] = field_ref[:, first + place, :]
        out_ref[pl.ds(STEPS * members, 8), :] = jnp.concatenate([flow_ref[:, edge, :]] * 2, axis=0)


def forecast_kernel(field_ref, flow_ref, emission_ref, before_ref, after_ref, out_ref, wide_ref):
    members, rows, width = field_ref.shape
    diagonal = lax.broadcasted_iota(jnp.int32, (members, members), 0) == lax.broadcasted_iota(
        jnp.int32, (members, members), 1
    )
    emission = jnp.sum(jnp.where(diagonal, emission_ref[...], 0.0), axis=1, keepdims=True)

    def flow_row(row):
        if row < 0:
            return before_ref[pl.ds(STEPS * members, 4), :]
        if row >= rows:
            return after_ref[pl.ds(STEPS * members, 4), :]
        return flow_ref[:, row, :]

    def start_row(row):
        if row < 0:
            return before_ref[pl.ds((row + STEPS) * members, members), :]
        if row >= rows:
            return after_ref[pl.ds((row - rows) * members, members), :]
        return field_ref[:, row, :]

    def advance(row, behind, field, ahead):
        flow = flow_row(row)
        row_flow, col_flow, kept, source = flow[0:1], flow[1:2], 1.0 - flow[2:3], flow[3:4]
        from_behind, from_ahead = jnp.maximum(row_flow, 0.0), -jnp.minimum(row_flow, 0.0)
        from_left, from_right = jnp.maximum(col_flow, 0.0), -jnp.minimum(col_flow, 0.0)
        stays = 1.0 - from_behind - from_ahead - from_left - from_right
        return (
            (kept * stays) * field
            + (kept * from_behind) * behind
            + (kept * from_ahead) * ahead
            + (kept * from_left) * pltpu.roll(field, 1, 1)
            + (kept * from_right) * pltpu.roll(field, width - 1, 1)
            + emission * source
        )

    margin = STEPS - 1
    for row in range(-margin, rows + margin):
        wide_ref[row + margin] = advance(row, start_row(row - 1), start_row(row), start_row(row + 1))
    for row in range(rows):
        place = row + margin
        out_ref[row] = advance(row, wide_ref[place - 1], wide_ref[place], wide_ref[place + 1])


def unpack_kernel(rows_ref, out_ref):
    for row in range(rows_ref.shape[0]):
        out_ref[:, row, :] = rows_ref[row]


def pieces(x, count):
    parts = []
    for _ in range(count - 1):
        part = x.astype(BF16)
        parts.append(part)
        x = x - part.astype(F32)
    return parts + [x.astype(BF16)]


def dot(a, b):
    return lax.dot_general(a, b, (((1,), (0,)), ((), ())), preferred_element_type=F32)


def dot_t(a, b):
    return lax.dot_general(a, b, (((0,), (0,)), ((), ())), preferred_element_type=F32)


def product(a, b):
    total = None
    for i, left in enumerate(a):
        for j, right in enumerate(b):
            if i + j < max(len(a), len(b)):
                term = dot(left, right)
                total = term if total is None else total + term
    return total


def region_kernel(
    turned_ref, up_ref, own_ref, down_ref, mine_ref, other_ref, out_ref,
    high_ref, low_ref, spread_high, spread_low, factor, answer,
):
    blocks, step, width = own_ref.shape
    members = blocks * step
    slots = mine_ref.shape[1]
    root = math.sqrt(members - 1)

    def at_block(which, block):
        return block + turned_ref[which] * (blocks - 1 - 2 * block)

    observed = jnp.where(turned_ref[1] == 1, other_ref[...], mine_ref[...])
    cells, values, scales, count = (observed[i : i + 1] for i in range(4))
    means = []
    for place, row in enumerate((up_ref, own_ref, down_ref)):
        mean = jnp.sum(jnp.sum(row[...], axis=0), axis=0, keepdims=True) * (1.0 / members)
        means.append(mean)
        for block in range(blocks):
            at = (pl.ds(block * step, step), pl.ds(place * width, width))
            high, low = pieces(row[at_block(place, block)] - mean, 2)
            high_ref[at] = high
            low_ref[at] = low
    chosen = (
        lax.broadcasted_iota(jnp.int32, (3 * width, slots), 0) == cells.astype(jnp.int32)
    ).astype(F32).astype(BF16)
    active = lax.broadcasted_iota(jnp.int32, (1, slots), 1) < count.astype(jnp.int32)
    slot_weight = jnp.where(active, scales, 0.0)
    scale = slot_weight * (1.0 / root)
    mean_parts = pieces(jnp.broadcast_to(jnp.concatenate(means, axis=1), (8, 3 * width)), 3)
    predicted_mean = (dot(mean_parts[0], chosen) + (dot(mean_parts[1], chosen) + dot(mean_parts[2], chosen)))[:1]
    innovation = slot_weight * (values - predicted_mean)
    for first in range(0, members, PART):
        rows = pl.ds(first, PART)
        spread = (dot(high_ref[rows, :], chosen) + dot(low_ref[rows, :], chosen)) * scale
        high, low = pieces(spread, 2)
        spread_high[rows, :] = high
        spread_low[rows, :] = low

    high, low = spread_high[...], spread_low[...]
    middle = pl.ds(width, width)
    eye = lax.broadcasted_iota(jnp.int32, (slots, slots), 0) == lax.broadcasted_iota(
        jnp.int32, (slots, slots), 1
    )
    cross = dot_t(high, low)
    matrix = dot_t(high, high) + (cross + cross.T) + jnp.where(eye, 1.0, 0.0)
    right = dot_t(high, high_ref[:, middle]) + (dot_t(high, low_ref[:, middle]) + dot_t(low, high_ref[:, middle]))

    norm = jnp.max(jnp.sum(jnp.abs(matrix), axis=0, keepdims=True))
    start = 2.0 / (1.0 + norm)
    factor[...] = matrix * start
    answer[...] = right * start

    def refine(bound, count):
        gain = 2.0 / (2.0 - bound * bound)
        parts = pieces(factor[...], count)
        answer[...] = gain * (2.0 * answer[...] - product(parts, pieces(answer[...], count)))
        factor[...] = gain * (2.0 * factor[...] - product(parts, parts))
        return bound * bound / (2.0 - bound * bound)

    def finish(bound):
        gain = 2.0 / (2.0 - bound * bound)
        rest = factor[...].astype(BF16)
        answer[...] = gain * (answer[...] + dot(rest, answer[...].astype(BF16)))
        factor[...] = gain * (dot(rest, rest) - jnp.where(eye, 0.5 * bound * bound, 0.0))
        return bound * bound / (2.0 - bound * bound)

    bound = 1.0 - start
    bound = lax.while_loop(
        lambda b: jnp.logical_and(b > COARSE, norm > LARGE), lambda b: refine(b, 3), bound
    )
    bound = lax.while_loop(lambda b: b > COARSE, lambda b: refine(b, 2), bound)
    factor[...] = jnp.where(eye, 1.0, 0.0) - factor[...]
    lax.while_loop(lambda b: b > DONE, finish, bound)

    solved = answer[...]
    solved_parts = pieces(solved, 2)
    innovation_parts = pieces(jnp.broadcast_to(innovation * (1.0 / root), (8, slots)), 3)
    shift = product(innovation_parts, pieces(solved, 3))[:1]
    half = [part * jnp.asarray(-0.5, BF16) for part in solved_parts]
    for block in range(blocks):
        rows = pl.ds(block * step, step)
        moved = product([spread_high[rows, :], spread_low[rows, :]], half)
        at = at_block(1, block)
        out_ref[at] = own_ref[at] + shift + moved


VMEM = pl.BlockSpec(memory_space=pltpu.VMEM)
LIMIT = pltpu.CompilerParams(vmem_limit_bytes=48 * 1024 * 1024)


def analyse(turned, up, own, down, mine, other):
    blocks, step, width = own.shape
    members = blocks * step
    slots = mine.shape[1]
    return pl.pallas_call(
        region_kernel,
        out_shape=jax.ShapeDtypeStruct(own.shape, F32),
        in_specs=[pl.BlockSpec(memory_space=pltpu.SMEM)] + [VMEM] * 5,
        out_specs=VMEM,
        scratch_shapes=[
            pltpu.VMEM((members, 3 * width), BF16),
            pltpu.VMEM((members, 3 * width), BF16),
            pltpu.VMEM((members, slots), BF16),
            pltpu.VMEM((members, slots), BF16),
            pltpu.VMEM((slots, slots), F32),
            pltpu.VMEM((slots, width), F32),
        ],
        compiler_params=LIMIT,
        name="region",
    )(turned, up, own, down, mine, other)


def per_device(
    init_field, flow_fields, emission, observed_cell, observed_count, observed_value, observed_scale
):
    members, rows, width = init_field.shape
    patches, lanes = lax.axis_size("patch"), lax.axis_size("member")
    axes = ("patch", "member")
    count = patches * lanes

    edge = jax.ShapeDtypeStruct((STEPS * members + 8, width), F32)
    tail, head = pl.pallas_call(
        pack_kernel, out_shape=(edge, edge), in_specs=[VMEM] * 2, out_specs=(VMEM, VMEM),
        compiler_params=LIMIT, name="pack",
    )(init_field, flow_fields)
    before = lax.ppermute(tail, "patch", [(i, i + 1) for i in range(patches - 1)])
    after = lax.ppermute(head, "patch", [(i + 1, i) for i in range(patches - 1)])

    def holder(region):
        patch, row = divmod(region, lanes)
        return patch * lanes + (lanes - 1 - row if patch % 2 else row)

    groups = [[holder(patch * lanes + row) for row in range(lanes)] for patch in range(patches)]
    mine = jnp.concatenate(
        [
            observed_cell.astype(F32),
            observed_value,
            observed_scale,
            jnp.broadcast_to(observed_count.astype(F32)[:, None], observed_cell.shape),
        ]
        * 2,
        axis=0,
    )
    other = lax.ppermute(
        mine, axes, [(g, holder(g)) for g in range(count) if (g // lanes) % 2]
    )

    forecast = pl.pallas_call(
        forecast_kernel, out_shape=jax.ShapeDtypeStruct((rows, members, width), F32),
        in_specs=[VMEM] * 5, out_specs=VMEM,
        scratch_shapes=[pltpu.VMEM((rows + 2 * (STEPS - 1), members, width), F32)],
        compiler_params=LIMIT, name="forecast",
    )(init_field, flow_fields, emission[None, :], before, after)
    own = lax.all_to_all(
        forecast, axes, split_axis=0, concat_axis=0, tiled=True, axis_index_groups=groups
    )
    up = lax.ppermute(own, axes, [(holder(g), holder(g + 1)) for g in range(count - 1)])
    down = lax.ppermute(own, axes, [(holder(g + 1), holder(g)) for g in range(count - 1)])
    patch, lane = lax.axis_index("patch"), lax.axis_index("member")
    region = patch * lanes + jnp.where(patch % 2 == 1, lanes - 1 - lane, lane)
    turned = ((region + jnp.arange(-1, 2, dtype=jnp.int32) + lanes) // lanes + 1) % 2
    analysed = analyse(turned, up, own, down, mine, other)
    returned = lax.all_to_all(
        analysed, axes, split_axis=0, concat_axis=0, tiled=True, axis_index_groups=groups
    )
    return pl.pallas_call(
        unpack_kernel, out_shape=jax.ShapeDtypeStruct((members, rows, width), F32),
        in_specs=[VMEM], out_specs=VMEM, compiler_params=LIMIT, name="unpack",
    )(returned)


def solution(mesh):
    return jax.shard_map(
        per_device,
        mesh=mesh,
        in_specs=(
            P("member", "patch", None),
            P(None, "patch", None),
            P("member"),
            P(("patch", "member"), None),
            P(("patch", "member")),
            P(("patch", "member"), None),
            P(("patch", "member"), None),
        ),
        out_specs=P("member", "patch", None),
        check_vma=False,
    )
```

time: 132 us -> 122 us (0.924)
  the two profiles are of different devices: /device:TPU:2 before, /device:TPU:0 now
where the time goes in v2:
time: 122 us; the launch traced here: 121 us
  blocking collectives  72.9 us (60%)
  Pallas kernels  21 us (17%)
  waiting for transfers between devices  12.2 us (10%)
  starting transfers between devices  11.3 us (9%)
  local copies, waits for them, and re-layouts  2.71 us (2%)
    all_to_all x1, blocking collectives, per_device(): lax.all_to_all(analysed, axes, split_axis=0, concat_axis=0, tiled=True, a...  41.6 us
    all_to_all x1, blocking collectives, per_device(): lax.all_to_all(forecast, axes, split_axis=0, concat_axis=0, tiled=True, a...  31.3 us
    pallas_call x1, Pallas kernels, analyse(): pl.pallas_call(region_kernel, out_shape=jax.ShapeDtypeStruct(own.shape, F...  17.2 us
    ppermute x1, waiting for transfers between devices, per_device(): lax.ppermute(head, 'patch', [(i + 1, i) for i in range(patches - 1)])  7.74 us
    ppermute x1, starting transfers between devices, per_device(): lax.ppermute(tail, 'patch', [(i, i + 1) for i in range(patches - 1)])  4.86 us
    ppermute x1, waiting for transfers between devices, per_device(): lax.ppermute(tail, 'patch', [(i, i + 1) for i in range(patches - 1)])  4.39 us
    ppermute x1, starting transfers between devices, per_device(): lax.ppermute(own, axes, [(holder(g), holder(g + 1)) for g in range(count...  3.1 us
    unnamed x12, local copies, waits for them, and re-layouts  2.66 us
  transfers between devices with their start and end apart: 5, of which 3 were waited for; matrix products, arithmetic and copies ran while one was open for 0% of the time, Pallas kernels for 0%

profile of v2, /device:TPU:0, one launch (start us, length us, event | category | flops | bytes accessed | tf_op | source)
XLA Modules:
  0.0 120.9 jit_solution(1854424348665882842)
XLA Ops:
  0.0 0.0 copy-start
  0.0 1.2 %copy-done = f32[128,8,256]{2,1,0:T(8,128)S(1)} copy-done((f32[128,8,256]{2,1,0:T(8,128)S(1)}, f32[128,8,256]{2,1,0:T(8,128)}, u32[]{:S(2)}) %copy-start) | copy-done | bytes 1048600
  1.2 0.0 copy-start.1
  1.2 0.8 copy-done.1
  2.0 0.2 pack.1
  2.2 4.9 %collective-permute-start = (f32[264,256]{1,0:T(8,128)S(1)}, f32[264,256]{1,0:T(8,128)S(1)}, u32[]{:S(2)}, u32[]{:S(2)}) collective-permute-start(f32[264,256]{1,0:T(8,128)S(1)} %get-tuple-element.7), channel_id=1, source_target_pairs={{0,8},{8,16},{16,24},{1,9},{9,17},{17,25},{2,10},{10,18},{18,26},{... | collective-permute-start | bytes 811016 | tf_op jit(solution)/shard_map/ppermute | solution.py:230
  7.0 0.0 copy-start.2
  7.0 1.3 %collective-permute-start.1 = (f32[264,256]{1,0:T(8,128)S(1)}, f32[264,256]{1,0:T(8,128)S(1)}, u32[]{:S(2)}, u32[]{:S(2)}) collective-permute-start(f32[264,256]{1,0:T(8,128)S(1)} %get-tuple-element.8), channel_id=1, source_target_pairs={{8,0},{16,8},{24,16},{9,1},{17,9},{25,17},{10,2},{18,10},{26,18},{... | collective-permute-start | bytes 811016 | tf_op jit(solution)/shard_map/ppermute | solution.py:231
  8.3 4.4 %collective-permute-done.before_ref = f32[264,256]{1,0:T(8,128)S(1)} collective-permute-done((f32[264,256]{1,0:T(8,128)S(1)}, f32[264,256]{1,0:T(8,128)S(1)}, u32[]{:S(2)}, u32[]{:S(2)}) %collective-permute-start) | collective-permute-done | bytes 270368 | tf_op jit(solution)/shard_map/ppermute | solution.py:230
  12.7 7.7 %collective-permute-done.1.after_ref = f32[264,256]{1,0:T(8,128)S(1)} collective-permute-done((f32[264,256]{1,0:T(8,128)S(1)}, f32[264,256]{1,0:T(8,128)S(1)}, u32[]{:S(2)}, u32[]{:S(2)}) %collective-permute-start.1) | collective-permute-done | bytes 270368 | tf_op jit(solution)/shard_map/ppermute | solution.py:231
  20.5 0.0 copy-done.2
  20.5 2.3 %forecast.1 = f32[8,128,256]{2,1,0:T(8,128)S(1)} custom-call(f32[128,8,256]{2,1,0:T(8,128)S(1)} %copy-done, f32[4,8,256]{2,1,0:T(8,128)S(1)} %copy-done.1, f32[1,128]{1,0:T(1,128)S(1)} %bitcast.2, f32[264,256]{1,0:T(8,128)S(1)} %collective-permute-done.before_ref, f32[264,256]{1,0:T(8,128)S(1)} %collective-permute-done.1.after_ref), custom_call_target="tpu_custom_call" | custom-call | tf_op jit(solution)/shard_map/forecast/pallas_call | solution.py:252
  22.8 31.3 %all_to_all.10.own_ref = f32[8,128,256]{2,1,0:T(8,128)S(1)} all-to-all(f32[8,128,256]{2,1,0:T(8,128)S(1)} %forecast.1), channel_id=1, replica_groups={{0,1,2,3,4,5,6,7},{15,14,13,12,11,10,9,8},{16,17,18,19,20,21,22,23},{31..., dimensions={0} | all-to-all | bytes 2097152 | tf_op jit(solution)/shard_map/all_to_all | solution.py:258
  54.1 0.0 copy-start.5
  54.1 1.4 %collective-permute-start.3 = (f32[8,128,256]{2,1,0:T(8,128)S(1)}, f32[8,128,256]{2,1,0:T(8,128)S(1)}, u32[]{:S(2)}, u32[]{:S(2)}) collective-permute-start(f32[8,128,256]{2,1,0:T(8,128)S(1)} %all_to_all.10.own_ref), channel_id=1, source_target_pairs={{1,0},{2,1},{3,2},{4,3},{5,4},{6,5},{7,6},{15,7},{14,15},{13,14},{... | collective-permute-start | bytes 3145736 | tf_op jit(solution)/shard_map/ppermute | solution.py:262
  55.5 3.1 %collective-permute-start.2 = (f32[8,128,256]{2,1,0:T(8,128)S(1)}, f32[8,128,256]{2,1,0:T(8,128)S(1)}, u32[]{:S(2)}, u32[]{:S(2)}) collective-permute-start(f32[8,128,256]{2,1,0:T(8,128)S(1)} %all_to_all.10.own_ref), channel_id=1, source_target_pairs={{0,1},{1,2},{2,3},{3,4},{4,5},{5,6},{6,7},{7,15},{15,14},{14,13},{... | collective-permute-start | bytes 3145736 | tf_op jit(solution)/shard_map/ppermute | solution.py:261
  59.2 0.0 copy-done.5
  59.3 0.0 copy-start.3
  59.3 0.0 copy-start.4
  59.3 0.6 copy-done.3
  59.9 0.0 copy-done.4
  60.0 0.7 collective-permute-start.4
  60.7 0.0 collective-permute-done.4.other_ref
  60.7 0.0 collective-permute-done.3.down_ref
  60.7 0.1 collective-permute-done.2.up_ref
  60.8 17.2 %region.1 = f32[8,128,256]{2,1,0:T(8,128)S(1)} custom-call(s32[3]{0:T(128)S(1)} %and_select_fusion.turned_ref, f32[8,128,256]{2,1,0:T(8,128)S(1)} %collective-permute-done.2.up_ref, f32[8,128,256]{2,1,0:T(8,128)S(1)} %all_to_all.10.own_ref, f32[8,128,256]{2,1,0:T(8,128)S(1)} %collective-permute-done.3.down_ref, f32[8,512]{1,0:T(8,128)S(1)} %concatenate.3.mine_ref, ...), custom_call_target="tpu_custom_call" | custom-call | tf_op jit(solution)/shard_map/region/pallas_call | solution.py:199
  78.0 41.6 %all_to_all.11.rows_ref = f32[8,128,256]{2,1,0:T(8,128)S(1)} all-to-all(f32[8,128,256]{2,1,0:T(8,128)S(1)} %region.1), channel_id=1, replica_groups={{0,1,2,3,4,5,6,7},{15,14,13,12,11,10,9,8},{16,17,18,19,20,21,22,23},{31..., dimensions={0} | all-to-all | bytes 2097152 | tf_op jit(solution)/shard_map/all_to_all | solution.py:267
  119.6 1.3 %unpack.1 = f32[128,8,256]{2,1,0:T(8,128)} custom-call(f32[8,128,256]{2,1,0:T(8,128)S(1)} %all_to_all.11.rows_ref), custom_call_target="tpu_custom_call" | custom-call | tf_op jit(solution)/shard_map/unpack/pallas_call | solution.py:270
  (4 shorter events, 0.1 us)
Async XLA Ops:
  0.0 1.2 %copy-start = (f32[128,8,256]{2,1,0:T(8,128)S(1)}, f32[128,8,256]{2,1,0:T(8,128)}, u32[]{:S(2)}) copy-start(f32[128,8,256]{2,1,0:T(8,128)} %field_ref.3) | copy-start | bytes 3145732
  1.2 0.8 copy-start.1
  2.2 10.6 %collective-permute-start = (f32[264,256]{1,0:T(8,128)S(1)}, f32[264,256]{1,0:T(8,128)S(1)}, u32[]{:S(2)}, u32[]{:S(2)}) collective-permute-start(f32[264,256]{1,0:T(8,128)S(1)} %get-tuple-element.7), channel_id=1, source_target_pairs={{0,8},{8,16},{16,24},{1,9},{9,17},{17,25},{2,10},{10,18},{18,26},{... | collective-permute-start | bytes 811016 | tf_op jit(solution)/shard_map/ppermute | solution.py:230
  7.0 13.4 %copy-start.2 = (f32[128]{0:T(128)S(1)}, f32[128]{0:T(128)}, u32[]{:S(2)}) copy-start(f32[128]{0:T(128)} %param.9) | copy-start | bytes 1540
  7.0 13.4 %collective-permute-start.1 = (f32[264,256]{1,0:T(8,128)S(1)}, f32[264,256]{1,0:T(8,128)S(1)}, u32[]{:S(2)}, u32[]{:S(2)}) collective-permute-start(f32[264,256]{1,0:T(8,128)S(1)} %get-tuple-element.8), channel_id=1, source_target_pairs={{8,0},{16,8},{24,16},{9,1},{17,9},{25,17},{10,2},{18,10},{26,18},{... | collective-permute-start | bytes 811016 | tf_op jit(solution)/shard_map/ppermute | solution.py:231
  54.1 5.2 %copy-start.5 = (s32[1,512]{1,0:T(1,128)S(1)}, s32[1,512]{1,0:T(1,128)}, u32[]{:S(2)}) copy-start(s32[1,512]{1,0:T(1,128)} %param.10) | copy-start | bytes 6148
  54.1 6.7 %collective-permute-start.3 = (f32[8,128,256]{2,1,0:T(8,128)S(1)}, f32[8,128,256]{2,1,0:T(8,128)S(1)}, u32[]{:S(2)}, u32[]{:S(2)}) collective-permute-start(f32[8,128,256]{2,1,0:T(8,128)S(1)} %all_to_all.10.own_ref), channel_id=1, source_target_pairs={{1,0},{2,1},{3,2},{4,3},{5,4},{6,5},{7,6},{15,7},{14,15},{13,14},{... | collective-permute-start | bytes 3145736 | tf_op jit(solution)/shard_map/ppermute | solution.py:262
  55.5 5.3 %collective-permute-start.2 = (f32[8,128,256]{2,1,0:T(8,128)S(1)}, f32[8,128,256]{2,1,0:T(8,128)S(1)}, u32[]{:S(2)}, u32[]{:S(2)}) collective-permute-start(f32[8,128,256]{2,1,0:T(8,128)S(1)} %all_to_all.10.own_ref), channel_id=1, source_target_pairs={{0,1},{1,2},{2,3},{3,4},{4,5},{5,6},{6,7},{7,15},{15,14},{14,13},{... | collective-permute-start | bytes 3145736 | tf_op jit(solution)/shard_map/ppermute | solution.py:261
  59.3 0.7 copy-start.3
  59.3 0.7 copy-start.4
  60.0 0.7 collective-permute-start.4

commit v3 on v2

v3 whole, which is shorter than its diff:
```python
import functools
import math

import jax
import jax.numpy as jnp
from jax import lax
from jax.experimental import pallas as pl
from jax.experimental.pallas import tpu as pltpu
from jax.sharding import PartitionSpec as P

STEPS = 2
COARSE = 0.06
DONE = 1e-4
LARGE = 2e4
PART = 256
F32 = jnp.float32
BF16 = jnp.bfloat16


def pack_kernel(field_ref, flow_ref, tail_ref, head_ref):
    members, rows, width = field_ref.shape
    for out_ref, first, edge in ((tail_ref, rows - STEPS, rows - 1), (head_ref, 0, 0)):
        for place in range(STEPS):
            out_ref[pl.ds(place * members, members), :] = field_ref[:, first + place, :]
        out_ref[pl.ds(STEPS * members, 8), :] = jnp.concatenate([flow_ref[:, edge, :]] * 2, axis=0)


def weights_of(flow):
    row_flow, col_flow, kept, source = flow[0:1], flow[1:2], 1.0 - flow[2:3], flow[3:4]
    behind, ahead = jnp.maximum(row_flow, 0.0), -jnp.minimum(row_flow, 0.0)
    left, right = jnp.maximum(col_flow, 0.0), -jnp.minimum(col_flow, 0.0)
    stays = 1.0 - behind - ahead - left - right
    return [kept * stays, kept * behind, kept * ahead, kept * left, kept * right, source]


def advance(weights, emission, behind, field, ahead):
    width = field.shape[1]
    return (
        weights[0] * field
        + weights[1] * behind
        + weights[2] * ahead
        + weights[3] * pltpu.roll(field, 1, 1)
        + weights[4] * pltpu.roll(field, width - 1, 1)
        + emission * weights[5]
    )


def emission_column(emission_ref):
    members = emission_ref.shape[1]
    diagonal = lax.broadcasted_iota(jnp.int32, (members, members), 0) == lax.broadcasted_iota(
        jnp.int32, (members, members), 1
    )
    return jnp.sum(jnp.where(diagonal, emission_ref[...], 0.0), axis=1, keepdims=True)


def second_step(info_ref, wanted, shift, emission, wide_ref, weight_ref, out_refs):
    chips = len(out_refs)
    rows = weight_ref.shape[0]
    for s, out_ref in enumerate(out_refs):
        chip = lax.rem(info_ref[0] + s, chips)

        @pl.when(wanted(chip))
        def _():
            for place in range(2):
                position = 2 * chip + place
                row = position + info_ref[2] * (rows - 1 - 2 * position)
                weights = weight_ref[row]
                at = row + shift
                out_ref[place] = advance(
                    [weights[i : i + 1] for i in range(6)],
                    emission, wide_ref[at - 1], wide_ref[at], wide_ref[at + 1],
                )


def store_weights(flow_ref, weight_ref, rows):
    for row in rows:
        for i, weight in enumerate(weights_of(flow_ref[:, row, :])):
            weight_ref[row, pl.ds(i, 1), :] = weight


def inner_kernel(info_ref, field_ref, flow_ref, emission_ref, *refs):
    out_refs, (wide_ref, weight_ref) = refs[:-2], refs[-2:]
    rows = field_ref.shape[1]
    chips = len(out_refs)
    emission = emission_column(emission_ref)
    store_weights(flow_ref, weight_ref, range(rows))
    for row in range(1, rows - 1):
        wide_ref[row] = advance(
            weights_of(flow_ref[:, row, :]), emission,
            field_ref[:, row - 1, :], field_ref[:, row, :], field_ref[:, row + 1, :],
        )
    wanted = lambda chip: jnp.logical_and(chip > 0, chip < chips - 1)
    second_step(info_ref, wanted, 0, emission, wide_ref, weight_ref, out_refs)


def edge_kernel(info_ref, field_ref, flow_ref, emission_ref, before_ref, after_ref, *refs):
    out_refs, (wide_ref, weight_ref) = refs[:-2], refs[-2:]
    members, rows, width = field_ref.shape
    chips = len(out_refs)
    emission = emission_column(emission_ref)
    store_weights(flow_ref, weight_ref, (0, 1, rows - 2, rows - 1))

    def flow_row(row):
        if row < 0:
            return before_ref[pl.ds(STEPS * members, 4), :]
        if row >= rows:
            return after_ref[pl.ds(STEPS * members, 4), :]
        return flow_ref[:, row, :]

    def start_row(row):
        if row < 0:
            return before_ref[pl.ds((row + STEPS) * members, members), :]
        if row >= rows:
            return after_ref[pl.ds((row - rows) * members, members), :]
        return field_ref[:, row, :]

    for row in (-1, 0, 1, 2, rows - 3, rows - 2, rows - 1, rows):
        wide_ref[row + 1] = advance(
            weights_of(flow_row(row)), emission, start_row(row - 1), start_row(row), start_row(row + 1)
        )
    wanted = lambda chip: jnp.logical_or(chip == 0, chip == chips - 1)
    second_step(info_ref, wanted, 1, emission, wide_ref, weight_ref, out_refs)


def collect_kernel(info_ref, *refs):
    chips = (len(refs) - 3) // 2
    both_ref, first_ref, second_ref = refs[-3:]
    chip, core = info_ref[0], info_ref[1]
    at_edge = jnp.logical_or(chip == 0, chip == chips - 1)
    for s in range(chips):
        block = lax.rem(chip + chips - s, chips)
        for ref, here in ((refs[s], jnp.logical_not(at_edge)), (refs[chips + s], at_edge)):

            @pl.when(here)
            def _():
                other, own = ref[1 - core], ref[core]
                both_ref[0, block] = other
                both_ref[1, block] = own
                first_ref[block] = other
                second_ref[block] = own


def unpack_kernel(info_ref, rows_ref, out_ref):
    rows = rows_ref.shape[0]
    for row in range(rows):
        out_ref[:, row, :] = rows_ref[row + info_ref[2] * (rows - 1 - 2 * row)]


def pieces(x, count):
    parts = []
    for _ in range(count - 1):
        part = x.astype(BF16)
        parts.append(part)
        x = x - part.astype(F32)
    return parts + [x.astype(BF16)]


def dot(a, b):
    return lax.dot_general(a, b, (((1,), (0,)), ((), ())), preferred_element_type=F32)


def dot_t(a, b):
    return lax.dot_general(a, b, (((0,), (0,)), ((), ())), preferred_element_type=F32)


def product(a, b):
    total = None
    for i, left in enumerate(a):
        for j, right in enumerate(b):
            if i + j < max(len(a), len(b)):
                term = dot(left, right)
                total = term if total is None else total + term
    return total


def region_kernel(
    info_ref, mine_ref, other_ref, near_ref, far_ref, first_ref, second_ref, out_ref,
    high_ref, low_ref, spread_high, spread_low, factor, answer,
):
    _, chips, step, width = near_ref.shape
    half_of = chips * step
    members = 2 * half_of
    slots = mine_ref.shape[1]
    root = math.sqrt(members - 1)
    core, turned = info_ref[1], info_ref[2] == 1
    swapped = jnp.logical_or(
        jnp.logical_and(info_ref[0] == 0, core == 0), jnp.logical_and(info_ref[0] == chips - 1, core == 1)
    )

    observed = jnp.where(turned, other_ref[...], mine_ref[...])
    cells, values, scales, count = (observed[i : i + 1] for i in range(4))
    cells = cells.astype(jnp.int32)
    offset = sum((cells >= i * width).astype(jnp.int32) for i in (1, 2)) - 1
    column = cells - (offset + 1) * width
    side = offset * jnp.where(turned, -1, 1) * (1 - 2 * core)
    cells = column + width * jnp.where(side == 0, 2, jnp.where(side < 0, 0, 1))

    def block_of(place, part, chip):
        if place == 0:
            pair = (first_ref[chip], second_ref[chip])
            return jnp.where(swapped, pair[1 - part], pair[part])
        if part == 0:
            return near_ref[place - 1, chip]
        return far_ref[2 - place, chip]

    blocks = [(part, chip) for part in range(2) for chip in range(chips)]
    means = []
    for place in range(3):
        total = None
        for part, chip in blocks:
            block = block_of(place, part, chip)
            total = block if total is None else total + block
        mean = jnp.sum(total, axis=0, keepdims=True) * (1.0 / members)
        means.append(mean)
        for index, (part, chip) in enumerate(blocks):
            at = (pl.ds(index * step, step), pl.ds(place * width, width))
            high, low = pieces(block_of(place, part, chip) - mean, 2)
            high_ref[at] = high
            low_ref[at] = low
    chosen = (
        lax.broadcasted_iota(jnp.int32, (3 * width, slots), 0) == cells
    ).astype(F32).astype(BF16)
    active = lax.broadcasted_iota(jnp.int32, (1, slots), 1) < count.astype(jnp.int32)
    slot_weight = jnp.where(active, scales, 0.0)
    scale = slot_weight * (1.0 / root)
    mean_parts = pieces(jnp.broadcast_to(jnp.concatenate(means, axis=1), (8, 3 * width)), 3)
    predicted_mean = (dot(mean_parts[0], chosen) + (dot(mean_parts[1], chosen) + dot(mean_parts[2], chosen)))[:1]
    innovation = slot_weight * (values - predicted_mean)
    for first in range(0, members, PART):
        rows = pl.ds(first, PART)
        spread = (dot(high_ref[rows, :], chosen) + dot(low_ref[rows, :], chosen)) * scale
        high, low = pieces(spread, 2)
        spread_high[rows, :] = high
        spread_low[rows, :] = low

    high, low = spread_high[...], spread_low[...]
    middle = pl.ds(2 * width, width)
    eye = lax.broadcasted_iota(jnp.int32, (slots, slots), 0) == lax.broadcasted_iota(
        jnp.int32, (slots, slots), 1
    )
    cross = dot_t(high, low)
    matrix = dot_t(high, high) + (cross + cross.T) + jnp.where(eye, 1.0, 0.0)
    right = dot_t(high, high_ref[:, middle]) + (dot_t(high, low_ref[:, middle]) + dot_t(low, high_ref[:, middle]))

    norm = jnp.max(jnp.sum(jnp.abs(matrix), axis=0, keepdims=True))
    start = 2.0 / (1.0 + norm)
    factor[...] = matrix * start
    answer[...] = right * start

    def refine(bound, count):
        gain = 2.0 / (2.0 - bound * bound)
        parts = pieces(factor[...], count)
        answer[...] = gain * (2.0 * answer[...] - product(parts, pieces(answer[...], count)))
        factor[...] = gain * (2.0 * factor[...] - product(parts, parts))
        return bound * bound / (2.0 - bound * bound)

    def finish(bound):
        gain = 2.0 / (2.0 - bound * bound)
        rest = factor[...].astype(BF16)
        answer[...] = gain * (answer[...] + dot(rest, answer[...].astype(BF16)))
        factor[...] = gain * (dot(rest, rest) - jnp.where(eye, 0.5 * bound * bound, 0.0))
        return bound * bound / (2.0 - bound * bound)

    bound = 1.0 - start
    bound = lax.while_loop(
        lambda b: jnp.logical_and(b > COARSE, norm > LARGE), lambda b: refine(b, 3), bound
    )
    bound = lax.while_loop(lambda b: b > COARSE, lambda b: refine(b, 2), bound)
    factor[...] = jnp.where(eye, 1.0, 0.0) - factor[...]
    lax.while_loop(lambda b: b > DONE, finish, bound)

    solved = answer[...]
    solved_parts = pieces(solved, 2)
    innovation_parts = pieces(jnp.broadcast_to(innovation * (1.0 / root), (8, slots)), 3)
    shift = product(innovation_parts, pieces(solved, 3))[:1]
    half = [part * jnp.asarray(-0.5, BF16) for part in solved_parts]
    for index, (part, chip) in enumerate(blocks):
        rows = pl.ds(index * step, step)
        moved = product([spread_high[rows, :], spread_low[rows, :]], half)
        out_ref[2 * chip + jnp.abs(core - part)] = block_of(2, part, chip) + shift + moved


VMEM = pl.BlockSpec(memory_space=pltpu.VMEM)
LIMIT = pltpu.CompilerParams(vmem_limit_bytes=48 * 1024 * 1024)


SMEM = pl.BlockSpec(memory_space=pltpu.SMEM)


def call(kernel, name, out_shape, args, scratch=()):
    several = isinstance(out_shape, (list, tuple))
    return pl.pallas_call(
        kernel,
        out_shape=out_shape,
        in_specs=[SMEM] + [VMEM] * (len(args) - 1),
        out_specs=[VMEM] * len(out_shape) if several else VMEM,
        scratch_shapes=scratch,
        compiler_params=LIMIT,
        name=name,
    )(*args)


def array(*shape):
    return jax.ShapeDtypeStruct(shape, F32)


def per_device(
    init_field, flow_fields, emission, observed_cell, observed_count, observed_value, observed_scale
):
    step, rows, width = init_field.shape
    slots = observed_cell.shape[1]
    patches, lanes = lax.axis_size("patch"), lax.axis_size("member")
    chips = lanes // 2
    members = lanes * step
    axes = ("patch", "member")
    count = patches * lanes
    patch, lane = lax.axis_index("patch"), lax.axis_index("member")
    info = jnp.stack([lane // 2, lane % 2, patch % 2]).astype(jnp.int32)

    edge = array(STEPS * step + 8, width)
    tail, head = pl.pallas_call(
        pack_kernel, out_shape=(edge, edge), in_specs=[VMEM] * 2, out_specs=(VMEM, VMEM),
        compiler_params=LIMIT, name="pack",
    )(init_field, flow_fields)
    before = lax.ppermute(tail, "patch", [(i, i + 1) for i in range(patches - 1)])
    after = lax.ppermute(head, "patch", [(i + 1, i) for i in range(patches - 1)])

    mine = jnp.concatenate(
        [
            observed_cell.astype(F32),
            observed_value,
            observed_scale,
            jnp.broadcast_to(observed_count.astype(F32)[:, None], observed_cell.shape),
        ]
        * 2,
        axis=0,
    )
    other = lax.ppermute(
        mine, axes,
        [(p * lanes + i, p * lanes + lanes - 1 - i) for p in range(1, patches, 2) for i in range(lanes)],
    )

    def along(piece, s, ends):
        pairs = []
        for chip in range(chips):
            to = (chip + s) % chips
            if (to in (0, chips - 1)) == ends:
                pairs += [(2 * chip + core, 2 * to + core) for core in range(2)]
        return lax.ppermute(piece, "member", pairs)

    pair = array(2, step, width)
    wide = [pltpu.VMEM((rows + 2, step, width), F32), pltpu.VMEM((rows, 8, width), F32)]
    args = [info, init_field, flow_fields, emission[None, :]]
    inner = call(inner_kernel, "inner", [pair] * chips, args, wide)
    order = [s for near in range(chips // 2, 0, -1) for s in sorted({near, chips - near})]
    got_inner = {s: along(inner[s], s, False) for s in order}
    outer = call(edge_kernel, "edge", [pair] * chips, args + [before, after], wide)
    got_outer = {s: along(outer[s], s, True) for s in order}
    pieces_in = [inner[0]] + [got_inner[s] for s in range(1, chips)]
    pieces_in += [outer[0]] + [got_outer[s] for s in range(1, chips)]
    half_row = array(chips, step, width)
    near, first, second = call(
        collect_kernel, "collect", [array(2, chips, step, width), half_row, half_row], [info] + pieces_in
    )

    def device(p, chip, core):
        return p * lanes + 2 * chip + core

    first_pairs, second_pairs, siblings = [], [], []
    for p in range(patches):
        for chip in range(chips):
            siblings += [(device(p, chip, core), device(p, chip, 1 - core)) for core in range(2)]
            for core, away in ((0, 1), (1, -1)):
                if 0 <= chip + away < chips:
                    to_first, to_second = device(p, chip + away, core), device(p, chip + away, core)
                    to = p
                else:
                    to = p + 1 if (p % 2 == 0) == (away == 1) else p - 1
                    if not 0 <= to < patches:
                        continue
                    to_first = to_second = device(to, chip, 1 - core)
                first_pairs.append((device(p, chip, core), to_first))
                second_pairs.append((device(p, chip, 1 - core), to_second))
    got_first = lax.ppermute(first, axes, first_pairs)
    got_second = lax.ppermute(second, axes, second_pairs)
    far = lax.ppermute(near, axes, siblings)

    analysed = call(
        region_kernel, "region", array(lanes, step, width),
        [info, mine, other, near, far, got_first, got_second],
        [
            pltpu.VMEM((members, 3 * width), BF16),
            pltpu.VMEM((members, 3 * width), BF16),
            pltpu.VMEM((members, slots), BF16),
            pltpu.VMEM((members, slots), BF16),
            pltpu.VMEM((slots, slots), F32),
            pltpu.VMEM((slots, width), F32),
        ],
    )
    returned = lax.all_to_all(analysed, "member", split_axis=0, concat_axis=0, tiled=True)
    return call(unpack_kernel, "unpack", array(step, rows, width), [info, returned])


def solution(mesh):
    return jax.shard_map(
        per_device,
        mesh=mesh,
        in_specs=(
            P("member", "patch", None),
            P(None, "patch", None),
            P("member"),
            P(("patch", "member"), None),
            P(("patch", "member")),
            P(("patch", "member"), None),
            P(("patch", "member"), None),
        ),
        out_specs=P("member", "patch", None),
        check_vma=False,
    )
```

time: 122 us -> 116 us (0.951)
  the two profiles are of different devices: /device:TPU:0 before, /device:TPU:2 now
where the time goes in v3:
time: 116 us; the launch traced here: 115 us
  blocking collectives  29 us (25%)
  starting transfers between devices  28.8 us (25%)
  Pallas kernels  27 us (23%)
  waiting for transfers between devices  26.1 us (22%)
  local copies, waits for them, and re-layouts  3.36 us (3%)
    all_to_all x1, blocking collectives, per_device(): lax.all_to_all(analysed, 'member', split_axis=0, concat_axis=0, tiled=True)  29 us
    pallas_call x5, Pallas kernels, call(): pl.pallas_call(kernel, out_shape=out_shape, in_specs=[SMEM] + [VMEM] * (l...  26.8 us
    ppermute x6, waiting for transfers between devices, along(): return lax.ppermute(piece, 'member', pairs)  16.2 us
    ppermute x6, starting transfers between devices, along(): return lax.ppermute(piece, 'member', pairs)  15.4 us
    ppermute x1, waiting for transfers between devices, per_device(): lax.ppermute(mine, axes, [(p * lanes + i, p * lanes + lanes - 1 - i) for...  5.05 us
    ppermute x1, starting transfers between devices, per_device(): got_second = lax.ppermute(second, axes, second_pairs)  3.59 us
    ppermute x1, starting transfers between devices, per_device(): lax.ppermute(tail, 'patch', [(i, i + 1) for i in range(patches - 1)])  3.53 us
    unnamed x16, local copies, waits for them, and re-layouts  3.32 us
  transfers between devices with their start and end apart: 12, of which 7 were waited for; matrix products, arithmetic and copies ran while one was open for 0% of the time, Pallas kernels for 4%

profile of v3, /device:TPU:2, one launch (start us, length us, event | category | flops | bytes accessed | tf_op | source)
XLA Modules:
  0.0 115.2 jit_solution(5880427118884685761)
XLA Ops:
  0.0 0.0 copy-start
  0.0 1.2 %copy-done = f32[128,8,256]{2,1,0:T(8,128)S(1)} copy-done((f32[128,8,256]{2,1,0:T(8,128)S(1)}, f32[128,8,256]{2,1,0:T(8,128)}, u32[]{:S(2)}) %copy-start) | copy-done | bytes 1048600
  1.2 0.0 copy-start.2
  1.2 0.8 copy-done.2
  2.0 0.0 copy-start.1
  2.0 0.2 pack.1
  2.2 3.5 %collective-permute-start.4 = (f32[264,256]{1,0:T(8,128)S(1)}, f32[264,256]{1,0:T(8,128)S(1)}, u32[]{:S(2)}, u32[]{:S(2)}) collective-permute-start(f32[264,256]{1,0:T(8,128)S(1)} %get-tuple-element.22), channel_id=1, source_target_pairs={{0,8},{8,16},{16,24},{1,9},{9,17},{17,25},{2,10},{10,18},{18,26},{... | collective-permute-start | bytes 811016 | tf_op jit(solution)/shard_map/ppermute | solution.py:325
  5.7 2.5 %collective-permute-start.5 = (f32[264,256]{1,0:T(8,128)S(1)}, f32[264,256]{1,0:T(8,128)S(1)}, u32[]{:S(2)}, u32[]{:S(2)}) collective-permute-start(f32[264,256]{1,0:T(8,128)S(1)} %get-tuple-element.23), channel_id=1, source_target_pairs={{8,0},{16,8},{24,16},{9,1},{17,9},{25,17},{10,2},{18,10},{26,18},{... | collective-permute-start | bytes 811016 | tf_op jit(solution)/shard_map/ppermute | solution.py:326
  8.2 0.0 copy-start.3
  8.2 0.1 pad_add_fusion.info_ref
  8.3 0.0 copy-start.4
  8.3 0.0 copy-done.1
  8.3 0.6 copy-done.3
  8.9 0.0 copy-done.4
  8.9 2.1 %inner.1 = (f32[2,128,256]{2,1,0:T(8,128)S(1)}, f32[2,128,256]{2,1,0:T(8,128)S(1)}, f32[2,128,256]{2,1,0:T(8,128)S(1)}, f32[2,128,256]{2,1,0:T(8,128)S(1)}) custom-call(s32[3]{0:T(128)S(1)} %pad_add_fusion.info_ref, f32[128,8,256]{2,1,0:T(8,128)S(1)} %copy-done.1, f32[4,8,256]{2,1,0:T(8,128)S(1)} %copy-done.3, f32[1,128]{1,0:T(1,128)S(1)} %bitcast.5), custom_call_target="tpu_custom_call" | custom-call | tf_op jit(solution)/shard_map/inner/pallas_call | solution.py:292
  11.1 3.5 %collective-permute-start.1 = (f32[2,128,256]{2,1,0:T(8,128)S(1)}, f32[2,128,256]{2,1,0:T(8,128)S(1)}, u32[]{:S(2)}, u32[]{:S(2)}) collective-permute-start(f32[2,128,256]{2,1,0:T(8,128)S(1)} %get-tuple-element.19), channel_id=1, source_target_pairs={{0,2},{1,3},{2,4},{3,5},{8,10},{9,11},{10,12},{11,13},{16,18},{17,... | collective-permute-start | bytes 786440 | tf_op jit(solution)/shard_map/ppermute | solution.py:349
  14.6 2.3 %collective-permute-start.2 = (f32[2,128,256]{2,1,0:T(8,128)S(1)}, f32[2,128,256]{2,1,0:T(8,128)S(1)}, u32[]{:S(2)}, u32[]{:S(2)}) collective-permute-start(f32[2,128,256]{2,1,0:T(8,128)S(1)} %get-tuple-element.20), channel_id=1, source_target_pairs={{0,4},{1,5},{6,2},{7,3},{8,12},{9,13},{14,10},{15,11},{16,20},{17,... | collective-permute-start | bytes 786440 | tf_op jit(solution)/shard_map/ppermute | solution.py:349
  16.9 0.7 collective-permute-start.3
  17.6 0.0 collective-permute-done.4.before_ref
  17.6 1.6 %collective-permute-done.5.after_ref = f32[264,256]{1,0:T(8,128)S(1)} collective-permute-done((f32[264,256]{1,0:T(8,128)S(1)}, f32[264,256]{1,0:T(8,128)S(1)}, u32[]{:S(2)}, u32[]{:S(2)}) %collective-permute-start.5) | collective-permute-done | bytes 270368 | tf_op jit(solution)/shard_map/ppermute | solution.py:326
  19.2 2.3 %edge.1 = (f32[2,128,256]{2,1,0:T(8,128)S(1)}, f32[2,128,256]{2,1,0:T(8,128)S(1)}, f32[2,128,256]{2,1,0:T(8,128)S(1)}, f32[2,128,256]{2,1,0:T(8,128)S(1)}) custom-call(s32[3]{0:T(128)S(1)} %pad_add_fusion.info_ref, f32[128,8,256]{2,1,0:T(8,128)S(1)} %copy-done.1, f32[4,8,256]{2,1,0:T(8,128)S(1)} %copy-done.3, f32[1,128]{1,0:T(1,128)S(1)} %bitcast.6, ...), custom_call_target="tpu_custom_call" | custom-call | tf_op jit(solution)/shard_map/edge/pallas_call | solution.py:292
  21.5 1.3 %collective-permute-start.6 = (f32[2,128,256]{2,1,0:T(8,128)S(1)}, f32[2,128,256]{2,1,0:T(8,128)S(1)}, u32[]{:S(2)}, u32[]{:S(2)}) collective-permute-start(f32[2,128,256]{2,1,0:T(8,128)S(1)} %get-tuple-element.25), channel_id=1, source_target_pairs={{4,6},{5,7},{6,0},{7,1},{12,14},{13,15},{14,8},{15,9},{20,22},{21,... | collective-permute-start | bytes 786440 | tf_op jit(solution)/shard_map/ppermute | solution.py:349
  22.8 1.3 %collective-permute-start.7 = (f32[2,128,256]{2,1,0:T(8,128)S(1)}, f32[2,128,256]{2,1,0:T(8,128)S(1)}, u32[]{:S(2)}, u32[]{:S(2)}) collective-permute-start(f32[2,128,256]{2,1,0:T(8,128)S(1)} %get-tuple-element.26), channel_id=1, source_target_pairs={{2,6},{3,7},{4,0},{5,1},{10,14},{11,15},{12,8},{13,9},{18,22},{19,... | collective-permute-start | bytes 786440 | tf_op jit(solution)/shard_map/ppermute | solution.py:349
  24.1 0.0 collective-permute-done.1.refs_1_
  24.1 6.3 %collective-permute-start.8 = (f32[2,128,256]{2,1,0:T(8,128)S(1)}, f32[2,128,256]{2,1,0:T(8,128)S(1)}, u32[]{:S(2)}, u32[]{:S(2)}) collective-permute-start(f32[2,128,256]{2,1,0:T(8,128)S(1)} %get-tuple-element.27), channel_id=1, source_target_pairs={{0,6},{1,7},{2,0},{3,1},{8,14},{9,15},{10,8},{11,9},{16,22},{17,23... | collective-permute-start | bytes 786440 | tf_op jit(solution)/shard_map/ppermute | solution.py:349
  30.4 0.0 collective-permute-done.2.refs_2_
  30.4 0.0 collective-permute-done.3.refs_3_
  30.4 6.6 %collective-permute-done.6.refs_5_ = f32[2,128,256]{2,1,0:T(8,128)S(1)} collective-permute-done((f32[2,128,256]{2,1,0:T(8,128)S(1)}, f32[2,128,256]{2,1,0:T(8,128)S(1)}, u32[]{:S(2)}, u32[]{:S(2)}) %collective-permute-start.6) | collective-permute-done | bytes 262176 | tf_op jit(solution)/shard_map/ppermute | solution.py:349
  37.0 5.5 %collective-permute-done.7.refs_6_ = f32[2,128,256]{2,1,0:T(8,128)S(1)} collective-permute-done((f32[2,128,256]{2,1,0:T(8,128)S(1)}, f32[2,128,256]{2,1,0:T(8,128)S(1)}, u32[]{:S(2)}, u32[]{:S(2)}) %collective-permute-start.7) | collective-permute-done | bytes 262176 | tf_op jit(solution)/shard_map/ppermute | solution.py:349
  42.5 4.1 %collective-permute-done.8.refs_7_ = f32[2,128,256]{2,1,0:T(8,128)S(1)} collective-permute-done((f32[2,128,256]{2,1,0:T(8,128)S(1)}, f32[2,128,256]{2,1,0:T(8,128)S(1)}, u32[]{:S(2)}, u32[]{:S(2)}) %collective-permute-start.8) | collective-permute-done | bytes 262176 | tf_op jit(solution)/shard_map/ppermute | solution.py:349
  46.6 1.7 %collect.1 = (f32[2,4,128,256]{3,2,1,0:T(8,128)S(1)}, f32[4,128,256]{2,1,0:T(8,128)}, f32[4,128,256]{2,1,0:T(8,128)}) custom-call(s32[3]{0:T(128)S(1)} %pad_add_fusion.info_ref, f32[2,128,256]{2,1,0:T(8,128)S(1)} %get-tuple-element.18.refs_0_, f32[2,128,256]{2,1,0:T(8,128)S(1)} %collective-permute-done.1.refs_1_, ...), custom_call_target="tpu_custom_call" | custom-call | tf_op jit(solution)/shard_map/collect/pallas_call | solution.py:292
  48.3 0.0 collective-permute-start.9
  48.3 1.9 %collective-permute-start.10 = (f32[4,128,256]{2,1,0:T(8,128)}, f32[4,128,256]{2,1,0:T(8,128)S(1)}, u32[]{:S(2)}, u32[]{:S(2)}) collective-permute-start(f32[4,128,256]{2,1,0:T(8,128)} %get-tuple-element.29), channel_id=1, source_target_pairs={{0,2},{2,4},{3,1},{4,6},{5,3},{6,15},{7,5},{8,10},{9,16},{10,12},{... | collective-permute-start | bytes 1572872 | tf_op jit(solution)/shard_map/ppermute | solution.py:384
  50.2 0.0 copy-start.7
  50.2 3.6 %collective-permute-start.11 = (f32[4,128,256]{2,1,0:T(8,128)}, f32[4,128,256]{2,1,0:T(8,128)S(1)}, u32[]{:S(2)}, u32[]{:S(2)}) collective-permute-start(f32[4,128,256]{2,1,0:T(8,128)} %get-tuple-element.30), channel_id=1, source_target_pairs={{1,2},{3,4},{2,1},{5,6},{4,3},{7,15},{6,5},{9,10},{8,16},{11,12},{... | collective-permute-start | bytes 1572872 | tf_op jit(solution)/shard_map/ppermute | solution.py:385
  54.5 0.0 copy-done.7
  54.5 0.0 copy-start.5
  54.5 0.0 copy-start.6
  54.5 0.6 copy-done.5
  55.2 0.0 copy-done.6
  55.2 1.9 %collective-permute-start = (f32[8,512]{1,0:T(8,128)S(1)}, f32[8,512]{1,0:T(8,128)S(1)}, u32[]{:S(2)}, u32[]{:S(2)}) collective-permute-start(f32[8,512]{1,0:T(8,128)S(1)} %concatenate.3.mine_ref), channel_id=1, source_target_pairs={{8,15},{9,14},{10,13},{11,12},{12,11},{13,10},{14,9},{15,8},{24,31... | collective-permute-start | bytes 49160 | tf_op jit(solution)/shard_map/ppermute | solution.py:338
  57.2 5.0 %collective-permute-done.other_ref = f32[8,512]{1,0:T(8,128)S(1)} collective-permute-done((f32[8,512]{1,0:T(8,128)S(1)}, f32[8,512]{1,0:T(8,128)S(1)}, u32[]{:S(2)}, u32[]{:S(2)}) %collective-permute-start) | collective-permute-done | bytes 16416 | tf_op jit(solution)/shard_map/ppermute | solution.py:338
  62.2 0.7 collective-permute-done.10.first_ref
  62.9 2.6 %collective-permute-done.11.second_ref = f32[4,128,256]{2,1,0:T(8,128)S(1)} collective-permute-done((f32[4,128,256]{2,1,0:T(8,128)}, f32[4,128,256]{2,1,0:T(8,128)S(1)}, u32[]{:S(2)}, u32[]{:S(2)}) %collective-permute-start.11) | collective-permute-done | bytes 524320 | tf_op jit(solution)/shard_map/ppermute | solution.py:385
  65.5 0.0 collective-permute-done.9.far_ref
  65.5 18.9 %region.1 = f32[8,128,256]{2,1,0:T(8,128)S(1)} custom-call(s32[3]{0:T(128)S(1)} %pad_add_fusion.info_ref, f32[8,512]{1,0:T(8,128)S(1)} %concatenate.3.mine_ref, f32[8,512]{1,0:T(8,128)S(1)} %collective-permute-done.other_ref, f32[2,4,128,256]{3,2,1,0:T(8,128)S(1)} %get-tuple-element.28.near_ref, f32[2,4,128,256]{3,2,1,0:T(8,128)S(1)} %collective-permute-done.9.far_ref, ...), custom_call_target="tpu_custom_call" | custom-call | tf_op jit(solution)/shard_map/region/pallas_call | solution.py:292
  84.4 29.0 %all_to_all.5.rows_ref = f32[8,128,256]{2,1,0:T(8,128)S(1)} all-to-all(f32[8,128,256]{2,1,0:T(8,128)S(1)} %region.1), channel_id=1, replica_groups=mesh['patch'=4,'member'=8] {'member'}, dimensions={0} | all-to-all | bytes 2097152 | tf_op jit(solution)/shard_map/all_to_all | solution.py:400
  113.4 1.9 %unpack.1 = f32[128,8,256]{2,1,0:T(8,128)} custom-call(s32[3]{0:T(128)S(1)} %pad_add_fusion.info_ref, f32[8,128,256]{2,1,0:T(8,128)S(1)} %all_to_all.5.rows_ref), custom_call_target="tpu_custom_call" | custom-call | tf_op jit(solution)/shard_map/unpack/pallas_call | solution.py:292
  (3 shorter events, 0.0 us)
Async XLA Ops:
  0.0 1.2 %copy-start = (f32[128,8,256]{2,1,0:T(8,128)S(1)}, f32[128,8,256]{2,1,0:T(8,128)}, u32[]{:S(2)}) copy-start(f32[128,8,256]{2,1,0:T(8,128)} %field_ref.5) | copy-start | bytes 3145732
  1.2 0.8 copy-start.2
  2.0 6.3 %copy-start.1 = (f32[128,8,256]{2,1,0:T(8,128)S(1)}, f32[128,8,256]{2,1,0:T(8,128)}, u32[]{:S(2)}) copy-start(f32[128,8,256]{2,1,0:T(8,128)} %field_ref.5) | copy-start | bytes 3145732
  2.2 15.4 %collective-permute-start.4 = (f32[264,256]{1,0:T(8,128)S(1)}, f32[264,256]{1,0:T(8,128)S(1)}, u32[]{:S(2)}, u32[]{:S(2)}) collective-permute-start(f32[264,256]{1,0:T(8,128)S(1)} %get-tuple-element.22), channel_id=1, source_target_pairs={{0,8},{8,16},{16,24},{1,9},{9,17},{17,25},{2,10},{10,18},{18,26},{... | collective-permute-start | bytes 811016 | tf_op jit(solution)/shard_map/ppermute | solution.py:325
  5.7 13.5 %collective-permute-start.5 = (f32[264,256]{1,0:T(8,128)S(1)}, f32[264,256]{1,0:T(8,128)S(1)}, u32[]{:S(2)}, u32[]{:S(2)}) collective-permute-start(f32[264,256]{1,0:T(8,128)S(1)} %get-tuple-element.23), channel_id=1, source_target_pairs={{8,0},{16,8},{24,16},{9,1},{17,9},{25,17},{10,2},{18,10},{26,18},{... | collective-permute-start | bytes 811016 | tf_op jit(solution)/shard_map/ppermute | solution.py:326
  8.2 0.8 copy-start.3
  8.3 0.7 copy-start.4
  11.1 13.0 %collective-permute-start.1 = (f32[2,128,256]{2,1,0:T(8,128)S(1)}, f32[2,128,256]{2,1,0:T(8,128)S(1)}, u32[]{:S(2)}, u32[]{:S(2)}) collective-permute-start(f32[2,128,256]{2,1,0:T(8,128)S(1)} %get-tuple-element.19), channel_id=1, source_target_pairs={{0,2},{1,3},{2,4},{3,5},{8,10},{9,11},{10,12},{11,13},{16,18},{17,... | collective-permute-start | bytes 786440 | tf_op jit(solution)/shard_map/ppermute | solution.py:349
  14.6 15.9 %collective-permute-start.2 = (f32[2,128,256]{2,1,0:T(8,128)S(1)}, f32[2,128,256]{2,1,0:T(8,128)S(1)}, u32[]{:S(2)}, u32[]{:S(2)}) collective-permute-start(f32[2,128,256]{2,1,0:T(8,128)S(1)} %get-tuple-element.20), channel_id=1, source_target_pairs={{0,4},{1,5},{6,2},{7,3},{8,12},{9,13},{14,10},{15,11},{16,20},{17,... | collective-permute-start | bytes 786440 | tf_op jit(solution)/shard_map/ppermute | solution.py:349
  16.9 13.6 %collective-permute-start.3 = (f32[2,128,256]{2,1,0:T(8,128)S(1)}, f32[2,128,256]{2,1,0:T(8,128)S(1)}, u32[]{:S(2)}, u32[]{:S(2)}) collective-permute-start(f32[2,128,256]{2,1,0:T(8,128)S(1)} %get-tuple-element.21), channel_id=1, source_target_pairs={{4,2},{5,3},{6,4},{7,5},{12,10},{13,11},{14,12},{15,13},{20,18},{2... | collective-permute-start | bytes 786440 | tf_op jit(solution)/shard_map/ppermute | solution.py:349
  21.5 15.5 %collective-permute-start.6 = (f32[2,128,256]{2,1,0:T(8,128)S(1)}, f32[2,128,256]{2,1,0:T(8,128)S(1)}, u32[]{:S(2)}, u32[]{:S(2)}) collective-permute-start(f32[2,128,256]{2,1,0:T(8,128)S(1)} %get-tuple-element.25), channel_id=1, source_target_pairs={{4,6},{5,7},{6,0},{7,1},{12,14},{13,15},{14,8},{15,9},{20,22},{21,... | collective-permute-start | bytes 786440 | tf_op jit(solution)/shard_map/ppermute | solution.py:349
  22.8 19.7 %collective-permute-start.7 = (f32[2,128,256]{2,1,0:T(8,128)S(1)}, f32[2,128,256]{2,1,0:T(8,128)S(1)}, u32[]{:S(2)}, u32[]{:S(2)}) collective-permute-start(f32[2,128,256]{2,1,0:T(8,128)S(1)} %get-tuple-element.26), channel_id=1, source_target_pairs={{2,6},{3,7},{4,0},{5,1},{10,14},{11,15},{12,8},{13,9},{18,22},{19,... | collective-permute-start | bytes 786440 | tf_op jit(solution)/shard_map/ppermute | solution.py:349
  24.1 22.5 %collective-permute-start.8 = (f32[2,128,256]{2,1,0:T(8,128)S(1)}, f32[2,128,256]{2,1,0:T(8,128)S(1)}, u32[]{:S(2)}, u32[]{:S(2)}) collective-permute-start(f32[2,128,256]{2,1,0:T(8,128)S(1)} %get-tuple-element.27), channel_id=1, source_target_pairs={{0,6},{1,7},{2,0},{3,1},{8,14},{9,15},{10,8},{11,9},{16,22},{17,23... | collective-permute-start | bytes 786440 | tf_op jit(solution)/shard_map/ppermute | solution.py:349
  48.3 17.2 %collective-permute-start.9 = (f32[2,4,128,256]{3,2,1,0:T(8,128)S(1)}, f32[2,4,128,256]{3,2,1,0:T(8,128)S(1)}, u32[]{:S(2)}, u32[]{:S(2)}) collective-permute-start(f32[2,4,128,256]{3,2,1,0:T(8,128)S(1)} %get-tuple-element.28.near_ref), channel_id=1, source_target_pairs={{0,1},{1,0},{2,3},{3,2},{4,5},{5,4},{6,7},{7,6},{8,9},{9,8},{10,11... | collective-permute-start | bytes 3145736 | tf_op jit(solution)/shard_map/ppermute | solution.py:386
  48.3 14.6 %collective-permute-start.10 = (f32[4,128,256]{2,1,0:T(8,128)}, f32[4,128,256]{2,1,0:T(8,128)S(1)}, u32[]{:S(2)}, u32[]{:S(2)}) collective-permute-start(f32[4,128,256]{2,1,0:T(8,128)} %get-tuple-element.29), channel_id=1, source_target_pairs={{0,2},{2,4},{3,1},{4,6},{5,3},{6,15},{7,5},{8,10},{9,16},{10,12},{... | collective-permute-start | bytes 1572872 | tf_op jit(solution)/shard_map/ppermute | solution.py:384
  50.2 4.3 %copy-start.7 = (s32[1,512]{1,0:T(1,128)S(1)}, s32[1,512]{1,0:T(1,128)}, u32[]{:S(2)}) copy-start(s32[1,512]{1,0:T(1,128)} %param.10) | copy-start | bytes 6148
  50.2 15.3 %collective-permute-start.11 = (f32[4,128,256]{2,1,0:T(8,128)}, f32[4,128,256]{2,1,0:T(8,128)S(1)}, u32[]{:S(2)}, u32[]{:S(2)}) collective-permute-start(f32[4,128,256]{2,1,0:T(8,128)} %get-tuple-element.30), channel_id=1, source_target_pairs={{1,2},{3,4},{2,1},{5,6},{4,3},{7,15},{6,5},{9,10},{8,16},{11,12},{... | collective-permute-start | bytes 1572872 | tf_op jit(solution)/shard_map/ppermute | solution.py:385
  54.5 0.7 copy-start.5
  54.5 0.7 copy-start.6
  55.2 7.0 %collective-permute-start = (f32[8,512]{1,0:T(8,128)S(1)}, f32[8,512]{1,0:T(8,128)S(1)}, u32[]{:S(2)}, u32[]{:S(2)}) collective-permute-start(f32[8,512]{1,0:T(8,128)S(1)} %concatenate.3.mine_ref), channel_id=1, source_target_pairs={{8,15},{9,14},{10,13},{11,12},{12,11},{13,10},{14,9},{15,8},{24,31... | collective-permute-start | bytes 49160 | tf_op jit(solution)/shard_map/ppermute | solution.py:338

commit v4 on v3

--- a/solution.py
+++ b/solution.py
@@ -10,7 +10,7 @@
 
 STEPS = 2
 COARSE = 0.06
-DONE = 1e-4
+DONE = 0.01
 LARGE = 2e4
 PART = 256
 F32 = jnp.float32
@@ -122,9 +122,10 @@
     second_step(info_ref, wanted, 1, emission, wide_ref, weight_ref, out_refs)
 
 
-def collect_kernel(info_ref, *refs):
-    chips = (len(refs) - 3) // 2
-    both_ref, first_ref, second_ref = refs[-3:]
+def collect_kernel(info_ref, mine_ref, other_ref, *refs):
+    chips = (len(refs) - 4) // 2
+    both_ref, first_ref, second_ref, observed_ref = refs[-4:]
+    observed_ref[...] = jnp.where(info_ref[2] == 1, other_ref[...], mine_ref[...])
     chip, core = info_ref[0], info_ref[1]
     at_edge = jnp.logical_or(chip == 0, chip == chips - 1)
     for s in range(chips):
@@ -173,59 +174,59 @@
     return total
 
 
-def region_kernel(
-    info_ref, mine_ref, other_ref, near_ref, far_ref, first_ref, second_ref, out_ref,
-    high_ref, low_ref, spread_high, spread_low, factor, answer,
-):
-    _, chips, step, width = near_ref.shape
-    half_of = chips * step
-    members = 2 * half_of
-    slots = mine_ref.shape[1]
-    root = math.sqrt(members - 1)
-    core, turned = info_ref[1], info_ref[2] == 1
-    swapped = jnp.logical_or(
-        jnp.logical_and(info_ref[0] == 0, core == 0), jnp.logical_and(info_ref[0] == chips - 1, core == 1)
-    )
-
-    observed = jnp.where(turned, other_ref[...], mine_ref[...])
-    cells, values, scales, count = (observed[i : i + 1] for i in range(4))
+def observations(info_ref, observed_ref, width, root):
+    slots = observed_ref.shape[1]
+    cells, values, scales, count = (observed_ref[pl.ds(i, 1), :] for i in range(4))
     cells = cells.astype(jnp.int32)
     offset = sum((cells >= i * width).astype(jnp.int32) for i in (1, 2)) - 1
     column = cells - (offset + 1) * width
-    side = offset * jnp.where(turned, -1, 1) * (1 - 2 * core)
+    side = offset * jnp.where(info_ref[2] == 1, -1, 1) * (1 - 2 * info_ref[1])
     cells = column + width * jnp.where(side == 0, 2, jnp.where(side < 0, 0, 1))
-
-    def block_of(place, part, chip):
-        if place == 0:
-            pair = (first_ref[chip], second_ref[chip])
-            return jnp.where(swapped, pair[1 - part], pair[part])
-        if part == 0:
-            return near_ref[place - 1, chip]
-        return far_ref[2 - place, chip]
-
-    blocks = [(part, chip) for part in range(2) for chip in range(chips)]
-    means = []
-    for place in range(3):
-        total = None
-        for part, chip in blocks:
-            block = block_of(place, part, chip)
-            total = block if total is None else total + block
-        mean = jnp.sum(total, axis=0, keepdims=True) * (1.0 / members)
-        means.append(mean)
-        for index, (part, chip) in enumerate(blocks):
-            at = (pl.ds(index * step, step), pl.ds(place * width, width))
-            high, low = pieces(block_of(place, part, chip) - mean, 2)
-            high_ref[at] = high
-            low_ref[at] = low
-    chosen = (
-        lax.broadcasted_iota(jnp.int32, (3 * width, slots), 0) == cells
-    ).astype(F32).astype(BF16)
     active = lax.broadcasted_iota(jnp.int32, (1, slots), 1) < count.astype(jnp.int32)
     slot_weight = jnp.where(active, scales, 0.0)
-    scale = slot_weight * (1.0 / root)
-    mean_parts = pieces(jnp.broadcast_to(jnp.concatenate(means, axis=1), (8, 3 * width)), 3)
-    predicted_mean = (dot(mean_parts[0], chosen) + (dot(mean_parts[1], chosen) + dot(mean_parts[2], chosen)))[:1]
-    innovation = slot_weight * (values - predicted_mean)
+    return cells, slot_weight, values, slot_weight * (1.0 / root)
+
+
+def one_hot(cells, first, count):
+    return (
+        lax.broadcasted_iota(jnp.int32, (count, cells.shape[1]), 0) + first == cells
+    ).astype(F32).astype(BF16)
+
+
+def mean_of(blocks, members):
+    total = blocks[0]
+    for block in blocks[1:]:
+        total = total + block
+    return jnp.sum(total, axis=0, keepdims=True) * (1.0 / members)
+
+
+def at_cells(row, chosen):
+    parts = pieces(jnp.broadcast_to(row, (8, row.shape[1])), 3)
+    return (dot(parts[0], chosen) + (dot(parts[1], chosen) + dot(parts[2], chosen)))[:1]
+
+
+def prepare_kernel(
+    info_ref, observed_ref, near_ref, far_ref,
+    spread_high, spread_low, own_high, own_low, mean_ref, high_ref, low_ref,
+):
+    _, chips, step, width = near_ref.shape
+    members = 2 * chips * step
+    cells, _, _, scale = observations(info_ref, observed_ref, width, math.sqrt(members - 1))
+    chosen = one_hot(cells, width, 2 * width)
+    means = []
+    for place in range(2):
+        blocks = [near_ref[place, chip] for chip in range(chips)] + [far_ref[1 - place, chip] for chip in range(chips)]
+        means.append(mean_of(blocks, members))
+        for index in range(2 * chips):
+            block = near_ref[place, index] if index < chips else far_ref[1 - place, index - chips]
+            rows = pl.ds(index * step, step)
+            high, low = pieces(block - means[-1], 2)
+            high_ref[rows, pl.ds(place * width, width)] = high
+            low_ref[rows, pl.ds(place * width, width)] = low
+            if place == 1:
+                own_high[rows, :] = high
+                own_low[rows, :] = low
+    mean_ref[...] = jnp.broadcast_to(at_cells(jnp.concatenate(means, axis=1), chosen), mean_ref.shape)
     for first in range(0, members, PART):
         rows = pl.ds(first, PART)
         spread = (dot(high_ref[rows, :], chosen) + dot(low_ref[rows, :], chosen)) * scale
@@ -233,31 +234,75 @@
         spread_high[rows, :] = high
         spread_low[rows, :] = low
 
+
+def square(parts):
+    half = parts[0].shape[0] // 2
+    upper = product([part[:half] for part in parts], parts)
+    lower = product([part[half:] for part in parts], [part[:, half:] for part in parts])
+    return upper, jnp.concatenate([upper[:, half:].T, lower], axis=1)
+
+
+def region_kernel(
+    info_ref, observed_ref, near_ref, far_ref, high_in, low_in, own_high, own_low, mean_ref, first_ref, second_ref,
+    out_ref, spread_high, spread_low, factor, answer,
+):
+    _, chips, step, width = near_ref.shape
+    members = 2 * chips * step
+    slots = observed_ref.shape[1]
+    root = math.sqrt(members - 1)
+    core = info_ref[1]
+    swapped = jnp.logical_or(
+        jnp.logical_and(info_ref[0] == 0, core == 0), jnp.logical_and(info_ref[0] == chips - 1, core == 1)
+    )
+    cells, slot_weight, values, scale = observations(info_ref, observed_ref, width, root)
+    chosen = one_hot(cells, 0, width)
+
+    def outer_block(index):
+        pair = (first_ref[index % chips], second_ref[index % chips])
+        part = index // chips
+        return jnp.where(swapped, pair[1 - part], pair[part])
+
+    mean = mean_of([ref[chip] for ref in (first_ref, second_ref) for chip in range(chips)], members)
+    innovation = slot_weight * (values - (mean_ref[pl.ds(0, 1), :] + at_cells(mean, chosen)))
+    for index in range(2 * chips):
+        rows = pl.ds(index * step, step)
+        high, low = pieces(outer_block(index) - mean, 2)
+        high, low = pieces((dot(high, chosen) + dot(low, chosen)) * scale, 2)
+        spread_high[rows, :] = high + high_in[rows, :]
+        spread_low[rows, :] = low + low_in[rows, :]
+
     high, low = spread_high[...], spread_low[...]
-    middle = pl.ds(2 * width, width)
     eye = lax.broadcasted_iota(jnp.int32, (slots, slots), 0) == lax.broadcasted_iota(
         jnp.int32, (slots, slots), 1
     )
     cross = dot_t(high, low)
     matrix = dot_t(high, high) + (cross + cross.T) + jnp.where(eye, 1.0, 0.0)
-    right = dot_t(high, high_ref[:, middle]) + (dot_t(high, low_ref[:, middle]) + dot_t(low, high_ref[:, middle]))
+    right = dot_t(high, own_high[...]) + (dot_t(high, own_low[...]) + dot_t(low, own_high[...]))
 
     norm = jnp.max(jnp.sum(jnp.abs(matrix), axis=0, keepdims=True))
     start = 2.0 / (1.0 + norm)
     factor[...] = matrix * start
     answer[...] = right * start
+    half = slots // 2
+    upper, lower = pl.ds(0, half), pl.ds(half, half)
 
     def refine(bound, count):
         gain = 2.0 / (2.0 - bound * bound)
         parts = pieces(factor[...], count)
         answer[...] = gain * (2.0 * answer[...] - product(parts, pieces(answer[...], count)))
-        factor[...] = gain * (2.0 * factor[...] - product(parts, parts))
+        top, bottom = square(parts)
+        factor[upper, :] = gain * (2.0 * factor[upper, :] - top)
+        factor[lower, :] = gain * (2.0 * factor[lower, :] - bottom)
         return bound * bound / (2.0 - bound * bound)
 
+    def close(bound, rest):
+        gain = 2.0 / (2.0 - bound * bound)
+        answer[...] = gain * (answer[...] + dot(rest, answer[...].astype(BF16)))
+        return gain
+
     def finish(bound):
-        gain = 2.0 / (2.0 - bound * bound)
         rest = factor[...].astype(BF16)
-        answer[...] = gain * (answer[...] + dot(rest, answer[...].astype(BF16)))
+        gain = close(bound, rest)
         factor[...] = gain * (dot(rest, rest) - jnp.where(eye, 0.5 * bound * bound, 0.0))
         return bound * bound / (2.0 - bound * bound)
 
@@ -267,27 +312,29 @@
     )
     bound = lax.while_loop(lambda b: b > COARSE, lambda b: refine(b, 2), bound)
     factor[...] = jnp.where(eye, 1.0, 0.0) - factor[...]
-    lax.while_loop(lambda b: b > DONE, finish, bound)
+    bound = lax.while_loop(lambda b: b > DONE, finish, bound)
+    close(bound, factor[...].astype(BF16))
 
     solved = answer[...]
     solved_parts = pieces(solved, 2)
     innovation_parts = pieces(jnp.broadcast_to(innovation * (1.0 / root), (8, slots)), 3)
     shift = product(innovation_parts, pieces(solved, 3))[:1]
-    half = [part * jnp.asarray(-0.5, BF16) for part in solved_parts]
-    for index, (part, chip) in enumerate(blocks):
-        rows = pl.ds(index * step, step)
-        moved = product([spread_high[rows, :], spread_low[rows, :]], half)
-        out_ref[2 * chip + jnp.abs(core - part)] = block_of(2, part, chip) + shift + moved
+    halved = [part * jnp.asarray(-0.5, BF16) for part in solved_parts]
+    for part, ref, place in ((0, near_ref, 1), (1, far_ref, 0)):
+        for chip in range(chips):
+            rows = pl.ds((part * chips + chip) * step, step)
+            moved = product([spread_high[rows, :], spread_low[rows, :]], halved)
+            out_ref[2 * chip + jnp.abs(core - part)] = ref[place, chip] + shift + moved
 
 
 VMEM = pl.BlockSpec(memory_space=pltpu.VMEM)
-LIMIT = pltpu.CompilerParams(vmem_limit_bytes=48 * 1024 * 1024)
+LIMIT = pltpu.CompilerParams(vmem_limit_bytes=32 * 1024 * 1024)
 
 
 SMEM = pl.BlockSpec(memory_space=pltpu.SMEM)
 
 
-def call(kernel, name, out_shape, args, scratch=()):
+def call(kernel, name, out_shape, args, scratch=(), flops=None):
     several = isinstance(out_shape, (list, tuple))
     return pl.pallas_call(
         kernel,
@@ -296,8 +343,13 @@
         out_specs=[VMEM] * len(out_shape) if several else VMEM,
         scratch_shapes=scratch,
         compiler_params=LIMIT,
+        cost_estimate=flops and pl.CostEstimate(flops=flops, bytes_accessed=0, transcendentals=0),
         name=name,
     )(*args)
+
+
+def bfloat(*shape):
+    return jax.ShapeDtypeStruct(shape, BF16)
 
 
 def array(*shape):
@@ -335,10 +387,6 @@
         * 2,
         axis=0,
     )
-    other = lax.ppermute(
-        mine, axes,
-        [(p * lanes + i, p * lanes + lanes - 1 - i) for p in range(1, patches, 2) for i in range(lanes)],
-    )
 
     def along(piece, s, ends):
         pairs = []
@@ -355,12 +403,18 @@
     order = [s for near in range(chips // 2, 0, -1) for s in sorted({near, chips - near})]
     got_inner = {s: along(inner[s], s, False) for s in order}
     outer = call(edge_kernel, "edge", [pair] * chips, args + [before, after], wide)
+    mine, _ = lax.optimization_barrier((mine, outer[0]))
+    other = lax.ppermute(
+        mine, axes,
+        [(p * lanes + i, p * lanes + lanes - 1 - i) for p in range(1, patches, 2) for i in range(lanes)],
+    )
     got_outer = {s: along(outer[s], s, True) for s in order}
     pieces_in = [inner[0]] + [got_inner[s] for s in range(1, chips)]
     pieces_in += [outer[0]] + [got_outer[s] for s in range(1, chips)]
     half_row = array(chips, step, width)
-    near, first, second = call(
-        collect_kernel, "collect", [array(2, chips, step, width), half_row, half_row], [info] + pieces_in
+    near, first, second, observed = call(
+        collect_kernel, "collect", [array(2, chips, step, width), half_row, half_row, array(8, slots)],
+        [info, mine, other] + pieces_in,
     )
 
     def device(p, chip, core):
@@ -381,21 +435,22 @@
                     to_first = to_second = device(to, chip, 1 - core)
                 first_pairs.append((device(p, chip, core), to_first))
                 second_pairs.append((device(p, chip, 1 - core), to_second))
+    far = lax.ppermute(near, axes, siblings)
     got_first = lax.ppermute(first, axes, first_pairs)
     got_second = lax.ppermute(second, axes, second_pairs)
-    far = lax.ppermute(near, axes, siblings)
-
+
+    split = [pltpu.VMEM((members, slots), BF16)] * 2
+    prepared = call(
+        prepare_kernel, "prepare",
+        [bfloat(members, slots)] * 2 + [bfloat(members, width)] * 2 + [array(8, slots)],
+        [info, observed, near, far],
+        [pltpu.VMEM((members, 2 * width), BF16)] * 2,
+        flops=8 * members * slots * width,
+    )
     analysed = call(
         region_kernel, "region", array(lanes, step, width),
-        [info, mine, other, near, far, got_first, got_second],
-        [
-            pltpu.VMEM((members, 3 * width), BF16),
-            pltpu.VMEM((members, 3 * width), BF16),
-            pltpu.VMEM((members, slots), BF16),
-            pltpu.VMEM((members, slots), BF16),
-            pltpu.VMEM((slots, slots), F32),
-            pltpu.VMEM((slots, width), F32),
-        ],
+        [info, observed, near, far, *prepared, got_first, got_second],
+        split + [pltpu.VMEM((slots, slots), F32), pltpu.VMEM((slots, width), F32)],
     )
     returned = lax.all_to_all(analysed, "member", split_axis=0, concat_axis=0, tiled=True)
     return call(unpack_kernel, "unpack", array(step, rows, width), [info, returned])

time: 116 us -> 113 us (0.974)
  the two profiles are of different devices: /device:TPU:2 before, /device:TPU:4 now
where the time goes in v4:
time: 113 us
  blocking collectives  29 us (26%)
  starting transfers between devices  28.3 us (25%)
  Pallas kernels  27.3 us (24%)
  waiting for transfers between devices  24.1 us (21%)
  local copies, waits for them, and re-layouts  3.36 us (3%)
    all_to_all x1, blocking collectives, per_device(): lax.all_to_all(analysed, 'member', split_axis=0, concat_axis=0, tiled=True)  29 us
    pallas_call x6, Pallas kernels, call(): pl.pallas_call(kernel, out_shape=out_shape, in_specs=[SMEM] + [VMEM] * (l...  27.1 us
    ppermute x6, starting transfers between devices, along(): return lax.ppermute(piece, 'member', pairs)  15.7 us
    ppermute x6, waiting for transfers between devices, along(): return lax.ppermute(piece, 'member', pairs)  14.4 us
    ppermute x1, waiting for transfers between devices, per_device(): got_first = lax.ppermute(first, axes, first_pairs)  7.06 us
    ppermute x1, starting transfers between devices, per_device(): lax.ppermute(tail, 'patch', [(i, i + 1) for i in range(patches - 1)])  3.53 us
    ppermute x1, starting transfers between devices, per_device(): lax.ppermute(head, 'patch', [(i + 1, i) for i in range(patches - 1)])  3.34 us
    unnamed x16, local copies, waits for them, and re-layouts  3.32 us
  transfers between devices with their start and end apart: 12, of which 5 were waited for; matrix products, arithmetic and copies ran while one was open for 0% of the time, Pallas kernels for 7%

profile of v4, /device:TPU:4, one launch (start us, length us, event | category | flops | bytes accessed | tf_op | source)
XLA Modules:
  0.0 113.0 jit_solution(13342081172655926607)
XLA Ops:
  0.0 0.0 copy-start
  0.0 1.2 %copy-done = f32[128,8,256]{2,1,0:T(8,128)S(1)} copy-done((f32[128,8,256]{2,1,0:T(8,128)S(1)}, f32[128,8,256]{2,1,0:T(8,128)}, u32[]{:S(2)}) %copy-start) | copy-done | bytes 1048600
  1.2 0.0 copy-start.2
  1.2 0.8 copy-done.2
  2.0 0.0 copy-start.1
  2.0 0.2 pack.1
  2.2 3.5 %collective-permute-start = (f32[264,256]{1,0:T(8,128)S(1)}, f32[264,256]{1,0:T(8,128)S(1)}, u32[]{:S(2)}, u32[]{:S(2)}) collective-permute-start(f32[264,256]{1,0:T(8,128)S(1)} %get-tuple-element.25), channel_id=1, source_target_pairs={{0,8},{8,16},{16,24},{1,9},{9,17},{17,25},{2,10},{10,18},{18,26},{... | collective-permute-start | bytes 811016 | tf_op jit(solution)/shard_map/ppermute | solution.py:377
  5.7 3.3 %collective-permute-start.1 = (f32[264,256]{1,0:T(8,128)S(1)}, f32[264,256]{1,0:T(8,128)S(1)}, u32[]{:S(2)}, u32[]{:S(2)}) collective-permute-start(f32[264,256]{1,0:T(8,128)S(1)} %get-tuple-element.26), channel_id=1, source_target_pairs={{8,0},{16,8},{24,16},{9,1},{17,9},{25,17},{10,2},{18,10},{26,18},{... | collective-permute-start | bytes 811016 | tf_op jit(solution)/shard_map/ppermute | solution.py:378
  9.1 0.0 copy-start.3
  9.1 0.1 pad_add_fusion.info_ref
  9.2 0.0 copy-start.4
  9.2 0.0 copy-done.1
  9.2 0.6 copy-done.3
  9.8 0.0 copy-done.4
  9.8 2.9 %inner.1 = (f32[2,128,256]{2,1,0:T(8,128)S(1)}, f32[2,128,256]{2,1,0:T(8,128)S(1)}, f32[2,128,256]{2,1,0:T(8,128)}, f32[2,128,256]{2,1,0:T(8,128)}) custom-call(s32[3]{0:T(128)S(1)} %pad_add_fusion.info_ref, f32[128,8,256]{2,1,0:T(8,128)S(1)} %copy-done.1, f32[4,8,256]{2,1,0:T(8,128)S(1)} %copy-done.3, f32[1,128]{1,0:T(1,128)S(1)} %bitcast.5), custom_call_target="tpu_custom_call" | custom-call | tf_op jit(solution)/shard_map/inner/pallas_call | solution.py:339
  12.7 3.5 %collective-permute-start.3 = (f32[2,128,256]{2,1,0:T(8,128)S(1)}, f32[2,128,256]{2,1,0:T(8,128)S(1)}, u32[]{:S(2)}, u32[]{:S(2)}) collective-permute-start(f32[2,128,256]{2,1,0:T(8,128)S(1)} %get-tuple-element.30), channel_id=1, source_target_pairs={{0,2},{1,3},{2,4},{3,5},{8,10},{9,11},{10,12},{11,13},{16,18},{17,... | collective-permute-start | bytes 786440 | tf_op jit(solution)/shard_map/ppermute | solution.py:397
  16.2 2.3 %collective-permute-start.4 = (f32[2,128,256]{2,1,0:T(8,128)}, f32[2,128,256]{2,1,0:T(8,128)S(1)}, u32[]{:S(2)}, u32[]{:S(2)}) collective-permute-start(f32[2,128,256]{2,1,0:T(8,128)} %get-tuple-element.31), channel_id=1, source_target_pairs={{0,4},{1,5},{6,2},{7,3},{8,12},{9,13},{14,10},{15,11},{16,20},{17,... | collective-permute-start | bytes 786440 | tf_op jit(solution)/shard_map/ppermute | solution.py:397
  18.6 0.7 collective-permute-start.5
  19.2 0.0 collective-permute-done.before_ref
  19.2 0.0 collective-permute-done.1.after_ref
  19.3 3.0 %edge.1 = (f32[2,128,256]{2,1,0:T(8,128)S(1)}, f32[2,128,256]{2,1,0:T(8,128)}, f32[2,128,256]{2,1,0:T(8,128)S(1)}, f32[2,128,256]{2,1,0:T(8,128)S(1)}) custom-call(s32[3]{0:T(128)S(1)} %pad_add_fusion.info_ref, f32[128,8,256]{2,1,0:T(8,128)S(1)} %copy-done.1, f32[4,8,256]{2,1,0:T(8,128)S(1)} %copy-done.3, f32[1,128]{1,0:T(1,128)S(1)} %bitcast.6, ...), custom_call_target="tpu_custom_call" | custom-call | tf_op jit(solution)/shard_map/edge/pallas_call | solution.py:339
  22.3 1.3 %collective-permute-start.6 = (f32[2,128,256]{2,1,0:T(8,128)}, f32[2,128,256]{2,1,0:T(8,128)S(1)}, u32[]{:S(2)}, u32[]{:S(2)}) collective-permute-start(f32[2,128,256]{2,1,0:T(8,128)} %get-tuple-element.33), channel_id=1, source_target_pairs={{4,6},{5,7},{6,0},{7,1},{12,14},{13,15},{14,8},{15,9},{20,22},{21,... | collective-permute-start | bytes 786440 | tf_op jit(solution)/shard_map/ppermute | solution.py:397
  23.6 1.3 %collective-permute-start.7 = (f32[2,128,256]{2,1,0:T(8,128)S(1)}, f32[2,128,256]{2,1,0:T(8,128)S(1)}, u32[]{:S(2)}, u32[]{:S(2)}) collective-permute-start(f32[2,128,256]{2,1,0:T(8,128)S(1)} %get-tuple-element.34), channel_id=1, source_target_pairs={{2,6},{3,7},{4,0},{5,1},{10,14},{11,15},{12,8},{13,9},{18,22},{19,... | collective-permute-start | bytes 786440 | tf_op jit(solution)/shard_map/ppermute | solution.py:397
  24.9 0.0 collective-permute-done.3.refs_1_
  24.9 0.0 copy-start.7
  24.9 6.7 %collective-permute-start.8 = (f32[2,128,256]{2,1,0:T(8,128)S(1)}, f32[2,128,256]{2,1,0:T(8,128)S(1)}, u32[]{:S(2)}, u32[]{:S(2)}) collective-permute-start(f32[2,128,256]{2,1,0:T(8,128)S(1)} %get-tuple-element.35), channel_id=1, source_target_pairs={{0,6},{1,7},{2,0},{3,1},{8,14},{9,15},{10,8},{11,9},{16,22},{17,23... | collective-permute-start | bytes 786440 | tf_op jit(solution)/shard_map/ppermute | solution.py:397
  32.2 0.0 copy-done.7
  32.3 0.0 copy-start.5
  32.3 0.0 copy-start.6
  32.3 0.6 copy-done.5
  32.9 0.0 copy-done.6
  33.0 0.0 collective-permute-done.4.refs_2_
  33.0 0.7 collective-permute-start.2
  33.7 0.0 collective-permute-done.5.refs_3_
  33.7 0.0 collective-permute-done.2.other_ref
  33.7 5.2 %collective-permute-done.6.refs_5_ = f32[2,128,256]{2,1,0:T(8,128)S(1)} collective-permute-done((f32[2,128,256]{2,1,0:T(8,128)}, f32[2,128,256]{2,1,0:T(8,128)S(1)}, u32[]{:S(2)}, u32[]{:S(2)}) %collective-permute-start.6) | collective-permute-done | bytes 262176 | tf_op jit(solution)/shard_map/ppermute | solution.py:397
  38.9 5.5 %collective-permute-done.7.refs_6_ = f32[2,128,256]{2,1,0:T(8,128)S(1)} collective-permute-done((f32[2,128,256]{2,1,0:T(8,128)S(1)}, f32[2,128,256]{2,1,0:T(8,128)S(1)}, u32[]{:S(2)}, u32[]{:S(2)}) %collective-permute-start.7) | collective-permute-done | bytes 262176 | tf_op jit(solution)/shard_map/ppermute | solution.py:397
  44.4 3.7 %collective-permute-done.8.refs_7_ = f32[2,128,256]{2,1,0:T(8,128)S(1)} collective-permute-done((f32[2,128,256]{2,1,0:T(8,128)S(1)}, f32[2,128,256]{2,1,0:T(8,128)S(1)}, u32[]{:S(2)}, u32[]{:S(2)}) %collective-permute-start.8) | collective-permute-done | bytes 262176 | tf_op jit(solution)/shard_map/ppermute | solution.py:397
  48.1 0.7 collect.1
  48.8 0.1 collective-permute-start.9
  48.9 1.9 %collective-permute-start.10 = (f32[4,128,256]{2,1,0:T(8,128)S(1)}, f32[4,128,256]{2,1,0:T(8,128)S(1)}, u32[]{:S(2)}, u32[]{:S(2)}) collective-permute-start(f32[4,128,256]{2,1,0:T(8,128)S(1)} %get-tuple-element.43), channel_id=1, source_target_pairs={{0,2},{2,4},{3,1},{4,6},{5,3},{6,15},{7,5},{8,10},{9,16},{10,12},{... | collective-permute-start | bytes 1572872 | tf_op jit(solution)/shard_map/ppermute | solution.py:439
  50.8 3.0 %collective-permute-start.11 = (f32[4,128,256]{2,1,0:T(8,128)S(1)}, f32[4,128,256]{2,1,0:T(8,128)S(1)}, u32[]{:S(2)}, u32[]{:S(2)}) collective-permute-start(f32[4,128,256]{2,1,0:T(8,128)S(1)} %get-tuple-element.44), channel_id=1, source_target_pairs={{1,2},{3,4},{2,1},{5,6},{4,3},{7,15},{6,5},{9,10},{8,16},{11,12},{... | collective-permute-start | bytes 1572872 | tf_op jit(solution)/shard_map/ppermute | solution.py:440
  53.9 0.0 collective-permute-done.9.far_ref
  53.9 2.4 %prepare.1 = (bf16[1024,512]{1,0:T(8,128)(2,1)S(1)}, bf16[1024,512]{1,0:T(8,128)(2,1)S(1)}, bf16[1024,256]{1,0:T(8,128)(2,1)S(1)}, bf16[1024,256]{1,0:T(8,128)(2,1)S(1)}, f32[8,512]{1,0:T(8,128)S(1)}) custom-call(s32[3]{0:T(128)S(1)} %pad_add_fusion.info_ref, f32[8,512]{1,0:T(8,128)S(1)} %get-tuple-element.36.observed_ref, ...), custom_call_target="tpu_custom_call" | custom-call | flops 1073741824 | tf_op jit(solution)/shard_map/prepare/pallas_call | solution.py:339
  56.3 7.1 %collective-permute-done.10.first_ref = f32[4,128,256]{2,1,0:T(8,128)S(1)} collective-permute-done((f32[4,128,256]{2,1,0:T(8,128)S(1)}, f32[4,128,256]{2,1,0:T(8,128)S(1)}, u32[]{:S(2)}, u32[]{:S(2)}) %collective-permute-start.10) | collective-permute-done | bytes 524320 | tf_op jit(solution)/shard_map/ppermute | solution.py:439
  63.3 2.6 %collective-permute-done.11.second_ref = f32[4,128,256]{2,1,0:T(8,128)S(1)} collective-permute-done((f32[4,128,256]{2,1,0:T(8,128)S(1)}, f32[4,128,256]{2,1,0:T(8,128)S(1)}, u32[]{:S(2)}, u32[]{:S(2)}) %collective-permute-start.11) | collective-permute-done | bytes 524320 | tf_op jit(solution)/shard_map/ppermute | solution.py:440
  65.9 16.2 %region.1 = f32[8,128,256]{2,1,0:T(8,128)S(1)} custom-call(s32[3]{0:T(128)S(1)} %pad_add_fusion.info_ref, f32[8,512]{1,0:T(8,128)S(1)} %get-tuple-element.36.observed_ref, f32[2,4,128,256]{3,2,1,0:T(8,128)S(1)} %get-tuple-element.37.near_ref, f32[2,4,128,256]{3,2,1,0:T(8,128)S(1)} %collective-permute-done.9.far_ref, ...), custom_call_target="tpu_custom_call" | custom-call | tf_op jit(solution)/shard_map/region/pallas_call | solution.py:339
  82.2 29.0 %all_to_all.5.rows_ref = f32[8,128,256]{2,1,0:T(8,128)S(1)} all-to-all(f32[8,128,256]{2,1,0:T(8,128)S(1)} %region.1), channel_id=1, replica_groups=mesh['patch'=4,'member'=8] {'member'}, dimensions={0} | all-to-all | bytes 2097152 | tf_op jit(solution)/shard_map/all_to_all | solution.py:455
  111.2 1.9 %unpack.1 = f32[128,8,256]{2,1,0:T(8,128)} custom-call(s32[3]{0:T(128)S(1)} %pad_add_fusion.info_ref, f32[8,128,256]{2,1,0:T(8,128)S(1)} %all_to_all.5.rows_ref), custom_call_target="tpu_custom_call" | custom-call | tf_op jit(solution)/shard_map/unpack/pallas_call | solution.py:339
  (3 shorter events, 0.0 us)
Async XLA Ops:
  0.0 1.2 %copy-start = (f32[128,8,256]{2,1,0:T(8,128)S(1)}, f32[128,8,256]{2,1,0:T(8,128)}, u32[]{:S(2)}) copy-start(f32[128,8,256]{2,1,0:T(8,128)} %field_ref.5) | copy-start | bytes 3145732
  1.2 0.8 copy-start.2
  2.0 7.2 %copy-start.1 = (f32[128,8,256]{2,1,0:T(8,128)S(1)}, f32[128,8,256]{2,1,0:T(8,128)}, u32[]{:S(2)}) copy-start(f32[128,8,256]{2,1,0:T(8,128)} %field_ref.5) | copy-start | bytes 3145732
  2.2 17.1 %collective-permute-start = (f32[264,256]{1,0:T(8,128)S(1)}, f32[264,256]{1,0:T(8,128)S(1)}, u32[]{:S(2)}, u32[]{:S(2)}) collective-permute-start(f32[264,256]{1,0:T(8,128)S(1)} %get-tuple-element.25), channel_id=1, source_target_pairs={{0,8},{8,16},{16,24},{1,9},{9,17},{17,25},{2,10},{10,18},{18,26},{... | collective-permute-start | bytes 811016 | tf_op jit(solution)/shard_map/ppermute | solution.py:377
  5.7 13.6 %collective-permute-start.1 = (f32[264,256]{1,0:T(8,128)S(1)}, f32[264,256]{1,0:T(8,128)S(1)}, u32[]{:S(2)}, u32[]{:S(2)}) collective-permute-start(f32[264,256]{1,0:T(8,128)S(1)} %get-tuple-element.26), channel_id=1, source_target_pairs={{8,0},{16,8},{24,16},{9,1},{17,9},{25,17},{10,2},{18,10},{26,18},{... | collective-permute-start | bytes 811016 | tf_op jit(solution)/shard_map/ppermute | solution.py:378
  9.1 0.8 copy-start.3
  9.2 0.7 copy-start.4
  12.7 12.1 %collective-permute-start.3 = (f32[2,128,256]{2,1,0:T(8,128)S(1)}, f32[2,128,256]{2,1,0:T(8,128)S(1)}, u32[]{:S(2)}, u32[]{:S(2)}) collective-permute-start(f32[2,128,256]{2,1,0:T(8,128)S(1)} %get-tuple-element.30), channel_id=1, source_target_pairs={{0,2},{1,3},{2,4},{3,5},{8,10},{9,11},{10,12},{11,13},{16,18},{17,... | collective-permute-start | bytes 786440 | tf_op jit(solution)/shard_map/ppermute | solution.py:397
  16.2 16.8 %collective-permute-start.4 = (f32[2,128,256]{2,1,0:T(8,128)}, f32[2,128,256]{2,1,0:T(8,128)S(1)}, u32[]{:S(2)}, u32[]{:S(2)}) collective-permute-start(f32[2,128,256]{2,1,0:T(8,128)} %get-tuple-element.31), channel_id=1, source_target_pairs={{0,4},{1,5},{6,2},{7,3},{8,12},{9,13},{14,10},{15,11},{16,20},{17,... | collective-permute-start | bytes 786440 | tf_op jit(solution)/shard_map/ppermute | solution.py:397
  18.6 15.1 %collective-permute-start.5 = (f32[2,128,256]{2,1,0:T(8,128)}, f32[2,128,256]{2,1,0:T(8,128)S(1)}, u32[]{:S(2)}, u32[]{:S(2)}) collective-permute-start(f32[2,128,256]{2,1,0:T(8,128)} %get-tuple-element.32), channel_id=1, source_target_pairs={{4,2},{5,3},{6,4},{7,5},{12,10},{13,11},{14,12},{15,13},{20,18},{2... | collective-permute-start | bytes 786440 | tf_op jit(solution)/shard_map/ppermute | solution.py:397
  22.3 16.6 %collective-permute-start.6 = (f32[2,128,256]{2,1,0:T(8,128)}, f32[2,128,256]{2,1,0:T(8,128)S(1)}, u32[]{:S(2)}, u32[]{:S(2)}) collective-permute-start(f32[2,128,256]{2,1,0:T(8,128)} %get-tuple-element.33), channel_id=1, source_target_pairs={{4,6},{5,7},{6,0},{7,1},{12,14},{13,15},{14,8},{15,9},{20,22},{21,... | collective-permute-start | bytes 786440 | tf_op jit(solution)/shard_map/ppermute | solution.py:397
  23.6 20.8 %collective-permute-start.7 = (f32[2,128,256]{2,1,0:T(8,128)S(1)}, f32[2,128,256]{2,1,0:T(8,128)S(1)}, u32[]{:S(2)}, u32[]{:S(2)}) collective-permute-start(f32[2,128,256]{2,1,0:T(8,128)S(1)} %get-tuple-element.34), channel_id=1, source_target_pairs={{2,6},{3,7},{4,0},{5,1},{10,14},{11,15},{12,8},{13,9},{18,22},{19,... | collective-permute-start | bytes 786440 | tf_op jit(solution)/shard_map/ppermute | solution.py:397
  24.9 7.4 %copy-start.7 = (s32[1,512]{1,0:T(1,128)S(1)}, s32[1,512]{1,0:T(1,128)}, u32[]{:S(2)}) copy-start(s32[1,512]{1,0:T(1,128)} %param.10) | copy-start | bytes 6148
  24.9 23.2 %collective-permute-start.8 = (f32[2,128,256]{2,1,0:T(8,128)S(1)}, f32[2,128,256]{2,1,0:T(8,128)S(1)}, u32[]{:S(2)}, u32[]{:S(2)}) collective-permute-start(f32[2,128,256]{2,1,0:T(8,128)S(1)} %get-tuple-element.35), channel_id=1, source_target_pairs={{0,6},{1,7},{2,0},{3,1},{8,14},{9,15},{10,8},{11,9},{16,22},{17,23... | collective-permute-start | bytes 786440 | tf_op jit(solution)/shard_map/ppermute | solution.py:397
  32.3 0.7 copy-start.5
  32.3 0.7 copy-start.6
  33.0 0.7 collective-permute-start.2
  48.8 5.1 %collective-permute-start.9 = (f32[2,4,128,256]{3,2,1,0:T(8,128)S(1)}, f32[2,4,128,256]{3,2,1,0:T(8,128)S(1)}, u32[]{:S(2)}, u32[]{:S(2)}) collective-permute-start(f32[2,4,128,256]{3,2,1,0:T(8,128)S(1)} %get-tuple-element.37.near_ref), channel_id=1, source_target_pairs={{0,1},{1,0},{2,3},{3,2},{4,5},{5,4},{6,7},{7,6},{8,9},{9,8},{10,11... | collective-permute-start | bytes 3145736 | tf_op jit(solution)/shard_map/ppermute | solution.py:438
  48.9 14.4 %collective-permute-start.10 = (f32[4,128,256]{2,1,0:T(8,128)S(1)}, f32[4,128,256]{2,1,0:T(8,128)S(1)}, u32[]{:S(2)}, u32[]{:S(2)}) collective-permute-start(f32[4,128,256]{2,1,0:T(8,128)S(1)} %get-tuple-element.43), channel_id=1, source_target_pairs={{0,2},{2,4},{3,1},{4,6},{5,3},{6,15},{7,5},{8,10},{9,16},{10,12},{... | collective-permute-start | bytes 1572872 | tf_op jit(solution)/shard_map/ppermute | solution.py:439
  50.8 15.1 %collective-permute-start.11 = (f32[4,128,256]{2,1,0:T(8,128)S(1)}, f32[4,128,256]{2,1,0:T(8,128)S(1)}, u32[]{:S(2)}, u32[]{:S(2)}) collective-permute-start(f32[4,128,256]{2,1,0:T(8,128)S(1)} %get-tuple-element.44), channel_id=1, source_target_pairs={{1,2},{3,4},{2,1},{5,6},{4,3},{7,15},{6,5},{9,10},{8,16},{11,12},{... | collective-permute-start | bytes 1572872 | tf_op jit(solution)/shard_map/ppermute | solution.py:440

commit v5 on v4

--- a/solution.py
+++ b/solution.py
@@ -53,13 +53,12 @@
     return jnp.sum(jnp.where(diagonal, emission_ref[...], 0.0), axis=1, keepdims=True)
 
 
-def second_step(info_ref, wanted, shift, emission, wide_ref, weight_ref, out_refs):
-    chips = len(out_refs)
+def second_step(info_ref, target, shift, emission, wide_ref, weight_ref, out_refs):
     rows = weight_ref.shape[0]
     for s, out_ref in enumerate(out_refs):
-        chip = lax.rem(info_ref[0] + s, chips)
-
-        @pl.when(wanted(chip))
+        chip, wanted = target(s)
+
+        @pl.when(wanted)
         def _():
             for place in range(2):
                 position = 2 * chip + place
@@ -89,8 +88,12 @@
             weights_of(flow_ref[:, row, :]), emission,
             field_ref[:, row - 1, :], field_ref[:, row, :], field_ref[:, row + 1, :],
         )
-    wanted = lambda chip: jnp.logical_and(chip > 0, chip < chips - 1)
-    second_step(info_ref, wanted, 0, emission, wide_ref, weight_ref, out_refs)
+
+    def target(s):
+        chip = lax.rem(info_ref[0] + s, chips)
+        return chip, jnp.logical_and(chip > 0, chip < chips - 1)
+
+    second_step(info_ref, target, 0, emission, wide_ref, weight_ref, out_refs)
 
 
 def edge_kernel(info_ref, field_ref, flow_ref, emission_ref, before_ref, after_ref, *refs):
@@ -118,8 +121,12 @@
         wide_ref[row + 1] = advance(
             weights_of(flow_row(row)), emission, start_row(row - 1), start_row(row), start_row(row + 1)
         )
-    wanted = lambda chip: jnp.logical_or(chip == 0, chip == chips - 1)
-    second_step(info_ref, wanted, 1, emission, wide_ref, weight_ref, out_refs)
+
+    def target(s):
+        first, last = info_ref[0] == s, info_ref[0] == chips - 1 - s
+        return jnp.where(first, 0, chips - 1), jnp.logical_or(first, last)
+
+    second_step(info_ref, target, 1, emission, wide_ref, weight_ref, out_refs)
 
 
 def collect_kernel(info_ref, mine_ref, other_ref, *refs):
@@ -129,8 +136,10 @@
     chip, core = info_ref[0], info_ref[1]
     at_edge = jnp.logical_or(chip == 0, chip == chips - 1)
     for s in range(chips):
-        block = lax.rem(chip + chips - s, chips)
-        for ref, here in ((refs[s], jnp.logical_not(at_edge)), (refs[chips + s], at_edge)):
+        turn, mirror = lax.rem(chip + chips - s, chips), jnp.where(chip == 0, s, chips - 1 - s)
+        for ref, here, block in (
+            (refs[s], jnp.logical_not(at_edge), turn), (refs[chips + s], at_edge, mirror)
+        ):
 
             @pl.when(here)
             def _():
@@ -205,28 +214,63 @@
     return (dot(parts[0], chosen) + (dot(parts[1], chosen) + dot(parts[2], chosen)))[:1]
 
 
+def doubled(x):
+    return jnp.concatenate([x, x], axis=1)
+
+
 def prepare_kernel(
     info_ref, observed_ref, near_ref, far_ref,
-    spread_high, spread_low, own_high, own_low, mean_ref, high_ref, low_ref,
+    spread_high, spread_low, own_high, own_low, own_part, seen_ref, direction_ref,
+    anomaly, high_ref, low_ref,
 ):
     _, chips, step, width = near_ref.shape
     members = 2 * chips * step
     cells, _, _, scale = observations(info_ref, observed_ref, width, math.sqrt(members - 1))
     chosen = one_hot(cells, width, 2 * width)
+    blocks = [pl.ds(index * step, step) for index in range(2 * chips)]
     means = []
     for place in range(2):
-        blocks = [near_ref[place, chip] for chip in range(chips)] + [far_ref[1 - place, chip] for chip in range(chips)]
-        means.append(mean_of(blocks, members))
-        for index in range(2 * chips):
-            block = near_ref[place, index] if index < chips else far_ref[1 - place, index - chips]
-            rows = pl.ds(index * step, step)
-            high, low = pieces(block - means[-1], 2)
-            high_ref[rows, pl.ds(place * width, width)] = high
-            low_ref[rows, pl.ds(place * width, width)] = low
-            if place == 1:
-                own_high[rows, :] = high
-                own_low[rows, :] = low
-    mean_ref[...] = jnp.broadcast_to(at_cells(jnp.concatenate(means, axis=1), chosen), mean_ref.shape)
+        columns = pl.ds(place * width, width)
+        rows = [near_ref.at[place, chip] for chip in range(chips)] + [far_ref.at[1 - place, chip] for chip in range(chips)]
+        means.append(mean_of([row[...] for row in rows], members))
+        for block, row in zip(blocks, rows):
+            part = row[...] - means[-1]
+            anomaly[block, columns] = part
+            high_ref[block, columns] = part.astype(BF16)
+
+    def unit(x):
+        return x * (1.0 / jnp.maximum(jnp.max(jnp.abs(x)), 1e-30))
+
+    high = high_ref[...]
+    along = lax.dot_general(high[:16], high, (((1,), (1,)), ((), ())), preferred_element_type=F32)
+    rows = unit(dot(unit(along).astype(BF16), high))
+    weight = jnp.sum(rows * rows[:1], axis=1, keepdims=True)
+    weight = weight + jnp.where(jnp.max(jnp.abs(weight)) > 0.0, 0.0, 1.0)
+    pattern = unit(jnp.sum(rows * weight, axis=0, keepdims=True))
+    total = jnp.zeros((1, 1), F32)
+    for block in blocks:
+        along = jnp.sum(anomaly[block, :] * pattern, axis=1, keepdims=True)
+        total = total + jnp.sum(along * along, axis=0, keepdims=True)
+        direction_ref[block, :] = jnp.broadcast_to(along, (step, direction_ref.shape[1]))
+    length = lax.rsqrt(jnp.maximum(total, 1e-30))
+    taken = None
+    for block in blocks:
+        direction = direction_ref[block, :] * length
+        direction_ref[block, :] = direction
+        term = anomaly[block, :] * doubled(doubled(direction))
+        taken = term if taken is None else taken + term
+    taken = jnp.sum(taken, axis=0, keepdims=True)
+    own_part[...] = jnp.broadcast_to(taken[:, width:], (own_part.shape[1], width)).T
+
+    for block in blocks:
+        rest = anomaly[block, :] - doubled(doubled(direction_ref[block, :])) * taken
+        high, low = pieces(rest, 2)
+        high_ref[block, :] = high
+        low_ref[block, :] = low
+        own = rest[:, width:].T
+        own_high[:, block], own_low[:, block] = pieces(own, 2)
+    seen_ref[pl.ds(0, 1), :] = at_cells(jnp.concatenate(means, axis=1), chosen)
+    seen_ref[pl.ds(1, 1), :] = at_cells(taken, chosen)
     for first in range(0, members, PART):
         rows = pl.ds(first, PART)
         spread = (dot(high_ref[rows, :], chosen) + dot(low_ref[rows, :], chosen)) * scale
@@ -243,8 +287,8 @@
 
 
 def region_kernel(
-    info_ref, observed_ref, near_ref, far_ref, high_in, low_in, own_high, own_low, mean_ref, first_ref, second_ref,
-    out_ref, spread_high, spread_low, factor, answer,
+    info_ref, observed_ref, near_ref, far_ref, high_in, low_in, own_high, own_low, own_part, seen_ref, direction_ref,
+    first_ref, second_ref, out_ref, spread_high, spread_low, factor, answer,
 ):
     _, chips, step, width = near_ref.shape
     members = 2 * chips * step
@@ -262,68 +306,99 @@
         part = index // chips
         return jnp.where(swapped, pair[1 - part], pair[part])
 
+    blocks = [pl.ds(index * step, step) for index in range(2 * chips)]
     mean = mean_of([ref[chip] for ref in (first_ref, second_ref) for chip in range(chips)], members)
-    innovation = slot_weight * (values - (mean_ref[pl.ds(0, 1), :] + at_cells(mean, chosen)))
-    for index in range(2 * chips):
-        rows = pl.ds(index * step, step)
-        high, low = pieces(outer_block(index) - mean, 2)
+    taken = None
+    for index, block in enumerate(blocks):
+        term = (outer_block(index) - mean) * doubled(direction_ref[block, :])
+        taken = term if taken is None else taken + term
+    taken = jnp.sum(taken, axis=0, keepdims=True)
+    seen_mean = seen_ref[pl.ds(0, 1), :] + at_cells(mean, chosen)
+    common = (seen_ref[pl.ds(1, 1), :] + at_cells(taken, chosen)) * scale
+    innovation = slot_weight * (values - seen_mean)
+    for index, block in enumerate(blocks):
+        rest = outer_block(index) - mean - doubled(direction_ref[block, :]) * taken
+        high, low = pieces(rest, 2)
         high, low = pieces((dot(high, chosen) + dot(low, chosen)) * scale, 2)
-        spread_high[rows, :] = high + high_in[rows, :]
-        spread_low[rows, :] = low + low_in[rows, :]
+        spread_high[block, :] = high + high_in[block, :]
+        spread_low[block, :] = low + low_in[block, :]
 
     high, low = spread_high[...], spread_low[...]
     eye = lax.broadcasted_iota(jnp.int32, (slots, slots), 0) == lax.broadcasted_iota(
         jnp.int32, (slots, slots), 1
     )
-    cross = dot_t(high, low)
-    matrix = dot_t(high, high) + (cross + cross.T) + jnp.where(eye, 1.0, 0.0)
-    right = dot_t(high, own_high[...]) + (dot_t(high, own_low[...]) + dot_t(low, own_high[...]))
-
-    norm = jnp.max(jnp.sum(jnp.abs(matrix), axis=0, keepdims=True))
-    start = 2.0 / (1.0 + norm)
-    factor[...] = matrix * start
-    answer[...] = right * start
+    turned = high.T
+    cross = dot(turned, low)
+    factor[...] = dot(turned, high) + (cross + cross.T) + jnp.where(eye, 1.0, 0.0)
+    answer[pl.ds(0, width), :] = product([own_high[...], own_low[...]], [high, low])
+    answer[pl.ds(width, 8), :] = jnp.where(
+        lax.broadcasted_iota(jnp.int32, (8, slots), 0) == 0, jnp.broadcast_to(common, (8, slots)), 0.0
+    )
     half = slots // 2
     upper, lower = pl.ds(0, half), pl.ds(half, half)
+
+    def after(bound):
+        return bound * bound / (2.0 - bound * bound)
+
+    def size(matrix):
+        return jnp.sum(jnp.sum(matrix * matrix, axis=0, keepdims=True))
+
+    def begin(count):
+        parts = pieces(factor[...], count)
+        top, bottom = square(parts)
+        limit = 1.0001 * jnp.sqrt(jnp.sqrt(size(top) + size(bottom)))
+        start = 2.0 / (1.0 + limit)
+        bound = 1.0 - start
+        gain = 2.0 / (2.0 - bound * bound)
+        answer[...] = (gain * start) * (2.0 * answer[...] - start * product(pieces(answer[...], count), parts))
+        factor[upper, :] = (gain * start) * (2.0 * factor[upper, :] - start * top)
+        factor[lower, :] = (gain * start) * (2.0 * factor[lower, :] - start * bottom)
+        return after(bound)
 
     def refine(bound, count):
         gain = 2.0 / (2.0 - bound * bound)
         parts = pieces(factor[...], count)
-        answer[...] = gain * (2.0 * answer[...] - product(parts, pieces(answer[...], count)))
+        answer[...] = gain * (2.0 * answer[...] - product(pieces(answer[...], count), parts))
         top, bottom = square(parts)
         factor[upper, :] = gain * (2.0 * factor[upper, :] - top)
         factor[lower, :] = gain * (2.0 * factor[lower, :] - bottom)
-        return bound * bound / (2.0 - bound * bound)
+        return after(bound)
 
     def close(bound, rest):
         gain = 2.0 / (2.0 - bound * bound)
-        answer[...] = gain * (answer[...] + dot(rest, answer[...].astype(BF16)))
+        answer[...] = gain * (answer[...] + dot(answer[...].astype(BF16), rest))
         return gain
 
     def finish(bound):
         rest = factor[...].astype(BF16)
         gain = close(bound, rest)
         factor[...] = gain * (dot(rest, rest) - jnp.where(eye, 0.5 * bound * bound, 0.0))
-        return bound * bound / (2.0 - bound * bound)
-
-    bound = 1.0 - start
-    bound = lax.while_loop(
-        lambda b: jnp.logical_and(b > COARSE, norm > LARGE), lambda b: refine(b, 3), bound
-    )
+        return after(bound)
+
+    large = size(factor[...]) > LARGE * LARGE
+    bound = lax.cond(large, lambda: begin(3), lambda: begin(2))
+    bound = lax.while_loop(lambda b: jnp.logical_and(b > COARSE, large), lambda b: refine(b, 3), bound)
     bound = lax.while_loop(lambda b: b > COARSE, lambda b: refine(b, 2), bound)
     factor[...] = jnp.where(eye, 1.0, 0.0) - factor[...]
     bound = lax.while_loop(lambda b: b > DONE, finish, bound)
     close(bound, factor[...].astype(BF16))
 
-    solved = answer[...]
-    solved_parts = pieces(solved, 2)
-    innovation_parts = pieces(jnp.broadcast_to(innovation * (1.0 / root), (8, slots)), 3)
-    shift = product(innovation_parts, pieces(solved, 3))[:1]
-    halved = [part * jnp.asarray(-0.5, BF16) for part in solved_parts]
+    solved = answer[pl.ds(0, width), :]
+    alone = answer[pl.ds(width, 1), :]
+    share = own_part[:, :1] - jnp.sum(solved * common, axis=1, keepdims=True)
+    solved = solved + (share / (1.0 + jnp.sum(common * alone, axis=1, keepdims=True))) * alone
+    solved = solved.T
+    which = lax.broadcasted_iota(jnp.int32, (8, slots), 0)
+    sides = jnp.where(which == 0, innovation * (1.0 / root), jnp.where(which == 1, -0.5 * common, 0.0))
+    parts = pieces(solved, 3)
+    sides = product(pieces(sides, 3), parts)
+    shift, along = sides[0:1], sides[1:2]
+    halved = [part * jnp.asarray(-0.5, BF16) for part in pieces(solved, 2)]
     for part, ref, place in ((0, near_ref, 1), (1, far_ref, 0)):
         for chip in range(chips):
-            rows = pl.ds((part * chips + chip) * step, step)
-            moved = product([spread_high[rows, :], spread_low[rows, :]], halved)
+            block = blocks[part * chips + chip]
+            moved = product([spread_high[block, :], spread_low[block, :]], halved)
+            moved = moved + doubled(direction_ref[block, :]) * along
             out_ref[2 * chip + jnp.abs(core - part)] = ref[place, chip] + shift + moved
 
 
@@ -389,12 +464,12 @@
     )
 
     def along(piece, s, ends):
-        pairs = []
-        for chip in range(chips):
-            to = (chip + s) % chips
-            if (to in (0, chips - 1)) == ends:
-                pairs += [(2 * chip + core, 2 * to + core) for core in range(2)]
-        return lax.ppermute(piece, "member", pairs)
+        if ends:
+            hops = [(s, 0), (chips - 1 - s, chips - 1)]
+        else:
+            hops = [(chip, (chip + s) % chips) for chip in range(chips)]
+            hops = [(chip, to) for chip, to in hops if 0 < to < chips - 1]
+        return lax.ppermute(piece, "member", [(2 * a + core, 2 * b + core) for a, b in hops for core in range(2)])
 
     pair = array(2, step, width)
     wide = [pltpu.VMEM((rows + 2, step, width), F32), pltpu.VMEM((rows, 8, width), F32)]
@@ -408,7 +483,7 @@
         mine, axes,
         [(p * lanes + i, p * lanes + lanes - 1 - i) for p in range(1, patches, 2) for i in range(lanes)],
     )
-    got_outer = {s: along(outer[s], s, True) for s in order}
+    got_outer = {s: along(outer[s], s, True) for s in range(chips - 1, 0, -1)}
     pieces_in = [inner[0]] + [got_inner[s] for s in range(1, chips)]
     pieces_in += [outer[0]] + [got_outer[s] for s in range(1, chips)]
     half_row = array(chips, step, width)
@@ -442,15 +517,16 @@
     split = [pltpu.VMEM((members, slots), BF16)] * 2
     prepared = call(
         prepare_kernel, "prepare",
-        [bfloat(members, slots)] * 2 + [bfloat(members, width)] * 2 + [array(8, slots)],
+        [bfloat(members, slots)] * 2 + [bfloat(width, members)] * 2
+        + [array(width, width // 2), array(8, slots), array(members, width // 2)],
         [info, observed, near, far],
-        [pltpu.VMEM((members, 2 * width), BF16)] * 2,
+        [pltpu.VMEM((members, 2 * width), F32)] + [pltpu.VMEM((members, 2 * width), BF16)] * 2,
         flops=8 * members * slots * width,
     )
     analysed = call(
         region_kernel, "region", array(lanes, step, width),
         [info, observed, near, far, *prepared, got_first, got_second],
-        split + [pltpu.VMEM((slots, slots), F32), pltpu.VMEM((slots, width), F32)],
+        split + [pltpu.VMEM((slots, slots), F32), pltpu.VMEM((width + 8, slots), F32)],
     )
     returned = lax.all_to_all(analysed, "member", split_axis=0, concat_axis=0, tiled=True)
     return call(unpack_kernel, "unpack", array(step, rows, width), [info, returned])

time: 113 us -> 108 us (0.956)
  the two profiles are of different devices: /device:TPU:4 before, /device:TPU:2 now
where the time goes in v5:
time: 108 us; the launch traced here: 106 us
  blocking collectives  29.8 us (28%)
  starting transfers between devices  28.3 us (26%)
  Pallas kernels  25.5 us (24%)
  waiting for transfers between devices  18.2 us (17%)
  local copies, waits for them, and re-layouts  3.36 us (3%)
    all_to_all x1, blocking collectives, per_device(): lax.all_to_all(analysed, 'member', split_axis=0, concat_axis=0, tiled=True)  29.8 us
    pallas_call x6, Pallas kernels, call(): pl.pallas_call(kernel, out_shape=out_shape, in_specs=[SMEM] + [VMEM] * (l...  25.3 us
    ppermute x6, starting transfers between devices, along(): lax.ppermute(piece, 'member', [(2 * a + core, 2 * b + core) for a, b in h...  14.6 us
    ppermute x6, waiting for transfers between devices, along(): lax.ppermute(piece, 'member', [(2 * a + core, 2 * b + core) for a, b in h...  5.31 us
    ppermute x1, waiting for transfers between devices, per_device(): lax.ppermute(mine, axes, [(p * lanes + i, p * lanes + lanes - 1 - i) for...  4.92 us
    ppermute x1, waiting for transfers between devices, per_device(): got_first = lax.ppermute(first, axes, first_pairs)  3.85 us
    ppermute x1, starting transfers between devices, per_device(): lax.ppermute(tail, 'patch', [(i, i + 1) for i in range(patches - 1)])  3.53 us
    ppermute x1, waiting for transfers between devices, per_device(): got_second = lax.ppermute(second, axes, second_pairs)  3.37 us
  transfers between devices with their start and end apart: 12, of which 5 were waited for; matrix products, arithmetic and copies ran while one was open for 0% of the time, Pallas kernels for 9%

profile of v5, /device:TPU:2, one launch (start us, length us, event | category | flops | bytes accessed | tf_op | source)
XLA Modules:
  0.0 106.2 jit_solution(14809849117072767701)
XLA Ops:
  0.0 0.0 copy-start
  0.0 1.2 %copy-done = f32[128,8,256]{2,1,0:T(8,128)S(1)} copy-done((f32[128,8,256]{2,1,0:T(8,128)S(1)}, f32[128,8,256]{2,1,0:T(8,128)}, u32[]{:S(2)}) %copy-start) | copy-done | bytes 1048600
  1.2 0.0 copy-start.2
  1.2 0.8 copy-done.2
  2.0 0.0 copy-start.1
  2.0 0.2 pack.1
  2.2 3.5 %collective-permute-start = (f32[264,256]{1,0:T(8,128)S(1)}, f32[264,256]{1,0:T(8,128)S(1)}, u32[]{:S(2)}, u32[]{:S(2)}) collective-permute-start(f32[264,256]{1,0:T(8,128)S(1)} %get-tuple-element.27), channel_id=1, source_target_pairs={{0,8},{8,16},{16,24},{1,9},{9,17},{17,25},{2,10},{10,18},{18,26},{... | collective-permute-start | bytes 811016 | tf_op jit(solution)/shard_map/ppermute | solution.py:452
  5.7 2.5 %collective-permute-start.1 = (f32[264,256]{1,0:T(8,128)S(1)}, f32[264,256]{1,0:T(8,128)S(1)}, u32[]{:S(2)}, u32[]{:S(2)}) collective-permute-start(f32[264,256]{1,0:T(8,128)S(1)} %get-tuple-element.28), channel_id=1, source_target_pairs={{8,0},{16,8},{24,16},{9,1},{17,9},{25,17},{10,2},{18,10},{26,18},{... | collective-permute-start | bytes 811016 | tf_op jit(solution)/shard_map/ppermute | solution.py:453
  8.2 0.0 copy-start.3
  8.2 0.1 pad_add_fusion.info_ref
  8.3 0.0 copy-start.4
  8.3 0.0 copy-done.1
  8.3 0.6 copy-done.3
  8.9 0.0 copy-done.4
  8.9 2.9 %inner.1 = (f32[2,128,256]{2,1,0:T(8,128)S(1)}, f32[2,128,256]{2,1,0:T(8,128)S(1)}, f32[2,128,256]{2,1,0:T(8,128)}, f32[2,128,256]{2,1,0:T(8,128)}) custom-call(s32[3]{0:T(128)S(1)} %pad_add_fusion.info_ref, f32[128,8,256]{2,1,0:T(8,128)S(1)} %copy-done.1, f32[4,8,256]{2,1,0:T(8,128)S(1)} %copy-done.3, f32[1,128]{1,0:T(1,128)S(1)} %bitcast.5), custom_call_target="tpu_custom_call" | custom-call | tf_op jit(solution)/shard_map/inner/pallas_call | solution.py:414
  11.9 3.5 %collective-permute-start.3 = (f32[2,128,256]{2,1,0:T(8,128)S(1)}, f32[2,128,256]{2,1,0:T(8,128)S(1)}, u32[]{:S(2)}, u32[]{:S(2)}) collective-permute-start(f32[2,128,256]{2,1,0:T(8,128)S(1)} %get-tuple-element.32), channel_id=1, source_target_pairs={{0,2},{1,3},{2,4},{3,5},{8,10},{9,11},{10,12},{11,13},{16,18},{17,... | collective-permute-start | bytes 786440 | tf_op jit(solution)/shard_map/ppermute | solution.py:472
  15.4 2.3 %collective-permute-start.4 = (f32[2,128,256]{2,1,0:T(8,128)}, f32[2,128,256]{2,1,0:T(8,128)S(1)}, u32[]{:S(2)}, u32[]{:S(2)}) collective-permute-start(f32[2,128,256]{2,1,0:T(8,128)} %get-tuple-element.33), channel_id=1, source_target_pairs={{0,4},{1,5},{6,2},{7,3},{8,12},{9,13},{14,10},{15,11},{16,20},{17,... | collective-permute-start | bytes 786440 | tf_op jit(solution)/shard_map/ppermute | solution.py:472
  17.7 0.7 collective-permute-start.5
  18.4 0.0 collective-permute-done.before_ref
  18.4 0.8 collective-permute-done.1.after_ref
  19.2 3.0 %edge.1 = (f32[2,128,256]{2,1,0:T(8,128)S(1)}, f32[2,128,256]{2,1,0:T(8,128)}, f32[2,128,256]{2,1,0:T(8,128)S(1)}, f32[2,128,256]{2,1,0:T(8,128)S(1)}) custom-call(s32[3]{0:T(128)S(1)} %pad_add_fusion.info_ref, f32[128,8,256]{2,1,0:T(8,128)S(1)} %copy-done.1, f32[4,8,256]{2,1,0:T(8,128)S(1)} %copy-done.3, f32[1,128]{1,0:T(1,128)S(1)} %bitcast.6, ...), custom_call_target="tpu_custom_call" | custom-call | tf_op jit(solution)/shard_map/edge/pallas_call | solution.py:414
  22.2 1.3 %collective-permute-start.6 = (f32[2,128,256]{2,1,0:T(8,128)}, f32[2,128,256]{2,1,0:T(8,128)S(1)}, u32[]{:S(2)}, u32[]{:S(2)}) collective-permute-start(f32[2,128,256]{2,1,0:T(8,128)} %get-tuple-element.35), channel_id=1, source_target_pairs={{2,0},{3,1},{4,6},{5,7},{10,8},{11,9},{12,14},{13,15},{18,16},{19,... | collective-permute-start | bytes 786440 | tf_op jit(solution)/shard_map/ppermute | solution.py:472
  23.4 1.3 %collective-permute-start.7 = (f32[2,128,256]{2,1,0:T(8,128)S(1)}, f32[2,128,256]{2,1,0:T(8,128)S(1)}, u32[]{:S(2)}, u32[]{:S(2)}) collective-permute-start(f32[2,128,256]{2,1,0:T(8,128)S(1)} %get-tuple-element.36), channel_id=1, source_target_pairs={{4,0},{5,1},{2,6},{3,7},{12,8},{13,9},{10,14},{11,15},{20,16},{21,... | collective-permute-start | bytes 786440 | tf_op jit(solution)/shard_map/ppermute | solution.py:472
  24.7 0.0 collective-permute-done.3.refs_1_
  24.8 0.0 copy-start.7
  24.8 5.5 %collective-permute-start.8 = (f32[2,128,256]{2,1,0:T(8,128)S(1)}, f32[2,128,256]{2,1,0:T(8,128)S(1)}, u32[]{:S(2)}, u32[]{:S(2)}) collective-permute-start(f32[2,128,256]{2,1,0:T(8,128)S(1)} %get-tuple-element.37), channel_id=1, source_target_pairs={{6,0},{7,1},{0,6},{1,7},{14,8},{15,9},{8,14},{9,15},{22,16},{23,17... | collective-permute-start | bytes 786440 | tf_op jit(solution)/shard_map/ppermute | solution.py:472
  30.9 0.0 copy-done.7
  31.0 0.0 copy-start.5
  31.0 0.0 copy-start.6
  31.0 0.6 copy-done.5
  31.6 0.0 copy-done.6
  31.7 0.0 collective-permute-done.4.refs_2_
  31.7 1.9 %collective-permute-start.2 = (f32[8,512]{1,0:T(8,128)S(1)}, f32[8,512]{1,0:T(8,128)S(1)}, u32[]{:S(2)}, u32[]{:S(2)}) collective-permute-start(f32[8,512]{1,0:T(8,128)S(1)} %concatenate.3.mine_ref), channel_id=1, source_target_pairs={{8,15},{9,14},{10,13},{11,12},{12,11},{13,10},{14,9},{15,8},{24,31... | collective-permute-start | bytes 49160 | tf_op jit(solution)/shard_map/ppermute | solution.py:482
  33.6 0.0 collective-permute-done.5.refs_3_
  33.6 4.9 %collective-permute-done.2.other_ref = f32[8,512]{1,0:T(8,128)S(1)} collective-permute-done((f32[8,512]{1,0:T(8,128)S(1)}, f32[8,512]{1,0:T(8,128)S(1)}, u32[]{:S(2)}, u32[]{:S(2)}) %collective-permute-start.2) | collective-permute-done | bytes 16416 | tf_op jit(solution)/shard_map/ppermute | solution.py:482
  38.6 0.0 collective-permute-done.6.refs_5_
  38.6 5.3 %collective-permute-done.7.refs_6_ = f32[2,128,256]{2,1,0:T(8,128)S(1)} collective-permute-done((f32[2,128,256]{2,1,0:T(8,128)S(1)}, f32[2,128,256]{2,1,0:T(8,128)S(1)}, u32[]{:S(2)}, u32[]{:S(2)}) %collective-permute-start.7) | collective-permute-done | bytes 262176 | tf_op jit(solution)/shard_map/ppermute | solution.py:472
  43.9 0.0 collective-permute-done.8.refs_7_
  43.9 0.7 collect.1
  44.6 0.1 collective-permute-start.9
  44.7 2.7 %collective-permute-start.10 = (f32[4,128,256]{2,1,0:T(8,128)S(1)}, f32[4,128,256]{2,1,0:T(8,128)S(1)}, u32[]{:S(2)}, u32[]{:S(2)}) collective-permute-start(f32[4,128,256]{2,1,0:T(8,128)S(1)} %get-tuple-element.47), channel_id=1, source_target_pairs={{0,2},{2,4},{3,1},{4,6},{5,3},{6,15},{7,5},{8,10},{9,16},{10,12},{... | collective-permute-start | bytes 1572872 | tf_op jit(solution)/shard_map/ppermute | solution.py:514
  47.4 3.0 %collective-permute-start.11 = (f32[4,128,256]{2,1,0:T(8,128)S(1)}, f32[4,128,256]{2,1,0:T(8,128)S(1)}, u32[]{:S(2)}, u32[]{:S(2)}) collective-permute-start(f32[4,128,256]{2,1,0:T(8,128)S(1)} %get-tuple-element.48), channel_id=1, source_target_pairs={{1,2},{3,4},{2,1},{5,6},{4,3},{7,15},{6,5},{9,10},{8,16},{11,12},{... | collective-permute-start | bytes 1572872 | tf_op jit(solution)/shard_map/ppermute | solution.py:515
  50.4 0.0 collective-permute-done.9.far_ref
  50.5 4.0 %prepare.1 = (bf16[1024,512]{1,0:T(8,128)(2,1)S(1)}, bf16[1024,512]{1,0:T(8,128)(2,1)S(1)}, bf16[256,1024]{1,0:T(8,128)(2,1)S(1)}, bf16[256,1024]{1,0:T(8,128)(2...) custom-call(s32[3]{0:T(128)S(1)} %pad_add_fusion.info_ref, ...), custom_call_target="tpu_custom_call" | custom-call | flops 1073741824 | tf_op jit(solution)/shard_map/prepare/pallas_call | solution.py:414
  54.5 3.8 %collective-permute-done.10.first_ref = f32[4,128,256]{2,1,0:T(8,128)S(1)} collective-permute-done((f32[4,128,256]{2,1,0:T(8,128)S(1)}, f32[4,128,256]{2,1,0:T(8,128)S(1)}, u32[]{:S(2)}, u32[]{:S(2)}) %collective-permute-start.10) | collective-permute-done | bytes 524320 | tf_op jit(solution)/shard_map/ppermute | solution.py:514
  58.3 3.4 %collective-permute-done.11.second_ref = f32[4,128,256]{2,1,0:T(8,128)S(1)} collective-permute-done((f32[4,128,256]{2,1,0:T(8,128)S(1)}, f32[4,128,256]{2,1,0:T(8,128)S(1)}, u32[]{:S(2)}, u32[]{:S(2)}) %collective-permute-start.11) | collective-permute-done | bytes 524320 | tf_op jit(solution)/shard_map/ppermute | solution.py:515
  61.7 12.8 %region.1 = f32[8,128,256]{2,1,0:T(8,128)S(1)} custom-call(s32[3]{0:T(128)S(1)} %pad_add_fusion.info_ref, f32[8,512]{1,0:T(8,128)S(1)} %get-tuple-element.38.observed_ref, f32[2,4,128,256]{3,2,1,0:T(8,128)S(1)} %get-tuple-element.39.near_ref, f32[2,4,128,256]{3,2,1,0:T(8,128)S(1)} %collective-permute-done.9.far_ref, ...), custom_call_target="tpu_custom_call" | custom-call | tf_op jit(solution)/shard_map/region/pallas_call | solution.py:414
  74.5 29.8 %all_to_all.5.rows_ref = f32[8,128,256]{2,1,0:T(8,128)S(1)} all-to-all(f32[8,128,256]{2,1,0:T(8,128)S(1)} %region.1), channel_id=1, replica_groups=mesh['patch'=4,'member'=8] {'member'}, dimensions={0} | all-to-all | bytes 2097152 | tf_op jit(solution)/shard_map/all_to_all | solution.py:531
  104.3 1.9 %unpack.1 = f32[128,8,256]{2,1,0:T(8,128)} custom-call(s32[3]{0:T(128)S(1)} %pad_add_fusion.info_ref, f32[8,128,256]{2,1,0:T(8,128)S(1)} %all_to_all.5.rows_ref), custom_call_target="tpu_custom_call" | custom-call | tf_op jit(solution)/shard_map/unpack/pallas_call | solution.py:414
  (3 shorter events, 0.0 us)
Async XLA Ops:
  0.0 1.2 %copy-start = (f32[128,8,256]{2,1,0:T(8,128)S(1)}, f32[128,8,256]{2,1,0:T(8,128)}, u32[]{:S(2)}) copy-start(f32[128,8,256]{2,1,0:T(8,128)} %field_ref.5) | copy-start | bytes 3145732
  1.2 0.8 copy-start.2
  2.0 6.3 %copy-start.1 = (f32[128,8,256]{2,1,0:T(8,128)S(1)}, f32[128,8,256]{2,1,0:T(8,128)}, u32[]{:S(2)}) copy-start(f32[128,8,256]{2,1,0:T(8,128)} %field_ref.5) | copy-start | bytes 3145732
  2.2 16.2 %collective-permute-start = (f32[264,256]{1,0:T(8,128)S(1)}, f32[264,256]{1,0:T(8,128)S(1)}, u32[]{:S(2)}, u32[]{:S(2)}) collective-permute-start(f32[264,256]{1,0:T(8,128)S(1)} %get-tuple-element.27), channel_id=1, source_target_pairs={{0,8},{8,16},{16,24},{1,9},{9,17},{17,25},{2,10},{10,18},{18,26},{... | collective-permute-start | bytes 811016 | tf_op jit(solution)/shard_map/ppermute | solution.py:452
  5.7 13.5 %collective-permute-start.1 = (f32[264,256]{1,0:T(8,128)S(1)}, f32[264,256]{1,0:T(8,128)S(1)}, u32[]{:S(2)}, u32[]{:S(2)}) collective-permute-start(f32[264,256]{1,0:T(8,128)S(1)} %get-tuple-element.28), channel_id=1, source_target_pairs={{8,0},{16,8},{24,16},{9,1},{17,9},{25,17},{10,2},{18,10},{26,18},{... | collective-permute-start | bytes 811016 | tf_op jit(solution)/shard_map/ppermute | solution.py:453
  8.2 0.8 copy-start.3
  8.3 0.7 copy-start.4
  11.9 12.9 %collective-permute-start.3 = (f32[2,128,256]{2,1,0:T(8,128)S(1)}, f32[2,128,256]{2,1,0:T(8,128)S(1)}, u32[]{:S(2)}, u32[]{:S(2)}) collective-permute-start(f32[2,128,256]{2,1,0:T(8,128)S(1)} %get-tuple-element.32), channel_id=1, source_target_pairs={{0,2},{1,3},{2,4},{3,5},{8,10},{9,11},{10,12},{11,13},{16,18},{17,... | collective-permute-start | bytes 786440 | tf_op jit(solution)/shard_map/ppermute | solution.py:472
  15.4 16.3 %collective-permute-start.4 = (f32[2,128,256]{2,1,0:T(8,128)}, f32[2,128,256]{2,1,0:T(8,128)S(1)}, u32[]{:S(2)}, u32[]{:S(2)}) collective-permute-start(f32[2,128,256]{2,1,0:T(8,128)} %get-tuple-element.33), channel_id=1, source_target_pairs={{0,4},{1,5},{6,2},{7,3},{8,12},{9,13},{14,10},{15,11},{16,20},{17,... | collective-permute-start | bytes 786440 | tf_op jit(solution)/shard_map/ppermute | solution.py:472
  17.7 16.0 %collective-permute-start.5 = (f32[2,128,256]{2,1,0:T(8,128)}, f32[2,128,256]{2,1,0:T(8,128)S(1)}, u32[]{:S(2)}, u32[]{:S(2)}) collective-permute-start(f32[2,128,256]{2,1,0:T(8,128)} %get-tuple-element.34), channel_id=1, source_target_pairs={{4,2},{5,3},{6,4},{7,5},{12,10},{13,11},{14,12},{15,13},{20,18},{2... | collective-permute-start | bytes 786440 | tf_op jit(solution)/shard_map/ppermute | solution.py:472
  22.2 16.4 %collective-permute-start.6 = (f32[2,128,256]{2,1,0:T(8,128)}, f32[2,128,256]{2,1,0:T(8,128)S(1)}, u32[]{:S(2)}, u32[]{:S(2)}) collective-permute-start(f32[2,128,256]{2,1,0:T(8,128)} %get-tuple-element.35), channel_id=1, source_target_pairs={{2,0},{3,1},{4,6},{5,7},{10,8},{11,9},{12,14},{13,15},{18,16},{19,... | collective-permute-start | bytes 786440 | tf_op jit(solution)/shard_map/ppermute | solution.py:472
  23.4 20.4 %collective-permute-start.7 = (f32[2,128,256]{2,1,0:T(8,128)S(1)}, f32[2,128,256]{2,1,0:T(8,128)S(1)}, u32[]{:S(2)}, u32[]{:S(2)}) collective-permute-start(f32[2,128,256]{2,1,0:T(8,128)S(1)} %get-tuple-element.36), channel_id=1, source_target_pairs={{4,0},{5,1},{2,6},{3,7},{12,8},{13,9},{10,14},{11,15},{20,16},{21,... | collective-permute-start | bytes 786440 | tf_op jit(solution)/shard_map/ppermute | solution.py:472
  24.8 6.2 %copy-start.7 = (s32[1,512]{1,0:T(1,128)S(1)}, s32[1,512]{1,0:T(1,128)}, u32[]{:S(2)}) copy-start(s32[1,512]{1,0:T(1,128)} %param.10) | copy-start | bytes 6148
  24.8 19.1 %collective-permute-start.8 = (f32[2,128,256]{2,1,0:T(8,128)S(1)}, f32[2,128,256]{2,1,0:T(8,128)S(1)}, u32[]{:S(2)}, u32[]{:S(2)}) collective-permute-start(f32[2,128,256]{2,1,0:T(8,128)S(1)} %get-tuple-element.37), channel_id=1, source_target_pairs={{6,0},{7,1},{0,6},{1,7},{14,8},{15,9},{8,14},{9,15},{22,16},{23,17... | collective-permute-start | bytes 786440 | tf_op jit(solution)/shard_map/ppermute | solution.py:472
  31.0 0.7 copy-start.5
  31.0 0.7 copy-start.6
  31.7 6.9 %collective-permute-start.2 = (f32[8,512]{1,0:T(8,128)S(1)}, f32[8,512]{1,0:T(8,128)S(1)}, u32[]{:S(2)}, u32[]{:S(2)}) collective-permute-start(f32[8,512]{1,0:T(8,128)S(1)} %concatenate.3.mine_ref), channel_id=1, source_target_pairs={{8,15},{9,14},{10,13},{11,12},{12,11},{13,10},{14,9},{15,8},{24,31... | collective-permute-start | bytes 49160 | tf_op jit(solution)/shard_map/ppermute | solution.py:482
  44.6 5.9 %collective-permute-start.9 = (f32[2,4,128,256]{3,2,1,0:T(8,128)S(1)}, f32[2,4,128,256]{3,2,1,0:T(8,128)S(1)}, u32[]{:S(2)}, u32[]{:S(2)}) collective-permute-start(f32[2,4,128,256]{3,2,1,0:T(8,128)S(1)} %get-tuple-element.39.near_ref), channel_id=1, source_target_pairs={{0,1},{1,0},{2,3},{3,2},{4,5},{5,4},{6,7},{7,6},{8,9},{9,8},{10,11... | collective-permute-start | bytes 3145736 | tf_op jit(solution)/shard_map/ppermute | solution.py:513
  44.7 13.6 %collective-permute-start.10 = (f32[4,128,256]{2,1,0:T(8,128)S(1)}, f32[4,128,256]{2,1,0:T(8,128)S(1)}, u32[]{:S(2)}, u32[]{:S(2)}) collective-permute-start(f32[4,128,256]{2,1,0:T(8,128)S(1)} %get-tuple-element.47), channel_id=1, source_target_pairs={{0,2},{2,4},{3,1},{4,6},{5,3},{6,15},{7,5},{8,10},{9,16},{10,12},{... | collective-permute-start | bytes 1572872 | tf_op jit(solution)/shard_map/ppermute | solution.py:514
  47.4 14.3 %collective-permute-start.11 = (f32[4,128,256]{2,1,0:T(8,128)S(1)}, f32[4,128,256]{2,1,0:T(8,128)S(1)}, u32[]{:S(2)}, u32[]{:S(2)}) collective-permute-start(f32[4,128,256]{2,1,0:T(8,128)S(1)} %get-tuple-element.48), channel_id=1, source_target_pairs={{1,2},{3,4},{2,1},{5,6},{4,3},{7,15},{6,5},{9,10},{8,16},{11,12},{... | collective-permute-start | bytes 1572872 | tf_op jit(solution)/shard_map/ppermute | solution.py:515

commit v6 on v5

--- a/solution.py
+++ b/solution.py
@@ -9,7 +9,7 @@
 from jax.sharding import PartitionSpec as P
 
 STEPS = 2
-COARSE = 0.06
+COARSE = 0.2
 DONE = 0.01
 LARGE = 2e4
 PART = 256
@@ -17,12 +17,17 @@
 BF16 = jnp.bfloat16
 
 
-def pack_kernel(field_ref, flow_ref, tail_ref, head_ref):
+def pack_kernel(info_ref, field_ref, flow_ref, first_ref, second_ref):
     members, rows, width = field_ref.shape
-    for out_ref, first, edge in ((tail_ref, rows - STEPS, rows - 1), (head_ref, 0, 0)):
-        for place in range(STEPS):
-            out_ref[pl.ds(place * members, members), :] = field_ref[:, first + place, :]
-        out_ref[pl.ds(STEPS * members, 8), :] = jnp.concatenate([flow_ref[:, edge, :]] * 2, axis=0)
+    for out_ref, last in ((first_ref, 0), (second_ref, 1)):
+        for parity in range(2):
+
+            @pl.when(info_ref[2] == parity)
+            def _():
+                first, edge = (rows - STEPS, rows - 1) if parity == last else (0, 0)
+                for place in range(STEPS):
+                    out_ref[pl.ds(place * members, members), :] = field_ref[:, first + place, :]
+                out_ref[pl.ds(STEPS * members, 8), :] = jnp.concatenate([flow_ref[:, edge, :]] * 2, axis=0)
 
 
 def weights_of(flow):
@@ -53,80 +58,79 @@
     return jnp.sum(jnp.where(diagonal, emission_ref[...], 0.0), axis=1, keepdims=True)
 
 
-def second_step(info_ref, target, shift, emission, wide_ref, weight_ref, out_refs):
-    rows = weight_ref.shape[0]
+def inner_kernel(info_ref, field_ref, flow_ref, emission_ref, kept_ref, *refs):
+    out_refs, (wide_ref, weight_ref) = refs[:-2], refs[-2:]
+    rows = field_ref.shape[1]
+    chips = len(out_refs)
+    emission = emission_column(emission_ref)
+    for row in range(1, rows - 1):
+        weights = weights_of(flow_ref[:, row, :])
+        for i, weight in enumerate(weights):
+            weight_ref[row, pl.ds(i, 1), :] = weight
+        wide_ref[row] = advance(
+            weights, emission, field_ref[:, row - 1, :], field_ref[:, row, :], field_ref[:, row + 1, :]
+        )
+    for place, row in enumerate((1, 2, rows - 3, rows - 2)):
+        kept_ref[place] = wide_ref[row]
     for s, out_ref in enumerate(out_refs):
-        chip, wanted = target(s)
-
-        @pl.when(wanted)
+        chip = lax.rem(info_ref[0] + s, chips)
+
+        @pl.when(jnp.logical_and(chip > 0, chip < chips - 1))
         def _():
             for place in range(2):
                 position = 2 * chip + place
                 row = position + info_ref[2] * (rows - 1 - 2 * position)
                 weights = weight_ref[row]
-                at = row + shift
                 out_ref[place] = advance(
                     [weights[i : i + 1] for i in range(6)],
-                    emission, wide_ref[at - 1], wide_ref[at], wide_ref[at + 1],
+                    emission, wide_ref[row - 1], wide_ref[row], wide_ref[row + 1],
                 )
 
 
-def store_weights(flow_ref, weight_ref, rows):
-    for row in rows:
-        for i, weight in enumerate(weights_of(flow_ref[:, row, :])):
-            weight_ref[row, pl.ds(i, 1), :] = weight
-
-
-def inner_kernel(info_ref, field_ref, flow_ref, emission_ref, *refs):
-    out_refs, (wide_ref, weight_ref) = refs[:-2], refs[-2:]
-    rows = field_ref.shape[1]
-    chips = len(out_refs)
+def end_rows(info_ref, last, field_ref, flow_ref, emission_ref, kept_ref, halo_ref, out_ref):
+    members, rows, width = field_ref.shape
     emission = emission_column(emission_ref)
-    store_weights(flow_ref, weight_ref, range(rows))
-    for row in range(1, rows - 1):
-        wide_ref[row] = advance(
-            weights_of(flow_ref[:, row, :]), emission,
-            field_ref[:, row - 1, :], field_ref[:, row, :], field_ref[:, row + 1, :],
-        )
-
-    def target(s):
-        chip = lax.rem(info_ref[0] + s, chips)
-        return chip, jnp.logical_and(chip > 0, chip < chips - 1)
-
-    second_step(info_ref, target, 0, emission, wide_ref, weight_ref, out_refs)
-
-
-def edge_kernel(info_ref, field_ref, flow_ref, emission_ref, before_ref, after_ref, *refs):
-    out_refs, (wide_ref, weight_ref) = refs[:-2], refs[-2:]
-    members, rows, width = field_ref.shape
-    chips = len(out_refs)
-    emission = emission_column(emission_ref)
-    store_weights(flow_ref, weight_ref, (0, 1, rows - 2, rows - 1))
-
-    def flow_row(row):
-        if row < 0:
-            return before_ref[pl.ds(STEPS * members, 4), :]
-        if row >= rows:
-            return after_ref[pl.ds(STEPS * members, 4), :]
-        return flow_ref[:, row, :]
-
-    def start_row(row):
-        if row < 0:
-            return before_ref[pl.ds((row + STEPS) * members, members), :]
-        if row >= rows:
-            return after_ref[pl.ds((row - rows) * members, members), :]
-        return field_ref[:, row, :]
-
-    for row in (-1, 0, 1, 2, rows - 3, rows - 2, rows - 1, rows):
-        wide_ref[row + 1] = advance(
-            weights_of(flow_row(row)), emission, start_row(row - 1), start_row(row), start_row(row + 1)
-        )
-
-    def target(s):
-        first, last = info_ref[0] == s, info_ref[0] == chips - 1 - s
-        return jnp.where(first, 0, chips - 1), jnp.logical_or(first, last)
-
-    second_step(info_ref, target, 1, emission, wide_ref, weight_ref, out_refs)
+
+    def halo_row(place):
+        return halo_ref[pl.ds(place * members, members), :]
+
+    halo_weights = weights_of(halo_ref[pl.ds(STEPS * members, 4), :])
+    for parity in range(2):
+
+        @pl.when(info_ref[2] == parity)
+        def _():
+            if parity == last:
+                end, near, outside, beyond = 0, 1, halo_row(1), halo_row(0)
+                inside, further = kept_ref[0], kept_ref[1]
+            else:
+                end, near, outside, beyond = rows - 1, rows - 2, halo_row(0), halo_row(1)
+                inside, further = kept_ref[3], kept_ref[2]
+
+            def ordered(weights, outer, own, inner):
+                behind, ahead = (outer, inner) if end == 0 else (inner, outer)
+                return advance(weights, emission, behind, own, ahead)
+
+            end_weights = weights_of(flow_ref[:, end, :])
+            end_field = field_ref[:, end, :]
+            outer = ordered(halo_weights, beyond, outside, end_field)
+            own = ordered(end_weights, outside, end_field, field_ref[:, near, :])
+            out_ref[last] = ordered(end_weights, outer, own, inside)
+            out_ref[1 - last] = ordered(weights_of(flow_ref[:, near, :]), own, inside, further)
+
+
+def last_kernel(info_ref, field_ref, flow_ref, emission_ref, kept_ref, halo_ref, *refs):
+    chips = (len(refs) - 1) // 2
+    scratch = refs[-1]
+    end_rows(info_ref, 1, field_ref, flow_ref, emission_ref, kept_ref, halo_ref, scratch)
+    for s, out_ref in enumerate(refs[chips:-1]):
+
+        @pl.when(info_ref[0] == chips - 1 - s)
+        def _():
+            out_ref[...] = scratch[...]
+
+
+def first_kernel(info_ref, field_ref, flow_ref, emission_ref, kept_ref, halo_ref, out_ref):
+    end_rows(info_ref, 0, field_ref, flow_ref, emission_ref, kept_ref, halo_ref, out_ref)
 
 
 def collect_kernel(info_ref, mine_ref, other_ref, *refs):
@@ -134,12 +138,9 @@
     both_ref, first_ref, second_ref, observed_ref = refs[-4:]
     observed_ref[...] = jnp.where(info_ref[2] == 1, other_ref[...], mine_ref[...])
     chip, core = info_ref[0], info_ref[1]
-    at_edge = jnp.logical_or(chip == 0, chip == chips - 1)
     for s in range(chips):
-        turn, mirror = lax.rem(chip + chips - s, chips), jnp.where(chip == 0, s, chips - 1 - s)
-        for ref, here, block in (
-            (refs[s], jnp.logical_not(at_edge), turn), (refs[chips + s], at_edge, mirror)
-        ):
+        turn = lax.rem(chip + chips - s, chips)
+        for ref, here, block in ((refs[s], chip > 0, turn), (refs[chips + s], chip == 0, s)):
 
             @pl.when(here)
             def _():
@@ -403,13 +404,10 @@
 
 
 VMEM = pl.BlockSpec(memory_space=pltpu.VMEM)
-LIMIT = pltpu.CompilerParams(vmem_limit_bytes=32 * 1024 * 1024)
-
-
 SMEM = pl.BlockSpec(memory_space=pltpu.SMEM)
 
 
-def call(kernel, name, out_shape, args, scratch=(), flops=None):
+def call(kernel, name, out_shape, args, scratch=(), flops=None, aliases={}, limit=8):
     several = isinstance(out_shape, (list, tuple))
     return pl.pallas_call(
         kernel,
@@ -417,7 +415,8 @@
         in_specs=[SMEM] + [VMEM] * (len(args) - 1),
         out_specs=[VMEM] * len(out_shape) if several else VMEM,
         scratch_shapes=scratch,
-        compiler_params=LIMIT,
+        input_output_aliases=aliases,
+        compiler_params=pltpu.CompilerParams(vmem_limit_bytes=limit * 1024 * 1024),
         cost_estimate=flops and pl.CostEstimate(flops=flops, bytes_accessed=0, transcendentals=0),
         name=name,
     )(*args)
@@ -445,12 +444,13 @@
     info = jnp.stack([lane // 2, lane % 2, patch % 2]).astype(jnp.int32)
 
     edge = array(STEPS * step + 8, width)
-    tail, head = pl.pallas_call(
-        pack_kernel, out_shape=(edge, edge), in_specs=[VMEM] * 2, out_specs=(VMEM, VMEM),
-        compiler_params=LIMIT, name="pack",
-    )(init_field, flow_fields)
-    before = lax.ppermute(tail, "patch", [(i, i + 1) for i in range(patches - 1)])
-    after = lax.ppermute(head, "patch", [(i + 1, i) for i in range(patches - 1)])
+    to_last, to_first = call(pack_kernel, "pack", [edge, edge], [info, init_field, flow_fields])
+
+    def swap(message, start):
+        lower = range(start, patches - 1, 2)
+        return lax.ppermute(message, "patch", [(p, p + 1) for p in lower] + [(p + 1, p) for p in lower])
+
+    halo_last, halo_first = swap(to_last, 0), swap(to_first, 1)
 
     mine = jnp.concatenate(
         [
@@ -463,30 +463,34 @@
         axis=0,
     )
 
-    def along(piece, s, ends):
-        if ends:
-            hops = [(s, 0), (chips - 1 - s, chips - 1)]
-        else:
-            hops = [(chip, (chip + s) % chips) for chip in range(chips)]
-            hops = [(chip, to) for chip, to in hops if 0 < to < chips - 1]
-        return lax.ppermute(piece, "member", [(2 * a + core, 2 * b + core) for a, b in hops for core in range(2)])
+    def between(hops):
+        return [(2 * a + core, 2 * b + core) for a, b in hops for core in range(2)]
 
     pair = array(2, step, width)
-    wide = [pltpu.VMEM((rows + 2, step, width), F32), pltpu.VMEM((rows, 8, width), F32)]
     args = [info, init_field, flow_fields, emission[None, :]]
-    inner = call(inner_kernel, "inner", [pair] * chips, args, wide)
+    kept, *inner = call(
+        inner_kernel, "inner", [array(4, step, width)] + [pair] * chips, args,
+        [pltpu.VMEM((rows, step, width), F32), pltpu.VMEM((rows, 8, width), F32)],
+    )
+    most = call(
+        last_kernel, "last", [pair] * chips, args + [kept, halo_last, *inner],
+        [pltpu.VMEM((2, step, width), F32)], aliases={6 + s: s for s in range(chips)},
+    )
     order = [s for near in range(chips // 2, 0, -1) for s in sorted({near, chips - near})]
-    got_inner = {s: along(inner[s], s, False) for s in order}
-    outer = call(edge_kernel, "edge", [pair] * chips, args + [before, after], wide)
-    mine, _ = lax.optimization_barrier((mine, outer[0]))
+    got_most = {
+        s: lax.ppermute(most[s], "member", between([(to - s + chips) % chips, to] for to in range(1, chips)))
+        for s in order
+    }
+    few = call(first_kernel, "first", pair, args + [kept, halo_first])
+    got_few = {s: lax.ppermute(few, "member", between([(s, 0)])) for s in range(chips - 1, 0, -1)}
+    pieces_in = [most[0]] + [got_most[s] for s in range(1, chips)]
+    pieces_in += [few] + [got_few[s] for s in range(1, chips)]
+    half_row = array(chips, step, width)
+    mine, _ = lax.optimization_barrier((mine, few))
     other = lax.ppermute(
         mine, axes,
         [(p * lanes + i, p * lanes + lanes - 1 - i) for p in range(1, patches, 2) for i in range(lanes)],
     )
-    got_outer = {s: along(outer[s], s, True) for s in range(chips - 1, 0, -1)}
-    pieces_in = [inner[0]] + [got_inner[s] for s in range(1, chips)]
-    pieces_in += [outer[0]] + [got_outer[s] for s in range(1, chips)]
-    half_row = array(chips, step, width)
     near, first, second, observed = call(
         collect_kernel, "collect", [array(2, chips, step, width), half_row, half_row, array(8, slots)],
         [info, mine, other] + pieces_in,
@@ -521,15 +525,24 @@
         + [array(width, width // 2), array(8, slots), array(members, width // 2)],
         [info, observed, near, far],
         [pltpu.VMEM((members, 2 * width), F32)] + [pltpu.VMEM((members, 2 * width), BF16)] * 2,
-        flops=8 * members * slots * width,
+        flops=8 * members * slots * width, limit=20,
     )
     analysed = call(
         region_kernel, "region", array(lanes, step, width),
         [info, observed, near, far, *prepared, got_first, got_second],
         split + [pltpu.VMEM((slots, slots), F32), pltpu.VMEM((width + 8, slots), F32)],
+        limit=24,
     )
     returned = lax.all_to_all(analysed, "member", split_axis=0, concat_axis=0, tiled=True)
-    return call(unpack_kernel, "unpack", array(step, rows, width), [info, returned])
+    part = step // 4
+    return pl.pallas_call(
+        unpack_kernel,
+        grid=(4,),
+        out_shape=array(step, rows, width),
+        in_specs=[SMEM, pl.BlockSpec((rows, part, width), lambda i: (0, i, 0))],
+        out_specs=pl.BlockSpec((part, rows, width), lambda i: (i, 0, 0)),
+        name="unpack",
+    )(info, returned)
 
 
 def solution(mesh):

time: 108 us -> 115 us (1.065)
  waiting for transfers between devices: 18.2 us -> 28.3 us
  Pallas kernels: 25.5 us -> 23 us
    ppermute x8, waiting for transfers between devices: 6.11 us -> 19.2 us  [the longest x3 13.7 us: per_device(): lax.ppermute(few, 'member', between([(s, 0)]))]
    pallas_call x6 -> x7, Pallas kernels: 25.3 us -> 19.5 us  [call(): pl.pallas_call(kernel, out_shape=out_shape, in_specs=[SMEM] + [VMEM] * (l...]
    ppermute x1, waiting for transfers between devices: 4.92 us -> 0.01 us  [per_device(): lax.ppermute(mine, axes, [(p * lanes + i, p * lanes + lanes - 1 - i) for...]
    pallas_call x1, Pallas kernels: 0.17 us -> 3.51 us  [per_device(): pl.pallas_call(unpack_kernel, grid=(4,), out_shape=array(step, rows, widt...]
    ppermute x1, waiting for transfers between devices: 3.85 us -> 6.57 us  [per_device(): got_first = lax.ppermute(first, axes, first_pairs)]
    ppermute x1, starting transfers between devices: 1.92 us -> 4.08 us  [per_device(): lax.ppermute(mine, axes, [(p * lanes + i, p * lanes + lanes - 1 - i) for...]
  transfers between devices with their start and end apart: 12 -> 12, of which waited for: 5 -> 6; matrix products, arithmetic and copies ran while one was open for 0% -> 0% of each run, Pallas kernels for 9% -> 7%
where the time goes in v6:
time: 115 us; the launch traced here: 114 us
  blocking collectives  30 us (26%)
  starting transfers between devices  28.8 us (25%)
  waiting for transfers between devices  28.3 us (25%)
  Pallas kernels  23 us (20%)
  local copies, waits for them, and re-layouts  2.64 us (2%)
    all_to_all x1, blocking collectives, per_device(): lax.all_to_all(analysed, 'member', split_axis=0, concat_axis=0, tiled=True)  30 us
    pallas_call x7, Pallas kernels, call(): pl.pallas_call(kernel, out_shape=out_shape, in_specs=[SMEM] + [VMEM] * (l...  19.5 us
    ppermute x3, waiting for transfers between devices, per_device(): lax.ppermute(few, 'member', between([(s, 0)]))  13.7 us
    ppermute x3, starting transfers between devices, per_device(): lax.ppermute(most[s], 'member', between(([(to - s + chips) % chips, to] f...  11.8 us
    ppermute x1, waiting for transfers between devices, per_device(): got_first = lax.ppermute(first, axes, first_pairs)  6.57 us
    ppermute x2, starting transfers between devices, swap(): lax.ppermute(message, 'patch', [(p, p + 1) for p in lower] + [(p + 1, p)...  5.06 us
    ppermute x1, starting transfers between devices, per_device(): lax.ppermute(mine, axes, [(p * lanes + i, p * lanes + lanes - 1 - i) for...  4.08 us
    ppermute x3, starting transfers between devices, per_device(): lax.ppermute(few, 'member', between([(s, 0)]))  3.88 us
  transfers between devices with their start and end apart: 12, of which 6 were waited for; matrix products, arithmetic and copies ran while one was open for 0% of the time, Pallas kernels for 7%

profile of v6, /device:TPU:2, one launch (start us, length us, event | category | flops | bytes accessed | tf_op | source)
XLA Modules:
  0.0 113.7 jit_solution(5034243957333598565)
XLA Ops:
  0.0 0.0 copy-start.2
  0.0 0.1 pad_add_fusion.info_ref
  0.1 0.7 copy-done.2
  0.8 0.0 copy-start
  0.8 1.2 %copy-done = f32[128,8,256]{2,1,0:T(8,128)S(1)} copy-done((f32[128,8,256]{2,1,0:T(8,128)S(1)}, f32[128,8,256]{2,1,0:T(8,128)}, u32[]{:S(2)}) %copy-start) | copy-done | bytes 1048600
  2.0 0.0 copy-start.3
  2.0 0.7 pack.1
  2.7 0.1 collective-permute-start.2
  2.8 0.0 copy-start.4
  2.8 5.0 %collective-permute-start = (f32[264,256]{1,0:T(8,128)S(1)}, f32[264,256]{1,0:T(8,128)S(1)}, u32[]{:S(2)}, u32[]{:S(2)}) collective-permute-start(f32[264,256]{1,0:T(8,128)S(1)} %get-tuple-element.29), channel_id=1, source_target_pairs={{8,16},{16,8},{9,17},{17,9},{10,18},{18,10},{11,19},{19,11},{12,20... | collective-permute-start | bytes 811016 | tf_op jit(solution)/shard_map/ppermute | solution.py:451
  7.8 0.0 copy-done.4
  7.8 2.2 %inner.1 = (f32[4,128,256]{2,1,0:T(8,128)S(1)}, f32[2,128,256]{2,1,0:T(8,128)S(1)}, f32[2,128,256]{2,1,0:T(8,128)S(1)}, f32[2,128,256]{2,1,0:T(8,128)S(1)}, f32[2,128,256]{2,1,0:T(8,128)S(1)}) custom-call(s32[3]{0:T(128)S(1)} %pad_add_fusion.info_ref, f32[128,8,256]{2,1,0:T(8,128)S(1)} %copy-done, f32[4,8,256]{2,1,0:T(8,128)S(1)} %copy-done.2, ...), custom_call_target="tpu_custom_call" | custom-call | tf_op jit(solution)/shard_map/inner/pallas_call | solution.py:412
  10.0 1.0 collective-permute-done.2.halo_ref
  11.0 0.0 copy-start.1
  11.0 1.1 last.1
  12.1 0.0 copy-start.7
  12.1 3.5 %collective-permute-start.3 = (f32[2,128,256]{2,1,0:T(8,128)S(1)}, f32[2,128,256]{2,1,0:T(8,128)S(1)}, u32[]{:S(2)}, u32[]{:S(2)}) collective-permute-start(f32[2,128,256]{2,1,0:T(8,128)S(1)} %get-tuple-element.37), channel_id=1, source_target_pairs={{0,2},{1,3},{2,4},{3,5},{4,6},{5,7},{8,10},{9,11},{10,12},{11,13},... | collective-permute-start | bytes 786440 | tf_op jit(solution)/shard_map/ppermute | solution.py:481
  16.3 0.0 copy-done.7
  16.3 0.0 copy-start.5
  16.3 0.0 copy-start.6
  16.4 0.6 copy-done.5
  17.0 0.0 copy-done.6
  17.1 0.7 collective-permute-done.halo_ref
  17.8 0.0 copy-done.1
  17.8 1.1 first.1.refs_4_
  18.8 4.1 %collective-permute-start.1 = (f32[8,512]{1,0:T(8,128)S(1)}, f32[8,512]{1,0:T(8,128)S(1)}, u32[]{:S(2)}, u32[]{:S(2)}) collective-permute-start(f32[8,512]{1,0:T(8,128)S(1)} %concatenate.3.mine_ref), channel_id=1, source_target_pairs={{8,15},{9,14},{10,13},{11,12},{12,11},{13,10},{14,9},{15,8},{24,31... | collective-permute-start | bytes 49160 | tf_op jit(solution)/shard_map/ppermute | solution.py:490
  22.9 1.3 %collective-permute-start.8 = (f32[2,128,256]{2,1,0:T(8,128)S(1)}, f32[2,128,256]{2,1,0:T(8,128)S(1)}, u32[]{:S(2)}, u32[]{:S(2)}) collective-permute-start(f32[2,128,256]{2,1,0:T(8,128)S(1)} %first.1.refs_4_), channel_id=1, source_target_pairs={{6,0},{7,1},{14,8},{15,9},{22,16},{23,17},{30,24},{31,25}} | collective-permute-start | bytes 786440 | tf_op jit(solution)/shard_map/ppermute | solution.py:485
  24.2 1.7 %collective-permute-start.4 = (f32[2,128,256]{2,1,0:T(8,128)S(1)}, f32[2,128,256]{2,1,0:T(8,128)S(1)}, u32[]{:S(2)}, u32[]{:S(2)}) collective-permute-start(f32[2,128,256]{2,1,0:T(8,128)S(1)} %get-tuple-element.38), channel_id=1, source_target_pairs={{6,2},{7,3},{0,4},{1,5},{2,6},{3,7},{14,10},{15,11},{8,12},{9,13},... | collective-permute-start | bytes 786440 | tf_op jit(solution)/shard_map/ppermute | solution.py:481
  26.0 6.6 %collective-permute-start.5 = (f32[2,128,256]{2,1,0:T(8,128)S(1)}, f32[2,128,256]{2,1,0:T(8,128)S(1)}, u32[]{:S(2)}, u32[]{:S(2)}) collective-permute-start(f32[2,128,256]{2,1,0:T(8,128)S(1)} %get-tuple-element.39), channel_id=1, source_target_pairs={{4,2},{5,3},{6,4},{7,5},{0,6},{1,7},{12,10},{13,11},{14,12},{15,13... | collective-permute-start | bytes 786440 | tf_op jit(solution)/shard_map/ppermute | solution.py:481
  32.5 0.0 collective-permute-done.1.other_ref
  32.5 1.3 %collective-permute-start.7 = (f32[2,128,256]{2,1,0:T(8,128)S(1)}, f32[2,128,256]{2,1,0:T(8,128)S(1)}, u32[]{:S(2)}, u32[]{:S(2)}) collective-permute-start(f32[2,128,256]{2,1,0:T(8,128)S(1)} %first.1.refs_4_), channel_id=1, source_target_pairs={{4,0},{5,1},{12,8},{13,9},{20,16},{21,17},{28,24},{29,25}} | collective-permute-start | bytes 786440 | tf_op jit(solution)/shard_map/ppermute | solution.py:485
  33.8 0.0 collective-permute-done.3.refs_1_
  33.8 1.3 %collective-permute-start.6 = (f32[2,128,256]{2,1,0:T(8,128)S(1)}, f32[2,128,256]{2,1,0:T(8,128)S(1)}, u32[]{:S(2)}, u32[]{:S(2)}) collective-permute-start(f32[2,128,256]{2,1,0:T(8,128)S(1)} %first.1.refs_4_), channel_id=1, source_target_pairs={{2,0},{3,1},{10,8},{11,9},{18,16},{19,17},{26,24},{27,25}} | collective-permute-start | bytes 786440 | tf_op jit(solution)/shard_map/ppermute | solution.py:485
  35.1 0.0 collective-permute-done.4.refs_2_
  35.2 3.8 %collective-permute-done.5.refs_3_ = f32[2,128,256]{2,1,0:T(8,128)S(1)} collective-permute-done((f32[2,128,256]{2,1,0:T(8,128)S(1)}, f32[2,128,256]{2,1,0:T(8,128)S(1)}, u32[]{:S(2)}, u32[]{:S(2)}) %collective-permute-start.5) | collective-permute-done | bytes 262176 | tf_op jit(solution)/shard_map/ppermute | solution.py:481
  38.9 0.0 collective-permute-done.8.refs_7_
  38.9 13.7 %collective-permute-done.7.refs_6_ = f32[2,128,256]{2,1,0:T(8,128)S(1)} collective-permute-done((f32[2,128,256]{2,1,0:T(8,128)S(1)}, f32[2,128,256]{2,1,0:T(8,128)S(1)}, u32[]{:S(2)}, u32[]{:S(2)}) %collective-permute-start.7) | collective-permute-done | bytes 262176 | tf_op jit(solution)/shard_map/ppermute | solution.py:485
  52.6 0.0 collective-permute-done.6.refs_5_
  52.6 0.7 collect.1
  53.4 0.2 collective-permute-start.9
  53.5 1.9 %collective-permute-start.10 = (f32[4,128,256]{2,1,0:T(8,128)S(1)}, f32[4,128,256]{2,1,0:T(8,128)S(1)}, u32[]{:S(2)}, u32[]{:S(2)}) collective-permute-start(f32[4,128,256]{2,1,0:T(8,128)S(1)} %get-tuple-element.49), channel_id=1, source_target_pairs={{0,2},{2,4},{3,1},{4,6},{5,3},{6,15},{7,5},{8,10},{9,16},{10,12},{... | collective-permute-start | bytes 1572872 | tf_op jit(solution)/shard_map/ppermute | solution.py:518
  55.5 1.9 %collective-permute-start.11 = (f32[4,128,256]{2,1,0:T(8,128)S(1)}, f32[4,128,256]{2,1,0:T(8,128)S(1)}, u32[]{:S(2)}, u32[]{:S(2)}) collective-permute-start(f32[4,128,256]{2,1,0:T(8,128)S(1)} %get-tuple-element.50), channel_id=1, source_target_pairs={{1,2},{3,4},{2,1},{5,6},{4,3},{7,15},{6,5},{9,10},{8,16},{11,12},{... | collective-permute-start | bytes 1572872 | tf_op jit(solution)/shard_map/ppermute | solution.py:519
  57.4 0.0 collective-permute-done.9.far_ref
  57.4 4.0 %prepare.1 = (bf16[1024,512]{1,0:T(8,128)(2,1)S(1)}, bf16[1024,512]{1,0:T(8,128)(2,1)S(1)}, bf16[256,1024]{1,0:T(8,128)(2,1)S(1)}, bf16[256,1024]{1,0:T(8,128)(2...) custom-call(s32[3]{0:T(128)S(1)} %pad_add_fusion.info_ref, ...), custom_call_target="tpu_custom_call" | custom-call | flops 1073741824 | tf_op jit(solution)/shard_map/prepare/pallas_call | solution.py:412
  61.4 6.6 %collective-permute-done.10.first_ref = f32[4,128,256]{2,1,0:T(8,128)S(1)} collective-permute-done((f32[4,128,256]{2,1,0:T(8,128)S(1)}, f32[4,128,256]{2,1,0:T(8,128)S(1)}, u32[]{:S(2)}, u32[]{:S(2)}) %collective-permute-start.10) | collective-permute-done | bytes 524320 | tf_op jit(solution)/shard_map/ppermute | solution.py:518
  68.0 2.6 %collective-permute-done.11.second_ref = f32[4,128,256]{2,1,0:T(8,128)S(1)} collective-permute-done((f32[4,128,256]{2,1,0:T(8,128)S(1)}, f32[4,128,256]{2,1,0:T(8,128)S(1)}, u32[]{:S(2)}, u32[]{:S(2)}) %collective-permute-start.11) | collective-permute-done | bytes 524320 | tf_op jit(solution)/shard_map/ppermute | solution.py:519
  70.5 0.0 copy-done.3
  70.5 9.7 %region.1 = f32[8,128,256]{2,1,0:T(8,128)S(1)} custom-call(s32[3]{0:T(128)S(1)} %pad_add_fusion.info_ref, f32[8,512]{1,0:T(8,128)S(1)} %get-tuple-element.40.observed_ref, f32[2,4,128,256]{3,2,1,0:T(8,128)S(1)} %get-tuple-element.41.near_ref, f32[2,4,128,256]{3,2,1,0:T(8,128)S(1)} %collective-permute-done.9.far_ref, ...), custom_call_target="tpu_custom_call" | custom-call | tf_op jit(solution)/shard_map/region/pallas_call | solution.py:412
  80.2 30.0 %all_to_all.5.rows_ref = f32[8,128,256]{2,1,0:T(8,128)} all-to-all(f32[8,128,256]{2,1,0:T(8,128)S(1)} %region.1), channel_id=1, replica_groups=mesh['patch'=4,'member'=8] {'member'}, dimensions={0} | all-to-all | bytes 2097152 | tf_op jit(solution)/shard_map/all_to_all | solution.py:536
  110.2 3.5 %unpack.1 = f32[128,8,256]{2,1,0:T(8,128)} custom-call(s32[3]{0:T(128)} %copy-done.3, f32[8,128,256]{2,1,0:T(8,128)} %all_to_all.5.rows_ref), custom_call_target="tpu_custom_call" | custom-call | tf_op jit(solution)/shard_map/unpack/pallas_call | solution.py:538
  (3 shorter events, 0.0 us)
Async XLA Ops:
  0.0 0.8 copy-start.2
  0.8 1.2 %copy-start = (f32[128,8,256]{2,1,0:T(8,128)S(1)}, f32[128,8,256]{2,1,0:T(8,128)}, u32[]{:S(2)}) copy-start(f32[128,8,256]{2,1,0:T(8,128)} %field_ref.7) | copy-start | bytes 3145732
  2.0 68.6 %copy-start.3 = (s32[3]{0:T(128)}, s32[3]{0:T(128)S(1)}, u32[]{:S(2)}) copy-start(s32[3]{0:T(128)S(1)} %pad_add_fusion.info_ref) | copy-start | bytes 40
  2.7 8.3 %collective-permute-start.2 = (f32[264,256]{1,0:T(8,128)S(1)}, f32[264,256]{1,0:T(8,128)S(1)}, u32[]{:S(2)}, u32[]{:S(2)}) collective-permute-start(f32[264,256]{1,0:T(8,128)S(1)} %get-tuple-element.31), channel_id=1, source_target_pairs={{0,8},{16,24},{8,0},{24,16},{1,9},{17,25},{9,1},{25,17},{2,10},{18... | collective-permute-start | bytes 811016 | tf_op jit(solution)/shard_map/ppermute | solution.py:451
  2.8 5.0 %copy-start.4 = (f32[128]{0:T(128)S(1)}, f32[128]{0:T(128)}, u32[]{:S(2)}) copy-start(f32[128]{0:T(128)} %param.9) | copy-start | bytes 1540
  2.8 14.9 %collective-permute-start = (f32[264,256]{1,0:T(8,128)S(1)}, f32[264,256]{1,0:T(8,128)S(1)}, u32[]{:S(2)}, u32[]{:S(2)}) collective-permute-start(f32[264,256]{1,0:T(8,128)S(1)} %get-tuple-element.29), channel_id=1, source_target_pairs={{8,16},{16,8},{9,17},{17,9},{10,18},{18,10},{11,19},{19,11},{12,20... | collective-permute-start | bytes 811016 | tf_op jit(solution)/shard_map/ppermute | solution.py:451
  11.0 6.8 %copy-start.1 = (f32[128,8,256]{2,1,0:T(8,128)S(1)}, f32[128,8,256]{2,1,0:T(8,128)}, u32[]{:S(2)}) copy-start(f32[128,8,256]{2,1,0:T(8,128)} %field_ref.7) | copy-start | bytes 3145732
  12.1 4.2 %copy-start.7 = (s32[1,512]{1,0:T(1,128)S(1)}, s32[1,512]{1,0:T(1,128)}, u32[]{:S(2)}) copy-start(s32[1,512]{1,0:T(1,128)} %param.10) | copy-start | bytes 6148
  12.1 21.7 %collective-permute-start.3 = (f32[2,128,256]{2,1,0:T(8,128)S(1)}, f32[2,128,256]{2,1,0:T(8,128)S(1)}, u32[]{:S(2)}, u32[]{:S(2)}) collective-permute-start(f32[2,128,256]{2,1,0:T(8,128)S(1)} %get-tuple-element.37), channel_id=1, source_target_pairs={{0,2},{1,3},{2,4},{3,5},{4,6},{5,7},{8,10},{9,11},{10,12},{11,13},... | collective-permute-start | bytes 786440 | tf_op jit(solution)/shard_map/ppermute | solution.py:481
  16.3 0.7 copy-start.5
  16.3 0.7 copy-start.6
  18.8 13.7 %collective-permute-start.1 = (f32[8,512]{1,0:T(8,128)S(1)}, f32[8,512]{1,0:T(8,128)S(1)}, u32[]{:S(2)}, u32[]{:S(2)}) collective-permute-start(f32[8,512]{1,0:T(8,128)S(1)} %concatenate.3.mine_ref), channel_id=1, source_target_pairs={{8,15},{9,14},{10,13},{11,12},{12,11},{13,10},{14,9},{15,8},{24,31... | collective-permute-start | bytes 49160 | tf_op jit(solution)/shard_map/ppermute | solution.py:490
  22.9 16.0 %collective-permute-start.8 = (f32[2,128,256]{2,1,0:T(8,128)S(1)}, f32[2,128,256]{2,1,0:T(8,128)S(1)}, u32[]{:S(2)}, u32[]{:S(2)}) collective-permute-start(f32[2,128,256]{2,1,0:T(8,128)S(1)} %first.1.refs_4_), channel_id=1, source_target_pairs={{6,0},{7,1},{14,8},{15,9},{22,16},{23,17},{30,24},{31,25}} | collective-permute-start | bytes 786440 | tf_op jit(solution)/shard_map/ppermute | solution.py:485
  24.2 10.9 %collective-permute-start.4 = (f32[2,128,256]{2,1,0:T(8,128)S(1)}, f32[2,128,256]{2,1,0:T(8,128)S(1)}, u32[]{:S(2)}, u32[]{:S(2)}) collective-permute-start(f32[2,128,256]{2,1,0:T(8,128)S(1)} %get-tuple-element.38), channel_id=1, source_target_pairs={{6,2},{7,3},{0,4},{1,5},{2,6},{3,7},{14,10},{15,11},{8,12},{9,13},... | collective-permute-start | bytes 786440 | tf_op jit(solution)/shard_map/ppermute | solution.py:481
  26.0 13.0 %collective-permute-start.5 = (f32[2,128,256]{2,1,0:T(8,128)S(1)}, f32[2,128,256]{2,1,0:T(8,128)S(1)}, u32[]{:S(2)}, u32[]{:S(2)}) collective-permute-start(f32[2,128,256]{2,1,0:T(8,128)S(1)} %get-tuple-element.39), channel_id=1, source_target_pairs={{4,2},{5,3},{6,4},{7,5},{0,6},{1,7},{12,10},{13,11},{14,12},{15,13... | collective-permute-start | bytes 786440 | tf_op jit(solution)/shard_map/ppermute | solution.py:481
  32.5 20.1 %collective-permute-start.7 = (f32[2,128,256]{2,1,0:T(8,128)S(1)}, f32[2,128,256]{2,1,0:T(8,128)S(1)}, u32[]{:S(2)}, u32[]{:S(2)}) collective-permute-start(f32[2,128,256]{2,1,0:T(8,128)S(1)} %first.1.refs_4_), channel_id=1, source_target_pairs={{4,0},{5,1},{12,8},{13,9},{20,16},{21,17},{28,24},{29,25}} | collective-permute-start | bytes 786440 | tf_op jit(solution)/shard_map/ppermute | solution.py:485
  33.8 18.8 %collective-permute-start.6 = (f32[2,128,256]{2,1,0:T(8,128)S(1)}, f32[2,128,256]{2,1,0:T(8,128)S(1)}, u32[]{:S(2)}, u32[]{:S(2)}) collective-permute-start(f32[2,128,256]{2,1,0:T(8,128)S(1)} %first.1.refs_4_), channel_id=1, source_target_pairs={{2,0},{3,1},{10,8},{11,9},{18,16},{19,17},{26,24},{27,25}} | collective-permute-start | bytes 786440 | tf_op jit(solution)/shard_map/ppermute | solution.py:485
  53.4 4.0 %collective-permute-start.9 = (f32[2,4,128,256]{3,2,1,0:T(8,128)S(1)}, f32[2,4,128,256]{3,2,1,0:T(8,128)S(1)}, u32[]{:S(2)}, u32[]{:S(2)}) collective-permute-start(f32[2,4,128,256]{3,2,1,0:T(8,128)S(1)} %get-tuple-element.41.near_ref), channel_id=1, source_target_pairs={{0,1},{1,0},{2,3},{3,2},{4,5},{5,4},{6,7},{7,6},{8,9},{9,8},{10,11... | collective-permute-start | bytes 3145736 | tf_op jit(solution)/shard_map/ppermute | solution.py:517
  53.5 14.4 %collective-permute-start.10 = (f32[4,128,256]{2,1,0:T(8,128)S(1)}, f32[4,128,256]{2,1,0:T(8,128)S(1)}, u32[]{:S(2)}, u32[]{:S(2)}) collective-permute-start(f32[4,128,256]{2,1,0:T(8,128)S(1)} %get-tuple-element.49), channel_id=1, source_target_pairs={{0,2},{2,4},{3,1},{4,6},{5,3},{6,15},{7,5},{8,10},{9,16},{10,12},{... | collective-permute-start | bytes 1572872 | tf_op jit(solution)/shard_map/ppermute | solution.py:518
  55.5 15.1 %collective-permute-start.11 = (f32[4,128,256]{2,1,0:T(8,128)S(1)}, f32[4,128,256]{2,1,0:T(8,128)S(1)}, u32[]{:S(2)}, u32[]{:S(2)}) collective-permute-start(f32[4,128,256]{2,1,0:T(8,128)S(1)} %get-tuple-element.50), channel_id=1, source_target_pairs={{1,2},{3,4},{2,1},{5,6},{4,3},{7,15},{6,5},{9,10},{8,16},{11,12},{... | collective-permute-start | bytes 1572872 | tf_op jit(solution)/shard_map/ppermute | solution.py:519

commit v7 on v5

--- a/solution.py
+++ b/solution.py
@@ -9,7 +9,7 @@
 from jax.sharding import PartitionSpec as P
 
 STEPS = 2
-COARSE = 0.06
+COARSE = 0.2
 DONE = 0.01
 LARGE = 2e4
 PART = 256
@@ -77,17 +77,19 @@
             weight_ref[row, pl.ds(i, 1), :] = weight
 
 
-def inner_kernel(info_ref, field_ref, flow_ref, emission_ref, *refs):
+def inner_kernel(info_ref, field_ref, flow_ref, emission_ref, kept_ref, *refs):
     out_refs, (wide_ref, weight_ref) = refs[:-2], refs[-2:]
     rows = field_ref.shape[1]
     chips = len(out_refs)
     emission = emission_column(emission_ref)
-    store_weights(flow_ref, weight_ref, range(rows))
+    store_weights(flow_ref, weight_ref, range(2, rows - 2))
     for row in range(1, rows - 1):
         wide_ref[row] = advance(
             weights_of(flow_ref[:, row, :]), emission,
             field_ref[:, row - 1, :], field_ref[:, row, :], field_ref[:, row + 1, :],
         )
+    for place, row in enumerate((1, 2, rows - 3, rows - 2)):
+        kept_ref[place] = wide_ref[row]
 
     def target(s):
         chip = lax.rem(info_ref[0] + s, chips)
@@ -96,7 +98,7 @@
     second_step(info_ref, target, 0, emission, wide_ref, weight_ref, out_refs)
 
 
-def edge_kernel(info_ref, field_ref, flow_ref, emission_ref, before_ref, after_ref, *refs):
+def edge_kernel(info_ref, field_ref, flow_ref, emission_ref, kept_ref, before_ref, after_ref, *refs):
     out_refs, (wide_ref, weight_ref) = refs[:-2], refs[-2:]
     members, rows, width = field_ref.shape
     chips = len(out_refs)
@@ -117,7 +119,9 @@
             return after_ref[pl.ds((row - rows) * members, members), :]
         return field_ref[:, row, :]
 
-    for row in (-1, 0, 1, 2, rows - 3, rows - 2, rows - 1, rows):
+    for place, row in enumerate((1, 2, rows - 3, rows - 2)):
+        wide_ref[row + 1] = kept_ref[place]
+    for row in (-1, 0, rows - 1, rows):
         wide_ref[row + 1] = advance(
             weights_of(flow_row(row)), emission, start_row(row - 1), start_row(row), start_row(row + 1)
         )
@@ -129,16 +133,16 @@
     second_step(info_ref, target, 1, emission, wide_ref, weight_ref, out_refs)
 
 
-def collect_kernel(info_ref, mine_ref, other_ref, *refs):
+def collect_kernel(order, info_ref, mine_ref, other_ref, *refs):
     chips = (len(refs) - 4) // 2
     both_ref, first_ref, second_ref, observed_ref = refs[-4:]
     observed_ref[...] = jnp.where(info_ref[2] == 1, other_ref[...], mine_ref[...])
     chip, core = info_ref[0], info_ref[1]
     at_edge = jnp.logical_or(chip == 0, chip == chips - 1)
-    for s in range(chips):
-        turn, mirror = lax.rem(chip + chips - s, chips), jnp.where(chip == 0, s, chips - 1 - s)
+    for index, (s, k) in enumerate(order):
+        turn, mirror = lax.rem(chip + chips - s, chips), jnp.where(chip == 0, k, chips - 1 - k)
         for ref, here, block in (
-            (refs[s], jnp.logical_not(at_edge), turn), (refs[chips + s], at_edge, mirror)
+            (refs[index], jnp.logical_not(at_edge), turn), (refs[chips + index], at_edge, mirror)
         ):
 
             @pl.when(here)
@@ -150,10 +154,9 @@
                 second_ref[block] = own
 
 
-def unpack_kernel(info_ref, rows_ref, out_ref):
-    rows = rows_ref.shape[0]
-    for row in range(rows):
-        out_ref[:, row, :] = rows_ref[row + info_ref[2] * (rows - 1 - 2 * row)]
+def unpack_kernel(rows_ref, out_ref):
+    for row in range(rows_ref.shape[0]):
+        out_ref[:, row, :] = rows_ref[row]
 
 
 def pieces(x, count):
@@ -399,17 +402,16 @@
             block = blocks[part * chips + chip]
             moved = product([spread_high[block, :], spread_low[block, :]], halved)
             moved = moved + doubled(direction_ref[block, :]) * along
-            out_ref[2 * chip + jnp.abs(core - part)] = ref[place, chip] + shift + moved
+            lane = 2 * chip + jnp.abs(core - part)
+            lane = lane + info_ref[2] * (2 * chips - 1 - 2 * lane)
+            out_ref[lane] = ref[place, chip] + shift + moved
 
 
 VMEM = pl.BlockSpec(memory_space=pltpu.VMEM)
-LIMIT = pltpu.CompilerParams(vmem_limit_bytes=32 * 1024 * 1024)
-
-
 SMEM = pl.BlockSpec(memory_space=pltpu.SMEM)
 
 
-def call(kernel, name, out_shape, args, scratch=(), flops=None):
+def call(kernel, name, out_shape, args, scratch=(), flops=None, aliases={}, limit=8):
     several = isinstance(out_shape, (list, tuple))
     return pl.pallas_call(
         kernel,
@@ -417,7 +419,8 @@
         in_specs=[SMEM] + [VMEM] * (len(args) - 1),
         out_specs=[VMEM] * len(out_shape) if several else VMEM,
         scratch_shapes=scratch,
-        compiler_params=LIMIT,
+        input_output_aliases=aliases,
+        compiler_params=pltpu.CompilerParams(vmem_limit_bytes=limit * 1024 * 1024),
         cost_estimate=flops and pl.CostEstimate(flops=flops, bytes_accessed=0, transcendentals=0),
         name=name,
     )(*args)
@@ -446,8 +449,7 @@
 
     edge = array(STEPS * step + 8, width)
     tail, head = pl.pallas_call(
-        pack_kernel, out_shape=(edge, edge), in_specs=[VMEM] * 2, out_specs=(VMEM, VMEM),
-        compiler_params=LIMIT, name="pack",
+        pack_kernel, out_shape=(edge, edge), in_specs=[VMEM] * 2, out_specs=(VMEM, VMEM), name="pack",
     )(init_field, flow_fields)
     before = lax.ppermute(tail, "patch", [(i, i + 1) for i in range(patches - 1)])
     after = lax.ppermute(head, "patch", [(i + 1, i) for i in range(patches - 1)])
@@ -474,21 +476,22 @@
     pair = array(2, step, width)
     wide = [pltpu.VMEM((rows + 2, step, width), F32), pltpu.VMEM((rows, 8, width), F32)]
     args = [info, init_field, flow_fields, emission[None, :]]
-    inner = call(inner_kernel, "inner", [pair] * chips, args, wide)
+    kept, *inner = call(inner_kernel, "inner", [array(4, step, width)] + [pair] * chips, args, wide)
     order = [s for near in range(chips // 2, 0, -1) for s in sorted({near, chips - near})]
     got_inner = {s: along(inner[s], s, False) for s in order}
-    outer = call(edge_kernel, "edge", [pair] * chips, args + [before, after], wide)
+    outer = call(edge_kernel, "edge", [pair] * chips, args + [kept, before, after], wide)
     mine, _ = lax.optimization_barrier((mine, outer[0]))
     other = lax.ppermute(
         mine, axes,
         [(p * lanes + i, p * lanes + lanes - 1 - i) for p in range(1, patches, 2) for i in range(lanes)],
     )
     got_outer = {s: along(outer[s], s, True) for s in range(chips - 1, 0, -1)}
-    pieces_in = [inner[0]] + [got_inner[s] for s in range(1, chips)]
-    pieces_in += [outer[0]] + [got_outer[s] for s in range(1, chips)]
+    got_inner[0], got_outer[0] = inner[0], outer[0]
+    order = list(zip(order + [0], range(chips - 1, -1, -1)))
+    pieces_in = [got_inner[s] for s, _ in order] + [got_outer[k] for _, k in order]
     half_row = array(chips, step, width)
     near, first, second, observed = call(
-        collect_kernel, "collect", [array(2, chips, step, width), half_row, half_row, array(8, slots)],
+        functools.partial(collect_kernel, order), "collect", [array(2, chips, step, width), half_row, half_row, array(8, slots)],
         [info, mine, other] + pieces_in,
     )
 
@@ -521,15 +524,21 @@
         + [array(width, width // 2), array(8, slots), array(members, width // 2)],
         [info, observed, near, far],
         [pltpu.VMEM((members, 2 * width), F32)] + [pltpu.VMEM((members, 2 * width), BF16)] * 2,
-        flops=8 * members * slots * width,
+        flops=8 * members * slots * width, limit=20,
     )
     analysed = call(
         region_kernel, "region", array(lanes, step, width),
         [info, observed, near, far, *prepared, got_first, got_second],
         split + [pltpu.VMEM((slots, slots), F32), pltpu.VMEM((width + 8, slots), F32)],
-    )
-    returned = lax.all_to_all(analysed, "member", split_axis=0, concat_axis=0, tiled=True)
-    return call(unpack_kernel, "unpack", array(step, rows, width), [info, returned])
+        limit=24,
+    )
+    groups = [[p * lanes + (lanes - 1 - i if p % 2 else i) for i in range(lanes)] for p in range(patches)]
+    returned = lax.all_to_all(
+        analysed, axes, split_axis=0, concat_axis=0, tiled=True, axis_index_groups=groups
+    )
+    return pl.pallas_call(
+        unpack_kernel, out_shape=array(step, rows, width), in_specs=[VMEM], out_specs=VMEM, name="unpack",
+    )(returned)
 
 
 def solution(mesh):

time: 108 us -> 109 us (level)
  waiting for transfers between devices: 18.2 us -> 21 us
  local copies, waits for them, and re-layouts: 3.36 us -> 1.38 us
    pallas_call x6 -> x5, Pallas kernels: 25.3 us -> 21.5 us  [call(): pl.pallas_call(kernel, out_shape=out_shape, in_specs=[SMEM] + [VMEM] * (l...]
    pallas_call x0 -> x1, Pallas kernels: none -> 2.54 us  [per_device(): pl.pallas_call(unpack_kernel, out_shape=array(step, rows, width), in_spec...]
    pallas_call x1, Pallas kernels: 0.17 us -> 2.2 us  [per_device(): pl.pallas_call(pack_kernel, out_shape=(edge, edge), in_specs=[VMEM] * 2,...]
    unnamed x16 -> x12, local copies, waits for them, and re-layouts: 3.32 us -> 1.34 us
    ppermute x6, waiting for transfers between devices: 5.31 us -> 6.79 us  [along(): lax.ppermute(piece, 'member', [(2 * a + core, 2 * b + core) for a, b in h...]
  transfers between devices with their start and end apart: 12 -> 12, of which waited for: 5 -> 6; matrix products, arithmetic and copies ran while one was open for 0% -> 0% of each run, Pallas kernels for 9% -> 8%
where the time goes in v7:
time: 109 us; the launch traced here: 107 us
  blocking collectives  29.4 us (27%)
  starting transfers between devices  28 us (26%)
  Pallas kernels  26.2 us (24%)
  waiting for transfers between devices  21 us (19%)
  local copies, waits for them, and re-layouts  1.38 us (1%)
    all_to_all x1, blocking collectives, per_device(): lax.all_to_all(analysed, axes, split_axis=0, concat_axis=0, tiled=True, a...  29.4 us
    pallas_call x5, Pallas kernels, call(): pl.pallas_call(kernel, out_shape=out_shape, in_specs=[SMEM] + [VMEM] * (l...  21.5 us
    ppermute x6, starting transfers between devices, along(): lax.ppermute(piece, 'member', [(2 * a + core, 2 * b + core) for a, b in h...  14.6 us
    ppermute x6, waiting for transfers between devices, along(): lax.ppermute(piece, 'member', [(2 * a + core, 2 * b + core) for a, b in h...  6.79 us
    ppermute x1, waiting for transfers between devices, per_device(): lax.ppermute(mine, axes, [(p * lanes + i, p * lanes + lanes - 1 - i) for...  5.07 us
    ppermute x1, waiting for transfers between devices, per_device(): got_first = lax.ppermute(first, axes, first_pairs)  4.83 us
    ppermute x1, starting transfers between devices, per_device(): got_second = lax.ppermute(second, axes, second_pairs)  3.65 us
    ppermute x1, starting transfers between devices, per_device(): lax.ppermute(tail, 'patch', [(i, i + 1) for i in range(patches - 1)])  3.39 us
  transfers between devices with their start and end apart: 12, of which 6 were waited for; matrix products, arithmetic and copies ran while one was open for 0% of the time, Pallas kernels for 8%

profile of v7, /device:TPU:2, one launch (start us, length us, event | category | flops | bytes accessed | tf_op | source)
XLA Modules:
  0.0 107.0 jit_solution(4976531324774892582)
XLA Ops:
  0.0 0.0 copy-start
  0.0 2.2 %pack.1 = (f32[264,256]{1,0:T(8,128)}, f32[264,256]{1,0:T(8,128)}) custom-call(f32[128,8,256]{2,1,0:T(8,128)} %field_ref.5, f32[4,8,256]{2,1,0:T(8,128)} %flow_ref.5), custom_call_target="tpu_custom_call" | custom-call | tf_op jit(solution)/shard_map/pack/pallas_call | solution.py:451
  2.2 3.4 %collective-permute-start = (f32[264,256]{1,0:T(8,128)}, f32[264,256]{1,0:T(8,128)S(1)}, u32[]{:S(2)}, u32[]{:S(2)}) collective-permute-start(f32[264,256]{1,0:T(8,128)} %get-tuple-element.29), channel_id=1, source_target_pairs={{0,8},{8,16},{16,24},{1,9},{9,17},{17,25},{2,10},{10,18},{18,26},{... | collective-permute-start | bytes 811016 | tf_op jit(solution)/shard_map/ppermute | solution.py:454
  5.6 2.5 %collective-permute-start.1 = (f32[264,256]{1,0:T(8,128)}, f32[264,256]{1,0:T(8,128)S(1)}, u32[]{:S(2)}, u32[]{:S(2)}) collective-permute-start(f32[264,256]{1,0:T(8,128)} %get-tuple-element.30), channel_id=1, source_target_pairs={{8,0},{16,8},{24,16},{9,1},{17,9},{25,17},{10,2},{18,10},{26,18},{... | collective-permute-start | bytes 811016 | tf_op jit(solution)/shard_map/ppermute | solution.py:455
  8.1 0.0 copy-start.1
  8.1 0.1 pad_add_fusion.info_ref
  8.2 0.0 copy-start.2
  8.2 0.0 copy-done
  8.2 0.6 copy-done.1
  8.8 0.0 copy-done.2
  8.8 2.1 %inner.1 = (f32[4,128,256]{2,1,0:T(8,128)S(1)}, f32[2,128,256]{2,1,0:T(8,128)S(1)}, f32[2,128,256]{2,1,0:T(8,128)S(1)}, f32[2,128,256]{2,1,0:T(8,128)S(1)}, f32[2,128,256]{2,1,0:T(8,128)S(1)}) custom-call(s32[3]{0:T(128)S(1)} %pad_add_fusion.info_ref, f32[128,8,256]{2,1,0:T(8,128)S(1)} %copy-done, f32[4,8,256]{2,1,0:T(8,128)S(1)} %copy-done.1, ...), custom_call_target="tpu_custom_call" | custom-call | tf_op jit(solution)/shard_map/inner/pallas_call | solution.py:416
  11.0 4.5 %collective-permute-start.3 = (f32[2,128,256]{2,1,0:T(8,128)S(1)}, f32[2,128,256]{2,1,0:T(8,128)S(1)}, u32[]{:S(2)}, u32[]{:S(2)}) collective-permute-start(f32[2,128,256]{2,1,0:T(8,128)S(1)} %get-tuple-element.33), channel_id=1, source_target_pairs={{0,4},{1,5},{6,2},{7,3},{8,12},{9,13},{14,10},{15,11},{16,20},{17,... | collective-permute-start | bytes 786440 | tf_op jit(solution)/shard_map/ppermute | solution.py:474
  15.5 1.3 %collective-permute-start.4 = (f32[2,128,256]{2,1,0:T(8,128)S(1)}, f32[2,128,256]{2,1,0:T(8,128)S(1)}, u32[]{:S(2)}, u32[]{:S(2)}) collective-permute-start(f32[2,128,256]{2,1,0:T(8,128)S(1)} %get-tuple-element.34), channel_id=1, source_target_pairs={{0,2},{1,3},{2,4},{3,5},{8,10},{9,11},{10,12},{11,13},{16,18},{17,... | collective-permute-start | bytes 786440 | tf_op jit(solution)/shard_map/ppermute | solution.py:474
  16.8 0.7 collective-permute-start.5
  17.5 0.0 collective-permute-done.before_ref
  17.5 1.8 %collective-permute-done.1.after_ref = f32[264,256]{1,0:T(8,128)S(1)} collective-permute-done((f32[264,256]{1,0:T(8,128)}, f32[264,256]{1,0:T(8,128)S(1)}, u32[]{:S(2)}, u32[]{:S(2)}) %collective-permute-start.1) | collective-permute-done | bytes 270368 | tf_op jit(solution)/shard_map/ppermute | solution.py:455
  19.3 2.5 %edge.1 = (f32[2,128,256]{2,1,0:T(8,128)S(1)}, f32[2,128,256]{2,1,0:T(8,128)}, f32[2,128,256]{2,1,0:T(8,128)}, f32[2,128,256]{2,1,0:T(8,128)}) custom-call(s32[3]{0:T(128)S(1)} %pad_add_fusion.info_ref, f32[128,8,256]{2,1,0:T(8,128)S(1)} %copy-done, f32[4,8,256]{2,1,0:T(8,128)S(1)} %copy-done.1, f32[1,128]{1,0:T(1,128)S(1)} %bitcast.6, ...), custom_call_target="tpu_custom_call" | custom-call | tf_op jit(solution)/shard_map/edge/pallas_call | solution.py:416
  21.7 5.5 %collective-permute-start.6 = (f32[2,128,256]{2,1,0:T(8,128)}, f32[2,128,256]{2,1,0:T(8,128)S(1)}, u32[]{:S(2)}, u32[]{:S(2)}) collective-permute-start(f32[2,128,256]{2,1,0:T(8,128)} %get-tuple-element.37), channel_id=1, source_target_pairs={{6,0},{7,1},{0,6},{1,7},{14,8},{15,9},{8,14},{9,15},{22,16},{23,17... | collective-permute-start | bytes 786440 | tf_op jit(solution)/shard_map/ppermute | solution.py:474
  27.2 1.3 %collective-permute-start.7 = (f32[2,128,256]{2,1,0:T(8,128)}, f32[2,128,256]{2,1,0:T(8,128)S(1)}, u32[]{:S(2)}, u32[]{:S(2)}) collective-permute-start(f32[2,128,256]{2,1,0:T(8,128)} %get-tuple-element.38), channel_id=1, source_target_pairs={{4,0},{5,1},{2,6},{3,7},{12,8},{13,9},{10,14},{11,15},{20,16},{21,... | collective-permute-start | bytes 786440 | tf_op jit(solution)/shard_map/ppermute | solution.py:474
  28.5 0.0 collective-permute-done.3.refs_0_
  28.6 0.0 copy-start.5
  28.6 1.3 %collective-permute-start.8 = (f32[2,128,256]{2,1,0:T(8,128)}, f32[2,128,256]{2,1,0:T(8,128)S(1)}, u32[]{:S(2)}, u32[]{:S(2)}) collective-permute-start(f32[2,128,256]{2,1,0:T(8,128)} %get-tuple-element.39), channel_id=1, source_target_pairs={{2,0},{3,1},{4,6},{5,7},{10,8},{11,9},{12,14},{13,15},{18,16},{19,... | collective-permute-start | bytes 786440 | tf_op jit(solution)/shard_map/ppermute | solution.py:474
  30.5 0.0 copy-done.5
  30.5 0.0 copy-start.3
  30.5 0.0 copy-start.4
  30.6 0.6 copy-done.3
  31.2 0.0 copy-done.4
  31.3 0.0 collective-permute-done.4.refs_1_
  31.3 1.9 %collective-permute-start.2 = (f32[8,512]{1,0:T(8,128)S(1)}, f32[8,512]{1,0:T(8,128)S(1)}, u32[]{:S(2)}, u32[]{:S(2)}) collective-permute-start(f32[8,512]{1,0:T(8,128)S(1)} %concatenate.3.mine_ref), channel_id=1, source_target_pairs={{8,15},{9,14},{10,13},{11,12},{12,11},{13,10},{14,9},{15,8},{24,31... | collective-permute-start | bytes 49160 | tf_op jit(solution)/shard_map/ppermute | solution.py:484
  33.2 0.0 collective-permute-done.5.refs_2_
  33.2 5.1 %collective-permute-done.2.other_ref = f32[8,512]{1,0:T(8,128)S(1)} collective-permute-done((f32[8,512]{1,0:T(8,128)S(1)}, f32[8,512]{1,0:T(8,128)S(1)}, u32[]{:S(2)}, u32[]{:S(2)}) %collective-permute-start.2) | collective-permute-done | bytes 16416 | tf_op jit(solution)/shard_map/ppermute | solution.py:484
  38.3 0.0 collective-permute-done.6.refs_4_
  38.3 1.4 %collective-permute-done.7.refs_5_ = f32[2,128,256]{2,1,0:T(8,128)S(1)} collective-permute-done((f32[2,128,256]{2,1,0:T(8,128)}, f32[2,128,256]{2,1,0:T(8,128)S(1)}, u32[]{:S(2)}, u32[]{:S(2)}) %collective-permute-start.7) | collective-permute-done | bytes 262176 | tf_op jit(solution)/shard_map/ppermute | solution.py:474
  39.7 5.4 %collective-permute-done.8.refs_6_ = f32[2,128,256]{2,1,0:T(8,128)S(1)} collective-permute-done((f32[2,128,256]{2,1,0:T(8,128)}, f32[2,128,256]{2,1,0:T(8,128)S(1)}, u32[]{:S(2)}, u32[]{:S(2)}) %collective-permute-start.8) | collective-permute-done | bytes 262176 | tf_op jit(solution)/shard_map/ppermute | solution.py:474
  45.1 0.7 collect.1
  45.8 0.1 collective-permute-start.9
  45.9 1.9 %collective-permute-start.10 = (f32[4,128,256]{2,1,0:T(8,128)S(1)}, f32[4,128,256]{2,1,0:T(8,128)S(1)}, u32[]{:S(2)}, u32[]{:S(2)}) collective-permute-start(f32[4,128,256]{2,1,0:T(8,128)S(1)} %get-tuple-element.49), channel_id=1, source_target_pairs={{0,2},{2,4},{3,1},{4,6},{5,3},{6,15},{7,5},{8,10},{9,16},{10,12},{... | collective-permute-start | bytes 1572872 | tf_op jit(solution)/shard_map/ppermute | solution.py:517
  47.8 3.7 %collective-permute-start.11 = (f32[4,128,256]{2,1,0:T(8,128)S(1)}, f32[4,128,256]{2,1,0:T(8,128)S(1)}, u32[]{:S(2)}, u32[]{:S(2)}) collective-permute-start(f32[4,128,256]{2,1,0:T(8,128)S(1)} %get-tuple-element.50), channel_id=1, source_target_pairs={{1,2},{3,4},{2,1},{5,6},{4,3},{7,15},{6,5},{9,10},{8,16},{11,12},{... | collective-permute-start | bytes 1572872 | tf_op jit(solution)/shard_map/ppermute | solution.py:518
  51.5 0.0 collective-permute-done.9.far_ref
  51.5 4.0 %prepare.1 = (bf16[1024,512]{1,0:T(8,128)(2,1)S(1)}, bf16[1024,512]{1,0:T(8,128)(2,1)S(1)}, bf16[256,1024]{1,0:T(8,128)(2,1)S(1)}, bf16[256,1024]{1,0:T(8,128)(2...) custom-call(s32[3]{0:T(128)S(1)} %pad_add_fusion.info_ref, ...), custom_call_target="tpu_custom_call" | custom-call | flops 1073741824 | tf_op jit(solution)/shard_map/prepare/pallas_call | solution.py:416
  55.5 4.8 %collective-permute-done.10.first_ref = f32[4,128,256]{2,1,0:T(8,128)S(1)} collective-permute-done((f32[4,128,256]{2,1,0:T(8,128)S(1)}, f32[4,128,256]{2,1,0:T(8,128)S(1)}, u32[]{:S(2)}, u32[]{:S(2)}) %collective-permute-start.10) | collective-permute-done | bytes 524320 | tf_op jit(solution)/shard_map/ppermute | solution.py:517
  60.3 2.6 %collective-permute-done.11.second_ref = f32[4,128,256]{2,1,0:T(8,128)S(1)} collective-permute-done((f32[4,128,256]{2,1,0:T(8,128)S(1)}, f32[4,128,256]{2,1,0:T(8,128)S(1)}, u32[]{:S(2)}, u32[]{:S(2)}) %collective-permute-start.11) | collective-permute-done | bytes 524320 | tf_op jit(solution)/shard_map/ppermute | solution.py:518
  62.9 12.2 %region.1 = f32[8,128,256]{2,1,0:T(8,128)S(1)} custom-call(s32[3]{0:T(128)S(1)} %pad_add_fusion.info_ref, f32[8,512]{1,0:T(8,128)S(1)} %get-tuple-element.40.observed_ref, f32[2,4,128,256]{3,2,1,0:T(8,128)S(1)} %get-tuple-element.41.near_ref, f32[2,4,128,256]{3,2,1,0:T(8,128)S(1)} %collective-permute-done.9.far_ref, ...), custom_call_target="tpu_custom_call" | custom-call | tf_op jit(solution)/shard_map/region/pallas_call | solution.py:416
  75.1 29.4 %all_to_all.5.rows_ref = f32[8,128,256]{2,1,0:T(8,128)} all-to-all(f32[8,128,256]{2,1,0:T(8,128)S(1)} %region.1), channel_id=1, replica_groups={{0,1,2,3,4,5,6,7},{15,14,13,12,11,10,9,8},{16,17,18,19,20,21,22,23},{31..., dimensions={0} | all-to-all | bytes 2097152 | tf_op jit(solution)/shard_map/all_to_all | solution.py:536
  104.5 2.5 %unpack.1 = f32[128,8,256]{2,1,0:T(8,128)} custom-call(f32[8,128,256]{2,1,0:T(8,128)} %all_to_all.5.rows_ref), custom_call_target="tpu_custom_call" | custom-call | tf_op jit(solution)/shard_map/unpack/pallas_call | solution.py:539
  (3 shorter events, 0.0 us)
Async XLA Ops:
  0.0 8.2 %copy-start = (f32[128,8,256]{2,1,0:T(8,128)S(1)}, f32[128,8,256]{2,1,0:T(8,128)}, u32[]{:S(2)}) copy-start(f32[128,8,256]{2,1,0:T(8,128)} %field_ref.5) | copy-start | bytes 3145732
  2.2 15.3 %collective-permute-start = (f32[264,256]{1,0:T(8,128)}, f32[264,256]{1,0:T(8,128)S(1)}, u32[]{:S(2)}, u32[]{:S(2)}) collective-permute-start(f32[264,256]{1,0:T(8,128)} %get-tuple-element.29), channel_id=1, source_target_pairs={{0,8},{8,16},{16,24},{1,9},{9,17},{17,25},{2,10},{10,18},{18,26},{... | collective-permute-start | bytes 811016 | tf_op jit(solution)/shard_map/ppermute | solution.py:454
  5.6 13.7 %collective-permute-start.1 = (f32[264,256]{1,0:T(8,128)}, f32[264,256]{1,0:T(8,128)S(1)}, u32[]{:S(2)}, u32[]{:S(2)}) collective-permute-start(f32[264,256]{1,0:T(8,128)} %get-tuple-element.30), channel_id=1, source_target_pairs={{8,0},{16,8},{24,16},{9,1},{17,9},{25,17},{10,2},{18,10},{26,18},{... | collective-permute-start | bytes 811016 | tf_op jit(solution)/shard_map/ppermute | solution.py:455
  8.1 0.8 copy-start.1
  8.2 0.7 copy-start.2
  11.0 17.6 %collective-permute-start.3 = (f32[2,128,256]{2,1,0:T(8,128)S(1)}, f32[2,128,256]{2,1,0:T(8,128)S(1)}, u32[]{:S(2)}, u32[]{:S(2)}) collective-permute-start(f32[2,128,256]{2,1,0:T(8,128)S(1)} %get-tuple-element.33), channel_id=1, source_target_pairs={{0,4},{1,5},{6,2},{7,3},{8,12},{9,13},{14,10},{15,11},{16,20},{17,... | collective-permute-start | bytes 786440 | tf_op jit(solution)/shard_map/ppermute | solution.py:474
  15.5 15.8 %collective-permute-start.4 = (f32[2,128,256]{2,1,0:T(8,128)S(1)}, f32[2,128,256]{2,1,0:T(8,128)S(1)}, u32[]{:S(2)}, u32[]{:S(2)}) collective-permute-start(f32[2,128,256]{2,1,0:T(8,128)S(1)} %get-tuple-element.34), channel_id=1, source_target_pairs={{0,2},{1,3},{2,4},{3,5},{8,10},{9,11},{10,12},{11,13},{16,18},{17,... | collective-permute-start | bytes 786440 | tf_op jit(solution)/shard_map/ppermute | solution.py:474
  16.8 16.4 %collective-permute-start.5 = (f32[2,128,256]{2,1,0:T(8,128)S(1)}, f32[2,128,256]{2,1,0:T(8,128)S(1)}, u32[]{:S(2)}, u32[]{:S(2)}) collective-permute-start(f32[2,128,256]{2,1,0:T(8,128)S(1)} %get-tuple-element.35), channel_id=1, source_target_pairs={{4,2},{5,3},{6,4},{7,5},{12,10},{13,11},{14,12},{15,13},{20,18},{2... | collective-permute-start | bytes 786440 | tf_op jit(solution)/shard_map/ppermute | solution.py:474
  21.7 16.6 %collective-permute-start.6 = (f32[2,128,256]{2,1,0:T(8,128)}, f32[2,128,256]{2,1,0:T(8,128)S(1)}, u32[]{:S(2)}, u32[]{:S(2)}) collective-permute-start(f32[2,128,256]{2,1,0:T(8,128)} %get-tuple-element.37), channel_id=1, source_target_pairs={{6,0},{7,1},{0,6},{1,7},{14,8},{15,9},{8,14},{9,15},{22,16},{23,17... | collective-permute-start | bytes 786440 | tf_op jit(solution)/shard_map/ppermute | solution.py:474
  27.2 12.4 %collective-permute-start.7 = (f32[2,128,256]{2,1,0:T(8,128)}, f32[2,128,256]{2,1,0:T(8,128)S(1)}, u32[]{:S(2)}, u32[]{:S(2)}) collective-permute-start(f32[2,128,256]{2,1,0:T(8,128)} %get-tuple-element.38), channel_id=1, source_target_pairs={{4,0},{5,1},{2,6},{3,7},{12,8},{13,9},{10,14},{11,15},{20,16},{21,... | collective-permute-start | bytes 786440 | tf_op jit(solution)/shard_map/ppermute | solution.py:474
  28.6 2.0 %copy-start.5 = (s32[1,512]{1,0:T(1,128)S(1)}, s32[1,512]{1,0:T(1,128)}, u32[]{:S(2)}) copy-start(s32[1,512]{1,0:T(1,128)} %param.10) | copy-start | bytes 6148
  28.6 16.5 %collective-permute-start.8 = (f32[2,128,256]{2,1,0:T(8,128)}, f32[2,128,256]{2,1,0:T(8,128)S(1)}, u32[]{:S(2)}, u32[]{:S(2)}) collective-permute-start(f32[2,128,256]{2,1,0:T(8,128)} %get-tuple-element.39), channel_id=1, source_target_pairs={{2,0},{3,1},{4,6},{5,7},{10,8},{11,9},{12,14},{13,15},{18,16},{19,... | collective-permute-start | bytes 786440 | tf_op jit(solution)/shard_map/ppermute | solution.py:474
  30.5 0.7 copy-start.3
  30.5 0.7 copy-start.4
  31.3 7.0 %collective-permute-start.2 = (f32[8,512]{1,0:T(8,128)S(1)}, f32[8,512]{1,0:T(8,128)S(1)}, u32[]{:S(2)}, u32[]{:S(2)}) collective-permute-start(f32[8,512]{1,0:T(8,128)S(1)} %concatenate.3.mine_ref), channel_id=1, source_target_pairs={{8,15},{9,14},{10,13},{11,12},{12,11},{13,10},{14,9},{15,8},{24,31... | collective-permute-start | bytes 49160 | tf_op jit(solution)/shard_map/ppermute | solution.py:484
  45.8 5.7 %collective-permute-start.9 = (f32[2,4,128,256]{3,2,1,0:T(8,128)S(1)}, f32[2,4,128,256]{3,2,1,0:T(8,128)S(1)}, u32[]{:S(2)}, u32[]{:S(2)}) collective-permute-start(f32[2,4,128,256]{3,2,1,0:T(8,128)S(1)} %get-tuple-element.41.near_ref), channel_id=1, source_target_pairs={{0,1},{1,0},{2,3},{3,2},{4,5},{5,4},{6,7},{7,6},{8,9},{9,8},{10,11... | collective-permute-start | bytes 3145736 | tf_op jit(solution)/shard_map/ppermute | solution.py:516
  45.9 14.4 %collective-permute-start.10 = (f32[4,128,256]{2,1,0:T(8,128)S(1)}, f32[4,128,256]{2,1,0:T(8,128)S(1)}, u32[]{:S(2)}, u32[]{:S(2)}) collective-permute-start(f32[4,128,256]{2,1,0:T(8,128)S(1)} %get-tuple-element.49), channel_id=1, source_target_pairs={{0,2},{2,4},{3,1},{4,6},{5,3},{6,15},{7,5},{8,10},{9,16},{10,12},{... | collective-permute-start | bytes 1572872 | tf_op jit(solution)/shard_map/ppermute | solution.py:517
  47.8 15.1 %collective-permute-start.11 = (f32[4,128,256]{2,1,0:T(8,128)S(1)}, f32[4,128,256]{2,1,0:T(8,128)S(1)}, u32[]{:S(2)}, u32[]{:S(2)}) collective-permute-start(f32[4,128,256]{2,1,0:T(8,128)S(1)} %get-tuple-element.50), channel_id=1, source_target_pairs={{1,2},{3,4},{2,1},{5,6},{4,3},{7,15},{6,5},{9,10},{8,16},{11,12},{... | collective-permute-start | bytes 1572872 | tf_op jit(solution)/shard_map/ppermute | solution.py:518

commit v8 on v7

--- a/solution.py
+++ b/solution.py
@@ -61,7 +61,7 @@
         @pl.when(wanted)
         def _():
             for place in range(2):
-                position = 2 * chip + place
+                position = 2 * chip + jnp.abs(info_ref[1] - 1 + place)
                 row = position + info_ref[2] * (rows - 1 - 2 * position)
                 weights = weight_ref[row]
                 at = row + shift
@@ -133,25 +133,39 @@
     second_step(info_ref, target, 1, emission, wide_ref, weight_ref, out_refs)
 
 
+def source_of(chip, chips, s, k):
+    inner = lax.rem(chip + chips - s, chips)
+    return jnp.where(chip == 0, k, jnp.where(chip == chips - 1, chips - 1 - k, inner))
+
+
+def choose_kernel(info_ref, *refs):
+    count = (len(refs) - 2) // 2
+    other_ref, own_ref = refs[-2:]
+    chips = info_ref[3]
+    at_edge = jnp.logical_or(info_ref[0] == 0, info_ref[0] == chips - 1)
+    for index in range(count):
+        for ref, here in ((refs[index], jnp.logical_not(at_edge)), (refs[count + index], at_edge)):
+
+            @pl.when(here)
+            def _():
+                other_ref[index] = ref[0]
+                own_ref[index] = ref[1]
+
+
 def collect_kernel(order, info_ref, mine_ref, other_ref, *refs):
-    chips = (len(refs) - 4) // 2
-    both_ref, first_ref, second_ref, observed_ref = refs[-4:]
+    chips = len(order)
+    both_ref, observed_ref = refs[-2:]
     observed_ref[...] = jnp.where(info_ref[2] == 1, other_ref[...], mine_ref[...])
-    chip, core = info_ref[0], info_ref[1]
+    chip = info_ref[0]
     at_edge = jnp.logical_or(chip == 0, chip == chips - 1)
     for index, (s, k) in enumerate(order):
-        turn, mirror = lax.rem(chip + chips - s, chips), jnp.where(chip == 0, k, chips - 1 - k)
-        for ref, here, block in (
-            (refs[index], jnp.logical_not(at_edge), turn), (refs[chips + index], at_edge, mirror)
-        ):
+        block = source_of(chip, chips, s, k)
+        for ref, here in ((refs[index], jnp.logical_not(at_edge)), (refs[chips + index], at_edge)):
 
             @pl.when(here)
             def _():
-                other, own = ref[1 - core], ref[core]
-                both_ref[0, block] = other
-                both_ref[1, block] = own
-                first_ref[block] = other
-                second_ref[block] = own
+                both_ref[0, block] = ref[0]
+                both_ref[1, block] = ref[1]
 
 
 def unpack_kernel(rows_ref, out_ref):
@@ -290,9 +304,10 @@
 
 
 def region_kernel(
-    info_ref, observed_ref, near_ref, far_ref, high_in, low_in, own_high, own_low, own_part, seen_ref, direction_ref,
-    first_ref, second_ref, out_ref, spread_high, spread_low, factor, answer,
+    order, groups, info_ref, observed_ref, near_ref, far_ref, high_in, low_in, own_high, own_low, own_part, seen_ref,
+    direction_ref, *refs,
 ):
+    outer_refs, (out_ref, spread_high, spread_low, factor, answer) = refs[:-5], refs[-5:]
     _, chips, step, width = near_ref.shape
     members = 2 * chips * step
     slots = observed_ref.shape[1]
@@ -301,26 +316,33 @@
     swapped = jnp.logical_or(
         jnp.logical_and(info_ref[0] == 0, core == 0), jnp.logical_and(info_ref[0] == chips - 1, core == 1)
     )
+    giver = jnp.where(swapped, info_ref[0], info_ref[0] - 1 + 2 * core)
     cells, slot_weight, values, scale = observations(info_ref, observed_ref, width, root)
     chosen = one_hot(cells, 0, width)
 
-    def outer_block(index):
-        pair = (first_ref[index % chips], second_ref[index % chips])
-        part = index // chips
-        return jnp.where(swapped, pair[1 - part], pair[part])
+    def outer_block(part, place):
+        for pair, group in zip(zip(outer_refs[::2], outer_refs[1::2]), groups):
+            if place in group:
+                mine, other = pair[part], pair[1 - part]
+                at = group.index(place)
+                return jnp.where(swapped, other[at], mine[at])
 
     blocks = [pl.ds(index * step, step) for index in range(2 * chips)]
-    mean = mean_of([ref[chip] for ref in (first_ref, second_ref) for chip in range(chips)], members)
+    arrivals = [
+        (part, place, pl.ds(pl.multiple_of((part * chips + source_of(giver, chips, *order[place])) * step, step), step))
+        for part in range(2) for place in range(chips)
+    ]
+    mean = mean_of([outer_block(part, place) for part, place, _ in arrivals], members)
     taken = None
-    for index, block in enumerate(blocks):
-        term = (outer_block(index) - mean) * doubled(direction_ref[block, :])
+    for part, place, block in arrivals:
+        term = (outer_block(part, place) - mean) * doubled(direction_ref[block, :])
         taken = term if taken is None else taken + term
     taken = jnp.sum(taken, axis=0, keepdims=True)
     seen_mean = seen_ref[pl.ds(0, 1), :] + at_cells(mean, chosen)
     common = (seen_ref[pl.ds(1, 1), :] + at_cells(taken, chosen)) * scale
     innovation = slot_weight * (values - seen_mean)
-    for index, block in enumerate(blocks):
-        rest = outer_block(index) - mean - doubled(direction_ref[block, :]) * taken
+    for part, place, block in arrivals:
+        rest = outer_block(part, place) - mean - doubled(direction_ref[block, :]) * taken
         high, low = pieces(rest, 2)
         high, low = pieces((dot(high, chosen) + dot(low, chosen)) * scale, 2)
         spread_high[block, :] = high + high_in[block, :]
@@ -411,12 +433,16 @@
 SMEM = pl.BlockSpec(memory_space=pltpu.SMEM)
 
 
-def call(kernel, name, out_shape, args, scratch=(), flops=None, aliases={}, limit=8):
+def call(kernel, name, out_shape, args, scratch=(), flops=None, aliases={}, limit=8, after=()):
     several = isinstance(out_shape, (list, tuple))
+    if after:
+        count, inner = len(args), kernel
+        args = [*args, *after]
+        kernel = lambda *refs: inner(*refs[:count], *refs[len(args) :])
     return pl.pallas_call(
         kernel,
         out_shape=out_shape,
-        in_specs=[SMEM] + [VMEM] * (len(args) - 1),
+        in_specs=[SMEM] + [VMEM] * (len(args) - 1 - len(after)) + [pl.BlockSpec(memory_space=pl.ANY)] * len(after),
         out_specs=[VMEM] * len(out_shape) if several else VMEM,
         scratch_shapes=scratch,
         input_output_aliases=aliases,
@@ -445,7 +471,7 @@
     axes = ("patch", "member")
     count = patches * lanes
     patch, lane = lax.axis_index("patch"), lax.axis_index("member")
-    info = jnp.stack([lane // 2, lane % 2, patch % 2]).astype(jnp.int32)
+    info = jnp.stack([lane // 2, lane % 2, patch % 2, jnp.int32(chips)]).astype(jnp.int32)
 
     edge = array(STEPS * step + 8, width)
     tail, head = pl.pallas_call(
@@ -489,12 +515,6 @@
     got_inner[0], got_outer[0] = inner[0], outer[0]
     order = list(zip(order + [0], range(chips - 1, -1, -1)))
     pieces_in = [got_inner[s] for s, _ in order] + [got_outer[k] for _, k in order]
-    half_row = array(chips, step, width)
-    near, first, second, observed = call(
-        functools.partial(collect_kernel, order), "collect", [array(2, chips, step, width), half_row, half_row, array(8, slots)],
-        [info, mine, other] + pieces_in,
-    )
-
     def device(p, chip, core):
         return p * lanes + 2 * chip + core
 
@@ -513,9 +533,19 @@
                     to_first = to_second = device(to, chip, 1 - core)
                 first_pairs.append((device(p, chip, core), to_first))
                 second_pairs.append((device(p, chip, 1 - core), to_second))
+    groups = [[chips - 1, *range(chips - 3)], [chips - 3, chips - 2]]
+    outer_rows = []
+    for group in groups:
+        got = [pieces_in[place] for place in group] + [pieces_in[chips + place] for place in group]
+        row = array(len(group), step, width)
+        ahead = pieces_in[: chips - 1] if group is groups[0] else ()
+        first, second = call(choose_kernel, "choose", [row, row], [info] + got, after=ahead)
+        outer_rows += [lax.ppermute(first, axes, first_pairs), lax.ppermute(second, axes, second_pairs)]
+    near, observed = call(
+        functools.partial(collect_kernel, order), "collect", [array(2, chips, step, width), array(8, slots)],
+        [info, mine, other] + pieces_in, after=outer_rows[:2],
+    )
     far = lax.ppermute(near, axes, siblings)
-    got_first = lax.ppermute(first, axes, first_pairs)
-    got_second = lax.ppermute(second, axes, second_pairs)
 
     split = [pltpu.VMEM((members, slots), BF16)] * 2
     prepared = call(
@@ -527,17 +557,18 @@
         flops=8 * members * slots * width, limit=20,
     )
     analysed = call(
-        region_kernel, "region", array(lanes, step, width),
-        [info, observed, near, far, *prepared, got_first, got_second],
+        functools.partial(region_kernel, order, groups), "region", array(lanes, step, width),
+        [info, observed, near, far, *prepared, *outer_rows],
         split + [pltpu.VMEM((slots, slots), F32), pltpu.VMEM((width + 8, slots), F32)],
         limit=24,
     )
-    groups = [[p * lanes + (lanes - 1 - i if p % 2 else i) for i in range(lanes)] for p in range(patches)]
+    lines = [[p * lanes + (lanes - 1 - i if p % 2 else i) for i in range(lanes)] for p in range(patches)]
     returned = lax.all_to_all(
-        analysed, axes, split_axis=0, concat_axis=0, tiled=True, axis_index_groups=groups
+        analysed, axes, split_axis=0, concat_axis=0, tiled=True, axis_index_groups=lines
     )
     return pl.pallas_call(
         unpack_kernel, out_shape=array(step, rows, width), in_specs=[VMEM], out_specs=VMEM, name="unpack",
+        compiler_params=pltpu.CompilerParams(vmem_limit_bytes=48 * 1024 * 1024),
     )(returned)
 
 

time: 109 us -> 109 us (level)
  the two profiles are of different devices: /device:TPU:2 before, /device:TPU:0 now
where the time goes in v8:
time: 109 us; the launch traced here: 108 us
  blocking collectives  35.9 us (33%)
  starting transfers between devices  31.2 us (29%)
  Pallas kernels  26.1 us (24%)
  waiting for transfers between devices  12.5 us (11%)
  local copies, waits for them, and re-layouts  1.38 us (1%)
    all_to_all x1, blocking collectives, per_device(): lax.all_to_all(analysed, axes, split_axis=0, concat_axis=0, tiled=True, a...  35.9 us
    pallas_call x7, Pallas kernels, call(): pl.pallas_call(kernel, out_shape=out_shape, in_specs=[SMEM] + [VMEM] * (l...  22.6 us
    ppermute x6, starting transfers between devices, along(): lax.ppermute(piece, 'member', [(2 * a + core, 2 * b + core) for a, b in h...  14.6 us
    ppermute x6, waiting for transfers between devices, along(): lax.ppermute(piece, 'member', [(2 * a + core, 2 * b + core) for a, b in h...  9.56 us
    ppermute x1, starting transfers between devices, per_device(): far = lax.ppermute(near, axes, siblings)  5.4 us
    ppermute x1, starting transfers between devices, per_device(): lax.ppermute(tail, 'patch', [(i, i + 1) for i in range(patches - 1)])  4.85 us
    ppermute x2, starting transfers between devices, per_device(): lax.ppermute(first, axes, first_pairs)  3.05 us
    ppermute x1, waiting for transfers between devices, per_device(): lax.ppermute(head, 'patch', [(i + 1, i) for i in range(patches - 1)])  2.92 us
  transfers between devices with their start and end apart: 14, of which 4 were waited for; matrix products, arithmetic and copies ran while one was open for 0% of the time, Pallas kernels for 9%

profile of v8, /device:TPU:0, one launch (start us, length us, event | category | flops | bytes accessed | tf_op | source)
XLA Modules:
  0.0 108.2 jit_solution(13061645025898902287)
XLA Ops:
  0.0 0.0 copy-start
  0.0 2.2 %pack.1 = (f32[264,256]{1,0:T(8,128)}, f32[264,256]{1,0:T(8,128)}) custom-call(f32[128,8,256]{2,1,0:T(8,128)} %field_ref.5, f32[4,8,256]{2,1,0:T(8,128)} %flow_ref.5), custom_call_target="tpu_custom_call" | custom-call | tf_op jit(solution)/shard_map/pack/pallas_call | solution.py:477
  2.2 4.8 %collective-permute-start = (f32[264,256]{1,0:T(8,128)}, f32[264,256]{1,0:T(8,128)S(1)}, u32[]{:S(2)}, u32[]{:S(2)}) collective-permute-start(f32[264,256]{1,0:T(8,128)} %get-tuple-element.31), channel_id=1, source_target_pairs={{0,8},{8,16},{16,24},{1,9},{9,17},{17,25},{2,10},{10,18},{18,26},{... | collective-permute-start | bytes 811016 | tf_op jit(solution)/shard_map/ppermute | solution.py:480
  7.1 1.3 %collective-permute-start.1 = (f32[264,256]{1,0:T(8,128)}, f32[264,256]{1,0:T(8,128)S(1)}, u32[]{:S(2)}, u32[]{:S(2)}) collective-permute-start(f32[264,256]{1,0:T(8,128)} %get-tuple-element.32), channel_id=1, source_target_pairs={{8,0},{16,8},{24,16},{9,1},{17,9},{25,17},{10,2},{18,10},{26,18},{... | collective-permute-start | bytes 811016 | tf_op jit(solution)/shard_map/ppermute | solution.py:481
  8.4 0.0 copy-start.1
  8.4 0.1 pad_add_fusion.info_ref.refs_0_
  8.5 0.0 copy-start.2
  8.5 0.0 copy-done
  8.5 0.6 copy-done.1
  9.1 0.0 copy-done.2
  9.1 2.1 %inner.1 = (f32[4,128,256]{2,1,0:T(8,128)S(1)}, f32[2,128,256]{2,1,0:T(8,128)S(1)}, f32[2,128,256]{2,1,0:T(8,128)S(1)}, f32[2,128,256]{2,1,0:T(8,128)S(1)}, f32[2,128,256]{2,1,0:T(8,128)S(1)}) custom-call(s32[4]{0:T(128)S(1)} %pad_add_fusion.info_ref.refs_0_, f32[128,8,256]{2,1,0:T(8,128)S(1)} %copy-done, f32[4,8,256]{2,1,0:T(8,128)S(1)} %copy-done.1, ...), custom_call_target="tpu_custom_call" | custom-call | tf_op jit(solution)/shard_map/inner/pallas_call | solution.py:442
  11.3 4.5 %collective-permute-start.3 = (f32[2,128,256]{2,1,0:T(8,128)S(1)}, f32[2,128,256]{2,1,0:T(8,128)S(1)}, u32[]{:S(2)}, u32[]{:S(2)}) collective-permute-start(f32[2,128,256]{2,1,0:T(8,128)S(1)} %get-tuple-element.35), channel_id=1, source_target_pairs={{0,4},{1,5},{6,2},{7,3},{8,12},{9,13},{14,10},{15,11},{16,20},{17,... | collective-permute-start | bytes 786440 | tf_op jit(solution)/shard_map/ppermute | solution.py:500
  15.8 1.3 %collective-permute-start.4 = (f32[2,128,256]{2,1,0:T(8,128)S(1)}, f32[2,128,256]{2,1,0:T(8,128)S(1)}, u32[]{:S(2)}, u32[]{:S(2)}) collective-permute-start(f32[2,128,256]{2,1,0:T(8,128)S(1)} %get-tuple-element.36), channel_id=1, source_target_pairs={{0,2},{1,3},{2,4},{3,5},{8,10},{9,11},{10,12},{11,13},{16,18},{17,... | collective-permute-start | bytes 786440 | tf_op jit(solution)/shard_map/ppermute | solution.py:500
  17.1 0.7 collective-permute-start.5
  17.8 0.0 collective-permute-done.before_ref
  17.8 2.9 %collective-permute-done.1.after_ref = f32[264,256]{1,0:T(8,128)S(1)} collective-permute-done((f32[264,256]{1,0:T(8,128)}, f32[264,256]{1,0:T(8,128)S(1)}, u32[]{:S(2)}, u32[]{:S(2)}) %collective-permute-start.1) | collective-permute-done | bytes 270368 | tf_op jit(solution)/shard_map/ppermute | solution.py:481
  20.7 1.6 %edge.1 = (f32[2,128,256]{2,1,0:T(8,128)S(1)}, f32[2,128,256]{2,1,0:T(8,128)S(1)}, f32[2,128,256]{2,1,0:T(8,128)S(1)}, f32[2,128,256]{2,1,0:T(8,128)S(1)}) custom-call(s32[4]{0:T(128)S(1)} %pad_add_fusion.info_ref.refs_0_, f32[128,8,256]{2,1,0:T(8,128)S(1)} %copy-done, f32[4,8,256]{2,1,0:T(8,128)S(1)} %copy-done.1, f32[1,128]{1,0:T(1,128)S(1)} %bitcast.6, ...), custom_call_target="tpu_custom_call" | custom-call | tf_op jit(solution)/shard_map/edge/pallas_call | solution.py:442
  22.3 5.5 %collective-permute-start.6 = (f32[2,128,256]{2,1,0:T(8,128)S(1)}, f32[2,128,256]{2,1,0:T(8,128)S(1)}, u32[]{:S(2)}, u32[]{:S(2)}) collective-permute-start(f32[2,128,256]{2,1,0:T(8,128)S(1)} %get-tuple-element.39), channel_id=1, source_target_pairs={{6,0},{7,1},{0,6},{1,7},{14,8},{15,9},{8,14},{9,15},{22,16},{23,17... | collective-permute-start | bytes 786440 | tf_op jit(solution)/shard_map/ppermute | solution.py:500
  27.8 1.3 %collective-permute-start.7 = (f32[2,128,256]{2,1,0:T(8,128)S(1)}, f32[2,128,256]{2,1,0:T(8,128)S(1)}, u32[]{:S(2)}, u32[]{:S(2)}) collective-permute-start(f32[2,128,256]{2,1,0:T(8,128)S(1)} %get-tuple-element.40), channel_id=1, source_target_pairs={{4,0},{5,1},{2,6},{3,7},{12,8},{13,9},{10,14},{11,15},{20,16},{21,... | collective-permute-start | bytes 786440 | tf_op jit(solution)/shard_map/ppermute | solution.py:500
  29.1 0.0 collective-permute-done.3.refs_2_.refs_5_.refs_3_
  29.1 1.3 %collective-permute-start.8 = (f32[2,128,256]{2,1,0:T(8,128)S(1)}, f32[2,128,256]{2,1,0:T(8,128)S(1)}, u32[]{:S(2)}, u32[]{:S(2)}) collective-permute-start(f32[2,128,256]{2,1,0:T(8,128)S(1)} %get-tuple-element.41), channel_id=1, source_target_pairs={{2,0},{3,1},{4,6},{5,7},{10,8},{11,9},{12,14},{13,15},{18,16},{19,... | collective-permute-start | bytes 786440 | tf_op jit(solution)/shard_map/ppermute | solution.py:500
  30.4 0.0 collective-permute-done.4.refs_6_.refs_4_.refs_0_
  30.5 0.0 collective-permute-done.5.refs_7_.refs_5_.refs_1_
  30.5 3.8 %collective-permute-done.6.refs_4_.refs_7_ = f32[2,128,256]{2,1,0:T(8,128)S(1)} collective-permute-done((f32[2,128,256]{2,1,0:T(8,128)S(1)}, f32[2,128,256]{2,1,0:T(8,128)S(1)}, u32[]{:S(2)}, u32[]{:S(2)}) %collective-permute-start.6) | collective-permute-done | bytes 262176 | tf_op jit(solution)/shard_map/ppermute | solution.py:500
  34.3 1.3 %choose.2 = (f32[2,128,256]{2,1,0:T(8,128)}, f32[2,128,256]{2,1,0:T(8,128)S(1)}) custom-call(s32[4]{0:T(128)S(1)} %pad_add_fusion.info_ref.refs_0_, f32[2,128,256]{2,1,0:T(8,128)S(1)} %get-tuple-element.38.refs_1_.refs_6_, f32[2,128,256]{2,1,0:T(8,128)S(1)} %collective-permute-done.3.refs_2_.refs_5_.refs_3_, ...), custom_call_target="tpu_custom_call" | custom-call | tf_op jit(solution)/shard_map/choose/pallas_call | solution.py:442
  35.6 1.3 %collective-permute-start.9 = (f32[2,128,256]{2,1,0:T(8,128)}, f32[2,128,256]{2,1,0:T(8,128)S(1)}, u32[]{:S(2)}, u32[]{:S(2)}) collective-permute-start(f32[2,128,256]{2,1,0:T(8,128)} %get-tuple-element.42), channel_id=1, source_target_pairs={{0,2},{2,4},{3,1},{4,6},{5,3},{6,15},{7,5},{8,10},{9,16},{10,12},{... | collective-permute-start | bytes 786440 | tf_op jit(solution)/shard_map/ppermute | solution.py:543
  36.9 0.0 copy-start.5
  36.9 0.7 collective-permute-start.10
  38.2 0.0 copy-done.5
  38.2 0.0 copy-start.3
  38.2 0.0 copy-start.4
  38.3 0.6 copy-done.3
  38.9 0.0 copy-done.4
  39.0 0.7 collective-permute-start.2
  39.6 0.0 collective-permute-done.2.refs_2_
  39.6 0.2 collective-permute-done.7.refs_8_.refs_2_
  39.8 5.6 %collective-permute-done.8.refs_9_.refs_3_ = f32[2,128,256]{2,1,0:T(8,128)S(1)} collective-permute-done((f32[2,128,256]{2,1,0:T(8,128)S(1)}, f32[2,128,256]{2,1,0:T(8,128)S(1)}, u32[]{:S(2)}, u32[]{:S(2)}) %collective-permute-start.8) | collective-permute-done | bytes 262176 | tf_op jit(solution)/shard_map/ppermute | solution.py:500
  45.4 0.0 collective-permute-done.9.refs_11_.refs_0_
  45.4 0.0 collective-permute-done.10.refs_12_.refs_1_
  45.4 0.7 collect.1
  46.1 5.4 %collective-permute-start.11 = (f32[2,4,128,256]{3,2,1,0:T(8,128)S(1)}, f32[2,4,128,256]{3,2,1,0:T(8,128)S(1)}, u32[]{:S(2)}, u32[]{:S(2)}) collective-permute-start(f32[2,4,128,256]{3,2,1,0:T(8,128)S(1)} %get-tuple-element.45.near_ref), channel_id=1, source_target_pairs={{0,1},{1,0},{2,3},{3,2},{4,5},{5,4},{6,7},{7,6},{8,9},{9,8},{10,11... | collective-permute-start | bytes 3145736 | tf_op jit(solution)/shard_map/ppermute | solution.py:548
  51.5 0.6 choose.3
  52.1 1.8 %collective-permute-start.12 = (f32[2,128,256]{2,1,0:T(8,128)S(1)}, f32[2,128,256]{2,1,0:T(8,128)S(1)}, u32[]{:S(2)}, u32[]{:S(2)}) collective-permute-start(f32[2,128,256]{2,1,0:T(8,128)S(1)} %get-tuple-element.53), channel_id=1, source_target_pairs={{0,2},{2,4},{3,1},{4,6},{5,3},{6,15},{7,5},{8,10},{9,16},{10,12},{... | collective-permute-start | bytes 786440 | tf_op jit(solution)/shard_map/ppermute | solution.py:543
  53.8 0.7 collective-permute-start.13
  54.5 0.0 collective-permute-done.11.far_ref
  54.5 4.0 %prepare.1 = (bf16[1024,512]{1,0:T(8,128)(2,1)S(1)}, bf16[1024,512]{1,0:T(8,128)(2,1)S(1)}, bf16[256,1024]{1,0:T(8,128)(2,1)S(1)}, bf16[256,1024]{1,0:T(8,128)(2...) custom-call(s32[4]{0:T(128)S(1)} %pad_add_fusion.info_ref.refs_0_, ...), custom_call_target="tpu_custom_call" | custom-call | flops 1073741824 | tf_op jit(solution)/shard_map/prepare/pallas_call | solution.py:442
  58.5 0.0 collective-permute-done.12.refs_2_
  58.5 0.0 collective-permute-done.13.refs_3_
  58.5 12.4 %region.1 = f32[8,128,256]{2,1,0:T(8,128)S(1)} custom-call(s32[4]{0:T(128)S(1)} %pad_add_fusion.info_ref.refs_0_, f32[8,512]{1,0:T(8,128)S(1)} %get-tuple-element.44.observed_ref, f32[2,4,128,256]{3,2,1,0:T(8,128)S(1)} %get-tuple-element.45.near_ref, f32[2,4,128,256]{3,2,1,0:T(8,128)S(1)} %collective-permute-done.11.far_ref, ...), custom_call_target="tpu_custom_call" | custom-call | tf_op jit(solution)/shard_map/region/pallas_call | solution.py:442
  71.0 35.9 %all_to_all.5.rows_ref = f32[8,128,256]{2,1,0:T(8,128)S(1)} all-to-all(f32[8,128,256]{2,1,0:T(8,128)S(1)} %region.1), channel_id=1, replica_groups={{0,1,2,3,4,5,6,7},{15,14,13,12,11,10,9,8},{16,17,18,19,20,21,22,23},{31..., dimensions={0} | all-to-all | bytes 2097152 | tf_op jit(solution)/shard_map/all_to_all | solution.py:566
  106.9 1.3 %unpack.1 = f32[128,8,256]{2,1,0:T(8,128)} custom-call(f32[8,128,256]{2,1,0:T(8,128)S(1)} %all_to_all.5.rows_ref), custom_call_target="tpu_custom_call" | custom-call | tf_op jit(solution)/shard_map/unpack/pallas_call | solution.py:569
  (3 shorter events, 0.0 us)
Async XLA Ops:
  0.0 8.5 %copy-start = (f32[128,8,256]{2,1,0:T(8,128)S(1)}, f32[128,8,256]{2,1,0:T(8,128)}, u32[]{:S(2)}) copy-start(f32[128,8,256]{2,1,0:T(8,128)} %field_ref.5) | copy-start | bytes 3145732
  2.2 15.6 %collective-permute-start = (f32[264,256]{1,0:T(8,128)}, f32[264,256]{1,0:T(8,128)S(1)}, u32[]{:S(2)}, u32[]{:S(2)}) collective-permute-start(f32[264,256]{1,0:T(8,128)} %get-tuple-element.31), channel_id=1, source_target_pairs={{0,8},{8,16},{16,24},{1,9},{9,17},{17,25},{2,10},{10,18},{18,26},{... | collective-permute-start | bytes 811016 | tf_op jit(solution)/shard_map/ppermute | solution.py:480
  7.1 13.7 %collective-permute-start.1 = (f32[264,256]{1,0:T(8,128)}, f32[264,256]{1,0:T(8,128)S(1)}, u32[]{:S(2)}, u32[]{:S(2)}) collective-permute-start(f32[264,256]{1,0:T(8,128)} %get-tuple-element.32), channel_id=1, source_target_pairs={{8,0},{16,8},{24,16},{9,1},{17,9},{25,17},{10,2},{18,10},{26,18},{... | collective-permute-start | bytes 811016 | tf_op jit(solution)/shard_map/ppermute | solution.py:481
  8.4 0.8 copy-start.1
  8.5 0.7 copy-start.2
  11.3 17.9 %collective-permute-start.3 = (f32[2,128,256]{2,1,0:T(8,128)S(1)}, f32[2,128,256]{2,1,0:T(8,128)S(1)}, u32[]{:S(2)}, u32[]{:S(2)}) collective-permute-start(f32[2,128,256]{2,1,0:T(8,128)S(1)} %get-tuple-element.35), channel_id=1, source_target_pairs={{0,4},{1,5},{6,2},{7,3},{8,12},{9,13},{14,10},{15,11},{16,20},{17,... | collective-permute-start | bytes 786440 | tf_op jit(solution)/shard_map/ppermute | solution.py:500
  15.8 14.7 %collective-permute-start.4 = (f32[2,128,256]{2,1,0:T(8,128)S(1)}, f32[2,128,256]{2,1,0:T(8,128)S(1)}, u32[]{:S(2)}, u32[]{:S(2)}) collective-permute-start(f32[2,128,256]{2,1,0:T(8,128)S(1)} %get-tuple-element.36), channel_id=1, source_target_pairs={{0,2},{1,3},{2,4},{3,5},{8,10},{9,11},{10,12},{11,13},{16,18},{17,... | collective-permute-start | bytes 786440 | tf_op jit(solution)/shard_map/ppermute | solution.py:500
  17.1 13.4 %collective-permute-start.5 = (f32[2,128,256]{2,1,0:T(8,128)S(1)}, f32[2,128,256]{2,1,0:T(8,128)S(1)}, u32[]{:S(2)}, u32[]{:S(2)}) collective-permute-start(f32[2,128,256]{2,1,0:T(8,128)S(1)} %get-tuple-element.37), channel_id=1, source_target_pairs={{4,2},{5,3},{6,4},{7,5},{12,10},{13,11},{14,12},{15,13},{20,18},{2... | collective-permute-start | bytes 786440 | tf_op jit(solution)/shard_map/ppermute | solution.py:500
  22.3 11.9 %collective-permute-start.6 = (f32[2,128,256]{2,1,0:T(8,128)S(1)}, f32[2,128,256]{2,1,0:T(8,128)S(1)}, u32[]{:S(2)}, u32[]{:S(2)}) collective-permute-start(f32[2,128,256]{2,1,0:T(8,128)S(1)} %get-tuple-element.39), channel_id=1, source_target_pairs={{6,0},{7,1},{0,6},{1,7},{14,8},{15,9},{8,14},{9,15},{22,16},{23,17... | collective-permute-start | bytes 786440 | tf_op jit(solution)/shard_map/ppermute | solution.py:500
  27.8 12.0 %collective-permute-start.7 = (f32[2,128,256]{2,1,0:T(8,128)S(1)}, f32[2,128,256]{2,1,0:T(8,128)S(1)}, u32[]{:S(2)}, u32[]{:S(2)}) collective-permute-start(f32[2,128,256]{2,1,0:T(8,128)S(1)} %get-tuple-element.40), channel_id=1, source_target_pairs={{4,0},{5,1},{2,6},{3,7},{12,8},{13,9},{10,14},{11,15},{20,16},{21,... | collective-permute-start | bytes 786440 | tf_op jit(solution)/shard_map/ppermute | solution.py:500
  29.1 16.2 %collective-permute-start.8 = (f32[2,128,256]{2,1,0:T(8,128)S(1)}, f32[2,128,256]{2,1,0:T(8,128)S(1)}, u32[]{:S(2)}, u32[]{:S(2)}) collective-permute-start(f32[2,128,256]{2,1,0:T(8,128)S(1)} %get-tuple-element.41), channel_id=1, source_target_pairs={{2,0},{3,1},{4,6},{5,7},{10,8},{11,9},{12,14},{13,15},{18,16},{19,... | collective-permute-start | bytes 786440 | tf_op jit(solution)/shard_map/ppermute | solution.py:500
  35.6 9.8 %collective-permute-start.9 = (f32[2,128,256]{2,1,0:T(8,128)}, f32[2,128,256]{2,1,0:T(8,128)S(1)}, u32[]{:S(2)}, u32[]{:S(2)}) collective-permute-start(f32[2,128,256]{2,1,0:T(8,128)} %get-tuple-element.42), channel_id=1, source_target_pairs={{0,2},{2,4},{3,1},{4,6},{5,3},{6,15},{7,5},{8,10},{9,16},{10,12},{... | collective-permute-start | bytes 786440 | tf_op jit(solution)/shard_map/ppermute | solution.py:543
  36.9 1.3 %copy-start.5 = (s32[1,512]{1,0:T(1,128)S(1)}, s32[1,512]{1,0:T(1,128)}, u32[]{:S(2)}) copy-start(s32[1,512]{1,0:T(1,128)} %param.10) | copy-start | bytes 6148
  36.9 8.5 %collective-permute-start.10 = (f32[2,128,256]{2,1,0:T(8,128)S(1)}, f32[2,128,256]{2,1,0:T(8,128)S(1)}, u32[]{:S(2)}, u32[]{:S(2)}) collective-permute-start(f32[2,128,256]{2,1,0:T(8,128)S(1)} %get-tuple-element.43), channel_id=1, source_target_pairs={{1,2},{3,4},{2,1},{5,6},{4,3},{7,15},{6,5},{9,10},{8,16},{11,12},{... | collective-permute-start | bytes 786440 | tf_op jit(solution)/shard_map/ppermute | solution.py:543
  38.2 0.7 copy-start.3
  38.2 0.7 copy-start.4
  39.0 0.7 collective-permute-start.2
  46.1 8.4 %collective-permute-start.11 = (f32[2,4,128,256]{3,2,1,0:T(8,128)S(1)}, f32[2,4,128,256]{3,2,1,0:T(8,128)S(1)}, u32[]{:S(2)}, u32[]{:S(2)}) collective-permute-start(f32[2,4,128,256]{3,2,1,0:T(8,128)S(1)} %get-tuple-element.45.near_ref), channel_id=1, source_target_pairs={{0,1},{1,0},{2,3},{3,2},{4,5},{5,4},{6,7},{7,6},{8,9},{9,8},{10,11... | collective-permute-start | bytes 3145736 | tf_op jit(solution)/shard_map/ppermute | solution.py:548
  52.1 6.5 %collective-permute-start.12 = (f32[2,128,256]{2,1,0:T(8,128)S(1)}, f32[2,128,256]{2,1,0:T(8,128)S(1)}, u32[]{:S(2)}, u32[]{:S(2)}) collective-permute-start(f32[2,128,256]{2,1,0:T(8,128)S(1)} %get-tuple-element.53), channel_id=1, source_target_pairs={{0,2},{2,4},{3,1},{4,6},{5,3},{6,15},{7,5},{8,10},{9,16},{10,12},{... | collective-permute-start | bytes 786440 | tf_op jit(solution)/shard_map/ppermute | solution.py:543
  53.8 4.7 %collective-permute-start.13 = (f32[2,128,256]{2,1,0:T(8,128)S(1)}, f32[2,128,256]{2,1,0:T(8,128)S(1)}, u32[]{:S(2)}, u32[]{:S(2)}) collective-permute-start(f32[2,128,256]{2,1,0:T(8,128)S(1)} %get-tuple-element.54), channel_id=1, source_target_pairs={{1,2},{3,4},{2,1},{5,6},{4,3},{7,15},{6,5},{9,10},{8,16},{11,12},{... | collective-permute-start | bytes 786440 | tf_op jit(solution)/shard_map/ppermute | solution.py:543

commit v9 on v8

--- a/solution.py
+++ b/solution.py
@@ -152,9 +152,9 @@
                 own_ref[index] = ref[1]
 
 
-def collect_kernel(order, info_ref, mine_ref, other_ref, *refs):
+def collect_kernel(order, late, info_ref, mine_ref, other_ref, *refs):
     chips = len(order)
-    both_ref, observed_ref = refs[-2:]
+    both_ref, late_other, late_own, observed_ref = refs[-4:]
     observed_ref[...] = jnp.where(info_ref[2] == 1, other_ref[...], mine_ref[...])
     chip = info_ref[0]
     at_edge = jnp.logical_or(chip == 0, chip == chips - 1)
@@ -166,6 +166,9 @@
             def _():
                 both_ref[0, block] = ref[0]
                 both_ref[1, block] = ref[1]
+                if index in late:
+                    late_other[late.index(index)] = ref[0]
+                    late_own[late.index(index)] = ref[1]
 
 
 def unpack_kernel(rows_ref, out_ref):
@@ -503,7 +506,7 @@
     wide = [pltpu.VMEM((rows + 2, step, width), F32), pltpu.VMEM((rows, 8, width), F32)]
     args = [info, init_field, flow_fields, emission[None, :]]
     kept, *inner = call(inner_kernel, "inner", [array(4, step, width)] + [pair] * chips, args, wide)
-    order = [s for near in range(chips // 2, 0, -1) for s in sorted({near, chips - near})]
+    order = list(range(1, chips))
     got_inner = {s: along(inner[s], s, False) for s in order}
     outer = call(edge_kernel, "edge", [pair] * chips, args + [kept, before, after], wide)
     mine, _ = lax.optimization_barrier((mine, outer[0]))
@@ -511,9 +514,9 @@
         mine, axes,
         [(p * lanes + i, p * lanes + lanes - 1 - i) for p in range(1, patches, 2) for i in range(lanes)],
     )
-    got_outer = {s: along(outer[s], s, True) for s in range(chips - 1, 0, -1)}
+    got_outer = {s: along(outer[s], s, True) for s in order}
     got_inner[0], got_outer[0] = inner[0], outer[0]
-    order = list(zip(order + [0], range(chips - 1, -1, -1)))
+    order = [(s, s) for s in range(chips)]
     pieces_in = [got_inner[s] for s, _ in order] + [got_outer[k] for _, k in order]
     def device(p, chip, core):
         return p * lanes + 2 * chip + core
@@ -533,18 +536,18 @@
                     to_first = to_second = device(to, chip, 1 - core)
                 first_pairs.append((device(p, chip, core), to_first))
                 second_pairs.append((device(p, chip, 1 - core), to_second))
-    groups = [[chips - 1, *range(chips - 3)], [chips - 3, chips - 2]]
-    outer_rows = []
-    for group in groups:
-        got = [pieces_in[place] for place in group] + [pieces_in[chips + place] for place in group]
-        row = array(len(group), step, width)
-        ahead = pieces_in[: chips - 1] if group is groups[0] else ()
-        first, second = call(choose_kernel, "choose", [row, row], [info] + got, after=ahead)
-        outer_rows += [lax.ppermute(first, axes, first_pairs), lax.ppermute(second, axes, second_pairs)]
-    near, observed = call(
-        functools.partial(collect_kernel, order), "collect", [array(2, chips, step, width), array(8, slots)],
-        [info, mine, other] + pieces_in, after=outer_rows[:2],
-    )
+    groups = [[0], list(range(1, chips))]
+    early, late = groups
+    got = [pieces_in[place] for place in early] + [pieces_in[chips + place] for place in early]
+    row = array(len(early), step, width)
+    early_rows = call(choose_kernel, "choose", [row, row], [info] + got)
+    outer_rows = [lax.ppermute(early_rows[0], axes, first_pairs), lax.ppermute(early_rows[1], axes, second_pairs)]
+    row = array(len(late), step, width)
+    near, *late_rows, observed = call(
+        functools.partial(collect_kernel, order, late), "collect",
+        [array(2, chips, step, width), row, row, array(8, slots)], [info, mine, other] + pieces_in, after=outer_rows,
+    )
+    outer_rows += [lax.ppermute(late_rows[0], axes, first_pairs), lax.ppermute(late_rows[1], axes, second_pairs)]
     far = lax.ppermute(near, axes, siblings)
 
     split = [pltpu.VMEM((members, slots), BF16)] * 2

time: 109 us -> 107 us (0.982)
  the two profiles are of different devices: /device:TPU:0 before, /device:TPU:2 now
where the time goes in v9:
time: 107 us; the launch traced here: 106 us
  starting transfers between devices  37 us (35%)
  blocking collectives  31 us (29%)
  Pallas kernels  23.9 us (22%)
  waiting for transfers between devices  12.1 us (11%)
  local copies, waits for them, and re-layouts  1.38 us (1%)
    all_to_all x1, blocking collectives, per_device(): lax.all_to_all(analysed, axes, split_axis=0, concat_axis=0, tiled=True, a...  31 us
    pallas_call x6, Pallas kernels, call(): pl.pallas_call(kernel, out_shape=out_shape, in_specs=[SMEM] + [VMEM] * (l...  20.4 us
    ppermute x6, starting transfers between devices, along(): lax.ppermute(piece, 'member', [(2 * a + core, 2 * b + core) for a, b in h...  14.6 us
    ppermute x1, waiting for transfers between devices, per_device(): lax.ppermute(early_rows[1], axes, second_pairs)  4.94 us
    ppermute x1, starting transfers between devices, per_device(): lax.ppermute(late_rows[0], axes, first_pairs)  3.63 us
    ppermute x1, starting transfers between devices, per_device(): lax.ppermute(tail, 'patch', [(i, i + 1) for i in range(patches - 1)])  3.39 us
    ppermute x1, starting transfers between devices, per_device(): far = lax.ppermute(near, axes, siblings)  3.31 us
    ppermute x1, starting transfers between devices, per_device(): lax.ppermute(early_rows[0], axes, first_pairs)  3.03 us
  transfers between devices with their start and end apart: 14, of which 5 were waited for; matrix products, arithmetic and copies ran while one was open for 0% of the time, Pallas kernels for 9%

profile of v9, /device:TPU:2, one launch (start us, length us, event | category | flops | bytes accessed | tf_op | source)
XLA Modules:
  0.0 106.3 jit_solution(11767529987629837799)
XLA Ops:
  0.0 0.0 copy-start
  0.0 2.2 %pack.1 = (f32[264,256]{1,0:T(8,128)}, f32[264,256]{1,0:T(8,128)}) custom-call(f32[128,8,256]{2,1,0:T(8,128)} %field_ref.5, f32[4,8,256]{2,1,0:T(8,128)} %flow_ref.5), custom_call_target="tpu_custom_call" | custom-call | tf_op jit(solution)/shard_map/pack/pallas_call | solution.py:480
  2.2 3.4 %collective-permute-start = (f32[264,256]{1,0:T(8,128)}, f32[264,256]{1,0:T(8,128)S(1)}, u32[]{:S(2)}, u32[]{:S(2)}) collective-permute-start(f32[264,256]{1,0:T(8,128)} %get-tuple-element.31), channel_id=1, source_target_pairs={{0,8},{8,16},{16,24},{1,9},{9,17},{17,25},{2,10},{10,18},{18,26},{... | collective-permute-start | bytes 811016 | tf_op jit(solution)/shard_map/ppermute | solution.py:483
  5.6 2.5 %collective-permute-start.1 = (f32[264,256]{1,0:T(8,128)}, f32[264,256]{1,0:T(8,128)S(1)}, u32[]{:S(2)}, u32[]{:S(2)}) collective-permute-start(f32[264,256]{1,0:T(8,128)} %get-tuple-element.32), channel_id=1, source_target_pairs={{8,0},{16,8},{24,16},{9,1},{17,9},{25,17},{10,2},{18,10},{26,18},{... | collective-permute-start | bytes 811016 | tf_op jit(solution)/shard_map/ppermute | solution.py:484
  8.1 0.0 copy-start.1
  8.1 0.1 pad_add_fusion.info_ref.refs_0_
  8.2 0.0 copy-start.2
  8.2 0.0 copy-done
  8.2 0.6 copy-done.1
  8.8 0.0 copy-done.2
  8.8 2.9 %inner.1 = (f32[4,128,256]{2,1,0:T(8,128)S(1)}, f32[2,128,256]{2,1,0:T(8,128)S(1)}, f32[2,128,256]{2,1,0:T(8,128)S(1)}, f32[2,128,256]{2,1,0:T(8,128)}, f32[2,128,256]{2,1,0:T(8,128)}) custom-call(s32[4]{0:T(128)S(1)} %pad_add_fusion.info_ref.refs_0_, f32[128,8,256]{2,1,0:T(8,128)S(1)} %copy-done, f32[4,8,256]{2,1,0:T(8,128)S(1)} %copy-done.1, ...), custom_call_target="tpu_custom_call" | custom-call | tf_op jit(solution)/shard_map/inner/pallas_call | solution.py:445
  11.7 3.5 %collective-permute-start.3 = (f32[2,128,256]{2,1,0:T(8,128)S(1)}, f32[2,128,256]{2,1,0:T(8,128)S(1)}, u32[]{:S(2)}, u32[]{:S(2)}) collective-permute-start(f32[2,128,256]{2,1,0:T(8,128)S(1)} %get-tuple-element.36), channel_id=1, source_target_pairs={{0,2},{1,3},{2,4},{3,5},{8,10},{9,11},{10,12},{11,13},{16,18},{17,... | collective-permute-start | bytes 786440 | tf_op jit(solution)/shard_map/ppermute | solution.py:503
  15.2 2.3 %collective-permute-start.4 = (f32[2,128,256]{2,1,0:T(8,128)}, f32[2,128,256]{2,1,0:T(8,128)S(1)}, u32[]{:S(2)}, u32[]{:S(2)}) collective-permute-start(f32[2,128,256]{2,1,0:T(8,128)} %get-tuple-element.37), channel_id=1, source_target_pairs={{0,4},{1,5},{6,2},{7,3},{8,12},{9,13},{14,10},{15,11},{16,20},{17,... | collective-permute-start | bytes 786440 | tf_op jit(solution)/shard_map/ppermute | solution.py:503
  17.5 0.7 collective-permute-start.5
  18.2 0.0 collective-permute-done.before_ref
  18.2 1.0 collective-permute-done.1.after_ref
  19.3 2.3 %edge.1 = (f32[2,128,256]{2,1,0:T(8,128)S(1)}, f32[2,128,256]{2,1,0:T(8,128)}, f32[2,128,256]{2,1,0:T(8,128)S(1)}, f32[2,128,256]{2,1,0:T(8,128)S(1)}) custom-call(s32[4]{0:T(128)S(1)} %pad_add_fusion.info_ref.refs_0_, f32[128,8,256]{2,1,0:T(8,128)S(1)} %copy-done, f32[4,8,256]{2,1,0:T(8,128)S(1)} %copy-done.1, f32[1,128]{1,0:T(1,128)S(1)} %bitcast.6, ...), custom_call_target="tpu_custom_call" | custom-call | tf_op jit(solution)/shard_map/edge/pallas_call | solution.py:445
  21.6 1.3 %collective-permute-start.6 = (f32[2,128,256]{2,1,0:T(8,128)}, f32[2,128,256]{2,1,0:T(8,128)S(1)}, u32[]{:S(2)}, u32[]{:S(2)}) collective-permute-start(f32[2,128,256]{2,1,0:T(8,128)} %get-tuple-element.39), channel_id=1, source_target_pairs={{2,0},{3,1},{4,6},{5,7},{10,8},{11,9},{12,14},{13,15},{18,16},{19,... | collective-permute-start | bytes 786440 | tf_op jit(solution)/shard_map/ppermute | solution.py:503
  22.9 1.3 %collective-permute-start.7 = (f32[2,128,256]{2,1,0:T(8,128)S(1)}, f32[2,128,256]{2,1,0:T(8,128)S(1)}, u32[]{:S(2)}, u32[]{:S(2)}) collective-permute-start(f32[2,128,256]{2,1,0:T(8,128)S(1)} %get-tuple-element.40), channel_id=1, source_target_pairs={{4,0},{5,1},{2,6},{3,7},{12,8},{13,9},{10,14},{11,15},{20,16},{21,... | collective-permute-start | bytes 786440 | tf_op jit(solution)/shard_map/ppermute | solution.py:503
  24.2 0.0 collective-permute-done.3.refs_4_
  24.2 0.0 copy-start.5
  24.2 5.5 %collective-permute-start.8 = (f32[2,128,256]{2,1,0:T(8,128)S(1)}, f32[2,128,256]{2,1,0:T(8,128)S(1)}, u32[]{:S(2)}, u32[]{:S(2)}) collective-permute-start(f32[2,128,256]{2,1,0:T(8,128)S(1)} %get-tuple-element.41), channel_id=1, source_target_pairs={{6,0},{7,1},{0,6},{1,7},{14,8},{15,9},{8,14},{9,15},{22,16},{23,17... | collective-permute-start | bytes 786440 | tf_op jit(solution)/shard_map/ppermute | solution.py:503
  30.3 0.0 copy-done.5
  30.4 0.0 copy-start.3
  30.4 0.0 copy-start.4
  30.4 0.6 copy-done.3
  31.1 0.0 copy-done.4
  31.1 0.0 collective-permute-done.4.refs_5_
  31.1 1.9 %collective-permute-start.2 = (f32[8,512]{1,0:T(8,128)S(1)}, f32[8,512]{1,0:T(8,128)S(1)}, u32[]{:S(2)}, u32[]{:S(2)}) collective-permute-start(f32[8,512]{1,0:T(8,128)S(1)} %concatenate.3.refs_1_), channel_id=1, source_target_pairs={{8,15},{9,14},{10,13},{11,12},{12,11},{13,10},{14,9},{15,8},{24,31... | collective-permute-start | bytes 49160 | tf_op jit(solution)/shard_map/ppermute | solution.py:513
  33.0 0.6 choose.1
  33.6 0.0 collective-permute-done.5.refs_6_
  33.6 3.0 %collective-permute-start.9 = (f32[1,128,256]{2,1,0:T(8,128)S(1)}, f32[1,128,256]{2,1,0:T(8,128)S(1)}, u32[]{:S(2)}, u32[]{:S(2)}) collective-permute-start(f32[1,128,256]{2,1,0:T(8,128)S(1)} %get-tuple-element.42), channel_id=1, source_target_pairs={{0,2},{2,4},{3,1},{4,6},{5,3},{6,15},{7,5},{8,10},{9,16},{10,12},{... | collective-permute-start | bytes 393224 | tf_op jit(solution)/shard_map/ppermute | solution.py:544
  36.7 1.5 %collective-permute-done.2.refs_2_ = f32[8,512]{1,0:T(8,128)S(1)} collective-permute-done((f32[8,512]{1,0:T(8,128)S(1)}, f32[8,512]{1,0:T(8,128)S(1)}, u32[]{:S(2)}, u32[]{:S(2)}) %collective-permute-start.2) | collective-permute-done | bytes 16416 | tf_op jit(solution)/shard_map/ppermute | solution.py:513
  38.2 2.8 %collective-permute-start.10 = (f32[1,128,256]{2,1,0:T(8,128)S(1)}, f32[1,128,256]{2,1,0:T(8,128)S(1)}, u32[]{:S(2)}, u32[]{:S(2)}) collective-permute-start(f32[1,128,256]{2,1,0:T(8,128)S(1)} %get-tuple-element.43), channel_id=1, source_target_pairs={{1,2},{3,4},{2,1},{5,6},{4,3},{7,15},{6,5},{9,10},{8,16},{11,12},{... | collective-permute-start | bytes 393224 | tf_op jit(solution)/shard_map/ppermute | solution.py:544
  41.0 0.0 collective-permute-done.9.refs_11_.refs_0_
  41.0 4.9 %collective-permute-done.10.refs_12_.refs_1_ = f32[1,128,256]{2,1,0:T(8,128)S(1)} collective-permute-done((f32[1,128,256]{2,1,0:T(8,128)S(1)}, f32[1,128,256]{2,1,0:T(8,128)S(1)}, u32[]{:S(2)}, u32[]{:S(2)}) %collective-permute-start.10) | collective-permute-done | bytes 131104 | tf_op jit(solution)/shard_map/ppermute | solution.py:544
  45.9 0.0 collective-permute-done.6.refs_8_
  45.9 0.0 collective-permute-done.7.refs_9_
  45.9 0.0 collective-permute-done.8.refs_10_
  45.9 0.7 collect.1
  46.6 3.3 %collective-permute-start.11 = (f32[2,4,128,256]{3,2,1,0:T(8,128)S(1)}, f32[2,4,128,256]{3,2,1,0:T(8,128)S(1)}, u32[]{:S(2)}, u32[]{:S(2)}) collective-permute-start(f32[2,4,128,256]{3,2,1,0:T(8,128)S(1)} %get-tuple-element.45.near_ref), channel_id=1, source_target_pairs={{0,1},{1,0},{2,3},{3,2},{4,5},{5,4},{6,7},{7,6},{8,9},{9,8},{10,11... | collective-permute-start | bytes 3145736 | tf_op jit(solution)/shard_map/ppermute | solution.py:551
  49.9 3.6 %collective-permute-start.12 = (f32[3,128,256]{2,1,0:T(8,128)S(1)}, f32[3,128,256]{2,1,0:T(8,128)S(1)}, u32[]{:S(2)}, u32[]{:S(2)}) collective-permute-start(f32[3,128,256]{2,1,0:T(8,128)S(1)} %get-tuple-element.53), channel_id=1, source_target_pairs={{0,2},{2,4},{3,1},{4,6},{5,3},{6,15},{7,5},{8,10},{9,16},{10,12},{... | collective-permute-start | bytes 1179656 | tf_op jit(solution)/shard_map/ppermute | solution.py:550
  53.6 1.9 %collective-permute-start.13 = (f32[3,128,256]{2,1,0:T(8,128)S(1)}, f32[3,128,256]{2,1,0:T(8,128)S(1)}, u32[]{:S(2)}, u32[]{:S(2)}) collective-permute-start(f32[3,128,256]{2,1,0:T(8,128)S(1)} %get-tuple-element.54), channel_id=1, source_target_pairs={{1,2},{3,4},{2,1},{5,6},{4,3},{7,15},{6,5},{9,10},{8,16},{11,12},{... | collective-permute-start | bytes 1179656 | tf_op jit(solution)/shard_map/ppermute | solution.py:550
  55.5 0.0 collective-permute-done.11.far_ref
  55.5 4.0 %prepare.1 = (bf16[1024,512]{1,0:T(8,128)(2,1)S(1)}, bf16[1024,512]{1,0:T(8,128)(2,1)S(1)}, bf16[256,1024]{1,0:T(8,128)(2,1)S(1)}, bf16[256,1024]{1,0:T(8,128)(2...) custom-call(s32[4]{0:T(128)S(1)} %pad_add_fusion.info_ref.refs_0_, ...), custom_call_target="tpu_custom_call" | custom-call | flops 1073741824 | tf_op jit(solution)/shard_map/prepare/pallas_call | solution.py:445
  59.5 2.1 %collective-permute-done.12.refs_2_ = f32[3,128,256]{2,1,0:T(8,128)S(1)} collective-permute-done((f32[3,128,256]{2,1,0:T(8,128)S(1)}, f32[3,128,256]{2,1,0:T(8,128)S(1)}, u32[]{:S(2)}, u32[]{:S(2)}) %collective-permute-start.12) | collective-permute-done | bytes 393248 | tf_op jit(solution)/shard_map/ppermute | solution.py:550
  61.7 2.5 %collective-permute-done.13.refs_3_ = f32[3,128,256]{2,1,0:T(8,128)S(1)} collective-permute-done((f32[3,128,256]{2,1,0:T(8,128)S(1)}, f32[3,128,256]{2,1,0:T(8,128)S(1)}, u32[]{:S(2)}, u32[]{:S(2)}) %collective-permute-start.13) | collective-permute-done | bytes 393248 | tf_op jit(solution)/shard_map/ppermute | solution.py:550
  64.2 9.9 %region.1 = f32[8,128,256]{2,1,0:T(8,128)S(1)} custom-call(s32[4]{0:T(128)S(1)} %pad_add_fusion.info_ref.refs_0_, f32[8,512]{1,0:T(8,128)S(1)} %get-tuple-element.44.observed_ref, f32[2,4,128,256]{3,2,1,0:T(8,128)S(1)} %get-tuple-element.45.near_ref, f32[2,4,128,256]{3,2,1,0:T(8,128)S(1)} %collective-permute-done.11.far_ref, ...), custom_call_target="tpu_custom_call" | custom-call | tf_op jit(solution)/shard_map/region/pallas_call | solution.py:445
  74.1 31.0 %all_to_all.5.rows_ref = f32[8,128,256]{2,1,0:T(8,128)S(1)} all-to-all(f32[8,128,256]{2,1,0:T(8,128)S(1)} %region.1), channel_id=1, replica_groups={{0,1,2,3,4,5,6,7},{15,14,13,12,11,10,9,8},{16,17,18,19,20,21,22,23},{31..., dimensions={0} | all-to-all | bytes 2097152 | tf_op jit(solution)/shard_map/all_to_all | solution.py:569
  105.0 1.3 %unpack.1 = f32[128,8,256]{2,1,0:T(8,128)} custom-call(f32[8,128,256]{2,1,0:T(8,128)S(1)} %all_to_all.5.rows_ref), custom_call_target="tpu_custom_call" | custom-call | tf_op jit(solution)/shard_map/unpack/pallas_call | solution.py:572
  (3 shorter events, 0.0 us)
Async XLA Ops:
  0.0 8.2 %copy-start = (f32[128,8,256]{2,1,0:T(8,128)S(1)}, f32[128,8,256]{2,1,0:T(8,128)}, u32[]{:S(2)}) copy-start(f32[128,8,256]{2,1,0:T(8,128)} %field_ref.5) | copy-start | bytes 3145732
  2.2 16.0 %collective-permute-start = (f32[264,256]{1,0:T(8,128)}, f32[264,256]{1,0:T(8,128)S(1)}, u32[]{:S(2)}, u32[]{:S(2)}) collective-permute-start(f32[264,256]{1,0:T(8,128)} %get-tuple-element.31), channel_id=1, source_target_pairs={{0,8},{8,16},{16,24},{1,9},{9,17},{17,25},{2,10},{10,18},{18,26},{... | collective-permute-start | bytes 811016 | tf_op jit(solution)/shard_map/ppermute | solution.py:483
  5.6 13.7 %collective-permute-start.1 = (f32[264,256]{1,0:T(8,128)}, f32[264,256]{1,0:T(8,128)S(1)}, u32[]{:S(2)}, u32[]{:S(2)}) collective-permute-start(f32[264,256]{1,0:T(8,128)} %get-tuple-element.32), channel_id=1, source_target_pairs={{8,0},{16,8},{24,16},{9,1},{17,9},{25,17},{10,2},{18,10},{26,18},{... | collective-permute-start | bytes 811016 | tf_op jit(solution)/shard_map/ppermute | solution.py:484
  8.1 0.8 copy-start.1
  8.2 0.7 copy-start.2
  11.7 12.4 %collective-permute-start.3 = (f32[2,128,256]{2,1,0:T(8,128)S(1)}, f32[2,128,256]{2,1,0:T(8,128)S(1)}, u32[]{:S(2)}, u32[]{:S(2)}) collective-permute-start(f32[2,128,256]{2,1,0:T(8,128)S(1)} %get-tuple-element.36), channel_id=1, source_target_pairs={{0,2},{1,3},{2,4},{3,5},{8,10},{9,11},{10,12},{11,13},{16,18},{17,... | collective-permute-start | bytes 786440 | tf_op jit(solution)/shard_map/ppermute | solution.py:503
  15.2 15.9 %collective-permute-start.4 = (f32[2,128,256]{2,1,0:T(8,128)}, f32[2,128,256]{2,1,0:T(8,128)S(1)}, u32[]{:S(2)}, u32[]{:S(2)}) collective-permute-start(f32[2,128,256]{2,1,0:T(8,128)} %get-tuple-element.37), channel_id=1, source_target_pairs={{0,4},{1,5},{6,2},{7,3},{8,12},{9,13},{14,10},{15,11},{16,20},{17,... | collective-permute-start | bytes 786440 | tf_op jit(solution)/shard_map/ppermute | solution.py:503
  17.5 16.1 %collective-permute-start.5 = (f32[2,128,256]{2,1,0:T(8,128)}, f32[2,128,256]{2,1,0:T(8,128)S(1)}, u32[]{:S(2)}, u32[]{:S(2)}) collective-permute-start(f32[2,128,256]{2,1,0:T(8,128)} %get-tuple-element.38), channel_id=1, source_target_pairs={{4,2},{5,3},{6,4},{7,5},{12,10},{13,11},{14,12},{15,13},{20,18},{2... | collective-permute-start | bytes 786440 | tf_op jit(solution)/shard_map/ppermute | solution.py:503
  21.6 24.4 %collective-permute-start.6 = (f32[2,128,256]{2,1,0:T(8,128)}, f32[2,128,256]{2,1,0:T(8,128)S(1)}, u32[]{:S(2)}, u32[]{:S(2)}) collective-permute-start(f32[2,128,256]{2,1,0:T(8,128)} %get-tuple-element.39), channel_id=1, source_target_pairs={{2,0},{3,1},{4,6},{5,7},{10,8},{11,9},{12,14},{13,15},{18,16},{19,... | collective-permute-start | bytes 786440 | tf_op jit(solution)/shard_map/ppermute | solution.py:503
  22.9 23.1 %collective-permute-start.7 = (f32[2,128,256]{2,1,0:T(8,128)S(1)}, f32[2,128,256]{2,1,0:T(8,128)S(1)}, u32[]{:S(2)}, u32[]{:S(2)}) collective-permute-start(f32[2,128,256]{2,1,0:T(8,128)S(1)} %get-tuple-element.40), channel_id=1, source_target_pairs={{4,0},{5,1},{2,6},{3,7},{12,8},{13,9},{10,14},{11,15},{20,16},{21,... | collective-permute-start | bytes 786440 | tf_op jit(solution)/shard_map/ppermute | solution.py:503
  24.2 6.2 %copy-start.5 = (s32[1,512]{1,0:T(1,128)S(1)}, s32[1,512]{1,0:T(1,128)}, u32[]{:S(2)}) copy-start(s32[1,512]{1,0:T(1,128)} %param.10) | copy-start | bytes 6148
  24.2 21.8 %collective-permute-start.8 = (f32[2,128,256]{2,1,0:T(8,128)S(1)}, f32[2,128,256]{2,1,0:T(8,128)S(1)}, u32[]{:S(2)}, u32[]{:S(2)}) collective-permute-start(f32[2,128,256]{2,1,0:T(8,128)S(1)} %get-tuple-element.41), channel_id=1, source_target_pairs={{6,0},{7,1},{0,6},{1,7},{14,8},{15,9},{8,14},{9,15},{22,16},{23,17... | collective-permute-start | bytes 786440 | tf_op jit(solution)/shard_map/ppermute | solution.py:503
  30.4 0.7 copy-start.3
  30.4 0.7 copy-start.4
  31.1 7.1 %collective-permute-start.2 = (f32[8,512]{1,0:T(8,128)S(1)}, f32[8,512]{1,0:T(8,128)S(1)}, u32[]{:S(2)}, u32[]{:S(2)}) collective-permute-start(f32[8,512]{1,0:T(8,128)S(1)} %concatenate.3.refs_1_), channel_id=1, source_target_pairs={{8,15},{9,14},{10,13},{11,12},{12,11},{13,10},{14,9},{15,8},{24,31... | collective-permute-start | bytes 49160 | tf_op jit(solution)/shard_map/ppermute | solution.py:513
  33.6 7.3 %collective-permute-start.9 = (f32[1,128,256]{2,1,0:T(8,128)S(1)}, f32[1,128,256]{2,1,0:T(8,128)S(1)}, u32[]{:S(2)}, u32[]{:S(2)}) collective-permute-start(f32[1,128,256]{2,1,0:T(8,128)S(1)} %get-tuple-element.42), channel_id=1, source_target_pairs={{0,2},{2,4},{3,1},{4,6},{5,3},{6,15},{7,5},{8,10},{9,16},{10,12},{... | collective-permute-start | bytes 393224 | tf_op jit(solution)/shard_map/ppermute | solution.py:544
  38.2 7.7 %collective-permute-start.10 = (f32[1,128,256]{2,1,0:T(8,128)S(1)}, f32[1,128,256]{2,1,0:T(8,128)S(1)}, u32[]{:S(2)}, u32[]{:S(2)}) collective-permute-start(f32[1,128,256]{2,1,0:T(8,128)S(1)} %get-tuple-element.43), channel_id=1, source_target_pairs={{1,2},{3,4},{2,1},{5,6},{4,3},{7,15},{6,5},{9,10},{8,16},{11,12},{... | collective-permute-start | bytes 393224 | tf_op jit(solution)/shard_map/ppermute | solution.py:544
  46.6 8.9 %collective-permute-start.11 = (f32[2,4,128,256]{3,2,1,0:T(8,128)S(1)}, f32[2,4,128,256]{3,2,1,0:T(8,128)S(1)}, u32[]{:S(2)}, u32[]{:S(2)}) collective-permute-start(f32[2,4,128,256]{3,2,1,0:T(8,128)S(1)} %get-tuple-element.45.near_ref), channel_id=1, source_target_pairs={{0,1},{1,0},{2,3},{3,2},{4,5},{5,4},{6,7},{7,6},{8,9},{9,8},{10,11... | collective-permute-start | bytes 3145736 | tf_op jit(solution)/shard_map/ppermute | solution.py:551
  49.9 11.7 %collective-permute-start.12 = (f32[3,128,256]{2,1,0:T(8,128)S(1)}, f32[3,128,256]{2,1,0:T(8,128)S(1)}, u32[]{:S(2)}, u32[]{:S(2)}) collective-permute-start(f32[3,128,256]{2,1,0:T(8,128)S(1)} %get-tuple-element.53), channel_id=1, source_target_pairs={{0,2},{2,4},{3,1},{4,6},{5,3},{6,15},{7,5},{8,10},{9,16},{10,12},{... | collective-permute-start | bytes 1179656 | tf_op jit(solution)/shard_map/ppermute | solution.py:550
  53.6 10.6 %collective-permute-start.13 = (f32[3,128,256]{2,1,0:T(8,128)S(1)}, f32[3,128,256]{2,1,0:T(8,128)S(1)}, u32[]{:S(2)}, u32[]{:S(2)}) collective-permute-start(f32[3,128,256]{2,1,0:T(8,128)S(1)} %get-tuple-element.54), channel_id=1, source_target_pairs={{1,2},{3,4},{2,1},{5,6},{4,3},{7,15},{6,5},{9,10},{8,16},{11,12},{... | collective-permute-start | bytes 1179656 | tf_op jit(solution)/shard_map/ppermute | solution.py:550

commit v10 on v9

--- a/solution.py
+++ b/solution.py
@@ -17,12 +17,39 @@
 BF16 = jnp.bfloat16
 
 
-def pack_kernel(field_ref, flow_ref, tail_ref, head_ref):
+def pack_kernel(info_ref, field_hbm, flow_hbm, emission_hbm, first_ref, second_ref, flow_ref, emission_ref,
+                field_ref, member_ref, sems):
     members, rows, width = field_ref.shape
-    for out_ref, first, edge in ((tail_ref, rows - STEPS, rows - 1), (head_ref, 0, 0)):
-        for place in range(STEPS):
-            out_ref[pl.ds(place * members, members), :] = field_ref[:, first + place, :]
-        out_ref[pl.ds(STEPS * members, 8), :] = jnp.concatenate([flow_ref[:, edge, :]] * 2, axis=0)
+    moves = [
+        pltpu.make_async_copy(source, target, sems.at[i])
+        for i, (source, target) in enumerate(
+            ((field_hbm, field_ref), (flow_hbm, flow_ref), (emission_hbm, member_ref))
+        )
+    ]
+    for move in moves:
+        move.start()
+    for move in moves[1:]:
+        move.wait()
+    diagonal = lax.broadcasted_iota(jnp.int32, (members, members), 0) == lax.broadcasted_iota(
+        jnp.int32, (members, members), 1
+    )
+    column = jnp.sum(jnp.where(diagonal, member_ref[...], 0.0), axis=1, keepdims=True)
+    emission_ref[...] = jnp.broadcast_to(column, emission_ref.shape)
+    moves[0].wait()
+    even = info_ref[2] == 0
+    for place in range(STEPS):
+        tail, head = field_ref[:, rows - STEPS + place, :], field_ref[:, place, :]
+        at = pl.ds(place * members, members)
+        first_ref[at, :] = jnp.where(even, tail, head)
+        second_ref[at, :] = jnp.where(even, head, tail)
+    tail, head = flow_ref[:, rows - 1, :], flow_ref[:, 0, :]
+    at = pl.ds(STEPS * members, 8)
+    first_ref[at, :] = jnp.concatenate([jnp.where(even, tail, head)] * 2, axis=0)
+    second_ref[at, :] = jnp.concatenate([jnp.where(even, head, tail)] * 2, axis=0)
+
+
+def doubled(x):
+    return jnp.concatenate([x, x], axis=1)
 
 
 def weights_of(flow):
@@ -45,96 +72,81 @@
     )
 
 
-def emission_column(emission_ref):
-    members = emission_ref.shape[1]
-    diagonal = lax.broadcasted_iota(jnp.int32, (members, members), 0) == lax.broadcasted_iota(
-        jnp.int32, (members, members), 1
-    )
-    return jnp.sum(jnp.where(diagonal, emission_ref[...], 0.0), axis=1, keepdims=True)
-
-
-def second_step(info_ref, target, shift, emission, wide_ref, weight_ref, out_refs):
-    rows = weight_ref.shape[0]
-    for s, out_ref in enumerate(out_refs):
-        chip, wanted = target(s)
-
-        @pl.when(wanted)
+def inner_kernel(targets, info_ref, field_ref, flow_ref, emission_ref, kept_ref, *refs):
+    out_refs, (wide_ref, weight_ref) = refs[:-2], refs[-2:]
+    rows = field_ref.shape[1]
+    emission = doubled(emission_ref[...])
+    for row in range(1, rows - 1):
+        weights = weights_of(flow_ref[:, row, :])
+        for i, weight in enumerate(weights):
+            weight_ref[row, pl.ds(i, 1), :] = weight
+        wide_ref[row] = advance(
+            weights, emission, field_ref[:, row - 1, :], field_ref[:, row, :], field_ref[:, row + 1, :]
+        )
+    for place, row in enumerate((1, 2, rows - 3, rows - 2)):
+        kept_ref[place] = wide_ref[row]
+    for out_ref, hops in zip(out_refs, targets):
+        chip = sum(jnp.where(info_ref[0] == source, to, 0) for source, to in hops)
+
+        @pl.when(chip > 0)
         def _():
             for place in range(2):
                 position = 2 * chip + jnp.abs(info_ref[1] - 1 + place)
                 row = position + info_ref[2] * (rows - 1 - 2 * position)
                 weights = weight_ref[row]
-                at = row + shift
                 out_ref[place] = advance(
                     [weights[i : i + 1] for i in range(6)],
-                    emission, wide_ref[at - 1], wide_ref[at], wide_ref[at + 1],
+                    emission, wide_ref[row - 1], wide_ref[row], wide_ref[row + 1],
                 )
 
 
-def store_weights(flow_ref, weight_ref, rows):
-    for row in rows:
-        for i, weight in enumerate(weights_of(flow_ref[:, row, :])):
-            weight_ref[row, pl.ds(i, 1), :] = weight
-
-
-def inner_kernel(info_ref, field_ref, flow_ref, emission_ref, kept_ref, *refs):
-    out_refs, (wide_ref, weight_ref) = refs[:-2], refs[-2:]
-    rows = field_ref.shape[1]
+def end_rows(info_ref, last, field_ref, flow_ref, emission_ref, kept_ref, halo_ref, out_ref):
+    members, rows, width = field_ref.shape
+    emission = doubled(emission_ref[...])
+
+    def halo_row(place):
+        return halo_ref[pl.ds(place * members, members), :]
+
+    halo_weights = weights_of(halo_ref[pl.ds(STEPS * members, 4), :])
+    for parity in range(2):
+
+        @pl.when(info_ref[2] == parity)
+        def _():
+            if parity == last:
+                end, near, outside, beyond = 0, 1, halo_row(1), halo_row(0)
+                inside, further = kept_ref[0], kept_ref[1]
+            else:
+                end, near, outside, beyond = rows - 1, rows - 2, halo_row(0), halo_row(1)
+                inside, further = kept_ref[3], kept_ref[2]
+
+            def ordered(weights, outer, own, inner):
+                behind, ahead = (outer, inner) if end == 0 else (inner, outer)
+                return advance(weights, emission, behind, own, ahead)
+
+            end_weights = weights_of(flow_ref[:, end, :])
+            end_field = field_ref[:, end, :]
+            outer = ordered(halo_weights, beyond, outside, end_field)
+            own = ordered(end_weights, outside, end_field, field_ref[:, near, :])
+            out_ref[last] = ordered(end_weights, outer, own, inside)
+            out_ref[1 - last] = ordered(weights_of(flow_ref[:, near, :]), own, inside, further)
+
+
+def edge_kernel(info_ref, field_ref, flow_ref, emission_ref, kept_ref, last_ref, first_ref, *refs):
+    out_refs, scratch = refs[:-1], refs[-1]
     chips = len(out_refs)
-    emission = emission_column(emission_ref)
-    store_weights(flow_ref, weight_ref, range(2, rows - 2))
-    for row in range(1, rows - 1):
-        wide_ref[row] = advance(
-            weights_of(flow_ref[:, row, :]), emission,
-            field_ref[:, row - 1, :], field_ref[:, row, :], field_ref[:, row + 1, :],
-        )
-    for place, row in enumerate((1, 2, rows - 3, rows - 2)):
-        kept_ref[place] = wide_ref[row]
-
-    def target(s):
-        chip = lax.rem(info_ref[0] + s, chips)
-        return chip, jnp.logical_and(chip > 0, chip < chips - 1)
-
-    second_step(info_ref, target, 0, emission, wide_ref, weight_ref, out_refs)
-
-
-def edge_kernel(info_ref, field_ref, flow_ref, emission_ref, kept_ref, before_ref, after_ref, *refs):
-    out_refs, (wide_ref, weight_ref) = refs[:-2], refs[-2:]
-    members, rows, width = field_ref.shape
-    chips = len(out_refs)
-    emission = emission_column(emission_ref)
-    store_weights(flow_ref, weight_ref, (0, 1, rows - 2, rows - 1))
-
-    def flow_row(row):
-        if row < 0:
-            return before_ref[pl.ds(STEPS * members, 4), :]
-        if row >= rows:
-            return after_ref[pl.ds(STEPS * members, 4), :]
-        return flow_ref[:, row, :]
-
-    def start_row(row):
-        if row < 0:
-            return before_ref[pl.ds((row + STEPS) * members, members), :]
-        if row >= rows:
-            return after_ref[pl.ds((row - rows) * members, members), :]
-        return field_ref[:, row, :]
-
-    for place, row in enumerate((1, 2, rows - 3, rows - 2)):
-        wide_ref[row + 1] = kept_ref[place]
-    for row in (-1, 0, rows - 1, rows):
-        wide_ref[row + 1] = advance(
-            weights_of(flow_row(row)), emission, start_row(row - 1), start_row(row), start_row(row + 1)
-        )
-
-    def target(s):
-        first, last = info_ref[0] == s, info_ref[0] == chips - 1 - s
-        return jnp.where(first, 0, chips - 1), jnp.logical_or(first, last)
-
-    second_step(info_ref, target, 1, emission, wide_ref, weight_ref, out_refs)
-
-
-def source_of(chip, chips, s, k):
-    inner = lax.rem(chip + chips - s, chips)
+    core = info_ref[1]
+    for last, halo_ref in enumerate((first_ref, last_ref)):
+        end_rows(info_ref, last, field_ref, flow_ref, emission_ref, kept_ref, halo_ref, scratch)
+        for s, out_ref in enumerate(out_refs):
+
+            @pl.when(info_ref[0] == (chips - 1 - s if last else s))
+            def _():
+                out_ref[0] = scratch[1 - core]
+                out_ref[1] = scratch[core]
+
+
+def source_of(chip, chips, hops, k):
+    inner = sum(jnp.where(chip == to, source, 0) for source, to in hops)
     return jnp.where(chip == 0, k, jnp.where(chip == chips - 1, chips - 1 - k, inner))
 
 
@@ -232,10 +244,6 @@
 def at_cells(row, chosen):
     parts = pieces(jnp.broadcast_to(row, (8, row.shape[1])), 3)
     return (dot(parts[0], chosen) + (dot(parts[1], chosen) + dot(parts[2], chosen)))[:1]
-
-
-def doubled(x):
-    return jnp.concatenate([x, x], axis=1)
 
 
 def prepare_kernel(
@@ -477,11 +485,22 @@
     info = jnp.stack([lane // 2, lane % 2, patch % 2, jnp.int32(chips)]).astype(jnp.int32)
 
     edge = array(STEPS * step + 8, width)
-    tail, head = pl.pallas_call(
-        pack_kernel, out_shape=(edge, edge), in_specs=[VMEM] * 2, out_specs=(VMEM, VMEM), name="pack",
-    )(init_field, flow_fields)
-    before = lax.ppermute(tail, "patch", [(i, i + 1) for i in range(patches - 1)])
-    after = lax.ppermute(head, "patch", [(i + 1, i) for i in range(patches - 1)])
+    place = pl.BlockSpec(memory_space=pltpu.HBM)
+    to_last, to_first, flow, emitted = pl.pallas_call(
+        pack_kernel,
+        out_shape=[edge, edge, array(*flow_fields.shape), array(step, width // 2)],
+        in_specs=[SMEM] + [place] * 3, out_specs=[VMEM] * 4,
+        scratch_shapes=[
+            pltpu.VMEM((step, rows, width), F32), pltpu.VMEM((1, step), F32), pltpu.SemaphoreType.DMA((3,))
+        ],
+        compiler_params=pltpu.CompilerParams(vmem_limit_bytes=32 * 1024 * 1024), name="pack",
+    )(info, init_field, flow_fields, emission[None, :])
+
+    def swap(message, start):
+        lower = range(start, patches - 1, 2)
+        return lax.ppermute(message, "patch", [(p, p + 1) for p in lower] + [(p + 1, p) for p in lower])
+
+    halo_last, halo_first = swap(to_last, 0), swap(to_first, 1)
 
     mine = jnp.concatenate(
         [
@@ -494,30 +513,38 @@
         axis=0,
     )
 
-    def along(piece, s, ends):
-        if ends:
-            hops = [(s, 0), (chips - 1 - s, chips - 1)]
-        else:
-            hops = [(chip, (chip + s) % chips) for chip in range(chips)]
-            hops = [(chip, to) for chip, to in hops if 0 < to < chips - 1]
-        return lax.ppermute(piece, "member", [(2 * a + core, 2 * b + core) for a, b in hops for core in range(2)])
-
+    def between(message, hops):
+        return lax.ppermute(message, "member", [(2 * a + core, 2 * b + core) for a, b in hops for core in range(2)])
+
+    mirrored = [
+        [hop for to in range(1, chips // 2) for hop in (((to + s) % chips, to), (chips - 1 - (to + s) % chips, chips - 1 - to))]
+        for s in range(chips)
+    ]
+    turning = [[((to - s) % chips, to) for to in range(1, chips - 1)] for s in range(chips)]
+    single = all(len({source for source, _ in hops}) == len(hops) for hops in mirrored)
+    targets = mirrored if single else turning
     pair = array(2, step, width)
-    wide = [pltpu.VMEM((rows + 2, step, width), F32), pltpu.VMEM((rows, 8, width), F32)]
-    args = [info, init_field, flow_fields, emission[None, :]]
-    kept, *inner = call(inner_kernel, "inner", [array(4, step, width)] + [pair] * chips, args, wide)
-    order = list(range(1, chips))
-    got_inner = {s: along(inner[s], s, False) for s in order}
-    outer = call(edge_kernel, "edge", [pair] * chips, args + [kept, before, after], wide)
+    args = [info, init_field, flow, emitted]
+    kept, *inner = call(
+        functools.partial(inner_kernel, targets), "inner", [array(4, step, width)] + [pair] * chips, args,
+        [pltpu.VMEM((rows, step, width), F32), pltpu.VMEM((rows, 8, width), F32)], limit=32,
+    )
+    got_inner = [inner[0]] + [between(inner[s], targets[s]) for s in range(1, chips)]
+    outer = call(
+        edge_kernel, "edge", [pair] * chips, args + [kept, halo_last, halo_first],
+        [pltpu.VMEM((2, step, width), F32)], limit=32,
+    )
+    got_outer = [outer[0]] + [
+        between(outer[s], [(s, 0), (chips - 1 - s, chips - 1)]) for s in range(1, chips)
+    ]
+    order = [(targets[s], s) for s in range(chips)]
+    pieces_in = got_inner + got_outer
     mine, _ = lax.optimization_barrier((mine, outer[0]))
     other = lax.ppermute(
         mine, axes,
         [(p * lanes + i, p * lanes + lanes - 1 - i) for p in range(1, patches, 2) for i in range(lanes)],
     )
-    got_outer = {s: along(outer[s], s, True) for s in order}
-    got_inner[0], got_outer[0] = inner[0], outer[0]
-    order = [(s, s) for s in range(chips)]
-    pieces_in = [got_inner[s] for s, _ in order] + [got_outer[k] for _, k in order]
+
     def device(p, chip, core):
         return p * lanes + 2 * chip + core
 

time: 107 us -> 104 us (0.972); the launches traced: 106 us -> 102 us
  starting transfers between devices: 37 us -> 33.2 us
  blocking collectives: 31 us -> 28.5 us
  local copies, waits for them, and re-layouts: 1.38 us -> 2.63 us
    ppermute x1, starting transfers between devices: 3.31 us -> 0.07 us  [per_device(): far = lax.ppermute(near, axes, siblings)]
    all_to_all x1, blocking collectives: 31 us -> 28.5 us  [per_device(): lax.all_to_all(analysed, axes, split_axis=0, concat_axis=0, tiled=True, a...]
    ppermute x1, waiting for transfers between devices: 1.51 us -> 2.76 us  [per_device(): lax.ppermute(mine, axes, [(p * lanes + i, p * lanes + lanes - 1 - i) for...]
    unnamed x12, local copies, waits for them, and re-layouts: 1.34 us -> 2.58 us
    pallas_call x1, Pallas kernels: 2.2 us -> 1.07 us  [per_device(): pl.pallas_call(pack_kernel, out_shape=[edge, edge, array(*flow_fields.sha...]
    ppermute x1, starting transfers between devices: 3.03 us -> 1.92 us  [per_device(): lax.ppermute(early_rows[0], axes, first_pairs)]
  transfers between devices with their start and end apart: 14 -> 14, of which waited for: 5 -> 5; matrix products, arithmetic and copies ran while one was open for 0% -> 0% of each run, Pallas kernels for 9% -> 8%
where the time goes in v10:
time: 104 us; the launch traced here: 102 us
  starting transfers between devices  33.2 us (32%)
  blocking collectives  28.5 us (27%)
  Pallas kernels  23.8 us (23%)
  waiting for transfers between devices  13.1 us (13%)
  local copies, waits for them, and re-layouts  2.63 us (3%)
    all_to_all x1, blocking collectives, per_device(): lax.all_to_all(analysed, axes, split_axis=0, concat_axis=0, tiled=True, a...  28.5 us
    pallas_call x6, Pallas kernels, call(): pl.pallas_call(kernel, out_shape=out_shape, in_specs=[SMEM] + [VMEM] * (l...  21.4 us
    ppermute x6, starting transfers between devices, between(): lax.ppermute(message, 'member', [(2 * a + core, 2 * b + core) for a, b in...  15.9 us
    ppermute x1, waiting for transfers between devices, per_device(): lax.ppermute(early_rows[1], axes, second_pairs)  5.26 us
    ppermute x2, starting transfers between devices, swap(): lax.ppermute(message, 'patch', [(p, p + 1) for p in lower] + [(p + 1, p)...  4.94 us
    ppermute x1, starting transfers between devices, per_device(): lax.ppermute(late_rows[0], axes, first_pairs)  4.43 us
    ppermute x1, waiting for transfers between devices, per_device(): lax.ppermute(mine, axes, [(p * lanes + i, p * lanes + lanes - 1 - i) for...  2.76 us
    unnamed x12, local copies, waits for them, and re-layouts  2.58 us
  transfers between devices with their start and end apart: 14, of which 5 were waited for; matrix products, arithmetic and copies ran while one was open for 0% of the time, Pallas kernels for 8%

profile of v10, /device:TPU:2, one launch (start us, length us, event | category | flops | bytes accessed | tf_op | source)
XLA Modules:
  0.0 102.2 jit_solution(9229094010141764766)
XLA Ops:
  0.0 0.0 copy-start.1
  0.0 0.1 pad_add_fusion.info_ref.refs_0_
  0.1 0.0 copy-start.2
  0.1 0.7 copy-done.1
  0.8 0.0 copy-done.2
  0.8 0.0 copy-start
  0.8 1.2 %copy-done = f32[128,8,256]{2,1,0:T(8,128)S(1)} copy-done((f32[128,8,256]{2,1,0:T(8,128)S(1)}, f32[128,8,256]{2,1,0:T(8,128)}, u32[]{:S(2)}) %copy-start) | copy-done | bytes 1048600
  2.0 1.1 %pack.1 = (f32[264,256]{1,0:T(8,128)S(1)}, f32[264,256]{1,0:T(8,128)S(1)}, f32[4,8,256]{2,1,0:T(8,128)S(1)}, f32[128,128]{1,0:T(8,128)S(1)}) custom-call(s32[4]{0:T(128)S(1)} %pad_add_fusion.info_ref.refs_0_, f32[128,8,256]{2,1,0:T(8,128)S(1)} %copy-done, f32[4,8,256]{2,1,0:T(8,128)S(1)} %copy-done.1, f32[1,128]{1,0:T(1,128)S(1)} %bitcast.5), custom_call_target="tpu_custom_call" | custom-call | tf_op jit(solution)/shard_map/pack/pallas_call | solution.py:489
  3.1 0.1 collective-permute-start
  3.1 4.9 %collective-permute-start.1 = (f32[264,256]{1,0:T(8,128)S(1)}, f32[264,256]{1,0:T(8,128)S(1)}, u32[]{:S(2)}, u32[]{:S(2)}) collective-permute-start(f32[264,256]{1,0:T(8,128)S(1)} %get-tuple-element.36), channel_id=1, source_target_pairs={{8,16},{16,8},{9,17},{17,9},{10,18},{18,10},{11,19},{19,11},{12,20... | collective-permute-start | bytes 811016 | tf_op jit(solution)/shard_map/ppermute | solution.py:501
  8.0 2.2 %inner.1 = (f32[4,128,256]{2,1,0:T(8,128)S(1)}, f32[2,128,256]{2,1,0:T(8,128)S(1)}, f32[2,128,256]{2,1,0:T(8,128)S(1)}, f32[2,128,256]{2,1,0:T(8,128)S(1)}, f32[2,128,256]{2,1,0:T(8,128)S(1)}) custom-call(s32[4]{0:T(128)S(1)} %pad_add_fusion.info_ref.refs_0_, f32[128,8,256]{2,1,0:T(8,128)S(1)} %copy-done, f32[4,8,256]{2,1,0:T(8,128)S(1)} %get-tuple-element.32.flow_ref, ...), custom_call_target="tpu_custom_call" | custom-call | tf_op jit(solution)/shard_map/inner/pallas_call | solution.py:453
  10.2 0.7 collective-permute-start.3
  10.9 6.2 %collective-permute-start.4 = (f32[2,128,256]{2,1,0:T(8,128)S(1)}, f32[2,128,256]{2,1,0:T(8,128)S(1)}, u32[]{:S(2)}, u32[]{:S(2)}) collective-permute-start(f32[2,128,256]{2,1,0:T(8,128)S(1)} %get-tuple-element.41), channel_id=1, source_target_pairs={{6,2},{7,3},{0,4},{1,5},{14,10},{15,11},{8,12},{9,13},{22,18},{23,... | collective-permute-start | bytes 786440 | tf_op jit(solution)/shard_map/ppermute | solution.py:517
  17.1 1.4 %collective-permute-start.5 = (f32[2,128,256]{2,1,0:T(8,128)S(1)}, f32[2,128,256]{2,1,0:T(8,128)S(1)}, u32[]{:S(2)}, u32[]{:S(2)}) collective-permute-start(f32[2,128,256]{2,1,0:T(8,128)S(1)} %get-tuple-element.42), channel_id=1, source_target_pairs={{0,2},{1,3},{6,4},{7,5},{8,10},{9,11},{14,12},{15,13},{16,18},{17,... | collective-permute-start | bytes 786440 | tf_op jit(solution)/shard_map/ppermute | solution.py:517
  18.5 0.0 collective-permute-done.last_ref
  18.6 0.0 collective-permute-done.1.first_ref
  18.6 1.6 %edge.1 = (f32[2,128,256]{2,1,0:T(8,128)S(1)}, f32[2,128,256]{2,1,0:T(8,128)S(1)}, f32[2,128,256]{2,1,0:T(8,128)S(1)}, f32[2,128,256]{2,1,0:T(8,128)S(1)}) custom-call(s32[4]{0:T(128)S(1)} %pad_add_fusion.info_ref.refs_0_, f32[128,8,256]{2,1,0:T(8,128)S(1)} %copy-done, f32[4,8,256]{2,1,0:T(8,128)S(1)} %get-tuple-element.32.flow_ref, ...), custom_call_target="tpu_custom_call" | custom-call | tf_op jit(solution)/shard_map/edge/pallas_call | solution.py:453
  20.1 1.3 %collective-permute-start.6 = (f32[2,128,256]{2,1,0:T(8,128)S(1)}, f32[2,128,256]{2,1,0:T(8,128)S(1)}, u32[]{:S(2)}, u32[]{:S(2)}) collective-permute-start(f32[2,128,256]{2,1,0:T(8,128)S(1)} %get-tuple-element.43), channel_id=1, source_target_pairs={{2,0},{3,1},{4,6},{5,7},{10,8},{11,9},{12,14},{13,15},{18,16},{19,... | collective-permute-start | bytes 786440 | tf_op jit(solution)/shard_map/ppermute | solution.py:517
  21.4 1.3 %collective-permute-start.7 = (f32[2,128,256]{2,1,0:T(8,128)S(1)}, f32[2,128,256]{2,1,0:T(8,128)S(1)}, u32[]{:S(2)}, u32[]{:S(2)}) collective-permute-start(f32[2,128,256]{2,1,0:T(8,128)S(1)} %get-tuple-element.44), channel_id=1, source_target_pairs={{4,0},{5,1},{2,6},{3,7},{12,8},{13,9},{10,14},{11,15},{20,16},{21,... | collective-permute-start | bytes 786440 | tf_op jit(solution)/shard_map/ppermute | solution.py:517
  22.7 0.0 collective-permute-done.3.refs_4_
  22.7 0.0 copy-start.5
  22.8 5.0 %collective-permute-start.8 = (f32[2,128,256]{2,1,0:T(8,128)S(1)}, f32[2,128,256]{2,1,0:T(8,128)S(1)}, u32[]{:S(2)}, u32[]{:S(2)}) collective-permute-start(f32[2,128,256]{2,1,0:T(8,128)S(1)} %get-tuple-element.45), channel_id=1, source_target_pairs={{6,0},{7,1},{0,6},{1,7},{14,8},{15,9},{8,14},{9,15},{22,16},{23,17... | collective-permute-start | bytes 786440 | tf_op jit(solution)/shard_map/ppermute | solution.py:517
  28.4 0.0 copy-done.5
  28.5 0.0 copy-start.3
  28.5 0.0 copy-start.4
  28.5 0.6 copy-done.3
  29.2 0.0 copy-done.4
  29.2 0.0 collective-permute-done.4.refs_5_
  29.2 1.9 %collective-permute-start.2 = (f32[8,512]{1,0:T(8,128)S(1)}, f32[8,512]{1,0:T(8,128)S(1)}, u32[]{:S(2)}, u32[]{:S(2)}) collective-permute-start(f32[8,512]{1,0:T(8,128)S(1)} %concatenate.3.refs_1_), channel_id=1, source_target_pairs={{8,15},{9,14},{10,13},{11,12},{12,11},{13,10},{14,9},{15,8},{24,31... | collective-permute-start | bytes 49160 | tf_op jit(solution)/shard_map/ppermute | solution.py:543
  31.1 0.6 choose.1
  31.7 0.0 collective-permute-done.5.refs_6_
  31.7 1.9 %collective-permute-start.9 = (f32[1,128,256]{2,1,0:T(8,128)S(1)}, f32[1,128,256]{2,1,0:T(8,128)S(1)}, u32[]{:S(2)}, u32[]{:S(2)}) collective-permute-start(f32[1,128,256]{2,1,0:T(8,128)S(1)} %get-tuple-element.46), channel_id=1, source_target_pairs={{0,2},{2,4},{3,1},{4,6},{5,3},{6,15},{7,5},{8,10},{9,16},{10,12},{... | collective-permute-start | bytes 393224 | tf_op jit(solution)/shard_map/ppermute | solution.py:571
  33.7 2.8 %collective-permute-done.2.refs_2_ = f32[8,512]{1,0:T(8,128)S(1)} collective-permute-done((f32[8,512]{1,0:T(8,128)S(1)}, f32[8,512]{1,0:T(8,128)S(1)}, u32[]{:S(2)}, u32[]{:S(2)}) %collective-permute-start.2) | collective-permute-done | bytes 16416 | tf_op jit(solution)/shard_map/ppermute | solution.py:543
  36.4 1.9 %collective-permute-start.10 = (f32[1,128,256]{2,1,0:T(8,128)S(1)}, f32[1,128,256]{2,1,0:T(8,128)S(1)}, u32[]{:S(2)}, u32[]{:S(2)}) collective-permute-start(f32[1,128,256]{2,1,0:T(8,128)S(1)} %get-tuple-element.47), channel_id=1, source_target_pairs={{1,2},{3,4},{2,1},{5,6},{4,3},{7,15},{6,5},{9,10},{8,16},{11,12},{... | collective-permute-start | bytes 393224 | tf_op jit(solution)/shard_map/ppermute | solution.py:571
  38.3 0.6 collective-permute-done.9.refs_11_.refs_0_
  38.9 5.3 %collective-permute-done.10.refs_12_.refs_1_ = f32[1,128,256]{2,1,0:T(8,128)S(1)} collective-permute-done((f32[1,128,256]{2,1,0:T(8,128)S(1)}, f32[1,128,256]{2,1,0:T(8,128)S(1)}, u32[]{:S(2)}, u32[]{:S(2)}) %collective-permute-start.10) | collective-permute-done | bytes 131104 | tf_op jit(solution)/shard_map/ppermute | solution.py:571
  44.2 0.0 collective-permute-done.6.refs_8_
  44.2 0.0 collective-permute-done.7.refs_9_
  44.2 0.0 collective-permute-done.8.refs_10_
  44.2 0.7 collect.1
  44.9 0.1 collective-permute-start.11
  45.0 4.4 %collective-permute-start.12 = (f32[3,128,256]{2,1,0:T(8,128)S(1)}, f32[3,128,256]{2,1,0:T(8,128)S(1)}, u32[]{:S(2)}, u32[]{:S(2)}) collective-permute-start(f32[3,128,256]{2,1,0:T(8,128)S(1)} %get-tuple-element.57), channel_id=1, source_target_pairs={{0,2},{2,4},{3,1},{4,6},{5,3},{6,15},{7,5},{8,10},{9,16},{10,12},{... | collective-permute-start | bytes 1179656 | tf_op jit(solution)/shard_map/ppermute | solution.py:577
  49.4 2.1 %collective-permute-start.13 = (f32[3,128,256]{2,1,0:T(8,128)S(1)}, f32[3,128,256]{2,1,0:T(8,128)S(1)}, u32[]{:S(2)}, u32[]{:S(2)}) collective-permute-start(f32[3,128,256]{2,1,0:T(8,128)S(1)} %get-tuple-element.58), channel_id=1, source_target_pairs={{1,2},{3,4},{2,1},{5,6},{4,3},{7,15},{6,5},{9,10},{8,16},{11,12},{... | collective-permute-start | bytes 1179656 | tf_op jit(solution)/shard_map/ppermute | solution.py:577
  51.5 0.0 collective-permute-done.11.far_ref
  51.5 4.0 %prepare.1 = (bf16[1024,512]{1,0:T(8,128)(2,1)S(1)}, bf16[1024,512]{1,0:T(8,128)(2,1)S(1)}, bf16[256,1024]{1,0:T(8,128)(2,1)S(1)}, bf16[256,1024]{1,0:T(8,128)(2...) custom-call(s32[4]{0:T(128)S(1)} %pad_add_fusion.info_ref.refs_0_, ...), custom_call_target="tpu_custom_call" | custom-call | flops 1073741824 | tf_op jit(solution)/shard_map/prepare/pallas_call | solution.py:453
  55.5 1.9 %collective-permute-done.12.refs_2_ = f32[3,128,256]{2,1,0:T(8,128)S(1)} collective-permute-done((f32[3,128,256]{2,1,0:T(8,128)S(1)}, f32[3,128,256]{2,1,0:T(8,128)S(1)}, u32[]{:S(2)}, u32[]{:S(2)}) %collective-permute-start.12) | collective-permute-done | bytes 393248 | tf_op jit(solution)/shard_map/ppermute | solution.py:577
  57.5 2.5 %collective-permute-done.13.refs_3_ = f32[3,128,256]{2,1,0:T(8,128)S(1)} collective-permute-done((f32[3,128,256]{2,1,0:T(8,128)S(1)}, f32[3,128,256]{2,1,0:T(8,128)S(1)}, u32[]{:S(2)}, u32[]{:S(2)}) %collective-permute-start.13) | collective-permute-done | bytes 393248 | tf_op jit(solution)/shard_map/ppermute | solution.py:577
  60.0 12.4 %region.1 = f32[8,128,256]{2,1,0:T(8,128)S(1)} custom-call(s32[4]{0:T(128)S(1)} %pad_add_fusion.info_ref.refs_0_, f32[8,512]{1,0:T(8,128)S(1)} %get-tuple-element.48.observed_ref, f32[2,4,128,256]{3,2,1,0:T(8,128)S(1)} %get-tuple-element.49.near_ref, f32[2,4,128,256]{3,2,1,0:T(8,128)S(1)} %collective-permute-done.11.far_ref, ...), custom_call_target="tpu_custom_call" | custom-call | tf_op jit(solution)/shard_map/region/pallas_call | solution.py:453
  72.4 28.5 %all_to_all.5.rows_ref = f32[8,128,256]{2,1,0:T(8,128)S(1)} all-to-all(f32[8,128,256]{2,1,0:T(8,128)S(1)} %region.1), channel_id=1, replica_groups={{0,1,2,3,4,5,6,7},{15,14,13,12,11,10,9,8},{16,17,18,19,20,21,22,23},{31..., dimensions={0} | all-to-all | bytes 2097152 | tf_op jit(solution)/shard_map/all_to_all | solution.py:596
  100.9 1.3 %unpack.1 = f32[128,8,256]{2,1,0:T(8,128)} custom-call(f32[8,128,256]{2,1,0:T(8,128)S(1)} %all_to_all.5.rows_ref), custom_call_target="tpu_custom_call" | custom-call | tf_op jit(solution)/shard_map/unpack/pallas_call | solution.py:599
  (3 shorter events, 0.0 us)
Async XLA Ops:
  0.0 0.8 copy-start.1
  0.1 0.7 copy-start.2
  0.8 1.2 %copy-start = (f32[128,8,256]{2,1,0:T(8,128)S(1)}, f32[128,8,256]{2,1,0:T(8,128)}, u32[]{:S(2)}) copy-start(f32[128,8,256]{2,1,0:T(8,128)} %field_ref.3) | copy-start | bytes 3145732
  3.1 15.5 %collective-permute-start = (f32[264,256]{1,0:T(8,128)S(1)}, f32[264,256]{1,0:T(8,128)S(1)}, u32[]{:S(2)}, u32[]{:S(2)}) collective-permute-start(f32[264,256]{1,0:T(8,128)S(1)} %get-tuple-element.35), channel_id=1, source_target_pairs={{0,8},{16,24},{8,0},{24,16},{1,9},{17,25},{9,1},{25,17},{2,10},{18... | collective-permute-start | bytes 811016 | tf_op jit(solution)/shard_map/ppermute | solution.py:501
  3.1 15.4 %collective-permute-start.1 = (f32[264,256]{1,0:T(8,128)S(1)}, f32[264,256]{1,0:T(8,128)S(1)}, u32[]{:S(2)}, u32[]{:S(2)}) collective-permute-start(f32[264,256]{1,0:T(8,128)S(1)} %get-tuple-element.36), channel_id=1, source_target_pairs={{8,16},{16,8},{9,17},{17,9},{10,18},{18,10},{11,19},{19,11},{12,20... | collective-permute-start | bytes 811016 | tf_op jit(solution)/shard_map/ppermute | solution.py:501
  10.2 12.5 %collective-permute-start.3 = (f32[2,128,256]{2,1,0:T(8,128)S(1)}, f32[2,128,256]{2,1,0:T(8,128)S(1)}, u32[]{:S(2)}, u32[]{:S(2)}) collective-permute-start(f32[2,128,256]{2,1,0:T(8,128)S(1)} %get-tuple-element.40), channel_id=1, source_target_pairs={{4,2},{5,3},{2,4},{3,5},{12,10},{13,11},{10,12},{11,13},{20,18},{2... | collective-permute-start | bytes 786440 | tf_op jit(solution)/shard_map/ppermute | solution.py:517
  10.9 18.3 %collective-permute-start.4 = (f32[2,128,256]{2,1,0:T(8,128)S(1)}, f32[2,128,256]{2,1,0:T(8,128)S(1)}, u32[]{:S(2)}, u32[]{:S(2)}) collective-permute-start(f32[2,128,256]{2,1,0:T(8,128)S(1)} %get-tuple-element.41), channel_id=1, source_target_pairs={{6,2},{7,3},{0,4},{1,5},{14,10},{15,11},{8,12},{9,13},{22,18},{23,... | collective-permute-start | bytes 786440 | tf_op jit(solution)/shard_map/ppermute | solution.py:517
  17.1 14.6 %collective-permute-start.5 = (f32[2,128,256]{2,1,0:T(8,128)S(1)}, f32[2,128,256]{2,1,0:T(8,128)S(1)}, u32[]{:S(2)}, u32[]{:S(2)}) collective-permute-start(f32[2,128,256]{2,1,0:T(8,128)S(1)} %get-tuple-element.42), channel_id=1, source_target_pairs={{0,2},{1,3},{6,4},{7,5},{8,10},{9,11},{14,12},{15,13},{16,18},{17,... | collective-permute-start | bytes 786440 | tf_op jit(solution)/shard_map/ppermute | solution.py:517
  20.1 24.0 %collective-permute-start.6 = (f32[2,128,256]{2,1,0:T(8,128)S(1)}, f32[2,128,256]{2,1,0:T(8,128)S(1)}, u32[]{:S(2)}, u32[]{:S(2)}) collective-permute-start(f32[2,128,256]{2,1,0:T(8,128)S(1)} %get-tuple-element.43), channel_id=1, source_target_pairs={{2,0},{3,1},{4,6},{5,7},{10,8},{11,9},{12,14},{13,15},{18,16},{19,... | collective-permute-start | bytes 786440 | tf_op jit(solution)/shard_map/ppermute | solution.py:517
  21.4 22.8 %collective-permute-start.7 = (f32[2,128,256]{2,1,0:T(8,128)S(1)}, f32[2,128,256]{2,1,0:T(8,128)S(1)}, u32[]{:S(2)}, u32[]{:S(2)}) collective-permute-start(f32[2,128,256]{2,1,0:T(8,128)S(1)} %get-tuple-element.44), channel_id=1, source_target_pairs={{4,0},{5,1},{2,6},{3,7},{12,8},{13,9},{10,14},{11,15},{20,16},{21,... | collective-permute-start | bytes 786440 | tf_op jit(solution)/shard_map/ppermute | solution.py:517
  22.7 5.7 %copy-start.5 = (s32[1,512]{1,0:T(1,128)S(1)}, s32[1,512]{1,0:T(1,128)}, u32[]{:S(2)}) copy-start(s32[1,512]{1,0:T(1,128)} %param.10) | copy-start | bytes 6148
  22.8 21.4 %collective-permute-start.8 = (f32[2,128,256]{2,1,0:T(8,128)S(1)}, f32[2,128,256]{2,1,0:T(8,128)S(1)}, u32[]{:S(2)}, u32[]{:S(2)}) collective-permute-start(f32[2,128,256]{2,1,0:T(8,128)S(1)} %get-tuple-element.45), channel_id=1, source_target_pairs={{6,0},{7,1},{0,6},{1,7},{14,8},{15,9},{8,14},{9,15},{22,16},{23,17... | collective-permute-start | bytes 786440 | tf_op jit(solution)/shard_map/ppermute | solution.py:517
  28.5 0.7 copy-start.3
  28.5 0.7 copy-start.4
  29.2 7.2 %collective-permute-start.2 = (f32[8,512]{1,0:T(8,128)S(1)}, f32[8,512]{1,0:T(8,128)S(1)}, u32[]{:S(2)}, u32[]{:S(2)}) collective-permute-start(f32[8,512]{1,0:T(8,128)S(1)} %concatenate.3.refs_1_), channel_id=1, source_target_pairs={{8,15},{9,14},{10,13},{11,12},{12,11},{13,10},{14,9},{15,8},{24,31... | collective-permute-start | bytes 49160 | tf_op jit(solution)/shard_map/ppermute | solution.py:543
  31.7 7.2 %collective-permute-start.9 = (f32[1,128,256]{2,1,0:T(8,128)S(1)}, f32[1,128,256]{2,1,0:T(8,128)S(1)}, u32[]{:S(2)}, u32[]{:S(2)}) collective-permute-start(f32[1,128,256]{2,1,0:T(8,128)S(1)} %get-tuple-element.46), channel_id=1, source_target_pairs={{0,2},{2,4},{3,1},{4,6},{5,3},{6,15},{7,5},{8,10},{9,16},{10,12},{... | collective-permute-start | bytes 393224 | tf_op jit(solution)/shard_map/ppermute | solution.py:571
  36.4 7.7 %collective-permute-start.10 = (f32[1,128,256]{2,1,0:T(8,128)S(1)}, f32[1,128,256]{2,1,0:T(8,128)S(1)}, u32[]{:S(2)}, u32[]{:S(2)}) collective-permute-start(f32[1,128,256]{2,1,0:T(8,128)S(1)} %get-tuple-element.47), channel_id=1, source_target_pairs={{1,2},{3,4},{2,1},{5,6},{4,3},{7,15},{6,5},{9,10},{8,16},{11,12},{... | collective-permute-start | bytes 393224 | tf_op jit(solution)/shard_map/ppermute | solution.py:571
  44.9 6.6 %collective-permute-start.11 = (f32[2,4,128,256]{3,2,1,0:T(8,128)S(1)}, f32[2,4,128,256]{3,2,1,0:T(8,128)S(1)}, u32[]{:S(2)}, u32[]{:S(2)}) collective-permute-start(f32[2,4,128,256]{3,2,1,0:T(8,128)S(1)} %get-tuple-element.49.near_ref), channel_id=1, source_target_pairs={{0,1},{1,0},{2,3},{3,2},{4,5},{5,4},{6,7},{7,6},{8,9},{9,8},{10,11... | collective-permute-start | bytes 3145736 | tf_op jit(solution)/shard_map/ppermute | solution.py:578
  45.0 12.5 %collective-permute-start.12 = (f32[3,128,256]{2,1,0:T(8,128)S(1)}, f32[3,128,256]{2,1,0:T(8,128)S(1)}, u32[]{:S(2)}, u32[]{:S(2)}) collective-permute-start(f32[3,128,256]{2,1,0:T(8,128)S(1)} %get-tuple-element.57), channel_id=1, source_target_pairs={{0,2},{2,4},{3,1},{4,6},{5,3},{6,15},{7,5},{8,10},{9,16},{10,12},{... | collective-permute-start | bytes 1179656 | tf_op jit(solution)/shard_map/ppermute | solution.py:577
  49.4 10.6 %collective-permute-start.13 = (f32[3,128,256]{2,1,0:T(8,128)S(1)}, f32[3,128,256]{2,1,0:T(8,128)S(1)}, u32[]{:S(2)}, u32[]{:S(2)}) collective-permute-start(f32[3,128,256]{2,1,0:T(8,128)S(1)} %get-tuple-element.58), channel_id=1, source_target_pairs={{1,2},{3,4},{2,1},{5,6},{4,3},{7,15},{6,5},{9,10},{8,16},{11,12},{... | collective-permute-start | bytes 1179656 | tf_op jit(solution)/shard_map/ppermute | solution.py:577

commit v11 on v10

--- a/solution.py
+++ b/solution.py
@@ -183,8 +183,13 @@
                     late_own[late.index(index)] = ref[1]
 
 
-def unpack_kernel(rows_ref, out_ref):
-    for row in range(rows_ref.shape[0]):
+def unpack_kernel(order, info_ref, *refs):
+    row_refs, out_ref, rows_ref = refs[:-2], refs[-2], refs[-1]
+    rows = rows_ref.shape[0]
+    for x, ref in zip(order, row_refs):
+        position = (2 * info_ref[0] + info_ref[1]) ^ x
+        rows_ref[position + info_ref[2] * (rows - 1 - 2 * position)] = ref[...]
+    for row in range(rows):
         out_ref[:, row, :] = rows_ref[row]
 
 
@@ -318,8 +323,9 @@
     order, groups, info_ref, observed_ref, near_ref, far_ref, high_in, low_in, own_high, own_low, own_part, seen_ref,
     direction_ref, *refs,
 ):
-    outer_refs, (out_ref, spread_high, spread_low, factor, answer) = refs[:-5], refs[-5:]
     _, chips, step, width = near_ref.shape
+    outer_refs, out_refs = refs[: 2 * len(groups)], refs[2 * len(groups) : -4]
+    spread_high, spread_low, factor, answer = refs[-4:]
     members = 2 * chips * step
     slots = observed_ref.shape[1]
     root = math.sqrt(members - 1)
@@ -430,14 +436,13 @@
     sides = product(pieces(sides, 3), parts)
     shift, along = sides[0:1], sides[1:2]
     halved = [part * jnp.asarray(-0.5, BF16) for part in pieces(solved, 2)]
-    for part, ref, place in ((0, near_ref, 1), (1, far_ref, 0)):
-        for chip in range(chips):
-            block = blocks[part * chips + chip]
-            moved = product([spread_high[block, :], spread_low[block, :]], halved)
-            moved = moved + doubled(direction_ref[block, :]) * along
-            lane = 2 * chip + jnp.abs(core - part)
-            lane = lane + info_ref[2] * (2 * chips - 1 - 2 * lane)
-            out_ref[lane] = ref[place, chip] + shift + moved
+    for x, out_ref in enumerate(out_refs):
+        chip, part = info_ref[0] ^ (x // 2), x % 2
+        rows = pl.ds(pl.multiple_of((part * chips + chip) * step, step), step)
+        moved = product([spread_high[rows, :], spread_low[rows, :]], halved)
+        moved = moved + doubled(direction_ref[rows, :]) * along
+        own = far_ref[0, chip] if part else near_ref[1, chip]
+        out_ref[...] = own + shift + moved
 
 
 VMEM = pl.BlockSpec(memory_space=pltpu.VMEM)
@@ -587,19 +592,19 @@
         flops=8 * members * slots * width, limit=20,
     )
     analysed = call(
-        functools.partial(region_kernel, order, groups), "region", array(lanes, step, width),
+        functools.partial(region_kernel, order, groups), "region", [array(step, width)] * lanes,
         [info, observed, near, far, *prepared, *outer_rows],
         split + [pltpu.VMEM((slots, slots), F32), pltpu.VMEM((width + 8, slots), F32)],
         limit=24,
     )
-    lines = [[p * lanes + (lanes - 1 - i if p % 2 else i) for i in range(lanes)] for p in range(patches)]
-    returned = lax.all_to_all(
-        analysed, axes, split_axis=0, concat_axis=0, tiled=True, axis_index_groups=lines
-    )
-    return pl.pallas_call(
-        unpack_kernel, out_shape=array(step, rows, width), in_specs=[VMEM], out_specs=VMEM, name="unpack",
-        compiler_params=pltpu.CompilerParams(vmem_limit_bytes=48 * 1024 * 1024),
-    )(returned)
+    def swapped(x):
+        return lax.ppermute(analysed[x], "member", [(i, i ^ x) for i in range(lanes)]) if x else analysed[0]
+
+    order = sorted(range(lanes), key=lambda x: (x.bit_length() != lanes.bit_length() - 1, -x))
+    return call(
+        functools.partial(unpack_kernel, order), "unpack", array(step, rows, width),
+        [info] + [swapped(x) for x in order], [pltpu.VMEM((rows, step, width), F32)], limit=48,
+    )
 
 
 def solution(mesh):

time: 104 us -> 102 us (0.981); the launches traced: 102 us -> 101 us
  blocking collectives: 28.5 us -> 0 us
  starting transfers between devices: 33.2 us -> 51.2 us
  waiting for transfers between devices: 13.1 us -> 22 us
    all_to_all x1 -> x0, blocking collectives: 28.5 us -> none  [per_device(): lax.all_to_all(analysed, axes, split_axis=0, concat_axis=0, tiled=True, a...]
    ppermute x0 -> x7, starting transfers between devices: none -> 18.1 us  [swapped(): lax.ppermute(analysed[x], 'member', [(i, i ^ x) for i in range(lanes)])]
    ppermute x0 -> x7, waiting for transfers between devices: none -> 8.91 us  [swapped(): lax.ppermute(analysed[x], 'member', [(i, i ^ x) for i in range(lanes)])]
    pallas_call x6 -> x7, Pallas kernels: 21.4 us -> 23.4 us  [call(): pl.pallas_call(kernel, out_shape=out_shape, in_specs=[SMEM] + [VMEM] * (l...]
    pallas_call x1 -> x0, Pallas kernels: 1.31 us -> none  [per_device(): pl.pallas_call(unpack_kernel, out_shape=array(step, rows, width), in_spec...]
  transfers between devices with their start and end apart: 14 -> 21, of which waited for: 5 -> 9; matrix products, arithmetic and copies ran while one was open for 0% -> 0% of each run, Pallas kernels for 8% -> 8%
where the time goes in v11:
time: 102 us; the launch traced here: 101 us
  starting transfers between devices  51.2 us (50%)
  Pallas kernels  24.4 us (24%)
  waiting for transfers between devices  22 us (22%)
  local copies, waits for them, and re-layouts  2.63 us (3%)
    pallas_call x7, Pallas kernels, call(): pl.pallas_call(kernel, out_shape=out_shape, in_specs=[SMEM] + [VMEM] * (l...  23.4 us
    ppermute x7, starting transfers between devices, swapped(): lax.ppermute(analysed[x], 'member', [(i, i ^ x) for i in range(lanes)])  18.1 us
    ppermute x6, starting transfers between devices, between(): lax.ppermute(message, 'member', [(2 * a + core, 2 * b + core) for a, b in...  15.9 us
    ppermute x7, waiting for transfers between devices, swapped(): lax.ppermute(analysed[x], 'member', [(i, i ^ x) for i in range(lanes)])  8.91 us
    ppermute x1, waiting for transfers between devices, per_device(): lax.ppermute(early_rows[1], axes, second_pairs)  5.26 us
    ppermute x2, starting transfers between devices, swap(): lax.ppermute(message, 'patch', [(p, p + 1) for p in lower] + [(p + 1, p)...  4.94 us
    ppermute x1, starting transfers between devices, per_device(): lax.ppermute(late_rows[0], axes, first_pairs)  4.43 us
    ppermute x1, waiting for transfers between devices, per_device(): lax.ppermute(mine, axes, [(p * lanes + i, p * lanes + lanes - 1 - i) for...  2.76 us
  transfers between devices with their start and end apart: 21, of which 9 were waited for; matrix products, arithmetic and copies ran while one was open for 0% of the time, Pallas kernels for 8%

profile of v11, /device:TPU:2, one launch (start us, length us, event | category | flops | bytes accessed | tf_op | source)
XLA Modules:
  0.0 101.3 jit_solution(15420960600562626205)
XLA Ops:
  0.0 0.0 copy-start.1
  0.0 0.1 pad_add_fusion.info_ref.refs_0_
  0.1 0.0 copy-start.2
  0.1 0.7 copy-done.1
  0.8 0.0 copy-done.2
  0.8 0.0 copy-start
  0.8 1.2 %copy-done = f32[128,8,256]{2,1,0:T(8,128)S(1)} copy-done((f32[128,8,256]{2,1,0:T(8,128)S(1)}, f32[128,8,256]{2,1,0:T(8,128)}, u32[]{:S(2)}) %copy-start) | copy-done | bytes 1048600
  2.0 1.1 %pack.1 = (f32[264,256]{1,0:T(8,128)S(1)}, f32[264,256]{1,0:T(8,128)S(1)}, f32[4,8,256]{2,1,0:T(8,128)S(1)}, f32[128,128]{1,0:T(8,128)S(1)}) custom-call(s32[4]{0:T(128)S(1)} %pad_add_fusion.info_ref.refs_0_, f32[128,8,256]{2,1,0:T(8,128)S(1)} %copy-done, f32[4,8,256]{2,1,0:T(8,128)S(1)} %copy-done.1, f32[1,128]{1,0:T(1,128)S(1)} %bitcast.5), custom_call_target="tpu_custom_call" | custom-call | tf_op jit(solution)/shard_map/pack/pallas_call | solution.py:494
  3.1 0.1 collective-permute-start
  3.1 4.9 %collective-permute-start.1 = (f32[264,256]{1,0:T(8,128)S(1)}, f32[264,256]{1,0:T(8,128)S(1)}, u32[]{:S(2)}, u32[]{:S(2)}) collective-permute-start(f32[264,256]{1,0:T(8,128)S(1)} %get-tuple-element.44), channel_id=1, source_target_pairs={{8,16},{16,8},{9,17},{17,9},{10,18},{18,10},{11,19},{19,11},{12,20... | collective-permute-start | bytes 811016 | tf_op jit(solution)/shard_map/ppermute | solution.py:506
  8.0 2.2 %inner.1 = (f32[4,128,256]{2,1,0:T(8,128)S(1)}, f32[2,128,256]{2,1,0:T(8,128)S(1)}, f32[2,128,256]{2,1,0:T(8,128)S(1)}, f32[2,128,256]{2,1,0:T(8,128)S(1)}, f32[2,128,256]{2,1,0:T(8,128)S(1)}) custom-call(s32[4]{0:T(128)S(1)} %pad_add_fusion.info_ref.refs_0_, f32[128,8,256]{2,1,0:T(8,128)S(1)} %copy-done, f32[4,8,256]{2,1,0:T(8,128)S(1)} %get-tuple-element.40.flow_ref, ...), custom_call_target="tpu_custom_call" | custom-call | tf_op jit(solution)/shard_map/inner/pallas_call | solution.py:458
  10.2 0.7 collective-permute-start.3
  10.9 6.2 %collective-permute-start.4 = (f32[2,128,256]{2,1,0:T(8,128)S(1)}, f32[2,128,256]{2,1,0:T(8,128)S(1)}, u32[]{:S(2)}, u32[]{:S(2)}) collective-permute-start(f32[2,128,256]{2,1,0:T(8,128)S(1)} %get-tuple-element.49), channel_id=1, source_target_pairs={{6,2},{7,3},{0,4},{1,5},{14,10},{15,11},{8,12},{9,13},{22,18},{23,... | collective-permute-start | bytes 786440 | tf_op jit(solution)/shard_map/ppermute | solution.py:522
  17.1 1.4 %collective-permute-start.5 = (f32[2,128,256]{2,1,0:T(8,128)S(1)}, f32[2,128,256]{2,1,0:T(8,128)S(1)}, u32[]{:S(2)}, u32[]{:S(2)}) collective-permute-start(f32[2,128,256]{2,1,0:T(8,128)S(1)} %get-tuple-element.50), channel_id=1, source_target_pairs={{0,2},{1,3},{6,4},{7,5},{8,10},{9,11},{14,12},{15,13},{16,18},{17,... | collective-permute-start | bytes 786440 | tf_op jit(solution)/shard_map/ppermute | solution.py:522
  18.5 0.0 collective-permute-done.last_ref
  18.6 0.0 collective-permute-done.1.first_ref
  18.6 1.6 %edge.1 = (f32[2,128,256]{2,1,0:T(8,128)S(1)}, f32[2,128,256]{2,1,0:T(8,128)S(1)}, f32[2,128,256]{2,1,0:T(8,128)S(1)}, f32[2,128,256]{2,1,0:T(8,128)S(1)}) custom-call(s32[4]{0:T(128)S(1)} %pad_add_fusion.info_ref.refs_0_, f32[128,8,256]{2,1,0:T(8,128)S(1)} %copy-done, f32[4,8,256]{2,1,0:T(8,128)S(1)} %get-tuple-element.40.flow_ref, ...), custom_call_target="tpu_custom_call" | custom-call | tf_op jit(solution)/shard_map/edge/pallas_call | solution.py:458
  20.1 1.3 %collective-permute-start.6 = (f32[2,128,256]{2,1,0:T(8,128)S(1)}, f32[2,128,256]{2,1,0:T(8,128)S(1)}, u32[]{:S(2)}, u32[]{:S(2)}) collective-permute-start(f32[2,128,256]{2,1,0:T(8,128)S(1)} %get-tuple-element.51), channel_id=1, source_target_pairs={{2,0},{3,1},{4,6},{5,7},{10,8},{11,9},{12,14},{13,15},{18,16},{19,... | collective-permute-start | bytes 786440 | tf_op jit(solution)/shard_map/ppermute | solution.py:522
  21.4 1.3 %collective-permute-start.7 = (f32[2,128,256]{2,1,0:T(8,128)S(1)}, f32[2,128,256]{2,1,0:T(8,128)S(1)}, u32[]{:S(2)}, u32[]{:S(2)}) collective-permute-start(f32[2,128,256]{2,1,0:T(8,128)S(1)} %get-tuple-element.52), channel_id=1, source_target_pairs={{4,0},{5,1},{2,6},{3,7},{12,8},{13,9},{10,14},{11,15},{20,16},{21,... | collective-permute-start | bytes 786440 | tf_op jit(solution)/shard_map/ppermute | solution.py:522
  22.7 0.0 collective-permute-done.3.refs_4_
  22.7 0.0 copy-start.5
  22.8 5.0 %collective-permute-start.8 = (f32[2,128,256]{2,1,0:T(8,128)S(1)}, f32[2,128,256]{2,1,0:T(8,128)S(1)}, u32[]{:S(2)}, u32[]{:S(2)}) collective-permute-start(f32[2,128,256]{2,1,0:T(8,128)S(1)} %get-tuple-element.53), channel_id=1, source_target_pairs={{6,0},{7,1},{0,6},{1,7},{14,8},{15,9},{8,14},{9,15},{22,16},{23,17... | collective-permute-start | bytes 786440 | tf_op jit(solution)/shard_map/ppermute | solution.py:522
  28.4 0.0 copy-done.5
  28.5 0.0 copy-start.3
  28.5 0.0 copy-start.4
  28.5 0.6 copy-done.3
  29.2 0.0 copy-done.4
  29.2 0.0 collective-permute-done.4.refs_5_
  29.2 1.9 %collective-permute-start.2 = (f32[8,512]{1,0:T(8,128)S(1)}, f32[8,512]{1,0:T(8,128)S(1)}, u32[]{:S(2)}, u32[]{:S(2)}) collective-permute-start(f32[8,512]{1,0:T(8,128)S(1)} %concatenate.3.refs_1_), channel_id=1, source_target_pairs={{8,15},{9,14},{10,13},{11,12},{12,11},{13,10},{14,9},{15,8},{24,31... | collective-permute-start | bytes 49160 | tf_op jit(solution)/shard_map/ppermute | solution.py:548
  31.1 0.6 choose.1
  31.7 0.0 collective-permute-done.5.refs_6_
  31.7 1.9 %collective-permute-start.9 = (f32[1,128,256]{2,1,0:T(8,128)S(1)}, f32[1,128,256]{2,1,0:T(8,128)S(1)}, u32[]{:S(2)}, u32[]{:S(2)}) collective-permute-start(f32[1,128,256]{2,1,0:T(8,128)S(1)} %get-tuple-element.54), channel_id=1, source_target_pairs={{0,2},{2,4},{3,1},{4,6},{5,3},{6,15},{7,5},{8,10},{9,16},{10,12},{... | collective-permute-start | bytes 393224 | tf_op jit(solution)/shard_map/ppermute | solution.py:576
  33.7 2.8 %collective-permute-done.2.refs_2_ = f32[8,512]{1,0:T(8,128)S(1)} collective-permute-done((f32[8,512]{1,0:T(8,128)S(1)}, f32[8,512]{1,0:T(8,128)S(1)}, u32[]{:S(2)}, u32[]{:S(2)}) %collective-permute-start.2) | collective-permute-done | bytes 16416 | tf_op jit(solution)/shard_map/ppermute | solution.py:548
  36.4 1.9 %collective-permute-start.10 = (f32[1,128,256]{2,1,0:T(8,128)S(1)}, f32[1,128,256]{2,1,0:T(8,128)S(1)}, u32[]{:S(2)}, u32[]{:S(2)}) collective-permute-start(f32[1,128,256]{2,1,0:T(8,128)S(1)} %get-tuple-element.55), channel_id=1, source_target_pairs={{1,2},{3,4},{2,1},{5,6},{4,3},{7,15},{6,5},{9,10},{8,16},{11,12},{... | collective-permute-start | bytes 393224 | tf_op jit(solution)/shard_map/ppermute | solution.py:576
  38.3 0.6 collective-permute-done.9.refs_11_.refs_0_
  38.9 5.3 %collective-permute-done.10.refs_12_.refs_1_ = f32[1,128,256]{2,1,0:T(8,128)S(1)} collective-permute-done((f32[1,128,256]{2,1,0:T(8,128)S(1)}, f32[1,128,256]{2,1,0:T(8,128)S(1)}, u32[]{:S(2)}, u32[]{:S(2)}) %collective-permute-start.10) | collective-permute-done | bytes 131104 | tf_op jit(solution)/shard_map/ppermute | solution.py:576
  44.2 0.0 collective-permute-done.6.refs_8_
  44.2 0.0 collective-permute-done.7.refs_9_
  44.2 0.0 collective-permute-done.8.refs_10_
  44.2 0.7 collect.1
  44.9 0.1 collective-permute-start.11
  45.0 4.4 %collective-permute-start.12 = (f32[3,128,256]{2,1,0:T(8,128)S(1)}, f32[3,128,256]{2,1,0:T(8,128)S(1)}, u32[]{:S(2)}, u32[]{:S(2)}) collective-permute-start(f32[3,128,256]{2,1,0:T(8,128)S(1)} %get-tuple-element.65), channel_id=1, source_target_pairs={{0,2},{2,4},{3,1},{4,6},{5,3},{6,15},{7,5},{8,10},{9,16},{10,12},{... | collective-permute-start | bytes 1179656 | tf_op jit(solution)/shard_map/ppermute | solution.py:582
  49.4 2.1 %collective-permute-start.13 = (f32[3,128,256]{2,1,0:T(8,128)S(1)}, f32[3,128,256]{2,1,0:T(8,128)S(1)}, u32[]{:S(2)}, u32[]{:S(2)}) collective-permute-start(f32[3,128,256]{2,1,0:T(8,128)S(1)} %get-tuple-element.66), channel_id=1, source_target_pairs={{1,2},{3,4},{2,1},{5,6},{4,3},{7,15},{6,5},{9,10},{8,16},{11,12},{... | collective-permute-start | bytes 1179656 | tf_op jit(solution)/shard_map/ppermute | solution.py:582
  51.5 0.0 collective-permute-done.11.far_ref
  51.5 4.0 %prepare.1 = (bf16[1024,512]{1,0:T(8,128)(2,1)S(1)}, bf16[1024,512]{1,0:T(8,128)(2,1)S(1)}, bf16[256,1024]{1,0:T(8,128)(2,1)S(1)}, bf16[256,1024]{1,0:T(8,128)(2...) custom-call(s32[4]{0:T(128)S(1)} %pad_add_fusion.info_ref.refs_0_, ...), custom_call_target="tpu_custom_call" | custom-call | flops 1073741824 | tf_op jit(solution)/shard_map/prepare/pallas_call | solution.py:458
  55.5 1.9 %collective-permute-done.12.refs_2_ = f32[3,128,256]{2,1,0:T(8,128)S(1)} collective-permute-done((f32[3,128,256]{2,1,0:T(8,128)S(1)}, f32[3,128,256]{2,1,0:T(8,128)S(1)}, u32[]{:S(2)}, u32[]{:S(2)}) %collective-permute-start.12) | collective-permute-done | bytes 393248 | tf_op jit(solution)/shard_map/ppermute | solution.py:582
  57.5 2.5 %collective-permute-done.13.refs_3_ = f32[3,128,256]{2,1,0:T(8,128)S(1)} collective-permute-done((f32[3,128,256]{2,1,0:T(8,128)S(1)}, f32[3,128,256]{2,1,0:T(8,128)S(1)}, u32[]{:S(2)}, u32[]{:S(2)}) %collective-permute-start.13) | collective-permute-done | bytes 393248 | tf_op jit(solution)/shard_map/ppermute | solution.py:582
  60.0 12.4 %region.1 = (f32[128,256]{1,0:T(8,128)S(1)}, f32[128,256]{1,0:T(8,128)S(1)}, f32[128,256]{1,0:T(8,128)S(1)}, f32[128,256]{1,0:T(8,128)S(1)}, f32[128,256]{1,0:T(...) custom-call(s32[4]{0:T(128)S(1)} %pad_add_fusion.info_ref.refs_0_, ...), custom_call_target="tpu_custom_call" | custom-call | tf_op jit(solution)/shard_map/region/pallas_call | solution.py:458
  72.4 1.2 %collective-permute-start.14 = (f32[128,256]{1,0:T(8,128)S(1)}, f32[128,256]{1,0:T(8,128)S(1)}, u32[]{:S(2)}, u32[]{:S(2)}) collective-permute-start(f32[128,256]{1,0:T(8,128)S(1)} %get-tuple-element.67), channel_id=1, source_target_pairs={{0,7},{1,6},{2,5},{3,4},{4,3},{5,2},{6,1},{7,0},{8,15},{9,14},{10,... | collective-permute-start | bytes 393224 | tf_op jit(solution)/shard_map/ppermute | solution.py:601
  73.6 0.7 collective-permute-start.15
  74.2 0.8 collective-permute-start.16
  75.0 3.6 %collective-permute-start.17 = (f32[128,256]{1,0:T(8,128)S(1)}, f32[128,256]{1,0:T(8,128)S(1)}, u32[]{:S(2)}, u32[]{:S(2)}) collective-permute-start(f32[128,256]{1,0:T(8,128)S(1)} %get-tuple-element.70), channel_id=1, source_target_pairs={{0,4},{1,5},{2,6},{3,7},{4,0},{5,1},{6,2},{7,3},{8,12},{9,13},{10,... | collective-permute-start | bytes 393224 | tf_op jit(solution)/shard_map/ppermute | solution.py:601
  78.6 0.0 collective-permute-start.18
  78.6 0.1 collective-permute-done.14.refs_0_
  78.7 11.8 %collective-permute-start.19 = (f32[128,256]{1,0:T(8,128)S(1)}, f32[128,256]{1,0:T(8,128)S(1)}, u32[]{:S(2)}, u32[]{:S(2)}) collective-permute-start(f32[128,256]{1,0:T(8,128)S(1)} %get-tuple-element.72), channel_id=1, source_target_pairs={{0,2},{1,3},{2,0},{3,1},{4,6},{5,7},{6,4},{7,5},{8,10},{9,11},{10,... | collective-permute-start | bytes 393224 | tf_op jit(solution)/shard_map/ppermute | solution.py:601
  90.5 0.0 collective-permute-done.15.refs_1_
  90.5 0.0 collective-permute-start.20
  90.5 5.2 %collective-permute-done.16.refs_2_ = f32[128,256]{1,0:T(8,128)S(1)} collective-permute-done((f32[128,256]{1,0:T(8,128)S(1)}, f32[128,256]{1,0:T(8,128)S(1)}, u32[]{:S(2)}, u32[]{:S(2)}) %collective-permute-start.16) | collective-permute-done | bytes 131104 | tf_op jit(solution)/shard_map/ppermute | solution.py:601
  95.6 2.3 %collective-permute-done.17.refs_3_ = f32[128,256]{1,0:T(8,128)S(1)} collective-permute-done((f32[128,256]{1,0:T(8,128)S(1)}, f32[128,256]{1,0:T(8,128)S(1)}, u32[]{:S(2)}, u32[]{:S(2)}) %collective-permute-start.17) | collective-permute-done | bytes 131104 | tf_op jit(solution)/shard_map/ppermute | solution.py:601
  97.9 0.0 collective-permute-done.18.refs_4_
  97.9 1.4 %collective-permute-done.19.refs_5_ = f32[128,256]{1,0:T(8,128)S(1)} collective-permute-done((f32[128,256]{1,0:T(8,128)S(1)}, f32[128,256]{1,0:T(8,128)S(1)}, u32[]{:S(2)}, u32[]{:S(2)}) %collective-permute-start.19) | collective-permute-done | bytes 131104 | tf_op jit(solution)/shard_map/ppermute | solution.py:601
  99.3 0.0 collective-permute-done.20.refs_6_
  99.3 1.9 %unpack.1 = f32[128,8,256]{2,1,0:T(8,128)} custom-call(s32[4]{0:T(128)S(1)} %pad_add_fusion.info_ref.refs_0_, f32[128,256]{1,0:T(8,128)S(1)} %collective-permute-done.14.refs_0_, f32[128,256]{1,0:T(8,128)S(1)} %collective-permute-done.15.refs_1_, f32[128,256]{1,0:T(8,128)S(1)} %collective-permute-done.16.refs_2_, ...), custom_call_target="tpu_custom_call" | custom-call | tf_op jit(solution)/shard_map/unpack/pallas_call | solution.py:458
  (3 shorter events, 0.0 us)
Async XLA Ops:
  0.0 0.8 copy-start.1
  0.1 0.7 copy-start.2
  0.8 1.2 %copy-start = (f32[128,8,256]{2,1,0:T(8,128)S(1)}, f32[128,8,256]{2,1,0:T(8,128)}, u32[]{:S(2)}) copy-start(f32[128,8,256]{2,1,0:T(8,128)} %field_ref.3) | copy-start | bytes 3145732
  3.1 15.5 %collective-permute-start = (f32[264,256]{1,0:T(8,128)S(1)}, f32[264,256]{1,0:T(8,128)S(1)}, u32[]{:S(2)}, u32[]{:S(2)}) collective-permute-start(f32[264,256]{1,0:T(8,128)S(1)} %get-tuple-element.43), channel_id=1, source_target_pairs={{0,8},{16,24},{8,0},{24,16},{1,9},{17,25},{9,1},{25,17},{2,10},{18... | collective-permute-start | bytes 811016 | tf_op jit(solution)/shard_map/ppermute | solution.py:506
  3.1 15.4 %collective-permute-start.1 = (f32[264,256]{1,0:T(8,128)S(1)}, f32[264,256]{1,0:T(8,128)S(1)}, u32[]{:S(2)}, u32[]{:S(2)}) collective-permute-start(f32[264,256]{1,0:T(8,128)S(1)} %get-tuple-element.44), channel_id=1, source_target_pairs={{8,16},{16,8},{9,17},{17,9},{10,18},{18,10},{11,19},{19,11},{12,20... | collective-permute-start | bytes 811016 | tf_op jit(solution)/shard_map/ppermute | solution.py:506
  10.2 12.5 %collective-permute-start.3 = (f32[2,128,256]{2,1,0:T(8,128)S(1)}, f32[2,128,256]{2,1,0:T(8,128)S(1)}, u32[]{:S(2)}, u32[]{:S(2)}) collective-permute-start(f32[2,128,256]{2,1,0:T(8,128)S(1)} %get-tuple-element.48), channel_id=1, source_target_pairs={{4,2},{5,3},{2,4},{3,5},{12,10},{13,11},{10,12},{11,13},{20,18},{2... | collective-permute-start | bytes 786440 | tf_op jit(solution)/shard_map/ppermute | solution.py:522
  10.9 18.3 %collective-permute-start.4 = (f32[2,128,256]{2,1,0:T(8,128)S(1)}, f32[2,128,256]{2,1,0:T(8,128)S(1)}, u32[]{:S(2)}, u32[]{:S(2)}) collective-permute-start(f32[2,128,256]{2,1,0:T(8,128)S(1)} %get-tuple-element.49), channel_id=1, source_target_pairs={{6,2},{7,3},{0,4},{1,5},{14,10},{15,11},{8,12},{9,13},{22,18},{23,... | collective-permute-start | bytes 786440 | tf_op jit(solution)/shard_map/ppermute | solution.py:522
  17.1 14.6 %collective-permute-start.5 = (f32[2,128,256]{2,1,0:T(8,128)S(1)}, f32[2,128,256]{2,1,0:T(8,128)S(1)}, u32[]{:S(2)}, u32[]{:S(2)}) collective-permute-start(f32[2,128,256]{2,1,0:T(8,128)S(1)} %get-tuple-element.50), channel_id=1, source_target_pairs={{0,2},{1,3},{6,4},{7,5},{8,10},{9,11},{14,12},{15,13},{16,18},{17,... | collective-permute-start | bytes 786440 | tf_op jit(solution)/shard_map/ppermute | solution.py:522
  20.1 24.0 %collective-permute-start.6 = (f32[2,128,256]{2,1,0:T(8,128)S(1)}, f32[2,128,256]{2,1,0:T(8,128)S(1)}, u32[]{:S(2)}, u32[]{:S(2)}) collective-permute-start(f32[2,128,256]{2,1,0:T(8,128)S(1)} %get-tuple-element.51), channel_id=1, source_target_pairs={{2,0},{3,1},{4,6},{5,7},{10,8},{11,9},{12,14},{13,15},{18,16},{19,... | collective-permute-start | bytes 786440 | tf_op jit(solution)/shard_map/ppermute | solution.py:522
  21.4 22.8 %collective-permute-start.7 = (f32[2,128,256]{2,1,0:T(8,128)S(1)}, f32[2,128,256]{2,1,0:T(8,128)S(1)}, u32[]{:S(2)}, u32[]{:S(2)}) collective-permute-start(f32[2,128,256]{2,1,0:T(8,128)S(1)} %get-tuple-element.52), channel_id=1, source_target_pairs={{4,0},{5,1},{2,6},{3,7},{12,8},{13,9},{10,14},{11,15},{20,16},{21,... | collective-permute-start | bytes 786440 | tf_op jit(solution)/shard_map/ppermute | solution.py:522
  22.7 5.7 %copy-start.5 = (s32[1,512]{1,0:T(1,128)S(1)}, s32[1,512]{1,0:T(1,128)}, u32[]{:S(2)}) copy-start(s32[1,512]{1,0:T(1,128)} %param.10) | copy-start | bytes 6148
  22.8 21.4 %collective-permute-start.8 = (f32[2,128,256]{2,1,0:T(8,128)S(1)}, f32[2,128,256]{2,1,0:T(8,128)S(1)}, u32[]{:S(2)}, u32[]{:S(2)}) collective-permute-start(f32[2,128,256]{2,1,0:T(8,128)S(1)} %get-tuple-element.53), channel_id=1, source_target_pairs={{6,0},{7,1},{0,6},{1,7},{14,8},{15,9},{8,14},{9,15},{22,16},{23,17... | collective-permute-start | bytes 786440 | tf_op jit(solution)/shard_map/ppermute | solution.py:522
  28.5 0.7 copy-start.3
  28.5 0.7 copy-start.4
  29.2 7.2 %collective-permute-start.2 = (f32[8,512]{1,0:T(8,128)S(1)}, f32[8,512]{1,0:T(8,128)S(1)}, u32[]{:S(2)}, u32[]{:S(2)}) collective-permute-start(f32[8,512]{1,0:T(8,128)S(1)} %concatenate.3.refs_1_), channel_id=1, source_target_pairs={{8,15},{9,14},{10,13},{11,12},{12,11},{13,10},{14,9},{15,8},{24,31... | collective-permute-start | bytes 49160 | tf_op jit(solution)/shard_map/ppermute | solution.py:548
  31.7 7.2 %collective-permute-start.9 = (f32[1,128,256]{2,1,0:T(8,128)S(1)}, f32[1,128,256]{2,1,0:T(8,128)S(1)}, u32[]{:S(2)}, u32[]{:S(2)}) collective-permute-start(f32[1,128,256]{2,1,0:T(8,128)S(1)} %get-tuple-element.54), channel_id=1, source_target_pairs={{0,2},{2,4},{3,1},{4,6},{5,3},{6,15},{7,5},{8,10},{9,16},{10,12},{... | collective-permute-start | bytes 393224 | tf_op jit(solution)/shard_map/ppermute | solution.py:576
  36.4 7.7 %collective-permute-start.10 = (f32[1,128,256]{2,1,0:T(8,128)S(1)}, f32[1,128,256]{2,1,0:T(8,128)S(1)}, u32[]{:S(2)}, u32[]{:S(2)}) collective-permute-start(f32[1,128,256]{2,1,0:T(8,128)S(1)} %get-tuple-element.55), channel_id=1, source_target_pairs={{1,2},{3,4},{2,1},{5,6},{4,3},{7,15},{6,5},{9,10},{8,16},{11,12},{... | collective-permute-start | bytes 393224 | tf_op jit(solution)/shard_map/ppermute | solution.py:576
  44.9 6.6 %collective-permute-start.11 = (f32[2,4,128,256]{3,2,1,0:T(8,128)S(1)}, f32[2,4,128,256]{3,2,1,0:T(8,128)S(1)}, u32[]{:S(2)}, u32[]{:S(2)}) collective-permute-start(f32[2,4,128,256]{3,2,1,0:T(8,128)S(1)} %get-tuple-element.57.near_ref), channel_id=1, source_target_pairs={{0,1},{1,0},{2,3},{3,2},{4,5},{5,4},{6,7},{7,6},{8,9},{9,8},{10,11... | collective-permute-start | bytes 3145736 | tf_op jit(solution)/shard_map/ppermute | solution.py:583
  45.0 12.5 %collective-permute-start.12 = (f32[3,128,256]{2,1,0:T(8,128)S(1)}, f32[3,128,256]{2,1,0:T(8,128)S(1)}, u32[]{:S(2)}, u32[]{:S(2)}) collective-permute-start(f32[3,128,256]{2,1,0:T(8,128)S(1)} %get-tuple-element.65), channel_id=1, source_target_pairs={{0,2},{2,4},{3,1},{4,6},{5,3},{6,15},{7,5},{8,10},{9,16},{10,12},{... | collective-permute-start | bytes 1179656 | tf_op jit(solution)/shard_map/ppermute | solution.py:582
  49.4 10.6 %collective-permute-start.13 = (f32[3,128,256]{2,1,0:T(8,128)S(1)}, f32[3,128,256]{2,1,0:T(8,128)S(1)}, u32[]{:S(2)}, u32[]{:S(2)}) collective-permute-start(f32[3,128,256]{2,1,0:T(8,128)S(1)} %get-tuple-element.66), channel_id=1, source_target_pairs={{1,2},{3,4},{2,1},{5,6},{4,3},{7,15},{6,5},{9,10},{8,16},{11,12},{... | collective-permute-start | bytes 1179656 | tf_op jit(solution)/shard_map/ppermute | solution.py:582
  72.4 6.3 %collective-permute-start.14 = (f32[128,256]{1,0:T(8,128)S(1)}, f32[128,256]{1,0:T(8,128)S(1)}, u32[]{:S(2)}, u32[]{:S(2)}) collective-permute-start(f32[128,256]{1,0:T(8,128)S(1)} %get-tuple-element.67), channel_id=1, source_target_pairs={{0,7},{1,6},{2,5},{3,4},{4,3},{5,2},{6,1},{7,0},{8,15},{9,14},{10,... | collective-permute-start | bytes 393224 | tf_op jit(solution)/shard_map/ppermute | solution.py:601
  73.6 16.9 %collective-permute-start.15 = (f32[128,256]{1,0:T(8,128)S(1)}, f32[128,256]{1,0:T(8,128)S(1)}, u32[]{:S(2)}, u32[]{:S(2)}) collective-permute-start(f32[128,256]{1,0:T(8,128)S(1)} %get-tuple-element.68), channel_id=1, source_target_pairs={{0,6},{1,7},{2,4},{3,5},{4,2},{5,3},{6,0},{7,1},{8,14},{9,15},{10,... | collective-permute-start | bytes 393224 | tf_op jit(solution)/shard_map/ppermute | solution.py:601
  74.2 21.4 %collective-permute-start.16 = (f32[128,256]{1,0:T(8,128)S(1)}, f32[128,256]{1,0:T(8,128)S(1)}, u32[]{:S(2)}, u32[]{:S(2)}) collective-permute-start(f32[128,256]{1,0:T(8,128)S(1)} %get-tuple-element.69), channel_id=1, source_target_pairs={{0,5},{1,4},{2,7},{3,6},{4,1},{5,0},{6,3},{7,2},{8,13},{9,12},{10,... | collective-permute-start | bytes 393224 | tf_op jit(solution)/shard_map/ppermute | solution.py:601
  75.0 22.9 %collective-permute-start.17 = (f32[128,256]{1,0:T(8,128)S(1)}, f32[128,256]{1,0:T(8,128)S(1)}, u32[]{:S(2)}, u32[]{:S(2)}) collective-permute-start(f32[128,256]{1,0:T(8,128)S(1)} %get-tuple-element.70), channel_id=1, source_target_pairs={{0,4},{1,5},{2,6},{3,7},{4,0},{5,1},{6,2},{7,3},{8,12},{9,13},{10,... | collective-permute-start | bytes 393224 | tf_op jit(solution)/shard_map/ppermute | solution.py:601
  78.6 19.3 %collective-permute-start.18 = (f32[128,256]{1,0:T(8,128)S(1)}, f32[128,256]{1,0:T(8,128)S(1)}, u32[]{:S(2)}, u32[]{:S(2)}) collective-permute-start(f32[128,256]{1,0:T(8,128)S(1)} %get-tuple-element.71), channel_id=1, source_target_pairs={{0,3},{1,2},{2,1},{3,0},{4,7},{5,6},{6,5},{7,4},{8,11},{9,10},{10,... | collective-permute-start | bytes 393224 | tf_op jit(solution)/shard_map/ppermute | solution.py:601
  78.7 20.6 %collective-permute-start.19 = (f32[128,256]{1,0:T(8,128)S(1)}, f32[128,256]{1,0:T(8,128)S(1)}, u32[]{:S(2)}, u32[]{:S(2)}) collective-permute-start(f32[128,256]{1,0:T(8,128)S(1)} %get-tuple-element.72), channel_id=1, source_target_pairs={{0,2},{1,3},{2,0},{3,1},{4,6},{5,7},{6,4},{7,5},{8,10},{9,11},{10,... | collective-permute-start | bytes 393224 | tf_op jit(solution)/shard_map/ppermute | solution.py:601
  90.5 8.8 %collective-permute-start.20 = (f32[128,256]{1,0:T(8,128)S(1)}, f32[128,256]{1,0:T(8,128)S(1)}, u32[]{:S(2)}, u32[]{:S(2)}) collective-permute-start(f32[128,256]{1,0:T(8,128)S(1)} %get-tuple-element.73), channel_id=1, source_target_pairs={{0,1},{1,0},{2,3},{3,2},{4,5},{5,4},{6,7},{7,6},{8,9},{9,8},{10,11... | collective-permute-start | bytes 393224 | tf_op jit(solution)/shard_map/ppermute | solution.py:601

commit v12 on v11

--- a/solution.py
+++ b/solution.py
@@ -150,23 +150,18 @@
     return jnp.where(chip == 0, k, jnp.where(chip == chips - 1, chips - 1 - k, inner))
 
 
-def choose_kernel(info_ref, *refs):
-    count = (len(refs) - 2) // 2
-    other_ref, own_ref = refs[-2:]
-    chips = info_ref[3]
-    at_edge = jnp.logical_or(info_ref[0] == 0, info_ref[0] == chips - 1)
-    for index in range(count):
-        for ref, here in ((refs[index], jnp.logical_not(at_edge)), (refs[count + index], at_edge)):
-
-            @pl.when(here)
-            def _():
-                other_ref[index] = ref[0]
-                own_ref[index] = ref[1]
-
-
-def collect_kernel(order, late, info_ref, mine_ref, other_ref, *refs):
+def choose_kernel(info_ref, inner_ref, edge_ref, own_ref):
+    at_edge = jnp.logical_or(info_ref[0] == 0, info_ref[0] == info_ref[3] - 1)
+    for ref, here in ((inner_ref, jnp.logical_not(at_edge)), (edge_ref, at_edge)):
+
+        @pl.when(here)
+        def _():
+            own_ref[...] = ref[1]
+
+
+def collect_kernel(order, info_ref, mine_ref, other_ref, *refs):
     chips = len(order)
-    both_ref, late_other, late_own, observed_ref = refs[-4:]
+    near_other, near_own, late_own, observed_ref = refs[-4:]
     observed_ref[...] = jnp.where(info_ref[2] == 1, other_ref[...], mine_ref[...])
     chip = info_ref[0]
     at_edge = jnp.logical_or(chip == 0, chip == chips - 1)
@@ -176,11 +171,10 @@
 
             @pl.when(here)
             def _():
-                both_ref[0, block] = ref[0]
-                both_ref[1, block] = ref[1]
-                if index in late:
-                    late_other[late.index(index)] = ref[0]
-                    late_own[late.index(index)] = ref[1]
+                near_other[block] = ref[0]
+                near_own[block] = ref[1]
+                if index:
+                    late_own[index - 1] = ref[1]
 
 
 def unpack_kernel(order, info_ref, *refs):
@@ -252,11 +246,11 @@
 
 
 def prepare_kernel(
-    info_ref, observed_ref, near_ref, far_ref,
+    info_ref, observed_ref, near_other, near_own, far_other, far_own,
     spread_high, spread_low, own_high, own_low, own_part, seen_ref, direction_ref,
     anomaly, high_ref, low_ref,
 ):
-    _, chips, step, width = near_ref.shape
+    chips, step, width = near_own.shape
     members = 2 * chips * step
     cells, _, _, scale = observations(info_ref, observed_ref, width, math.sqrt(members - 1))
     chosen = one_hot(cells, width, 2 * width)
@@ -264,7 +258,8 @@
     means = []
     for place in range(2):
         columns = pl.ds(place * width, width)
-        rows = [near_ref.at[place, chip] for chip in range(chips)] + [far_ref.at[1 - place, chip] for chip in range(chips)]
+        halves = (near_own, far_own) if place else (near_other, far_other)
+        rows = [half.at[chip] for half in halves for chip in range(chips)]
         means.append(mean_of([row[...] for row in rows], members))
         for block, row in zip(blocks, rows):
             part = row[...] - means[-1]
@@ -320,46 +315,43 @@
 
 
 def region_kernel(
-    order, groups, info_ref, observed_ref, near_ref, far_ref, high_in, low_in, own_high, own_low, own_part, seen_ref,
-    direction_ref, *refs,
+    order, info_ref, observed_ref, near_own, far_own, high_in, low_in, own_high, own_low, own_part, seen_ref,
+    direction_ref, early_ref, late_ref, rest_ref, *refs,
 ):
-    _, chips, step, width = near_ref.shape
-    outer_refs, out_refs = refs[: 2 * len(groups)], refs[2 * len(groups) : -4]
+    chips, step, width = near_own.shape
+    out_refs = refs[:-4]
     spread_high, spread_low, factor, answer = refs[-4:]
     members = 2 * chips * step
     slots = observed_ref.shape[1]
     root = math.sqrt(members - 1)
     core = info_ref[1]
-    swapped = jnp.logical_or(
+    ends = jnp.logical_or(
         jnp.logical_and(info_ref[0] == 0, core == 0), jnp.logical_and(info_ref[0] == chips - 1, core == 1)
     )
-    giver = jnp.where(swapped, info_ref[0], info_ref[0] - 1 + 2 * core)
+    giver = jnp.where(ends, info_ref[0], info_ref[0] - 1 + 2 * core)
+    part = jnp.where(ends, 0, 1)
     cells, slot_weight, values, scale = observations(info_ref, observed_ref, width, root)
     chosen = one_hot(cells, 0, width)
 
-    def outer_block(part, place):
-        for pair, group in zip(zip(outer_refs[::2], outer_refs[1::2]), groups):
-            if place in group:
-                mine, other = pair[part], pair[1 - part]
-                at = group.index(place)
-                return jnp.where(swapped, other[at], mine[at])
-
-    blocks = [pl.ds(index * step, step) for index in range(2 * chips)]
-    arrivals = [
-        (part, place, pl.ds(pl.multiple_of((part * chips + source_of(giver, chips, *order[place])) * step, step), step))
-        for part in range(2) for place in range(chips)
+    def rows_at(half, chip):
+        return pl.ds(pl.multiple_of((half * chips + chip) * step, step), step)
+
+    blocks = [(early_ref, rows_at(part, source_of(giver, chips, *order[0])))]
+    blocks += [
+        (late_ref.at[place - 1], rows_at(part, source_of(giver, chips, *order[place]))) for place in range(1, chips)
     ]
-    mean = mean_of([outer_block(part, place) for part, place, _ in arrivals], members)
+    blocks += [(rest_ref.at[chip], rows_at(1 - part, chip)) for chip in range(chips)]
+    mean = mean_of([ref[...] for ref, _ in blocks], members)
     taken = None
-    for part, place, block in arrivals:
-        term = (outer_block(part, place) - mean) * doubled(direction_ref[block, :])
+    for ref, block in blocks:
+        term = (ref[...] - mean) * doubled(direction_ref[block, :])
         taken = term if taken is None else taken + term
     taken = jnp.sum(taken, axis=0, keepdims=True)
     seen_mean = seen_ref[pl.ds(0, 1), :] + at_cells(mean, chosen)
     common = (seen_ref[pl.ds(1, 1), :] + at_cells(taken, chosen)) * scale
     innovation = slot_weight * (values - seen_mean)
-    for part, place, block in arrivals:
-        rest = outer_block(part, place) - mean - doubled(direction_ref[block, :]) * taken
+    for ref, block in blocks:
+        rest = ref[...] - mean - doubled(direction_ref[block, :]) * taken
         high, low = pieces(rest, 2)
         high, low = pieces((dot(high, chosen) + dot(low, chosen)) * scale, 2)
         spread_high[block, :] = high + high_in[block, :]
@@ -441,7 +433,7 @@
         rows = pl.ds(pl.multiple_of((part * chips + chip) * step, step), step)
         moved = product([spread_high[rows, :], spread_low[rows, :]], halved)
         moved = moved + doubled(direction_ref[rows, :]) * along
-        own = far_ref[0, chip] if part else near_ref[1, chip]
+        own = (far_own if part else near_own)[chip]
         out_ref[...] = own + shift + moved
 
 
@@ -553,47 +545,42 @@
     def device(p, chip, core):
         return p * lanes + 2 * chip + core
 
-    first_pairs, second_pairs, siblings = [], [], []
+    borders, siblings = [], []
     for p in range(patches):
         for chip in range(chips):
-            siblings += [(device(p, chip, core), device(p, chip, 1 - core)) for core in range(2)]
-            for core, away in ((0, 1), (1, -1)):
+            for core, away in ((0, -1), (1, 1)):
+                siblings.append((device(p, chip, core), device(p, chip, 1 - core)))
                 if 0 <= chip + away < chips:
-                    to_first, to_second = device(p, chip + away, core), device(p, chip + away, core)
-                    to = p
+                    borders.append((device(p, chip, core), device(p, chip + away, 1 - core)))
                 else:
                     to = p + 1 if (p % 2 == 0) == (away == 1) else p - 1
-                    if not 0 <= to < patches:
-                        continue
-                    to_first = to_second = device(to, chip, 1 - core)
-                first_pairs.append((device(p, chip, core), to_first))
-                second_pairs.append((device(p, chip, 1 - core), to_second))
-    groups = [[0], list(range(1, chips))]
-    early, late = groups
-    got = [pieces_in[place] for place in early] + [pieces_in[chips + place] for place in early]
-    row = array(len(early), step, width)
-    early_rows = call(choose_kernel, "choose", [row, row], [info] + got)
-    outer_rows = [lax.ppermute(early_rows[0], axes, first_pairs), lax.ppermute(early_rows[1], axes, second_pairs)]
-    row = array(len(late), step, width)
-    near, *late_rows, observed = call(
-        functools.partial(collect_kernel, order, late), "collect",
-        [array(2, chips, step, width), row, row, array(8, slots)], [info, mine, other] + pieces_in, after=outer_rows,
-    )
-    outer_rows += [lax.ppermute(late_rows[0], axes, first_pairs), lax.ppermute(late_rows[1], axes, second_pairs)]
-    far = lax.ppermute(near, axes, siblings)
+                    if 0 <= to < patches:
+                        borders.append((device(p, chip, core), device(to, chip, core)))
+
+    early = call(choose_kernel, "choose", array(step, width), [info, inner[0], outer[0]])
+    got_early = lax.ppermute(early, axes, borders)
+    half = array(chips, step, width)
+    near_other, near_own, late, observed = call(
+        functools.partial(collect_kernel, order), "collect",
+        [half, half, array(chips - 1, step, width), array(8, slots)], [info, mine, other] + pieces_in, after=[got_early],
+    )
+    far_own = lax.ppermute(near_other, axes, siblings)
+    got_late = lax.ppermute(late, axes, borders)
+    far_other = lax.ppermute(near_own, axes, siblings)
+    got_rest = lax.ppermute(far_own, axes, borders)
 
     split = [pltpu.VMEM((members, slots), BF16)] * 2
     prepared = call(
         prepare_kernel, "prepare",
         [bfloat(members, slots)] * 2 + [bfloat(width, members)] * 2
         + [array(width, width // 2), array(8, slots), array(members, width // 2)],
-        [info, observed, near, far],
+        [info, observed, near_other, near_own, far_other, far_own],
         [pltpu.VMEM((members, 2 * width), F32)] + [pltpu.VMEM((members, 2 * width), BF16)] * 2,
         flops=8 * members * slots * width, limit=20,
     )
     analysed = call(
-        functools.partial(region_kernel, order, groups), "region", [array(step, width)] * lanes,
-        [info, observed, near, far, *prepared, *outer_rows],
+        functools.partial(region_kernel, order), "region", [array(step, width)] * lanes,
+        [info, observed, near_own, far_own, *prepared, got_early, got_late, got_rest],
         split + [pltpu.VMEM((slots, slots), F32), pltpu.VMEM((width + 8, slots), F32)],
         limit=24,
     )

time: 102 us -> 100 us (0.980)
    ppermute x5, waiting for transfers between devices: 10.3 us -> 6.86 us  [the longest x1 5.4 us: per_device(): got_late = lax.ppermute(late, axes, borders)]
    ppermute x1, waiting for transfers between devices: 2.76 us -> 5.02 us  [per_device(): lax.ppermute(mine, axes, [(p * lanes + i, p * lanes + lanes - 1 - i) for...]
    ppermute x6, waiting for transfers between devices: 0.02 us -> 1.4 us  [between(): lax.ppermute(message, 'member', [(2 * a + core, 2 * b + core) for a, b in...]
  transfers between devices with their start and end apart: 21 -> 21, of which waited for: 9 -> 7; matrix products, arithmetic and copies ran while one was open for 0% -> 0% of each run, Pallas kernels for 8% -> 8%
where the time goes in v12:
time: 100 us
  starting transfers between devices  51.2 us (51%)
  Pallas kernels  24.1 us (24%)
  waiting for transfers between devices  21.3 us (21%)
  local copies, waits for them, and re-layouts  2.63 us (3%)
    pallas_call x7, Pallas kernels, call(): pl.pallas_call(kernel, out_shape=out_shape, in_specs=[SMEM] + [VMEM] * (l...  23.1 us
    ppermute x7, starting transfers between devices, swapped(): lax.ppermute(analysed[x], 'member', [(i, i ^ x) for i in range(lanes)])  17.9 us
    ppermute x6, starting transfers between devices, between(): lax.ppermute(message, 'member', [(2 * a + core, 2 * b + core) for a, b in...  15.9 us
    ppermute x7, waiting for transfers between devices, swapped(): lax.ppermute(analysed[x], 'member', [(i, i ^ x) for i in range(lanes)])  8.03 us
    ppermute x1, waiting for transfers between devices, per_device(): got_late = lax.ppermute(late, axes, borders)  5.4 us
    ppermute x1, waiting for transfers between devices, per_device(): lax.ppermute(mine, axes, [(p * lanes + i, p * lanes + lanes - 1 - i) for...  5.02 us
    ppermute x2, starting transfers between devices, swap(): lax.ppermute(message, 'patch', [(p, p + 1) for p in lower] + [(p + 1, p)...  4.94 us
    ppermute x1, starting transfers between devices, per_device(): got_late = lax.ppermute(late, axes, borders)  4.7 us
  transfers between devices with their start and end apart: 21, of which 7 were waited for; matrix products, arithmetic and copies ran while one was open for 0% of the time, Pallas kernels for 8%

profile of v12, /device:TPU:2, one launch (start us, length us, event | category | flops | bytes accessed | tf_op | source)
XLA Modules:
  0.0 100.3 jit_solution(11386295501361016093)
XLA Ops:
  0.0 0.0 copy-start.1
  0.0 0.1 pad_add_fusion.info_ref.refs_0_
  0.1 0.0 copy-start.2
  0.1 0.7 copy-done.1
  0.8 0.0 copy-done.2
  0.8 0.0 copy-start
  0.8 1.2 %copy-done = f32[128,8,256]{2,1,0:T(8,128)S(1)} copy-done((f32[128,8,256]{2,1,0:T(8,128)S(1)}, f32[128,8,256]{2,1,0:T(8,128)}, u32[]{:S(2)}) %copy-start) | copy-done | bytes 1048600
  2.0 1.1 %pack.1 = (f32[264,256]{1,0:T(8,128)S(1)}, f32[264,256]{1,0:T(8,128)S(1)}, f32[4,8,256]{2,1,0:T(8,128)S(1)}, f32[128,128]{1,0:T(8,128)S(1)}) custom-call(s32[4]{0:T(128)S(1)} %pad_add_fusion.info_ref.refs_0_, f32[128,8,256]{2,1,0:T(8,128)S(1)} %copy-done, f32[4,8,256]{2,1,0:T(8,128)S(1)} %copy-done.1, f32[1,128]{1,0:T(1,128)S(1)} %bitcast.5), custom_call_target="tpu_custom_call" | custom-call | tf_op jit(solution)/shard_map/pack/pallas_call | solution.py:486
  3.1 0.1 collective-permute-start
  3.1 4.9 %collective-permute-start.1 = (f32[264,256]{1,0:T(8,128)S(1)}, f32[264,256]{1,0:T(8,128)S(1)}, u32[]{:S(2)}, u32[]{:S(2)}) collective-permute-start(f32[264,256]{1,0:T(8,128)S(1)} %get-tuple-element.42), channel_id=1, source_target_pairs={{8,16},{16,8},{9,17},{17,9},{10,18},{18,10},{11,19},{19,11},{12,20... | collective-permute-start | bytes 811016 | tf_op jit(solution)/shard_map/ppermute | solution.py:498
  8.0 2.2 %inner.1 = (f32[4,128,256]{2,1,0:T(8,128)S(1)}, f32[2,128,256]{2,1,0:T(8,128)S(1)}, f32[2,128,256]{2,1,0:T(8,128)S(1)}, f32[2,128,256]{2,1,0:T(8,128)S(1)}, f32[2,128,256]{2,1,0:T(8,128)S(1)}) custom-call(s32[4]{0:T(128)S(1)} %pad_add_fusion.info_ref.refs_0_, f32[128,8,256]{2,1,0:T(8,128)S(1)} %copy-done, f32[4,8,256]{2,1,0:T(8,128)S(1)} %get-tuple-element.38.flow_ref, ...), custom_call_target="tpu_custom_call" | custom-call | tf_op jit(solution)/shard_map/inner/pallas_call | solution.py:450
  10.2 0.7 collective-permute-start.3
  10.9 6.2 %collective-permute-start.4 = (f32[2,128,256]{2,1,0:T(8,128)S(1)}, f32[2,128,256]{2,1,0:T(8,128)S(1)}, u32[]{:S(2)}, u32[]{:S(2)}) collective-permute-start(f32[2,128,256]{2,1,0:T(8,128)S(1)} %get-tuple-element.47), channel_id=1, source_target_pairs={{6,2},{7,3},{0,4},{1,5},{14,10},{15,11},{8,12},{9,13},{22,18},{23,... | collective-permute-start | bytes 786440 | tf_op jit(solution)/shard_map/ppermute | solution.py:514
  17.1 1.4 %collective-permute-start.5 = (f32[2,128,256]{2,1,0:T(8,128)S(1)}, f32[2,128,256]{2,1,0:T(8,128)S(1)}, u32[]{:S(2)}, u32[]{:S(2)}) collective-permute-start(f32[2,128,256]{2,1,0:T(8,128)S(1)} %get-tuple-element.48), channel_id=1, source_target_pairs={{0,2},{1,3},{6,4},{7,5},{8,10},{9,11},{14,12},{15,13},{16,18},{17,... | collective-permute-start | bytes 786440 | tf_op jit(solution)/shard_map/ppermute | solution.py:514
  18.5 0.0 collective-permute-done.last_ref
  18.6 0.0 collective-permute-done.1.first_ref
  18.6 1.5 %edge.1 = (f32[2,128,256]{2,1,0:T(8,128)S(1)}, f32[2,128,256]{2,1,0:T(8,128)S(1)}, f32[2,128,256]{2,1,0:T(8,128)S(1)}, f32[2,128,256]{2,1,0:T(8,128)S(1)}) custom-call(s32[4]{0:T(128)S(1)} %pad_add_fusion.info_ref.refs_0_, f32[128,8,256]{2,1,0:T(8,128)S(1)} %copy-done, f32[4,8,256]{2,1,0:T(8,128)S(1)} %get-tuple-element.38.flow_ref, ...), custom_call_target="tpu_custom_call" | custom-call | tf_op jit(solution)/shard_map/edge/pallas_call | solution.py:450
  20.1 1.3 %collective-permute-start.6 = (f32[2,128,256]{2,1,0:T(8,128)S(1)}, f32[2,128,256]{2,1,0:T(8,128)S(1)}, u32[]{:S(2)}, u32[]{:S(2)}) collective-permute-start(f32[2,128,256]{2,1,0:T(8,128)S(1)} %get-tuple-element.49), channel_id=1, source_target_pairs={{2,0},{3,1},{4,6},{5,7},{10,8},{11,9},{12,14},{13,15},{18,16},{19,... | collective-permute-start | bytes 786440 | tf_op jit(solution)/shard_map/ppermute | solution.py:514
  21.4 1.3 %collective-permute-start.7 = (f32[2,128,256]{2,1,0:T(8,128)S(1)}, f32[2,128,256]{2,1,0:T(8,128)S(1)}, u32[]{:S(2)}, u32[]{:S(2)}) collective-permute-start(f32[2,128,256]{2,1,0:T(8,128)S(1)} %get-tuple-element.50), channel_id=1, source_target_pairs={{4,0},{5,1},{2,6},{3,7},{12,8},{13,9},{10,14},{11,15},{20,16},{21,... | collective-permute-start | bytes 786440 | tf_op jit(solution)/shard_map/ppermute | solution.py:514
  22.7 0.0 collective-permute-done.3.refs_4_
  22.7 5.0 %collective-permute-start.8 = (f32[2,128,256]{2,1,0:T(8,128)S(1)}, f32[2,128,256]{2,1,0:T(8,128)S(1)}, u32[]{:S(2)}, u32[]{:S(2)}) collective-permute-start(f32[2,128,256]{2,1,0:T(8,128)S(1)} %get-tuple-element.51), channel_id=1, source_target_pairs={{6,0},{7,1},{0,6},{1,7},{14,8},{15,9},{8,14},{9,15},{22,16},{23,17... | collective-permute-start | bytes 786440 | tf_op jit(solution)/shard_map/ppermute | solution.py:514
  27.8 0.6 choose.1
  28.4 0.0 copy-start.5
  28.4 0.0 collective-permute-done.4.refs_5_
  28.4 2.4 %collective-permute-start.9 = (f32[128,256]{1,0:T(8,128)S(1)}, f32[128,256]{1,0:T(8,128)S(1)}, u32[]{:S(2)}, u32[]{:S(2)}) collective-permute-start(f32[128,256]{1,0:T(8,128)S(1)} %choose.1), channel_id=1, source_target_pairs={{1,2},{2,1},{3,4},{4,3},{5,6},{6,5},{7,15},{8,16},{9,10},{10,9},{1... | collective-permute-start | bytes 393224 | tf_op jit(solution)/shard_map/ppermute | solution.py:561
  31.4 0.0 copy-done.5
  31.4 0.0 copy-start.3
  31.5 0.0 copy-start.4
  31.5 0.6 copy-done.3
  32.1 0.0 copy-done.4
  32.2 0.0 collective-permute-done.5.refs_6_
  32.2 1.9 %collective-permute-start.2 = (f32[8,512]{1,0:T(8,128)S(1)}, f32[8,512]{1,0:T(8,128)S(1)}, u32[]{:S(2)}, u32[]{:S(2)}) collective-permute-start(f32[8,512]{1,0:T(8,128)S(1)} %concatenate.3.refs_1_), channel_id=1, source_target_pairs={{8,15},{9,14},{10,13},{11,12},{12,11},{13,10},{14,9},{15,8},{24,31... | collective-permute-start | bytes 49160 | tf_op jit(solution)/shard_map/ppermute | solution.py:540
  34.1 5.0 %collective-permute-done.2.refs_2_ = f32[8,512]{1,0:T(8,128)S(1)} collective-permute-done((f32[8,512]{1,0:T(8,128)S(1)}, f32[8,512]{1,0:T(8,128)S(1)}, u32[]{:S(2)}, u32[]{:S(2)}) %collective-permute-start.2) | collective-permute-done | bytes 16416 | tf_op jit(solution)/shard_map/ppermute | solution.py:540
  39.1 0.0 collective-permute-done.9.refs_11_.early_ref
  39.1 1.4 %collective-permute-done.6.refs_8_ = f32[2,128,256]{2,1,0:T(8,128)S(1)} collective-permute-done((f32[2,128,256]{2,1,0:T(8,128)S(1)}, f32[2,128,256]{2,1,0:T(8,128)S(1)}, u32[]{:S(2)}, u32[]{:S(2)}) %collective-permute-start.6) | collective-permute-done | bytes 262176 | tf_op jit(solution)/shard_map/ppermute | solution.py:514
  40.5 0.0 collective-permute-done.7.refs_9_
  40.5 0.0 collective-permute-done.8.refs_10_
  40.5 0.7 collect.1
  41.2 1.3 %collective-permute-start.10 = (f32[4,128,256]{2,1,0:T(8,128)S(1)}, f32[4,128,256]{2,1,0:T(8,128)S(1)}, u32[]{:S(2)}, u32[]{:S(2)}) collective-permute-start(f32[4,128,256]{2,1,0:T(8,128)S(1)} %get-tuple-element.54.near_other), channel_id=1, source_target_pairs={{0,1},{1,0},{2,3},{3,2},{4,5},{5,4},{6,7},{7,6},{8,9},{9,8},{10,11... | collective-permute-start | bytes 1572872 | tf_op jit(solution)/shard_map/ppermute | solution.py:567
  42.5 0.1 collective-permute-start.11
  42.6 1.5 %collective-permute-done.10.far_own = f32[4,128,256]{2,1,0:T(8,128)S(1)} collective-permute-done((f32[4,128,256]{2,1,0:T(8,128)S(1)}, f32[4,128,256]{2,1,0:T(8,128)S(1)}, u32[]{:S(2)}, u32[]{:S(2)}) %collective-permute-start.10) | collective-permute-done | bytes 524320 | tf_op jit(solution)/shard_map/ppermute | solution.py:567
  44.0 2.0 %collective-permute-start.13 = (f32[4,128,256]{2,1,0:T(8,128)S(1)}, f32[4,128,256]{2,1,0:T(8,128)S(1)}, u32[]{:S(2)}, u32[]{:S(2)}) collective-permute-start(f32[4,128,256]{2,1,0:T(8,128)S(1)} %collective-permute-done.10.far_own), channel_id=1, source_target_pairs={{1,2},{2,1},{3,4},{4,3},{5,6},{6,5},{7,15},{8,16},{9,10},{10,9},{1... | collective-permute-start | bytes 1572872 | tf_op jit(solution)/shard_map/ppermute | solution.py:570
  46.1 4.7 %collective-permute-start.12 = (f32[3,128,256]{2,1,0:T(8,128)S(1)}, f32[3,128,256]{2,1,0:T(8,128)S(1)}, u32[]{:S(2)}, u32[]{:S(2)}) collective-permute-start(f32[3,128,256]{2,1,0:T(8,128)S(1)} %get-tuple-element.62), channel_id=1, source_target_pairs={{1,2},{2,1},{3,4},{4,3},{5,6},{6,5},{7,15},{8,16},{9,10},{10,9},{1... | collective-permute-start | bytes 1179656 | tf_op jit(solution)/shard_map/ppermute | solution.py:568
  50.8 0.0 collective-permute-done.11.far_other
  50.8 4.0 %prepare.1 = (bf16[1024,512]{1,0:T(8,128)(2,1)S(1)}, bf16[1024,512]{1,0:T(8,128)(2,1)S(1)}, bf16[256,1024]{1,0:T(8,128)(2,1)S(1)}, bf16[256,1024]{1,0:T(8,128)(2...) custom-call(s32[4]{0:T(128)S(1)} %pad_add_fusion.info_ref.refs_0_, ...), custom_call_target="tpu_custom_call" | custom-call | flops 1073741824 | tf_op jit(solution)/shard_map/prepare/pallas_call | solution.py:450
  54.8 5.4 %collective-permute-done.12.late_ref = f32[3,128,256]{2,1,0:T(8,128)S(1)} collective-permute-done((f32[3,128,256]{2,1,0:T(8,128)S(1)}, f32[3,128,256]{2,1,0:T(8,128)S(1)}, u32[]{:S(2)}, u32[]{:S(2)}) %collective-permute-start.12) | collective-permute-done | bytes 393248 | tf_op jit(solution)/shard_map/ppermute | solution.py:568
  60.2 0.0 collective-permute-done.13.rest_ref
  60.2 12.1 %region.1 = (f32[128,256]{1,0:T(8,128)S(1)}, f32[128,256]{1,0:T(8,128)S(1)}, f32[128,256]{1,0:T(8,128)S(1)}, f32[128,256]{1,0:T(8,128)S(1)}, f32[128,256]{1,0:T(...) custom-call(s32[4]{0:T(128)S(1)} %pad_add_fusion.info_ref.refs_0_, ...), custom_call_target="tpu_custom_call" | custom-call | tf_op jit(solution)/shard_map/region/pallas_call | solution.py:450
  72.3 3.2 %collective-permute-start.14 = (f32[128,256]{1,0:T(8,128)S(1)}, f32[128,256]{1,0:T(8,128)S(1)}, u32[]{:S(2)}, u32[]{:S(2)}) collective-permute-start(f32[128,256]{1,0:T(8,128)S(1)} %get-tuple-element.63), channel_id=1, source_target_pairs={{0,7},{1,6},{2,5},{3,4},{4,3},{5,2},{6,1},{7,0},{8,15},{9,14},{10,... | collective-permute-start | bytes 393224 | tf_op jit(solution)/shard_map/ppermute | solution.py:588
  75.6 0.0 collective-permute-start.15
  75.6 0.0 collective-permute-start.16
  75.6 3.0 %collective-permute-start.17 = (f32[128,256]{1,0:T(8,128)S(1)}, f32[128,256]{1,0:T(8,128)S(1)}, u32[]{:S(2)}, u32[]{:S(2)}) collective-permute-start(f32[128,256]{1,0:T(8,128)S(1)} %get-tuple-element.66), channel_id=1, source_target_pairs={{0,4},{1,5},{2,6},{3,7},{4,0},{5,1},{6,2},{7,3},{8,12},{9,13},{10,... | collective-permute-start | bytes 393224 | tf_op jit(solution)/shard_map/ppermute | solution.py:588
  78.6 1.1 %collective-permute-start.18 = (f32[128,256]{1,0:T(8,128)S(1)}, f32[128,256]{1,0:T(8,128)S(1)}, u32[]{:S(2)}, u32[]{:S(2)}) collective-permute-start(f32[128,256]{1,0:T(8,128)S(1)} %get-tuple-element.67), channel_id=1, source_target_pairs={{0,3},{1,2},{2,1},{3,0},{4,7},{5,6},{6,5},{7,4},{8,11},{9,10},{10,... | collective-permute-start | bytes 393224 | tf_op jit(solution)/shard_map/ppermute | solution.py:588
  79.7 0.0 collective-permute-done.14.refs_0_
  79.7 10.6 %collective-permute-start.19 = (f32[128,256]{1,0:T(8,128)S(1)}, f32[128,256]{1,0:T(8,128)S(1)}, u32[]{:S(2)}, u32[]{:S(2)}) collective-permute-start(f32[128,256]{1,0:T(8,128)S(1)} %get-tuple-element.68), channel_id=1, source_target_pairs={{0,2},{1,3},{2,0},{3,1},{4,6},{5,7},{6,4},{7,5},{8,10},{9,11},{10,... | collective-permute-start | bytes 393224 | tf_op jit(solution)/shard_map/ppermute | solution.py:588
  90.3 0.0 collective-permute-done.15.refs_1_
  90.3 0.0 collective-permute-start.20
  90.3 4.6 %collective-permute-done.16.refs_2_ = f32[128,256]{1,0:T(8,128)S(1)} collective-permute-done((f32[128,256]{1,0:T(8,128)S(1)}, f32[128,256]{1,0:T(8,128)S(1)}, u32[]{:S(2)}, u32[]{:S(2)}) %collective-permute-start.16) | collective-permute-done | bytes 131104 | tf_op jit(solution)/shard_map/ppermute | solution.py:588
  94.9 1.6 %collective-permute-done.17.refs_3_ = f32[128,256]{1,0:T(8,128)S(1)} collective-permute-done((f32[128,256]{1,0:T(8,128)S(1)}, f32[128,256]{1,0:T(8,128)S(1)}, u32[]{:S(2)}, u32[]{:S(2)}) %collective-permute-start.17) | collective-permute-done | bytes 131104 | tf_op jit(solution)/shard_map/ppermute | solution.py:588
  96.5 0.0 collective-permute-done.18.refs_4_
  96.5 1.8 %collective-permute-done.19.refs_5_ = f32[128,256]{1,0:T(8,128)S(1)} collective-permute-done((f32[128,256]{1,0:T(8,128)S(1)}, f32[128,256]{1,0:T(8,128)S(1)}, u32[]{:S(2)}, u32[]{:S(2)}) %collective-permute-start.19) | collective-permute-done | bytes 131104 | tf_op jit(solution)/shard_map/ppermute | solution.py:588
  98.3 0.0 collective-permute-done.20.refs_6_
  98.3 1.9 %unpack.1 = f32[128,8,256]{2,1,0:T(8,128)} custom-call(s32[4]{0:T(128)S(1)} %pad_add_fusion.info_ref.refs_0_, f32[128,256]{1,0:T(8,128)S(1)} %collective-permute-done.14.refs_0_, f32[128,256]{1,0:T(8,128)S(1)} %collective-permute-done.15.refs_1_, f32[128,256]{1,0:T(8,128)S(1)} %collective-permute-done.16.refs_2_, ...), custom_call_target="tpu_custom_call" | custom-call | tf_op jit(solution)/shard_map/unpack/pallas_call | solution.py:450
  (3 shorter events, 0.0 us)
Async XLA Ops:
  0.0 0.8 copy-start.1
  0.1 0.7 copy-start.2
  0.8 1.2 %copy-start = (f32[128,8,256]{2,1,0:T(8,128)S(1)}, f32[128,8,256]{2,1,0:T(8,128)}, u32[]{:S(2)}) copy-start(f32[128,8,256]{2,1,0:T(8,128)} %field_ref.3) | copy-start | bytes 3145732
  3.1 15.5 %collective-permute-start = (f32[264,256]{1,0:T(8,128)S(1)}, f32[264,256]{1,0:T(8,128)S(1)}, u32[]{:S(2)}, u32[]{:S(2)}) collective-permute-start(f32[264,256]{1,0:T(8,128)S(1)} %get-tuple-element.41), channel_id=1, source_target_pairs={{0,8},{16,24},{8,0},{24,16},{1,9},{17,25},{9,1},{25,17},{2,10},{18... | collective-permute-start | bytes 811016 | tf_op jit(solution)/shard_map/ppermute | solution.py:498
  3.1 15.4 %collective-permute-start.1 = (f32[264,256]{1,0:T(8,128)S(1)}, f32[264,256]{1,0:T(8,128)S(1)}, u32[]{:S(2)}, u32[]{:S(2)}) collective-permute-start(f32[264,256]{1,0:T(8,128)S(1)} %get-tuple-element.42), channel_id=1, source_target_pairs={{8,16},{16,8},{9,17},{17,9},{10,18},{18,10},{11,19},{19,11},{12,20... | collective-permute-start | bytes 811016 | tf_op jit(solution)/shard_map/ppermute | solution.py:498
  10.2 12.5 %collective-permute-start.3 = (f32[2,128,256]{2,1,0:T(8,128)S(1)}, f32[2,128,256]{2,1,0:T(8,128)S(1)}, u32[]{:S(2)}, u32[]{:S(2)}) collective-permute-start(f32[2,128,256]{2,1,0:T(8,128)S(1)} %get-tuple-element.46), channel_id=1, source_target_pairs={{4,2},{5,3},{2,4},{3,5},{12,10},{13,11},{10,12},{11,13},{20,18},{2... | collective-permute-start | bytes 786440 | tf_op jit(solution)/shard_map/ppermute | solution.py:514
  10.9 17.4 %collective-permute-start.4 = (f32[2,128,256]{2,1,0:T(8,128)S(1)}, f32[2,128,256]{2,1,0:T(8,128)S(1)}, u32[]{:S(2)}, u32[]{:S(2)}) collective-permute-start(f32[2,128,256]{2,1,0:T(8,128)S(1)} %get-tuple-element.47), channel_id=1, source_target_pairs={{6,2},{7,3},{0,4},{1,5},{14,10},{15,11},{8,12},{9,13},{22,18},{23,... | collective-permute-start | bytes 786440 | tf_op jit(solution)/shard_map/ppermute | solution.py:514
  17.1 15.1 %collective-permute-start.5 = (f32[2,128,256]{2,1,0:T(8,128)S(1)}, f32[2,128,256]{2,1,0:T(8,128)S(1)}, u32[]{:S(2)}, u32[]{:S(2)}) collective-permute-start(f32[2,128,256]{2,1,0:T(8,128)S(1)} %get-tuple-element.48), channel_id=1, source_target_pairs={{0,2},{1,3},{6,4},{7,5},{8,10},{9,11},{14,12},{15,13},{16,18},{17,... | collective-permute-start | bytes 786440 | tf_op jit(solution)/shard_map/ppermute | solution.py:514
  20.1 20.4 %collective-permute-start.6 = (f32[2,128,256]{2,1,0:T(8,128)S(1)}, f32[2,128,256]{2,1,0:T(8,128)S(1)}, u32[]{:S(2)}, u32[]{:S(2)}) collective-permute-start(f32[2,128,256]{2,1,0:T(8,128)S(1)} %get-tuple-element.49), channel_id=1, source_target_pairs={{2,0},{3,1},{4,6},{5,7},{10,8},{11,9},{12,14},{13,15},{18,16},{19,... | collective-permute-start | bytes 786440 | tf_op jit(solution)/shard_map/ppermute | solution.py:514
  21.4 19.1 %collective-permute-start.7 = (f32[2,128,256]{2,1,0:T(8,128)S(1)}, f32[2,128,256]{2,1,0:T(8,128)S(1)}, u32[]{:S(2)}, u32[]{:S(2)}) collective-permute-start(f32[2,128,256]{2,1,0:T(8,128)S(1)} %get-tuple-element.50), channel_id=1, source_target_pairs={{4,0},{5,1},{2,6},{3,7},{12,8},{13,9},{10,14},{11,15},{20,16},{21,... | collective-permute-start | bytes 786440 | tf_op jit(solution)/shard_map/ppermute | solution.py:514
  22.7 17.8 %collective-permute-start.8 = (f32[2,128,256]{2,1,0:T(8,128)S(1)}, f32[2,128,256]{2,1,0:T(8,128)S(1)}, u32[]{:S(2)}, u32[]{:S(2)}) collective-permute-start(f32[2,128,256]{2,1,0:T(8,128)S(1)} %get-tuple-element.51), channel_id=1, source_target_pairs={{6,0},{7,1},{0,6},{1,7},{14,8},{15,9},{8,14},{9,15},{22,16},{23,17... | collective-permute-start | bytes 786440 | tf_op jit(solution)/shard_map/ppermute | solution.py:514
  28.4 3.1 %copy-start.5 = (s32[1,512]{1,0:T(1,128)S(1)}, s32[1,512]{1,0:T(1,128)}, u32[]{:S(2)}) copy-start(s32[1,512]{1,0:T(1,128)} %param.10) | copy-start | bytes 6148
  28.4 10.8 %collective-permute-start.9 = (f32[128,256]{1,0:T(8,128)S(1)}, f32[128,256]{1,0:T(8,128)S(1)}, u32[]{:S(2)}, u32[]{:S(2)}) collective-permute-start(f32[128,256]{1,0:T(8,128)S(1)} %choose.1), channel_id=1, source_target_pairs={{1,2},{2,1},{3,4},{4,3},{5,6},{6,5},{7,15},{8,16},{9,10},{10,9},{1... | collective-permute-start | bytes 393224 | tf_op jit(solution)/shard_map/ppermute | solution.py:561
  31.4 0.7 copy-start.3
  31.5 0.7 copy-start.4
  32.2 6.9 %collective-permute-start.2 = (f32[8,512]{1,0:T(8,128)S(1)}, f32[8,512]{1,0:T(8,128)S(1)}, u32[]{:S(2)}, u32[]{:S(2)}) collective-permute-start(f32[8,512]{1,0:T(8,128)S(1)} %concatenate.3.refs_1_), channel_id=1, source_target_pairs={{8,15},{9,14},{10,13},{11,12},{12,11},{13,10},{14,9},{15,8},{24,31... | collective-permute-start | bytes 49160 | tf_op jit(solution)/shard_map/ppermute | solution.py:540
  41.2 2.8 %collective-permute-start.10 = (f32[4,128,256]{2,1,0:T(8,128)S(1)}, f32[4,128,256]{2,1,0:T(8,128)S(1)}, u32[]{:S(2)}, u32[]{:S(2)}) collective-permute-start(f32[4,128,256]{2,1,0:T(8,128)S(1)} %get-tuple-element.54.near_other), channel_id=1, source_target_pairs={{0,1},{1,0},{2,3},{3,2},{4,5},{5,4},{6,7},{7,6},{8,9},{9,8},{10,11... | collective-permute-start | bytes 1572872 | tf_op jit(solution)/shard_map/ppermute | solution.py:567
  42.5 8.3 %collective-permute-start.11 = (f32[4,128,256]{2,1,0:T(8,128)S(1)}, f32[4,128,256]{2,1,0:T(8,128)S(1)}, u32[]{:S(2)}, u32[]{:S(2)}) collective-permute-start(f32[4,128,256]{2,1,0:T(8,128)S(1)} %get-tuple-element.53.near_own), channel_id=1, source_target_pairs={{0,1},{1,0},{2,3},{3,2},{4,5},{5,4},{6,7},{7,6},{8,9},{9,8},{10,11... | collective-permute-start | bytes 1572872 | tf_op jit(solution)/shard_map/ppermute | solution.py:569
  44.0 16.2 %collective-permute-start.13 = (f32[4,128,256]{2,1,0:T(8,128)S(1)}, f32[4,128,256]{2,1,0:T(8,128)S(1)}, u32[]{:S(2)}, u32[]{:S(2)}) collective-permute-start(f32[4,128,256]{2,1,0:T(8,128)S(1)} %collective-permute-done.10.far_own), channel_id=1, source_target_pairs={{1,2},{2,1},{3,4},{4,3},{5,6},{6,5},{7,15},{8,16},{9,10},{10,9},{1... | collective-permute-start | bytes 1572872 | tf_op jit(solution)/shard_map/ppermute | solution.py:570
  46.1 14.1 %collective-permute-start.12 = (f32[3,128,256]{2,1,0:T(8,128)S(1)}, f32[3,128,256]{2,1,0:T(8,128)S(1)}, u32[]{:S(2)}, u32[]{:S(2)}) collective-permute-start(f32[3,128,256]{2,1,0:T(8,128)S(1)} %get-tuple-element.62), channel_id=1, source_target_pairs={{1,2},{2,1},{3,4},{4,3},{5,6},{6,5},{7,15},{8,16},{9,10},{10,9},{1... | collective-permute-start | bytes 1179656 | tf_op jit(solution)/shard_map/ppermute | solution.py:568
  72.3 7.4 %collective-permute-start.14 = (f32[128,256]{1,0:T(8,128)S(1)}, f32[128,256]{1,0:T(8,128)S(1)}, u32[]{:S(2)}, u32[]{:S(2)}) collective-permute-start(f32[128,256]{1,0:T(8,128)S(1)} %get-tuple-element.63), channel_id=1, source_target_pairs={{0,7},{1,6},{2,5},{3,4},{4,3},{5,2},{6,1},{7,0},{8,15},{9,14},{10,... | collective-permute-start | bytes 393224 | tf_op jit(solution)/shard_map/ppermute | solution.py:588
  75.6 14.7 %collective-permute-start.15 = (f32[128,256]{1,0:T(8,128)S(1)}, f32[128,256]{1,0:T(8,128)S(1)}, u32[]{:S(2)}, u32[]{:S(2)}) collective-permute-start(f32[128,256]{1,0:T(8,128)S(1)} %get-tuple-element.64), channel_id=1, source_target_pairs={{0,6},{1,7},{2,4},{3,5},{4,2},{5,3},{6,0},{7,1},{8,14},{9,15},{10,... | collective-permute-start | bytes 393224 | tf_op jit(solution)/shard_map/ppermute | solution.py:588
  75.6 19.3 %collective-permute-start.16 = (f32[128,256]{1,0:T(8,128)S(1)}, f32[128,256]{1,0:T(8,128)S(1)}, u32[]{:S(2)}, u32[]{:S(2)}) collective-permute-start(f32[128,256]{1,0:T(8,128)S(1)} %get-tuple-element.65), channel_id=1, source_target_pairs={{0,5},{1,4},{2,7},{3,6},{4,1},{5,0},{6,3},{7,2},{8,13},{9,12},{10,... | collective-permute-start | bytes 393224 | tf_op jit(solution)/shard_map/ppermute | solution.py:588
  75.6 20.9 %collective-permute-start.17 = (f32[128,256]{1,0:T(8,128)S(1)}, f32[128,256]{1,0:T(8,128)S(1)}, u32[]{:S(2)}, u32[]{:S(2)}) collective-permute-start(f32[128,256]{1,0:T(8,128)S(1)} %get-tuple-element.66), channel_id=1, source_target_pairs={{0,4},{1,5},{2,6},{3,7},{4,0},{5,1},{6,2},{7,3},{8,12},{9,13},{10,... | collective-permute-start | bytes 393224 | tf_op jit(solution)/shard_map/ppermute | solution.py:588
  78.6 17.9 %collective-permute-start.18 = (f32[128,256]{1,0:T(8,128)S(1)}, f32[128,256]{1,0:T(8,128)S(1)}, u32[]{:S(2)}, u32[]{:S(2)}) collective-permute-start(f32[128,256]{1,0:T(8,128)S(1)} %get-tuple-element.67), channel_id=1, source_target_pairs={{0,3},{1,2},{2,1},{3,0},{4,7},{5,6},{6,5},{7,4},{8,11},{9,10},{10,... | collective-permute-start | bytes 393224 | tf_op jit(solution)/shard_map/ppermute | solution.py:588
  79.7 18.6 %collective-permute-start.19 = (f32[128,256]{1,0:T(8,128)S(1)}, f32[128,256]{1,0:T(8,128)S(1)}, u32[]{:S(2)}, u32[]{:S(2)}) collective-permute-start(f32[128,256]{1,0:T(8,128)S(1)} %get-tuple-element.68), channel_id=1, source_target_pairs={{0,2},{1,3},{2,0},{3,1},{4,6},{5,7},{6,4},{7,5},{8,10},{9,11},{10,... | collective-permute-start | bytes 393224 | tf_op jit(solution)/shard_map/ppermute | solution.py:588
  90.3 8.0 %collective-permute-start.20 = (f32[128,256]{1,0:T(8,128)S(1)}, f32[128,256]{1,0:T(8,128)S(1)}, u32[]{:S(2)}, u32[]{:S(2)}) collective-permute-start(f32[128,256]{1,0:T(8,128)S(1)} %get-tuple-element.69), channel_id=1, source_target_pairs={{0,1},{1,0},{2,3},{3,2},{4,5},{5,4},{6,7},{7,6},{8,9},{9,8},{10,11... | collective-permute-start | bytes 393224 | tf_op jit(solution)/shard_map/ppermute | solution.py:588

commit v13 on v12

--- a/solution.py
+++ b/solution.py
@@ -13,6 +13,7 @@
 DONE = 0.01
 LARGE = 2e4
 PART = 256
+PADDING = 8
 F32 = jnp.float32
 BF16 = jnp.bfloat16
 
@@ -150,41 +151,32 @@
     return jnp.where(chip == 0, k, jnp.where(chip == chips - 1, chips - 1 - k, inner))
 
 
-def choose_kernel(info_ref, inner_ref, edge_ref, own_ref):
-    at_edge = jnp.logical_or(info_ref[0] == 0, info_ref[0] == info_ref[3] - 1)
-    for ref, here in ((inner_ref, jnp.logical_not(at_edge)), (edge_ref, at_edge)):
-
-        @pl.when(here)
-        def _():
-            own_ref[...] = ref[1]
-
-
 def collect_kernel(order, info_ref, mine_ref, other_ref, *refs):
     chips = len(order)
-    near_other, near_own, late_own, observed_ref = refs[-4:]
+    near_other, near_own, observed_ref = refs[-3:]
+    step = near_other.shape[1]
     observed_ref[...] = jnp.where(info_ref[2] == 1, other_ref[...], mine_ref[...])
+    near_own[pl.ds(chips * step, PADDING), :] = jnp.zeros((PADDING, near_own.shape[1]), F32)
     chip = info_ref[0]
     at_edge = jnp.logical_or(chip == 0, chip == chips - 1)
     for index, (s, k) in enumerate(order):
         block = source_of(chip, chips, s, k)
+        rows = pl.ds(pl.multiple_of(block * step, step), step)
         for ref, here in ((refs[index], jnp.logical_not(at_edge)), (refs[chips + index], at_edge)):
 
             @pl.when(here)
             def _():
                 near_other[block] = ref[0]
-                near_own[block] = ref[1]
-                if index:
-                    late_own[index - 1] = ref[1]
+                near_own[rows, :] = ref[1]
 
 
 def unpack_kernel(order, info_ref, *refs):
-    row_refs, out_ref, rows_ref = refs[:-2], refs[-2], refs[-1]
-    rows = rows_ref.shape[0]
+    row_refs, out_ref = refs[:-1], refs[-1]
+    rows = out_ref.shape[1]
     for x, ref in zip(order, row_refs):
         position = (2 * info_ref[0] + info_ref[1]) ^ x
-        rows_ref[position + info_ref[2] * (rows - 1 - 2 * position)] = ref[...]
-    for row in range(rows):
-        out_ref[:, row, :] = rows_ref[row]
+        row = position + info_ref[2] * (rows - 1 - 2 * position)
+        out_ref[:, pl.ds(row, 1), :] = ref[...][:, None, :]
 
 
 def pieces(x, count):
@@ -250,7 +242,7 @@
     spread_high, spread_low, own_high, own_low, own_part, seen_ref, direction_ref,
     anomaly, high_ref, low_ref,
 ):
-    chips, step, width = near_own.shape
+    chips, step, width = near_other.shape
     members = 2 * chips * step
     cells, _, _, scale = observations(info_ref, observed_ref, width, math.sqrt(members - 1))
     chosen = one_hot(cells, width, 2 * width)
@@ -258,8 +250,10 @@
     means = []
     for place in range(2):
         columns = pl.ds(place * width, width)
-        halves = (near_own, far_own) if place else (near_other, far_other)
-        rows = [half.at[chip] for half in halves for chip in range(chips)]
+        if place:
+            rows = [near_own.at[block, :] for block in blocks[:chips]] + [far_own.at[chip] for chip in range(chips)]
+        else:
+            rows = [near_other.at[chip] for chip in range(chips)] + [far_other.at[block, :] for block in blocks[:chips]]
         means.append(mean_of([row[...] for row in rows], members))
         for block, row in zip(blocks, rows):
             part = row[...] - means[-1]
@@ -315,10 +309,10 @@
 
 
 def region_kernel(
-    order, info_ref, observed_ref, near_own, far_own, high_in, low_in, own_high, own_low, own_part, seen_ref,
-    direction_ref, early_ref, late_ref, rest_ref, *refs,
+    info_ref, observed_ref, near_own, far_own, high_in, low_in, own_high, own_low, own_part, seen_ref,
+    direction_ref, half_ref, rest_ref, *refs,
 ):
-    chips, step, width = near_own.shape
+    chips, step, width = far_own.shape
     out_refs = refs[:-4]
     spread_high, spread_low, factor, answer = refs[-4:]
     members = 2 * chips * step
@@ -328,7 +322,6 @@
     ends = jnp.logical_or(
         jnp.logical_and(info_ref[0] == 0, core == 0), jnp.logical_and(info_ref[0] == chips - 1, core == 1)
     )
-    giver = jnp.where(ends, info_ref[0], info_ref[0] - 1 + 2 * core)
     part = jnp.where(ends, 0, 1)
     cells, slot_weight, values, scale = observations(info_ref, observed_ref, width, root)
     chosen = one_hot(cells, 0, width)
@@ -336,10 +329,7 @@
     def rows_at(half, chip):
         return pl.ds(pl.multiple_of((half * chips + chip) * step, step), step)
 
-    blocks = [(early_ref, rows_at(part, source_of(giver, chips, *order[0])))]
-    blocks += [
-        (late_ref.at[place - 1], rows_at(part, source_of(giver, chips, *order[place]))) for place in range(1, chips)
-    ]
+    blocks = [(half_ref.at[pl.ds(chip * step, step), :], rows_at(part, chip)) for chip in range(chips)]
     blocks += [(rest_ref.at[chip], rows_at(1 - part, chip)) for chip in range(chips)]
     mean = mean_of([ref[...] for ref, _ in blocks], members)
     taken = None
@@ -433,7 +423,7 @@
         rows = pl.ds(pl.multiple_of((part * chips + chip) * step, step), step)
         moved = product([spread_high[rows, :], spread_low[rows, :]], halved)
         moved = moved + doubled(direction_ref[rows, :]) * along
-        own = (far_own if part else near_own)[chip]
+        own = far_own[chip] if part else near_own[rows_at(0, chip), :]
         out_ref[...] = own + shift + moved
 
 
@@ -557,15 +547,13 @@
                     if 0 <= to < patches:
                         borders.append((device(p, chip, core), device(to, chip, core)))
 
-    early = call(choose_kernel, "choose", array(step, width), [info, inner[0], outer[0]])
-    got_early = lax.ppermute(early, axes, borders)
     half = array(chips, step, width)
-    near_other, near_own, late, observed = call(
+    near_other, near_own, observed = call(
         functools.partial(collect_kernel, order), "collect",
-        [half, half, array(chips - 1, step, width), array(8, slots)], [info, mine, other] + pieces_in, after=[got_early],
+        [half, array(chips * step + PADDING, width), array(8, slots)], [info, mine, other] + pieces_in,
     )
     far_own = lax.ppermute(near_other, axes, siblings)
-    got_late = lax.ppermute(late, axes, borders)
+    got_half = lax.ppermute(near_own, axes, borders)
     far_other = lax.ppermute(near_own, axes, siblings)
     got_rest = lax.ppermute(far_own, axes, borders)
 
@@ -579,8 +567,8 @@
         flops=8 * members * slots * width, limit=20,
     )
     analysed = call(
-        functools.partial(region_kernel, order), "region", [array(step, width)] * lanes,
-        [info, observed, near_own, far_own, *prepared, got_early, got_late, got_rest],
+        region_kernel, "region", [array(step, width)] * lanes,
+        [info, observed, near_own, far_own, *prepared, got_half, got_rest],
         split + [pltpu.VMEM((slots, slots), F32), pltpu.VMEM((width + 8, slots), F32)],
         limit=24,
     )
@@ -590,7 +578,7 @@
     order = sorted(range(lanes), key=lambda x: (x.bit_length() != lanes.bit_length() - 1, -x))
     return call(
         functools.partial(unpack_kernel, order), "unpack", array(step, rows, width),
-        [info] + [swapped(x) for x in order], [pltpu.VMEM((rows, step, width), F32)], limit=48,
+        [info] + [swapped(x) for x in order], limit=48,
     )
 
 

time: 100 us -> 97.5 us (0.975); the launches traced: 100 us -> 96.3 us
  starting transfers between devices: 51.2 us -> 36.3 us
  waiting for transfers between devices: 21.3 us -> 32.8 us
    ppermute x7, starting transfers between devices: 17.9 us -> 6.27 us  [swapped(): lax.ppermute(analysed[x], 'member', [(i, i ^ x) for i in range(lanes)])]
    ppermute x7, waiting for transfers between devices: 8.03 us -> 16.6 us  [swapped(): lax.ppermute(analysed[x], 'member', [(i, i ^ x) for i in range(lanes)])]
    ppermute x1, waiting for transfers between devices: 0.01 us -> 5.62 us  [per_device(): got_rest = lax.ppermute(far_own, axes, borders)]
    ppermute x2 -> x1, starting transfers between devices: 7.09 us -> 2.02 us  [per_device(): got_half = lax.ppermute(near_own, axes, borders)]
    ppermute x2 -> x1, waiting for transfers between devices: 5.4 us -> 1.28 us  [per_device(): got_half = lax.ppermute(near_own, axes, borders)]
    ppermute x6, waiting for transfers between devices: 1.4 us -> 4.12 us  [between(): lax.ppermute(message, 'member', [(2 * a + core, 2 * b + core) for a, b in...]
    ppermute x1, starting transfers between devices: 2.03 us -> 4.7 us  [per_device(): got_rest = lax.ppermute(far_own, axes, borders)]
    ppermute x1, waiting for transfers between devices: 1.46 us -> 0.01 us  [per_device(): far_own = lax.ppermute(near_other, axes, siblings)]
  transfers between devices with their start and end apart: 21 -> 20, of which waited for: 7 -> 8; matrix products, arithmetic and copies ran while one was open for 0% -> 0% of each run, Pallas kernels for 8% -> 8%
where the time goes in v13:
time: 97.5 us; the launch traced here: 96.3 us
  starting transfers between devices  36.3 us (37%)
  waiting for transfers between devices  32.8 us (34%)
  Pallas kernels  23.5 us (24%)
  local copies, waits for them, and re-layouts  2.63 us (3%)
    pallas_call x6, Pallas kernels, call(): pl.pallas_call(kernel, out_shape=out_shape, in_specs=[SMEM] + [VMEM] * (l...  22.4 us
    ppermute x7, waiting for transfers between devices, swapped(): lax.ppermute(analysed[x], 'member', [(i, i ^ x) for i in range(lanes)])  16.6 us
    ppermute x6, starting transfers between devices, between(): lax.ppermute(message, 'member', [(2 * a + core, 2 * b + core) for a, b in...  15.9 us
    ppermute x7, starting transfers between devices, swapped(): lax.ppermute(analysed[x], 'member', [(i, i ^ x) for i in range(lanes)])  6.27 us
    ppermute x1, waiting for transfers between devices, per_device(): got_rest = lax.ppermute(far_own, axes, borders)  5.62 us
    ppermute x1, waiting for transfers between devices, per_device(): lax.ppermute(mine, axes, [(p * lanes + i, p * lanes + lanes - 1 - i) for...  5.27 us
    ppermute x2, starting transfers between devices, swap(): lax.ppermute(message, 'patch', [(p, p + 1) for p in lower] + [(p + 1, p)...  4.94 us
    ppermute x1, starting transfers between devices, per_device(): got_rest = lax.ppermute(far_own, axes, borders)  4.7 us
  transfers between devices with their start and end apart: 20, of which 8 were waited for; matrix products, arithmetic and copies ran while one was open for 0% of the time, Pallas kernels for 8%

profile of v13, /device:TPU:2, one launch (start us, length us, event | category | flops | bytes accessed | tf_op | source)
XLA Modules:
  0.0 96.3 jit_solution(1819454825770585433)
XLA Ops:
  0.0 0.0 copy-start.1
  0.0 0.1 pad_add_fusion.info_ref
  0.1 0.0 copy-start.2
  0.1 0.7 copy-done.1
  0.8 0.0 copy-done.2
  0.8 0.0 copy-start
  0.8 1.2 %copy-done = f32[128,8,256]{2,1,0:T(8,128)S(1)} copy-done((f32[128,8,256]{2,1,0:T(8,128)S(1)}, f32[128,8,256]{2,1,0:T(8,128)}, u32[]{:S(2)}) %copy-start) | copy-done | bytes 1048600
  2.0 1.1 %pack.1 = (f32[264,256]{1,0:T(8,128)S(1)}, f32[264,256]{1,0:T(8,128)S(1)}, f32[4,8,256]{2,1,0:T(8,128)S(1)}, f32[128,128]{1,0:T(8,128)S(1)}) custom-call(s32[4]{0:T(128)S(1)} %pad_add_fusion.info_ref, f32[128,8,256]{2,1,0:T(8,128)S(1)} %copy-done, f32[4,8,256]{2,1,0:T(8,128)S(1)} %copy-done.1, f32[1,128]{1,0:T(1,128)S(1)} %bitcast.5), custom_call_target="tpu_custom_call" | custom-call | tf_op jit(solution)/shard_map/pack/pallas_call | solution.py:476
  3.1 0.1 collective-permute-start
  3.1 4.9 %collective-permute-start.1 = (f32[264,256]{1,0:T(8,128)S(1)}, f32[264,256]{1,0:T(8,128)S(1)}, u32[]{:S(2)}, u32[]{:S(2)}) collective-permute-start(f32[264,256]{1,0:T(8,128)S(1)} %get-tuple-element.41), channel_id=1, source_target_pairs={{8,16},{16,8},{9,17},{17,9},{10,18},{18,10},{11,19},{19,11},{12,20... | collective-permute-start | bytes 811016 | tf_op jit(solution)/shard_map/ppermute | solution.py:488
  8.0 2.2 %inner.1 = (f32[4,128,256]{2,1,0:T(8,128)S(1)}, f32[2,128,256]{2,1,0:T(8,128)S(1)}, f32[2,128,256]{2,1,0:T(8,128)S(1)}, f32[2,128,256]{2,1,0:T(8,128)S(1)}, f32[2,128,256]{2,1,0:T(8,128)S(1)}) custom-call(s32[4]{0:T(128)S(1)} %pad_add_fusion.info_ref, f32[128,8,256]{2,1,0:T(8,128)S(1)} %copy-done, f32[4,8,256]{2,1,0:T(8,128)S(1)} %get-tuple-element.37.flow_ref, ...), custom_call_target="tpu_custom_call" | custom-call | tf_op jit(solution)/shard_map/inner/pallas_call | solution.py:440
  10.2 0.7 collective-permute-start.3
  10.9 6.2 %collective-permute-start.4 = (f32[2,128,256]{2,1,0:T(8,128)S(1)}, f32[2,128,256]{2,1,0:T(8,128)S(1)}, u32[]{:S(2)}, u32[]{:S(2)}) collective-permute-start(f32[2,128,256]{2,1,0:T(8,128)S(1)} %get-tuple-element.46), channel_id=1, source_target_pairs={{6,2},{7,3},{0,4},{1,5},{14,10},{15,11},{8,12},{9,13},{22,18},{23,... | collective-permute-start | bytes 786440 | tf_op jit(solution)/shard_map/ppermute | solution.py:504
  17.1 1.4 %collective-permute-start.5 = (f32[2,128,256]{2,1,0:T(8,128)S(1)}, f32[2,128,256]{2,1,0:T(8,128)S(1)}, u32[]{:S(2)}, u32[]{:S(2)}) collective-permute-start(f32[2,128,256]{2,1,0:T(8,128)S(1)} %get-tuple-element.47), channel_id=1, source_target_pairs={{0,2},{1,3},{6,4},{7,5},{8,10},{9,11},{14,12},{15,13},{16,18},{17,... | collective-permute-start | bytes 786440 | tf_op jit(solution)/shard_map/ppermute | solution.py:504
  18.5 0.0 collective-permute-done.last_ref
  18.6 0.0 collective-permute-done.1.first_ref
  18.6 1.6 %edge.1 = (f32[2,128,256]{2,1,0:T(8,128)S(1)}, f32[2,128,256]{2,1,0:T(8,128)S(1)}, f32[2,128,256]{2,1,0:T(8,128)S(1)}, f32[2,128,256]{2,1,0:T(8,128)S(1)}) custom-call(s32[4]{0:T(128)S(1)} %pad_add_fusion.info_ref, f32[128,8,256]{2,1,0:T(8,128)S(1)} %copy-done, f32[4,8,256]{2,1,0:T(8,128)S(1)} %get-tuple-element.37.flow_ref, ...), custom_call_target="tpu_custom_call" | custom-call | tf_op jit(solution)/shard_map/edge/pallas_call | solution.py:440
  20.1 1.3 %collective-permute-start.6 = (f32[2,128,256]{2,1,0:T(8,128)S(1)}, f32[2,128,256]{2,1,0:T(8,128)S(1)}, u32[]{:S(2)}, u32[]{:S(2)}) collective-permute-start(f32[2,128,256]{2,1,0:T(8,128)S(1)} %get-tuple-element.48), channel_id=1, source_target_pairs={{2,0},{3,1},{4,6},{5,7},{10,8},{11,9},{12,14},{13,15},{18,16},{19,... | collective-permute-start | bytes 786440 | tf_op jit(solution)/shard_map/ppermute | solution.py:504
  21.4 1.3 %collective-permute-start.7 = (f32[2,128,256]{2,1,0:T(8,128)S(1)}, f32[2,128,256]{2,1,0:T(8,128)S(1)}, u32[]{:S(2)}, u32[]{:S(2)}) collective-permute-start(f32[2,128,256]{2,1,0:T(8,128)S(1)} %get-tuple-element.49), channel_id=1, source_target_pairs={{4,0},{5,1},{2,6},{3,7},{12,8},{13,9},{10,14},{11,15},{20,16},{21,... | collective-permute-start | bytes 786440 | tf_op jit(solution)/shard_map/ppermute | solution.py:504
  22.7 0.0 collective-permute-done.3.refs_1_
  22.7 0.0 copy-start.5
  22.8 5.0 %collective-permute-start.8 = (f32[2,128,256]{2,1,0:T(8,128)S(1)}, f32[2,128,256]{2,1,0:T(8,128)S(1)}, u32[]{:S(2)}, u32[]{:S(2)}) collective-permute-start(f32[2,128,256]{2,1,0:T(8,128)S(1)} %get-tuple-element.50), channel_id=1, source_target_pairs={{6,0},{7,1},{0,6},{1,7},{14,8},{15,9},{8,14},{9,15},{22,16},{23,17... | collective-permute-start | bytes 786440 | tf_op jit(solution)/shard_map/ppermute | solution.py:504
  28.4 0.0 copy-done.5
  28.5 0.0 copy-start.3
  28.5 0.0 copy-start.4
  28.5 0.6 copy-done.3
  29.2 0.0 copy-done.4
  29.2 0.0 collective-permute-done.4.refs_2_
  29.2 1.9 %collective-permute-start.2 = (f32[8,512]{1,0:T(8,128)S(1)}, f32[8,512]{1,0:T(8,128)S(1)}, u32[]{:S(2)}, u32[]{:S(2)}) collective-permute-start(f32[8,512]{1,0:T(8,128)S(1)} %concatenate.3.mine_ref), channel_id=1, source_target_pairs={{8,15},{9,14},{10,13},{11,12},{12,11},{13,10},{14,9},{15,8},{24,31... | collective-permute-start | bytes 49160 | tf_op jit(solution)/shard_map/ppermute | solution.py:530
  31.1 0.0 collective-permute-done.5.refs_3_
  31.2 5.3 %collective-permute-done.2.other_ref = f32[8,512]{1,0:T(8,128)S(1)} collective-permute-done((f32[8,512]{1,0:T(8,128)S(1)}, f32[8,512]{1,0:T(8,128)S(1)}, u32[]{:S(2)}, u32[]{:S(2)}) %collective-permute-start.2) | collective-permute-done | bytes 16416 | tf_op jit(solution)/shard_map/ppermute | solution.py:530
  36.4 4.1 %collective-permute-done.6.refs_5_ = f32[2,128,256]{2,1,0:T(8,128)S(1)} collective-permute-done((f32[2,128,256]{2,1,0:T(8,128)S(1)}, f32[2,128,256]{2,1,0:T(8,128)S(1)}, u32[]{:S(2)}, u32[]{:S(2)}) %collective-permute-start.6) | collective-permute-done | bytes 262176 | tf_op jit(solution)/shard_map/ppermute | solution.py:504
  40.5 0.0 collective-permute-done.7.refs_6_
  40.5 0.0 collective-permute-done.8.refs_7_
  40.5 0.6 collect.1
  41.2 0.1 collective-permute-start.9
  41.3 0.5 collective-permute-start.10
  41.8 2.0 %collective-permute-start.11 = (f32[520,256]{1,0:T(8,128)S(1)}, f32[520,256]{1,0:T(8,128)S(1)}, u32[]{:S(2)}, u32[]{:S(2)}) collective-permute-start(f32[520,256]{1,0:T(8,128)S(1)} %get-tuple-element.52.near_own), channel_id=1, source_target_pairs={{1,2},{2,1},{3,4},{4,3},{5,6},{6,5},{7,15},{8,16},{9,10},{10,9},{1... | collective-permute-start | bytes 1597448 | tf_op jit(solution)/shard_map/ppermute | solution.py:556
  43.8 0.0 collective-permute-done.9.far_own
  43.8 4.7 %collective-permute-start.12 = (f32[4,128,256]{2,1,0:T(8,128)S(1)}, f32[4,128,256]{2,1,0:T(8,128)S(1)}, u32[]{:S(2)}, u32[]{:S(2)}) collective-permute-start(f32[4,128,256]{2,1,0:T(8,128)S(1)} %collective-permute-done.9.far_own), channel_id=1, source_target_pairs={{1,2},{2,1},{3,4},{4,3},{5,6},{6,5},{7,15},{8,16},{9,10},{10,9},{1... | collective-permute-start | bytes 1572872 | tf_op jit(solution)/shard_map/ppermute | solution.py:558
  48.5 0.0 collective-permute-done.10.far_other
  48.5 4.0 %prepare.1 = (bf16[1024,512]{1,0:T(8,128)(2,1)S(1)}, bf16[1024,512]{1,0:T(8,128)(2,1)S(1)}, bf16[256,1024]{1,0:T(8,128)(2,1)S(1)}, bf16[256,1024]{1,0:T(8,128)(2...) custom-call(s32[4]{0:T(128)S(1)} %pad_add_fusion.info_ref, ...), custom_call_target="tpu_custom_call" | custom-call | flops 1073741824 | tf_op jit(solution)/shard_map/prepare/pallas_call | solution.py:440
  52.5 1.3 %collective-permute-done.11.half_ref = f32[520,256]{1,0:T(8,128)S(1)} collective-permute-done((f32[520,256]{1,0:T(8,128)S(1)}, f32[520,256]{1,0:T(8,128)S(1)}, u32[]{:S(2)}, u32[]{:S(2)}) %collective-permute-start.11) | collective-permute-done | bytes 532512 | tf_op jit(solution)/shard_map/ppermute | solution.py:556
  53.8 5.6 %collective-permute-done.12.rest_ref = f32[4,128,256]{2,1,0:T(8,128)S(1)} collective-permute-done((f32[4,128,256]{2,1,0:T(8,128)S(1)}, f32[4,128,256]{2,1,0:T(8,128)S(1)}, u32[]{:S(2)}, u32[]{:S(2)}) %collective-permute-start.12) | collective-permute-done | bytes 524320 | tf_op jit(solution)/shard_map/ppermute | solution.py:558
  59.4 12.1 %region.1 = (f32[128,256]{1,0:T(8,128)S(1)}, f32[128,256]{1,0:T(8,128)S(1)}, f32[128,256]{1,0:T(8,128)S(1)}, f32[128,256]{1,0:T(8,128)S(1)}, f32[128,256]{1,0:T(...) custom-call(s32[4]{0:T(128)S(1)} %pad_add_fusion.info_ref, ...), custom_call_target="tpu_custom_call" | custom-call | tf_op jit(solution)/shard_map/region/pallas_call | solution.py:440
  71.6 2.0 %collective-permute-start.13 = (f32[128,256]{1,0:T(8,128)S(1)}, f32[128,256]{1,0:T(8,128)S(1)}, u32[]{:S(2)}, u32[]{:S(2)}) collective-permute-start(f32[128,256]{1,0:T(8,128)S(1)} %get-tuple-element.61), channel_id=1, source_target_pairs={{0,7},{1,6},{2,5},{3,4},{4,3},{5,2},{6,1},{7,0},{8,15},{9,14},{10,... | collective-permute-start | bytes 393224 | tf_op jit(solution)/shard_map/ppermute | solution.py:576
  73.6 0.1 collective-permute-start.14
  73.7 0.0 collective-permute-start.15
  73.7 4.2 %collective-permute-start.16 = (f32[128,256]{1,0:T(8,128)S(1)}, f32[128,256]{1,0:T(8,128)S(1)}, u32[]{:S(2)}, u32[]{:S(2)}) collective-permute-start(f32[128,256]{1,0:T(8,128)S(1)} %get-tuple-element.64), channel_id=1, source_target_pairs={{0,4},{1,5},{2,6},{3,7},{4,0},{5,1},{6,2},{7,3},{8,12},{9,13},{10,... | collective-permute-start | bytes 393224 | tf_op jit(solution)/shard_map/ppermute | solution.py:576
  77.8 0.0 collective-permute-start.17
  77.8 0.2 collective-permute-done.13.refs_0_
  78.0 0.0 collective-permute-start.18
  78.1 3.7 %collective-permute-done.14.refs_1_ = f32[128,256]{1,0:T(8,128)S(1)} collective-permute-done((f32[128,256]{1,0:T(8,128)S(1)}, f32[128,256]{1,0:T(8,128)S(1)}, u32[]{:S(2)}, u32[]{:S(2)}) %collective-permute-start.14) | collective-permute-done | bytes 131104 | tf_op jit(solution)/shard_map/ppermute | solution.py:576
  81.8 0.0 collective-permute-start.19
  81.8 9.5 %collective-permute-done.15.refs_2_ = f32[128,256]{1,0:T(8,128)S(1)} collective-permute-done((f32[128,256]{1,0:T(8,128)S(1)}, f32[128,256]{1,0:T(8,128)S(1)}, u32[]{:S(2)}, u32[]{:S(2)}) %collective-permute-start.15) | collective-permute-done | bytes 131104 | tf_op jit(solution)/shard_map/ppermute | solution.py:576
  91.2 3.2 %collective-permute-done.16.refs_3_ = f32[128,256]{1,0:T(8,128)S(1)} collective-permute-done((f32[128,256]{1,0:T(8,128)S(1)}, f32[128,256]{1,0:T(8,128)S(1)}, u32[]{:S(2)}, u32[]{:S(2)}) %collective-permute-start.16) | collective-permute-done | bytes 131104 | tf_op jit(solution)/shard_map/ppermute | solution.py:576
  94.4 0.0 collective-permute-done.17.refs_4_
  94.4 0.0 collective-permute-done.18.refs_5_
  94.4 0.0 collective-permute-done.19.refs_6_
  94.4 1.9 %unpack.1 = f32[128,8,256]{2,1,0:T(8,128)} custom-call(s32[4]{0:T(128)S(1)} %pad_add_fusion.info_ref, f32[128,256]{1,0:T(8,128)S(1)} %collective-permute-done.13.refs_0_, f32[128,256]{1,0:T(8,128)S(1)} %collective-permute-done.14.refs_1_, f32[128,256]{1,0:T(8,128)S(1)} %collective-permute-done.15.refs_2_, f32[128,256]{1,0:T(8,128)S(1)} %collective-permute-done.16.refs_3_, ...), custom_call_target="tpu_custom_call" | custom-call | tf_op jit(solution)/shard_map/unpack/pallas_call | solution.py:440
  (3 shorter events, 0.0 us)
Async XLA Ops:
  0.0 0.8 copy-start.1
  0.1 0.7 copy-start.2
  0.8 1.2 %copy-start = (f32[128,8,256]{2,1,0:T(8,128)S(1)}, f32[128,8,256]{2,1,0:T(8,128)}, u32[]{:S(2)}) copy-start(f32[128,8,256]{2,1,0:T(8,128)} %field_ref.3) | copy-start | bytes 3145732
  3.1 15.5 %collective-permute-start = (f32[264,256]{1,0:T(8,128)S(1)}, f32[264,256]{1,0:T(8,128)S(1)}, u32[]{:S(2)}, u32[]{:S(2)}) collective-permute-start(f32[264,256]{1,0:T(8,128)S(1)} %get-tuple-element.40), channel_id=1, source_target_pairs={{0,8},{16,24},{8,0},{24,16},{1,9},{17,25},{9,1},{25,17},{2,10},{18... | collective-permute-start | bytes 811016 | tf_op jit(solution)/shard_map/ppermute | solution.py:488
  3.1 15.4 %collective-permute-start.1 = (f32[264,256]{1,0:T(8,128)S(1)}, f32[264,256]{1,0:T(8,128)S(1)}, u32[]{:S(2)}, u32[]{:S(2)}) collective-permute-start(f32[264,256]{1,0:T(8,128)S(1)} %get-tuple-element.41), channel_id=1, source_target_pairs={{8,16},{16,8},{9,17},{17,9},{10,18},{18,10},{11,19},{19,11},{12,20... | collective-permute-start | bytes 811016 | tf_op jit(solution)/shard_map/ppermute | solution.py:488
  10.2 12.5 %collective-permute-start.3 = (f32[2,128,256]{2,1,0:T(8,128)S(1)}, f32[2,128,256]{2,1,0:T(8,128)S(1)}, u32[]{:S(2)}, u32[]{:S(2)}) collective-permute-start(f32[2,128,256]{2,1,0:T(8,128)S(1)} %get-tuple-element.45), channel_id=1, source_target_pairs={{4,2},{5,3},{2,4},{3,5},{12,10},{13,11},{10,12},{11,13},{20,18},{2... | collective-permute-start | bytes 786440 | tf_op jit(solution)/shard_map/ppermute | solution.py:504
  10.9 18.3 %collective-permute-start.4 = (f32[2,128,256]{2,1,0:T(8,128)S(1)}, f32[2,128,256]{2,1,0:T(8,128)S(1)}, u32[]{:S(2)}, u32[]{:S(2)}) collective-permute-start(f32[2,128,256]{2,1,0:T(8,128)S(1)} %get-tuple-element.46), channel_id=1, source_target_pairs={{6,2},{7,3},{0,4},{1,5},{14,10},{15,11},{8,12},{9,13},{22,18},{23,... | collective-permute-start | bytes 786440 | tf_op jit(solution)/shard_map/ppermute | solution.py:504
  17.1 14.0 %collective-permute-start.5 = (f32[2,128,256]{2,1,0:T(8,128)S(1)}, f32[2,128,256]{2,1,0:T(8,128)S(1)}, u32[]{:S(2)}, u32[]{:S(2)}) collective-permute-start(f32[2,128,256]{2,1,0:T(8,128)S(1)} %get-tuple-element.47), channel_id=1, source_target_pairs={{0,2},{1,3},{6,4},{7,5},{8,10},{9,11},{14,12},{15,13},{16,18},{17,... | collective-permute-start | bytes 786440 | tf_op jit(solution)/shard_map/ppermute | solution.py:504
  20.1 20.4 %collective-permute-start.6 = (f32[2,128,256]{2,1,0:T(8,128)S(1)}, f32[2,128,256]{2,1,0:T(8,128)S(1)}, u32[]{:S(2)}, u32[]{:S(2)}) collective-permute-start(f32[2,128,256]{2,1,0:T(8,128)S(1)} %get-tuple-element.48), channel_id=1, source_target_pairs={{2,0},{3,1},{4,6},{5,7},{10,8},{11,9},{12,14},{13,15},{18,16},{19,... | collective-permute-start | bytes 786440 | tf_op jit(solution)/shard_map/ppermute | solution.py:504
  21.4 19.1 %collective-permute-start.7 = (f32[2,128,256]{2,1,0:T(8,128)S(1)}, f32[2,128,256]{2,1,0:T(8,128)S(1)}, u32[]{:S(2)}, u32[]{:S(2)}) collective-permute-start(f32[2,128,256]{2,1,0:T(8,128)S(1)} %get-tuple-element.49), channel_id=1, source_target_pairs={{4,0},{5,1},{2,6},{3,7},{12,8},{13,9},{10,14},{11,15},{20,16},{21,... | collective-permute-start | bytes 786440 | tf_op jit(solution)/shard_map/ppermute | solution.py:504
  22.7 5.7 %copy-start.5 = (s32[1,512]{1,0:T(1,128)S(1)}, s32[1,512]{1,0:T(1,128)}, u32[]{:S(2)}) copy-start(s32[1,512]{1,0:T(1,128)} %param.10) | copy-start | bytes 6148
  22.8 17.8 %collective-permute-start.8 = (f32[2,128,256]{2,1,0:T(8,128)S(1)}, f32[2,128,256]{2,1,0:T(8,128)S(1)}, u32[]{:S(2)}, u32[]{:S(2)}) collective-permute-start(f32[2,128,256]{2,1,0:T(8,128)S(1)} %get-tuple-element.50), channel_id=1, source_target_pairs={{6,0},{7,1},{0,6},{1,7},{14,8},{15,9},{8,14},{9,15},{22,16},{23,17... | collective-permute-start | bytes 786440 | tf_op jit(solution)/shard_map/ppermute | solution.py:504
  28.5 0.7 copy-start.3
  28.5 0.7 copy-start.4
  29.2 7.2 %collective-permute-start.2 = (f32[8,512]{1,0:T(8,128)S(1)}, f32[8,512]{1,0:T(8,128)S(1)}, u32[]{:S(2)}, u32[]{:S(2)}) collective-permute-start(f32[8,512]{1,0:T(8,128)S(1)} %concatenate.3.mine_ref), channel_id=1, source_target_pairs={{8,15},{9,14},{10,13},{11,12},{12,11},{13,10},{14,9},{15,8},{24,31... | collective-permute-start | bytes 49160 | tf_op jit(solution)/shard_map/ppermute | solution.py:530
  41.2 2.6 %collective-permute-start.9 = (f32[4,128,256]{2,1,0:T(8,128)S(1)}, f32[4,128,256]{2,1,0:T(8,128)S(1)}, u32[]{:S(2)}, u32[]{:S(2)}) collective-permute-start(f32[4,128,256]{2,1,0:T(8,128)S(1)} %get-tuple-element.53.near_other), channel_id=1, source_target_pairs={{0,1},{1,0},{2,3},{3,2},{4,5},{5,4},{6,7},{7,6},{8,9},{9,8},{10,11... | collective-permute-start | bytes 1572872 | tf_op jit(solution)/shard_map/ppermute | solution.py:555
  41.3 7.3 %collective-permute-start.10 = (f32[520,256]{1,0:T(8,128)S(1)}, f32[520,256]{1,0:T(8,128)S(1)}, u32[]{:S(2)}, u32[]{:S(2)}) collective-permute-start(f32[520,256]{1,0:T(8,128)S(1)} %get-tuple-element.52.near_own), channel_id=1, source_target_pairs={{0,1},{1,0},{2,3},{3,2},{4,5},{5,4},{6,7},{7,6},{8,9},{9,8},{10,11... | collective-permute-start | bytes 1597448 | tf_op jit(solution)/shard_map/ppermute | solution.py:557
  41.8 12.0 %collective-permute-start.11 = (f32[520,256]{1,0:T(8,128)S(1)}, f32[520,256]{1,0:T(8,128)S(1)}, u32[]{:S(2)}, u32[]{:S(2)}) collective-permute-start(f32[520,256]{1,0:T(8,128)S(1)} %get-tuple-element.52.near_own), channel_id=1, source_target_pairs={{1,2},{2,1},{3,4},{4,3},{5,6},{6,5},{7,15},{8,16},{9,10},{10,9},{1... | collective-permute-start | bytes 1597448 | tf_op jit(solution)/shard_map/ppermute | solution.py:556
  43.8 15.6 %collective-permute-start.12 = (f32[4,128,256]{2,1,0:T(8,128)S(1)}, f32[4,128,256]{2,1,0:T(8,128)S(1)}, u32[]{:S(2)}, u32[]{:S(2)}) collective-permute-start(f32[4,128,256]{2,1,0:T(8,128)S(1)} %collective-permute-done.9.far_own), channel_id=1, source_target_pairs={{1,2},{2,1},{3,4},{4,3},{5,6},{6,5},{7,15},{8,16},{9,10},{10,9},{1... | collective-permute-start | bytes 1572872 | tf_op jit(solution)/shard_map/ppermute | solution.py:558
  71.6 6.5 %collective-permute-start.13 = (f32[128,256]{1,0:T(8,128)S(1)}, f32[128,256]{1,0:T(8,128)S(1)}, u32[]{:S(2)}, u32[]{:S(2)}) collective-permute-start(f32[128,256]{1,0:T(8,128)S(1)} %get-tuple-element.61), channel_id=1, source_target_pairs={{0,7},{1,6},{2,5},{3,4},{4,3},{5,2},{6,1},{7,0},{8,15},{9,14},{10,... | collective-permute-start | bytes 393224 | tf_op jit(solution)/shard_map/ppermute | solution.py:576
  73.6 8.2 %collective-permute-start.14 = (f32[128,256]{1,0:T(8,128)S(1)}, f32[128,256]{1,0:T(8,128)S(1)}, u32[]{:S(2)}, u32[]{:S(2)}) collective-permute-start(f32[128,256]{1,0:T(8,128)S(1)} %get-tuple-element.62), channel_id=1, source_target_pairs={{0,6},{1,7},{2,4},{3,5},{4,2},{5,3},{6,0},{7,1},{8,14},{9,15},{10,... | collective-permute-start | bytes 393224 | tf_op jit(solution)/shard_map/ppermute | solution.py:576
  73.7 17.6 %collective-permute-start.15 = (f32[128,256]{1,0:T(8,128)S(1)}, f32[128,256]{1,0:T(8,128)S(1)}, u32[]{:S(2)}, u32[]{:S(2)}) collective-permute-start(f32[128,256]{1,0:T(8,128)S(1)} %get-tuple-element.63), channel_id=1, source_target_pairs={{0,5},{1,4},{2,7},{3,6},{4,1},{5,0},{6,3},{7,2},{8,13},{9,12},{10,... | collective-permute-start | bytes 393224 | tf_op jit(solution)/shard_map/ppermute | solution.py:576
  73.7 20.7 %collective-permute-start.16 = (f32[128,256]{1,0:T(8,128)S(1)}, f32[128,256]{1,0:T(8,128)S(1)}, u32[]{:S(2)}, u32[]{:S(2)}) collective-permute-start(f32[128,256]{1,0:T(8,128)S(1)} %get-tuple-element.64), channel_id=1, source_target_pairs={{0,4},{1,5},{2,6},{3,7},{4,0},{5,1},{6,2},{7,3},{8,12},{9,13},{10,... | collective-permute-start | bytes 393224 | tf_op jit(solution)/shard_map/ppermute | solution.py:576
  77.8 16.6 %collective-permute-start.17 = (f32[128,256]{1,0:T(8,128)S(1)}, f32[128,256]{1,0:T(8,128)S(1)}, u32[]{:S(2)}, u32[]{:S(2)}) collective-permute-start(f32[128,256]{1,0:T(8,128)S(1)} %get-tuple-element.65), channel_id=1, source_target_pairs={{0,3},{1,2},{2,1},{3,0},{4,7},{5,6},{6,5},{7,4},{8,11},{9,10},{10,... | collective-permute-start | bytes 393224 | tf_op jit(solution)/shard_map/ppermute | solution.py:576
  78.0 16.4 %collective-permute-start.18 = (f32[128,256]{1,0:T(8,128)S(1)}, f32[128,256]{1,0:T(8,128)S(1)}, u32[]{:S(2)}, u32[]{:S(2)}) collective-permute-start(f32[128,256]{1,0:T(8,128)S(1)} %get-tuple-element.66), channel_id=1, source_target_pairs={{0,2},{1,3},{2,0},{3,1},{4,6},{5,7},{6,4},{7,5},{8,10},{9,11},{10,... | collective-permute-start | bytes 393224 | tf_op jit(solution)/shard_map/ppermute | solution.py:576
  81.8 12.7 %collective-permute-start.19 = (f32[128,256]{1,0:T(8,128)S(1)}, f32[128,256]{1,0:T(8,128)S(1)}, u32[]{:S(2)}, u32[]{:S(2)}) collective-permute-start(f32[128,256]{1,0:T(8,128)S(1)} %get-tuple-element.67), channel_id=1, source_target_pairs={{0,1},{1,0},{2,3},{3,2},{4,5},{5,4},{6,7},{7,6},{8,9},{9,8},{10,11... | collective-permute-start | bytes 393224 | tf_op jit(solution)/shard_map/ppermute | solution.py:576

commit v14 on v13

--- a/solution.py
+++ b/solution.py
@@ -9,8 +9,8 @@
 from jax.sharding import PartitionSpec as P
 
 STEPS = 2
-COARSE = 0.2
-DONE = 0.01
+COARSE = 0.35
+DONE = 0.02
 LARGE = 2e4
 PART = 256
 PADDING = 8
@@ -132,7 +132,7 @@
             out_ref[1 - last] = ordered(weights_of(flow_ref[:, near, :]), own, inside, further)
 
 
-def edge_kernel(info_ref, field_ref, flow_ref, emission_ref, kept_ref, last_ref, first_ref, *refs):
+def edge_kernel(info_ref, field_ref, flow_ref, emission_ref, kept_ref, first_ref, last_ref, *refs):
     out_refs, scratch = refs[:-1], refs[-1]
     chips = len(out_refs)
     core = info_ref[1]
@@ -313,8 +313,8 @@
     direction_ref, half_ref, rest_ref, *refs,
 ):
     chips, step, width = far_own.shape
-    out_refs = refs[:-4]
-    spread_high, spread_low, factor, answer = refs[-4:]
+    out_refs = refs[:-5]
+    spread_high, spread_low, factor, squared, answer = refs[-5:]
     members = 2 * chips * step
     slots = observed_ref.shape[1]
     root = math.sqrt(members - 1)
@@ -369,14 +369,12 @@
 
     def begin(count):
         parts = pieces(factor[...], count)
-        top, bottom = square(parts)
-        limit = 1.0001 * jnp.sqrt(jnp.sqrt(size(top) + size(bottom)))
-        start = 2.0 / (1.0 + limit)
+        if count > 2:
+            squared[upper, :], squared[lower, :] = square(parts)
         bound = 1.0 - start
         gain = 2.0 / (2.0 - bound * bound)
         answer[...] = (gain * start) * (2.0 * answer[...] - start * product(pieces(answer[...], count), parts))
-        factor[upper, :] = (gain * start) * (2.0 * factor[upper, :] - start * top)
-        factor[lower, :] = (gain * start) * (2.0 * factor[lower, :] - start * bottom)
+        factor[...] = (gain * start) * (2.0 * factor[...] - start * squared[...])
         return after(bound)
 
     def refine(bound, count):
@@ -399,7 +397,12 @@
         factor[...] = gain * (dot(rest, rest) - jnp.where(eye, 0.5 * bound * bound, 0.0))
         return after(bound)
 
-    large = size(factor[...]) > LARGE * LARGE
+    top, bottom = square(pieces(factor[...], 2))
+    squared[upper, :] = top
+    squared[lower, :] = bottom
+    limit = 1.0001 * jnp.sqrt(jnp.sqrt(size(top) + size(bottom)))
+    start = 2.0 / (1.0 + limit)
+    large = limit > LARGE
     bound = lax.cond(large, lambda: begin(3), lambda: begin(2))
     bound = lax.while_loop(lambda b: jnp.logical_and(b > COARSE, large), lambda b: refine(b, 3), bound)
     bound = lax.while_loop(lambda b: b > COARSE, lambda b: refine(b, 2), bound)
@@ -414,10 +417,10 @@
     solved = solved.T
     which = lax.broadcasted_iota(jnp.int32, (8, slots), 0)
     sides = jnp.where(which == 0, innovation * (1.0 / root), jnp.where(which == 1, -0.5 * common, 0.0))
-    parts = pieces(solved, 3)
-    sides = product(pieces(sides, 3), parts)
+    parts = pieces(solved, 2)
+    sides = product(pieces(sides, 2), parts)
     shift, along = sides[0:1], sides[1:2]
-    halved = [part * jnp.asarray(-0.5, BF16) for part in pieces(solved, 2)]
+    halved = [part * jnp.asarray(-0.5, BF16) for part in parts]
     for x, out_ref in enumerate(out_refs):
         chip, part = info_ref[0] ^ (x // 2), x % 2
         rows = pl.ds(pl.multiple_of((part * chips + chip) * step, step), step)
@@ -487,7 +490,7 @@
         lower = range(start, patches - 1, 2)
         return lax.ppermute(message, "patch", [(p, p + 1) for p in lower] + [(p + 1, p) for p in lower])
 
-    halo_last, halo_first = swap(to_last, 0), swap(to_first, 1)
+    halo_first, halo_last = swap(to_first, 1), swap(to_last, 0)
 
     mine = jnp.concatenate(
         [
@@ -518,7 +521,7 @@
     )
     got_inner = [inner[0]] + [between(inner[s], targets[s]) for s in range(1, chips)]
     outer = call(
-        edge_kernel, "edge", [pair] * chips, args + [kept, halo_last, halo_first],
+        edge_kernel, "edge", [pair] * chips, args + [kept, halo_first, halo_last],
         [pltpu.VMEM((2, step, width), F32)], limit=32,
     )
     got_outer = [outer[0]] + [
@@ -569,7 +572,7 @@
     analysed = call(
         region_kernel, "region", [array(step, width)] * lanes,
         [info, observed, near_own, far_own, *prepared, got_half, got_rest],
-        split + [pltpu.VMEM((slots, slots), F32), pltpu.VMEM((width + 8, slots), F32)],
+        split + [pltpu.VMEM((slots, slots), F32)] * 2 + [pltpu.VMEM((width + 8, slots), F32)],
         limit=24,
     )
     def swapped(x):

time: 97.5 us -> 101 us (1.036)
  the two profiles are of different devices: /device:TPU:2 before, /device:TPU:0 now
where the time goes in v14:
time: 101 us
  starting transfers between devices  52.9 us (52%)
  Pallas kernels  23.7 us (23%)
  waiting for transfers between devices  21.1 us (21%)
  local copies, waits for them, and re-layouts  2.63 us (3%)
    ppermute x7, starting transfers between devices, swapped(): lax.ppermute(analysed[x], 'member', [(i, i ^ x) for i in range(lanes)])  27.3 us
    pallas_call x6, Pallas kernels, call(): pl.pallas_call(kernel, out_shape=out_shape, in_specs=[SMEM] + [VMEM] * (l...  22.6 us
    ppermute x6, starting transfers between devices, between(): lax.ppermute(message, 'member', [(2 * a + core, 2 * b + core) for a, b in...  16.4 us
    ppermute x6, waiting for transfers between devices, between(): lax.ppermute(message, 'member', [(2 * a + core, 2 * b + core) for a, b in...  10.1 us
    ppermute x7, waiting for transfers between devices, swapped(): lax.ppermute(analysed[x], 'member', [(i, i ^ x) for i in range(lanes)])  8.93 us
    ppermute x2, starting transfers between devices, swap(): lax.ppermute(message, 'patch', [(p, p + 1) for p in lower] + [(p + 1, p)...  6.4 us
    unnamed x12, local copies, waits for them, and re-layouts  2.58 us
  transfers between devices with their start and end apart: 20, of which 6 were waited for; matrix products, arithmetic and copies ran while one was open for 0% of the time, Pallas kernels for 8%

profile of v14, /device:TPU:0, one launch (start us, length us, event | category | flops | bytes accessed | tf_op | source)
XLA Modules:
  0.0 101.2 jit_solution(995564849766307007)
XLA Ops:
  0.0 0.0 copy-start.1
  0.0 0.1 pad_add_fusion.info_ref
  0.1 0.0 copy-start.2
  0.1 0.7 copy-done.1
  0.8 0.0 copy-done.2
  0.8 0.0 copy-start
  0.8 1.2 %copy-done = f32[128,8,256]{2,1,0:T(8,128)S(1)} copy-done((f32[128,8,256]{2,1,0:T(8,128)S(1)}, f32[128,8,256]{2,1,0:T(8,128)}, u32[]{:S(2)}) %copy-start) | copy-done | bytes 1048600
  2.0 1.1 %pack.1 = (f32[264,256]{1,0:T(8,128)S(1)}, f32[264,256]{1,0:T(8,128)S(1)}, f32[4,8,256]{2,1,0:T(8,128)S(1)}, f32[128,128]{1,0:T(8,128)S(1)}) custom-call(s32[4]{0:T(128)S(1)} %pad_add_fusion.info_ref, f32[128,8,256]{2,1,0:T(8,128)S(1)} %copy-done, f32[4,8,256]{2,1,0:T(8,128)S(1)} %copy-done.1, f32[1,128]{1,0:T(1,128)S(1)} %bitcast.5), custom_call_target="tpu_custom_call" | custom-call | tf_op jit(solution)/shard_map/pack/pallas_call | solution.py:479
  3.1 0.7 collective-permute-start
  3.8 5.7 %collective-permute-start.1 = (f32[264,256]{1,0:T(8,128)S(1)}, f32[264,256]{1,0:T(8,128)S(1)}, u32[]{:S(2)}, u32[]{:S(2)}) collective-permute-start(f32[264,256]{1,0:T(8,128)S(1)} %get-tuple-element.41), channel_id=1, source_target_pairs={{0,8},{16,24},{8,0},{24,16},{1,9},{17,25},{9,1},{25,17},{2,10},{18... | collective-permute-start | bytes 811016 | tf_op jit(solution)/shard_map/ppermute | solution.py:491
  9.5 2.2 %inner.1 = (f32[4,128,256]{2,1,0:T(8,128)S(1)}, f32[2,128,256]{2,1,0:T(8,128)S(1)}, f32[2,128,256]{2,1,0:T(8,128)S(1)}, f32[2,128,256]{2,1,0:T(8,128)S(1)}, f32[2,128,256]{2,1,0:T(8,128)S(1)}) custom-call(s32[4]{0:T(128)S(1)} %pad_add_fusion.info_ref, f32[128,8,256]{2,1,0:T(8,128)S(1)} %copy-done, f32[4,8,256]{2,1,0:T(8,128)S(1)} %get-tuple-element.37.flow_ref, ...), custom_call_target="tpu_custom_call" | custom-call | tf_op jit(solution)/shard_map/inner/pallas_call | solution.py:443
  11.7 0.7 collective-permute-start.3
  12.4 6.2 %collective-permute-start.4 = (f32[2,128,256]{2,1,0:T(8,128)S(1)}, f32[2,128,256]{2,1,0:T(8,128)S(1)}, u32[]{:S(2)}, u32[]{:S(2)}) collective-permute-start(f32[2,128,256]{2,1,0:T(8,128)S(1)} %get-tuple-element.46), channel_id=1, source_target_pairs={{6,2},{7,3},{0,4},{1,5},{14,10},{15,11},{8,12},{9,13},{22,18},{23,... | collective-permute-start | bytes 786440 | tf_op jit(solution)/shard_map/ppermute | solution.py:507
  18.6 1.4 %collective-permute-start.5 = (f32[2,128,256]{2,1,0:T(8,128)S(1)}, f32[2,128,256]{2,1,0:T(8,128)S(1)}, u32[]{:S(2)}, u32[]{:S(2)}) collective-permute-start(f32[2,128,256]{2,1,0:T(8,128)S(1)} %get-tuple-element.47), channel_id=1, source_target_pairs={{0,2},{1,3},{6,4},{7,5},{8,10},{9,11},{14,12},{15,13},{16,18},{17,... | collective-permute-start | bytes 786440 | tf_op jit(solution)/shard_map/ppermute | solution.py:507
  20.0 0.0 collective-permute-done.first_ref
  20.0 1.4 %collective-permute-done.1.last_ref = f32[264,256]{1,0:T(8,128)S(1)} collective-permute-done((f32[264,256]{1,0:T(8,128)S(1)}, f32[264,256]{1,0:T(8,128)S(1)}, u32[]{:S(2)}, u32[]{:S(2)}) %collective-permute-start.1) | collective-permute-done | bytes 270368 | tf_op jit(solution)/shard_map/ppermute | solution.py:491
  21.4 1.5 %edge.1 = (f32[2,128,256]{2,1,0:T(8,128)S(1)}, f32[2,128,256]{2,1,0:T(8,128)S(1)}, f32[2,128,256]{2,1,0:T(8,128)S(1)}, f32[2,128,256]{2,1,0:T(8,128)S(1)}) custom-call(s32[4]{0:T(128)S(1)} %pad_add_fusion.info_ref, f32[128,8,256]{2,1,0:T(8,128)S(1)} %copy-done, f32[4,8,256]{2,1,0:T(8,128)S(1)} %get-tuple-element.37.flow_ref, ...), custom_call_target="tpu_custom_call" | custom-call | tf_op jit(solution)/shard_map/edge/pallas_call | solution.py:443
  22.9 1.3 %collective-permute-start.6 = (f32[2,128,256]{2,1,0:T(8,128)S(1)}, f32[2,128,256]{2,1,0:T(8,128)S(1)}, u32[]{:S(2)}, u32[]{:S(2)}) collective-permute-start(f32[2,128,256]{2,1,0:T(8,128)S(1)} %get-tuple-element.48), channel_id=1, source_target_pairs={{2,0},{3,1},{4,6},{5,7},{10,8},{11,9},{12,14},{13,15},{18,16},{19,... | collective-permute-start | bytes 786440 | tf_op jit(solution)/shard_map/ppermute | solution.py:507
  24.2 1.3 %collective-permute-start.7 = (f32[2,128,256]{2,1,0:T(8,128)S(1)}, f32[2,128,256]{2,1,0:T(8,128)S(1)}, u32[]{:S(2)}, u32[]{:S(2)}) collective-permute-start(f32[2,128,256]{2,1,0:T(8,128)S(1)} %get-tuple-element.49), channel_id=1, source_target_pairs={{4,0},{5,1},{2,6},{3,7},{12,8},{13,9},{10,14},{11,15},{20,16},{21,... | collective-permute-start | bytes 786440 | tf_op jit(solution)/shard_map/ppermute | solution.py:507
  25.5 0.0 collective-permute-done.3.refs_1_
  25.5 0.0 copy-start.5
  25.6 5.5 %collective-permute-start.8 = (f32[2,128,256]{2,1,0:T(8,128)S(1)}, f32[2,128,256]{2,1,0:T(8,128)S(1)}, u32[]{:S(2)}, u32[]{:S(2)}) collective-permute-start(f32[2,128,256]{2,1,0:T(8,128)S(1)} %get-tuple-element.50), channel_id=1, source_target_pairs={{6,0},{7,1},{0,6},{1,7},{14,8},{15,9},{8,14},{9,15},{22,16},{23,17... | collective-permute-start | bytes 786440 | tf_op jit(solution)/shard_map/ppermute | solution.py:507
  31.7 0.0 copy-done.5
  31.7 0.0 copy-start.3
  31.8 0.0 copy-start.4
  31.8 0.6 copy-done.3
  32.4 0.0 copy-done.4
  32.5 0.0 collective-permute-done.4.refs_2_
  32.5 0.7 collective-permute-start.2
  33.2 0.0 collective-permute-done.5.refs_3_
  33.2 0.0 collective-permute-done.2.other_ref
  33.2 10.1 %collective-permute-done.6.refs_5_ = f32[2,128,256]{2,1,0:T(8,128)S(1)} collective-permute-done((f32[2,128,256]{2,1,0:T(8,128)S(1)}, f32[2,128,256]{2,1,0:T(8,128)S(1)}, u32[]{:S(2)}, u32[]{:S(2)}) %collective-permute-start.6) | collective-permute-done | bytes 262176 | tf_op jit(solution)/shard_map/ppermute | solution.py:507
  43.2 0.0 collective-permute-done.7.refs_6_
  43.2 0.0 collective-permute-done.8.refs_7_
  43.2 0.6 collect.1
  43.9 0.1 collective-permute-start.9
  44.0 0.5 collective-permute-start.10
  44.5 0.7 collective-permute-start.11
  45.2 0.7 collective-permute-done.9.far_own
  45.9 0.9 collective-permute-start.12
  46.7 0.0 collective-permute-done.10.far_other
  46.8 4.0 %prepare.1 = (bf16[1024,512]{1,0:T(8,128)(2,1)S(1)}, bf16[1024,512]{1,0:T(8,128)(2,1)S(1)}, bf16[256,1024]{1,0:T(8,128)(2,1)S(1)}, bf16[256,1024]{1,0:T(8,128)(2...) custom-call(s32[4]{0:T(128)S(1)} %pad_add_fusion.info_ref, ...), custom_call_target="tpu_custom_call" | custom-call | flops 1073741824 | tf_op jit(solution)/shard_map/prepare/pallas_call | solution.py:443
  50.8 0.0 collective-permute-done.11.half_ref
  50.8 0.0 collective-permute-done.12.rest_ref
  50.8 12.3 %region.1 = (f32[128,256]{1,0:T(8,128)S(1)}, f32[128,256]{1,0:T(8,128)S(1)}, f32[128,256]{1,0:T(8,128)S(1)}, f32[128,256]{1,0:T(8,128)S(1)}, f32[128,256]{1,0:T(...) custom-call(s32[4]{0:T(128)S(1)} %pad_add_fusion.info_ref, ...), custom_call_target="tpu_custom_call" | custom-call | tf_op jit(solution)/shard_map/region/pallas_call | solution.py:443
  63.1 12.3 %collective-permute-start.13 = (f32[128,256]{1,0:T(8,128)S(1)}, f32[128,256]{1,0:T(8,128)S(1)}, u32[]{:S(2)}, u32[]{:S(2)}) collective-permute-start(f32[128,256]{1,0:T(8,128)S(1)} %get-tuple-element.61), channel_id=1, source_target_pairs={{0,7},{1,6},{2,5},{3,4},{4,3},{5,2},{6,1},{7,0},{8,15},{9,14},{10,... | collective-permute-start | bytes 393224 | tf_op jit(solution)/shard_map/ppermute | solution.py:579
  75.4 1.4 %collective-permute-start.14 = (f32[128,256]{1,0:T(8,128)S(1)}, f32[128,256]{1,0:T(8,128)S(1)}, u32[]{:S(2)}, u32[]{:S(2)}) collective-permute-start(f32[128,256]{1,0:T(8,128)S(1)} %get-tuple-element.62), channel_id=1, source_target_pairs={{0,6},{1,7},{2,4},{3,5},{4,2},{5,3},{6,0},{7,1},{8,14},{9,15},{10,... | collective-permute-start | bytes 393224 | tf_op jit(solution)/shard_map/ppermute | solution.py:579
  76.8 0.0 collective-permute-start.15
  76.8 2.6 %collective-permute-start.16 = (f32[128,256]{1,0:T(8,128)S(1)}, f32[128,256]{1,0:T(8,128)S(1)}, u32[]{:S(2)}, u32[]{:S(2)}) collective-permute-start(f32[128,256]{1,0:T(8,128)S(1)} %get-tuple-element.64), channel_id=1, source_target_pairs={{0,4},{1,5},{2,6},{3,7},{4,0},{5,1},{6,2},{7,3},{8,12},{9,13},{10,... | collective-permute-start | bytes 393224 | tf_op jit(solution)/shard_map/ppermute | solution.py:579
  79.3 0.9 collective-permute-start.17
  80.3 0.0 collective-permute-done.13.refs_0_
  80.3 10.2 %collective-permute-start.18 = (f32[128,256]{1,0:T(8,128)S(1)}, f32[128,256]{1,0:T(8,128)S(1)}, u32[]{:S(2)}, u32[]{:S(2)}) collective-permute-start(f32[128,256]{1,0:T(8,128)S(1)} %get-tuple-element.66), channel_id=1, source_target_pairs={{0,2},{1,3},{2,0},{3,1},{4,6},{5,7},{6,4},{7,5},{8,10},{9,11},{10,... | collective-permute-start | bytes 393224 | tf_op jit(solution)/shard_map/ppermute | solution.py:579
  90.4 0.0 collective-permute-done.14.refs_1_
  90.5 0.0 collective-permute-start.19
  90.5 5.2 %collective-permute-done.15.refs_2_ = f32[128,256]{1,0:T(8,128)S(1)} collective-permute-done((f32[128,256]{1,0:T(8,128)S(1)}, f32[128,256]{1,0:T(8,128)S(1)}, u32[]{:S(2)}, u32[]{:S(2)}) %collective-permute-start.15) | collective-permute-done | bytes 131104 | tf_op jit(solution)/shard_map/ppermute | solution.py:579
  95.6 2.4 %collective-permute-done.16.refs_3_ = f32[128,256]{1,0:T(8,128)S(1)} collective-permute-done((f32[128,256]{1,0:T(8,128)S(1)}, f32[128,256]{1,0:T(8,128)S(1)}, u32[]{:S(2)}, u32[]{:S(2)}) %collective-permute-start.16) | collective-permute-done | bytes 131104 | tf_op jit(solution)/shard_map/ppermute | solution.py:579
  98.0 0.0 collective-permute-done.17.refs_4_
  98.0 1.3 %collective-permute-done.18.refs_5_ = f32[128,256]{1,0:T(8,128)S(1)} collective-permute-done((f32[128,256]{1,0:T(8,128)S(1)}, f32[128,256]{1,0:T(8,128)S(1)}, u32[]{:S(2)}, u32[]{:S(2)}) %collective-permute-start.18) | collective-permute-done | bytes 131104 | tf_op jit(solution)/shard_map/ppermute | solution.py:579
  99.4 0.0 collective-permute-done.19.refs_6_
  99.4 1.9 %unpack.1 = f32[128,8,256]{2,1,0:T(8,128)} custom-call(s32[4]{0:T(128)S(1)} %pad_add_fusion.info_ref, f32[128,256]{1,0:T(8,128)S(1)} %collective-permute-done.13.refs_0_, f32[128,256]{1,0:T(8,128)S(1)} %collective-permute-done.14.refs_1_, f32[128,256]{1,0:T(8,128)S(1)} %collective-permute-done.15.refs_2_, f32[128,256]{1,0:T(8,128)S(1)} %collective-permute-done.16.refs_3_, ...), custom_call_target="tpu_custom_call" | custom-call | tf_op jit(solution)/shard_map/unpack/pallas_call | solution.py:443
  (3 shorter events, 0.0 us)
Async XLA Ops:
  0.0 0.8 copy-start.1
  0.1 0.7 copy-start.2
  0.8 1.2 %copy-start = (f32[128,8,256]{2,1,0:T(8,128)S(1)}, f32[128,8,256]{2,1,0:T(8,128)}, u32[]{:S(2)}) copy-start(f32[128,8,256]{2,1,0:T(8,128)} %field_ref.3) | copy-start | bytes 3145732
  3.1 16.9 %collective-permute-start = (f32[264,256]{1,0:T(8,128)S(1)}, f32[264,256]{1,0:T(8,128)S(1)}, u32[]{:S(2)}, u32[]{:S(2)}) collective-permute-start(f32[264,256]{1,0:T(8,128)S(1)} %get-tuple-element.40), channel_id=1, source_target_pairs={{8,16},{16,8},{9,17},{17,9},{10,18},{18,10},{11,19},{19,11},{12,20... | collective-permute-start | bytes 811016 | tf_op jit(solution)/shard_map/ppermute | solution.py:491
  3.8 17.6 %collective-permute-start.1 = (f32[264,256]{1,0:T(8,128)S(1)}, f32[264,256]{1,0:T(8,128)S(1)}, u32[]{:S(2)}, u32[]{:S(2)}) collective-permute-start(f32[264,256]{1,0:T(8,128)S(1)} %get-tuple-element.41), channel_id=1, source_target_pairs={{0,8},{16,24},{8,0},{24,16},{1,9},{17,25},{9,1},{25,17},{2,10},{18... | collective-permute-start | bytes 811016 | tf_op jit(solution)/shard_map/ppermute | solution.py:491
  11.7 13.8 %collective-permute-start.3 = (f32[2,128,256]{2,1,0:T(8,128)S(1)}, f32[2,128,256]{2,1,0:T(8,128)S(1)}, u32[]{:S(2)}, u32[]{:S(2)}) collective-permute-start(f32[2,128,256]{2,1,0:T(8,128)S(1)} %get-tuple-element.45), channel_id=1, source_target_pairs={{4,2},{5,3},{2,4},{3,5},{12,10},{13,11},{10,12},{11,13},{20,18},{2... | collective-permute-start | bytes 786440 | tf_op jit(solution)/shard_map/ppermute | solution.py:507
  12.4 20.1 %collective-permute-start.4 = (f32[2,128,256]{2,1,0:T(8,128)S(1)}, f32[2,128,256]{2,1,0:T(8,128)S(1)}, u32[]{:S(2)}, u32[]{:S(2)}) collective-permute-start(f32[2,128,256]{2,1,0:T(8,128)S(1)} %get-tuple-element.46), channel_id=1, source_target_pairs={{6,2},{7,3},{0,4},{1,5},{14,10},{15,11},{8,12},{9,13},{22,18},{23,... | collective-permute-start | bytes 786440 | tf_op jit(solution)/shard_map/ppermute | solution.py:507
  18.6 14.6 %collective-permute-start.5 = (f32[2,128,256]{2,1,0:T(8,128)S(1)}, f32[2,128,256]{2,1,0:T(8,128)S(1)}, u32[]{:S(2)}, u32[]{:S(2)}) collective-permute-start(f32[2,128,256]{2,1,0:T(8,128)S(1)} %get-tuple-element.47), channel_id=1, source_target_pairs={{0,2},{1,3},{6,4},{7,5},{8,10},{9,11},{14,12},{15,13},{16,18},{17,... | collective-permute-start | bytes 786440 | tf_op jit(solution)/shard_map/ppermute | solution.py:507
  22.9 20.3 %collective-permute-start.6 = (f32[2,128,256]{2,1,0:T(8,128)S(1)}, f32[2,128,256]{2,1,0:T(8,128)S(1)}, u32[]{:S(2)}, u32[]{:S(2)}) collective-permute-start(f32[2,128,256]{2,1,0:T(8,128)S(1)} %get-tuple-element.48), channel_id=1, source_target_pairs={{2,0},{3,1},{4,6},{5,7},{10,8},{11,9},{12,14},{13,15},{18,16},{19,... | collective-permute-start | bytes 786440 | tf_op jit(solution)/shard_map/ppermute | solution.py:507
  24.2 19.0 %collective-permute-start.7 = (f32[2,128,256]{2,1,0:T(8,128)S(1)}, f32[2,128,256]{2,1,0:T(8,128)S(1)}, u32[]{:S(2)}, u32[]{:S(2)}) collective-permute-start(f32[2,128,256]{2,1,0:T(8,128)S(1)} %get-tuple-element.49), channel_id=1, source_target_pairs={{4,0},{5,1},{2,6},{3,7},{12,8},{13,9},{10,14},{11,15},{20,16},{21,... | collective-permute-start | bytes 786440 | tf_op jit(solution)/shard_map/ppermute | solution.py:507
  25.5 6.2 %copy-start.5 = (s32[1,512]{1,0:T(1,128)S(1)}, s32[1,512]{1,0:T(1,128)}, u32[]{:S(2)}) copy-start(s32[1,512]{1,0:T(1,128)} %param.10) | copy-start | bytes 6148
  25.6 17.7 %collective-permute-start.8 = (f32[2,128,256]{2,1,0:T(8,128)S(1)}, f32[2,128,256]{2,1,0:T(8,128)S(1)}, u32[]{:S(2)}, u32[]{:S(2)}) collective-permute-start(f32[2,128,256]{2,1,0:T(8,128)S(1)} %get-tuple-element.50), channel_id=1, source_target_pairs={{6,0},{7,1},{0,6},{1,7},{14,8},{15,9},{8,14},{9,15},{22,16},{23,17... | collective-permute-start | bytes 786440 | tf_op jit(solution)/shard_map/ppermute | solution.py:507
  31.7 0.7 copy-start.3
  31.8 0.7 copy-start.4
  32.5 0.7 collective-permute-start.2
  43.9 2.0 %collective-permute-start.9 = (f32[4,128,256]{2,1,0:T(8,128)S(1)}, f32[4,128,256]{2,1,0:T(8,128)S(1)}, u32[]{:S(2)}, u32[]{:S(2)}) collective-permute-start(f32[4,128,256]{2,1,0:T(8,128)S(1)} %get-tuple-element.53.near_other), channel_id=1, source_target_pairs={{0,1},{1,0},{2,3},{3,2},{4,5},{5,4},{6,7},{7,6},{8,9},{9,8},{10,11... | collective-permute-start | bytes 1572872 | tf_op jit(solution)/shard_map/ppermute | solution.py:558
  44.0 2.8 %collective-permute-start.10 = (f32[520,256]{1,0:T(8,128)S(1)}, f32[520,256]{1,0:T(8,128)S(1)}, u32[]{:S(2)}, u32[]{:S(2)}) collective-permute-start(f32[520,256]{1,0:T(8,128)S(1)} %get-tuple-element.52.near_own), channel_id=1, source_target_pairs={{0,1},{1,0},{2,3},{3,2},{4,5},{5,4},{6,7},{7,6},{8,9},{9,8},{10,11... | collective-permute-start | bytes 1597448 | tf_op jit(solution)/shard_map/ppermute | solution.py:560
  44.5 6.3 %collective-permute-start.11 = (f32[520,256]{1,0:T(8,128)S(1)}, f32[520,256]{1,0:T(8,128)S(1)}, u32[]{:S(2)}, u32[]{:S(2)}) collective-permute-start(f32[520,256]{1,0:T(8,128)S(1)} %get-tuple-element.52.near_own), channel_id=1, source_target_pairs={{1,2},{2,1},{3,4},{4,3},{5,6},{6,5},{7,15},{8,16},{9,10},{10,9},{1... | collective-permute-start | bytes 1597448 | tf_op jit(solution)/shard_map/ppermute | solution.py:559
  45.9 4.9 %collective-permute-start.12 = (f32[4,128,256]{2,1,0:T(8,128)S(1)}, f32[4,128,256]{2,1,0:T(8,128)S(1)}, u32[]{:S(2)}, u32[]{:S(2)}) collective-permute-start(f32[4,128,256]{2,1,0:T(8,128)S(1)} %collective-permute-done.9.far_own), channel_id=1, source_target_pairs={{1,2},{2,1},{3,4},{4,3},{5,6},{6,5},{7,15},{8,16},{9,10},{10,9},{1... | collective-permute-start | bytes 1572872 | tf_op jit(solution)/shard_map/ppermute | solution.py:561
  63.1 17.2 %collective-permute-start.13 = (f32[128,256]{1,0:T(8,128)S(1)}, f32[128,256]{1,0:T(8,128)S(1)}, u32[]{:S(2)}, u32[]{:S(2)}) collective-permute-start(f32[128,256]{1,0:T(8,128)S(1)} %get-tuple-element.61), channel_id=1, source_target_pairs={{0,7},{1,6},{2,5},{3,4},{4,3},{5,2},{6,1},{7,0},{8,15},{9,14},{10,... | collective-permute-start | bytes 393224 | tf_op jit(solution)/shard_map/ppermute | solution.py:579
  75.4 15.1 %collective-permute-start.14 = (f32[128,256]{1,0:T(8,128)S(1)}, f32[128,256]{1,0:T(8,128)S(1)}, u32[]{:S(2)}, u32[]{:S(2)}) collective-permute-start(f32[128,256]{1,0:T(8,128)S(1)} %get-tuple-element.62), channel_id=1, source_target_pairs={{0,6},{1,7},{2,4},{3,5},{4,2},{5,3},{6,0},{7,1},{8,14},{9,15},{10,... | collective-permute-start | bytes 393224 | tf_op jit(solution)/shard_map/ppermute | solution.py:579
  76.8 18.8 %collective-permute-start.15 = (f32[128,256]{1,0:T(8,128)S(1)}, f32[128,256]{1,0:T(8,128)S(1)}, u32[]{:S(2)}, u32[]{:S(2)}) collective-permute-start(f32[128,256]{1,0:T(8,128)S(1)} %get-tuple-element.63), channel_id=1, source_target_pairs={{0,5},{1,4},{2,7},{3,6},{4,1},{5,0},{6,3},{7,2},{8,13},{9,12},{10,... | collective-permute-start | bytes 393224 | tf_op jit(solution)/shard_map/ppermute | solution.py:579
  76.8 21.3 %collective-permute-start.16 = (f32[128,256]{1,0:T(8,128)S(1)}, f32[128,256]{1,0:T(8,128)S(1)}, u32[]{:S(2)}, u32[]{:S(2)}) collective-permute-start(f32[128,256]{1,0:T(8,128)S(1)} %get-tuple-element.64), channel_id=1, source_target_pairs={{0,4},{1,5},{2,6},{3,7},{4,0},{5,1},{6,2},{7,3},{8,12},{9,13},{10,... | collective-permute-start | bytes 393224 | tf_op jit(solution)/shard_map/ppermute | solution.py:579
  79.3 18.7 %collective-permute-start.17 = (f32[128,256]{1,0:T(8,128)S(1)}, f32[128,256]{1,0:T(8,128)S(1)}, u32[]{:S(2)}, u32[]{:S(2)}) collective-permute-start(f32[128,256]{1,0:T(8,128)S(1)} %get-tuple-element.65), channel_id=1, source_target_pairs={{0,3},{1,2},{2,1},{3,0},{4,7},{5,6},{6,5},{7,4},{8,11},{9,10},{10,... | collective-permute-start | bytes 393224 | tf_op jit(solution)/shard_map/ppermute | solution.py:579
  80.3 19.1 %collective-permute-start.18 = (f32[128,256]{1,0:T(8,128)S(1)}, f32[128,256]{1,0:T(8,128)S(1)}, u32[]{:S(2)}, u32[]{:S(2)}) collective-permute-start(f32[128,256]{1,0:T(8,128)S(1)} %get-tuple-element.66), channel_id=1, source_target_pairs={{0,2},{1,3},{2,0},{3,1},{4,6},{5,7},{6,4},{7,5},{8,10},{9,11},{10,... | collective-permute-start | bytes 393224 | tf_op jit(solution)/shard_map/ppermute | solution.py:579
  90.5 8.9 %collective-permute-start.19 = (f32[128,256]{1,0:T(8,128)S(1)}, f32[128,256]{1,0:T(8,128)S(1)}, u32[]{:S(2)}, u32[]{:S(2)}) collective-permute-start(f32[128,256]{1,0:T(8,128)S(1)} %get-tuple-element.67), channel_id=1, source_target_pairs={{0,1},{1,0},{2,3},{3,2},{4,5},{5,4},{6,7},{7,6},{8,9},{9,8},{10,11... | collective-permute-start | bytes 393224 | tf_op jit(solution)/shard_map/ppermute | solution.py:579

commit v15 on v14

--- a/solution.py
+++ b/solution.py
@@ -9,7 +9,7 @@
 from jax.sharding import PartitionSpec as P
 
 STEPS = 2
-COARSE = 0.35
+COARSE = 0.3
 DONE = 0.02
 LARGE = 2e4
 PART = 256
@@ -18,25 +18,16 @@
 BF16 = jnp.bfloat16
 
 
-def pack_kernel(info_ref, field_hbm, flow_hbm, emission_hbm, first_ref, second_ref, flow_ref, emission_ref,
-                field_ref, member_ref, sems):
+def pack_kernel(info_ref, field_hbm, flow_hbm, first_ref, second_ref, field_ref, flow_ref, sems):
     members, rows, width = field_ref.shape
     moves = [
-        pltpu.make_async_copy(source, target, sems.at[i])
-        for i, (source, target) in enumerate(
-            ((field_hbm, field_ref), (flow_hbm, flow_ref), (emission_hbm, member_ref))
-        )
+        pltpu.make_async_copy(field_hbm, field_ref, sems.at[0]),
+        pltpu.make_async_copy(flow_hbm, flow_ref, sems.at[1]),
     ]
     for move in moves:
         move.start()
-    for move in moves[1:]:
+    for move in moves:
         move.wait()
-    diagonal = lax.broadcasted_iota(jnp.int32, (members, members), 0) == lax.broadcasted_iota(
-        jnp.int32, (members, members), 1
-    )
-    column = jnp.sum(jnp.where(diagonal, member_ref[...], 0.0), axis=1, keepdims=True)
-    emission_ref[...] = jnp.broadcast_to(column, emission_ref.shape)
-    moves[0].wait()
     even = info_ref[2] == 0
     for place in range(STEPS):
         tail, head = field_ref[:, rows - STEPS + place, :], field_ref[:, place, :]
@@ -73,10 +64,18 @@
     )
 
 
+def emission_column(emission_ref):
+    members = emission_ref.shape[1]
+    diagonal = lax.broadcasted_iota(jnp.int32, (members, members), 0) == lax.broadcasted_iota(
+        jnp.int32, (members, members), 1
+    )
+    return jnp.sum(jnp.where(diagonal, emission_ref[...], 0.0), axis=1, keepdims=True)
+
+
 def inner_kernel(targets, info_ref, field_ref, flow_ref, emission_ref, kept_ref, *refs):
     out_refs, (wide_ref, weight_ref) = refs[:-2], refs[-2:]
     rows = field_ref.shape[1]
-    emission = doubled(emission_ref[...])
+    emission = emission_column(emission_ref)
     for row in range(1, rows - 1):
         weights = weights_of(flow_ref[:, row, :])
         for i, weight in enumerate(weights):
@@ -101,9 +100,8 @@
                 )
 
 
-def end_rows(info_ref, last, field_ref, flow_ref, emission_ref, kept_ref, halo_ref, out_ref):
+def end_rows(info_ref, last, field_ref, flow_ref, emission, kept_ref, halo_ref, out_ref):
     members, rows, width = field_ref.shape
-    emission = doubled(emission_ref[...])
 
     def halo_row(place):
         return halo_ref[pl.ds(place * members, members), :]
@@ -132,12 +130,13 @@
             out_ref[1 - last] = ordered(weights_of(flow_ref[:, near, :]), own, inside, further)
 
 
-def edge_kernel(info_ref, field_ref, flow_ref, emission_ref, kept_ref, first_ref, last_ref, *refs):
+def edge_kernel(info_ref, field_ref, flow_ref, emission_ref, kept_ref, last_ref, first_ref, *refs):
     out_refs, scratch = refs[:-1], refs[-1]
     chips = len(out_refs)
     core = info_ref[1]
+    emission = emission_column(emission_ref)
     for last, halo_ref in enumerate((first_ref, last_ref)):
-        end_rows(info_ref, last, field_ref, flow_ref, emission_ref, kept_ref, halo_ref, scratch)
+        end_rows(info_ref, last, field_ref, flow_ref, emission, kept_ref, halo_ref, scratch)
         for s, out_ref in enumerate(out_refs):
 
             @pl.when(info_ref[0] == (chips - 1 - s if last else s))
@@ -475,22 +474,22 @@
     info = jnp.stack([lane // 2, lane % 2, patch % 2, jnp.int32(chips)]).astype(jnp.int32)
 
     edge = array(STEPS * step + 8, width)
-    place = pl.BlockSpec(memory_space=pltpu.HBM)
-    to_last, to_first, flow, emitted = pl.pallas_call(
+    place = pl.BlockSpec(memory_space=pl.ANY)
+    to_last, to_first = pl.pallas_call(
         pack_kernel,
-        out_shape=[edge, edge, array(*flow_fields.shape), array(step, width // 2)],
-        in_specs=[SMEM] + [place] * 3, out_specs=[VMEM] * 4,
+        out_shape=[edge, edge],
+        in_specs=[SMEM] + [place] * 2, out_specs=[VMEM] * 2,
         scratch_shapes=[
-            pltpu.VMEM((step, rows, width), F32), pltpu.VMEM((1, step), F32), pltpu.SemaphoreType.DMA((3,))
+            pltpu.VMEM((step, rows, width), F32), pltpu.VMEM(flow_fields.shape, F32), pltpu.SemaphoreType.DMA((2,))
         ],
-        compiler_params=pltpu.CompilerParams(vmem_limit_bytes=32 * 1024 * 1024), name="pack",
-    )(info, init_field, flow_fields, emission[None, :])
+        compiler_params=pltpu.CompilerParams(vmem_limit_bytes=60 * 1024 * 1024), name="pack",
+    )(info, init_field, flow_fields)
 
     def swap(message, start):
         lower = range(start, patches - 1, 2)
         return lax.ppermute(message, "patch", [(p, p + 1) for p in lower] + [(p + 1, p) for p in lower])
 
-    halo_first, halo_last = swap(to_first, 1), swap(to_last, 0)
+    halo_last, halo_first = swap(to_last, 0), swap(to_first, 1)
 
     mine = jnp.concatenate(
         [
@@ -514,14 +513,14 @@
     single = all(len({source for source, _ in hops}) == len(hops) for hops in mirrored)
     targets = mirrored if single else turning
     pair = array(2, step, width)
-    args = [info, init_field, flow, emitted]
+    args = [info, init_field, flow_fields, emission[None, :]]
     kept, *inner = call(
         functools.partial(inner_kernel, targets), "inner", [array(4, step, width)] + [pair] * chips, args,
         [pltpu.VMEM((rows, step, width), F32), pltpu.VMEM((rows, 8, width), F32)], limit=32,
     )
     got_inner = [inner[0]] + [between(inner[s], targets[s]) for s in range(1, chips)]
     outer = call(
-        edge_kernel, "edge", [pair] * chips, args + [kept, halo_first, halo_last],
+        edge_kernel, "edge", [pair] * chips, args + [kept, halo_last, halo_first],
         [pltpu.VMEM((2, step, width), F32)], limit=32,
     )
     got_outer = [outer[0]] + [

time: 101 us -> 101 us (level)
  the two profiles are of different devices: /device:TPU:0 before, /device:TPU:2 now
where the time goes in v15:
time: 101 us; the launch traced here: 99 us
  starting transfers between devices  45.9 us (45%)
  Pallas kernels  25.7 us (25%)
  waiting for transfers between devices  25.1 us (25%)
    pallas_call x6, Pallas kernels, call(): pl.pallas_call(kernel, out_shape=out_shape, in_specs=[SMEM] + [VMEM] * (l...  22.6 us
    ppermute x6, starting transfers between devices, between(): lax.ppermute(message, 'member', [(2 * a + core, 2 * b + core) for a, b in...  16 us
    ppermute x7, starting transfers between devices, swapped(): lax.ppermute(analysed[x], 'member', [(i, i ^ x) for i in range(lanes)])  15.4 us
    ppermute x7, waiting for transfers between devices, swapped(): lax.ppermute(analysed[x], 'member', [(i, i ^ x) for i in range(lanes)])  8.94 us
    ppermute x1, waiting for transfers between devices, per_device(): got_rest = lax.ppermute(far_own, axes, borders)  5.62 us
    ppermute x1, waiting for transfers between devices, per_device(): lax.ppermute(mine, axes, [(p * lanes + i, p * lanes + lanes - 1 - i) for...  5.08 us
    ppermute x2, starting transfers between devices, swap(): lax.ppermute(message, 'patch', [(p, p + 1) for p in lower] + [(p + 1, p)...  5.05 us
    ppermute x1, starting transfers between devices, per_device(): got_rest = lax.ppermute(far_own, axes, borders)  4.88 us
  transfers between devices with their start and end apart: 20, of which 7 were waited for; matrix products, arithmetic and copies ran while one was open for 0% of the time, Pallas kernels for 9%

profile of v15, /device:TPU:2, one launch (start us, length us, event | category | flops | bytes accessed | tf_op | source)
XLA Modules:
  0.0 99.0 jit_solution(2029073341340645212)
XLA Ops:
  0.0 0.0 copy-start
  0.0 0.6 pad_add_fusion.info_ref
  0.6 0.0 copy-start.1
  0.6 3.1 %pack.1 = (f32[264,256]{1,0:T(8,128)}, f32[264,256]{1,0:T(8,128)}) custom-call(s32[4]{0:T(128)} %pad_add_fusion.info_ref, f32[128,8,256]{2,1,0:T(8,128)} %field_ref.3, f32[4,8,256]{2,1,0:T(8,128)} %flow_ref.3), custom_call_target="tpu_custom_call" | custom-call | tf_op jit(solution)/shard_map/pack/pallas_call | solution.py:478
  3.7 0.1 collective-permute-start
  3.8 0.0 copy-start.2
  3.8 0.0 copy-start.3
  3.8 5.0 %collective-permute-start.1 = (f32[264,256]{1,0:T(8,128)}, f32[264,256]{1,0:T(8,128)S(1)}, u32[]{:S(2)}, u32[]{:S(2)}) collective-permute-start(f32[264,256]{1,0:T(8,128)} %get-tuple-element.37), channel_id=1, source_target_pairs={{8,16},{16,8},{9,17},{17,9},{10,18},{18,10},{11,19},{19,11},{12,20... | collective-permute-start | bytes 811016 | tf_op jit(solution)/shard_map/ppermute | solution.py:490
  8.8 0.0 copy-done
  8.8 0.0 copy-done.1
  8.8 0.0 copy-done.2
  8.8 0.0 copy-done.3
  8.8 2.1 %inner.1 = (f32[4,128,256]{2,1,0:T(8,128)S(1)}, f32[2,128,256]{2,1,0:T(8,128)S(1)}, f32[2,128,256]{2,1,0:T(8,128)S(1)}, f32[2,128,256]{2,1,0:T(8,128)S(1)}, f32[2,128,256]{2,1,0:T(8,128)S(1)}) custom-call(s32[4]{0:T(128)S(1)} %copy-done.2, f32[128,8,256]{2,1,0:T(8,128)S(1)} %copy-done, f32[4,8,256]{2,1,0:T(8,128)S(1)} %copy-done.1, f32[1,128]{1,0:T(1,128)S(1)} %bitcast.5), custom_call_target="tpu_custom_call" | custom-call | tf_op jit(solution)/shard_map/inner/pallas_call | solution.py:442
  11.0 0.7 collective-permute-start.3
  11.7 6.2 %collective-permute-start.4 = (f32[2,128,256]{2,1,0:T(8,128)S(1)}, f32[2,128,256]{2,1,0:T(8,128)S(1)}, u32[]{:S(2)}, u32[]{:S(2)}) collective-permute-start(f32[2,128,256]{2,1,0:T(8,128)S(1)} %get-tuple-element.42), channel_id=1, source_target_pairs={{6,2},{7,3},{0,4},{1,5},{14,10},{15,11},{8,12},{9,13},{22,18},{23,... | collective-permute-start | bytes 786440 | tf_op jit(solution)/shard_map/ppermute | solution.py:506
  17.9 1.4 %collective-permute-start.5 = (f32[2,128,256]{2,1,0:T(8,128)S(1)}, f32[2,128,256]{2,1,0:T(8,128)S(1)}, u32[]{:S(2)}, u32[]{:S(2)}) collective-permute-start(f32[2,128,256]{2,1,0:T(8,128)S(1)} %get-tuple-element.43), channel_id=1, source_target_pairs={{0,2},{1,3},{6,4},{7,5},{8,10},{9,11},{14,12},{15,13},{16,18},{17,... | collective-permute-start | bytes 786440 | tf_op jit(solution)/shard_map/ppermute | solution.py:506
  19.3 0.0 collective-permute-done.last_ref
  19.3 0.0 collective-permute-done.1.first_ref
  19.3 2.3 %edge.1 = (f32[2,128,256]{2,1,0:T(8,128)S(1)}, f32[2,128,256]{2,1,0:T(8,128)}, f32[2,128,256]{2,1,0:T(8,128)S(1)}, f32[2,128,256]{2,1,0:T(8,128)S(1)}) custom-call(s32[4]{0:T(128)S(1)} %copy-done.2, f32[128,8,256]{2,1,0:T(8,128)S(1)} %copy-done, f32[4,8,256]{2,1,0:T(8,128)S(1)} %copy-done.1, f32[1,128]{1,0:T(1,128)S(1)} %bitcast.6, ...), custom_call_target="tpu_custom_call" | custom-call | tf_op jit(solution)/shard_map/edge/pallas_call | solution.py:442
  21.6 1.3 %collective-permute-start.6 = (f32[2,128,256]{2,1,0:T(8,128)}, f32[2,128,256]{2,1,0:T(8,128)S(1)}, u32[]{:S(2)}, u32[]{:S(2)}) collective-permute-start(f32[2,128,256]{2,1,0:T(8,128)} %get-tuple-element.44), channel_id=1, source_target_pairs={{2,0},{3,1},{4,6},{5,7},{10,8},{11,9},{12,14},{13,15},{18,16},{19,... | collective-permute-start | bytes 786440 | tf_op jit(solution)/shard_map/ppermute | solution.py:506
  22.9 1.3 %collective-permute-start.7 = (f32[2,128,256]{2,1,0:T(8,128)S(1)}, f32[2,128,256]{2,1,0:T(8,128)S(1)}, u32[]{:S(2)}, u32[]{:S(2)}) collective-permute-start(f32[2,128,256]{2,1,0:T(8,128)S(1)} %get-tuple-element.45), channel_id=1, source_target_pairs={{4,0},{5,1},{2,6},{3,7},{12,8},{13,9},{10,14},{11,15},{20,16},{21,... | collective-permute-start | bytes 786440 | tf_op jit(solution)/shard_map/ppermute | solution.py:506
  24.2 0.0 collective-permute-done.3.refs_1_
  24.2 0.0 copy-start.6
  24.2 5.2 %collective-permute-start.8 = (f32[2,128,256]{2,1,0:T(8,128)S(1)}, f32[2,128,256]{2,1,0:T(8,128)S(1)}, u32[]{:S(2)}, u32[]{:S(2)}) collective-permute-start(f32[2,128,256]{2,1,0:T(8,128)S(1)} %get-tuple-element.46), channel_id=1, source_target_pairs={{6,0},{7,1},{0,6},{1,7},{14,8},{15,9},{8,14},{9,15},{22,16},{23,17... | collective-permute-start | bytes 786440 | tf_op jit(solution)/shard_map/ppermute | solution.py:506
  30.1 0.0 copy-done.6
  30.1 0.0 copy-start.4
  30.1 0.0 copy-start.5
  30.1 0.6 copy-done.4
  30.8 0.0 copy-done.5
  30.8 0.0 collective-permute-done.4.refs_2_
  30.8 1.9 %collective-permute-start.2 = (f32[8,512]{1,0:T(8,128)S(1)}, f32[8,512]{1,0:T(8,128)S(1)}, u32[]{:S(2)}, u32[]{:S(2)}) collective-permute-start(f32[8,512]{1,0:T(8,128)S(1)} %concatenate.3.mine_ref), channel_id=1, source_target_pairs={{8,15},{9,14},{10,13},{11,12},{12,11},{13,10},{14,9},{15,8},{24,31... | collective-permute-start | bytes 49160 | tf_op jit(solution)/shard_map/ppermute | solution.py:532
  32.8 0.0 collective-permute-done.5.refs_3_
  32.8 5.1 %collective-permute-done.2.other_ref = f32[8,512]{1,0:T(8,128)S(1)} collective-permute-done((f32[8,512]{1,0:T(8,128)S(1)}, f32[8,512]{1,0:T(8,128)S(1)}, u32[]{:S(2)}, u32[]{:S(2)}) %collective-permute-start.2) | collective-permute-done | bytes 16416 | tf_op jit(solution)/shard_map/ppermute | solution.py:532
  37.8 4.4 %collective-permute-done.6.refs_5_ = f32[2,128,256]{2,1,0:T(8,128)S(1)} collective-permute-done((f32[2,128,256]{2,1,0:T(8,128)}, f32[2,128,256]{2,1,0:T(8,128)S(1)}, u32[]{:S(2)}, u32[]{:S(2)}) %collective-permute-start.6) | collective-permute-done | bytes 262176 | tf_op jit(solution)/shard_map/ppermute | solution.py:506
  42.2 0.0 collective-permute-done.7.refs_6_
  42.2 0.0 collective-permute-done.8.refs_7_
  42.2 0.6 collect.1
  42.9 0.1 collective-permute-start.9
  43.0 0.5 collective-permute-start.10
  43.5 2.0 %collective-permute-start.11 = (f32[520,256]{1,0:T(8,128)S(1)}, f32[520,256]{1,0:T(8,128)S(1)}, u32[]{:S(2)}, u32[]{:S(2)}) collective-permute-start(f32[520,256]{1,0:T(8,128)S(1)} %get-tuple-element.48.near_own), channel_id=1, source_target_pairs={{1,2},{2,1},{3,4},{4,3},{5,6},{6,5},{7,15},{8,16},{9,10},{10,9},{1... | collective-permute-start | bytes 1597448 | tf_op jit(solution)/shard_map/ppermute | solution.py:558
  45.5 0.0 collective-permute-done.9.far_own
  45.5 4.9 %collective-permute-start.12 = (f32[4,128,256]{2,1,0:T(8,128)S(1)}, f32[4,128,256]{2,1,0:T(8,128)S(1)}, u32[]{:S(2)}, u32[]{:S(2)}) collective-permute-start(f32[4,128,256]{2,1,0:T(8,128)S(1)} %collective-permute-done.9.far_own), channel_id=1, source_target_pairs={{1,2},{2,1},{3,4},{4,3},{5,6},{6,5},{7,15},{8,16},{9,10},{10,9},{1... | collective-permute-start | bytes 1572872 | tf_op jit(solution)/shard_map/ppermute | solution.py:560
  50.4 0.0 collective-permute-done.10.far_other
  50.4 4.0 %prepare.1 = (bf16[1024,512]{1,0:T(8,128)(2,1)S(1)}, bf16[1024,512]{1,0:T(8,128)(2,1)S(1)}, bf16[256,1024]{1,0:T(8,128)(2,1)S(1)}, bf16[256,1024]{1,0:T(8,128)(2...) custom-call(s32[4]{0:T(128)S(1)} %copy-done.2, ...), custom_call_target="tpu_custom_call" | custom-call | flops 1073741824 | tf_op jit(solution)/shard_map/prepare/pallas_call | solution.py:442
  54.4 1.1 %collective-permute-done.11.half_ref = f32[520,256]{1,0:T(8,128)S(1)} collective-permute-done((f32[520,256]{1,0:T(8,128)S(1)}, f32[520,256]{1,0:T(8,128)S(1)}, u32[]{:S(2)}, u32[]{:S(2)}) %collective-permute-start.11) | collective-permute-done | bytes 532512 | tf_op jit(solution)/shard_map/ppermute | solution.py:558
  55.5 5.6 %collective-permute-done.12.rest_ref = f32[4,128,256]{2,1,0:T(8,128)S(1)} collective-permute-done((f32[4,128,256]{2,1,0:T(8,128)S(1)}, f32[4,128,256]{2,1,0:T(8,128)S(1)}, u32[]{:S(2)}, u32[]{:S(2)}) %collective-permute-start.12) | collective-permute-done | bytes 524320 | tf_op jit(solution)/shard_map/ppermute | solution.py:560
  61.1 11.7 %region.1 = (f32[128,256]{1,0:T(8,128)S(1)}, f32[128,256]{1,0:T(8,128)S(1)}, f32[128,256]{1,0:T(8,128)S(1)}, f32[128,256]{1,0:T(8,128)S(1)}, f32[128,256]{1,0:T(...) custom-call(s32[4]{0:T(128)S(1)} %copy-done.2, ...), custom_call_target="tpu_custom_call" | custom-call | tf_op jit(solution)/shard_map/region/pallas_call | solution.py:442
  72.8 2.2 %collective-permute-start.13 = (f32[128,256]{1,0:T(8,128)S(1)}, f32[128,256]{1,0:T(8,128)S(1)}, u32[]{:S(2)}, u32[]{:S(2)}) collective-permute-start(f32[128,256]{1,0:T(8,128)S(1)} %get-tuple-element.57), channel_id=1, source_target_pairs={{0,7},{1,6},{2,5},{3,4},{4,3},{5,2},{6,1},{7,0},{8,15},{9,14},{10,... | collective-permute-start | bytes 393224 | tf_op jit(solution)/shard_map/ppermute | solution.py:578
  74.9 0.0 collective-permute-start.14
  74.9 0.0 collective-permute-start.15
  74.9 4.1 %collective-permute-start.16 = (f32[128,256]{1,0:T(8,128)S(1)}, f32[128,256]{1,0:T(8,128)S(1)}, u32[]{:S(2)}, u32[]{:S(2)}) collective-permute-start(f32[128,256]{1,0:T(8,128)S(1)} %get-tuple-element.60), channel_id=1, source_target_pairs={{0,4},{1,5},{2,6},{3,7},{4,0},{5,1},{6,2},{7,3},{8,12},{9,13},{10,... | collective-permute-start | bytes 393224 | tf_op jit(solution)/shard_map/ppermute | solution.py:578
  79.0 0.0 collective-permute-start.17
  79.1 0.0 collective-permute-done.13.refs_0_
  79.1 9.2 %collective-permute-start.18 = (f32[128,256]{1,0:T(8,128)S(1)}, f32[128,256]{1,0:T(8,128)S(1)}, u32[]{:S(2)}, u32[]{:S(2)}) collective-permute-start(f32[128,256]{1,0:T(8,128)S(1)} %get-tuple-element.62), channel_id=1, source_target_pairs={{0,2},{1,3},{2,0},{3,1},{4,6},{5,7},{6,4},{7,5},{8,10},{9,11},{10,... | collective-permute-start | bytes 393224 | tf_op jit(solution)/shard_map/ppermute | solution.py:578
  88.3 0.0 collective-permute-done.14.refs_1_
  88.3 0.0 collective-permute-start.19
  88.3 5.6 %collective-permute-done.15.refs_2_ = f32[128,256]{1,0:T(8,128)S(1)} collective-permute-done((f32[128,256]{1,0:T(8,128)S(1)}, f32[128,256]{1,0:T(8,128)S(1)}, u32[]{:S(2)}, u32[]{:S(2)}) %collective-permute-start.15) | collective-permute-done | bytes 131104 | tf_op jit(solution)/shard_map/ppermute | solution.py:578
  93.9 2.6 %collective-permute-done.16.refs_3_ = f32[128,256]{1,0:T(8,128)S(1)} collective-permute-done((f32[128,256]{1,0:T(8,128)S(1)}, f32[128,256]{1,0:T(8,128)S(1)}, u32[]{:S(2)}, u32[]{:S(2)}) %collective-permute-start.16) | collective-permute-done | bytes 131104 | tf_op jit(solution)/shard_map/ppermute | solution.py:578
  96.5 0.0 collective-permute-done.17.refs_4_
  96.5 0.6 collective-permute-done.18.refs_5_
  97.1 0.0 collective-permute-done.19.refs_6_
  97.1 1.9 %unpack.1 = f32[128,8,256]{2,1,0:T(8,128)} custom-call(s32[4]{0:T(128)S(1)} %copy-done.2, f32[128,256]{1,0:T(8,128)S(1)} %collective-permute-done.13.refs_0_, f32[128,256]{1,0:T(8,128)S(1)} %collective-permute-done.14.refs_1_, f32[128,256]{1,0:T(8,128)S(1)} %collective-permute-done.15.refs_2_, f32[128,256]{1,0:T(8,128)S(1)} %collective-permute-done.16.refs_3_, ...), custom_call_target="tpu_custom_call" | custom-call | tf_op jit(solution)/shard_map/unpack/pallas_call | solution.py:442
  (3 shorter events, 0.0 us)
Async XLA Ops:
  0.0 8.8 %copy-start = (f32[128,8,256]{2,1,0:T(8,128)S(1)}, f32[128,8,256]{2,1,0:T(8,128)}, u32[]{:S(2)}) copy-start(f32[128,8,256]{2,1,0:T(8,128)} %field_ref.3) | copy-start | bytes 3145732
  0.6 8.2 %copy-start.1 = (f32[4,8,256]{2,1,0:T(8,128)S(1)}, f32[4,8,256]{2,1,0:T(8,128)}, u32[]{:S(2)}) copy-start(f32[4,8,256]{2,1,0:T(8,128)} %flow_ref.3) | copy-start | bytes 98308
  3.7 15.6 %collective-permute-start = (f32[264,256]{1,0:T(8,128)}, f32[264,256]{1,0:T(8,128)S(1)}, u32[]{:S(2)}, u32[]{:S(2)}) collective-permute-start(f32[264,256]{1,0:T(8,128)} %get-tuple-element.36), channel_id=1, source_target_pairs={{0,8},{16,24},{8,0},{24,16},{1,9},{17,25},{9,1},{25,17},{2,10},{18... | collective-permute-start | bytes 811016 | tf_op jit(solution)/shard_map/ppermute | solution.py:490
  3.8 5.0 %copy-start.2 = (s32[4]{0:T(128)S(1)}, s32[4]{0:T(128)}, u32[]{:S(2)}) copy-start(s32[4]{0:T(128)} %pad_add_fusion.info_ref) | copy-start | bytes 52
  3.8 5.0 %copy-start.3 = (f32[128]{0:T(128)S(1)}, f32[128]{0:T(128)}, u32[]{:S(2)}) copy-start(f32[128]{0:T(128)} %param.9) | copy-start | bytes 1540
  3.8 15.5 %collective-permute-start.1 = (f32[264,256]{1,0:T(8,128)}, f32[264,256]{1,0:T(8,128)S(1)}, u32[]{:S(2)}, u32[]{:S(2)}) collective-permute-start(f32[264,256]{1,0:T(8,128)} %get-tuple-element.37), channel_id=1, source_target_pairs={{8,16},{16,8},{9,17},{17,9},{10,18},{18,10},{11,19},{19,11},{12,20... | collective-permute-start | bytes 811016 | tf_op jit(solution)/shard_map/ppermute | solution.py:490
  11.0 13.2 %collective-permute-start.3 = (f32[2,128,256]{2,1,0:T(8,128)S(1)}, f32[2,128,256]{2,1,0:T(8,128)S(1)}, u32[]{:S(2)}, u32[]{:S(2)}) collective-permute-start(f32[2,128,256]{2,1,0:T(8,128)S(1)} %get-tuple-element.41), channel_id=1, source_target_pairs={{4,2},{5,3},{2,4},{3,5},{12,10},{13,11},{10,12},{11,13},{20,18},{2... | collective-permute-start | bytes 786440 | tf_op jit(solution)/shard_map/ppermute | solution.py:506
  11.7 19.2 %collective-permute-start.4 = (f32[2,128,256]{2,1,0:T(8,128)S(1)}, f32[2,128,256]{2,1,0:T(8,128)S(1)}, u32[]{:S(2)}, u32[]{:S(2)}) collective-permute-start(f32[2,128,256]{2,1,0:T(8,128)S(1)} %get-tuple-element.42), channel_id=1, source_target_pairs={{6,2},{7,3},{0,4},{1,5},{14,10},{15,11},{8,12},{9,13},{22,18},{23,... | collective-permute-start | bytes 786440 | tf_op jit(solution)/shard_map/ppermute | solution.py:506
  17.9 14.9 %collective-permute-start.5 = (f32[2,128,256]{2,1,0:T(8,128)S(1)}, f32[2,128,256]{2,1,0:T(8,128)S(1)}, u32[]{:S(2)}, u32[]{:S(2)}) collective-permute-start(f32[2,128,256]{2,1,0:T(8,128)S(1)} %get-tuple-element.43), channel_id=1, source_target_pairs={{0,2},{1,3},{6,4},{7,5},{8,10},{9,11},{14,12},{15,13},{16,18},{17,... | collective-permute-start | bytes 786440 | tf_op jit(solution)/shard_map/ppermute | solution.py:506
  21.6 20.6 %collective-permute-start.6 = (f32[2,128,256]{2,1,0:T(8,128)}, f32[2,128,256]{2,1,0:T(8,128)S(1)}, u32[]{:S(2)}, u32[]{:S(2)}) collective-permute-start(f32[2,128,256]{2,1,0:T(8,128)} %get-tuple-element.44), channel_id=1, source_target_pairs={{2,0},{3,1},{4,6},{5,7},{10,8},{11,9},{12,14},{13,15},{18,16},{19,... | collective-permute-start | bytes 786440 | tf_op jit(solution)/shard_map/ppermute | solution.py:506
  22.9 19.3 %collective-permute-start.7 = (f32[2,128,256]{2,1,0:T(8,128)S(1)}, f32[2,128,256]{2,1,0:T(8,128)S(1)}, u32[]{:S(2)}, u32[]{:S(2)}) collective-permute-start(f32[2,128,256]{2,1,0:T(8,128)S(1)} %get-tuple-element.45), channel_id=1, source_target_pairs={{4,0},{5,1},{2,6},{3,7},{12,8},{13,9},{10,14},{11,15},{20,16},{21,... | collective-permute-start | bytes 786440 | tf_op jit(solution)/shard_map/ppermute | solution.py:506
  24.2 5.8 %copy-start.6 = (s32[1,512]{1,0:T(1,128)S(1)}, s32[1,512]{1,0:T(1,128)}, u32[]{:S(2)}) copy-start(s32[1,512]{1,0:T(1,128)} %param.10) | copy-start | bytes 6148
  24.2 18.0 %collective-permute-start.8 = (f32[2,128,256]{2,1,0:T(8,128)S(1)}, f32[2,128,256]{2,1,0:T(8,128)S(1)}, u32[]{:S(2)}, u32[]{:S(2)}) collective-permute-start(f32[2,128,256]{2,1,0:T(8,128)S(1)} %get-tuple-element.46), channel_id=1, source_target_pairs={{6,0},{7,1},{0,6},{1,7},{14,8},{15,9},{8,14},{9,15},{22,16},{23,17... | collective-permute-start | bytes 786440 | tf_op jit(solution)/shard_map/ppermute | solution.py:506
  30.1 0.7 copy-start.4
  30.1 0.7 copy-start.5
  30.8 7.0 %collective-permute-start.2 = (f32[8,512]{1,0:T(8,128)S(1)}, f32[8,512]{1,0:T(8,128)S(1)}, u32[]{:S(2)}, u32[]{:S(2)}) collective-permute-start(f32[8,512]{1,0:T(8,128)S(1)} %concatenate.3.mine_ref), channel_id=1, source_target_pairs={{8,15},{9,14},{10,13},{11,12},{12,11},{13,10},{14,9},{15,8},{24,31... | collective-permute-start | bytes 49160 | tf_op jit(solution)/shard_map/ppermute | solution.py:532
  42.9 2.6 %collective-permute-start.9 = (f32[4,128,256]{2,1,0:T(8,128)S(1)}, f32[4,128,256]{2,1,0:T(8,128)S(1)}, u32[]{:S(2)}, u32[]{:S(2)}) collective-permute-start(f32[4,128,256]{2,1,0:T(8,128)S(1)} %get-tuple-element.49.near_other), channel_id=1, source_target_pairs={{0,1},{1,0},{2,3},{3,2},{4,5},{5,4},{6,7},{7,6},{8,9},{9,8},{10,11... | collective-permute-start | bytes 1572872 | tf_op jit(solution)/shard_map/ppermute | solution.py:557
  43.0 7.4 %collective-permute-start.10 = (f32[520,256]{1,0:T(8,128)S(1)}, f32[520,256]{1,0:T(8,128)S(1)}, u32[]{:S(2)}, u32[]{:S(2)}) collective-permute-start(f32[520,256]{1,0:T(8,128)S(1)} %get-tuple-element.48.near_own), channel_id=1, source_target_pairs={{0,1},{1,0},{2,3},{3,2},{4,5},{5,4},{6,7},{7,6},{8,9},{9,8},{10,11... | collective-permute-start | bytes 1597448 | tf_op jit(solution)/shard_map/ppermute | solution.py:559
  43.5 12.0 %collective-permute-start.11 = (f32[520,256]{1,0:T(8,128)S(1)}, f32[520,256]{1,0:T(8,128)S(1)}, u32[]{:S(2)}, u32[]{:S(2)}) collective-permute-start(f32[520,256]{1,0:T(8,128)S(1)} %get-tuple-element.48.near_own), channel_id=1, source_target_pairs={{1,2},{2,1},{3,4},{4,3},{5,6},{6,5},{7,15},{8,16},{9,10},{10,9},{1... | collective-permute-start | bytes 1597448 | tf_op jit(solution)/shard_map/ppermute | solution.py:558
  45.5 15.6 %collective-permute-start.12 = (f32[4,128,256]{2,1,0:T(8,128)S(1)}, f32[4,128,256]{2,1,0:T(8,128)S(1)}, u32[]{:S(2)}, u32[]{:S(2)}) collective-permute-start(f32[4,128,256]{2,1,0:T(8,128)S(1)} %collective-permute-done.9.far_own), channel_id=1, source_target_pairs={{1,2},{2,1},{3,4},{4,3},{5,6},{6,5},{7,15},{8,16},{9,10},{10,9},{1... | collective-permute-start | bytes 1572872 | tf_op jit(solution)/shard_map/ppermute | solution.py:560
  72.8 6.3 %collective-permute-start.13 = (f32[128,256]{1,0:T(8,128)S(1)}, f32[128,256]{1,0:T(8,128)S(1)}, u32[]{:S(2)}, u32[]{:S(2)}) collective-permute-start(f32[128,256]{1,0:T(8,128)S(1)} %get-tuple-element.57), channel_id=1, source_target_pairs={{0,7},{1,6},{2,5},{3,4},{4,3},{5,2},{6,1},{7,0},{8,15},{9,14},{10,... | collective-permute-start | bytes 393224 | tf_op jit(solution)/shard_map/ppermute | solution.py:578
  74.9 13.3 %collective-permute-start.14 = (f32[128,256]{1,0:T(8,128)S(1)}, f32[128,256]{1,0:T(8,128)S(1)}, u32[]{:S(2)}, u32[]{:S(2)}) collective-permute-start(f32[128,256]{1,0:T(8,128)S(1)} %get-tuple-element.58), channel_id=1, source_target_pairs={{0,6},{1,7},{2,4},{3,5},{4,2},{5,3},{6,0},{7,1},{8,14},{9,15},{10,... | collective-permute-start | bytes 393224 | tf_op jit(solution)/shard_map/ppermute | solution.py:578
  74.9 19.0 %collective-permute-start.15 = (f32[128,256]{1,0:T(8,128)S(1)}, f32[128,256]{1,0:T(8,128)S(1)}, u32[]{:S(2)}, u32[]{:S(2)}) collective-permute-start(f32[128,256]{1,0:T(8,128)S(1)} %get-tuple-element.59), channel_id=1, source_target_pairs={{0,5},{1,4},{2,7},{3,6},{4,1},{5,0},{6,3},{7,2},{8,13},{9,12},{10,... | collective-permute-start | bytes 393224 | tf_op jit(solution)/shard_map/ppermute | solution.py:578
  74.9 21.6 %collective-permute-start.16 = (f32[128,256]{1,0:T(8,128)S(1)}, f32[128,256]{1,0:T(8,128)S(1)}, u32[]{:S(2)}, u32[]{:S(2)}) collective-permute-start(f32[128,256]{1,0:T(8,128)S(1)} %get-tuple-element.60), channel_id=1, source_target_pairs={{0,4},{1,5},{2,6},{3,7},{4,0},{5,1},{6,2},{7,3},{8,12},{9,13},{10,... | collective-permute-start | bytes 393224 | tf_op jit(solution)/shard_map/ppermute | solution.py:578
  79.0 17.5 %collective-permute-start.17 = (f32[128,256]{1,0:T(8,128)S(1)}, f32[128,256]{1,0:T(8,128)S(1)}, u32[]{:S(2)}, u32[]{:S(2)}) collective-permute-start(f32[128,256]{1,0:T(8,128)S(1)} %get-tuple-element.61), channel_id=1, source_target_pairs={{0,3},{1,2},{2,1},{3,0},{4,7},{5,6},{6,5},{7,4},{8,11},{9,10},{10,... | collective-permute-start | bytes 393224 | tf_op jit(solution)/shard_map/ppermute | solution.py:578
  79.1 18.0 %collective-permute-start.18 = (f32[128,256]{1,0:T(8,128)S(1)}, f32[128,256]{1,0:T(8,128)S(1)}, u32[]{:S(2)}, u32[]{:S(2)}) collective-permute-start(f32[128,256]{1,0:T(8,128)S(1)} %get-tuple-element.62), channel_id=1, source_target_pairs={{0,2},{1,3},{2,0},{3,1},{4,6},{5,7},{6,4},{7,5},{8,10},{9,11},{10,... | collective-permute-start | bytes 393224 | tf_op jit(solution)/shard_map/ppermute | solution.py:578
  88.3 8.9 %collective-permute-start.19 = (f32[128,256]{1,0:T(8,128)S(1)}, f32[128,256]{1,0:T(8,128)S(1)}, u32[]{:S(2)}, u32[]{:S(2)}) collective-permute-start(f32[128,256]{1,0:T(8,128)S(1)} %get-tuple-element.63), channel_id=1, source_target_pairs={{0,1},{1,0},{2,3},{3,2},{4,5},{5,4},{6,7},{7,6},{8,9},{9,8},{10,11... | collective-permute-start | bytes 393224 | tf_op jit(solution)/shard_map/ppermute | solution.py:578

commit v16 on v14

--- a/solution.py
+++ b/solution.py
@@ -18,25 +18,13 @@
 BF16 = jnp.bfloat16
 
 
-def pack_kernel(info_ref, field_hbm, flow_hbm, emission_hbm, first_ref, second_ref, flow_ref, emission_ref,
-                field_ref, member_ref, sems):
+def pack_kernel(info_ref, field_ref, flow_ref, member_ref, first_ref, second_ref, emission_ref):
     members, rows, width = field_ref.shape
-    moves = [
-        pltpu.make_async_copy(source, target, sems.at[i])
-        for i, (source, target) in enumerate(
-            ((field_hbm, field_ref), (flow_hbm, flow_ref), (emission_hbm, member_ref))
-        )
-    ]
-    for move in moves:
-        move.start()
-    for move in moves[1:]:
-        move.wait()
     diagonal = lax.broadcasted_iota(jnp.int32, (members, members), 0) == lax.broadcasted_iota(
         jnp.int32, (members, members), 1
     )
     column = jnp.sum(jnp.where(diagonal, member_ref[...], 0.0), axis=1, keepdims=True)
     emission_ref[...] = jnp.broadcast_to(column, emission_ref.shape)
-    moves[0].wait()
     even = info_ref[2] == 0
     for place in range(STEPS):
         tail, head = field_ref[:, rows - STEPS + place, :], field_ref[:, place, :]
@@ -132,7 +120,7 @@
             out_ref[1 - last] = ordered(weights_of(flow_ref[:, near, :]), own, inside, further)
 
 
-def edge_kernel(info_ref, field_ref, flow_ref, emission_ref, kept_ref, first_ref, last_ref, *refs):
+def edge_kernel(info_ref, field_ref, flow_ref, emission_ref, kept_ref, last_ref, first_ref, *refs):
     out_refs, scratch = refs[:-1], refs[-1]
     chips = len(out_refs)
     core = info_ref[1]
@@ -475,22 +463,16 @@
     info = jnp.stack([lane // 2, lane % 2, patch % 2, jnp.int32(chips)]).astype(jnp.int32)
 
     edge = array(STEPS * step + 8, width)
-    place = pl.BlockSpec(memory_space=pltpu.HBM)
-    to_last, to_first, flow, emitted = pl.pallas_call(
-        pack_kernel,
-        out_shape=[edge, edge, array(*flow_fields.shape), array(step, width // 2)],
-        in_specs=[SMEM] + [place] * 3, out_specs=[VMEM] * 4,
-        scratch_shapes=[
-            pltpu.VMEM((step, rows, width), F32), pltpu.VMEM((1, step), F32), pltpu.SemaphoreType.DMA((3,))
-        ],
-        compiler_params=pltpu.CompilerParams(vmem_limit_bytes=32 * 1024 * 1024), name="pack",
-    )(info, init_field, flow_fields, emission[None, :])
+    to_last, to_first, emitted = call(
+        pack_kernel, "pack", [edge, edge, array(step, width // 2)],
+        [info, init_field, flow_fields, emission[None, :]], limit=32,
+    )
 
     def swap(message, start):
         lower = range(start, patches - 1, 2)
         return lax.ppermute(message, "patch", [(p, p + 1) for p in lower] + [(p + 1, p) for p in lower])
 
-    halo_first, halo_last = swap(to_first, 1), swap(to_last, 0)
+    halo_last, halo_first = swap(to_last, 0), swap(to_first, 1)
 
     mine = jnp.concatenate(
         [
@@ -514,14 +496,14 @@
     single = all(len({source for source, _ in hops}) == len(hops) for hops in mirrored)
     targets = mirrored if single else turning
     pair = array(2, step, width)
-    args = [info, init_field, flow, emitted]
+    args = [info, init_field, flow_fields, emitted]
     kept, *inner = call(
         functools.partial(inner_kernel, targets), "inner", [array(4, step, width)] + [pair] * chips, args,
         [pltpu.VMEM((rows, step, width), F32), pltpu.VMEM((rows, 8, width), F32)], limit=32,
     )
     got_inner = [inner[0]] + [between(inner[s], targets[s]) for s in range(1, chips)]
     outer = call(
-        edge_kernel, "edge", [pair] * chips, args + [kept, halo_first, halo_last],
+        edge_kernel, "edge", [pair] * chips, args + [kept, halo_last, halo_first],
         [pltpu.VMEM((2, step, width), F32)], limit=32,
     )
     got_outer = [outer[0]] + [

time: 101 us -> 98.9 us (0.979)
  the two profiles are of different devices: /device:TPU:0 before, /device:TPU:2 now
where the time goes in v16:
time: 98.9 us; the launch traced here: 99.2 us
  starting transfers between devices  47.3 us (48%)
  waiting for transfers between devices  25.2 us (25%)
  Pallas kernels  23.1 us (23%)
  local copies, waits for them, and re-layouts  2.63 us (3%)
    pallas_call x7, Pallas kernels, call(): pl.pallas_call(kernel, out_shape=out_shape, in_specs=[SMEM] + [VMEM] * (l...  23.1 us
    ppermute x7, starting transfers between devices, swapped(): lax.ppermute(analysed[x], 'member', [(i, i ^ x) for i in range(lanes)])  17 us
    ppermute x6, starting transfers between devices, between(): lax.ppermute(message, 'member', [(2 * a + core, 2 * b + core) for a, b in...  15.9 us
    ppermute x7, waiting for transfers between devices, swapped(): lax.ppermute(analysed[x], 'member', [(i, i ^ x) for i in range(lanes)])  9.13 us
    ppermute x1, waiting for transfers between devices, per_device(): got_rest = lax.ppermute(far_own, axes, borders)  5.62 us
    ppermute x1, waiting for transfers between devices, per_device(): lax.ppermute(mine, axes, [(p * lanes + i, p * lanes + lanes - 1 - i) for...  5.27 us
    ppermute x2, starting transfers between devices, swap(): lax.ppermute(message, 'patch', [(p, p + 1) for p in lower] + [(p + 1, p)...  4.94 us
    ppermute x1, starting transfers between devices, per_device(): got_rest = lax.ppermute(far_own, axes, borders)  4.88 us
  transfers between devices with their start and end apart: 20, of which 7 were waited for; matrix products, arithmetic and copies ran while one was open for 0% of the time, Pallas kernels for 8%

profile of v16, /device:TPU:2, one launch (start us, length us, event | category | flops | bytes accessed | tf_op | source)
XLA Modules:
  0.0 99.2 jit_solution(10085833441465262248)
XLA Ops:
  0.0 0.0 copy-start.1
  0.0 0.1 pad_add_fusion.info_ref
  0.1 0.0 copy-start.2
  0.1 0.7 copy-done.1
  0.8 0.0 copy-done.2
  0.8 0.0 copy-start
  0.8 1.2 %copy-done = f32[128,8,256]{2,1,0:T(8,128)S(1)} copy-done((f32[128,8,256]{2,1,0:T(8,128)S(1)}, f32[128,8,256]{2,1,0:T(8,128)}, u32[]{:S(2)}) %copy-start) | copy-done | bytes 1048600
  2.0 1.2 %pack.1 = (f32[264,256]{1,0:T(8,128)S(1)}, f32[264,256]{1,0:T(8,128)S(1)}, f32[128,128]{1,0:T(8,128)S(1)}) custom-call(s32[4]{0:T(128)S(1)} %pad_add_fusion.info_ref, f32[128,8,256]{2,1,0:T(8,128)S(1)} %copy-done, f32[4,8,256]{2,1,0:T(8,128)S(1)} %copy-done.1, f32[1,128]{1,0:T(1,128)S(1)} %bitcast.5), custom_call_target="tpu_custom_call" | custom-call | tf_op jit(solution)/shard_map/pack/pallas_call | solution.py:431
  3.2 0.1 collective-permute-start
  3.2 4.9 %collective-permute-start.1 = (f32[264,256]{1,0:T(8,128)S(1)}, f32[264,256]{1,0:T(8,128)S(1)}, u32[]{:S(2)}, u32[]{:S(2)}) collective-permute-start(f32[264,256]{1,0:T(8,128)S(1)} %get-tuple-element.39), channel_id=1, source_target_pairs={{8,16},{16,8},{9,17},{17,9},{10,18},{18,10},{11,19},{19,11},{12,20... | collective-permute-start | bytes 811016 | tf_op jit(solution)/shard_map/ppermute | solution.py:473
  8.1 2.2 %inner.1 = (f32[4,128,256]{2,1,0:T(8,128)S(1)}, f32[2,128,256]{2,1,0:T(8,128)S(1)}, f32[2,128,256]{2,1,0:T(8,128)S(1)}, f32[2,128,256]{2,1,0:T(8,128)S(1)}, f32[2,128,256]{2,1,0:T(8,128)S(1)}) custom-call(s32[4]{0:T(128)S(1)} %pad_add_fusion.info_ref, f32[128,8,256]{2,1,0:T(8,128)S(1)} %copy-done, f32[4,8,256]{2,1,0:T(8,128)S(1)} %copy-done.1, ...), custom_call_target="tpu_custom_call" | custom-call | tf_op jit(solution)/shard_map/inner/pallas_call | solution.py:431
  10.3 0.7 collective-permute-start.3
  11.0 6.2 %collective-permute-start.4 = (f32[2,128,256]{2,1,0:T(8,128)S(1)}, f32[2,128,256]{2,1,0:T(8,128)S(1)}, u32[]{:S(2)}, u32[]{:S(2)}) collective-permute-start(f32[2,128,256]{2,1,0:T(8,128)S(1)} %get-tuple-element.44), channel_id=1, source_target_pairs={{6,2},{7,3},{0,4},{1,5},{14,10},{15,11},{8,12},{9,13},{22,18},{23,... | collective-permute-start | bytes 786440 | tf_op jit(solution)/shard_map/ppermute | solution.py:489
  17.2 1.4 %collective-permute-start.5 = (f32[2,128,256]{2,1,0:T(8,128)S(1)}, f32[2,128,256]{2,1,0:T(8,128)S(1)}, u32[]{:S(2)}, u32[]{:S(2)}) collective-permute-start(f32[2,128,256]{2,1,0:T(8,128)S(1)} %get-tuple-element.45), channel_id=1, source_target_pairs={{0,2},{1,3},{6,4},{7,5},{8,10},{9,11},{14,12},{15,13},{16,18},{17,... | collective-permute-start | bytes 786440 | tf_op jit(solution)/shard_map/ppermute | solution.py:489
  18.6 0.0 collective-permute-done.last_ref
  18.6 0.0 collective-permute-done.1.first_ref
  18.7 1.5 %edge.1 = (f32[2,128,256]{2,1,0:T(8,128)S(1)}, f32[2,128,256]{2,1,0:T(8,128)S(1)}, f32[2,128,256]{2,1,0:T(8,128)S(1)}, f32[2,128,256]{2,1,0:T(8,128)S(1)}) custom-call(s32[4]{0:T(128)S(1)} %pad_add_fusion.info_ref, f32[128,8,256]{2,1,0:T(8,128)S(1)} %copy-done, f32[4,8,256]{2,1,0:T(8,128)S(1)} %copy-done.1, f32[128,128]{1,0:T(8,128)S(1)} %get-tuple-element.36.emission_ref, ...), custom_call_target="tpu_custom_call" | custom-call | tf_op jit(solution)/shard_map/edge/pallas_call | solution.py:431
  20.2 1.3 %collective-permute-start.6 = (f32[2,128,256]{2,1,0:T(8,128)S(1)}, f32[2,128,256]{2,1,0:T(8,128)S(1)}, u32[]{:S(2)}, u32[]{:S(2)}) collective-permute-start(f32[2,128,256]{2,1,0:T(8,128)S(1)} %get-tuple-element.46), channel_id=1, source_target_pairs={{2,0},{3,1},{4,6},{5,7},{10,8},{11,9},{12,14},{13,15},{18,16},{19,... | collective-permute-start | bytes 786440 | tf_op jit(solution)/shard_map/ppermute | solution.py:489
  21.5 1.3 %collective-permute-start.7 = (f32[2,128,256]{2,1,0:T(8,128)S(1)}, f32[2,128,256]{2,1,0:T(8,128)S(1)}, u32[]{:S(2)}, u32[]{:S(2)}) collective-permute-start(f32[2,128,256]{2,1,0:T(8,128)S(1)} %get-tuple-element.47), channel_id=1, source_target_pairs={{4,0},{5,1},{2,6},{3,7},{12,8},{13,9},{10,14},{11,15},{20,16},{21,... | collective-permute-start | bytes 786440 | tf_op jit(solution)/shard_map/ppermute | solution.py:489
  22.8 0.0 collective-permute-done.3.refs_1_
  22.8 0.0 copy-start.5
  22.8 5.0 %collective-permute-start.8 = (f32[2,128,256]{2,1,0:T(8,128)S(1)}, f32[2,128,256]{2,1,0:T(8,128)S(1)}, u32[]{:S(2)}, u32[]{:S(2)}) collective-permute-start(f32[2,128,256]{2,1,0:T(8,128)S(1)} %get-tuple-element.48), channel_id=1, source_target_pairs={{6,0},{7,1},{0,6},{1,7},{14,8},{15,9},{8,14},{9,15},{22,16},{23,17... | collective-permute-start | bytes 786440 | tf_op jit(solution)/shard_map/ppermute | solution.py:489
  28.5 0.0 copy-done.5
  28.6 0.0 copy-start.3
  28.6 0.0 copy-start.4
  28.6 0.6 copy-done.3
  29.2 0.0 copy-done.4
  29.3 0.0 collective-permute-done.4.refs_2_
  29.3 1.9 %collective-permute-start.2 = (f32[8,512]{1,0:T(8,128)S(1)}, f32[8,512]{1,0:T(8,128)S(1)}, u32[]{:S(2)}, u32[]{:S(2)}) collective-permute-start(f32[8,512]{1,0:T(8,128)S(1)} %concatenate.3.mine_ref), channel_id=1, source_target_pairs={{8,15},{9,14},{10,13},{11,12},{12,11},{13,10},{14,9},{15,8},{24,31... | collective-permute-start | bytes 49160 | tf_op jit(solution)/shard_map/ppermute | solution.py:515
  31.2 0.0 collective-permute-done.5.refs_3_
  31.2 5.3 %collective-permute-done.2.other_ref = f32[8,512]{1,0:T(8,128)S(1)} collective-permute-done((f32[8,512]{1,0:T(8,128)S(1)}, f32[8,512]{1,0:T(8,128)S(1)}, u32[]{:S(2)}, u32[]{:S(2)}) %collective-permute-start.2) | collective-permute-done | bytes 16416 | tf_op jit(solution)/shard_map/ppermute | solution.py:515
  36.5 4.1 %collective-permute-done.6.refs_5_ = f32[2,128,256]{2,1,0:T(8,128)S(1)} collective-permute-done((f32[2,128,256]{2,1,0:T(8,128)S(1)}, f32[2,128,256]{2,1,0:T(8,128)S(1)}, u32[]{:S(2)}, u32[]{:S(2)}) %collective-permute-start.6) | collective-permute-done | bytes 262176 | tf_op jit(solution)/shard_map/ppermute | solution.py:489
  40.6 0.0 collective-permute-done.7.refs_6_
  40.6 0.0 collective-permute-done.8.refs_7_
  40.6 0.6 collect.1
  41.3 0.1 collective-permute-start.9
  41.4 0.5 collective-permute-start.10
  41.9 2.0 %collective-permute-start.11 = (f32[520,256]{1,0:T(8,128)S(1)}, f32[520,256]{1,0:T(8,128)S(1)}, u32[]{:S(2)}, u32[]{:S(2)}) collective-permute-start(f32[520,256]{1,0:T(8,128)S(1)} %get-tuple-element.50.near_own), channel_id=1, source_target_pairs={{1,2},{2,1},{3,4},{4,3},{5,6},{6,5},{7,15},{8,16},{9,10},{10,9},{1... | collective-permute-start | bytes 1597448 | tf_op jit(solution)/shard_map/ppermute | solution.py:541
  43.9 0.0 collective-permute-done.9.far_own
  43.9 4.9 %collective-permute-start.12 = (f32[4,128,256]{2,1,0:T(8,128)S(1)}, f32[4,128,256]{2,1,0:T(8,128)S(1)}, u32[]{:S(2)}, u32[]{:S(2)}) collective-permute-start(f32[4,128,256]{2,1,0:T(8,128)S(1)} %collective-permute-done.9.far_own), channel_id=1, source_target_pairs={{1,2},{2,1},{3,4},{4,3},{5,6},{6,5},{7,15},{8,16},{9,10},{10,9},{1... | collective-permute-start | bytes 1572872 | tf_op jit(solution)/shard_map/ppermute | solution.py:543
  48.8 0.0 collective-permute-done.10.far_other
  48.8 4.0 %prepare.1 = (bf16[1024,512]{1,0:T(8,128)(2,1)S(1)}, bf16[1024,512]{1,0:T(8,128)(2,1)S(1)}, bf16[256,1024]{1,0:T(8,128)(2,1)S(1)}, bf16[256,1024]{1,0:T(8,128)(2...) custom-call(s32[4]{0:T(128)S(1)} %pad_add_fusion.info_ref, ...), custom_call_target="tpu_custom_call" | custom-call | flops 1073741824 | tf_op jit(solution)/shard_map/prepare/pallas_call | solution.py:431
  52.8 1.1 %collective-permute-done.11.half_ref = f32[520,256]{1,0:T(8,128)S(1)} collective-permute-done((f32[520,256]{1,0:T(8,128)S(1)}, f32[520,256]{1,0:T(8,128)S(1)}, u32[]{:S(2)}, u32[]{:S(2)}) %collective-permute-start.11) | collective-permute-done | bytes 532512 | tf_op jit(solution)/shard_map/ppermute | solution.py:541
  53.9 5.6 %collective-permute-done.12.rest_ref = f32[4,128,256]{2,1,0:T(8,128)S(1)} collective-permute-done((f32[4,128,256]{2,1,0:T(8,128)S(1)}, f32[4,128,256]{2,1,0:T(8,128)S(1)}, u32[]{:S(2)}, u32[]{:S(2)}) %collective-permute-start.12) | collective-permute-done | bytes 524320 | tf_op jit(solution)/shard_map/ppermute | solution.py:543
  59.5 11.6 %region.1 = (f32[128,256]{1,0:T(8,128)S(1)}, f32[128,256]{1,0:T(8,128)S(1)}, f32[128,256]{1,0:T(8,128)S(1)}, f32[128,256]{1,0:T(8,128)S(1)}, f32[128,256]{1,0:T(...) custom-call(s32[4]{0:T(128)S(1)} %pad_add_fusion.info_ref, ...), custom_call_target="tpu_custom_call" | custom-call | tf_op jit(solution)/shard_map/region/pallas_call | solution.py:431
  71.2 1.4 %collective-permute-start.13 = (f32[128,256]{1,0:T(8,128)S(1)}, f32[128,256]{1,0:T(8,128)S(1)}, u32[]{:S(2)}, u32[]{:S(2)}) collective-permute-start(f32[128,256]{1,0:T(8,128)S(1)} %get-tuple-element.59), channel_id=1, source_target_pairs={{0,7},{1,6},{2,5},{3,4},{4,3},{5,2},{6,1},{7,0},{8,15},{9,14},{10,... | collective-permute-start | bytes 393224 | tf_op jit(solution)/shard_map/ppermute | solution.py:561
  72.6 0.5 collective-permute-start.14
  73.0 0.4 collective-permute-start.15
  73.4 4.1 %collective-permute-start.16 = (f32[128,256]{1,0:T(8,128)S(1)}, f32[128,256]{1,0:T(8,128)S(1)}, u32[]{:S(2)}, u32[]{:S(2)}) collective-permute-start(f32[128,256]{1,0:T(8,128)S(1)} %get-tuple-element.62), channel_id=1, source_target_pairs={{0,4},{1,5},{2,6},{3,7},{4,0},{5,1},{6,2},{7,3},{8,12},{9,13},{10,... | collective-permute-start | bytes 393224 | tf_op jit(solution)/shard_map/ppermute | solution.py:561
  77.4 0.0 collective-permute-start.17
  77.4 0.0 collective-permute-done.13.refs_0_
  77.5 10.8 %collective-permute-start.18 = (f32[128,256]{1,0:T(8,128)S(1)}, f32[128,256]{1,0:T(8,128)S(1)}, u32[]{:S(2)}, u32[]{:S(2)}) collective-permute-start(f32[128,256]{1,0:T(8,128)S(1)} %get-tuple-element.64), channel_id=1, source_target_pairs={{0,2},{1,3},{2,0},{3,1},{4,6},{5,7},{6,4},{7,5},{8,10},{9,11},{10,... | collective-permute-start | bytes 393224 | tf_op jit(solution)/shard_map/ppermute | solution.py:561
  88.2 0.0 collective-permute-done.14.refs_1_
  88.3 0.0 collective-permute-start.19
  88.3 5.2 %collective-permute-done.15.refs_2_ = f32[128,256]{1,0:T(8,128)S(1)} collective-permute-done((f32[128,256]{1,0:T(8,128)S(1)}, f32[128,256]{1,0:T(8,128)S(1)}, u32[]{:S(2)}, u32[]{:S(2)}) %collective-permute-start.15) | collective-permute-done | bytes 131104 | tf_op jit(solution)/shard_map/ppermute | solution.py:561
  93.4 2.5 %collective-permute-done.16.refs_3_ = f32[128,256]{1,0:T(8,128)S(1)} collective-permute-done((f32[128,256]{1,0:T(8,128)S(1)}, f32[128,256]{1,0:T(8,128)S(1)}, u32[]{:S(2)}, u32[]{:S(2)}) %collective-permute-start.16) | collective-permute-done | bytes 131104 | tf_op jit(solution)/shard_map/ppermute | solution.py:561
  95.9 0.0 collective-permute-done.17.refs_4_
  95.9 1.4 %collective-permute-done.18.refs_5_ = f32[128,256]{1,0:T(8,128)S(1)} collective-permute-done((f32[128,256]{1,0:T(8,128)S(1)}, f32[128,256]{1,0:T(8,128)S(1)}, u32[]{:S(2)}, u32[]{:S(2)}) %collective-permute-start.18) | collective-permute-done | bytes 131104 | tf_op jit(solution)/shard_map/ppermute | solution.py:561
  97.3 0.0 collective-permute-done.19.refs_6_
  97.3 1.9 %unpack.1 = f32[128,8,256]{2,1,0:T(8,128)} custom-call(s32[4]{0:T(128)S(1)} %pad_add_fusion.info_ref, f32[128,256]{1,0:T(8,128)S(1)} %collective-permute-done.13.refs_0_, f32[128,256]{1,0:T(8,128)S(1)} %collective-permute-done.14.refs_1_, f32[128,256]{1,0:T(8,128)S(1)} %collective-permute-done.15.refs_2_, f32[128,256]{1,0:T(8,128)S(1)} %collective-permute-done.16.refs_3_, ...), custom_call_target="tpu_custom_call" | custom-call | tf_op jit(solution)/shard_map/unpack/pallas_call | solution.py:431
  (3 shorter events, 0.0 us)
Async XLA Ops:
  0.0 0.8 copy-start.1
  0.1 0.7 copy-start.2
  0.8 1.2 %copy-start = (f32[128,8,256]{2,1,0:T(8,128)S(1)}, f32[128,8,256]{2,1,0:T(8,128)}, u32[]{:S(2)}) copy-start(f32[128,8,256]{2,1,0:T(8,128)} %field_ref.5) | copy-start | bytes 3145732
  3.2 15.5 %collective-permute-start = (f32[264,256]{1,0:T(8,128)S(1)}, f32[264,256]{1,0:T(8,128)S(1)}, u32[]{:S(2)}, u32[]{:S(2)}) collective-permute-start(f32[264,256]{1,0:T(8,128)S(1)} %get-tuple-element.38), channel_id=1, source_target_pairs={{0,8},{16,24},{8,0},{24,16},{1,9},{17,25},{9,1},{25,17},{2,10},{18... | collective-permute-start | bytes 811016 | tf_op jit(solution)/shard_map/ppermute | solution.py:473
  3.2 15.4 %collective-permute-start.1 = (f32[264,256]{1,0:T(8,128)S(1)}, f32[264,256]{1,0:T(8,128)S(1)}, u32[]{:S(2)}, u32[]{:S(2)}) collective-permute-start(f32[264,256]{1,0:T(8,128)S(1)} %get-tuple-element.39), channel_id=1, source_target_pairs={{8,16},{16,8},{9,17},{17,9},{10,18},{18,10},{11,19},{19,11},{12,20... | collective-permute-start | bytes 811016 | tf_op jit(solution)/shard_map/ppermute | solution.py:473
  10.3 12.5 %collective-permute-start.3 = (f32[2,128,256]{2,1,0:T(8,128)S(1)}, f32[2,128,256]{2,1,0:T(8,128)S(1)}, u32[]{:S(2)}, u32[]{:S(2)}) collective-permute-start(f32[2,128,256]{2,1,0:T(8,128)S(1)} %get-tuple-element.43), channel_id=1, source_target_pairs={{4,2},{5,3},{2,4},{3,5},{12,10},{13,11},{10,12},{11,13},{20,18},{2... | collective-permute-start | bytes 786440 | tf_op jit(solution)/shard_map/ppermute | solution.py:489
  11.0 18.3 %collective-permute-start.4 = (f32[2,128,256]{2,1,0:T(8,128)S(1)}, f32[2,128,256]{2,1,0:T(8,128)S(1)}, u32[]{:S(2)}, u32[]{:S(2)}) collective-permute-start(f32[2,128,256]{2,1,0:T(8,128)S(1)} %get-tuple-element.44), channel_id=1, source_target_pairs={{6,2},{7,3},{0,4},{1,5},{14,10},{15,11},{8,12},{9,13},{22,18},{23,... | collective-permute-start | bytes 786440 | tf_op jit(solution)/shard_map/ppermute | solution.py:489
  17.2 14.0 %collective-permute-start.5 = (f32[2,128,256]{2,1,0:T(8,128)S(1)}, f32[2,128,256]{2,1,0:T(8,128)S(1)}, u32[]{:S(2)}, u32[]{:S(2)}) collective-permute-start(f32[2,128,256]{2,1,0:T(8,128)S(1)} %get-tuple-element.45), channel_id=1, source_target_pairs={{0,2},{1,3},{6,4},{7,5},{8,10},{9,11},{14,12},{15,13},{16,18},{17,... | collective-permute-start | bytes 786440 | tf_op jit(solution)/shard_map/ppermute | solution.py:489
  20.2 20.4 %collective-permute-start.6 = (f32[2,128,256]{2,1,0:T(8,128)S(1)}, f32[2,128,256]{2,1,0:T(8,128)S(1)}, u32[]{:S(2)}, u32[]{:S(2)}) collective-permute-start(f32[2,128,256]{2,1,0:T(8,128)S(1)} %get-tuple-element.46), channel_id=1, source_target_pairs={{2,0},{3,1},{4,6},{5,7},{10,8},{11,9},{12,14},{13,15},{18,16},{19,... | collective-permute-start | bytes 786440 | tf_op jit(solution)/shard_map/ppermute | solution.py:489
  21.5 19.1 %collective-permute-start.7 = (f32[2,128,256]{2,1,0:T(8,128)S(1)}, f32[2,128,256]{2,1,0:T(8,128)S(1)}, u32[]{:S(2)}, u32[]{:S(2)}) collective-permute-start(f32[2,128,256]{2,1,0:T(8,128)S(1)} %get-tuple-element.47), channel_id=1, source_target_pairs={{4,0},{5,1},{2,6},{3,7},{12,8},{13,9},{10,14},{11,15},{20,16},{21,... | collective-permute-start | bytes 786440 | tf_op jit(solution)/shard_map/ppermute | solution.py:489
  22.8 5.7 %copy-start.5 = (s32[1,512]{1,0:T(1,128)S(1)}, s32[1,512]{1,0:T(1,128)}, u32[]{:S(2)}) copy-start(s32[1,512]{1,0:T(1,128)} %param.10) | copy-start | bytes 6148
  22.8 17.8 %collective-permute-start.8 = (f32[2,128,256]{2,1,0:T(8,128)S(1)}, f32[2,128,256]{2,1,0:T(8,128)S(1)}, u32[]{:S(2)}, u32[]{:S(2)}) collective-permute-start(f32[2,128,256]{2,1,0:T(8,128)S(1)} %get-tuple-element.48), channel_id=1, source_target_pairs={{6,0},{7,1},{0,6},{1,7},{14,8},{15,9},{8,14},{9,15},{22,16},{23,17... | collective-permute-start | bytes 786440 | tf_op jit(solution)/shard_map/ppermute | solution.py:489
  28.6 0.7 copy-start.3
  28.6 0.7 copy-start.4
  29.3 7.2 %collective-permute-start.2 = (f32[8,512]{1,0:T(8,128)S(1)}, f32[8,512]{1,0:T(8,128)S(1)}, u32[]{:S(2)}, u32[]{:S(2)}) collective-permute-start(f32[8,512]{1,0:T(8,128)S(1)} %concatenate.3.mine_ref), channel_id=1, source_target_pairs={{8,15},{9,14},{10,13},{11,12},{12,11},{13,10},{14,9},{15,8},{24,31... | collective-permute-start | bytes 49160 | tf_op jit(solution)/shard_map/ppermute | solution.py:515
  41.3 2.6 %collective-permute-start.9 = (f32[4,128,256]{2,1,0:T(8,128)S(1)}, f32[4,128,256]{2,1,0:T(8,128)S(1)}, u32[]{:S(2)}, u32[]{:S(2)}) collective-permute-start(f32[4,128,256]{2,1,0:T(8,128)S(1)} %get-tuple-element.51.near_other), channel_id=1, source_target_pairs={{0,1},{1,0},{2,3},{3,2},{4,5},{5,4},{6,7},{7,6},{8,9},{9,8},{10,11... | collective-permute-start | bytes 1572872 | tf_op jit(solution)/shard_map/ppermute | solution.py:540
  41.4 7.4 %collective-permute-start.10 = (f32[520,256]{1,0:T(8,128)S(1)}, f32[520,256]{1,0:T(8,128)S(1)}, u32[]{:S(2)}, u32[]{:S(2)}) collective-permute-start(f32[520,256]{1,0:T(8,128)S(1)} %get-tuple-element.50.near_own), channel_id=1, source_target_pairs={{0,1},{1,0},{2,3},{3,2},{4,5},{5,4},{6,7},{7,6},{8,9},{9,8},{10,11... | collective-permute-start | bytes 1597448 | tf_op jit(solution)/shard_map/ppermute | solution.py:542
  41.9 12.0 %collective-permute-start.11 = (f32[520,256]{1,0:T(8,128)S(1)}, f32[520,256]{1,0:T(8,128)S(1)}, u32[]{:S(2)}, u32[]{:S(2)}) collective-permute-start(f32[520,256]{1,0:T(8,128)S(1)} %get-tuple-element.50.near_own), channel_id=1, source_target_pairs={{1,2},{2,1},{3,4},{4,3},{5,6},{6,5},{7,15},{8,16},{9,10},{10,9},{1... | collective-permute-start | bytes 1597448 | tf_op jit(solution)/shard_map/ppermute | solution.py:541
  43.9 15.6 %collective-permute-start.12 = (f32[4,128,256]{2,1,0:T(8,128)S(1)}, f32[4,128,256]{2,1,0:T(8,128)S(1)}, u32[]{:S(2)}, u32[]{:S(2)}) collective-permute-start(f32[4,128,256]{2,1,0:T(8,128)S(1)} %collective-permute-done.9.far_own), channel_id=1, source_target_pairs={{1,2},{2,1},{3,4},{4,3},{5,6},{6,5},{7,15},{8,16},{9,10},{10,9},{1... | collective-permute-start | bytes 1572872 | tf_op jit(solution)/shard_map/ppermute | solution.py:543
  71.2 6.3 %collective-permute-start.13 = (f32[128,256]{1,0:T(8,128)S(1)}, f32[128,256]{1,0:T(8,128)S(1)}, u32[]{:S(2)}, u32[]{:S(2)}) collective-permute-start(f32[128,256]{1,0:T(8,128)S(1)} %get-tuple-element.59), channel_id=1, source_target_pairs={{0,7},{1,6},{2,5},{3,4},{4,3},{5,2},{6,1},{7,0},{8,15},{9,14},{10,... | collective-permute-start | bytes 393224 | tf_op jit(solution)/shard_map/ppermute | solution.py:561
  72.6 15.7 %collective-permute-start.14 = (f32[128,256]{1,0:T(8,128)S(1)}, f32[128,256]{1,0:T(8,128)S(1)}, u32[]{:S(2)}, u32[]{:S(2)}) collective-permute-start(f32[128,256]{1,0:T(8,128)S(1)} %get-tuple-element.60), channel_id=1, source_target_pairs={{0,6},{1,7},{2,4},{3,5},{4,2},{5,3},{6,0},{7,1},{8,14},{9,15},{10,... | collective-permute-start | bytes 393224 | tf_op jit(solution)/shard_map/ppermute | solution.py:561
  73.0 20.4 %collective-permute-start.15 = (f32[128,256]{1,0:T(8,128)S(1)}, f32[128,256]{1,0:T(8,128)S(1)}, u32[]{:S(2)}, u32[]{:S(2)}) collective-permute-start(f32[128,256]{1,0:T(8,128)S(1)} %get-tuple-element.61), channel_id=1, source_target_pairs={{0,5},{1,4},{2,7},{3,6},{4,1},{5,0},{6,3},{7,2},{8,13},{9,12},{10,... | collective-permute-start | bytes 393224 | tf_op jit(solution)/shard_map/ppermute | solution.py:561
  73.4 22.5 %collective-permute-start.16 = (f32[128,256]{1,0:T(8,128)S(1)}, f32[128,256]{1,0:T(8,128)S(1)}, u32[]{:S(2)}, u32[]{:S(2)}) collective-permute-start(f32[128,256]{1,0:T(8,128)S(1)} %get-tuple-element.62), channel_id=1, source_target_pairs={{0,4},{1,5},{2,6},{3,7},{4,0},{5,1},{6,2},{7,3},{8,12},{9,13},{10,... | collective-permute-start | bytes 393224 | tf_op jit(solution)/shard_map/ppermute | solution.py:561
  77.4 18.5 %collective-permute-start.17 = (f32[128,256]{1,0:T(8,128)S(1)}, f32[128,256]{1,0:T(8,128)S(1)}, u32[]{:S(2)}, u32[]{:S(2)}) collective-permute-start(f32[128,256]{1,0:T(8,128)S(1)} %get-tuple-element.63), channel_id=1, source_target_pairs={{0,3},{1,2},{2,1},{3,0},{4,7},{5,6},{6,5},{7,4},{8,11},{9,10},{10,... | collective-permute-start | bytes 393224 | tf_op jit(solution)/shard_map/ppermute | solution.py:561
  77.5 19.8 %collective-permute-start.18 = (f32[128,256]{1,0:T(8,128)S(1)}, f32[128,256]{1,0:T(8,128)S(1)}, u32[]{:S(2)}, u32[]{:S(2)}) collective-permute-start(f32[128,256]{1,0:T(8,128)S(1)} %get-tuple-element.64), channel_id=1, source_target_pairs={{0,2},{1,3},{2,0},{3,1},{4,6},{5,7},{6,4},{7,5},{8,10},{9,11},{10,... | collective-permute-start | bytes 393224 | tf_op jit(solution)/shard_map/ppermute | solution.py:561
  88.3 9.1 %collective-permute-start.19 = (f32[128,256]{1,0:T(8,128)S(1)}, f32[128,256]{1,0:T(8,128)S(1)}, u32[]{:S(2)}, u32[]{:S(2)}) collective-permute-start(f32[128,256]{1,0:T(8,128)S(1)} %get-tuple-element.65), channel_id=1, source_target_pairs={{0,1},{1,0},{2,3},{3,2},{4,5},{5,4},{6,7},{7,6},{8,9},{9,8},{10,11... | collective-permute-start | bytes 393224 | tf_op jit(solution)/shard_map/ppermute | solution.py:561

commit v17 on v16

--- a/solution.py
+++ b/solution.py
@@ -18,14 +18,14 @@
 BF16 = jnp.bfloat16
 
 
-def pack_kernel(info_ref, field_ref, flow_ref, member_ref, first_ref, second_ref, emission_ref):
+def pack_kernel(info, field_ref, flow_ref, member_ref, first_ref, second_ref, emission_ref):
     members, rows, width = field_ref.shape
     diagonal = lax.broadcasted_iota(jnp.int32, (members, members), 0) == lax.broadcasted_iota(
         jnp.int32, (members, members), 1
     )
     column = jnp.sum(jnp.where(diagonal, member_ref[...], 0.0), axis=1, keepdims=True)
     emission_ref[...] = jnp.broadcast_to(column, emission_ref.shape)
-    even = info_ref[2] == 0
+    even = info[2] == 0
     for place in range(STEPS):
         tail, head = field_ref[:, rows - STEPS + place, :], field_ref[:, place, :]
         at = pl.ds(place * members, members)
@@ -61,7 +61,7 @@
     )
 
 
-def inner_kernel(targets, info_ref, field_ref, flow_ref, emission_ref, kept_ref, *refs):
+def inner_kernel(targets, info, field_ref, flow_ref, emission_ref, kept_ref, *refs):
     out_refs, (wide_ref, weight_ref) = refs[:-2], refs[-2:]
     rows = field_ref.shape[1]
     emission = doubled(emission_ref[...])
@@ -75,13 +75,13 @@
     for place, row in enumerate((1, 2, rows - 3, rows - 2)):
         kept_ref[place] = wide_ref[row]
     for out_ref, hops in zip(out_refs, targets):
-        chip = sum(jnp.where(info_ref[0] == source, to, 0) for source, to in hops)
+        chip = sum(jnp.where(info[0] == source, to, 0) for source, to in hops)
 
         @pl.when(chip > 0)
         def _():
             for place in range(2):
-                position = 2 * chip + jnp.abs(info_ref[1] - 1 + place)
-                row = position + info_ref[2] * (rows - 1 - 2 * position)
+                position = 2 * chip + jnp.abs(info[1] - 1 + place)
+                row = position + info[2] * (rows - 1 - 2 * position)
                 weights = weight_ref[row]
                 out_ref[place] = advance(
                     [weights[i : i + 1] for i in range(6)],
@@ -89,7 +89,7 @@
                 )
 
 
-def end_rows(info_ref, last, field_ref, flow_ref, emission_ref, kept_ref, halo_ref, out_ref):
+def end_rows(info, last, field_ref, flow_ref, emission_ref, kept_ref, halo_ref, out_ref):
     members, rows, width = field_ref.shape
     emission = doubled(emission_ref[...])
 
@@ -99,7 +99,7 @@
     halo_weights = weights_of(halo_ref[pl.ds(STEPS * members, 4), :])
     for parity in range(2):
 
-        @pl.when(info_ref[2] == parity)
+        @pl.when(info[2] == parity)
         def _():
             if parity == last:
                 end, near, outside, beyond = 0, 1, halo_row(1), halo_row(0)
@@ -120,15 +120,15 @@
             out_ref[1 - last] = ordered(weights_of(flow_ref[:, near, :]), own, inside, further)
 
 
-def edge_kernel(info_ref, field_ref, flow_ref, emission_ref, kept_ref, last_ref, first_ref, *refs):
+def edge_kernel(info, field_ref, flow_ref, emission_ref, kept_ref, last_ref, first_ref, *refs):
     out_refs, scratch = refs[:-1], refs[-1]
     chips = len(out_refs)
-    core = info_ref[1]
+    core = info[1]
     for last, halo_ref in enumerate((first_ref, last_ref)):
-        end_rows(info_ref, last, field_ref, flow_ref, emission_ref, kept_ref, halo_ref, scratch)
+        end_rows(info, last, field_ref, flow_ref, emission_ref, kept_ref, halo_ref, scratch)
         for s, out_ref in enumerate(out_refs):
 
-            @pl.when(info_ref[0] == (chips - 1 - s if last else s))
+            @pl.when(info[0] == (chips - 1 - s if last else s))
             def _():
                 out_ref[0] = scratch[1 - core]
                 out_ref[1] = scratch[core]
@@ -139,13 +139,13 @@
     return jnp.where(chip == 0, k, jnp.where(chip == chips - 1, chips - 1 - k, inner))
 
 
-def collect_kernel(order, info_ref, mine_ref, other_ref, *refs):
+def collect_kernel(order, info, mine_ref, other_ref, *refs):
     chips = len(order)
     near_other, near_own, observed_ref = refs[-3:]
     step = near_other.shape[1]
-    observed_ref[...] = jnp.where(info_ref[2] == 1, other_ref[...], mine_ref[...])
+    observed_ref[...] = jnp.where(info[2] == 1, other_ref[...], mine_ref[...])
     near_own[pl.ds(chips * step, PADDING), :] = jnp.zeros((PADDING, near_own.shape[1]), F32)
-    chip = info_ref[0]
+    chip = info[0]
     at_edge = jnp.logical_or(chip == 0, chip == chips - 1)
     for index, (s, k) in enumerate(order):
         block = source_of(chip, chips, s, k)
@@ -158,12 +158,12 @@
                 near_own[rows, :] = ref[1]
 
 
-def unpack_kernel(order, info_ref, *refs):
+def unpack_kernel(order, info, *refs):
     row_refs, out_ref = refs[:-1], refs[-1]
     rows = out_ref.shape[1]
     for x, ref in zip(order, row_refs):
-        position = (2 * info_ref[0] + info_ref[1]) ^ x
-        row = position + info_ref[2] * (rows - 1 - 2 * position)
+        position = (2 * info[0] + info[1]) ^ x
+        row = position + info[2] * (rows - 1 - 2 * position)
         out_ref[:, pl.ds(row, 1), :] = ref[...][:, None, :]
 
 
@@ -194,13 +194,13 @@
     return total
 
 
-def observations(info_ref, observed_ref, width, root):
+def observations(info, observed_ref, width, root):
     slots = observed_ref.shape[1]
     cells, values, scales, count = (observed_ref[pl.ds(i, 1), :] for i in range(4))
     cells = cells.astype(jnp.int32)
     offset = sum((cells >= i * width).astype(jnp.int32) for i in (1, 2)) - 1
     column = cells - (offset + 1) * width
-    side = offset * jnp.where(info_ref[2] == 1, -1, 1) * (1 - 2 * info_ref[1])
+    side = offset * jnp.where(info[2] == 1, -1, 1) * (1 - 2 * info[1])
     cells = column + width * jnp.where(side == 0, 2, jnp.where(side < 0, 0, 1))
     active = lax.broadcasted_iota(jnp.int32, (1, slots), 1) < count.astype(jnp.int32)
     slot_weight = jnp.where(active, scales, 0.0)
@@ -226,13 +226,13 @@
 
 
 def prepare_kernel(
-    info_ref, observed_ref, near_other, near_own, far_other, far_own,
+    info, observed_ref, near_other, near_own, far_other, far_own,
     spread_high, spread_low, own_high, own_low, own_part, seen_ref, direction_ref,
     anomaly, high_ref, low_ref,
 ):
     chips, step, width = near_other.shape
     members = 2 * chips * step
-    cells, _, _, scale = observations(info_ref, observed_ref, width, math.sqrt(members - 1))
+    cells, _, _, scale = observations(info, observed_ref, width, math.sqrt(members - 1))
     chosen = one_hot(cells, width, 2 * width)
     blocks = [pl.ds(index * step, step) for index in range(2 * chips)]
     means = []
@@ -297,7 +297,7 @@
 
 
 def region_kernel(
-    info_ref, observed_ref, near_own, far_own, high_in, low_in, own_high, own_low, own_part, seen_ref,
+    info, observed_ref, near_own, far_own, high_in, low_in, own_high, own_low, own_part, seen_ref,
     direction_ref, half_ref, rest_ref, *refs,
 ):
     chips, step, width = far_own.shape
@@ -306,12 +306,12 @@
     members = 2 * chips * step
     slots = observed_ref.shape[1]
     root = math.sqrt(members - 1)
-    core = info_ref[1]
+    core = info[1]
     ends = jnp.logical_or(
-        jnp.logical_and(info_ref[0] == 0, core == 0), jnp.logical_and(info_ref[0] == chips - 1, core == 1)
+        jnp.logical_and(info[0] == 0, core == 0), jnp.logical_and(info[0] == chips - 1, core == 1)
     )
     part = jnp.where(ends, 0, 1)
-    cells, slot_weight, values, scale = observations(info_ref, observed_ref, width, root)
+    cells, slot_weight, values, scale = observations(info, observed_ref, width, root)
     chosen = one_hot(cells, 0, width)
 
     def rows_at(half, chip):
@@ -410,7 +410,7 @@
     shift, along = sides[0:1], sides[1:2]
     halved = [part * jnp.asarray(-0.5, BF16) for part in parts]
     for x, out_ref in enumerate(out_refs):
-        chip, part = info_ref[0] ^ (x // 2), x % 2
+        chip, part = info[0] ^ (x // 2), x % 2
         rows = pl.ds(pl.multiple_of((part * chips + chip) * step, step), step)
         moved = product([spread_high[rows, :], spread_low[rows, :]], halved)
         moved = moved + doubled(direction_ref[rows, :]) * along
@@ -419,22 +419,21 @@
 
 
 VMEM = pl.BlockSpec(memory_space=pltpu.VMEM)
-SMEM = pl.BlockSpec(memory_space=pltpu.SMEM)
-
-
-def call(kernel, name, out_shape, args, scratch=(), flops=None, aliases={}, limit=8, after=()):
+
+
+def position():
+    lane, patch = lax.axis_index("member"), lax.axis_index("patch")
+    return lax.div(lane, 2), lax.rem(lane, 2), lax.rem(patch, 2), lax.axis_size("member") // 2
+
+
+def call(kernel, name, out_shape, args, scratch=(), flops=None, limit=8):
     several = isinstance(out_shape, (list, tuple))
-    if after:
-        count, inner = len(args), kernel
-        args = [*args, *after]
-        kernel = lambda *refs: inner(*refs[:count], *refs[len(args) :])
     return pl.pallas_call(
-        kernel,
+        lambda *refs: kernel(position(), *refs),
         out_shape=out_shape,
-        in_specs=[SMEM] + [VMEM] * (len(args) - 1 - len(after)) + [pl.BlockSpec(memory_space=pl.ANY)] * len(after),
+        in_specs=[VMEM] * len(args),
         out_specs=[VMEM] * len(out_shape) if several else VMEM,
         scratch_shapes=scratch,
-        input_output_aliases=aliases,
         compiler_params=pltpu.CompilerParams(vmem_limit_bytes=limit * 1024 * 1024),
         cost_estimate=flops and pl.CostEstimate(flops=flops, bytes_accessed=0, transcendentals=0),
         name=name,
@@ -459,13 +458,11 @@
     members = lanes * step
     axes = ("patch", "member")
     count = patches * lanes
-    patch, lane = lax.axis_index("patch"), lax.axis_index("member")
-    info = jnp.stack([lane // 2, lane % 2, patch % 2, jnp.int32(chips)]).astype(jnp.int32)
 
     edge = array(STEPS * step + 8, width)
     to_last, to_first, emitted = call(
         pack_kernel, "pack", [edge, edge, array(step, width // 2)],
-        [info, init_field, flow_fields, emission[None, :]], limit=32,
+        [init_field, flow_fields, emission[None, :]], limit=32,
     )
 
     def swap(message, start):
@@ -496,7 +493,7 @@
     single = all(len({source for source, _ in hops}) == len(hops) for hops in mirrored)
     targets = mirrored if single else turning
     pair = array(2, step, width)
-    args = [info, init_field, flow_fields, emitted]
+    args = [init_field, flow_fields, emitted]
     kept, *inner = call(
         functools.partial(inner_kernel, targets), "inner", [array(4, step, width)] + [pair] * chips, args,
         [pltpu.VMEM((rows, step, width), F32), pltpu.VMEM((rows, 8, width), F32)], limit=32,
@@ -535,7 +532,7 @@
     half = array(chips, step, width)
     near_other, near_own, observed = call(
         functools.partial(collect_kernel, order), "collect",
-        [half, array(chips * step + PADDING, width), array(8, slots)], [info, mine, other] + pieces_in,
+        [half, array(chips * step + PADDING, width), array(8, slots)], [mine, other] + pieces_in,
     )
     far_own = lax.ppermute(near_other, axes, siblings)
     got_half = lax.ppermute(near_own, axes, borders)
@@ -547,13 +544,13 @@
         prepare_kernel, "prepare",
         [bfloat(members, slots)] * 2 + [bfloat(width, members)] * 2
         + [array(width, width // 2), array(8, slots), array(members, width // 2)],
-        [info, observed, near_other, near_own, far_other, far_own],
+        [observed, near_other, near_own, far_other, far_own],
         [pltpu.VMEM((members, 2 * width), F32)] + [pltpu.VMEM((members, 2 * width), BF16)] * 2,
         flops=8 * members * slots * width, limit=20,
     )
     analysed = call(
         region_kernel, "region", [array(step, width)] * lanes,
-        [info, observed, near_own, far_own, *prepared, got_half, got_rest],
+        [observed, near_own, far_own, *prepared, got_half, got_rest],
         split + [pltpu.VMEM((slots, slots), F32)] * 2 + [pltpu.VMEM((width + 8, slots), F32)],
         limit=24,
     )
@@ -563,7 +560,7 @@
     order = sorted(range(lanes), key=lambda x: (x.bit_length() != lanes.bit_length() - 1, -x))
     return call(
         functools.partial(unpack_kernel, order), "unpack", array(step, rows, width),
-        [info] + [swapped(x) for x in order], limit=48,
+        [swapped(x) for x in order], limit=48,
     )
 
 

time: 98.9 us -> 97.5 us (0.986)
  Pallas kernels: 23.1 us -> 19.6 us
  waiting for transfers between devices: 25.2 us -> 26.8 us
    pallas_call x7, Pallas kernels: 23.1 us -> 19.6 us  [call(): pl.pallas_call(lambda *refs: kernel(position(), *refs), out_shape=out_sha...]
    ppermute x7, waiting for transfers between devices: 9.13 us -> 10.1 us  [swapped(): lax.ppermute(analysed[x], 'member', [(i, i ^ x) for i in range(lanes)])]
  transfers between devices with their start and end apart: 20 -> 20, of which waited for: 7 -> 9; matrix products, arithmetic and copies ran while one was open for 0% -> 0% of each run, Pallas kernels for 8% -> 6%
where the time goes in v17:
time: 97.5 us; the launch traced here: 97.6 us
  starting transfers between devices  46.9 us (48%)
  waiting for transfers between devices  26.8 us (27%)
  Pallas kernels  19.6 us (20%)
  local copies, waits for them, and re-layouts  3.36 us (3%)
    pallas_call x7, Pallas kernels, call(): pl.pallas_call(lambda *refs: kernel(position(), *refs), out_shape=out_sha...  19.6 us
    ppermute x6, starting transfers between devices, between(): lax.ppermute(message, 'member', [(2 * a + core, 2 * b + core) for a, b in...  16.4 us
    ppermute x7, starting transfers between devices, swapped(): lax.ppermute(analysed[x], 'member', [(i, i ^ x) for i in range(lanes)])  16.2 us
    ppermute x7, waiting for transfers between devices, swapped(): lax.ppermute(analysed[x], 'member', [(i, i ^ x) for i in range(lanes)])  10.1 us
    ppermute x1, waiting for transfers between devices, per_device(): got_rest = lax.ppermute(far_own, axes, borders)  5.62 us
    ppermute x1, waiting for transfers between devices, per_device(): lax.ppermute(mine, axes, [(p * lanes + i, p * lanes + lanes - 1 - i) for...  5.27 us
    ppermute x2, starting transfers between devices, swap(): lax.ppermute(message, 'patch', [(p, p + 1) for p in lower] + [(p + 1, p)...  4.94 us
    ppermute x1, starting transfers between devices, per_device(): got_rest = lax.ppermute(far_own, axes, borders)  4.82 us
  transfers between devices with their start and end apart: 20, of which 9 were waited for; matrix products, arithmetic and copies ran while one was open for 0% of the time, Pallas kernels for 6%

profile of v17, /device:TPU:2, one launch (start us, length us, event | category | flops | bytes accessed | tf_op | source)
XLA Modules:
  0.0 97.6 jit_solution(8912558880754270884)
XLA Ops:
  0.0 0.0 copy-start.2
  0.0 0.7 copy-done.2
  0.7 0.0 copy-start
  0.7 1.2 %copy-done = f32[128,8,256]{2,1,0:T(8,128)S(1)} copy-done((f32[128,8,256]{2,1,0:T(8,128)S(1)}, f32[128,8,256]{2,1,0:T(8,128)}, u32[]{:S(2)}) %copy-start) | copy-done | bytes 1048600
  1.9 0.0 copy-start.1
  1.9 0.8 copy-done.1
  2.6 0.6 pack.1
  3.2 0.1 collective-permute-start
  3.3 4.9 %collective-permute-start.1 = (f32[264,256]{1,0:T(8,128)S(1)}, f32[264,256]{1,0:T(8,128)S(1)}, u32[]{:S(2)}, u32[]{:S(2)}) collective-permute-start(f32[264,256]{1,0:T(8,128)S(1)} %get-tuple-element.39), channel_id=1, source_target_pairs={{8,16},{16,8},{9,17},{17,9},{10,18},{18,10},{11,19},{19,11},{12,20... | collective-permute-start | bytes 811016 | tf_op jit(solution)/shard_map/ppermute | solution.py:470
  8.2 1.6 %inner.1 = (f32[4,128,256]{2,1,0:T(8,128)S(1)}, f32[2,128,256]{2,1,0:T(8,128)S(1)}, f32[2,128,256]{2,1,0:T(8,128)S(1)}, f32[2,128,256]{2,1,0:T(8,128)S(1)}, f32[2,128,256]{2,1,0:T(8,128)S(1)}) custom-call(f32[128,8,256]{2,1,0:T(8,128)S(1)} %copy-done, f32[4,8,256]{2,1,0:T(8,128)S(1)} %copy-done.1, f32[128,128]{1,0:T(8,128)S(1)} %get-tuple-element.36.refs_2_), custom_call_target="tpu_custom_call" | custom-call | tf_op jit(solution)/shard_map/inner/pallas_call | solution.py:431
  9.8 0.7 collective-permute-start.3
  10.5 6.2 %collective-permute-start.4 = (f32[2,128,256]{2,1,0:T(8,128)S(1)}, f32[2,128,256]{2,1,0:T(8,128)S(1)}, u32[]{:S(2)}, u32[]{:S(2)}) collective-permute-start(f32[2,128,256]{2,1,0:T(8,128)S(1)} %get-tuple-element.44), channel_id=1, source_target_pairs={{6,2},{7,3},{0,4},{1,5},{14,10},{15,11},{8,12},{9,13},{22,18},{23,... | collective-permute-start | bytes 786440 | tf_op jit(solution)/shard_map/ppermute | solution.py:486
  16.7 1.4 %collective-permute-start.5 = (f32[2,128,256]{2,1,0:T(8,128)S(1)}, f32[2,128,256]{2,1,0:T(8,128)S(1)}, u32[]{:S(2)}, u32[]{:S(2)}) collective-permute-start(f32[2,128,256]{2,1,0:T(8,128)S(1)} %get-tuple-element.45), channel_id=1, source_target_pairs={{0,2},{1,3},{6,4},{7,5},{8,10},{9,11},{14,12},{15,13},{16,18},{17,... | collective-permute-start | bytes 786440 | tf_op jit(solution)/shard_map/ppermute | solution.py:486
  18.1 0.0 collective-permute-done.refs_4_
  18.1 0.2 collective-permute-done.1.refs_5_
  18.3 0.9 edge.1
  19.2 1.3 %collective-permute-start.6 = (f32[2,128,256]{2,1,0:T(8,128)S(1)}, f32[2,128,256]{2,1,0:T(8,128)S(1)}, u32[]{:S(2)}, u32[]{:S(2)}) collective-permute-start(f32[2,128,256]{2,1,0:T(8,128)S(1)} %get-tuple-element.46), channel_id=1, source_target_pairs={{2,0},{3,1},{4,6},{5,7},{10,8},{11,9},{12,14},{13,15},{18,16},{19,... | collective-permute-start | bytes 786440 | tf_op jit(solution)/shard_map/ppermute | solution.py:486
  20.5 1.3 %collective-permute-start.7 = (f32[2,128,256]{2,1,0:T(8,128)S(1)}, f32[2,128,256]{2,1,0:T(8,128)S(1)}, u32[]{:S(2)}, u32[]{:S(2)}) collective-permute-start(f32[2,128,256]{2,1,0:T(8,128)S(1)} %get-tuple-element.47), channel_id=1, source_target_pairs={{4,0},{5,1},{2,6},{3,7},{12,8},{13,9},{10,14},{11,15},{20,16},{21,... | collective-permute-start | bytes 786440 | tf_op jit(solution)/shard_map/ppermute | solution.py:486
  21.8 0.0 collective-permute-done.3.refs_3_
  21.8 0.0 copy-start.5
  21.9 5.5 %collective-permute-start.8 = (f32[2,128,256]{2,1,0:T(8,128)S(1)}, f32[2,128,256]{2,1,0:T(8,128)S(1)}, u32[]{:S(2)}, u32[]{:S(2)}) collective-permute-start(f32[2,128,256]{2,1,0:T(8,128)S(1)} %get-tuple-element.48), channel_id=1, source_target_pairs={{6,0},{7,1},{0,6},{1,7},{14,8},{15,9},{8,14},{9,15},{22,16},{23,17... | collective-permute-start | bytes 786440 | tf_op jit(solution)/shard_map/ppermute | solution.py:486
  28.0 0.0 copy-done.5
  28.0 0.0 copy-start.3
  28.1 0.0 copy-start.4
  28.1 0.6 copy-done.3
  28.7 0.0 copy-done.4
  28.8 0.0 collective-permute-done.4.refs_4_
  28.8 1.9 %collective-permute-start.2 = (f32[8,512]{1,0:T(8,128)S(1)}, f32[8,512]{1,0:T(8,128)S(1)}, u32[]{:S(2)}, u32[]{:S(2)}) collective-permute-start(f32[8,512]{1,0:T(8,128)S(1)} %concatenate.3.refs_0_), channel_id=1, source_target_pairs={{8,15},{9,14},{10,13},{11,12},{12,11},{13,10},{14,9},{15,8},{24,31... | collective-permute-start | bytes 49160 | tf_op jit(solution)/shard_map/ppermute | solution.py:512
  30.7 0.0 collective-permute-done.5.refs_5_
  30.7 5.3 %collective-permute-done.2.refs_1_ = f32[8,512]{1,0:T(8,128)S(1)} collective-permute-done((f32[8,512]{1,0:T(8,128)S(1)}, f32[8,512]{1,0:T(8,128)S(1)}, u32[]{:S(2)}, u32[]{:S(2)}) %collective-permute-start.2) | collective-permute-done | bytes 16416 | tf_op jit(solution)/shard_map/ppermute | solution.py:512
  36.0 3.9 %collective-permute-done.6.refs_7_ = f32[2,128,256]{2,1,0:T(8,128)S(1)} collective-permute-done((f32[2,128,256]{2,1,0:T(8,128)S(1)}, f32[2,128,256]{2,1,0:T(8,128)S(1)}, u32[]{:S(2)}, u32[]{:S(2)}) %collective-permute-start.6) | collective-permute-done | bytes 262176 | tf_op jit(solution)/shard_map/ppermute | solution.py:486
  39.9 0.0 collective-permute-done.7.refs_8_
  39.9 0.0 collective-permute-done.8.refs_9_
  39.9 0.1 collect.1
  40.0 0.1 collective-permute-start.9
  40.1 0.5 collective-permute-start.10
  40.6 2.1 %collective-permute-start.11 = (f32[520,256]{1,0:T(8,128)S(1)}, f32[520,256]{1,0:T(8,128)S(1)}, u32[]{:S(2)}, u32[]{:S(2)}) collective-permute-start(f32[520,256]{1,0:T(8,128)S(1)} %get-tuple-element.50.refs_2_.refs_1_), channel_id=1, source_target_pairs={{1,2},{2,1},{3,4},{4,3},{5,6},{6,5},{7,15},{8,16},{9,10},{10,9},{1... | collective-permute-start | bytes 1597448 | tf_op jit(solution)/shard_map/ppermute | solution.py:538
  42.7 0.0 collective-permute-done.9.refs_4_.refs_2_
  42.7 4.8 %collective-permute-start.12 = (f32[4,128,256]{2,1,0:T(8,128)S(1)}, f32[4,128,256]{2,1,0:T(8,128)S(1)}, u32[]{:S(2)}, u32[]{:S(2)}) collective-permute-start(f32[4,128,256]{2,1,0:T(8,128)S(1)} %collective-permute-done.9.refs_4_.refs_2_), channel_id=1, source_target_pairs={{1,2},{2,1},{3,4},{4,3},{5,6},{6,5},{7,15},{8,16},{9,10},{10,9},{1... | collective-permute-start | bytes 1572872 | tf_op jit(solution)/shard_map/ppermute | solution.py:540
  47.5 0.0 collective-permute-done.10.refs_3_
  47.5 3.4 %prepare.1 = (bf16[1024,512]{1,0:T(8,128)(2,1)S(1)}, bf16[1024,512]{1,0:T(8,128)(2,1)S(1)}, bf16[256,1024]{1,0:T(8,128)(2,1)S(1)}, bf16[256,1024]{1,0:T(8,128)(2...) custom-call(f32[8,512]{1,0:T(8,128)S(1)} %get-tuple-element.49.refs_0_, ...), custom_call_target="tpu_custom_call" | custom-call | flops 1073741824 | tf_op jit(solution)/shard_map/prepare/pallas_call | solution.py:431
  50.9 1.7 %collective-permute-done.11.refs_10_ = f32[520,256]{1,0:T(8,128)S(1)} collective-permute-done((f32[520,256]{1,0:T(8,128)S(1)}, f32[520,256]{1,0:T(8,128)S(1)}, u32[]{:S(2)}, u32[]{:S(2)}) %collective-permute-start.11) | collective-permute-done | bytes 532512 | tf_op jit(solution)/shard_map/ppermute | solution.py:538
  52.6 5.6 %collective-permute-done.12.refs_11_ = f32[4,128,256]{2,1,0:T(8,128)S(1)} collective-permute-done((f32[4,128,256]{2,1,0:T(8,128)S(1)}, f32[4,128,256]{2,1,0:T(8,128)S(1)}, u32[]{:S(2)}, u32[]{:S(2)}) %collective-permute-start.12) | collective-permute-done | bytes 524320 | tf_op jit(solution)/shard_map/ppermute | solution.py:540
  58.2 11.6 %region.1 = (f32[128,256]{1,0:T(8,128)S(1)}, f32[128,256]{1,0:T(8,128)S(1)}, f32[128,256]{1,0:T(8,128)S(1)}, f32[128,256]{1,0:T(8,128)S(1)}, f32[128,256]{1,0:T(...) custom-call(f32[8,512]{1,0:T(8,128)S(1)} %get-tuple-element.49.refs_0_, ...), custom_call_target="tpu_custom_call" | custom-call | tf_op jit(solution)/shard_map/region/pallas_call | solution.py:431
  69.9 1.6 %collective-permute-start.13 = (f32[128,256]{1,0:T(8,128)S(1)}, f32[128,256]{1,0:T(8,128)S(1)}, u32[]{:S(2)}, u32[]{:S(2)}) collective-permute-start(f32[128,256]{1,0:T(8,128)S(1)} %get-tuple-element.59), channel_id=1, source_target_pairs={{0,7},{1,6},{2,5},{3,4},{4,3},{5,2},{6,1},{7,0},{8,15},{9,14},{10,... | collective-permute-start | bytes 393224 | tf_op jit(solution)/shard_map/ppermute | solution.py:558
  71.5 0.8 collective-permute-start.14
  72.3 0.0 collective-permute-start.15
  72.3 3.8 %collective-permute-start.16 = (f32[128,256]{1,0:T(8,128)S(1)}, f32[128,256]{1,0:T(8,128)S(1)}, u32[]{:S(2)}, u32[]{:S(2)}) collective-permute-start(f32[128,256]{1,0:T(8,128)S(1)} %get-tuple-element.62), channel_id=1, source_target_pairs={{0,4},{1,5},{2,6},{3,7},{4,0},{5,1},{6,2},{7,3},{8,12},{9,13},{10,... | collective-permute-start | bytes 393224 | tf_op jit(solution)/shard_map/ppermute | solution.py:558
  76.2 0.0 collective-permute-start.17
  76.2 0.6 collective-permute-done.13.refs_0_
  76.8 9.5 %collective-permute-start.18 = (f32[128,256]{1,0:T(8,128)S(1)}, f32[128,256]{1,0:T(8,128)S(1)}, u32[]{:S(2)}, u32[]{:S(2)}) collective-permute-start(f32[128,256]{1,0:T(8,128)S(1)} %get-tuple-element.64), channel_id=1, source_target_pairs={{0,2},{1,3},{2,0},{3,1},{4,6},{5,7},{6,4},{7,5},{8,10},{9,11},{10,... | collective-permute-start | bytes 393224 | tf_op jit(solution)/shard_map/ppermute | solution.py:558
  86.3 0.0 collective-permute-done.14.refs_1_
  86.3 0.4 collective-permute-start.19
  86.7 4.6 %collective-permute-done.15.refs_2_ = f32[128,256]{1,0:T(8,128)S(1)} collective-permute-done((f32[128,256]{1,0:T(8,128)S(1)}, f32[128,256]{1,0:T(8,128)S(1)}, u32[]{:S(2)}, u32[]{:S(2)}) %collective-permute-start.15) | collective-permute-done | bytes 131104 | tf_op jit(solution)/shard_map/ppermute | solution.py:558
  91.3 3.2 %collective-permute-done.16.refs_3_ = f32[128,256]{1,0:T(8,128)S(1)} collective-permute-done((f32[128,256]{1,0:T(8,128)S(1)}, f32[128,256]{1,0:T(8,128)S(1)}, u32[]{:S(2)}, u32[]{:S(2)}) %collective-permute-start.16) | collective-permute-done | bytes 131104 | tf_op jit(solution)/shard_map/ppermute | solution.py:558
  94.5 0.0 collective-permute-done.17.refs_4_
  94.5 1.7 %collective-permute-done.18.refs_5_ = f32[128,256]{1,0:T(8,128)S(1)} collective-permute-done((f32[128,256]{1,0:T(8,128)S(1)}, f32[128,256]{1,0:T(8,128)S(1)}, u32[]{:S(2)}, u32[]{:S(2)}) %collective-permute-start.18) | collective-permute-done | bytes 131104 | tf_op jit(solution)/shard_map/ppermute | solution.py:558
  96.2 0.0 collective-permute-done.19.refs_6_
  96.2 1.3 %unpack.1 = f32[128,8,256]{2,1,0:T(8,128)} custom-call(f32[128,256]{1,0:T(8,128)S(1)} %collective-permute-done.13.refs_0_, f32[128,256]{1,0:T(8,128)S(1)} %collective-permute-done.14.refs_1_, f32[128,256]{1,0:T(8,128)S(1)} %collective-permute-done.15.refs_2_, f32[128,256]{1,0:T(8,128)S(1)} %collective-permute-done.16.refs_3_, ...), custom_call_target="tpu_custom_call" | custom-call | tf_op jit(solution)/shard_map/unpack/pallas_call | solution.py:431
  (3 shorter events, 0.0 us)
Async XLA Ops:
  0.0 0.7 copy-start.2
  0.7 1.2 %copy-start = (f32[128,8,256]{2,1,0:T(8,128)S(1)}, f32[128,8,256]{2,1,0:T(8,128)}, u32[]{:S(2)}) copy-start(f32[128,8,256]{2,1,0:T(8,128)} %refs_0_.5) | copy-start | bytes 3145732
  1.9 0.8 copy-start.1
  3.2 14.8 %collective-permute-start = (f32[264,256]{1,0:T(8,128)S(1)}, f32[264,256]{1,0:T(8,128)S(1)}, u32[]{:S(2)}, u32[]{:S(2)}) collective-permute-start(f32[264,256]{1,0:T(8,128)S(1)} %get-tuple-element.38), channel_id=1, source_target_pairs={{0,8},{16,24},{8,0},{24,16},{1,9},{17,25},{9,1},{25,17},{2,10},{18... | collective-permute-start | bytes 811016 | tf_op jit(solution)/shard_map/ppermute | solution.py:470
  3.3 15.0 %collective-permute-start.1 = (f32[264,256]{1,0:T(8,128)S(1)}, f32[264,256]{1,0:T(8,128)S(1)}, u32[]{:S(2)}, u32[]{:S(2)}) collective-permute-start(f32[264,256]{1,0:T(8,128)S(1)} %get-tuple-element.39), channel_id=1, source_target_pairs={{8,16},{16,8},{9,17},{17,9},{10,18},{18,10},{11,19},{19,11},{12,20... | collective-permute-start | bytes 811016 | tf_op jit(solution)/shard_map/ppermute | solution.py:470
  9.8 12.1 %collective-permute-start.3 = (f32[2,128,256]{2,1,0:T(8,128)S(1)}, f32[2,128,256]{2,1,0:T(8,128)S(1)}, u32[]{:S(2)}, u32[]{:S(2)}) collective-permute-start(f32[2,128,256]{2,1,0:T(8,128)S(1)} %get-tuple-element.43), channel_id=1, source_target_pairs={{4,2},{5,3},{2,4},{3,5},{12,10},{13,11},{10,12},{11,13},{20,18},{2... | collective-permute-start | bytes 786440 | tf_op jit(solution)/shard_map/ppermute | solution.py:486
  10.5 18.3 %collective-permute-start.4 = (f32[2,128,256]{2,1,0:T(8,128)S(1)}, f32[2,128,256]{2,1,0:T(8,128)S(1)}, u32[]{:S(2)}, u32[]{:S(2)}) collective-permute-start(f32[2,128,256]{2,1,0:T(8,128)S(1)} %get-tuple-element.44), channel_id=1, source_target_pairs={{6,2},{7,3},{0,4},{1,5},{14,10},{15,11},{8,12},{9,13},{22,18},{23,... | collective-permute-start | bytes 786440 | tf_op jit(solution)/shard_map/ppermute | solution.py:486
  16.7 14.1 %collective-permute-start.5 = (f32[2,128,256]{2,1,0:T(8,128)S(1)}, f32[2,128,256]{2,1,0:T(8,128)S(1)}, u32[]{:S(2)}, u32[]{:S(2)}) collective-permute-start(f32[2,128,256]{2,1,0:T(8,128)S(1)} %get-tuple-element.45), channel_id=1, source_target_pairs={{0,2},{1,3},{6,4},{7,5},{8,10},{9,11},{14,12},{15,13},{16,18},{17,... | collective-permute-start | bytes 786440 | tf_op jit(solution)/shard_map/ppermute | solution.py:486
  19.2 20.7 %collective-permute-start.6 = (f32[2,128,256]{2,1,0:T(8,128)S(1)}, f32[2,128,256]{2,1,0:T(8,128)S(1)}, u32[]{:S(2)}, u32[]{:S(2)}) collective-permute-start(f32[2,128,256]{2,1,0:T(8,128)S(1)} %get-tuple-element.46), channel_id=1, source_target_pairs={{2,0},{3,1},{4,6},{5,7},{10,8},{11,9},{12,14},{13,15},{18,16},{19,... | collective-permute-start | bytes 786440 | tf_op jit(solution)/shard_map/ppermute | solution.py:486
  20.5 19.4 %collective-permute-start.7 = (f32[2,128,256]{2,1,0:T(8,128)S(1)}, f32[2,128,256]{2,1,0:T(8,128)S(1)}, u32[]{:S(2)}, u32[]{:S(2)}) collective-permute-start(f32[2,128,256]{2,1,0:T(8,128)S(1)} %get-tuple-element.47), channel_id=1, source_target_pairs={{4,0},{5,1},{2,6},{3,7},{12,8},{13,9},{10,14},{11,15},{20,16},{21,... | collective-permute-start | bytes 786440 | tf_op jit(solution)/shard_map/ppermute | solution.py:486
  21.8 6.2 %copy-start.5 = (s32[1,512]{1,0:T(1,128)S(1)}, s32[1,512]{1,0:T(1,128)}, u32[]{:S(2)}) copy-start(s32[1,512]{1,0:T(1,128)} %param.10) | copy-start | bytes 6148
  21.9 18.0 %collective-permute-start.8 = (f32[2,128,256]{2,1,0:T(8,128)S(1)}, f32[2,128,256]{2,1,0:T(8,128)S(1)}, u32[]{:S(2)}, u32[]{:S(2)}) collective-permute-start(f32[2,128,256]{2,1,0:T(8,128)S(1)} %get-tuple-element.48), channel_id=1, source_target_pairs={{6,0},{7,1},{0,6},{1,7},{14,8},{15,9},{8,14},{9,15},{22,16},{23,17... | collective-permute-start | bytes 786440 | tf_op jit(solution)/shard_map/ppermute | solution.py:486
  28.0 0.7 copy-start.3
  28.1 0.7 copy-start.4
  28.8 7.2 %collective-permute-start.2 = (f32[8,512]{1,0:T(8,128)S(1)}, f32[8,512]{1,0:T(8,128)S(1)}, u32[]{:S(2)}, u32[]{:S(2)}) collective-permute-start(f32[8,512]{1,0:T(8,128)S(1)} %concatenate.3.refs_0_), channel_id=1, source_target_pairs={{8,15},{9,14},{10,13},{11,12},{12,11},{13,10},{14,9},{15,8},{24,31... | collective-permute-start | bytes 49160 | tf_op jit(solution)/shard_map/ppermute | solution.py:512
  40.0 2.7 %collective-permute-start.9 = (f32[4,128,256]{2,1,0:T(8,128)S(1)}, f32[4,128,256]{2,1,0:T(8,128)S(1)}, u32[]{:S(2)}, u32[]{:S(2)}) collective-permute-start(f32[4,128,256]{2,1,0:T(8,128)S(1)} %get-tuple-element.51.refs_1_), channel_id=1, source_target_pairs={{0,1},{1,0},{2,3},{3,2},{4,5},{5,4},{6,7},{7,6},{8,9},{9,8},{10,11... | collective-permute-start | bytes 1572872 | tf_op jit(solution)/shard_map/ppermute | solution.py:537
  40.1 7.4 %collective-permute-start.10 = (f32[520,256]{1,0:T(8,128)S(1)}, f32[520,256]{1,0:T(8,128)S(1)}, u32[]{:S(2)}, u32[]{:S(2)}) collective-permute-start(f32[520,256]{1,0:T(8,128)S(1)} %get-tuple-element.50.refs_2_.refs_1_), channel_id=1, source_target_pairs={{0,1},{1,0},{2,3},{3,2},{4,5},{5,4},{6,7},{7,6},{8,9},{9,8},{10,11... | collective-permute-start | bytes 1597448 | tf_op jit(solution)/shard_map/ppermute | solution.py:539
  40.6 12.0 %collective-permute-start.11 = (f32[520,256]{1,0:T(8,128)S(1)}, f32[520,256]{1,0:T(8,128)S(1)}, u32[]{:S(2)}, u32[]{:S(2)}) collective-permute-start(f32[520,256]{1,0:T(8,128)S(1)} %get-tuple-element.50.refs_2_.refs_1_), channel_id=1, source_target_pairs={{1,2},{2,1},{3,4},{4,3},{5,6},{6,5},{7,15},{8,16},{9,10},{10,9},{1... | collective-permute-start | bytes 1597448 | tf_op jit(solution)/shard_map/ppermute | solution.py:538
  42.7 15.6 %collective-permute-start.12 = (f32[4,128,256]{2,1,0:T(8,128)S(1)}, f32[4,128,256]{2,1,0:T(8,128)S(1)}, u32[]{:S(2)}, u32[]{:S(2)}) collective-permute-start(f32[4,128,256]{2,1,0:T(8,128)S(1)} %collective-permute-done.9.refs_4_.refs_2_), channel_id=1, source_target_pairs={{1,2},{2,1},{3,4},{4,3},{5,6},{6,5},{7,15},{8,16},{9,10},{10,9},{1... | collective-permute-start | bytes 1572872 | tf_op jit(solution)/shard_map/ppermute | solution.py:540
  69.9 6.9 %collective-permute-start.13 = (f32[128,256]{1,0:T(8,128)S(1)}, f32[128,256]{1,0:T(8,128)S(1)}, u32[]{:S(2)}, u32[]{:S(2)}) collective-permute-start(f32[128,256]{1,0:T(8,128)S(1)} %get-tuple-element.59), channel_id=1, source_target_pairs={{0,7},{1,6},{2,5},{3,4},{4,3},{5,2},{6,1},{7,0},{8,15},{9,14},{10,... | collective-permute-start | bytes 393224 | tf_op jit(solution)/shard_map/ppermute | solution.py:558
  71.5 14.8 %collective-permute-start.14 = (f32[128,256]{1,0:T(8,128)S(1)}, f32[128,256]{1,0:T(8,128)S(1)}, u32[]{:S(2)}, u32[]{:S(2)}) collective-permute-start(f32[128,256]{1,0:T(8,128)S(1)} %get-tuple-element.60), channel_id=1, source_target_pairs={{0,6},{1,7},{2,4},{3,5},{4,2},{5,3},{6,0},{7,1},{8,14},{9,15},{10,... | collective-permute-start | bytes 393224 | tf_op jit(solution)/shard_map/ppermute | solution.py:558
  72.3 19.0 %collective-permute-start.15 = (f32[128,256]{1,0:T(8,128)S(1)}, f32[128,256]{1,0:T(8,128)S(1)}, u32[]{:S(2)}, u32[]{:S(2)}) collective-permute-start(f32[128,256]{1,0:T(8,128)S(1)} %get-tuple-element.61), channel_id=1, source_target_pairs={{0,5},{1,4},{2,7},{3,6},{4,1},{5,0},{6,3},{7,2},{8,13},{9,12},{10,... | collective-permute-start | bytes 393224 | tf_op jit(solution)/shard_map/ppermute | solution.py:558
  72.3 22.2 %collective-permute-start.16 = (f32[128,256]{1,0:T(8,128)S(1)}, f32[128,256]{1,0:T(8,128)S(1)}, u32[]{:S(2)}, u32[]{:S(2)}) collective-permute-start(f32[128,256]{1,0:T(8,128)S(1)} %get-tuple-element.62), channel_id=1, source_target_pairs={{0,4},{1,5},{2,6},{3,7},{4,0},{5,1},{6,2},{7,3},{8,12},{9,13},{10,... | collective-permute-start | bytes 393224 | tf_op jit(solution)/shard_map/ppermute | solution.py:558
  76.2 18.3 %collective-permute-start.17 = (f32[128,256]{1,0:T(8,128)S(1)}, f32[128,256]{1,0:T(8,128)S(1)}, u32[]{:S(2)}, u32[]{:S(2)}) collective-permute-start(f32[128,256]{1,0:T(8,128)S(1)} %get-tuple-element.63), channel_id=1, source_target_pairs={{0,3},{1,2},{2,1},{3,0},{4,7},{5,6},{6,5},{7,4},{8,11},{9,10},{10,... | collective-permute-start | bytes 393224 | tf_op jit(solution)/shard_map/ppermute | solution.py:558
  76.8 19.4 %collective-permute-start.18 = (f32[128,256]{1,0:T(8,128)S(1)}, f32[128,256]{1,0:T(8,128)S(1)}, u32[]{:S(2)}, u32[]{:S(2)}) collective-permute-start(f32[128,256]{1,0:T(8,128)S(1)} %get-tuple-element.64), channel_id=1, source_target_pairs={{0,2},{1,3},{2,0},{3,1},{4,6},{5,7},{6,4},{7,5},{8,10},{9,11},{10,... | collective-permute-start | bytes 393224 | tf_op jit(solution)/shard_map/ppermute | solution.py:558
  86.3 9.9 %collective-permute-start.19 = (f32[128,256]{1,0:T(8,128)S(1)}, f32[128,256]{1,0:T(8,128)S(1)}, u32[]{:S(2)}, u32[]{:S(2)}) collective-permute-start(f32[128,256]{1,0:T(8,128)S(1)} %get-tuple-element.65), channel_id=1, source_target_pairs={{0,1},{1,0},{2,3},{3,2},{4,5},{5,4},{6,7},{7,6},{8,9},{9,8},{10,11... | collective-permute-start | bytes 393224 | tf_op jit(solution)/shard_map/ppermute | solution.py:558

commit v18 on v17

--- a/solution.py
+++ b/solution.py
@@ -18,13 +18,8 @@
 BF16 = jnp.bfloat16
 
 
-def pack_kernel(info, field_ref, flow_ref, member_ref, first_ref, second_ref, emission_ref):
+def pack_kernel(info, field_ref, flow_ref, first_ref, second_ref):
     members, rows, width = field_ref.shape
-    diagonal = lax.broadcasted_iota(jnp.int32, (members, members), 0) == lax.broadcasted_iota(
-        jnp.int32, (members, members), 1
-    )
-    column = jnp.sum(jnp.where(diagonal, member_ref[...], 0.0), axis=1, keepdims=True)
-    emission_ref[...] = jnp.broadcast_to(column, emission_ref.shape)
     even = info[2] == 0
     for place in range(STEPS):
         tail, head = field_ref[:, rows - STEPS + place, :], field_ref[:, place, :]
@@ -61,9 +56,14 @@
     )
 
 
-def inner_kernel(targets, info, field_ref, flow_ref, emission_ref, kept_ref, *refs):
+def inner_kernel(targets, info, field_ref, flow_ref, member_ref, kept_ref, emission_ref, *refs):
     out_refs, (wide_ref, weight_ref) = refs[:-2], refs[-2:]
-    rows = field_ref.shape[1]
+    members, rows, _ = field_ref.shape
+    diagonal = lax.broadcasted_iota(jnp.int32, (members, members), 0) == lax.broadcasted_iota(
+        jnp.int32, (members, members), 1
+    )
+    column = jnp.sum(jnp.where(diagonal, member_ref[...], 0.0), axis=1, keepdims=True)
+    emission_ref[...] = jnp.broadcast_to(column, emission_ref.shape)
     emission = doubled(emission_ref[...])
     for row in range(1, rows - 1):
         weights = weights_of(flow_ref[:, row, :])
@@ -159,12 +159,20 @@
 
 
 def unpack_kernel(order, info, *refs):
-    row_refs, out_ref = refs[:-1], refs[-1]
-    rows = out_ref.shape[1]
-    for x, ref in zip(order, row_refs):
-        position = (2 * info[0] + info[1]) ^ x
-        row = position + info[2] * (rows - 1 - 2 * position)
-        out_ref[:, pl.ds(row, 1), :] = ref[...][:, None, :]
+    row_refs, (out_hbm, out_ref, sems) = refs[:-3], refs[-3:]
+    members, rows, _ = out_ref.shape
+    part = members // 4
+    moves = []
+    for index in range(4):
+        some = pl.ds(index * part, part)
+        for x, ref in zip(order, row_refs):
+            position = (2 * info[0] + info[1]) ^ x
+            row = position + info[2] * (rows - 1 - 2 * position)
+            out_ref[some, pl.ds(row, 1), :] = ref[some, :][:, None, :]
+        moves.append(pltpu.make_async_copy(out_ref.at[some], out_hbm.at[some], sems.at[index]))
+        moves[-1].start()
+    for move in moves:
+        move.wait()
 
 
 def pieces(x, count):
@@ -426,13 +434,13 @@
     return lax.div(lane, 2), lax.rem(lane, 2), lax.rem(patch, 2), lax.axis_size("member") // 2
 
 
-def call(kernel, name, out_shape, args, scratch=(), flops=None, limit=8):
+def call(kernel, name, out_shape, args, scratch=(), flops=None, limit=8, out=VMEM):
     several = isinstance(out_shape, (list, tuple))
     return pl.pallas_call(
         lambda *refs: kernel(position(), *refs),
         out_shape=out_shape,
         in_specs=[VMEM] * len(args),
-        out_specs=[VMEM] * len(out_shape) if several else VMEM,
+        out_specs=[out] * len(out_shape) if several else out,
         scratch_shapes=scratch,
         compiler_params=pltpu.CompilerParams(vmem_limit_bytes=limit * 1024 * 1024),
         cost_estimate=flops and pl.CostEstimate(flops=flops, bytes_accessed=0, transcendentals=0),
@@ -460,10 +468,7 @@
     count = patches * lanes
 
     edge = array(STEPS * step + 8, width)
-    to_last, to_first, emitted = call(
-        pack_kernel, "pack", [edge, edge, array(step, width // 2)],
-        [init_field, flow_fields, emission[None, :]], limit=32,
-    )
+    to_last, to_first = call(pack_kernel, "pack", [edge, edge], [init_field, flow_fields], limit=32)
 
     def swap(message, start):
         lower = range(start, patches - 1, 2)
@@ -493,14 +498,15 @@
     single = all(len({source for source, _ in hops}) == len(hops) for hops in mirrored)
     targets = mirrored if single else turning
     pair = array(2, step, width)
-    args = [init_field, flow_fields, emitted]
-    kept, *inner = call(
-        functools.partial(inner_kernel, targets), "inner", [array(4, step, width)] + [pair] * chips, args,
+    kept, emitted, *inner = call(
+        functools.partial(inner_kernel, targets), "inner",
+        [array(4, step, width), array(step, width // 2)] + [pair] * chips,
+        [init_field, flow_fields, emission[None, :]],
         [pltpu.VMEM((rows, step, width), F32), pltpu.VMEM((rows, 8, width), F32)], limit=32,
     )
     got_inner = [inner[0]] + [between(inner[s], targets[s]) for s in range(1, chips)]
     outer = call(
-        edge_kernel, "edge", [pair] * chips, args + [kept, halo_last, halo_first],
+        edge_kernel, "edge", [pair] * chips, [init_field, flow_fields, emitted, kept, halo_last, halo_first],
         [pltpu.VMEM((2, step, width), F32)], limit=32,
     )
     got_outer = [outer[0]] + [
@@ -560,7 +566,8 @@
     order = sorted(range(lanes), key=lambda x: (x.bit_length() != lanes.bit_length() - 1, -x))
     return call(
         functools.partial(unpack_kernel, order), "unpack", array(step, rows, width),
-        [swapped(x) for x in order], limit=48,
+        [swapped(x) for x in order], [pltpu.VMEM((step, rows, width), F32), pltpu.SemaphoreType.DMA((4,))],
+        limit=48, out=pl.BlockSpec(memory_space=pltpu.HBM),
     )
 
 

time: 97.5 us -> 95 us (0.974)
  Pallas kernels: 19.6 us -> 17.8 us
    pallas_call x7, Pallas kernels: 19.6 us -> 17.8 us  [call(): pl.pallas_call(lambda *refs: kernel(position(), *refs), out_shape=out_sha...]
  transfers between devices with their start and end apart: 20 -> 20, of which waited for: 9 -> 8; matrix products, arithmetic and copies ran while one was open for 0% -> 0% of each run, Pallas kernels for 6% -> 6%
where the time goes in v18:
time: 95 us; the launch traced here: 95.2 us
  starting transfers between devices  47.5 us (50%)
  waiting for transfers between devices  26.1 us (27%)
  Pallas kernels  17.8 us (19%)
  local copies, waits for them, and re-layouts  2.71 us (3%)
  between operations  1.09 us (1%)
    pallas_call x7, Pallas kernels, call(): pl.pallas_call(lambda *refs: kernel(position(), *refs), out_shape=out_sha...  17.8 us
    ppermute x7, starting transfers between devices, swapped(): lax.ppermute(analysed[x], 'member', [(i, i ^ x) for i in range(lanes)])  16.7 us
    ppermute x6, starting transfers between devices, between(): lax.ppermute(message, 'member', [(2 * a + core, 2 * b + core) for a, b in...  16.4 us
    ppermute x7, waiting for transfers between devices, swapped(): lax.ppermute(analysed[x], 'member', [(i, i ^ x) for i in range(lanes)])  9.62 us
    ppermute x1, waiting for transfers between devices, per_device(): got_rest = lax.ppermute(far_own, axes, borders)  5.62 us
    ppermute x1, waiting for transfers between devices, per_device(): lax.ppermute(mine, axes, [(p * lanes + i, p * lanes + lanes - 1 - i) for...  5.27 us
    ppermute x2, starting transfers between devices, swap(): lax.ppermute(message, 'patch', [(p, p + 1) for p in lower] + [(p + 1, p)...  5.06 us
    ppermute x1, starting transfers between devices, per_device(): got_rest = lax.ppermute(far_own, axes, borders)  4.81 us
  transfers between devices with their start and end apart: 20, of which 8 were waited for; matrix products, arithmetic and copies ran while one was open for 0% of the time, Pallas kernels for 6%

profile of v18, /device:TPU:2, one launch (start us, length us, event | category | flops | bytes accessed | tf_op | source)
XLA Modules:
  0.0 95.2 jit_solution(10139152863451674979)
XLA Ops:
  0.0 0.0 copy-start
  0.0 1.2 %copy-done = f32[128,8,256]{2,1,0:T(8,128)S(1)} copy-done((f32[128,8,256]{2,1,0:T(8,128)S(1)}, f32[128,8,256]{2,1,0:T(8,128)}, u32[]{:S(2)}) %copy-start) | copy-done | bytes 1048600
  1.2 0.0 copy-start.1
  1.2 0.8 copy-done.1
  2.0 0.3 pack.1
  2.3 0.1 collective-permute-start
  2.4 0.0 copy-start.2
  2.4 5.0 %collective-permute-start.1 = (f32[264,256]{1,0:T(8,128)S(1)}, f32[264,256]{1,0:T(8,128)S(1)}, u32[]{:S(2)}, u32[]{:S(2)}) collective-permute-start(f32[264,256]{1,0:T(8,128)S(1)} %get-tuple-element.39), channel_id=1, source_target_pairs={{8,16},{16,8},{9,17},{17,9},{10,18},{18,10},{11,19},{19,11},{12,20... | collective-permute-start | bytes 811016 | tf_op jit(solution)/shard_map/ppermute | solution.py:475
  7.4 0.0 copy-done.2
  7.4 1.6 %inner.1 = (f32[4,128,256]{2,1,0:T(8,128)S(1)}, f32[128,128]{1,0:T(8,128)S(1)}, f32[2,128,256]{2,1,0:T(8,128)S(1)}, f32[2,128,256]{2,1,0:T(8,128)S(1)}, f32[2,12...) custom-call(f32[128,8,256]{2,1,0:T(8,128)S(1)} %copy-done, f32[4,8,256]{2,1,0:T(8,128)S(1)} %copy-done.1, f32[1,128]{1,0:T(1,128)S(1)} %bitcast.2), custom_call_target="tpu_custom_call" | custom-call | tf_op jit(solution)/shard_map/inner/pallas_call | solution.py:439
  9.0 0.7 collective-permute-start.3
  9.6 6.2 %collective-permute-start.4 = (f32[2,128,256]{2,1,0:T(8,128)S(1)}, f32[2,128,256]{2,1,0:T(8,128)S(1)}, u32[]{:S(2)}, u32[]{:S(2)}) collective-permute-start(f32[2,128,256]{2,1,0:T(8,128)S(1)} %get-tuple-element.44), channel_id=1, source_target_pairs={{6,2},{7,3},{0,4},{1,5},{14,10},{15,11},{8,12},{9,13},{22,18},{23,... | collective-permute-start | bytes 786440 | tf_op jit(solution)/shard_map/ppermute | solution.py:491
  15.8 1.4 %collective-permute-start.5 = (f32[2,128,256]{2,1,0:T(8,128)S(1)}, f32[2,128,256]{2,1,0:T(8,128)S(1)}, u32[]{:S(2)}, u32[]{:S(2)}) collective-permute-start(f32[2,128,256]{2,1,0:T(8,128)S(1)} %get-tuple-element.45), channel_id=1, source_target_pairs={{0,2},{1,3},{6,4},{7,5},{8,10},{9,11},{14,12},{15,13},{16,18},{17,... | collective-permute-start | bytes 786440 | tf_op jit(solution)/shard_map/ppermute | solution.py:491
  17.3 0.0 collective-permute-done.refs_4_
  17.3 0.0 collective-permute-done.1.refs_5_
  17.3 0.9 edge.1
  18.3 1.3 %collective-permute-start.6 = (f32[2,128,256]{2,1,0:T(8,128)S(1)}, f32[2,128,256]{2,1,0:T(8,128)S(1)}, u32[]{:S(2)}, u32[]{:S(2)}) collective-permute-start(f32[2,128,256]{2,1,0:T(8,128)S(1)} %get-tuple-element.46), channel_id=1, source_target_pairs={{2,0},{3,1},{4,6},{5,7},{10,8},{11,9},{12,14},{13,15},{18,16},{19,... | collective-permute-start | bytes 786440 | tf_op jit(solution)/shard_map/ppermute | solution.py:491
  19.6 1.3 %collective-permute-start.7 = (f32[2,128,256]{2,1,0:T(8,128)S(1)}, f32[2,128,256]{2,1,0:T(8,128)S(1)}, u32[]{:S(2)}, u32[]{:S(2)}) collective-permute-start(f32[2,128,256]{2,1,0:T(8,128)S(1)} %get-tuple-element.47), channel_id=1, source_target_pairs={{4,0},{5,1},{2,6},{3,7},{12,8},{13,9},{10,14},{11,15},{20,16},{21,... | collective-permute-start | bytes 786440 | tf_op jit(solution)/shard_map/ppermute | solution.py:491
  20.9 0.0 collective-permute-done.3.refs_3_
  20.9 0.0 copy-start.5
  20.9 5.5 %collective-permute-start.8 = (f32[2,128,256]{2,1,0:T(8,128)S(1)}, f32[2,128,256]{2,1,0:T(8,128)S(1)}, u32[]{:S(2)}, u32[]{:S(2)}) collective-permute-start(f32[2,128,256]{2,1,0:T(8,128)S(1)} %get-tuple-element.48), channel_id=1, source_target_pairs={{6,0},{7,1},{0,6},{1,7},{14,8},{15,9},{8,14},{9,15},{22,16},{23,17... | collective-permute-start | bytes 786440 | tf_op jit(solution)/shard_map/ppermute | solution.py:491
  27.0 0.0 copy-done.5
  27.1 0.0 copy-start.3
  27.1 0.0 copy-start.4
  27.1 0.6 copy-done.3
  27.8 0.0 copy-done.4
  27.8 0.0 collective-permute-done.4.refs_4_
  27.8 1.9 %collective-permute-start.2 = (f32[8,512]{1,0:T(8,128)S(1)}, f32[8,512]{1,0:T(8,128)S(1)}, u32[]{:S(2)}, u32[]{:S(2)}) collective-permute-start(f32[8,512]{1,0:T(8,128)S(1)} %concatenate.3.refs_0_), channel_id=1, source_target_pairs={{8,15},{9,14},{10,13},{11,12},{12,11},{13,10},{14,9},{15,8},{24,31... | collective-permute-start | bytes 49160 | tf_op jit(solution)/shard_map/ppermute | solution.py:518
  29.7 0.0 collective-permute-done.5.refs_5_
  29.8 5.3 %collective-permute-done.2.refs_1_ = f32[8,512]{1,0:T(8,128)S(1)} collective-permute-done((f32[8,512]{1,0:T(8,128)S(1)}, f32[8,512]{1,0:T(8,128)S(1)}, u32[]{:S(2)}, u32[]{:S(2)}) %collective-permute-start.2) | collective-permute-done | bytes 16416 | tf_op jit(solution)/shard_map/ppermute | solution.py:518
  35.0 3.9 %collective-permute-done.6.refs_7_ = f32[2,128,256]{2,1,0:T(8,128)S(1)} collective-permute-done((f32[2,128,256]{2,1,0:T(8,128)S(1)}, f32[2,128,256]{2,1,0:T(8,128)S(1)}, u32[]{:S(2)}, u32[]{:S(2)}) %collective-permute-start.6) | collective-permute-done | bytes 262176 | tf_op jit(solution)/shard_map/ppermute | solution.py:491
  38.9 0.0 collective-permute-done.7.refs_8_
  38.9 0.0 collective-permute-done.8.refs_9_
  38.9 0.1 collect.1
  39.0 0.1 collective-permute-start.9
  39.1 0.5 collective-permute-start.10
  39.6 2.1 %collective-permute-start.11 = (f32[520,256]{1,0:T(8,128)S(1)}, f32[520,256]{1,0:T(8,128)S(1)}, u32[]{:S(2)}, u32[]{:S(2)}) collective-permute-start(f32[520,256]{1,0:T(8,128)S(1)} %get-tuple-element.50.refs_2_.refs_1_), channel_id=1, source_target_pairs={{1,2},{2,1},{3,4},{4,3},{5,6},{6,5},{7,15},{8,16},{9,10},{10,9},{1... | collective-permute-start | bytes 1597448 | tf_op jit(solution)/shard_map/ppermute | solution.py:544
  41.7 0.0 collective-permute-done.9.refs_4_.refs_2_
  41.7 4.8 %collective-permute-start.12 = (f32[4,128,256]{2,1,0:T(8,128)S(1)}, f32[4,128,256]{2,1,0:T(8,128)S(1)}, u32[]{:S(2)}, u32[]{:S(2)}) collective-permute-start(f32[4,128,256]{2,1,0:T(8,128)S(1)} %collective-permute-done.9.refs_4_.refs_2_), channel_id=1, source_target_pairs={{1,2},{2,1},{3,4},{4,3},{5,6},{6,5},{7,15},{8,16},{9,10},{10,9},{1... | collective-permute-start | bytes 1572872 | tf_op jit(solution)/shard_map/ppermute | solution.py:546
  46.5 0.0 collective-permute-done.10.refs_3_
  46.6 3.4 %prepare.1 = (bf16[1024,512]{1,0:T(8,128)(2,1)S(1)}, bf16[1024,512]{1,0:T(8,128)(2,1)S(1)}, bf16[256,1024]{1,0:T(8,128)(2,1)S(1)}, bf16[256,1024]{1,0:T(8,128)(2...) custom-call(f32[8,512]{1,0:T(8,128)S(1)} %get-tuple-element.49.refs_0_, ...), custom_call_target="tpu_custom_call" | custom-call | flops 1073741824 | tf_op jit(solution)/shard_map/prepare/pallas_call | solution.py:439
  50.0 1.7 %collective-permute-done.11.refs_10_ = f32[520,256]{1,0:T(8,128)S(1)} collective-permute-done((f32[520,256]{1,0:T(8,128)S(1)}, f32[520,256]{1,0:T(8,128)S(1)}, u32[]{:S(2)}, u32[]{:S(2)}) %collective-permute-start.11) | collective-permute-done | bytes 532512 | tf_op jit(solution)/shard_map/ppermute | solution.py:544
  51.7 5.6 %collective-permute-done.12.refs_11_ = f32[4,128,256]{2,1,0:T(8,128)S(1)} collective-permute-done((f32[4,128,256]{2,1,0:T(8,128)S(1)}, f32[4,128,256]{2,1,0:T(8,128)S(1)}, u32[]{:S(2)}, u32[]{:S(2)}) %collective-permute-start.12) | collective-permute-done | bytes 524320 | tf_op jit(solution)/shard_map/ppermute | solution.py:546
  57.3 10.4 %region.1 = (f32[128,256]{1,0:T(8,128)S(1)}, f32[128,256]{1,0:T(8,128)S(1)}, f32[128,256]{1,0:T(8,128)S(1)}, f32[128,256]{1,0:T(8,128)S(1)}, f32[128,256]{1,0:T(...) custom-call(f32[8,512]{1,0:T(8,128)S(1)} %get-tuple-element.49.refs_0_, ...), custom_call_target="tpu_custom_call" | custom-call | tf_op jit(solution)/shard_map/region/pallas_call | solution.py:439
  67.7 2.2 %collective-permute-start.13 = (f32[128,256]{1,0:T(8,128)S(1)}, f32[128,256]{1,0:T(8,128)S(1)}, u32[]{:S(2)}, u32[]{:S(2)}) collective-permute-start(f32[128,256]{1,0:T(8,128)S(1)} %get-tuple-element.59), channel_id=1, source_target_pairs={{0,7},{1,6},{2,5},{3,4},{4,3},{5,2},{6,1},{7,0},{8,15},{9,14},{10,... | collective-permute-start | bytes 393224 | tf_op jit(solution)/shard_map/ppermute | solution.py:564
  69.9 0.2 collective-permute-start.14
  70.1 0.0 collective-permute-start.15
  70.1 3.8 %collective-permute-start.16 = (f32[128,256]{1,0:T(8,128)S(1)}, f32[128,256]{1,0:T(8,128)S(1)}, u32[]{:S(2)}, u32[]{:S(2)}) collective-permute-start(f32[128,256]{1,0:T(8,128)S(1)} %get-tuple-element.62), channel_id=1, source_target_pairs={{0,4},{1,5},{2,6},{3,7},{4,0},{5,1},{6,2},{7,3},{8,12},{9,13},{10,... | collective-permute-start | bytes 393224 | tf_op jit(solution)/shard_map/ppermute | solution.py:564
  73.9 0.0 collective-permute-start.17
  74.0 0.6 collective-permute-done.13.refs_0_
  74.6 10.3 %collective-permute-start.18 = (f32[128,256]{1,0:T(8,128)S(1)}, f32[128,256]{1,0:T(8,128)S(1)}, u32[]{:S(2)}, u32[]{:S(2)}) collective-permute-start(f32[128,256]{1,0:T(8,128)S(1)} %get-tuple-element.64), channel_id=1, source_target_pairs={{0,2},{1,3},{2,0},{3,1},{4,6},{5,7},{6,4},{7,5},{8,10},{9,11},{10,... | collective-permute-start | bytes 393224 | tf_op jit(solution)/shard_map/ppermute | solution.py:564
  84.9 0.0 collective-permute-done.14.refs_1_
  84.9 0.0 collective-permute-start.19
  84.9 5.2 %collective-permute-done.15.refs_2_ = f32[128,256]{1,0:T(8,128)S(1)} collective-permute-done((f32[128,256]{1,0:T(8,128)S(1)}, f32[128,256]{1,0:T(8,128)S(1)}, u32[]{:S(2)}, u32[]{:S(2)}) %collective-permute-start.15) | collective-permute-done | bytes 131104 | tf_op jit(solution)/shard_map/ppermute | solution.py:564
  90.1 2.5 %collective-permute-done.16.refs_3_ = f32[128,256]{1,0:T(8,128)S(1)} collective-permute-done((f32[128,256]{1,0:T(8,128)S(1)}, f32[128,256]{1,0:T(8,128)S(1)}, u32[]{:S(2)}, u32[]{:S(2)}) %collective-permute-start.16) | collective-permute-done | bytes 131104 | tf_op jit(solution)/shard_map/ppermute | solution.py:564
  92.5 0.0 collective-permute-done.17.refs_4_
  92.5 1.4 %collective-permute-done.18.refs_5_ = f32[128,256]{1,0:T(8,128)S(1)} collective-permute-done((f32[128,256]{1,0:T(8,128)S(1)}, f32[128,256]{1,0:T(8,128)S(1)}, u32[]{:S(2)}, u32[]{:S(2)}) %collective-permute-start.18) | collective-permute-done | bytes 131104 | tf_op jit(solution)/shard_map/ppermute | solution.py:564
  94.0 0.0 collective-permute-done.19.refs_6_
  94.0 1.1 %unpack.1 = f32[128,8,256]{2,1,0:T(8,128)} custom-call(f32[128,256]{1,0:T(8,128)S(1)} %collective-permute-done.13.refs_0_, f32[128,256]{1,0:T(8,128)S(1)} %collective-permute-done.14.refs_1_, f32[128,256]{1,0:T(8,128)S(1)} %collective-permute-done.15.refs_2_, f32[128,256]{1,0:T(8,128)S(1)} %collective-permute-done.16.refs_3_, ...), custom_call_target="tpu_custom_call" | custom-call | tf_op jit(solution)/shard_map/unpack/pallas_call | solution.py:439
  (3 shorter events, 0.0 us)
Async XLA Ops:
  0.0 1.2 %copy-start = (f32[128,8,256]{2,1,0:T(8,128)S(1)}, f32[128,8,256]{2,1,0:T(8,128)}, u32[]{:S(2)}) copy-start(f32[128,8,256]{2,1,0:T(8,128)} %refs_0_.5) | copy-start | bytes 3145732
  1.2 0.8 copy-start.1
  2.3 15.0 %collective-permute-start = (f32[264,256]{1,0:T(8,128)S(1)}, f32[264,256]{1,0:T(8,128)S(1)}, u32[]{:S(2)}, u32[]{:S(2)}) collective-permute-start(f32[264,256]{1,0:T(8,128)S(1)} %get-tuple-element.38), channel_id=1, source_target_pairs={{0,8},{16,24},{8,0},{24,16},{1,9},{17,25},{9,1},{25,17},{2,10},{18... | collective-permute-start | bytes 811016 | tf_op jit(solution)/shard_map/ppermute | solution.py:475
  2.4 5.0 %copy-start.2 = (f32[128]{0:T(128)S(1)}, f32[128]{0:T(128)}, u32[]{:S(2)}) copy-start(f32[128]{0:T(128)} %param.9) | copy-start | bytes 1540
  2.4 14.9 %collective-permute-start.1 = (f32[264,256]{1,0:T(8,128)S(1)}, f32[264,256]{1,0:T(8,128)S(1)}, u32[]{:S(2)}, u32[]{:S(2)}) collective-permute-start(f32[264,256]{1,0:T(8,128)S(1)} %get-tuple-element.39), channel_id=1, source_target_pairs={{8,16},{16,8},{9,17},{17,9},{10,18},{18,10},{11,19},{19,11},{12,20... | collective-permute-start | bytes 811016 | tf_op jit(solution)/shard_map/ppermute | solution.py:475
  9.0 11.9 %collective-permute-start.3 = (f32[2,128,256]{2,1,0:T(8,128)S(1)}, f32[2,128,256]{2,1,0:T(8,128)S(1)}, u32[]{:S(2)}, u32[]{:S(2)}) collective-permute-start(f32[2,128,256]{2,1,0:T(8,128)S(1)} %get-tuple-element.43), channel_id=1, source_target_pairs={{4,2},{5,3},{2,4},{3,5},{12,10},{13,11},{10,12},{11,13},{20,18},{2... | collective-permute-start | bytes 786440 | tf_op jit(solution)/shard_map/ppermute | solution.py:491
  9.6 18.2 %collective-permute-start.4 = (f32[2,128,256]{2,1,0:T(8,128)S(1)}, f32[2,128,256]{2,1,0:T(8,128)S(1)}, u32[]{:S(2)}, u32[]{:S(2)}) collective-permute-start(f32[2,128,256]{2,1,0:T(8,128)S(1)} %get-tuple-element.44), channel_id=1, source_target_pairs={{6,2},{7,3},{0,4},{1,5},{14,10},{15,11},{8,12},{9,13},{22,18},{23,... | collective-permute-start | bytes 786440 | tf_op jit(solution)/shard_map/ppermute | solution.py:491
  15.8 13.9 %collective-permute-start.5 = (f32[2,128,256]{2,1,0:T(8,128)S(1)}, f32[2,128,256]{2,1,0:T(8,128)S(1)}, u32[]{:S(2)}, u32[]{:S(2)}) collective-permute-start(f32[2,128,256]{2,1,0:T(8,128)S(1)} %get-tuple-element.45), channel_id=1, source_target_pairs={{0,2},{1,3},{6,4},{7,5},{8,10},{9,11},{14,12},{15,13},{16,18},{17,... | collective-permute-start | bytes 786440 | tf_op jit(solution)/shard_map/ppermute | solution.py:491
  18.3 20.7 %collective-permute-start.6 = (f32[2,128,256]{2,1,0:T(8,128)S(1)}, f32[2,128,256]{2,1,0:T(8,128)S(1)}, u32[]{:S(2)}, u32[]{:S(2)}) collective-permute-start(f32[2,128,256]{2,1,0:T(8,128)S(1)} %get-tuple-element.46), channel_id=1, source_target_pairs={{2,0},{3,1},{4,6},{5,7},{10,8},{11,9},{12,14},{13,15},{18,16},{19,... | collective-permute-start | bytes 786440 | tf_op jit(solution)/shard_map/ppermute | solution.py:491
  19.6 19.4 %collective-permute-start.7 = (f32[2,128,256]{2,1,0:T(8,128)S(1)}, f32[2,128,256]{2,1,0:T(8,128)S(1)}, u32[]{:S(2)}, u32[]{:S(2)}) collective-permute-start(f32[2,128,256]{2,1,0:T(8,128)S(1)} %get-tuple-element.47), channel_id=1, source_target_pairs={{4,0},{5,1},{2,6},{3,7},{12,8},{13,9},{10,14},{11,15},{20,16},{21,... | collective-permute-start | bytes 786440 | tf_op jit(solution)/shard_map/ppermute | solution.py:491
  20.9 6.2 %copy-start.5 = (s32[1,512]{1,0:T(1,128)S(1)}, s32[1,512]{1,0:T(1,128)}, u32[]{:S(2)}) copy-start(s32[1,512]{1,0:T(1,128)} %param.10) | copy-start | bytes 6148
  20.9 18.0 %collective-permute-start.8 = (f32[2,128,256]{2,1,0:T(8,128)S(1)}, f32[2,128,256]{2,1,0:T(8,128)S(1)}, u32[]{:S(2)}, u32[]{:S(2)}) collective-permute-start(f32[2,128,256]{2,1,0:T(8,128)S(1)} %get-tuple-element.48), channel_id=1, source_target_pairs={{6,0},{7,1},{0,6},{1,7},{14,8},{15,9},{8,14},{9,15},{22,16},{23,17... | collective-permute-start | bytes 786440 | tf_op jit(solution)/shard_map/ppermute | solution.py:491
  27.1 0.7 copy-start.3
  27.1 0.7 copy-start.4
  27.8 7.2 %collective-permute-start.2 = (f32[8,512]{1,0:T(8,128)S(1)}, f32[8,512]{1,0:T(8,128)S(1)}, u32[]{:S(2)}, u32[]{:S(2)}) collective-permute-start(f32[8,512]{1,0:T(8,128)S(1)} %concatenate.3.refs_0_), channel_id=1, source_target_pairs={{8,15},{9,14},{10,13},{11,12},{12,11},{13,10},{14,9},{15,8},{24,31... | collective-permute-start | bytes 49160 | tf_op jit(solution)/shard_map/ppermute | solution.py:518
  39.0 2.7 %collective-permute-start.9 = (f32[4,128,256]{2,1,0:T(8,128)S(1)}, f32[4,128,256]{2,1,0:T(8,128)S(1)}, u32[]{:S(2)}, u32[]{:S(2)}) collective-permute-start(f32[4,128,256]{2,1,0:T(8,128)S(1)} %get-tuple-element.51.refs_1_), channel_id=1, source_target_pairs={{0,1},{1,0},{2,3},{3,2},{4,5},{5,4},{6,7},{7,6},{8,9},{9,8},{10,11... | collective-permute-start | bytes 1572872 | tf_op jit(solution)/shard_map/ppermute | solution.py:543
  39.1 7.4 %collective-permute-start.10 = (f32[520,256]{1,0:T(8,128)S(1)}, f32[520,256]{1,0:T(8,128)S(1)}, u32[]{:S(2)}, u32[]{:S(2)}) collective-permute-start(f32[520,256]{1,0:T(8,128)S(1)} %get-tuple-element.50.refs_2_.refs_1_), channel_id=1, source_target_pairs={{0,1},{1,0},{2,3},{3,2},{4,5},{5,4},{6,7},{7,6},{8,9},{9,8},{10,11... | collective-permute-start | bytes 1597448 | tf_op jit(solution)/shard_map/ppermute | solution.py:545
  39.6 12.0 %collective-permute-start.11 = (f32[520,256]{1,0:T(8,128)S(1)}, f32[520,256]{1,0:T(8,128)S(1)}, u32[]{:S(2)}, u32[]{:S(2)}) collective-permute-start(f32[520,256]{1,0:T(8,128)S(1)} %get-tuple-element.50.refs_2_.refs_1_), channel_id=1, source_target_pairs={{1,2},{2,1},{3,4},{4,3},{5,6},{6,5},{7,15},{8,16},{9,10},{10,9},{1... | collective-permute-start | bytes 1597448 | tf_op jit(solution)/shard_map/ppermute | solution.py:544
  41.7 15.5 %collective-permute-start.12 = (f32[4,128,256]{2,1,0:T(8,128)S(1)}, f32[4,128,256]{2,1,0:T(8,128)S(1)}, u32[]{:S(2)}, u32[]{:S(2)}) collective-permute-start(f32[4,128,256]{2,1,0:T(8,128)S(1)} %collective-permute-done.9.refs_4_.refs_2_), channel_id=1, source_target_pairs={{1,2},{2,1},{3,4},{4,3},{5,6},{6,5},{7,15},{8,16},{9,10},{10,9},{1... | collective-permute-start | bytes 1572872 | tf_op jit(solution)/shard_map/ppermute | solution.py:546
  67.7 6.9 %collective-permute-start.13 = (f32[128,256]{1,0:T(8,128)S(1)}, f32[128,256]{1,0:T(8,128)S(1)}, u32[]{:S(2)}, u32[]{:S(2)}) collective-permute-start(f32[128,256]{1,0:T(8,128)S(1)} %get-tuple-element.59), channel_id=1, source_target_pairs={{0,7},{1,6},{2,5},{3,4},{4,3},{5,2},{6,1},{7,0},{8,15},{9,14},{10,... | collective-permute-start | bytes 393224 | tf_op jit(solution)/shard_map/ppermute | solution.py:564
  69.9 15.0 %collective-permute-start.14 = (f32[128,256]{1,0:T(8,128)S(1)}, f32[128,256]{1,0:T(8,128)S(1)}, u32[]{:S(2)}, u32[]{:S(2)}) collective-permute-start(f32[128,256]{1,0:T(8,128)S(1)} %get-tuple-element.60), channel_id=1, source_target_pairs={{0,6},{1,7},{2,4},{3,5},{4,2},{5,3},{6,0},{7,1},{8,14},{9,15},{10,... | collective-permute-start | bytes 393224 | tf_op jit(solution)/shard_map/ppermute | solution.py:564
  70.1 19.9 %collective-permute-start.15 = (f32[128,256]{1,0:T(8,128)S(1)}, f32[128,256]{1,0:T(8,128)S(1)}, u32[]{:S(2)}, u32[]{:S(2)}) collective-permute-start(f32[128,256]{1,0:T(8,128)S(1)} %get-tuple-element.61), channel_id=1, source_target_pairs={{0,5},{1,4},{2,7},{3,6},{4,1},{5,0},{6,3},{7,2},{8,13},{9,12},{10,... | collective-permute-start | bytes 393224 | tf_op jit(solution)/shard_map/ppermute | solution.py:564
  70.1 22.4 %collective-permute-start.16 = (f32[128,256]{1,0:T(8,128)S(1)}, f32[128,256]{1,0:T(8,128)S(1)}, u32[]{:S(2)}, u32[]{:S(2)}) collective-permute-start(f32[128,256]{1,0:T(8,128)S(1)} %get-tuple-element.62), channel_id=1, source_target_pairs={{0,4},{1,5},{2,6},{3,7},{4,0},{5,1},{6,2},{7,3},{8,12},{9,13},{10,... | collective-permute-start | bytes 393224 | tf_op jit(solution)/shard_map/ppermute | solution.py:564
  73.9 18.6 %collective-permute-start.17 = (f32[128,256]{1,0:T(8,128)S(1)}, f32[128,256]{1,0:T(8,128)S(1)}, u32[]{:S(2)}, u32[]{:S(2)}) collective-permute-start(f32[128,256]{1,0:T(8,128)S(1)} %get-tuple-element.63), channel_id=1, source_target_pairs={{0,3},{1,2},{2,1},{3,0},{4,7},{5,6},{6,5},{7,4},{8,11},{9,10},{10,... | collective-permute-start | bytes 393224 | tf_op jit(solution)/shard_map/ppermute | solution.py:564
  74.6 19.4 %collective-permute-start.18 = (f32[128,256]{1,0:T(8,128)S(1)}, f32[128,256]{1,0:T(8,128)S(1)}, u32[]{:S(2)}, u32[]{:S(2)}) collective-permute-start(f32[128,256]{1,0:T(8,128)S(1)} %get-tuple-element.64), channel_id=1, source_target_pairs={{0,2},{1,3},{2,0},{3,1},{4,6},{5,7},{6,4},{7,5},{8,10},{9,11},{10,... | collective-permute-start | bytes 393224 | tf_op jit(solution)/shard_map/ppermute | solution.py:564
  84.9 9.0 %collective-permute-start.19 = (f32[128,256]{1,0:T(8,128)S(1)}, f32[128,256]{1,0:T(8,128)S(1)}, u32[]{:S(2)}, u32[]{:S(2)}) collective-permute-start(f32[128,256]{1,0:T(8,128)S(1)} %get-tuple-element.65), channel_id=1, source_target_pairs={{0,1},{1,0},{2,3},{3,2},{4,5},{5,4},{6,7},{7,6},{8,9},{9,8},{10,11... | collective-permute-start | bytes 393224 | tf_op jit(solution)/shard_map/ppermute | solution.py:564

commit v19 on v18

--- a/solution.py
+++ b/solution.py
@@ -304,53 +304,106 @@
     return upper, jnp.concatenate([upper[:, half:].T, lower], axis=1)
 
 
+def at_border(info):
+    chip, core, _, chips = info
+    ends = jnp.logical_or(jnp.logical_and(chip == 0, core == 0), jnp.logical_and(chip == chips - 1, core == 1))
+    return jnp.where(ends, 0, 1)
+
+
+def shifted_spread(rows, blocks, direction_ref, shift, along, chosen, scale, high_in, low_in, high_out, low_out):
+    total, taken = None, None
+    step = rows[0].shape[0]
+    for index, (row, block) in enumerate(zip(rows, blocks)):
+        here = pl.ds(index * step, step)
+        direction = doubled(direction_ref[block, :])
+        rest = row[...] - shift - direction * along
+        total = rest if total is None else total + rest
+        taken = direction * rest if taken is None else taken + direction * rest
+        high, low = pieces(rest, 2)
+        high, low = pieces((dot(high, chosen) + dot(low, chosen)) * scale, 2)
+        high_out[here, :] = high + high_in[block, :]
+        low_out[here, :] = low + low_in[block, :]
+    return jnp.sum(total, axis=0, keepdims=True), jnp.sum(taken, axis=0, keepdims=True)
+
+
+def gram(high, low):
+    turned = high.T
+    cross = dot(turned, low)
+    return dot(turned, high) + (cross + cross.T)
+
+
+def middle_kernel(
+    info, observed_ref, high_in, low_in, own_high, own_low, direction_ref, half_ref,
+    high_ref, low_ref, gram_ref, right_ref, known_ref,
+):
+    chips = info[3]
+    count, slots = high_ref.shape
+    step = count // chips
+    width = half_ref.shape[1]
+    first = at_border(info) * count
+    cells, _, _, scale = observations(info, observed_ref, width, math.sqrt(2 * count - 1))
+    chosen = one_hot(cells, 0, width)
+    rows = [half_ref.at[pl.ds(chip * step, step), :] for chip in range(chips)]
+    blocks = [pl.ds(pl.multiple_of(first + chip * step, step), step) for chip in range(chips)]
+    mean = mean_of([row[...] for row in rows], count)
+    along, weight = None, None
+    for row, block in zip(rows, blocks):
+        direction = direction_ref[block, :]
+        term = (row[...] - mean) * doubled(direction)
+        along = term if along is None else along + term
+        weight = direction * direction if weight is None else weight + direction * direction
+    weight = doubled(jnp.sum(weight, axis=0, keepdims=True))
+    along = jnp.sum(along, axis=0, keepdims=True) / jnp.maximum(weight, 0.1)
+    total, taken = shifted_spread(
+        rows, blocks, direction_ref, mean, along, chosen, scale, high_in, low_in, high_ref, low_ref
+    )
+    for index, known in enumerate((mean, along, total, taken)):
+        known_ref[pl.ds(index, 1), :] = known
+    high, low = high_ref[...], low_ref[...]
+    gram_ref[...] = gram(high, low)
+    members = pl.ds(pl.multiple_of(first, count), count)
+    right_ref[...] = product([own_high[:, members], own_low[:, members]], [high, low])
+
+
 def region_kernel(
     info, observed_ref, near_own, far_own, high_in, low_in, own_high, own_low, own_part, seen_ref,
-    direction_ref, half_ref, rest_ref, *refs,
+    direction_ref, high_half, low_half, gram_half, right_half, known_ref, rest_ref, *refs,
 ):
     chips, step, width = far_own.shape
     out_refs = refs[:-5]
-    spread_high, spread_low, factor, squared, answer = refs[-5:]
-    members = 2 * chips * step
+    high_rest, low_rest, factor, squared, answer = refs[-5:]
+    count = chips * step
+    members = 2 * count
     slots = observed_ref.shape[1]
     root = math.sqrt(members - 1)
-    core = info[1]
-    ends = jnp.logical_or(
-        jnp.logical_and(info[0] == 0, core == 0), jnp.logical_and(info[0] == chips - 1, core == 1)
-    )
-    part = jnp.where(ends, 0, 1)
+    part = at_border(info)
+    first = (1 - part) * count
     cells, slot_weight, values, scale = observations(info, observed_ref, width, root)
     chosen = one_hot(cells, 0, width)
-
-    def rows_at(half, chip):
-        return pl.ds(pl.multiple_of((half * chips + chip) * step, step), step)
-
-    blocks = [(half_ref.at[pl.ds(chip * step, step), :], rows_at(part, chip)) for chip in range(chips)]
-    blocks += [(rest_ref.at[chip], rows_at(1 - part, chip)) for chip in range(chips)]
-    mean = mean_of([ref[...] for ref, _ in blocks], members)
-    taken = None
-    for ref, block in blocks:
-        term = (ref[...] - mean) * doubled(direction_ref[block, :])
-        taken = term if taken is None else taken + term
-    taken = jnp.sum(taken, axis=0, keepdims=True)
-    seen_mean = seen_ref[pl.ds(0, 1), :] + at_cells(mean, chosen)
-    common = (seen_ref[pl.ds(1, 1), :] + at_cells(taken, chosen)) * scale
+    shift, along, total, taken = (known_ref[pl.ds(index, 1), :] for index in range(4))
+    more, further = shifted_spread(
+        [rest_ref.at[chip] for chip in range(chips)],
+        [pl.ds(pl.multiple_of(first + chip * step, step), step) for chip in range(chips)],
+        direction_ref, shift, along, chosen, scale, high_in, low_in, high_rest, low_rest,
+    )
+    left = (total + more) * (1.0 / members)
+    taken = taken + further
+    seen_mean = seen_ref[pl.ds(0, 1), :] + at_cells(shift + left, chosen)
+    left, taken_here = at_cells(left, chosen) * scale, at_cells(taken, chosen) * scale
+    common = (seen_ref[pl.ds(1, 1), :] + at_cells(along + taken, chosen)) * scale
     innovation = slot_weight * (values - seen_mean)
-    for ref, block in blocks:
-        rest = ref[...] - mean - doubled(direction_ref[block, :]) * taken
-        high, low = pieces(rest, 2)
-        high, low = pieces((dot(high, chosen) + dot(low, chosen)) * scale, 2)
-        spread_high[block, :] = high + high_in[block, :]
-        spread_low[block, :] = low + low_in[block, :]
-
-    high, low = spread_high[...], spread_low[...]
+    place = lax.broadcasted_iota(jnp.int32, (8, slots), 0)
+    excess = jnp.where(place == 0, left * math.sqrt(members), jnp.where(place == 1, taken_here, 0.0))
+    excess = pieces(excess, 2)
+
     eye = lax.broadcasted_iota(jnp.int32, (slots, slots), 0) == lax.broadcasted_iota(
         jnp.int32, (slots, slots), 1
     )
-    turned = high.T
-    cross = dot(turned, low)
-    factor[...] = dot(turned, high) + (cross + cross.T) + jnp.where(eye, 1.0, 0.0)
-    answer[pl.ds(0, width), :] = product([own_high[...], own_low[...]], [high, low])
+    high, low = high_rest[...], low_rest[...]
+    over = dot_t(excess[0], excess[0]) + (dot_t(excess[0], excess[1]) + dot_t(excess[1], excess[0]))
+    factor[...] = gram(high, low) + (gram_half[...] - over) + jnp.where(eye, 1.0, 0.0)
+    rows = pl.ds(pl.multiple_of(first, count), count)
+    answer[pl.ds(0, width), :] = right_half[...] + product([own_high[:, rows], own_low[:, rows]], [high, low])
     answer[pl.ds(width, 8), :] = jnp.where(
         lax.broadcasted_iota(jnp.int32, (8, slots), 0) == 0, jnp.broadcast_to(common, (8, slots)), 0.0
     )
@@ -412,17 +465,23 @@
     solved = solved + (share / (1.0 + jnp.sum(common * alone, axis=1, keepdims=True))) * alone
     solved = solved.T
     which = lax.broadcasted_iota(jnp.int32, (8, slots), 0)
-    sides = jnp.where(which == 0, innovation * (1.0 / root), jnp.where(which == 1, -0.5 * common, 0.0))
+    sides = jnp.where(
+        which == 0, innovation * (1.0 / root) + 0.5 * left, jnp.where(which == 1, 0.5 * (taken_here - common), 0.0)
+    )
     parts = pieces(solved, 2)
     sides = product(pieces(sides, 2), parts)
     shift, along = sides[0:1], sides[1:2]
     halved = [part * jnp.asarray(-0.5, BF16) for part in parts]
     for x, out_ref in enumerate(out_refs):
-        chip, part = info[0] ^ (x // 2), x % 2
-        rows = pl.ds(pl.multiple_of((part * chips + chip) * step, step), step)
-        moved = product([spread_high[rows, :], spread_low[rows, :]], halved)
-        moved = moved + doubled(direction_ref[rows, :]) * along
-        own = far_own[chip] if part else near_own[rows_at(0, chip), :]
+        chip, mine = info[0] ^ (x // 2), x % 2
+        rows = pl.ds(pl.multiple_of(chip * step, step), step)
+        spread = [
+            jnp.where(part == mine, half[rows, :], rest[rows, :])
+            for half, rest in ((high_half, high_rest), (low_half, low_rest))
+        ]
+        block = pl.ds(pl.multiple_of((mine * chips + chip) * step, step), step)
+        moved = product(spread, halved) + doubled(direction_ref[block, :]) * along
+        own = far_own[chip] if mine else near_own[rows, :]
         out_ref[...] = own + shift + moved
 
 
@@ -545,7 +604,7 @@
     far_other = lax.ppermute(near_own, axes, siblings)
     got_rest = lax.ppermute(far_own, axes, borders)
 
-    split = [pltpu.VMEM((members, slots), BF16)] * 2
+    split = [pltpu.VMEM((members // 2, slots), BF16)] * 2
     prepared = call(
         prepare_kernel, "prepare",
         [bfloat(members, slots)] * 2 + [bfloat(width, members)] * 2
@@ -554,12 +613,20 @@
         [pltpu.VMEM((members, 2 * width), F32)] + [pltpu.VMEM((members, 2 * width), BF16)] * 2,
         flops=8 * members * slots * width, limit=20,
     )
+    halves = members // 2
+    middle = call(
+        middle_kernel, "middle",
+        [bfloat(halves, slots)] * 2 + [array(slots, slots), array(width, slots), array(8, width)],
+        [observed, *prepared[:4], prepared[6], got_half],
+        flops=10 * halves * slots * slots, limit=20,
+    )
     analysed = call(
         region_kernel, "region", [array(step, width)] * lanes,
-        [observed, near_own, far_own, *prepared, got_half, got_rest],
+        [observed, near_own, far_own, *prepared, *middle, got_rest],
         split + [pltpu.VMEM((slots, slots), F32)] * 2 + [pltpu.VMEM((width + 8, slots), F32)],
         limit=24,
     )
+
     def swapped(x):
         return lax.ppermute(analysed[x], "member", [(i, i ^ x) for i in range(lanes)]) if x else analysed[0]
 

time: 95 us -> 94.7 us (level); the launches traced: 95.2 us -> 93.5 us
  starting transfers between devices: 47.5 us -> 44.4 us
  Pallas kernels: 17.8 us -> 20.1 us
  waiting for transfers between devices: 26.1 us -> 25.1 us
    ppermute x7, starting transfers between devices: 16.7 us -> 13.6 us  [swapped(): lax.ppermute(analysed[x], 'member', [(i, i ^ x) for i in range(lanes)])]
    pallas_call x7 -> x8, Pallas kernels: 17.8 us -> 20.1 us  [call(): pl.pallas_call(lambda *refs: kernel(position(), *refs), out_shape=out_sha...]
    ppermute x1, waiting for transfers between devices: 5.62 us -> 3.85 us  [per_device(): got_rest = lax.ppermute(far_own, axes, borders)]
  transfers between devices with their start and end apart: 20 -> 20, of which waited for: 8 -> 8; matrix products, arithmetic and copies ran while one was open for 0% -> 0% of each run, Pallas kernels for 6% -> 8%
where the time goes in v19:
time: 94.7 us; the launch traced here: 93.5 us
  starting transfers between devices  44.4 us (47%)
  waiting for transfers between devices  25.1 us (27%)
  Pallas kernels  20.1 us (21%)
  local copies, waits for them, and re-layouts  2.71 us (3%)
  between operations  1.1 us (1%)
    pallas_call x8, Pallas kernels, call(): pl.pallas_call(lambda *refs: kernel(position(), *refs), out_shape=out_sha...  20.1 us
    ppermute x6, starting transfers between devices, between(): lax.ppermute(message, 'member', [(2 * a + core, 2 * b + core) for a, b in...  16.4 us
    ppermute x7, starting transfers between devices, swapped(): lax.ppermute(analysed[x], 'member', [(i, i ^ x) for i in range(lanes)])  13.6 us
    ppermute x7, waiting for transfers between devices, swapped(): lax.ppermute(analysed[x], 'member', [(i, i ^ x) for i in range(lanes)])  10.4 us
    ppermute x1, waiting for transfers between devices, per_device(): lax.ppermute(mine, axes, [(p * lanes + i, p * lanes + lanes - 1 - i) for...  5.27 us
    ppermute x2, starting transfers between devices, swap(): lax.ppermute(message, 'patch', [(p, p + 1) for p in lower] + [(p + 1, p)...  5.06 us
    ppermute x1, starting transfers between devices, per_device(): got_rest = lax.ppermute(far_own, axes, borders)  4.81 us
    ppermute x6, waiting for transfers between devices, between(): lax.ppermute(message, 'member', [(2 * a + core, 2 * b + core) for a, b in...  3.9 us
  transfers between devices with their start and end apart: 20, of which 8 were waited for; matrix products, arithmetic and copies ran while one was open for 0% of the time, Pallas kernels for 8%

profile of v19, /device:TPU:2, one launch (start us, length us, event | category | flops | bytes accessed | tf_op | source)
XLA Modules:
  0.0 93.5 jit_solution(7457926557477717930)
XLA Ops:
  0.0 0.0 copy-start
  0.0 1.2 %copy-done = f32[128,8,256]{2,1,0:T(8,128)S(1)} copy-done((f32[128,8,256]{2,1,0:T(8,128)S(1)}, f32[128,8,256]{2,1,0:T(8,128)}, u32[]{:S(2)}) %copy-start) | copy-done | bytes 1048600
  1.2 0.0 copy-start.1
  1.2 0.8 copy-done.1
  2.0 0.3 pack.1
  2.3 0.1 collective-permute-start
  2.4 0.0 copy-start.2
  2.4 5.0 %collective-permute-start.1 = (f32[264,256]{1,0:T(8,128)S(1)}, f32[264,256]{1,0:T(8,128)S(1)}, u32[]{:S(2)}, u32[]{:S(2)}) collective-permute-start(f32[264,256]{1,0:T(8,128)S(1)} %get-tuple-element.44), channel_id=1, source_target_pairs={{8,16},{16,8},{9,17},{17,9},{10,18},{18,10},{11,19},{19,11},{12,20... | collective-permute-start | bytes 811016 | tf_op jit(solution)/shard_map/ppermute | solution.py:534
  7.4 0.0 copy-done.2
  7.4 1.6 %inner.1 = (f32[4,128,256]{2,1,0:T(8,128)S(1)}, f32[128,128]{1,0:T(8,128)S(1)}, f32[2,128,256]{2,1,0:T(8,128)S(1)}, f32[2,128,256]{2,1,0:T(8,128)S(1)}, f32[2,12...) custom-call(f32[128,8,256]{2,1,0:T(8,128)S(1)} %copy-done, f32[4,8,256]{2,1,0:T(8,128)S(1)} %copy-done.1, f32[1,128]{1,0:T(1,128)S(1)} %bitcast.2), custom_call_target="tpu_custom_call" | custom-call | tf_op jit(solution)/shard_map/inner/pallas_call | solution.py:498
  9.0 0.7 collective-permute-start.3
  9.6 6.2 %collective-permute-start.4 = (f32[2,128,256]{2,1,0:T(8,128)S(1)}, f32[2,128,256]{2,1,0:T(8,128)S(1)}, u32[]{:S(2)}, u32[]{:S(2)}) collective-permute-start(f32[2,128,256]{2,1,0:T(8,128)S(1)} %get-tuple-element.49), channel_id=1, source_target_pairs={{6,2},{7,3},{0,4},{1,5},{14,10},{15,11},{8,12},{9,13},{22,18},{23,... | collective-permute-start | bytes 786440 | tf_op jit(solution)/shard_map/ppermute | solution.py:550
  15.8 1.4 %collective-permute-start.5 = (f32[2,128,256]{2,1,0:T(8,128)S(1)}, f32[2,128,256]{2,1,0:T(8,128)S(1)}, u32[]{:S(2)}, u32[]{:S(2)}) collective-permute-start(f32[2,128,256]{2,1,0:T(8,128)S(1)} %get-tuple-element.50), channel_id=1, source_target_pairs={{0,2},{1,3},{6,4},{7,5},{8,10},{9,11},{14,12},{15,13},{16,18},{17,... | collective-permute-start | bytes 786440 | tf_op jit(solution)/shard_map/ppermute | solution.py:550
  17.3 0.0 collective-permute-done.refs_4_
  17.3 0.0 collective-permute-done.1.refs_5_
  17.3 0.9 edge.1
  18.3 1.3 %collective-permute-start.6 = (f32[2,128,256]{2,1,0:T(8,128)S(1)}, f32[2,128,256]{2,1,0:T(8,128)S(1)}, u32[]{:S(2)}, u32[]{:S(2)}) collective-permute-start(f32[2,128,256]{2,1,0:T(8,128)S(1)} %get-tuple-element.51), channel_id=1, source_target_pairs={{2,0},{3,1},{4,6},{5,7},{10,8},{11,9},{12,14},{13,15},{18,16},{19,... | collective-permute-start | bytes 786440 | tf_op jit(solution)/shard_map/ppermute | solution.py:550
  19.6 1.3 %collective-permute-start.7 = (f32[2,128,256]{2,1,0:T(8,128)S(1)}, f32[2,128,256]{2,1,0:T(8,128)S(1)}, u32[]{:S(2)}, u32[]{:S(2)}) collective-permute-start(f32[2,128,256]{2,1,0:T(8,128)S(1)} %get-tuple-element.52), channel_id=1, source_target_pairs={{4,0},{5,1},{2,6},{3,7},{12,8},{13,9},{10,14},{11,15},{20,16},{21,... | collective-permute-start | bytes 786440 | tf_op jit(solution)/shard_map/ppermute | solution.py:550
  20.9 0.0 collective-permute-done.3.refs_3_
  20.9 0.0 copy-start.5
  20.9 5.5 %collective-permute-start.8 = (f32[2,128,256]{2,1,0:T(8,128)S(1)}, f32[2,128,256]{2,1,0:T(8,128)S(1)}, u32[]{:S(2)}, u32[]{:S(2)}) collective-permute-start(f32[2,128,256]{2,1,0:T(8,128)S(1)} %get-tuple-element.53), channel_id=1, source_target_pairs={{6,0},{7,1},{0,6},{1,7},{14,8},{15,9},{8,14},{9,15},{22,16},{23,17... | collective-permute-start | bytes 786440 | tf_op jit(solution)/shard_map/ppermute | solution.py:550
  27.0 0.0 copy-done.5
  27.1 0.0 copy-start.3
  27.1 0.0 copy-start.4
  27.1 0.6 copy-done.3
  27.8 0.0 copy-done.4
  27.8 0.0 collective-permute-done.4.refs_4_
  27.8 1.9 %collective-permute-start.2 = (f32[8,512]{1,0:T(8,128)S(1)}, f32[8,512]{1,0:T(8,128)S(1)}, u32[]{:S(2)}, u32[]{:S(2)}) collective-permute-start(f32[8,512]{1,0:T(8,128)S(1)} %concatenate.3.refs_0_), channel_id=1, source_target_pairs={{8,15},{9,14},{10,13},{11,12},{12,11},{13,10},{14,9},{15,8},{24,31... | collective-permute-start | bytes 49160 | tf_op jit(solution)/shard_map/ppermute | solution.py:577
  29.7 0.0 collective-permute-done.5.refs_5_
  29.8 5.3 %collective-permute-done.2.refs_1_ = f32[8,512]{1,0:T(8,128)S(1)} collective-permute-done((f32[8,512]{1,0:T(8,128)S(1)}, f32[8,512]{1,0:T(8,128)S(1)}, u32[]{:S(2)}, u32[]{:S(2)}) %collective-permute-start.2) | collective-permute-done | bytes 16416 | tf_op jit(solution)/shard_map/ppermute | solution.py:577
  35.0 3.9 %collective-permute-done.6.refs_7_ = f32[2,128,256]{2,1,0:T(8,128)S(1)} collective-permute-done((f32[2,128,256]{2,1,0:T(8,128)S(1)}, f32[2,128,256]{2,1,0:T(8,128)S(1)}, u32[]{:S(2)}, u32[]{:S(2)}) %collective-permute-start.6) | collective-permute-done | bytes 262176 | tf_op jit(solution)/shard_map/ppermute | solution.py:550
  38.9 0.0 collective-permute-done.7.refs_8_
  38.9 0.0 collective-permute-done.8.refs_9_
  38.9 0.1 collect.1
  39.0 0.1 collective-permute-start.9
  39.1 0.5 collective-permute-start.10
  39.6 2.1 %collective-permute-start.11 = (f32[520,256]{1,0:T(8,128)S(1)}, f32[520,256]{1,0:T(8,128)S(1)}, u32[]{:S(2)}, u32[]{:S(2)}) collective-permute-start(f32[520,256]{1,0:T(8,128)S(1)} %get-tuple-element.55.refs_2_.refs_1_), channel_id=1, source_target_pairs={{1,2},{2,1},{3,4},{4,3},{5,6},{6,5},{7,15},{8,16},{9,10},{10,9},{1... | collective-permute-start | bytes 1597448 | tf_op jit(solution)/shard_map/ppermute | solution.py:603
  41.7 0.0 collective-permute-done.9.refs_4_.refs_2_
  41.7 4.8 %collective-permute-start.12 = (f32[4,128,256]{2,1,0:T(8,128)S(1)}, f32[4,128,256]{2,1,0:T(8,128)S(1)}, u32[]{:S(2)}, u32[]{:S(2)}) collective-permute-start(f32[4,128,256]{2,1,0:T(8,128)S(1)} %collective-permute-done.9.refs_4_.refs_2_), channel_id=1, source_target_pairs={{1,2},{2,1},{3,4},{4,3},{5,6},{6,5},{7,15},{8,16},{9,10},{10,9},{1... | collective-permute-start | bytes 1572872 | tf_op jit(solution)/shard_map/ppermute | solution.py:605
  46.5 0.0 collective-permute-done.10.refs_3_
  46.6 3.4 %prepare.1 = (bf16[1024,512]{1,0:T(8,128)(2,1)S(1)}, bf16[1024,512]{1,0:T(8,128)(2,1)S(1)}, bf16[256,1024]{1,0:T(8,128)(2,1)S(1)}, bf16[256,1024]{1,0:T(8,128)(2...) custom-call(f32[8,512]{1,0:T(8,128)S(1)} %get-tuple-element.54.refs_0_, ...), custom_call_target="tpu_custom_call" | custom-call | flops 1073741824 | tf_op jit(solution)/shard_map/prepare/pallas_call | solution.py:498
  50.0 1.7 %collective-permute-done.11.refs_6_ = f32[520,256]{1,0:T(8,128)S(1)} collective-permute-done((f32[520,256]{1,0:T(8,128)S(1)}, f32[520,256]{1,0:T(8,128)S(1)}, u32[]{:S(2)}, u32[]{:S(2)}) %collective-permute-start.11) | collective-permute-done | bytes 532512 | tf_op jit(solution)/shard_map/ppermute | solution.py:603
  51.7 1.8 %middle.1 = (bf16[512,512]{1,0:T(8,128)(2,1)S(1)}, bf16[512,512]{1,0:T(8,128)(2,1)S(1)}, f32[512,512]{1,0:T(8,128)S(1)}, f32[256,512]{1,0:T(8,128)S(1)}, f32[8,256]{1,0:T(8,128)S(1)}) custom-call(f32[8,512]{1,0:T(8,128)S(1)} %get-tuple-element.54.refs_0_, bf16[1024,512]{1,0:T(8,128)(2,1)S(1)} %get-tuple-element.57.refs_1_.refs_3_, ...), custom_call_target="tpu_custom_call" | custom-call | flops 1342177280 | tf_op jit(solution)/shard_map/middle/pallas_call | solution.py:498
  53.4 3.8 %collective-permute-done.12.refs_15_ = f32[4,128,256]{2,1,0:T(8,128)S(1)} collective-permute-done((f32[4,128,256]{2,1,0:T(8,128)S(1)}, f32[4,128,256]{2,1,0:T(8,128)S(1)}, u32[]{:S(2)}, u32[]{:S(2)}) %collective-permute-start.12) | collective-permute-done | bytes 524320 | tf_op jit(solution)/shard_map/ppermute | solution.py:605
  57.3 10.9 %region.1 = (f32[128,256]{1,0:T(8,128)S(1)}, f32[128,256]{1,0:T(8,128)S(1)}, f32[128,256]{1,0:T(8,128)S(1)}, f32[128,256]{1,0:T(8,128)S(1)}, f32[128,256]{1,0:T(...) custom-call(f32[8,512]{1,0:T(8,128)S(1)} %get-tuple-element.54.refs_0_, ...), custom_call_target="tpu_custom_call" | custom-call | tf_op jit(solution)/shard_map/region/pallas_call | solution.py:498
  68.2 0.1 collective-permute-start.13
  68.3 2.2 %collective-permute-start.14 = (f32[128,256]{1,0:T(8,128)S(1)}, f32[128,256]{1,0:T(8,128)S(1)}, u32[]{:S(2)}, u32[]{:S(2)}) collective-permute-start(f32[128,256]{1,0:T(8,128)S(1)} %get-tuple-element.70), channel_id=1, source_target_pairs={{0,6},{1,7},{2,4},{3,5},{4,2},{5,3},{6,0},{7,1},{8,14},{9,15},{10,... | collective-permute-start | bytes 393224 | tf_op jit(solution)/shard_map/ppermute | solution.py:631
  70.5 0.0 collective-permute-start.15
  70.5 4.0 %collective-permute-start.16 = (f32[128,256]{1,0:T(8,128)S(1)}, f32[128,256]{1,0:T(8,128)S(1)}, u32[]{:S(2)}, u32[]{:S(2)}) collective-permute-start(f32[128,256]{1,0:T(8,128)S(1)} %get-tuple-element.72), channel_id=1, source_target_pairs={{0,4},{1,5},{2,6},{3,7},{4,0},{5,1},{6,2},{7,3},{8,12},{9,13},{10,... | collective-permute-start | bytes 393224 | tf_op jit(solution)/shard_map/ppermute | solution.py:631
  74.5 0.0 collective-permute-start.17
  74.5 1.4 %collective-permute-done.13.refs_0_ = f32[128,256]{1,0:T(8,128)S(1)} collective-permute-done((f32[128,256]{1,0:T(8,128)S(1)}, f32[128,256]{1,0:T(8,128)S(1)}, u32[]{:S(2)}, u32[]{:S(2)}) %collective-permute-start.13) | collective-permute-done | bytes 131104 | tf_op jit(solution)/shard_map/ppermute | solution.py:631
  75.9 7.3 %collective-permute-start.18 = (f32[128,256]{1,0:T(8,128)S(1)}, f32[128,256]{1,0:T(8,128)S(1)}, u32[]{:S(2)}, u32[]{:S(2)}) collective-permute-start(f32[128,256]{1,0:T(8,128)S(1)} %get-tuple-element.74), channel_id=1, source_target_pairs={{0,2},{1,3},{2,0},{3,1},{4,6},{5,7},{6,4},{7,5},{8,10},{9,11},{10,... | collective-permute-start | bytes 393224 | tf_op jit(solution)/shard_map/ppermute | solution.py:631
  83.2 0.0 collective-permute-done.14.refs_1_
  83.2 0.0 collective-permute-start.19
  83.2 5.5 %collective-permute-done.15.refs_2_ = f32[128,256]{1,0:T(8,128)S(1)} collective-permute-done((f32[128,256]{1,0:T(8,128)S(1)}, f32[128,256]{1,0:T(8,128)S(1)}, u32[]{:S(2)}, u32[]{:S(2)}) %collective-permute-start.15) | collective-permute-done | bytes 131104 | tf_op jit(solution)/shard_map/ppermute | solution.py:631
  88.8 3.0 %collective-permute-done.16.refs_3_ = f32[128,256]{1,0:T(8,128)S(1)} collective-permute-done((f32[128,256]{1,0:T(8,128)S(1)}, f32[128,256]{1,0:T(8,128)S(1)}, u32[]{:S(2)}, u32[]{:S(2)}) %collective-permute-start.16) | collective-permute-done | bytes 131104 | tf_op jit(solution)/shard_map/ppermute | solution.py:631
  91.8 0.0 collective-permute-done.17.refs_4_
  91.8 0.4 collective-permute-done.18.refs_5_
  92.2 0.0 collective-permute-done.19.refs_6_
  92.2 1.1 %unpack.1 = f32[128,8,256]{2,1,0:T(8,128)} custom-call(f32[128,256]{1,0:T(8,128)S(1)} %collective-permute-done.13.refs_0_, f32[128,256]{1,0:T(8,128)S(1)} %collective-permute-done.14.refs_1_, f32[128,256]{1,0:T(8,128)S(1)} %collective-permute-done.15.refs_2_, f32[128,256]{1,0:T(8,128)S(1)} %collective-permute-done.16.refs_3_, ...), custom_call_target="tpu_custom_call" | custom-call | tf_op jit(solution)/shard_map/unpack/pallas_call | solution.py:498
  (3 shorter events, 0.0 us)
Async XLA Ops:
  0.0 1.2 %copy-start = (f32[128,8,256]{2,1,0:T(8,128)S(1)}, f32[128,8,256]{2,1,0:T(8,128)}, u32[]{:S(2)}) copy-start(f32[128,8,256]{2,1,0:T(8,128)} %refs_0_.5) | copy-start | bytes 3145732
  1.2 0.8 copy-start.1
  2.3 15.0 %collective-permute-start = (f32[264,256]{1,0:T(8,128)S(1)}, f32[264,256]{1,0:T(8,128)S(1)}, u32[]{:S(2)}, u32[]{:S(2)}) collective-permute-start(f32[264,256]{1,0:T(8,128)S(1)} %get-tuple-element.43), channel_id=1, source_target_pairs={{0,8},{16,24},{8,0},{24,16},{1,9},{17,25},{9,1},{25,17},{2,10},{18... | collective-permute-start | bytes 811016 | tf_op jit(solution)/shard_map/ppermute | solution.py:534
  2.4 5.0 %copy-start.2 = (f32[128]{0:T(128)S(1)}, f32[128]{0:T(128)}, u32[]{:S(2)}) copy-start(f32[128]{0:T(128)} %param.9) | copy-start | bytes 1540
  2.4 14.9 %collective-permute-start.1 = (f32[264,256]{1,0:T(8,128)S(1)}, f32[264,256]{1,0:T(8,128)S(1)}, u32[]{:S(2)}, u32[]{:S(2)}) collective-permute-start(f32[264,256]{1,0:T(8,128)S(1)} %get-tuple-element.44), channel_id=1, source_target_pairs={{8,16},{16,8},{9,17},{17,9},{10,18},{18,10},{11,19},{19,11},{12,20... | collective-permute-start | bytes 811016 | tf_op jit(solution)/shard_map/ppermute | solution.py:534
  9.0 11.9 %collective-permute-start.3 = (f32[2,128,256]{2,1,0:T(8,128)S(1)}, f32[2,128,256]{2,1,0:T(8,128)S(1)}, u32[]{:S(2)}, u32[]{:S(2)}) collective-permute-start(f32[2,128,256]{2,1,0:T(8,128)S(1)} %get-tuple-element.48), channel_id=1, source_target_pairs={{4,2},{5,3},{2,4},{3,5},{12,10},{13,11},{10,12},{11,13},{20,18},{2... | collective-permute-start | bytes 786440 | tf_op jit(solution)/shard_map/ppermute | solution.py:550
  9.6 18.2 %collective-permute-start.4 = (f32[2,128,256]{2,1,0:T(8,128)S(1)}, f32[2,128,256]{2,1,0:T(8,128)S(1)}, u32[]{:S(2)}, u32[]{:S(2)}) collective-permute-start(f32[2,128,256]{2,1,0:T(8,128)S(1)} %get-tuple-element.49), channel_id=1, source_target_pairs={{6,2},{7,3},{0,4},{1,5},{14,10},{15,11},{8,12},{9,13},{22,18},{23,... | collective-permute-start | bytes 786440 | tf_op jit(solution)/shard_map/ppermute | solution.py:550
  15.8 13.9 %collective-permute-start.5 = (f32[2,128,256]{2,1,0:T(8,128)S(1)}, f32[2,128,256]{2,1,0:T(8,128)S(1)}, u32[]{:S(2)}, u32[]{:S(2)}) collective-permute-start(f32[2,128,256]{2,1,0:T(8,128)S(1)} %get-tuple-element.50), channel_id=1, source_target_pairs={{0,2},{1,3},{6,4},{7,5},{8,10},{9,11},{14,12},{15,13},{16,18},{17,... | collective-permute-start | bytes 786440 | tf_op jit(solution)/shard_map/ppermute | solution.py:550
  18.3 20.7 %collective-permute-start.6 = (f32[2,128,256]{2,1,0:T(8,128)S(1)}, f32[2,128,256]{2,1,0:T(8,128)S(1)}, u32[]{:S(2)}, u32[]{:S(2)}) collective-permute-start(f32[2,128,256]{2,1,0:T(8,128)S(1)} %get-tuple-element.51), channel_id=1, source_target_pairs={{2,0},{3,1},{4,6},{5,7},{10,8},{11,9},{12,14},{13,15},{18,16},{19,... | collective-permute-start | bytes 786440 | tf_op jit(solution)/shard_map/ppermute | solution.py:550
  19.6 19.4 %collective-permute-start.7 = (f32[2,128,256]{2,1,0:T(8,128)S(1)}, f32[2,128,256]{2,1,0:T(8,128)S(1)}, u32[]{:S(2)}, u32[]{:S(2)}) collective-permute-start(f32[2,128,256]{2,1,0:T(8,128)S(1)} %get-tuple-element.52), channel_id=1, source_target_pairs={{4,0},{5,1},{2,6},{3,7},{12,8},{13,9},{10,14},{11,15},{20,16},{21,... | collective-permute-start | bytes 786440 | tf_op jit(solution)/shard_map/ppermute | solution.py:550
  20.9 6.2 %copy-start.5 = (s32[1,512]{1,0:T(1,128)S(1)}, s32[1,512]{1,0:T(1,128)}, u32[]{:S(2)}) copy-start(s32[1,512]{1,0:T(1,128)} %param.10) | copy-start | bytes 6148
  20.9 18.0 %collective-permute-start.8 = (f32[2,128,256]{2,1,0:T(8,128)S(1)}, f32[2,128,256]{2,1,0:T(8,128)S(1)}, u32[]{:S(2)}, u32[]{:S(2)}) collective-permute-start(f32[2,128,256]{2,1,0:T(8,128)S(1)} %get-tuple-element.53), channel_id=1, source_target_pairs={{6,0},{7,1},{0,6},{1,7},{14,8},{15,9},{8,14},{9,15},{22,16},{23,17... | collective-permute-start | bytes 786440 | tf_op jit(solution)/shard_map/ppermute | solution.py:550
  27.1 0.7 copy-start.3
  27.1 0.7 copy-start.4
  27.8 7.2 %collective-permute-start.2 = (f32[8,512]{1,0:T(8,128)S(1)}, f32[8,512]{1,0:T(8,128)S(1)}, u32[]{:S(2)}, u32[]{:S(2)}) collective-permute-start(f32[8,512]{1,0:T(8,128)S(1)} %concatenate.3.refs_0_), channel_id=1, source_target_pairs={{8,15},{9,14},{10,13},{11,12},{12,11},{13,10},{14,9},{15,8},{24,31... | collective-permute-start | bytes 49160 | tf_op jit(solution)/shard_map/ppermute | solution.py:577
  39.0 2.7 %collective-permute-start.9 = (f32[4,128,256]{2,1,0:T(8,128)S(1)}, f32[4,128,256]{2,1,0:T(8,128)S(1)}, u32[]{:S(2)}, u32[]{:S(2)}) collective-permute-start(f32[4,128,256]{2,1,0:T(8,128)S(1)} %get-tuple-element.56.refs_1_), channel_id=1, source_target_pairs={{0,1},{1,0},{2,3},{3,2},{4,5},{5,4},{6,7},{7,6},{8,9},{9,8},{10,11... | collective-permute-start | bytes 1572872 | tf_op jit(solution)/shard_map/ppermute | solution.py:602
  39.1 7.4 %collective-permute-start.10 = (f32[520,256]{1,0:T(8,128)S(1)}, f32[520,256]{1,0:T(8,128)S(1)}, u32[]{:S(2)}, u32[]{:S(2)}) collective-permute-start(f32[520,256]{1,0:T(8,128)S(1)} %get-tuple-element.55.refs_2_.refs_1_), channel_id=1, source_target_pairs={{0,1},{1,0},{2,3},{3,2},{4,5},{5,4},{6,7},{7,6},{8,9},{9,8},{10,11... | collective-permute-start | bytes 1597448 | tf_op jit(solution)/shard_map/ppermute | solution.py:604
  39.6 12.0 %collective-permute-start.11 = (f32[520,256]{1,0:T(8,128)S(1)}, f32[520,256]{1,0:T(8,128)S(1)}, u32[]{:S(2)}, u32[]{:S(2)}) collective-permute-start(f32[520,256]{1,0:T(8,128)S(1)} %get-tuple-element.55.refs_2_.refs_1_), channel_id=1, source_target_pairs={{1,2},{2,1},{3,4},{4,3},{5,6},{6,5},{7,15},{8,16},{9,10},{10,9},{1... | collective-permute-start | bytes 1597448 | tf_op jit(solution)/shard_map/ppermute | solution.py:603
  41.7 15.5 %collective-permute-start.12 = (f32[4,128,256]{2,1,0:T(8,128)S(1)}, f32[4,128,256]{2,1,0:T(8,128)S(1)}, u32[]{:S(2)}, u32[]{:S(2)}) collective-permute-start(f32[4,128,256]{2,1,0:T(8,128)S(1)} %collective-permute-done.9.refs_4_.refs_2_), channel_id=1, source_target_pairs={{1,2},{2,1},{3,4},{4,3},{5,6},{6,5},{7,15},{8,16},{9,10},{10,9},{1... | collective-permute-start | bytes 1572872 | tf_op jit(solution)/shard_map/ppermute | solution.py:605
  68.2 7.7 %collective-permute-start.13 = (f32[128,256]{1,0:T(8,128)S(1)}, f32[128,256]{1,0:T(8,128)S(1)}, u32[]{:S(2)}, u32[]{:S(2)}) collective-permute-start(f32[128,256]{1,0:T(8,128)S(1)} %get-tuple-element.69), channel_id=1, source_target_pairs={{0,7},{1,6},{2,5},{3,4},{4,3},{5,2},{6,1},{7,0},{8,15},{9,14},{10,... | collective-permute-start | bytes 393224 | tf_op jit(solution)/shard_map/ppermute | solution.py:631
  68.3 15.0 %collective-permute-start.14 = (f32[128,256]{1,0:T(8,128)S(1)}, f32[128,256]{1,0:T(8,128)S(1)}, u32[]{:S(2)}, u32[]{:S(2)}) collective-permute-start(f32[128,256]{1,0:T(8,128)S(1)} %get-tuple-element.70), channel_id=1, source_target_pairs={{0,6},{1,7},{2,4},{3,5},{4,2},{5,3},{6,0},{7,1},{8,14},{9,15},{10,... | collective-permute-start | bytes 393224 | tf_op jit(solution)/shard_map/ppermute | solution.py:631
  70.5 18.3 %collective-permute-start.15 = (f32[128,256]{1,0:T(8,128)S(1)}, f32[128,256]{1,0:T(8,128)S(1)}, u32[]{:S(2)}, u32[]{:S(2)}) collective-permute-start(f32[128,256]{1,0:T(8,128)S(1)} %get-tuple-element.71), channel_id=1, source_target_pairs={{0,5},{1,4},{2,7},{3,6},{4,1},{5,0},{6,3},{7,2},{8,13},{9,12},{10,... | collective-permute-start | bytes 393224 | tf_op jit(solution)/shard_map/ppermute | solution.py:631
  70.5 21.3 %collective-permute-start.16 = (f32[128,256]{1,0:T(8,128)S(1)}, f32[128,256]{1,0:T(8,128)S(1)}, u32[]{:S(2)}, u32[]{:S(2)}) collective-permute-start(f32[128,256]{1,0:T(8,128)S(1)} %get-tuple-element.72), channel_id=1, source_target_pairs={{0,4},{1,5},{2,6},{3,7},{4,0},{5,1},{6,2},{7,3},{8,12},{9,13},{10,... | collective-permute-start | bytes 393224 | tf_op jit(solution)/shard_map/ppermute | solution.py:631
  74.5 17.3 %collective-permute-start.17 = (f32[128,256]{1,0:T(8,128)S(1)}, f32[128,256]{1,0:T(8,128)S(1)}, u32[]{:S(2)}, u32[]{:S(2)}) collective-permute-start(f32[128,256]{1,0:T(8,128)S(1)} %get-tuple-element.73), channel_id=1, source_target_pairs={{0,3},{1,2},{2,1},{3,0},{4,7},{5,6},{6,5},{7,4},{8,11},{9,10},{10,... | collective-permute-start | bytes 393224 | tf_op jit(solution)/shard_map/ppermute | solution.py:631
  75.9 16.3 %collective-permute-start.18 = (f32[128,256]{1,0:T(8,128)S(1)}, f32[128,256]{1,0:T(8,128)S(1)}, u32[]{:S(2)}, u32[]{:S(2)}) collective-permute-start(f32[128,256]{1,0:T(8,128)S(1)} %get-tuple-element.74), channel_id=1, source_target_pairs={{0,2},{1,3},{2,0},{3,1},{4,6},{5,7},{6,4},{7,5},{8,10},{9,11},{10,... | collective-permute-start | bytes 393224 | tf_op jit(solution)/shard_map/ppermute | solution.py:631
  83.2 8.9 %collective-permute-start.19 = (f32[128,256]{1,0:T(8,128)S(1)}, f32[128,256]{1,0:T(8,128)S(1)}, u32[]{:S(2)}, u32[]{:S(2)}) collective-permute-start(f32[128,256]{1,0:T(8,128)S(1)} %get-tuple-element.75), channel_id=1, source_target_pairs={{0,1},{1,0},{2,3},{3,2},{4,5},{5,4},{6,7},{7,6},{8,9},{9,8},{10,11... | collective-permute-start | bytes 393224 | tf_op jit(solution)/shard_map/ppermute | solution.py:631

commit v20 on v19

--- a/solution.py
+++ b/solution.py
@@ -365,13 +365,36 @@
     right_ref[...] = product([own_high[:, members], own_low[:, members]], [high, low])
 
 
+def analysed_row(info, x, near_own, far_own, direction_ref, halves, rests, parts, sides):
+    chips, step, _ = far_own.shape
+    chip, mine = info[0] ^ (x // 2), x % 2
+    rows = pl.ds(pl.multiple_of(chip * step, step), step)
+    spread = [
+        jnp.where(at_border(info) == mine, half[rows, :], rest[rows, :]) for half, rest in zip(halves, rests)
+    ]
+    block = pl.ds(pl.multiple_of((mine * chips + chip) * step, step), step)
+    own = far_own[chip] if mine else near_own[rows, :]
+    return own + sides[0:1] + product(spread, parts) + doubled(direction_ref[block, :]) * sides[1:2]
+
+
+def others_kernel(
+    order, info, near_own, far_own, direction_ref, high_half, low_half, high_rest, low_rest,
+    solved_high, solved_low, sides_ref, *out_refs,
+):
+    parts = [solved_high[...], solved_low[...]]
+    for x, out_ref in zip(order, out_refs):
+        out_ref[...] = analysed_row(
+            info, x, near_own, far_own, direction_ref, (high_half, low_half), (high_rest, low_rest), parts, sides_ref[...]
+        )
+
+
 def region_kernel(
-    info, observed_ref, near_own, far_own, high_in, low_in, own_high, own_low, own_part, seen_ref,
+    order, info, observed_ref, near_own, far_own, high_in, low_in, own_high, own_low, own_part, seen_ref,
     direction_ref, high_half, low_half, gram_half, right_half, known_ref, rest_ref, *refs,
 ):
     chips, step, width = far_own.shape
-    out_refs = refs[:-5]
-    high_rest, low_rest, factor, squared, answer = refs[-5:]
+    high_rest, low_rest, solved_high, solved_low, sides_ref = refs[:5]
+    out_refs, (factor, squared, answer) = refs[5:-3], refs[-3:]
     count = chips * step
     members = 2 * count
     slots = observed_ref.shape[1]
@@ -470,19 +493,13 @@
     )
     parts = pieces(solved, 2)
     sides = product(pieces(sides, 2), parts)
-    shift, along = sides[0:1], sides[1:2]
-    halved = [part * jnp.asarray(-0.5, BF16) for part in parts]
-    for x, out_ref in enumerate(out_refs):
-        chip, mine = info[0] ^ (x // 2), x % 2
-        rows = pl.ds(pl.multiple_of(chip * step, step), step)
-        spread = [
-            jnp.where(part == mine, half[rows, :], rest[rows, :])
-            for half, rest in ((high_half, high_rest), (low_half, low_rest))
-        ]
-        block = pl.ds(pl.multiple_of((mine * chips + chip) * step, step), step)
-        moved = product(spread, halved) + doubled(direction_ref[block, :]) * along
-        own = far_own[chip] if mine else near_own[rows, :]
-        out_ref[...] = own + shift + moved
+    parts = [part * jnp.asarray(-0.5, BF16) for part in parts]
+    sides_ref[...] = sides
+    solved_high[...], solved_low[...] = parts
+    for x, out_ref in zip(order, out_refs):
+        out_ref[...] = analysed_row(
+            info, x, near_own, far_own, direction_ref, (high_half, low_half), (high_rest, low_rest), parts, sides
+        )
 
 
 VMEM = pl.BlockSpec(memory_space=pltpu.VMEM)
@@ -604,7 +621,6 @@
     far_other = lax.ppermute(near_own, axes, siblings)
     got_rest = lax.ppermute(far_own, axes, borders)
 
-    split = [pltpu.VMEM((members // 2, slots), BF16)] * 2
     prepared = call(
         prepare_kernel, "prepare",
         [bfloat(members, slots)] * 2 + [bfloat(width, members)] * 2
@@ -620,17 +636,25 @@
         [observed, *prepared[:4], prepared[6], got_half],
         flops=10 * halves * slots * slots, limit=20,
     )
-    analysed = call(
-        region_kernel, "region", [array(step, width)] * lanes,
+    order = sorted(range(lanes), key=lambda x: (x.bit_length() != lanes.bit_length() - 1, -x))
+    row = array(step, width)
+    *shared, first, second = call(
+        functools.partial(region_kernel, order[:2]), "region",
+        [bfloat(halves, slots)] * 2 + [bfloat(slots, width)] * 2 + [array(8, width)] + [row] * 2,
         [observed, near_own, far_own, *prepared, *middle, got_rest],
-        split + [pltpu.VMEM((slots, slots), F32)] * 2 + [pltpu.VMEM((width + 8, slots), F32)],
+        [pltpu.VMEM((slots, slots), F32)] * 2 + [pltpu.VMEM((width + 8, slots), F32)],
         limit=24,
     )
+    others = call(
+        functools.partial(others_kernel, order[2:]), "others", [row] * (lanes - 2),
+        [near_own, far_own, prepared[6], *middle[:2], *shared],
+        flops=6 * members * slots * width, limit=16,
+    )
+    analysed = dict(zip(order, [first, second, *others]))
 
     def swapped(x):
         return lax.ppermute(analysed[x], "member", [(i, i ^ x) for i in range(lanes)]) if x else analysed[0]
 
-    order = sorted(range(lanes), key=lambda x: (x.bit_length() != lanes.bit_length() - 1, -x))
     return call(
         functools.partial(unpack_kernel, order), "unpack", array(step, rows, width),
         [swapped(x) for x in order], [pltpu.VMEM((step, rows, width), F32), pltpu.SemaphoreType.DMA((4,))],

time: 94.7 us -> 94.4 us (level)
  starting transfers between devices: 44.4 us -> 46.8 us
  Pallas kernels: 20.1 us -> 18.9 us
    ppermute x7, starting transfers between devices: 13.6 us -> 16 us  [swapped(): lax.ppermute(analysed[x], 'member', [(i, i ^ x) for i in range(lanes)])]
    pallas_call x8 -> x9, Pallas kernels: 20.1 us -> 18.9 us  [call(): pl.pallas_call(lambda *refs: kernel(position(), *refs), out_shape=out_sha...]
  transfers between devices with their start and end apart: 20 -> 20, of which waited for: 8 -> 7; matrix products, arithmetic and copies ran while one was open for 0% -> 0% of each run, Pallas kernels for 8% -> 9%
where the time goes in v20:
time: 94.4 us; the launch traced here: 93.9 us
  starting transfers between devices  46.8 us (50%)
  waiting for transfers between devices  24.3 us (26%)
  Pallas kernels  18.9 us (20%)
  local copies, waits for them, and re-layouts  2.71 us (3%)
  between operations  1.11 us (1%)
    pallas_call x9, Pallas kernels, call(): pl.pallas_call(lambda *refs: kernel(position(), *refs), out_shape=out_sha...  18.9 us
    ppermute x6, starting transfers between devices, between(): lax.ppermute(message, 'member', [(2 * a + core, 2 * b + core) for a, b in...  16.4 us
    ppermute x7, starting transfers between devices, swapped(): lax.ppermute(analysed[x], 'member', [(i, i ^ x) for i in range(lanes)])  16 us
    ppermute x7, waiting for transfers between devices, swapped(): lax.ppermute(analysed[x], 'member', [(i, i ^ x) for i in range(lanes)])  9.56 us
    ppermute x1, waiting for transfers between devices, per_device(): lax.ppermute(mine, axes, [(p * lanes + i, p * lanes + lanes - 1 - i) for...  5.27 us
    ppermute x2, starting transfers between devices, swap(): lax.ppermute(message, 'patch', [(p, p + 1) for p in lower] + [(p + 1, p)...  5.06 us
    ppermute x1, starting transfers between devices, per_device(): got_rest = lax.ppermute(far_own, axes, borders)  4.81 us
    ppermute x6, waiting for transfers between devices, between(): lax.ppermute(message, 'member', [(2 * a + core, 2 * b + core) for a, b in...  3.9 us
  transfers between devices with their start and end apart: 20, of which 7 were waited for; matrix products, arithmetic and copies ran while one was open for 0% of the time, Pallas kernels for 9%

profile of v20, /device:TPU:2, one launch (start us, length us, event | category | flops | bytes accessed | tf_op | source)
XLA Modules:
  0.0 93.9 jit_solution(6419396165443654169)
XLA Ops:
  0.0 0.0 copy-start
  0.0 1.2 %copy-done = f32[128,8,256]{2,1,0:T(8,128)S(1)} copy-done((f32[128,8,256]{2,1,0:T(8,128)S(1)}, f32[128,8,256]{2,1,0:T(8,128)}, u32[]{:S(2)}) %copy-start) | copy-done | bytes 1048600
  1.2 0.0 copy-start.1
  1.2 0.8 copy-done.1
  2.0 0.3 pack.1
  2.3 0.1 collective-permute-start
  2.4 0.0 copy-start.2
  2.4 5.0 %collective-permute-start.1 = (f32[264,256]{1,0:T(8,128)S(1)}, f32[264,256]{1,0:T(8,128)S(1)}, u32[]{:S(2)}, u32[]{:S(2)}) collective-permute-start(f32[264,256]{1,0:T(8,128)S(1)} %get-tuple-element.49), channel_id=1, source_target_pairs={{8,16},{16,8},{9,17},{17,9},{10,18},{18,10},{11,19},{19,11},{12,20... | collective-permute-start | bytes 811016 | tf_op jit(solution)/shard_map/ppermute | solution.py:551
  7.4 0.0 copy-done.2
  7.4 1.6 %inner.1 = (f32[4,128,256]{2,1,0:T(8,128)S(1)}, f32[128,128]{1,0:T(8,128)S(1)}, f32[2,128,256]{2,1,0:T(8,128)S(1)}, f32[2,128,256]{2,1,0:T(8,128)S(1)}, f32[2,12...) custom-call(f32[128,8,256]{2,1,0:T(8,128)S(1)} %copy-done, f32[4,8,256]{2,1,0:T(8,128)S(1)} %copy-done.1, f32[1,128]{1,0:T(1,128)S(1)} %bitcast.2), custom_call_target="tpu_custom_call" | custom-call | tf_op jit(solution)/shard_map/inner/pallas_call | solution.py:515
  9.0 0.7 collective-permute-start.3
  9.6 6.2 %collective-permute-start.4 = (f32[2,128,256]{2,1,0:T(8,128)S(1)}, f32[2,128,256]{2,1,0:T(8,128)S(1)}, u32[]{:S(2)}, u32[]{:S(2)}) collective-permute-start(f32[2,128,256]{2,1,0:T(8,128)S(1)} %get-tuple-element.54), channel_id=1, source_target_pairs={{6,2},{7,3},{0,4},{1,5},{14,10},{15,11},{8,12},{9,13},{22,18},{23,... | collective-permute-start | bytes 786440 | tf_op jit(solution)/shard_map/ppermute | solution.py:567
  15.8 1.4 %collective-permute-start.5 = (f32[2,128,256]{2,1,0:T(8,128)S(1)}, f32[2,128,256]{2,1,0:T(8,128)S(1)}, u32[]{:S(2)}, u32[]{:S(2)}) collective-permute-start(f32[2,128,256]{2,1,0:T(8,128)S(1)} %get-tuple-element.55), channel_id=1, source_target_pairs={{0,2},{1,3},{6,4},{7,5},{8,10},{9,11},{14,12},{15,13},{16,18},{17,... | collective-permute-start | bytes 786440 | tf_op jit(solution)/shard_map/ppermute | solution.py:567
  17.3 0.0 collective-permute-done.refs_4_
  17.3 0.0 collective-permute-done.1.refs_5_
  17.3 0.9 edge.1
  18.3 1.3 %collective-permute-start.6 = (f32[2,128,256]{2,1,0:T(8,128)S(1)}, f32[2,128,256]{2,1,0:T(8,128)S(1)}, u32[]{:S(2)}, u32[]{:S(2)}) collective-permute-start(f32[2,128,256]{2,1,0:T(8,128)S(1)} %get-tuple-element.56), channel_id=1, source_target_pairs={{2,0},{3,1},{4,6},{5,7},{10,8},{11,9},{12,14},{13,15},{18,16},{19,... | collective-permute-start | bytes 786440 | tf_op jit(solution)/shard_map/ppermute | solution.py:567
  19.6 1.3 %collective-permute-start.7 = (f32[2,128,256]{2,1,0:T(8,128)S(1)}, f32[2,128,256]{2,1,0:T(8,128)S(1)}, u32[]{:S(2)}, u32[]{:S(2)}) collective-permute-start(f32[2,128,256]{2,1,0:T(8,128)S(1)} %get-tuple-element.57), channel_id=1, source_target_pairs={{4,0},{5,1},{2,6},{3,7},{12,8},{13,9},{10,14},{11,15},{20,16},{21,... | collective-permute-start | bytes 786440 | tf_op jit(solution)/shard_map/ppermute | solution.py:567
  20.9 0.0 collective-permute-done.3.refs_3_
  20.9 0.0 copy-start.5
  20.9 5.5 %collective-permute-start.8 = (f32[2,128,256]{2,1,0:T(8,128)S(1)}, f32[2,128,256]{2,1,0:T(8,128)S(1)}, u32[]{:S(2)}, u32[]{:S(2)}) collective-permute-start(f32[2,128,256]{2,1,0:T(8,128)S(1)} %get-tuple-element.58), channel_id=1, source_target_pairs={{6,0},{7,1},{0,6},{1,7},{14,8},{15,9},{8,14},{9,15},{22,16},{23,17... | collective-permute-start | bytes 786440 | tf_op jit(solution)/shard_map/ppermute | solution.py:567
  27.0 0.0 copy-done.5
  27.1 0.0 copy-start.3
  27.1 0.0 copy-start.4
  27.1 0.6 copy-done.3
  27.8 0.0 copy-done.4
  27.8 0.0 collective-permute-done.4.refs_4_
  27.8 1.9 %collective-permute-start.2 = (f32[8,512]{1,0:T(8,128)S(1)}, f32[8,512]{1,0:T(8,128)S(1)}, u32[]{:S(2)}, u32[]{:S(2)}) collective-permute-start(f32[8,512]{1,0:T(8,128)S(1)} %concatenate.3.refs_0_), channel_id=1, source_target_pairs={{8,15},{9,14},{10,13},{11,12},{12,11},{13,10},{14,9},{15,8},{24,31... | collective-permute-start | bytes 49160 | tf_op jit(solution)/shard_map/ppermute | solution.py:594
  29.7 0.0 collective-permute-done.5.refs_5_
  29.8 5.3 %collective-permute-done.2.refs_1_ = f32[8,512]{1,0:T(8,128)S(1)} collective-permute-done((f32[8,512]{1,0:T(8,128)S(1)}, f32[8,512]{1,0:T(8,128)S(1)}, u32[]{:S(2)}, u32[]{:S(2)}) %collective-permute-start.2) | collective-permute-done | bytes 16416 | tf_op jit(solution)/shard_map/ppermute | solution.py:594
  35.0 3.9 %collective-permute-done.6.refs_7_ = f32[2,128,256]{2,1,0:T(8,128)S(1)} collective-permute-done((f32[2,128,256]{2,1,0:T(8,128)S(1)}, f32[2,128,256]{2,1,0:T(8,128)S(1)}, u32[]{:S(2)}, u32[]{:S(2)}) %collective-permute-start.6) | collective-permute-done | bytes 262176 | tf_op jit(solution)/shard_map/ppermute | solution.py:567
  38.9 0.0 collective-permute-done.7.refs_8_
  38.9 0.0 collective-permute-done.8.refs_9_
  38.9 0.1 collect.1
  39.0 0.1 collective-permute-start.9
  39.1 0.5 collective-permute-start.10
  39.6 2.1 %collective-permute-start.11 = (f32[520,256]{1,0:T(8,128)S(1)}, f32[520,256]{1,0:T(8,128)S(1)}, u32[]{:S(2)}, u32[]{:S(2)}) collective-permute-start(f32[520,256]{1,0:T(8,128)S(1)} %get-tuple-element.60.refs_2_.refs_1_.refs_0_), channel_id=1, source_target_pairs={{1,2},{2,1},{3,4},{4,3},{5,6},{6,5},{7,15},{8,16},{9,10},{10,9},{1... | collective-permute-start | bytes 1597448 | tf_op jit(solution)/shard_map/ppermute | solution.py:620
  41.7 0.0 collective-permute-done.9.refs_4_.refs_2_.refs_1_
  41.7 4.8 %collective-permute-start.12 = (f32[4,128,256]{2,1,0:T(8,128)S(1)}, f32[4,128,256]{2,1,0:T(8,128)S(1)}, u32[]{:S(2)}, u32[]{:S(2)}) collective-permute-start(f32[4,128,256]{2,1,0:T(8,128)S(1)} %collective-permute-done.9.refs_4_.refs_2_.refs_1_), channel_id=1, source_target_pairs={{1,2},{2,1},{3,4},{4,3},{5,6},{6,5},{7,15},{8,16},{9,10},{10,9},{1... | collective-permute-start | bytes 1572872 | tf_op jit(solution)/shard_map/ppermute | solution.py:622
  46.5 0.0 collective-permute-done.10.refs_3_
  46.6 3.4 %prepare.1 = (bf16[1024,512]{1,0:T(8,128)(2,1)S(1)}, bf16[1024,512]{1,0:T(8,128)(2,1)S(1)}, bf16[256,1024]{1,0:T(8,128)(2,1)S(1)}, bf16[256,1024]{1,0:T(8,128)(2...) custom-call(f32[8,512]{1,0:T(8,128)S(1)} %get-tuple-element.59.refs_0_, ...), custom_call_target="tpu_custom_call" | custom-call | flops 1073741824 | tf_op jit(solution)/shard_map/prepare/pallas_call | solution.py:515
  50.0 1.7 %collective-permute-done.11.refs_6_ = f32[520,256]{1,0:T(8,128)S(1)} collective-permute-done((f32[520,256]{1,0:T(8,128)S(1)}, f32[520,256]{1,0:T(8,128)S(1)}, u32[]{:S(2)}, u32[]{:S(2)}) %collective-permute-start.11) | collective-permute-done | bytes 532512 | tf_op jit(solution)/shard_map/ppermute | solution.py:620
  51.7 1.8 %middle.1 = (bf16[512,512]{1,0:T(8,128)(2,1)S(1)}, bf16[512,512]{1,0:T(8,128)(2,1)S(1)}, f32[512,512]{1,0:T(8,128)S(1)}, f32[256,512]{1,0:T(8,128)S(1)}, f32[8,256]{1,0:T(8,128)S(1)}) custom-call(f32[8,512]{1,0:T(8,128)S(1)} %get-tuple-element.59.refs_0_, bf16[1024,512]{1,0:T(8,128)(2,1)S(1)} %get-tuple-element.62.refs_1_.refs_3_, ...), custom_call_target="tpu_custom_call" | custom-call | flops 1342177280 | tf_op jit(solution)/shard_map/middle/pallas_call | solution.py:515
  53.5 3.8 %collective-permute-done.12.refs_15_ = f32[4,128,256]{2,1,0:T(8,128)S(1)} collective-permute-done((f32[4,128,256]{2,1,0:T(8,128)S(1)}, f32[4,128,256]{2,1,0:T(8,128)S(1)}, u32[]{:S(2)}, u32[]{:S(2)}) %collective-permute-start.12) | collective-permute-done | bytes 524320 | tf_op jit(solution)/shard_map/ppermute | solution.py:622
  57.3 8.9 %region.1 = (bf16[512,512]{1,0:T(8,128)(2,1)S(1)}, bf16[512,512]{1,0:T(8,128)(2,1)S(1)}, bf16[512,256]{1,0:T(8,128)(2,1)S(1)}, bf16[512,256]{1,0:T(8,128)(2,1)S(...) custom-call(f32[8,512]{1,0:T(8,128)S(1)} %get-tuple-element.59.refs_0_, ...), custom_call_target="tpu_custom_call" | custom-call | tf_op jit(solution)/shard_map/region/pallas_call | solution.py:515
  66.2 2.2 %collective-permute-start.13 = (f32[128,256]{1,0:T(8,128)S(1)}, f32[128,256]{1,0:T(8,128)S(1)}, u32[]{:S(2)}, u32[]{:S(2)}) collective-permute-start(f32[128,256]{1,0:T(8,128)S(1)} %get-tuple-element.74), channel_id=1, source_target_pairs={{0,7},{1,6},{2,5},{3,4},{4,3},{5,2},{6,1},{7,0},{8,15},{9,14},{10,... | collective-permute-start | bytes 393224 | tf_op jit(solution)/shard_map/ppermute | solution.py:656
  68.4 0.2 collective-permute-start.14
  68.6 0.8 others.1
  69.4 0.1 collective-permute-start.15
  69.5 3.8 %collective-permute-start.16 = (f32[128,256]{1,0:T(8,128)S(1)}, f32[128,256]{1,0:T(8,128)S(1)}, u32[]{:S(2)}, u32[]{:S(2)}) collective-permute-start(f32[128,256]{1,0:T(8,128)S(1)} %get-tuple-element.82), channel_id=1, source_target_pairs={{0,4},{1,5},{2,6},{3,7},{4,0},{5,1},{6,2},{7,3},{8,12},{9,13},{10,... | collective-permute-start | bytes 393224 | tf_op jit(solution)/shard_map/ppermute | solution.py:656
  73.3 0.1 collective-permute-start.17
  73.4 0.0 collective-permute-done.13.refs_0_
  73.4 9.4 %collective-permute-start.18 = (f32[128,256]{1,0:T(8,128)S(1)}, f32[128,256]{1,0:T(8,128)S(1)}, u32[]{:S(2)}, u32[]{:S(2)}) collective-permute-start(f32[128,256]{1,0:T(8,128)S(1)} %get-tuple-element.84), channel_id=1, source_target_pairs={{0,2},{1,3},{2,0},{3,1},{4,6},{5,7},{6,4},{7,5},{8,10},{9,11},{10,... | collective-permute-start | bytes 393224 | tf_op jit(solution)/shard_map/ppermute | solution.py:656
  82.9 0.0 collective-permute-done.14.refs_1_
  82.9 0.2 collective-permute-start.19
  83.1 5.0 %collective-permute-done.15.refs_2_ = f32[128,256]{1,0:T(8,128)S(1)} collective-permute-done((f32[128,256]{1,0:T(8,128)S(1)}, f32[128,256]{1,0:T(8,128)S(1)}, u32[]{:S(2)}, u32[]{:S(2)}) %collective-permute-start.15) | collective-permute-done | bytes 131104 | tf_op jit(solution)/shard_map/ppermute | solution.py:656
  88.0 3.0 %collective-permute-done.16.refs_3_ = f32[128,256]{1,0:T(8,128)S(1)} collective-permute-done((f32[128,256]{1,0:T(8,128)S(1)}, f32[128,256]{1,0:T(8,128)S(1)}, u32[]{:S(2)}, u32[]{:S(2)}) %collective-permute-start.16) | collective-permute-done | bytes 131104 | tf_op jit(solution)/shard_map/ppermute | solution.py:656
  91.0 0.0 collective-permute-done.17.refs_4_
  91.0 1.6 %collective-permute-done.18.refs_5_ = f32[128,256]{1,0:T(8,128)S(1)} collective-permute-done((f32[128,256]{1,0:T(8,128)S(1)}, f32[128,256]{1,0:T(8,128)S(1)}, u32[]{:S(2)}, u32[]{:S(2)}) %collective-permute-start.18) | collective-permute-done | bytes 131104 | tf_op jit(solution)/shard_map/ppermute | solution.py:656
  92.6 0.0 collective-permute-done.19.refs_6_
  92.6 1.1 %unpack.1 = f32[128,8,256]{2,1,0:T(8,128)} custom-call(f32[128,256]{1,0:T(8,128)S(1)} %collective-permute-done.13.refs_0_, f32[128,256]{1,0:T(8,128)S(1)} %collective-permute-done.14.refs_1_, f32[128,256]{1,0:T(8,128)S(1)} %collective-permute-done.15.refs_2_, f32[128,256]{1,0:T(8,128)S(1)} %collective-permute-done.16.refs_3_, ...), custom_call_target="tpu_custom_call" | custom-call | tf_op jit(solution)/shard_map/unpack/pallas_call | solution.py:515
  (3 shorter events, 0.0 us)
Async XLA Ops:
  0.0 1.2 %copy-start = (f32[128,8,256]{2,1,0:T(8,128)S(1)}, f32[128,8,256]{2,1,0:T(8,128)}, u32[]{:S(2)}) copy-start(f32[128,8,256]{2,1,0:T(8,128)} %refs_0_.5) | copy-start | bytes 3145732
  1.2 0.8 copy-start.1
  2.3 15.0 %collective-permute-start = (f32[264,256]{1,0:T(8,128)S(1)}, f32[264,256]{1,0:T(8,128)S(1)}, u32[]{:S(2)}, u32[]{:S(2)}) collective-permute-start(f32[264,256]{1,0:T(8,128)S(1)} %get-tuple-element.48), channel_id=1, source_target_pairs={{0,8},{16,24},{8,0},{24,16},{1,9},{17,25},{9,1},{25,17},{2,10},{18... | collective-permute-start | bytes 811016 | tf_op jit(solution)/shard_map/ppermute | solution.py:551
  2.4 5.0 %copy-start.2 = (f32[128]{0:T(128)S(1)}, f32[128]{0:T(128)}, u32[]{:S(2)}) copy-start(f32[128]{0:T(128)} %param.9) | copy-start | bytes 1540
  2.4 14.9 %collective-permute-start.1 = (f32[264,256]{1,0:T(8,128)S(1)}, f32[264,256]{1,0:T(8,128)S(1)}, u32[]{:S(2)}, u32[]{:S(2)}) collective-permute-start(f32[264,256]{1,0:T(8,128)S(1)} %get-tuple-element.49), channel_id=1, source_target_pairs={{8,16},{16,8},{9,17},{17,9},{10,18},{18,10},{11,19},{19,11},{12,20... | collective-permute-start | bytes 811016 | tf_op jit(solution)/shard_map/ppermute | solution.py:551
  9.0 11.9 %collective-permute-start.3 = (f32[2,128,256]{2,1,0:T(8,128)S(1)}, f32[2,128,256]{2,1,0:T(8,128)S(1)}, u32[]{:S(2)}, u32[]{:S(2)}) collective-permute-start(f32[2,128,256]{2,1,0:T(8,128)S(1)} %get-tuple-element.53), channel_id=1, source_target_pairs={{4,2},{5,3},{2,4},{3,5},{12,10},{13,11},{10,12},{11,13},{20,18},{2... | collective-permute-start | bytes 786440 | tf_op jit(solution)/shard_map/ppermute | solution.py:567
  9.6 18.2 %collective-permute-start.4 = (f32[2,128,256]{2,1,0:T(8,128)S(1)}, f32[2,128,256]{2,1,0:T(8,128)S(1)}, u32[]{:S(2)}, u32[]{:S(2)}) collective-permute-start(f32[2,128,256]{2,1,0:T(8,128)S(1)} %get-tuple-element.54), channel_id=1, source_target_pairs={{6,2},{7,3},{0,4},{1,5},{14,10},{15,11},{8,12},{9,13},{22,18},{23,... | collective-permute-start | bytes 786440 | tf_op jit(solution)/shard_map/ppermute | solution.py:567
  15.8 13.9 %collective-permute-start.5 = (f32[2,128,256]{2,1,0:T(8,128)S(1)}, f32[2,128,256]{2,1,0:T(8,128)S(1)}, u32[]{:S(2)}, u32[]{:S(2)}) collective-permute-start(f32[2,128,256]{2,1,0:T(8,128)S(1)} %get-tuple-element.55), channel_id=1, source_target_pairs={{0,2},{1,3},{6,4},{7,5},{8,10},{9,11},{14,12},{15,13},{16,18},{17,... | collective-permute-start | bytes 786440 | tf_op jit(solution)/shard_map/ppermute | solution.py:567
  18.3 20.7 %collective-permute-start.6 = (f32[2,128,256]{2,1,0:T(8,128)S(1)}, f32[2,128,256]{2,1,0:T(8,128)S(1)}, u32[]{:S(2)}, u32[]{:S(2)}) collective-permute-start(f32[2,128,256]{2,1,0:T(8,128)S(1)} %get-tuple-element.56), channel_id=1, source_target_pairs={{2,0},{3,1},{4,6},{5,7},{10,8},{11,9},{12,14},{13,15},{18,16},{19,... | collective-permute-start | bytes 786440 | tf_op jit(solution)/shard_map/ppermute | solution.py:567
  19.6 19.4 %collective-permute-start.7 = (f32[2,128,256]{2,1,0:T(8,128)S(1)}, f32[2,128,256]{2,1,0:T(8,128)S(1)}, u32[]{:S(2)}, u32[]{:S(2)}) collective-permute-start(f32[2,128,256]{2,1,0:T(8,128)S(1)} %get-tuple-element.57), channel_id=1, source_target_pairs={{4,0},{5,1},{2,6},{3,7},{12,8},{13,9},{10,14},{11,15},{20,16},{21,... | collective-permute-start | bytes 786440 | tf_op jit(solution)/shard_map/ppermute | solution.py:567
  20.9 6.2 %copy-start.5 = (s32[1,512]{1,0:T(1,128)S(1)}, s32[1,512]{1,0:T(1,128)}, u32[]{:S(2)}) copy-start(s32[1,512]{1,0:T(1,128)} %param.10) | copy-start | bytes 6148
  20.9 18.0 %collective-permute-start.8 = (f32[2,128,256]{2,1,0:T(8,128)S(1)}, f32[2,128,256]{2,1,0:T(8,128)S(1)}, u32[]{:S(2)}, u32[]{:S(2)}) collective-permute-start(f32[2,128,256]{2,1,0:T(8,128)S(1)} %get-tuple-element.58), channel_id=1, source_target_pairs={{6,0},{7,1},{0,6},{1,7},{14,8},{15,9},{8,14},{9,15},{22,16},{23,17... | collective-permute-start | bytes 786440 | tf_op jit(solution)/shard_map/ppermute | solution.py:567
  27.1 0.7 copy-start.3
  27.1 0.7 copy-start.4
  27.8 7.2 %collective-permute-start.2 = (f32[8,512]{1,0:T(8,128)S(1)}, f32[8,512]{1,0:T(8,128)S(1)}, u32[]{:S(2)}, u32[]{:S(2)}) collective-permute-start(f32[8,512]{1,0:T(8,128)S(1)} %concatenate.3.refs_0_), channel_id=1, source_target_pairs={{8,15},{9,14},{10,13},{11,12},{12,11},{13,10},{14,9},{15,8},{24,31... | collective-permute-start | bytes 49160 | tf_op jit(solution)/shard_map/ppermute | solution.py:594
  39.0 2.7 %collective-permute-start.9 = (f32[4,128,256]{2,1,0:T(8,128)S(1)}, f32[4,128,256]{2,1,0:T(8,128)S(1)}, u32[]{:S(2)}, u32[]{:S(2)}) collective-permute-start(f32[4,128,256]{2,1,0:T(8,128)S(1)} %get-tuple-element.61.refs_1_), channel_id=1, source_target_pairs={{0,1},{1,0},{2,3},{3,2},{4,5},{5,4},{6,7},{7,6},{8,9},{9,8},{10,11... | collective-permute-start | bytes 1572872 | tf_op jit(solution)/shard_map/ppermute | solution.py:619
  39.1 7.4 %collective-permute-start.10 = (f32[520,256]{1,0:T(8,128)S(1)}, f32[520,256]{1,0:T(8,128)S(1)}, u32[]{:S(2)}, u32[]{:S(2)}) collective-permute-start(f32[520,256]{1,0:T(8,128)S(1)} %get-tuple-element.60.refs_2_.refs_1_.refs_0_), channel_id=1, source_target_pairs={{0,1},{1,0},{2,3},{3,2},{4,5},{5,4},{6,7},{7,6},{8,9},{9,8},{10,11... | collective-permute-start | bytes 1597448 | tf_op jit(solution)/shard_map/ppermute | solution.py:621
  39.6 12.0 %collective-permute-start.11 = (f32[520,256]{1,0:T(8,128)S(1)}, f32[520,256]{1,0:T(8,128)S(1)}, u32[]{:S(2)}, u32[]{:S(2)}) collective-permute-start(f32[520,256]{1,0:T(8,128)S(1)} %get-tuple-element.60.refs_2_.refs_1_.refs_0_), channel_id=1, source_target_pairs={{1,2},{2,1},{3,4},{4,3},{5,6},{6,5},{7,15},{8,16},{9,10},{10,9},{1... | collective-permute-start | bytes 1597448 | tf_op jit(solution)/shard_map/ppermute | solution.py:620
  41.7 15.5 %collective-permute-start.12 = (f32[4,128,256]{2,1,0:T(8,128)S(1)}, f32[4,128,256]{2,1,0:T(8,128)S(1)}, u32[]{:S(2)}, u32[]{:S(2)}) collective-permute-start(f32[4,128,256]{2,1,0:T(8,128)S(1)} %collective-permute-done.9.refs_4_.refs_2_.refs_1_), channel_id=1, source_target_pairs={{1,2},{2,1},{3,4},{4,3},{5,6},{6,5},{7,15},{8,16},{9,10},{10,9},{1... | collective-permute-start | bytes 1572872 | tf_op jit(solution)/shard_map/ppermute | solution.py:622
  66.2 7.2 %collective-permute-start.13 = (f32[128,256]{1,0:T(8,128)S(1)}, f32[128,256]{1,0:T(8,128)S(1)}, u32[]{:S(2)}, u32[]{:S(2)}) collective-permute-start(f32[128,256]{1,0:T(8,128)S(1)} %get-tuple-element.74), channel_id=1, source_target_pairs={{0,7},{1,6},{2,5},{3,4},{4,3},{5,2},{6,1},{7,0},{8,15},{9,14},{10,... | collective-permute-start | bytes 393224 | tf_op jit(solution)/shard_map/ppermute | solution.py:656
  68.4 14.5 %collective-permute-start.14 = (f32[128,256]{1,0:T(8,128)S(1)}, f32[128,256]{1,0:T(8,128)S(1)}, u32[]{:S(2)}, u32[]{:S(2)}) collective-permute-start(f32[128,256]{1,0:T(8,128)S(1)} %get-tuple-element.75), channel_id=1, source_target_pairs={{0,6},{1,7},{2,4},{3,5},{4,2},{5,3},{6,0},{7,1},{8,14},{9,15},{10,... | collective-permute-start | bytes 393224 | tf_op jit(solution)/shard_map/ppermute | solution.py:656
  69.4 18.6 %collective-permute-start.15 = (f32[128,256]{1,0:T(8,128)S(1)}, f32[128,256]{1,0:T(8,128)S(1)}, u32[]{:S(2)}, u32[]{:S(2)}) collective-permute-start(f32[128,256]{1,0:T(8,128)S(1)} %get-tuple-element.81), channel_id=1, source_target_pairs={{0,5},{1,4},{2,7},{3,6},{4,1},{5,0},{6,3},{7,2},{8,13},{9,12},{10,... | collective-permute-start | bytes 393224 | tf_op jit(solution)/shard_map/ppermute | solution.py:656
  69.5 21.5 %collective-permute-start.16 = (f32[128,256]{1,0:T(8,128)S(1)}, f32[128,256]{1,0:T(8,128)S(1)}, u32[]{:S(2)}, u32[]{:S(2)}) collective-permute-start(f32[128,256]{1,0:T(8,128)S(1)} %get-tuple-element.82), channel_id=1, source_target_pairs={{0,4},{1,5},{2,6},{3,7},{4,0},{5,1},{6,2},{7,3},{8,12},{9,13},{10,... | collective-permute-start | bytes 393224 | tf_op jit(solution)/shard_map/ppermute | solution.py:656
  73.3 17.7 %collective-permute-start.17 = (f32[128,256]{1,0:T(8,128)S(1)}, f32[128,256]{1,0:T(8,128)S(1)}, u32[]{:S(2)}, u32[]{:S(2)}) collective-permute-start(f32[128,256]{1,0:T(8,128)S(1)} %get-tuple-element.83), channel_id=1, source_target_pairs={{0,3},{1,2},{2,1},{3,0},{4,7},{5,6},{6,5},{7,4},{8,11},{9,10},{10,... | collective-permute-start | bytes 393224 | tf_op jit(solution)/shard_map/ppermute | solution.py:656
  73.4 19.2 %collective-permute-start.18 = (f32[128,256]{1,0:T(8,128)S(1)}, f32[128,256]{1,0:T(8,128)S(1)}, u32[]{:S(2)}, u32[]{:S(2)}) collective-permute-start(f32[128,256]{1,0:T(8,128)S(1)} %get-tuple-element.84), channel_id=1, source_target_pairs={{0,2},{1,3},{2,0},{3,1},{4,6},{5,7},{6,4},{7,5},{8,10},{9,11},{10,... | collective-permute-start | bytes 393224 | tf_op jit(solution)/shard_map/ppermute | solution.py:656
  82.9 9.7 %collective-permute-start.19 = (f32[128,256]{1,0:T(8,128)S(1)}, f32[128,256]{1,0:T(8,128)S(1)}, u32[]{:S(2)}, u32[]{:S(2)}) collective-permute-start(f32[128,256]{1,0:T(8,128)S(1)} %get-tuple-element.85), channel_id=1, source_target_pairs={{0,1},{1,0},{2,3},{3,2},{4,5},{5,4},{6,7},{7,6},{8,9},{9,8},{10,11... | collective-permute-start | bytes 393224 | tf_op jit(solution)/shard_map/ppermute | solution.py:656

commit v21 on v20

--- a/solution.py
+++ b/solution.py
@@ -141,8 +141,8 @@
 
 def collect_kernel(order, info, mine_ref, other_ref, *refs):
     chips = len(order)
-    near_other, near_own, observed_ref = refs[-3:]
-    step = near_other.shape[1]
+    *near_others, near_own, observed_ref = refs[-4:]
+    portion, step, _ = near_others[0].shape
     observed_ref[...] = jnp.where(info[2] == 1, other_ref[...], mine_ref[...])
     near_own[pl.ds(chips * step, PADDING), :] = jnp.zeros((PADDING, near_own.shape[1]), F32)
     chip = info[0]
@@ -154,8 +154,12 @@
 
             @pl.when(here)
             def _():
-                near_other[block] = ref[0]
                 near_own[rows, :] = ref[1]
+                for index, near_other in enumerate(near_others):
+
+                    @pl.when(lax.div(block, portion) == index)
+                    def _():
+                        near_other[lax.rem(block, portion)] = ref[0]
 
 
 def unpack_kernel(order, info, *refs):
@@ -233,12 +237,16 @@
     return (dot(parts[0], chosen) + (dot(parts[1], chosen) + dot(parts[2], chosen)))[:1]
 
 
+def each(*refs):
+    return [ref.at[index] for ref in refs for index in range(ref.shape[0])]
+
+
 def prepare_kernel(
-    info, observed_ref, near_other, near_own, far_other, far_own,
+    info, observed_ref, near_first, near_second, near_own, far_other, far_first, far_second,
     spread_high, spread_low, own_high, own_low, own_part, seen_ref, direction_ref,
     anomaly, high_ref, low_ref,
 ):
-    chips, step, width = near_other.shape
+    chips, (_, step, width) = info[3], near_first.shape
     members = 2 * chips * step
     cells, _, _, scale = observations(info, observed_ref, width, math.sqrt(members - 1))
     chosen = one_hot(cells, width, 2 * width)
@@ -247,9 +255,9 @@
     for place in range(2):
         columns = pl.ds(place * width, width)
         if place:
-            rows = [near_own.at[block, :] for block in blocks[:chips]] + [far_own.at[chip] for chip in range(chips)]
+            rows = [near_own.at[block, :] for block in blocks[:chips]] + each(far_first, far_second)
         else:
-            rows = [near_other.at[chip] for chip in range(chips)] + [far_other.at[block, :] for block in blocks[:chips]]
+            rows = each(near_first, near_second) + [far_other.at[block, :] for block in blocks[:chips]]
         means.append(mean_of([row[...] for row in rows], members))
         for block, row in zip(blocks, rows):
             part = row[...] - means[-1]
@@ -365,48 +373,74 @@
     right_ref[...] = product([own_high[:, members], own_low[:, members]], [high, low])
 
 
-def analysed_row(info, x, near_own, far_own, direction_ref, halves, rests, parts, sides):
-    chips, step, _ = far_own.shape
+def more_kernel(
+    info, observed_ref, high_in, low_in, own_high, own_low, direction_ref, gram_half, right_half, known_half, rest_ref,
+    high_ref, low_ref, gram_ref, right_ref, known_ref,
+):
+    portion, step, width = rest_ref.shape
+    count = info[3] * step
+    first = (1 - at_border(info)) * count
+    cells, _, _, scale = observations(info, observed_ref, width, math.sqrt(2 * count - 1))
+    shift, along, total, taken = (known_half[pl.ds(index, 1), :] for index in range(4))
+    more, further = shifted_spread(
+        each(rest_ref),
+        [pl.ds(pl.multiple_of(first + index * step, step), step) for index in range(portion)],
+        direction_ref, shift, along, one_hot(cells, 0, width), scale, high_in, low_in, high_ref, low_ref,
+    )
+    for index, known in enumerate((shift, along, total + more, taken + further)):
+        known_ref[pl.ds(index, 1), :] = known
+    high, low = high_ref[...], low_ref[...]
+    gram_ref[...] = gram_half[...] + gram(high, low)
+    members = pl.ds(pl.multiple_of(first, portion * step), portion * step)
+    right_ref[...] = right_half[...] + product([own_high[:, members], own_low[:, members]], [high, low])
+
+
+def analysed_row(info, x, near_own, far_owns, direction_ref, spreads, parts, sides):
+    portion, step, _ = far_owns[0].shape
     chip, mine = info[0] ^ (x // 2), x % 2
+    early = chip < portion
     rows = pl.ds(pl.multiple_of(chip * step, step), step)
+    place = lax.rem(chip, portion)
+    within = pl.ds(pl.multiple_of(place * step, step), step)
     spread = [
-        jnp.where(at_border(info) == mine, half[rows, :], rest[rows, :]) for half, rest in zip(halves, rests)
+        jnp.where(at_border(info) == mine, half[rows, :], jnp.where(early, first[within, :], second[within, :]))
+        for half, first, second in spreads
     ]
-    block = pl.ds(pl.multiple_of((mine * chips + chip) * step, step), step)
-    own = far_own[chip] if mine else near_own[rows, :]
+    block = pl.ds(pl.multiple_of((mine * info[3] + chip) * step, step), step)
+    own = jnp.where(early, far_owns[0][place], far_owns[1][place]) if mine else near_own[rows, :]
     return own + sides[0:1] + product(spread, parts) + doubled(direction_ref[block, :]) * sides[1:2]
 
 
 def others_kernel(
-    order, info, near_own, far_own, direction_ref, high_half, low_half, high_rest, low_rest,
-    solved_high, solved_low, sides_ref, *out_refs,
+    order, info, near_own, far_first, far_second, direction_ref, high_half, low_half, high_first, low_first,
+    high_second, low_second, solved_high, solved_low, sides_ref, *out_refs,
 ):
     parts = [solved_high[...], solved_low[...]]
+    spreads = ((high_half, high_first, high_second), (low_half, low_first, low_second))
     for x, out_ref in zip(order, out_refs):
         out_ref[...] = analysed_row(
-            info, x, near_own, far_own, direction_ref, (high_half, low_half), (high_rest, low_rest), parts, sides_ref[...]
+            info, x, near_own, (far_first, far_second), direction_ref, spreads, parts, sides_ref[...]
         )
 
 
 def region_kernel(
-    order, info, observed_ref, near_own, far_own, high_in, low_in, own_high, own_low, own_part, seen_ref,
-    direction_ref, high_half, low_half, gram_half, right_half, known_ref, rest_ref, *refs,
+    order, info, observed_ref, near_own, far_first, far_second, high_in, low_in, own_high, own_low, own_part, seen_ref,
+    direction_ref, high_half, low_half, high_first, low_first, gram_half, right_half, known_ref, rest_ref, *refs,
 ):
-    chips, step, width = far_own.shape
+    chips, (portion, step, width) = info[3], rest_ref.shape
     high_rest, low_rest, solved_high, solved_low, sides_ref = refs[:5]
     out_refs, (factor, squared, answer) = refs[5:-3], refs[-3:]
     count = chips * step
     members = 2 * count
     slots = observed_ref.shape[1]
     root = math.sqrt(members - 1)
-    part = at_border(info)
-    first = (1 - part) * count
+    first = (1 - at_border(info)) * count + (chips - portion) * step
     cells, slot_weight, values, scale = observations(info, observed_ref, width, root)
     chosen = one_hot(cells, 0, width)
     shift, along, total, taken = (known_ref[pl.ds(index, 1), :] for index in range(4))
     more, further = shifted_spread(
-        [rest_ref.at[chip] for chip in range(chips)],
-        [pl.ds(pl.multiple_of(first + chip * step, step), step) for chip in range(chips)],
+        each(rest_ref),
+        [pl.ds(pl.multiple_of(first + index * step, step), step) for index in range(portion)],
         direction_ref, shift, along, chosen, scale, high_in, low_in, high_rest, low_rest,
     )
     left = (total + more) * (1.0 / members)
@@ -425,7 +459,7 @@
     high, low = high_rest[...], low_rest[...]
     over = dot_t(excess[0], excess[0]) + (dot_t(excess[0], excess[1]) + dot_t(excess[1], excess[0]))
     factor[...] = gram(high, low) + (gram_half[...] - over) + jnp.where(eye, 1.0, 0.0)
-    rows = pl.ds(pl.multiple_of(first, count), count)
+    rows = pl.ds(pl.multiple_of(first, portion * step), portion * step)
     answer[pl.ds(0, width), :] = right_half[...] + product([own_high[:, rows], own_low[:, rows]], [high, low])
     answer[pl.ds(width, 8), :] = jnp.where(
         lax.broadcasted_iota(jnp.int32, (8, slots), 0) == 0, jnp.broadcast_to(common, (8, slots)), 0.0
@@ -496,9 +530,10 @@
     parts = [part * jnp.asarray(-0.5, BF16) for part in parts]
     sides_ref[...] = sides
     solved_high[...], solved_low[...] = parts
+    spreads = ((high_half, high_first, high_rest), (low_half, low_first, low_rest))
     for x, out_ref in zip(order, out_refs):
         out_ref[...] = analysed_row(
-            info, x, near_own, far_own, direction_ref, (high_half, low_half), (high_rest, low_rest), parts, sides
+            info, x, near_own, (far_first, far_second), direction_ref, spreads, parts, sides
         )
 
 
@@ -611,21 +646,21 @@
                     if 0 <= to < patches:
                         borders.append((device(p, chip, core), device(to, chip, core)))
 
-    half = array(chips, step, width)
-    near_other, near_own, observed = call(
+    portion = array(chips // 2, step, width)
+    near_first, near_second, near_own, observed = call(
         functools.partial(collect_kernel, order), "collect",
-        [half, array(chips * step + PADDING, width), array(8, slots)], [mine, other] + pieces_in,
-    )
-    far_own = lax.ppermute(near_other, axes, siblings)
+        [portion, portion, array(chips * step + PADDING, width), array(8, slots)], [mine, other] + pieces_in,
+    )
+    far_first, far_second = (lax.ppermute(near, axes, siblings) for near in (near_first, near_second))
     got_half = lax.ppermute(near_own, axes, borders)
     far_other = lax.ppermute(near_own, axes, siblings)
-    got_rest = lax.ppermute(far_own, axes, borders)
+    got_first, got_second = (lax.ppermute(far, axes, borders) for far in (far_first, far_second))
 
     prepared = call(
         prepare_kernel, "prepare",
         [bfloat(members, slots)] * 2 + [bfloat(width, members)] * 2
         + [array(width, width // 2), array(8, slots), array(members, width // 2)],
-        [observed, near_other, near_own, far_other, far_own],
+        [observed, near_first, near_second, near_own, far_other, far_first, far_second],
         [pltpu.VMEM((members, 2 * width), F32)] + [pltpu.VMEM((members, 2 * width), BF16)] * 2,
         flops=8 * members * slots * width, limit=20,
     )
@@ -636,18 +671,25 @@
         [observed, *prepared[:4], prepared[6], got_half],
         flops=10 * halves * slots * slots, limit=20,
     )
+    quarter = members // 4
+    more = call(
+        more_kernel, "more",
+        [bfloat(quarter, slots)] * 2 + [array(slots, slots), array(width, slots), array(8, width)],
+        [observed, *prepared[:4], prepared[6], *middle[2:], got_first],
+        flops=5 * halves * slots * slots, limit=20,
+    )
     order = sorted(range(lanes), key=lambda x: (x.bit_length() != lanes.bit_length() - 1, -x))
     row = array(step, width)
     *shared, first, second = call(
         functools.partial(region_kernel, order[:2]), "region",
-        [bfloat(halves, slots)] * 2 + [bfloat(slots, width)] * 2 + [array(8, width)] + [row] * 2,
-        [observed, near_own, far_own, *prepared, *middle, got_rest],
+        [bfloat(quarter, slots)] * 2 + [bfloat(slots, width)] * 2 + [array(8, width)] + [row] * 2,
+        [observed, near_own, far_first, far_second, *prepared, *middle[:2], *more, got_second],
         [pltpu.VMEM((slots, slots), F32)] * 2 + [pltpu.VMEM((width + 8, slots), F32)],
         limit=24,
     )
     others = call(
         functools.partial(others_kernel, order[2:]), "others", [row] * (lanes - 2),
-        [near_own, far_own, prepared[6], *middle[:2], *shared],
+        [near_own, far_first, far_second, prepared[6], *middle[:2], *more[:2], *shared],
         flops=6 * members * slots * width, limit=16,
     )
     analysed = dict(zip(order, [first, second, *others]))

time: 94.4 us -> 94.7 us (level)
  starting transfers between devices: 46.8 us -> 51.2 us
  waiting for transfers between devices: 24.3 us -> 20.6 us
    ppermute x2 -> x4, starting transfers between devices: 4.88 us -> 7.49 us  [the longest x2 6.91 us: per_device(): lax.ppermute(far, axes, borders)]
    ppermute x7, starting transfers between devices: 16 us -> 18.2 us  [swapped(): lax.ppermute(analysed[x], 'member', [(i, i ^ x) for i in range(lanes)])]
    ppermute x2 -> x4, waiting for transfers between devices: 3.83 us -> 1.7 us  [the longest x2 1.03 us: per_device(): lax.ppermute(near, axes, siblings)]
    ppermute x1, waiting for transfers between devices: 1.69 us -> 0.01 us  [per_device(): got_half = lax.ppermute(near_own, axes, borders)]
    pallas_call x9 -> x10, Pallas kernels: 18.9 us -> 19.5 us  [call(): pl.pallas_call(lambda *refs: kernel(position(), *refs), out_shape=out_sha...]
  transfers between devices with their start and end apart: 20 -> 22, of which waited for: 7 -> 8; matrix products, arithmetic and copies ran while one was open for 0% -> 0% of each run, Pallas kernels for 9% -> 10%
where the time goes in v21:
time: 94.7 us; the launch traced here: 95.1 us
  starting transfers between devices  51.2 us (54%)
  waiting for transfers between devices  20.6 us (22%)
  Pallas kernels  19.5 us (21%)
  local copies, waits for them, and re-layouts  2.71 us (3%)
  between operations  1.14 us (1%)
    pallas_call x10, Pallas kernels, call(): pl.pallas_call(lambda *refs: kernel(position(), *refs), out_shape=out_sha...  19.5 us
    ppermute x7, starting transfers between devices, swapped(): lax.ppermute(analysed[x], 'member', [(i, i ^ x) for i in range(lanes)])  18.2 us
    ppermute x6, starting transfers between devices, between(): lax.ppermute(message, 'member', [(2 * a + core, 2 * b + core) for a, b in...  16.4 us
    ppermute x7, waiting for transfers between devices, swapped(): lax.ppermute(analysed[x], 'member', [(i, i ^ x) for i in range(lanes)])  9.68 us
    ppermute x2, starting transfers between devices, per_device(): lax.ppermute(far, axes, borders)  6.91 us
    ppermute x1, waiting for transfers between devices, per_device(): lax.ppermute(mine, axes, [(p * lanes + i, p * lanes + lanes - 1 - i) for...  5.27 us
    ppermute x2, starting transfers between devices, swap(): lax.ppermute(message, 'patch', [(p, p + 1) for p in lower] + [(p + 1, p)...  5.06 us
    ppermute x6, waiting for transfers between devices, between(): lax.ppermute(message, 'member', [(2 * a + core, 2 * b + core) for a, b in...  3.91 us
  transfers between devices with their start and end apart: 22, of which 8 were waited for; matrix products, arithmetic and copies ran while one was open for 0% of the time, Pallas kernels for 10%

profile of v21, /device:TPU:2, one launch (start us, length us, event | category | flops | bytes accessed | tf_op | source)
XLA Modules:
  0.0 95.1 jit_solution(12331613392321613338)
XLA Ops:
  0.0 1.2 %copy-done = f32[128,8,256]{2,1,0:T(8,128)S(1)} copy-done((f32[128,8,256]{2,1,0:T(8,128)S(1)}, f32[128,8,256]{2,1,0:T(8,128)}, u32[]{:S(2)}) %copy-start) | copy-done | bytes 1048600
  1.2 0.8 copy-done.1
  2.0 0.3 pack.1
  2.3 0.1 collective-permute-start
  2.4 0.0 copy-start.2
  2.4 5.0 %collective-permute-start.1 = (f32[264,256]{1,0:T(8,128)S(1)}, f32[264,256]{1,0:T(8,128)S(1)}, u32[]{:S(2)}, u32[]{:S(2)}) collective-permute-start(f32[264,256]{1,0:T(8,128)S(1)} %get-tuple-element.55), channel_id=1, source_target_pairs={{8,16},{16,8},{9,17},{17,9},{10,18},{18,10},{11,19},{19,11},{12,20... | collective-permute-start | bytes 811016 | tf_op jit(solution)/shard_map/ppermute | solution.py:586
  7.4 0.0 copy-done.2
  7.4 1.6 %inner.1 = (f32[4,128,256]{2,1,0:T(8,128)S(1)}, f32[128,128]{1,0:T(8,128)S(1)}, f32[2,128,256]{2,1,0:T(8,128)S(1)}, f32[2,128,256]{2,1,0:T(8,128)S(1)}, f32[2,12...) custom-call(f32[128,8,256]{2,1,0:T(8,128)S(1)} %copy-done, f32[4,8,256]{2,1,0:T(8,128)S(1)} %copy-done.1, f32[1,128]{1,0:T(1,128)S(1)} %bitcast.2), custom_call_target="tpu_custom_call" | custom-call | tf_op jit(solution)/shard_map/inner/pallas_call | solution.py:550
  9.0 0.7 collective-permute-start.3
  9.6 6.2 %collective-permute-start.4 = (f32[2,128,256]{2,1,0:T(8,128)S(1)}, f32[2,128,256]{2,1,0:T(8,128)S(1)}, u32[]{:S(2)}, u32[]{:S(2)}) collective-permute-start(f32[2,128,256]{2,1,0:T(8,128)S(1)} %get-tuple-element.60), channel_id=1, source_target_pairs={{6,2},{7,3},{0,4},{1,5},{14,10},{15,11},{8,12},{9,13},{22,18},{23,... | collective-permute-start | bytes 786440 | tf_op jit(solution)/shard_map/ppermute | solution.py:602
  15.8 1.4 %collective-permute-start.5 = (f32[2,128,256]{2,1,0:T(8,128)S(1)}, f32[2,128,256]{2,1,0:T(8,128)S(1)}, u32[]{:S(2)}, u32[]{:S(2)}) collective-permute-start(f32[2,128,256]{2,1,0:T(8,128)S(1)} %get-tuple-element.61), channel_id=1, source_target_pairs={{0,2},{1,3},{6,4},{7,5},{8,10},{9,11},{14,12},{15,13},{16,18},{17,... | collective-permute-start | bytes 786440 | tf_op jit(solution)/shard_map/ppermute | solution.py:602
  17.3 0.0 collective-permute-done.refs_4_
  17.3 0.0 collective-permute-done.1.refs_5_
  17.3 0.9 edge.1
  18.3 0.0 copy-start.5
  18.3 1.3 %collective-permute-start.6 = (f32[2,128,256]{2,1,0:T(8,128)S(1)}, f32[2,128,256]{2,1,0:T(8,128)S(1)}, u32[]{:S(2)}, u32[]{:S(2)}) collective-permute-start(f32[2,128,256]{2,1,0:T(8,128)S(1)} %get-tuple-element.62), channel_id=1, source_target_pairs={{2,0},{3,1},{4,6},{5,7},{10,8},{11,9},{12,14},{13,15},{18,16},{19,... | collective-permute-start | bytes 786440 | tf_op jit(solution)/shard_map/ppermute | solution.py:602
  19.6 1.3 %collective-permute-start.7 = (f32[2,128,256]{2,1,0:T(8,128)S(1)}, f32[2,128,256]{2,1,0:T(8,128)S(1)}, u32[]{:S(2)}, u32[]{:S(2)}) collective-permute-start(f32[2,128,256]{2,1,0:T(8,128)S(1)} %get-tuple-element.63), channel_id=1, source_target_pairs={{4,0},{5,1},{2,6},{3,7},{12,8},{13,9},{10,14},{11,15},{20,16},{21,... | collective-permute-start | bytes 786440 | tf_op jit(solution)/shard_map/ppermute | solution.py:602
  20.9 0.0 collective-permute-done.3.refs_3_
  20.9 5.5 %collective-permute-start.8 = (f32[2,128,256]{2,1,0:T(8,128)S(1)}, f32[2,128,256]{2,1,0:T(8,128)S(1)}, u32[]{:S(2)}, u32[]{:S(2)}) collective-permute-start(f32[2,128,256]{2,1,0:T(8,128)S(1)} %get-tuple-element.64), channel_id=1, source_target_pairs={{6,0},{7,1},{0,6},{1,7},{14,8},{15,9},{8,14},{9,15},{22,16},{23,17... | collective-permute-start | bytes 786440 | tf_op jit(solution)/shard_map/ppermute | solution.py:602
  26.4 0.0 copy-done.5
  27.1 0.0 copy-start.3
  27.1 0.0 copy-start.4
  27.1 0.6 copy-done.3
  27.8 0.0 copy-done.4
  27.8 0.0 collective-permute-done.4.refs_4_
  27.8 1.9 %collective-permute-start.2 = (f32[8,512]{1,0:T(8,128)S(1)}, f32[8,512]{1,0:T(8,128)S(1)}, u32[]{:S(2)}, u32[]{:S(2)}) collective-permute-start(f32[8,512]{1,0:T(8,128)S(1)} %concatenate.3.refs_0_), channel_id=1, source_target_pairs={{8,15},{9,14},{10,13},{11,12},{12,11},{13,10},{14,9},{15,8},{24,31... | collective-permute-start | bytes 49160 | tf_op jit(solution)/shard_map/ppermute | solution.py:629
  29.7 0.0 collective-permute-done.5.refs_5_
  29.8 5.3 %collective-permute-done.2.refs_1_ = f32[8,512]{1,0:T(8,128)S(1)} collective-permute-done((f32[8,512]{1,0:T(8,128)S(1)}, f32[8,512]{1,0:T(8,128)S(1)}, u32[]{:S(2)}, u32[]{:S(2)}) %collective-permute-start.2) | collective-permute-done | bytes 16416 | tf_op jit(solution)/shard_map/ppermute | solution.py:629
  35.0 3.9 %collective-permute-done.6.refs_7_ = f32[2,128,256]{2,1,0:T(8,128)S(1)} collective-permute-done((f32[2,128,256]{2,1,0:T(8,128)S(1)}, f32[2,128,256]{2,1,0:T(8,128)S(1)}, u32[]{:S(2)}, u32[]{:S(2)}) %collective-permute-start.6) | collective-permute-done | bytes 262176 | tf_op jit(solution)/shard_map/ppermute | solution.py:602
  38.9 0.0 collective-permute-done.7.refs_8_
  38.9 0.0 collective-permute-done.8.refs_9_
  38.9 0.1 collect.1
  39.1 0.1 collective-permute-start.11
  39.2 2.1 %collective-permute-start.12 = (f32[520,256]{1,0:T(8,128)S(1)}, f32[520,256]{1,0:T(8,128)S(1)}, u32[]{:S(2)}, u32[]{:S(2)}) collective-permute-start(f32[520,256]{1,0:T(8,128)S(1)} %get-tuple-element.66.refs_3_.refs_1_.refs_0_), channel_id=1, source_target_pairs={{1,2},{2,1},{3,4},{4,3},{5,6},{6,5},{7,15},{8,16},{9,10},{10,9},{1... | collective-permute-start | bytes 1597448 | tf_op jit(solution)/shard_map/ppermute | solution.py:655
  41.3 0.4 collective-permute-start.9
  41.6 0.2 collective-permute-start.10
  41.8 1.0 %collective-permute-done.9.refs_5_.refs_2_.refs_1_ = f32[2,128,256]{2,1,0:T(8,128)S(1)} collective-permute-done((f32[2,128,256]{2,1,0:T(8,128)S(1)}, f32[2,128,256]{2,1,0:T(8,128)S(1)}, u32[]{:S(2)}, u32[]{:S(2)}) %collective-permute-start.9) | collective-permute-done | bytes 262176 | tf_op jit(solution)/shard_map/ppermute | solution.py:654
  42.9 4.6 %collective-permute-start.13 = (f32[2,128,256]{2,1,0:T(8,128)S(1)}, f32[2,128,256]{2,1,0:T(8,128)S(1)}, u32[]{:S(2)}, u32[]{:S(2)}) collective-permute-start(f32[2,128,256]{2,1,0:T(8,128)S(1)} %collective-permute-done.9.refs_5_.refs_2_.refs_1_), channel_id=1, source_target_pairs={{1,2},{2,1},{3,4},{4,3},{5,6},{6,5},{7,15},{8,16},{9,10},{10,9},{1... | collective-permute-start | bytes 786440 | tf_op jit(solution)/shard_map/ppermute | solution.py:657
  47.5 0.0 collective-permute-done.10.refs_6_.refs_3_.refs_2_
  47.5 2.3 %collective-permute-start.14 = (f32[2,128,256]{2,1,0:T(8,128)S(1)}, f32[2,128,256]{2,1,0:T(8,128)S(1)}, u32[]{:S(2)}, u32[]{:S(2)}) collective-permute-start(f32[2,128,256]{2,1,0:T(8,128)S(1)} %collective-permute-done.10.refs_6_.refs_3_.refs_2_), channel_id=1, source_target_pairs={{1,2},{2,1},{3,4},{4,3},{5,6},{6,5},{7,15},{8,16},{9,10},{10,9},{1... | collective-permute-start | bytes 786440 | tf_op jit(solution)/shard_map/ppermute | solution.py:657
  49.8 0.0 collective-permute-done.11.refs_4_
  49.8 3.5 %prepare.1 = (bf16[1024,512]{1,0:T(8,128)(2,1)S(1)}, bf16[1024,512]{1,0:T(8,128)(2,1)S(1)}, bf16[256,1024]{1,0:T(8,128)(2,1)S(1)}, bf16[256,1024]{1,0:T(8,128)(2...) custom-call(f32[8,512]{1,0:T(8,128)S(1)} %get-tuple-element.65.refs_0_, ...), custom_call_target="tpu_custom_call" | custom-call | flops 1073741824 | tf_op jit(solution)/shard_map/prepare/pallas_call | solution.py:550
  53.3 0.0 collective-permute-done.12.refs_6_
  53.3 1.8 %middle.1 = (bf16[512,512]{1,0:T(8,128)(2,1)S(1)}, bf16[512,512]{1,0:T(8,128)(2,1)S(1)}, f32[512,512]{1,0:T(8,128)S(1)}, f32[256,512]{1,0:T(8,128)S(1)}, f32[8,256]{1,0:T(8,128)S(1)}) custom-call(f32[8,512]{1,0:T(8,128)S(1)} %get-tuple-element.65.refs_0_, bf16[1024,512]{1,0:T(8,128)(2,1)S(1)} %get-tuple-element.69.refs_1_.refs_4_, ...), custom_call_target="tpu_custom_call" | custom-call | flops 1342177280 | tf_op jit(solution)/shard_map/middle/pallas_call | solution.py:550
  55.1 0.0 collective-permute-done.13.refs_9_
  55.1 1.0 %more.1 = (bf16[256,512]{1,0:T(8,128)(2,1)S(1)}, bf16[256,512]{1,0:T(8,128)(2,1)S(1)}, f32[512,512]{1,0:T(8,128)S(1)}, f32[256,512]{1,0:T(8,128)S(1)}, f32[8,256]{1,0:T(8,128)S(1)}) custom-call(f32[8,512]{1,0:T(8,128)S(1)} %get-tuple-element.65.refs_0_, bf16[1024,512]{1,0:T(8,128)(2,1)S(1)} %get-tuple-element.69.refs_1_.refs_4_, ...), custom_call_target="tpu_custom_call" | custom-call | flops 671088640 | tf_op jit(solution)/shard_map/more/pallas_call | solution.py:550
  56.2 0.7 collective-permute-done.14.refs_18_
  56.8 8.3 %region.1 = (bf16[256,512]{1,0:T(8,128)(2,1)S(1)}, bf16[256,512]{1,0:T(8,128)(2,1)S(1)}, bf16[512,256]{1,0:T(8,128)(2,1)S(1)}, bf16[512,256]{1,0:T(8,128)(2,1)S(...) custom-call(f32[8,512]{1,0:T(8,128)S(1)} %get-tuple-element.65.refs_0_, ...), custom_call_target="tpu_custom_call" | custom-call | tf_op jit(solution)/shard_map/region/pallas_call | solution.py:550
  65.1 2.5 %collective-permute-start.15 = (f32[128,256]{1,0:T(8,128)S(1)}, f32[128,256]{1,0:T(8,128)S(1)}, u32[]{:S(2)}, u32[]{:S(2)}) collective-permute-start(f32[128,256]{1,0:T(8,128)S(1)} %get-tuple-element.86), channel_id=1, source_target_pairs={{0,7},{1,6},{2,5},{3,4},{4,3},{5,2},{6,1},{7,0},{8,15},{9,14},{10,... | collective-permute-start | bytes 393224 | tf_op jit(solution)/shard_map/ppermute | solution.py:698
  67.6 0.9 collective-permute-start.16
  68.5 0.9 others.1
  69.4 0.7 collective-permute-start.17
  70.0 2.3 %collective-permute-start.18 = (f32[128,256]{1,0:T(8,128)S(1)}, f32[128,256]{1,0:T(8,128)S(1)}, u32[]{:S(2)}, u32[]{:S(2)}) collective-permute-start(f32[128,256]{1,0:T(8,128)S(1)} %get-tuple-element.94), channel_id=1, source_target_pairs={{0,4},{1,5},{2,6},{3,7},{4,0},{5,1},{6,2},{7,3},{8,12},{9,13},{10,... | collective-permute-start | bytes 393224 | tf_op jit(solution)/shard_map/ppermute | solution.py:698
  72.3 0.3 collective-permute-start.19
  72.7 0.1 collective-permute-done.15.refs_0_
  72.8 11.2 %collective-permute-start.20 = (f32[128,256]{1,0:T(8,128)S(1)}, f32[128,256]{1,0:T(8,128)S(1)}, u32[]{:S(2)}, u32[]{:S(2)}) collective-permute-start(f32[128,256]{1,0:T(8,128)S(1)} %get-tuple-element.96), channel_id=1, source_target_pairs={{0,2},{1,3},{2,0},{3,1},{4,6},{5,7},{6,4},{7,5},{8,10},{9,11},{10,... | collective-permute-start | bytes 393224 | tf_op jit(solution)/shard_map/ppermute | solution.py:698
  84.0 0.0 collective-permute-done.16.refs_1_
  84.0 0.3 collective-permute-start.21
  84.3 4.7 %collective-permute-done.17.refs_2_ = f32[128,256]{1,0:T(8,128)S(1)} collective-permute-done((f32[128,256]{1,0:T(8,128)S(1)}, f32[128,256]{1,0:T(8,128)S(1)}, u32[]{:S(2)}, u32[]{:S(2)}) %collective-permute-start.17) | collective-permute-done | bytes 131104 | tf_op jit(solution)/shard_map/ppermute | solution.py:698
  89.0 3.1 %collective-permute-done.18.refs_3_ = f32[128,256]{1,0:T(8,128)S(1)} collective-permute-done((f32[128,256]{1,0:T(8,128)S(1)}, f32[128,256]{1,0:T(8,128)S(1)}, u32[]{:S(2)}, u32[]{:S(2)}) %collective-permute-start.18) | collective-permute-done | bytes 131104 | tf_op jit(solution)/shard_map/ppermute | solution.py:698
  92.1 0.0 collective-permute-done.19.refs_4_
  92.1 1.7 %collective-permute-done.20.refs_5_ = f32[128,256]{1,0:T(8,128)S(1)} collective-permute-done((f32[128,256]{1,0:T(8,128)S(1)}, f32[128,256]{1,0:T(8,128)S(1)}, u32[]{:S(2)}, u32[]{:S(2)}) %collective-permute-start.20) | collective-permute-done | bytes 131104 | tf_op jit(solution)/shard_map/ppermute | solution.py:698
  93.8 0.0 collective-permute-done.21.refs_6_
  93.8 1.1 %unpack.1 = f32[128,8,256]{2,1,0:T(8,128)} custom-call(f32[128,256]{1,0:T(8,128)S(1)} %collective-permute-done.15.refs_0_, f32[128,256]{1,0:T(8,128)S(1)} %collective-permute-done.16.refs_1_, f32[128,256]{1,0:T(8,128)S(1)} %collective-permute-done.17.refs_2_, f32[128,256]{1,0:T(8,128)S(1)} %collective-permute-done.18.refs_3_, ...), custom_call_target="tpu_custom_call" | custom-call | tf_op jit(solution)/shard_map/unpack/pallas_call | solution.py:550
  (5 shorter events, 0.0 us)
Async XLA Ops:
  0.0 1.2 %copy-start = (f32[128,8,256]{2,1,0:T(8,128)S(1)}, f32[128,8,256]{2,1,0:T(8,128)}, u32[]{:S(2)}) copy-start(f32[128,8,256]{2,1,0:T(8,128)} %refs_0_.5) | copy-start | bytes 3145732
  1.2 0.8 copy-start.1
  2.3 15.0 %collective-permute-start = (f32[264,256]{1,0:T(8,128)S(1)}, f32[264,256]{1,0:T(8,128)S(1)}, u32[]{:S(2)}, u32[]{:S(2)}) collective-permute-start(f32[264,256]{1,0:T(8,128)S(1)} %get-tuple-element.54), channel_id=1, source_target_pairs={{0,8},{16,24},{8,0},{24,16},{1,9},{17,25},{9,1},{25,17},{2,10},{18... | collective-permute-start | bytes 811016 | tf_op jit(solution)/shard_map/ppermute | solution.py:586
  2.4 5.0 %copy-start.2 = (f32[128]{0:T(128)S(1)}, f32[128]{0:T(128)}, u32[]{:S(2)}) copy-start(f32[128]{0:T(128)} %param.9) | copy-start | bytes 1540
  2.4 14.9 %collective-permute-start.1 = (f32[264,256]{1,0:T(8,128)S(1)}, f32[264,256]{1,0:T(8,128)S(1)}, u32[]{:S(2)}, u32[]{:S(2)}) collective-permute-start(f32[264,256]{1,0:T(8,128)S(1)} %get-tuple-element.55), channel_id=1, source_target_pairs={{8,16},{16,8},{9,17},{17,9},{10,18},{18,10},{11,19},{19,11},{12,20... | collective-permute-start | bytes 811016 | tf_op jit(solution)/shard_map/ppermute | solution.py:586
  9.0 11.9 %collective-permute-start.3 = (f32[2,128,256]{2,1,0:T(8,128)S(1)}, f32[2,128,256]{2,1,0:T(8,128)S(1)}, u32[]{:S(2)}, u32[]{:S(2)}) collective-permute-start(f32[2,128,256]{2,1,0:T(8,128)S(1)} %get-tuple-element.59), channel_id=1, source_target_pairs={{4,2},{5,3},{2,4},{3,5},{12,10},{13,11},{10,12},{11,13},{20,18},{2... | collective-permute-start | bytes 786440 | tf_op jit(solution)/shard_map/ppermute | solution.py:602
  9.6 18.2 %collective-permute-start.4 = (f32[2,128,256]{2,1,0:T(8,128)S(1)}, f32[2,128,256]{2,1,0:T(8,128)S(1)}, u32[]{:S(2)}, u32[]{:S(2)}) collective-permute-start(f32[2,128,256]{2,1,0:T(8,128)S(1)} %get-tuple-element.60), channel_id=1, source_target_pairs={{6,2},{7,3},{0,4},{1,5},{14,10},{15,11},{8,12},{9,13},{22,18},{23,... | collective-permute-start | bytes 786440 | tf_op jit(solution)/shard_map/ppermute | solution.py:602
  15.8 13.9 %collective-permute-start.5 = (f32[2,128,256]{2,1,0:T(8,128)S(1)}, f32[2,128,256]{2,1,0:T(8,128)S(1)}, u32[]{:S(2)}, u32[]{:S(2)}) collective-permute-start(f32[2,128,256]{2,1,0:T(8,128)S(1)} %get-tuple-element.61), channel_id=1, source_target_pairs={{0,2},{1,3},{6,4},{7,5},{8,10},{9,11},{14,12},{15,13},{16,18},{17,... | collective-permute-start | bytes 786440 | tf_op jit(solution)/shard_map/ppermute | solution.py:602
  18.3 8.1 %copy-start.5 = (s32[1,512]{1,0:T(1,128)S(1)}, s32[1,512]{1,0:T(1,128)}, u32[]{:S(2)}) copy-start(s32[1,512]{1,0:T(1,128)} %param.10) | copy-start | bytes 6148
  18.3 20.7 %collective-permute-start.6 = (f32[2,128,256]{2,1,0:T(8,128)S(1)}, f32[2,128,256]{2,1,0:T(8,128)S(1)}, u32[]{:S(2)}, u32[]{:S(2)}) collective-permute-start(f32[2,128,256]{2,1,0:T(8,128)S(1)} %get-tuple-element.62), channel_id=1, source_target_pairs={{2,0},{3,1},{4,6},{5,7},{10,8},{11,9},{12,14},{13,15},{18,16},{19,... | collective-permute-start | bytes 786440 | tf_op jit(solution)/shard_map/ppermute | solution.py:602
  19.6 19.4 %collective-permute-start.7 = (f32[2,128,256]{2,1,0:T(8,128)S(1)}, f32[2,128,256]{2,1,0:T(8,128)S(1)}, u32[]{:S(2)}, u32[]{:S(2)}) collective-permute-start(f32[2,128,256]{2,1,0:T(8,128)S(1)} %get-tuple-element.63), channel_id=1, source_target_pairs={{4,0},{5,1},{2,6},{3,7},{12,8},{13,9},{10,14},{11,15},{20,16},{21,... | collective-permute-start | bytes 786440 | tf_op jit(solution)/shard_map/ppermute | solution.py:602
  20.9 18.1 %collective-permute-start.8 = (f32[2,128,256]{2,1,0:T(8,128)S(1)}, f32[2,128,256]{2,1,0:T(8,128)S(1)}, u32[]{:S(2)}, u32[]{:S(2)}) collective-permute-start(f32[2,128,256]{2,1,0:T(8,128)S(1)} %get-tuple-element.64), channel_id=1, source_target_pairs={{6,0},{7,1},{0,6},{1,7},{14,8},{15,9},{8,14},{9,15},{22,16},{23,17... | collective-permute-start | bytes 786440 | tf_op jit(solution)/shard_map/ppermute | solution.py:602
  27.1 0.7 copy-start.3
  27.1 0.7 copy-start.4
  27.8 7.2 %collective-permute-start.2 = (f32[8,512]{1,0:T(8,128)S(1)}, f32[8,512]{1,0:T(8,128)S(1)}, u32[]{:S(2)}, u32[]{:S(2)}) collective-permute-start(f32[8,512]{1,0:T(8,128)S(1)} %concatenate.3.refs_0_), channel_id=1, source_target_pairs={{8,15},{9,14},{10,13},{11,12},{12,11},{13,10},{14,9},{15,8},{24,31... | collective-permute-start | bytes 49160 | tf_op jit(solution)/shard_map/ppermute | solution.py:629
  39.1 10.7 %collective-permute-start.11 = (f32[520,256]{1,0:T(8,128)S(1)}, f32[520,256]{1,0:T(8,128)S(1)}, u32[]{:S(2)}, u32[]{:S(2)}) collective-permute-start(f32[520,256]{1,0:T(8,128)S(1)} %get-tuple-element.66.refs_3_.refs_1_.refs_0_), channel_id=1, source_target_pairs={{0,1},{1,0},{2,3},{3,2},{4,5},{5,4},{6,7},{7,6},{8,9},{9,8},{10,11... | collective-permute-start | bytes 1597448 | tf_op jit(solution)/shard_map/ppermute | solution.py:656
  39.2 14.1 %collective-permute-start.12 = (f32[520,256]{1,0:T(8,128)S(1)}, f32[520,256]{1,0:T(8,128)S(1)}, u32[]{:S(2)}, u32[]{:S(2)}) collective-permute-start(f32[520,256]{1,0:T(8,128)S(1)} %get-tuple-element.66.refs_3_.refs_1_.refs_0_), channel_id=1, source_target_pairs={{1,2},{2,1},{3,4},{4,3},{5,6},{6,5},{7,15},{8,16},{9,10},{10,9},{1... | collective-permute-start | bytes 1597448 | tf_op jit(solution)/shard_map/ppermute | solution.py:655
  41.3 1.6 %collective-permute-start.9 = (f32[2,128,256]{2,1,0:T(8,128)S(1)}, f32[2,128,256]{2,1,0:T(8,128)S(1)}, u32[]{:S(2)}, u32[]{:S(2)}) collective-permute-start(f32[2,128,256]{2,1,0:T(8,128)S(1)} %get-tuple-element.67.refs_1_), channel_id=1, source_target_pairs={{0,1},{1,0},{2,3},{3,2},{4,5},{5,4},{6,7},{7,6},{8,9},{9,8},{10,11... | collective-permute-start | bytes 786440 | tf_op jit(solution)/shard_map/ppermute | solution.py:654
  41.6 5.9 %collective-permute-start.10 = (f32[2,128,256]{2,1,0:T(8,128)S(1)}, f32[2,128,256]{2,1,0:T(8,128)S(1)}, u32[]{:S(2)}, u32[]{:S(2)}) collective-permute-start(f32[2,128,256]{2,1,0:T(8,128)S(1)} %get-tuple-element.68.refs_2_), channel_id=1, source_target_pairs={{0,1},{1,0},{2,3},{3,2},{4,5},{5,4},{6,7},{7,6},{8,9},{9,8},{10,11... | collective-permute-start | bytes 786440 | tf_op jit(solution)/shard_map/ppermute | solution.py:654
  42.9 12.2 %collective-permute-start.13 = (f32[2,128,256]{2,1,0:T(8,128)S(1)}, f32[2,128,256]{2,1,0:T(8,128)S(1)}, u32[]{:S(2)}, u32[]{:S(2)}) collective-permute-start(f32[2,128,256]{2,1,0:T(8,128)S(1)} %collective-permute-done.9.refs_5_.refs_2_.refs_1_), channel_id=1, source_target_pairs={{1,2},{2,1},{3,4},{4,3},{5,6},{6,5},{7,15},{8,16},{9,10},{10,9},{1... | collective-permute-start | bytes 786440 | tf_op jit(solution)/shard_map/ppermute | solution.py:657
  47.5 9.3 %collective-permute-start.14 = (f32[2,128,256]{2,1,0:T(8,128)S(1)}, f32[2,128,256]{2,1,0:T(8,128)S(1)}, u32[]{:S(2)}, u32[]{:S(2)}) collective-permute-start(f32[2,128,256]{2,1,0:T(8,128)S(1)} %collective-permute-done.10.refs_6_.refs_3_.refs_2_), channel_id=1, source_target_pairs={{1,2},{2,1},{3,4},{4,3},{5,6},{6,5},{7,15},{8,16},{9,10},{10,9},{1... | collective-permute-start | bytes 786440 | tf_op jit(solution)/shard_map/ppermute | solution.py:657
  65.1 7.7 %collective-permute-start.15 = (f32[128,256]{1,0:T(8,128)S(1)}, f32[128,256]{1,0:T(8,128)S(1)}, u32[]{:S(2)}, u32[]{:S(2)}) collective-permute-start(f32[128,256]{1,0:T(8,128)S(1)} %get-tuple-element.86), channel_id=1, source_target_pairs={{0,7},{1,6},{2,5},{3,4},{4,3},{5,2},{6,1},{7,0},{8,15},{9,14},{10,... | collective-permute-start | bytes 393224 | tf_op jit(solution)/shard_map/ppermute | solution.py:698
  67.6 16.4 %collective-permute-start.16 = (f32[128,256]{1,0:T(8,128)S(1)}, f32[128,256]{1,0:T(8,128)S(1)}, u32[]{:S(2)}, u32[]{:S(2)}) collective-permute-start(f32[128,256]{1,0:T(8,128)S(1)} %get-tuple-element.87), channel_id=1, source_target_pairs={{0,6},{1,7},{2,4},{3,5},{4,2},{5,3},{6,0},{7,1},{8,14},{9,15},{10,... | collective-permute-start | bytes 393224 | tf_op jit(solution)/shard_map/ppermute | solution.py:698
  69.4 19.6 %collective-permute-start.17 = (f32[128,256]{1,0:T(8,128)S(1)}, f32[128,256]{1,0:T(8,128)S(1)}, u32[]{:S(2)}, u32[]{:S(2)}) collective-permute-start(f32[128,256]{1,0:T(8,128)S(1)} %get-tuple-element.93), channel_id=1, source_target_pairs={{0,5},{1,4},{2,7},{3,6},{4,1},{5,0},{6,3},{7,2},{8,13},{9,12},{10,... | collective-permute-start | bytes 393224 | tf_op jit(solution)/shard_map/ppermute | solution.py:698
  70.0 22.1 %collective-permute-start.18 = (f32[128,256]{1,0:T(8,128)S(1)}, f32[128,256]{1,0:T(8,128)S(1)}, u32[]{:S(2)}, u32[]{:S(2)}) collective-permute-start(f32[128,256]{1,0:T(8,128)S(1)} %get-tuple-element.94), channel_id=1, source_target_pairs={{0,4},{1,5},{2,6},{3,7},{4,0},{5,1},{6,2},{7,3},{8,12},{9,13},{10,... | collective-permute-start | bytes 393224 | tf_op jit(solution)/shard_map/ppermute | solution.py:698
  72.3 19.8 %collective-permute-start.19 = (f32[128,256]{1,0:T(8,128)S(1)}, f32[128,256]{1,0:T(8,128)S(1)}, u32[]{:S(2)}, u32[]{:S(2)}) collective-permute-start(f32[128,256]{1,0:T(8,128)S(1)} %get-tuple-element.95), channel_id=1, source_target_pairs={{0,3},{1,2},{2,1},{3,0},{4,7},{5,6},{6,5},{7,4},{8,11},{9,10},{10,... | collective-permute-start | bytes 393224 | tf_op jit(solution)/shard_map/ppermute | solution.py:698
  72.8 21.0 %collective-permute-start.20 = (f32[128,256]{1,0:T(8,128)S(1)}, f32[128,256]{1,0:T(8,128)S(1)}, u32[]{:S(2)}, u32[]{:S(2)}) collective-permute-start(f32[128,256]{1,0:T(8,128)S(1)} %get-tuple-element.96), channel_id=1, source_target_pairs={{0,2},{1,3},{2,0},{3,1},{4,6},{5,7},{6,4},{7,5},{8,10},{9,11},{10,... | collective-permute-start | bytes 393224 | tf_op jit(solution)/shard_map/ppermute | solution.py:698
  84.0 9.9 %collective-permute-start.21 = (f32[128,256]{1,0:T(8,128)S(1)}, f32[128,256]{1,0:T(8,128)S(1)}, u32[]{:S(2)}, u32[]{:S(2)}) collective-permute-start(f32[128,256]{1,0:T(8,128)S(1)} %get-tuple-element.97), channel_id=1, source_target_pairs={{0,1},{1,0},{2,3},{3,2},{4,5},{5,4},{6,7},{7,6},{8,9},{9,8},{10,11... | collective-permute-start | bytes 393224 | tf_op jit(solution)/shard_map/ppermute | solution.py:698

commit v22 on v20

--- a/solution.py
+++ b/solution.py
@@ -26,7 +26,7 @@
         at = pl.ds(place * members, members)
         first_ref[at, :] = jnp.where(even, tail, head)
         second_ref[at, :] = jnp.where(even, head, tail)
-    tail, head = flow_ref[:, rows - 1, :], flow_ref[:, 0, :]
+    head, tail = flow_ref[0], flow_ref[1]
     at = pl.ds(STEPS * members, 8)
     first_ref[at, :] = jnp.concatenate([jnp.where(even, tail, head)] * 2, axis=0)
     second_ref[at, :] = jnp.concatenate([jnp.where(even, head, tail)] * 2, axis=0)
@@ -544,7 +544,8 @@
     count = patches * lanes
 
     edge = array(STEPS * step + 8, width)
-    to_last, to_first = call(pack_kernel, "pack", [edge, edge], [init_field, flow_fields], limit=32)
+    flow_edges = jnp.stack([flow_fields[:, 0], flow_fields[:, rows - 1]]) * 1.0
+    to_last, to_first = call(pack_kernel, "pack", [edge, edge], [init_field, flow_edges], limit=32)
 
     def swap(message, start):
         lower = range(start, patches - 1, 2)

time: 94.4 us -> 94.4 us (level); the launches traced: 93.9 us -> 92.8 us
  Pallas kernels: 18.9 us -> 17.1 us
  starting transfers between devices: 46.8 us -> 48.4 us
    pallas_call x9, Pallas kernels: 18.9 us -> 17.1 us  [call(): pl.pallas_call(lambda *refs: kernel(position(), *refs), out_shape=out_sha...]
    ppermute x7, starting transfers between devices: 16 us -> 17.6 us  [swapped(): lax.ppermute(analysed[x], 'member', [(i, i ^ x) for i in range(lanes)])]
where the time goes in v22:
time: 94.4 us; the launch traced here: 92.8 us
  starting transfers between devices  48.4 us (51%)
  waiting for transfers between devices  23.4 us (25%)
  Pallas kernels  17.1 us (18%)
  local copies, waits for them, and re-layouts  2.8 us (3%)
  between operations  1.14 us (1%)
    ppermute x7, starting transfers between devices, swapped(): lax.ppermute(analysed[x], 'member', [(i, i ^ x) for i in range(lanes)])  17.6 us
    pallas_call x9, Pallas kernels, call(): pl.pallas_call(lambda *refs: kernel(position(), *refs), out_shape=out_sha...  17.1 us
    ppermute x6, starting transfers between devices, between(): lax.ppermute(message, 'member', [(2 * a + core, 2 * b + core) for a, b in...  16.4 us
    ppermute x7, waiting for transfers between devices, swapped(): lax.ppermute(analysed[x], 'member', [(i, i ^ x) for i in range(lanes)])  8.64 us
    ppermute x1, waiting for transfers between devices, per_device(): lax.ppermute(mine, axes, [(p * lanes + i, p * lanes + lanes - 1 - i) for...  5.27 us
    ppermute x2, starting transfers between devices, swap(): lax.ppermute(message, 'patch', [(p, p + 1) for p in lower] + [(p + 1, p)...  5.06 us
    ppermute x1, starting transfers between devices, per_device(): got_rest = lax.ppermute(far_own, axes, borders)  4.81 us
    ppermute x6, waiting for transfers between devices, between(): lax.ppermute(message, 'member', [(2 * a + core, 2 * b + core) for a, b in...  3.9 us
  transfers between devices with their start and end apart: 20, of which 7 were waited for; matrix products, arithmetic and copies ran while one was open for 0% of the time, Pallas kernels for 9%

profile of v22, /device:TPU:2, one launch (start us, length us, event | category | flops | bytes accessed | tf_op | source)
XLA Modules:
  0.0 92.8 jit_solution(13927165914075429999)
XLA Ops:
  0.0 0.8 fusion
  0.9 0.0 copy-start
  0.9 1.2 %copy-done = f32[128,8,256]{2,1,0:T(8,128)S(1)} copy-done((f32[128,8,256]{2,1,0:T(8,128)S(1)}, f32[128,8,256]{2,1,0:T(8,128)}, u32[]{:S(2)}) %copy-start) | copy-done | bytes 1048600
  2.1 0.0 copy-start.1
  2.1 0.3 pack.1
  2.4 0.1 collective-permute-start
  2.5 0.0 copy-start.2
  2.5 5.0 %collective-permute-start.1 = (f32[264,256]{1,0:T(8,128)S(1)}, f32[264,256]{1,0:T(8,128)S(1)}, u32[]{:S(2)}, u32[]{:S(2)}) collective-permute-start(f32[264,256]{1,0:T(8,128)S(1)} %get-tuple-element.49), channel_id=1, source_target_pairs={{8,16},{16,8},{9,17},{17,9},{10,18},{18,10},{11,19},{19,11},{12,20... | collective-permute-start | bytes 811016 | tf_op jit(solution)/shard_map/ppermute | solution.py:552
  7.5 0.0 copy-done.1
  7.5 0.0 copy-done.2
  7.5 1.6 %inner.1 = (f32[4,128,256]{2,1,0:T(8,128)S(1)}, f32[128,128]{1,0:T(8,128)S(1)}, f32[2,128,256]{2,1,0:T(8,128)S(1)}, f32[2,128,256]{2,1,0:T(8,128)S(1)}, f32[2,12...) custom-call(f32[128,8,256]{2,1,0:T(8,128)S(1)} %copy-done, f32[4,8,256]{2,1,0:T(8,128)S(1)} %copy-done.1, f32[1,128]{1,0:T(1,128)S(1)} %bitcast.6), custom_call_target="tpu_custom_call" | custom-call | tf_op jit(solution)/shard_map/inner/pallas_call | solution.py:515
  9.1 0.7 collective-permute-start.3
  9.8 6.2 %collective-permute-start.4 = (f32[2,128,256]{2,1,0:T(8,128)S(1)}, f32[2,128,256]{2,1,0:T(8,128)S(1)}, u32[]{:S(2)}, u32[]{:S(2)}) collective-permute-start(f32[2,128,256]{2,1,0:T(8,128)S(1)} %get-tuple-element.54), channel_id=1, source_target_pairs={{6,2},{7,3},{0,4},{1,5},{14,10},{15,11},{8,12},{9,13},{22,18},{23,... | collective-permute-start | bytes 786440 | tf_op jit(solution)/shard_map/ppermute | solution.py:568
  16.0 1.4 %collective-permute-start.5 = (f32[2,128,256]{2,1,0:T(8,128)S(1)}, f32[2,128,256]{2,1,0:T(8,128)S(1)}, u32[]{:S(2)}, u32[]{:S(2)}) collective-permute-start(f32[2,128,256]{2,1,0:T(8,128)S(1)} %get-tuple-element.55), channel_id=1, source_target_pairs={{0,2},{1,3},{6,4},{7,5},{8,10},{9,11},{14,12},{15,13},{16,18},{17,... | collective-permute-start | bytes 786440 | tf_op jit(solution)/shard_map/ppermute | solution.py:568
  17.4 0.0 collective-permute-done.refs_4_
  17.4 0.0 collective-permute-done.1.refs_5_
  17.4 0.9 %edge.1 = (f32[2,128,256]{2,1,0:T(8,128)S(1)}, f32[2,128,256]{2,1,0:T(8,128)S(1)}, f32[2,128,256]{2,1,0:T(8,128)S(1)}, f32[2,128,256]{2,1,0:T(8,128)S(1)}) custom-call(f32[128,8,256]{2,1,0:T(8,128)S(1)} %copy-done, f32[4,8,256]{2,1,0:T(8,128)S(1)} %copy-done.1, f32[128,128]{1,0:T(8,128)S(1)} %get-tuple-element.46.refs_2_, ...), custom_call_target="tpu_custom_call" | custom-call | tf_op jit(solution)/shard_map/edge/pallas_call | solution.py:515
  18.4 1.3 %collective-permute-start.6 = (f32[2,128,256]{2,1,0:T(8,128)S(1)}, f32[2,128,256]{2,1,0:T(8,128)S(1)}, u32[]{:S(2)}, u32[]{:S(2)}) collective-permute-start(f32[2,128,256]{2,1,0:T(8,128)S(1)} %get-tuple-element.56), channel_id=1, source_target_pairs={{2,0},{3,1},{4,6},{5,7},{10,8},{11,9},{12,14},{13,15},{18,16},{19,... | collective-permute-start | bytes 786440 | tf_op jit(solution)/shard_map/ppermute | solution.py:568
  19.7 1.3 %collective-permute-start.7 = (f32[2,128,256]{2,1,0:T(8,128)S(1)}, f32[2,128,256]{2,1,0:T(8,128)S(1)}, u32[]{:S(2)}, u32[]{:S(2)}) collective-permute-start(f32[2,128,256]{2,1,0:T(8,128)S(1)} %get-tuple-element.57), channel_id=1, source_target_pairs={{4,0},{5,1},{2,6},{3,7},{12,8},{13,9},{10,14},{11,15},{20,16},{21,... | collective-permute-start | bytes 786440 | tf_op jit(solution)/shard_map/ppermute | solution.py:568
  21.0 0.0 collective-permute-done.3.refs_3_
  21.0 0.0 copy-start.5
  21.0 5.5 %collective-permute-start.8 = (f32[2,128,256]{2,1,0:T(8,128)S(1)}, f32[2,128,256]{2,1,0:T(8,128)S(1)}, u32[]{:S(2)}, u32[]{:S(2)}) collective-permute-start(f32[2,128,256]{2,1,0:T(8,128)S(1)} %get-tuple-element.58), channel_id=1, source_target_pairs={{6,0},{7,1},{0,6},{1,7},{14,8},{15,9},{8,14},{9,15},{22,16},{23,17... | collective-permute-start | bytes 786440 | tf_op jit(solution)/shard_map/ppermute | solution.py:568
  27.2 0.0 copy-done.5
  27.2 0.0 copy-start.3
  27.2 0.0 copy-start.4
  27.2 0.6 copy-done.3
  27.9 0.0 copy-done.4
  27.9 0.0 collective-permute-done.4.refs_4_
  27.9 1.9 %collective-permute-start.2 = (f32[8,512]{1,0:T(8,128)S(1)}, f32[8,512]{1,0:T(8,128)S(1)}, u32[]{:S(2)}, u32[]{:S(2)}) collective-permute-start(f32[8,512]{1,0:T(8,128)S(1)} %concatenate.3.refs_0_), channel_id=1, source_target_pairs={{8,15},{9,14},{10,13},{11,12},{12,11},{13,10},{14,9},{15,8},{24,31... | collective-permute-start | bytes 49160 | tf_op jit(solution)/shard_map/ppermute | solution.py:595
  29.9 0.0 collective-permute-done.5.refs_5_
  29.9 5.3 %collective-permute-done.2.refs_1_ = f32[8,512]{1,0:T(8,128)S(1)} collective-permute-done((f32[8,512]{1,0:T(8,128)S(1)}, f32[8,512]{1,0:T(8,128)S(1)}, u32[]{:S(2)}, u32[]{:S(2)}) %collective-permute-start.2) | collective-permute-done | bytes 16416 | tf_op jit(solution)/shard_map/ppermute | solution.py:595
  35.1 3.9 %collective-permute-done.6.refs_7_ = f32[2,128,256]{2,1,0:T(8,128)S(1)} collective-permute-done((f32[2,128,256]{2,1,0:T(8,128)S(1)}, f32[2,128,256]{2,1,0:T(8,128)S(1)}, u32[]{:S(2)}, u32[]{:S(2)}) %collective-permute-start.6) | collective-permute-done | bytes 262176 | tf_op jit(solution)/shard_map/ppermute | solution.py:568
  39.0 0.0 collective-permute-done.7.refs_8_
  39.0 0.0 collective-permute-done.8.refs_9_
  39.0 0.1 collect.1
  39.1 0.1 collective-permute-start.9
  39.2 0.5 collective-permute-start.10
  39.7 2.1 %collective-permute-start.11 = (f32[520,256]{1,0:T(8,128)S(1)}, f32[520,256]{1,0:T(8,128)S(1)}, u32[]{:S(2)}, u32[]{:S(2)}) collective-permute-start(f32[520,256]{1,0:T(8,128)S(1)} %get-tuple-element.60.refs_2_.refs_1_.refs_0_), channel_id=1, source_target_pairs={{1,2},{2,1},{3,4},{4,3},{5,6},{6,5},{7,15},{8,16},{9,10},{10,9},{1... | collective-permute-start | bytes 1597448 | tf_op jit(solution)/shard_map/ppermute | solution.py:621
  41.8 0.0 collective-permute-done.9.refs_4_.refs_2_.refs_1_
  41.8 4.8 %collective-permute-start.12 = (f32[4,128,256]{2,1,0:T(8,128)S(1)}, f32[4,128,256]{2,1,0:T(8,128)S(1)}, u32[]{:S(2)}, u32[]{:S(2)}) collective-permute-start(f32[4,128,256]{2,1,0:T(8,128)S(1)} %collective-permute-done.9.refs_4_.refs_2_.refs_1_), channel_id=1, source_target_pairs={{1,2},{2,1},{3,4},{4,3},{5,6},{6,5},{7,15},{8,16},{9,10},{10,9},{1... | collective-permute-start | bytes 1572872 | tf_op jit(solution)/shard_map/ppermute | solution.py:623
  46.7 0.0 collective-permute-done.10.refs_3_
  46.7 3.4 %prepare.1 = (bf16[1024,512]{1,0:T(8,128)(2,1)S(1)}, bf16[1024,512]{1,0:T(8,128)(2,1)S(1)}, bf16[256,1024]{1,0:T(8,128)(2,1)S(1)}, bf16[256,1024]{1,0:T(8,128)(2...) custom-call(f32[8,512]{1,0:T(8,128)S(1)} %get-tuple-element.59.refs_0_, ...), custom_call_target="tpu_custom_call" | custom-call | flops 1073741824 | tf_op jit(solution)/shard_map/prepare/pallas_call | solution.py:515
  50.1 1.7 %collective-permute-done.11.refs_6_ = f32[520,256]{1,0:T(8,128)S(1)} collective-permute-done((f32[520,256]{1,0:T(8,128)S(1)}, f32[520,256]{1,0:T(8,128)S(1)}, u32[]{:S(2)}, u32[]{:S(2)}) %collective-permute-start.11) | collective-permute-done | bytes 532512 | tf_op jit(solution)/shard_map/ppermute | solution.py:621
  51.8 1.8 %middle.1 = (bf16[512,512]{1,0:T(8,128)(2,1)S(1)}, bf16[512,512]{1,0:T(8,128)(2,1)S(1)}, f32[512,512]{1,0:T(8,128)S(1)}, f32[256,512]{1,0:T(8,128)S(1)}, f32[8,256]{1,0:T(8,128)S(1)}) custom-call(f32[8,512]{1,0:T(8,128)S(1)} %get-tuple-element.59.refs_0_, bf16[1024,512]{1,0:T(8,128)(2,1)S(1)} %get-tuple-element.62.refs_1_.refs_3_, ...), custom_call_target="tpu_custom_call" | custom-call | flops 1342177280 | tf_op jit(solution)/shard_map/middle/pallas_call | solution.py:515
  53.6 3.8 %collective-permute-done.12.refs_15_ = f32[4,128,256]{2,1,0:T(8,128)S(1)} collective-permute-done((f32[4,128,256]{2,1,0:T(8,128)S(1)}, f32[4,128,256]{2,1,0:T(8,128)S(1)}, u32[]{:S(2)}, u32[]{:S(2)}) %collective-permute-start.12) | collective-permute-done | bytes 524320 | tf_op jit(solution)/shard_map/ppermute | solution.py:623
  57.4 7.0 %region.1 = (bf16[512,512]{1,0:T(8,128)(2,1)S(1)}, bf16[512,512]{1,0:T(8,128)(2,1)S(1)}, bf16[512,256]{1,0:T(8,128)(2,1)S(1)}, bf16[512,256]{1,0:T(8,128)(2,1)S(...) custom-call(f32[8,512]{1,0:T(8,128)S(1)} %get-tuple-element.59.refs_0_, ...), custom_call_target="tpu_custom_call" | custom-call | tf_op jit(solution)/shard_map/region/pallas_call | solution.py:515
  64.4 4.7 %collective-permute-start.13 = (f32[128,256]{1,0:T(8,128)S(1)}, f32[128,256]{1,0:T(8,128)S(1)}, u32[]{:S(2)}, u32[]{:S(2)}) collective-permute-start(f32[128,256]{1,0:T(8,128)S(1)} %get-tuple-element.74), channel_id=1, source_target_pairs={{0,7},{1,6},{2,5},{3,4},{4,3},{5,2},{6,1},{7,0},{8,15},{9,14},{10,... | collective-permute-start | bytes 393224 | tf_op jit(solution)/shard_map/ppermute | solution.py:657
  69.2 1.4 %collective-permute-start.14 = (f32[128,256]{1,0:T(8,128)S(1)}, f32[128,256]{1,0:T(8,128)S(1)}, u32[]{:S(2)}, u32[]{:S(2)}) collective-permute-start(f32[128,256]{1,0:T(8,128)S(1)} %get-tuple-element.75), channel_id=1, source_target_pairs={{0,6},{1,7},{2,4},{3,5},{4,2},{5,3},{6,0},{7,1},{8,14},{9,15},{10,... | collective-permute-start | bytes 393224 | tf_op jit(solution)/shard_map/ppermute | solution.py:657
  70.5 0.8 others.1
  71.4 0.1 collective-permute-start.15
  71.4 1.8 %collective-permute-start.16 = (f32[128,256]{1,0:T(8,128)S(1)}, f32[128,256]{1,0:T(8,128)S(1)}, u32[]{:S(2)}, u32[]{:S(2)}) collective-permute-start(f32[128,256]{1,0:T(8,128)S(1)} %get-tuple-element.82), channel_id=1, source_target_pairs={{0,4},{1,5},{2,6},{3,7},{4,0},{5,1},{6,2},{7,3},{8,12},{9,13},{10,... | collective-permute-start | bytes 393224 | tf_op jit(solution)/shard_map/ppermute | solution.py:657
  73.3 1.0 %collective-permute-start.17 = (f32[128,256]{1,0:T(8,128)S(1)}, f32[128,256]{1,0:T(8,128)S(1)}, u32[]{:S(2)}, u32[]{:S(2)}) collective-permute-start(f32[128,256]{1,0:T(8,128)S(1)} %get-tuple-element.83), channel_id=1, source_target_pairs={{0,3},{1,2},{2,1},{3,0},{4,7},{5,6},{6,5},{7,4},{8,11},{9,10},{10,... | collective-permute-start | bytes 393224 | tf_op jit(solution)/shard_map/ppermute | solution.py:657
  74.3 0.0 collective-permute-done.13.refs_0_
  74.3 1.5 %collective-permute-start.18 = (f32[128,256]{1,0:T(8,128)S(1)}, f32[128,256]{1,0:T(8,128)S(1)}, u32[]{:S(2)}, u32[]{:S(2)}) collective-permute-start(f32[128,256]{1,0:T(8,128)S(1)} %get-tuple-element.84), channel_id=1, source_target_pairs={{0,2},{1,3},{2,0},{3,1},{4,6},{5,7},{6,4},{7,5},{8,10},{9,11},{10,... | collective-permute-start | bytes 393224 | tf_op jit(solution)/shard_map/ppermute | solution.py:657
  75.8 1.6 %collective-permute-done.14.refs_1_ = f32[128,256]{1,0:T(8,128)S(1)} collective-permute-done((f32[128,256]{1,0:T(8,128)S(1)}, f32[128,256]{1,0:T(8,128)S(1)}, u32[]{:S(2)}, u32[]{:S(2)}) %collective-permute-start.14) | collective-permute-done | bytes 131104 | tf_op jit(solution)/shard_map/ppermute | solution.py:657
  77.4 7.0 %collective-permute-start.19 = (f32[128,256]{1,0:T(8,128)S(1)}, f32[128,256]{1,0:T(8,128)S(1)}, u32[]{:S(2)}, u32[]{:S(2)}) collective-permute-start(f32[128,256]{1,0:T(8,128)S(1)} %get-tuple-element.85), channel_id=1, source_target_pairs={{0,1},{1,0},{2,3},{3,2},{4,5},{5,4},{6,7},{7,6},{8,9},{9,8},{10,11... | collective-permute-start | bytes 393224 | tf_op jit(solution)/shard_map/ppermute | solution.py:657
  84.4 3.1 %collective-permute-done.15.refs_2_ = f32[128,256]{1,0:T(8,128)S(1)} collective-permute-done((f32[128,256]{1,0:T(8,128)S(1)}, f32[128,256]{1,0:T(8,128)S(1)}, u32[]{:S(2)}, u32[]{:S(2)}) %collective-permute-start.15) | collective-permute-done | bytes 131104 | tf_op jit(solution)/shard_map/ppermute | solution.py:657
  87.6 3.9 %collective-permute-done.16.refs_3_ = f32[128,256]{1,0:T(8,128)S(1)} collective-permute-done((f32[128,256]{1,0:T(8,128)S(1)}, f32[128,256]{1,0:T(8,128)S(1)}, u32[]{:S(2)}, u32[]{:S(2)}) %collective-permute-start.16) | collective-permute-done | bytes 131104 | tf_op jit(solution)/shard_map/ppermute | solution.py:657
  91.5 0.0 collective-permute-done.17.refs_4_
  91.5 0.0 collective-permute-done.18.refs_5_
  91.5 0.0 collective-permute-done.19.refs_6_
  91.5 1.1 %unpack.1 = f32[128,8,256]{2,1,0:T(8,128)} custom-call(f32[128,256]{1,0:T(8,128)S(1)} %collective-permute-done.13.refs_0_, f32[128,256]{1,0:T(8,128)S(1)} %collective-permute-done.14.refs_1_, f32[128,256]{1,0:T(8,128)S(1)} %collective-permute-done.15.refs_2_, f32[128,256]{1,0:T(8,128)S(1)} %collective-permute-done.16.refs_3_, ...), custom_call_target="tpu_custom_call" | custom-call | tf_op jit(solution)/shard_map/unpack/pallas_call | solution.py:515
  (5 shorter events, 0.1 us)
Async XLA Ops:
  0.9 1.2 %copy-start = (f32[128,8,256]{2,1,0:T(8,128)S(1)}, f32[128,8,256]{2,1,0:T(8,128)}, u32[]{:S(2)}) copy-start(f32[128,8,256]{2,1,0:T(8,128)} %refs_0_.5) | copy-start | bytes 3145732
  2.1 5.4 %copy-start.1 = (f32[4,8,256]{2,1,0:T(8,128)S(1)}, f32[4,8,256]{2,1,0:T(8,128)}, u32[]{:S(2)}) copy-start(f32[4,8,256]{2,1,0:T(8,128)} %refs_1_.3) | copy-start | bytes 98308
  2.4 15.0 %collective-permute-start = (f32[264,256]{1,0:T(8,128)S(1)}, f32[264,256]{1,0:T(8,128)S(1)}, u32[]{:S(2)}, u32[]{:S(2)}) collective-permute-start(f32[264,256]{1,0:T(8,128)S(1)} %get-tuple-element.48), channel_id=1, source_target_pairs={{0,8},{16,24},{8,0},{24,16},{1,9},{17,25},{9,1},{25,17},{2,10},{18... | collective-permute-start | bytes 811016 | tf_op jit(solution)/shard_map/ppermute | solution.py:552
  2.5 5.0 %copy-start.2 = (f32[128]{0:T(128)S(1)}, f32[128]{0:T(128)}, u32[]{:S(2)}) copy-start(f32[128]{0:T(128)} %param.9) | copy-start | bytes 1540
  2.5 14.9 %collective-permute-start.1 = (f32[264,256]{1,0:T(8,128)S(1)}, f32[264,256]{1,0:T(8,128)S(1)}, u32[]{:S(2)}, u32[]{:S(2)}) collective-permute-start(f32[264,256]{1,0:T(8,128)S(1)} %get-tuple-element.49), channel_id=1, source_target_pairs={{8,16},{16,8},{9,17},{17,9},{10,18},{18,10},{11,19},{19,11},{12,20... | collective-permute-start | bytes 811016 | tf_op jit(solution)/shard_map/ppermute | solution.py:552
  9.1 11.9 %collective-permute-start.3 = (f32[2,128,256]{2,1,0:T(8,128)S(1)}, f32[2,128,256]{2,1,0:T(8,128)S(1)}, u32[]{:S(2)}, u32[]{:S(2)}) collective-permute-start(f32[2,128,256]{2,1,0:T(8,128)S(1)} %get-tuple-element.53), channel_id=1, source_target_pairs={{4,2},{5,3},{2,4},{3,5},{12,10},{13,11},{10,12},{11,13},{20,18},{2... | collective-permute-start | bytes 786440 | tf_op jit(solution)/shard_map/ppermute | solution.py:568
  9.8 18.2 %collective-permute-start.4 = (f32[2,128,256]{2,1,0:T(8,128)S(1)}, f32[2,128,256]{2,1,0:T(8,128)S(1)}, u32[]{:S(2)}, u32[]{:S(2)}) collective-permute-start(f32[2,128,256]{2,1,0:T(8,128)S(1)} %get-tuple-element.54), channel_id=1, source_target_pairs={{6,2},{7,3},{0,4},{1,5},{14,10},{15,11},{8,12},{9,13},{22,18},{23,... | collective-permute-start | bytes 786440 | tf_op jit(solution)/shard_map/ppermute | solution.py:568
  16.0 13.9 %collective-permute-start.5 = (f32[2,128,256]{2,1,0:T(8,128)S(1)}, f32[2,128,256]{2,1,0:T(8,128)S(1)}, u32[]{:S(2)}, u32[]{:S(2)}) collective-permute-start(f32[2,128,256]{2,1,0:T(8,128)S(1)} %get-tuple-element.55), channel_id=1, source_target_pairs={{0,2},{1,3},{6,4},{7,5},{8,10},{9,11},{14,12},{15,13},{16,18},{17,... | collective-permute-start | bytes 786440 | tf_op jit(solution)/shard_map/ppermute | solution.py:568
  18.4 20.7 %collective-permute-start.6 = (f32[2,128,256]{2,1,0:T(8,128)S(1)}, f32[2,128,256]{2,1,0:T(8,128)S(1)}, u32[]{:S(2)}, u32[]{:S(2)}) collective-permute-start(f32[2,128,256]{2,1,0:T(8,128)S(1)} %get-tuple-element.56), channel_id=1, source_target_pairs={{2,0},{3,1},{4,6},{5,7},{10,8},{11,9},{12,14},{13,15},{18,16},{19,... | collective-permute-start | bytes 786440 | tf_op jit(solution)/shard_map/ppermute | solution.py:568
  19.7 19.4 %collective-permute-start.7 = (f32[2,128,256]{2,1,0:T(8,128)S(1)}, f32[2,128,256]{2,1,0:T(8,128)S(1)}, u32[]{:S(2)}, u32[]{:S(2)}) collective-permute-start(f32[2,128,256]{2,1,0:T(8,128)S(1)} %get-tuple-element.57), channel_id=1, source_target_pairs={{4,0},{5,1},{2,6},{3,7},{12,8},{13,9},{10,14},{11,15},{20,16},{21,... | collective-permute-start | bytes 786440 | tf_op jit(solution)/shard_map/ppermute | solution.py:568
  21.0 6.2 %copy-start.5 = (s32[1,512]{1,0:T(1,128)S(1)}, s32[1,512]{1,0:T(1,128)}, u32[]{:S(2)}) copy-start(s32[1,512]{1,0:T(1,128)} %param.10) | copy-start | bytes 6148
  21.0 18.0 %collective-permute-start.8 = (f32[2,128,256]{2,1,0:T(8,128)S(1)}, f32[2,128,256]{2,1,0:T(8,128)S(1)}, u32[]{:S(2)}, u32[]{:S(2)}) collective-permute-start(f32[2,128,256]{2,1,0:T(8,128)S(1)} %get-tuple-element.58), channel_id=1, source_target_pairs={{6,0},{7,1},{0,6},{1,7},{14,8},{15,9},{8,14},{9,15},{22,16},{23,17... | collective-permute-start | bytes 786440 | tf_op jit(solution)/shard_map/ppermute | solution.py:568
  27.2 0.7 copy-start.3
  27.2 0.7 copy-start.4
  27.9 7.2 %collective-permute-start.2 = (f32[8,512]{1,0:T(8,128)S(1)}, f32[8,512]{1,0:T(8,128)S(1)}, u32[]{:S(2)}, u32[]{:S(2)}) collective-permute-start(f32[8,512]{1,0:T(8,128)S(1)} %concatenate.3.refs_0_), channel_id=1, source_target_pairs={{8,15},{9,14},{10,13},{11,12},{12,11},{13,10},{14,9},{15,8},{24,31... | collective-permute-start | bytes 49160 | tf_op jit(solution)/shard_map/ppermute | solution.py:595
  39.1 2.7 %collective-permute-start.9 = (f32[4,128,256]{2,1,0:T(8,128)S(1)}, f32[4,128,256]{2,1,0:T(8,128)S(1)}, u32[]{:S(2)}, u32[]{:S(2)}) collective-permute-start(f32[4,128,256]{2,1,0:T(8,128)S(1)} %get-tuple-element.61.refs_1_), channel_id=1, source_target_pairs={{0,1},{1,0},{2,3},{3,2},{4,5},{5,4},{6,7},{7,6},{8,9},{9,8},{10,11... | collective-permute-start | bytes 1572872 | tf_op jit(solution)/shard_map/ppermute | solution.py:620
  39.2 7.4 %collective-permute-start.10 = (f32[520,256]{1,0:T(8,128)S(1)}, f32[520,256]{1,0:T(8,128)S(1)}, u32[]{:S(2)}, u32[]{:S(2)}) collective-permute-start(f32[520,256]{1,0:T(8,128)S(1)} %get-tuple-element.60.refs_2_.refs_1_.refs_0_), channel_id=1, source_target_pairs={{0,1},{1,0},{2,3},{3,2},{4,5},{5,4},{6,7},{7,6},{8,9},{9,8},{10,11... | collective-permute-start | bytes 1597448 | tf_op jit(solution)/shard_map/ppermute | solution.py:622
  39.7 12.0 %collective-permute-start.11 = (f32[520,256]{1,0:T(8,128)S(1)}, f32[520,256]{1,0:T(8,128)S(1)}, u32[]{:S(2)}, u32[]{:S(2)}) collective-permute-start(f32[520,256]{1,0:T(8,128)S(1)} %get-tuple-element.60.refs_2_.refs_1_.refs_0_), channel_id=1, source_target_pairs={{1,2},{2,1},{3,4},{4,3},{5,6},{6,5},{7,15},{8,16},{9,10},{10,9},{1... | collective-permute-start | bytes 1597448 | tf_op jit(solution)/shard_map/ppermute | solution.py:621
  41.8 15.5 %collective-permute-start.12 = (f32[4,128,256]{2,1,0:T(8,128)S(1)}, f32[4,128,256]{2,1,0:T(8,128)S(1)}, u32[]{:S(2)}, u32[]{:S(2)}) collective-permute-start(f32[4,128,256]{2,1,0:T(8,128)S(1)} %collective-permute-done.9.refs_4_.refs_2_.refs_1_), channel_id=1, source_target_pairs={{1,2},{2,1},{3,4},{4,3},{5,6},{6,5},{7,15},{8,16},{9,10},{10,9},{1... | collective-permute-start | bytes 1572872 | tf_op jit(solution)/shard_map/ppermute | solution.py:623
  64.4 9.9 %collective-permute-start.13 = (f32[128,256]{1,0:T(8,128)S(1)}, f32[128,256]{1,0:T(8,128)S(1)}, u32[]{:S(2)}, u32[]{:S(2)}) collective-permute-start(f32[128,256]{1,0:T(8,128)S(1)} %get-tuple-element.74), channel_id=1, source_target_pairs={{0,7},{1,6},{2,5},{3,4},{4,3},{5,2},{6,1},{7,0},{8,15},{9,14},{10,... | collective-permute-start | bytes 393224 | tf_op jit(solution)/shard_map/ppermute | solution.py:657
  69.2 8.3 %collective-permute-start.14 = (f32[128,256]{1,0:T(8,128)S(1)}, f32[128,256]{1,0:T(8,128)S(1)}, u32[]{:S(2)}, u32[]{:S(2)}) collective-permute-start(f32[128,256]{1,0:T(8,128)S(1)} %get-tuple-element.75), channel_id=1, source_target_pairs={{0,6},{1,7},{2,4},{3,5},{4,2},{5,3},{6,0},{7,1},{8,14},{9,15},{10,... | collective-permute-start | bytes 393224 | tf_op jit(solution)/shard_map/ppermute | solution.py:657
  71.4 16.2 %collective-permute-start.15 = (f32[128,256]{1,0:T(8,128)S(1)}, f32[128,256]{1,0:T(8,128)S(1)}, u32[]{:S(2)}, u32[]{:S(2)}) collective-permute-start(f32[128,256]{1,0:T(8,128)S(1)} %get-tuple-element.81), channel_id=1, source_target_pairs={{0,5},{1,4},{2,7},{3,6},{4,1},{5,0},{6,3},{7,2},{8,13},{9,12},{10,... | collective-permute-start | bytes 393224 | tf_op jit(solution)/shard_map/ppermute | solution.py:657
  71.4 20.0 %collective-permute-start.16 = (f32[128,256]{1,0:T(8,128)S(1)}, f32[128,256]{1,0:T(8,128)S(1)}, u32[]{:S(2)}, u32[]{:S(2)}) collective-permute-start(f32[128,256]{1,0:T(8,128)S(1)} %get-tuple-element.82), channel_id=1, source_target_pairs={{0,4},{1,5},{2,6},{3,7},{4,0},{5,1},{6,2},{7,3},{8,12},{9,13},{10,... | collective-permute-start | bytes 393224 | tf_op jit(solution)/shard_map/ppermute | solution.py:657
  73.3 18.2 %collective-permute-start.17 = (f32[128,256]{1,0:T(8,128)S(1)}, f32[128,256]{1,0:T(8,128)S(1)}, u32[]{:S(2)}, u32[]{:S(2)}) collective-permute-start(f32[128,256]{1,0:T(8,128)S(1)} %get-tuple-element.83), channel_id=1, source_target_pairs={{0,3},{1,2},{2,1},{3,0},{4,7},{5,6},{6,5},{7,4},{8,11},{9,10},{10,... | collective-permute-start | bytes 393224 | tf_op jit(solution)/shard_map/ppermute | solution.py:657
  74.3 17.2 %collective-permute-start.18 = (f32[128,256]{1,0:T(8,128)S(1)}, f32[128,256]{1,0:T(8,128)S(1)}, u32[]{:S(2)}, u32[]{:S(2)}) collective-permute-start(f32[128,256]{1,0:T(8,128)S(1)} %get-tuple-element.84), channel_id=1, source_target_pairs={{0,2},{1,3},{2,0},{3,1},{4,6},{5,7},{6,4},{7,5},{8,10},{9,11},{10,... | collective-permute-start | bytes 393224 | tf_op jit(solution)/shard_map/ppermute | solution.py:657
  77.4 14.0 %collective-permute-start.19 = (f32[128,256]{1,0:T(8,128)S(1)}, f32[128,256]{1,0:T(8,128)S(1)}, u32[]{:S(2)}, u32[]{:S(2)}) collective-permute-start(f32[128,256]{1,0:T(8,128)S(1)} %get-tuple-element.85), channel_id=1, source_target_pairs={{0,1},{1,0},{2,3},{3,2},{4,5},{5,4},{6,7},{7,6},{8,9},{9,8},{10,11... | collective-permute-start | bytes 393224 | tf_op jit(solution)/shard_map/ppermute | solution.py:657

commit v23 on v20

--- a/solution.py
+++ b/solution.py
@@ -10,7 +10,7 @@
 
 STEPS = 2
 COARSE = 0.35
-DONE = 0.02
+DONE = 0.03
 LARGE = 2e4
 PART = 256
 PADDING = 8
@@ -439,8 +439,7 @@
     def size(matrix):
         return jnp.sum(jnp.sum(matrix * matrix, axis=0, keepdims=True))
 
-    def begin(count):
-        parts = pieces(factor[...], count)
+    def begin(parts, count):
         if count > 2:
             squared[upper, :], squared[lower, :] = square(parts)
         bound = 1.0 - start
@@ -469,13 +468,14 @@
         factor[...] = gain * (dot(rest, rest) - jnp.where(eye, 0.5 * bound * bound, 0.0))
         return after(bound)
 
-    top, bottom = square(pieces(factor[...], 2))
+    parts = pieces(factor[...], 2)
+    top, bottom = square(parts)
     squared[upper, :] = top
     squared[lower, :] = bottom
     limit = 1.0001 * jnp.sqrt(jnp.sqrt(size(top) + size(bottom)))
     start = 2.0 / (1.0 + limit)
     large = limit > LARGE
-    bound = lax.cond(large, lambda: begin(3), lambda: begin(2))
+    bound = lax.cond(large, lambda: begin(pieces(factor[...], 3), 3), lambda: begin(parts, 2))
     bound = lax.while_loop(lambda b: jnp.logical_and(b > COARSE, large), lambda b: refine(b, 3), bound)
     bound = lax.while_loop(lambda b: b > COARSE, lambda b: refine(b, 2), bound)
     factor[...] = jnp.where(eye, 1.0, 0.0) - factor[...]

time: 94.4 us -> 94.7 us (level)
  transfers between devices with their start and end apart: 20 -> 20, of which waited for: 7 -> 8; matrix products, arithmetic and copies ran while one was open for 0% -> 0% of each run, Pallas kernels for 9% -> 9%
where the time goes in v23:
time: 94.7 us; the launch traced here: 94.2 us
  starting transfers between devices  46.4 us (49%)
  waiting for transfers between devices  24.4 us (26%)
  Pallas kernels  19.5 us (21%)
  local copies, waits for them, and re-layouts  2.71 us (3%)
  between operations  1.11 us (1%)
    pallas_call x9, Pallas kernels, call(): pl.pallas_call(lambda *refs: kernel(position(), *refs), out_shape=out_sha...  19.5 us
    ppermute x6, starting transfers between devices, between(): lax.ppermute(message, 'member', [(2 * a + core, 2 * b + core) for a, b in...  16.4 us
    ppermute x7, starting transfers between devices, swapped(): lax.ppermute(analysed[x], 'member', [(i, i ^ x) for i in range(lanes)])  15.6 us
    ppermute x7, waiting for transfers between devices, swapped(): lax.ppermute(analysed[x], 'member', [(i, i ^ x) for i in range(lanes)])  9.7 us
    ppermute x1, waiting for transfers between devices, per_device(): lax.ppermute(mine, axes, [(p * lanes + i, p * lanes + lanes - 1 - i) for...  5.27 us
    ppermute x2, starting transfers between devices, swap(): lax.ppermute(message, 'patch', [(p, p + 1) for p in lower] + [(p + 1, p)...  5.06 us
    ppermute x1, starting transfers between devices, per_device(): got_rest = lax.ppermute(far_own, axes, borders)  4.81 us
    ppermute x6, waiting for transfers between devices, between(): lax.ppermute(message, 'member', [(2 * a + core, 2 * b + core) for a, b in...  3.9 us
  transfers between devices with their start and end apart: 20, of which 8 were waited for; matrix products, arithmetic and copies ran while one was open for 0% of the time, Pallas kernels for 9%

profile of v23, /device:TPU:2, one launch (start us, length us, event | category | flops | bytes accessed | tf_op | source)
XLA Modules:
  0.0 94.2 jit_solution(13467215618267787843)
XLA Ops:
  0.0 0.0 copy-start
  0.0 1.2 %copy-done = f32[128,8,256]{2,1,0:T(8,128)S(1)} copy-done((f32[128,8,256]{2,1,0:T(8,128)S(1)}, f32[128,8,256]{2,1,0:T(8,128)}, u32[]{:S(2)}) %copy-start) | copy-done | bytes 1048600
  1.2 0.0 copy-start.1
  1.2 0.8 copy-done.1
  2.0 0.3 pack.1
  2.3 0.1 collective-permute-start
  2.4 0.0 copy-start.2
  2.4 5.0 %collective-permute-start.1 = (f32[264,256]{1,0:T(8,128)S(1)}, f32[264,256]{1,0:T(8,128)S(1)}, u32[]{:S(2)}, u32[]{:S(2)}) collective-permute-start(f32[264,256]{1,0:T(8,128)S(1)} %get-tuple-element.49), channel_id=1, source_target_pairs={{8,16},{16,8},{9,17},{17,9},{10,18},{18,10},{11,19},{19,11},{12,20... | collective-permute-start | bytes 811016 | tf_op jit(solution)/shard_map/ppermute | solution.py:551
  7.4 0.0 copy-done.2
  7.4 1.6 %inner.1 = (f32[4,128,256]{2,1,0:T(8,128)S(1)}, f32[128,128]{1,0:T(8,128)S(1)}, f32[2,128,256]{2,1,0:T(8,128)S(1)}, f32[2,128,256]{2,1,0:T(8,128)S(1)}, f32[2,12...) custom-call(f32[128,8,256]{2,1,0:T(8,128)S(1)} %copy-done, f32[4,8,256]{2,1,0:T(8,128)S(1)} %copy-done.1, f32[1,128]{1,0:T(1,128)S(1)} %bitcast.2), custom_call_target="tpu_custom_call" | custom-call | tf_op jit(solution)/shard_map/inner/pallas_call | solution.py:515
  9.0 0.7 collective-permute-start.3
  9.6 6.2 %collective-permute-start.4 = (f32[2,128,256]{2,1,0:T(8,128)S(1)}, f32[2,128,256]{2,1,0:T(8,128)S(1)}, u32[]{:S(2)}, u32[]{:S(2)}) collective-permute-start(f32[2,128,256]{2,1,0:T(8,128)S(1)} %get-tuple-element.54), channel_id=1, source_target_pairs={{6,2},{7,3},{0,4},{1,5},{14,10},{15,11},{8,12},{9,13},{22,18},{23,... | collective-permute-start | bytes 786440 | tf_op jit(solution)/shard_map/ppermute | solution.py:567
  15.8 1.4 %collective-permute-start.5 = (f32[2,128,256]{2,1,0:T(8,128)S(1)}, f32[2,128,256]{2,1,0:T(8,128)S(1)}, u32[]{:S(2)}, u32[]{:S(2)}) collective-permute-start(f32[2,128,256]{2,1,0:T(8,128)S(1)} %get-tuple-element.55), channel_id=1, source_target_pairs={{0,2},{1,3},{6,4},{7,5},{8,10},{9,11},{14,12},{15,13},{16,18},{17,... | collective-permute-start | bytes 786440 | tf_op jit(solution)/shard_map/ppermute | solution.py:567
  17.3 0.0 collective-permute-done.refs_4_
  17.3 0.0 collective-permute-done.1.refs_5_
  17.3 0.9 edge.1
  18.3 1.3 %collective-permute-start.6 = (f32[2,128,256]{2,1,0:T(8,128)S(1)}, f32[2,128,256]{2,1,0:T(8,128)S(1)}, u32[]{:S(2)}, u32[]{:S(2)}) collective-permute-start(f32[2,128,256]{2,1,0:T(8,128)S(1)} %get-tuple-element.56), channel_id=1, source_target_pairs={{2,0},{3,1},{4,6},{5,7},{10,8},{11,9},{12,14},{13,15},{18,16},{19,... | collective-permute-start | bytes 786440 | tf_op jit(solution)/shard_map/ppermute | solution.py:567
  19.6 1.3 %collective-permute-start.7 = (f32[2,128,256]{2,1,0:T(8,128)S(1)}, f32[2,128,256]{2,1,0:T(8,128)S(1)}, u32[]{:S(2)}, u32[]{:S(2)}) collective-permute-start(f32[2,128,256]{2,1,0:T(8,128)S(1)} %get-tuple-element.57), channel_id=1, source_target_pairs={{4,0},{5,1},{2,6},{3,7},{12,8},{13,9},{10,14},{11,15},{20,16},{21,... | collective-permute-start | bytes 786440 | tf_op jit(solution)/shard_map/ppermute | solution.py:567
  20.9 0.0 collective-permute-done.3.refs_3_
  20.9 0.0 copy-start.5
  20.9 5.5 %collective-permute-start.8 = (f32[2,128,256]{2,1,0:T(8,128)S(1)}, f32[2,128,256]{2,1,0:T(8,128)S(1)}, u32[]{:S(2)}, u32[]{:S(2)}) collective-permute-start(f32[2,128,256]{2,1,0:T(8,128)S(1)} %get-tuple-element.58), channel_id=1, source_target_pairs={{6,0},{7,1},{0,6},{1,7},{14,8},{15,9},{8,14},{9,15},{22,16},{23,17... | collective-permute-start | bytes 786440 | tf_op jit(solution)/shard_map/ppermute | solution.py:567
  27.0 0.0 copy-done.5
  27.1 0.0 copy-start.3
  27.1 0.0 copy-start.4
  27.1 0.6 copy-done.3
  27.8 0.0 copy-done.4
  27.8 0.0 collective-permute-done.4.refs_4_
  27.8 1.9 %collective-permute-start.2 = (f32[8,512]{1,0:T(8,128)S(1)}, f32[8,512]{1,0:T(8,128)S(1)}, u32[]{:S(2)}, u32[]{:S(2)}) collective-permute-start(f32[8,512]{1,0:T(8,128)S(1)} %concatenate.3.refs_0_), channel_id=1, source_target_pairs={{8,15},{9,14},{10,13},{11,12},{12,11},{13,10},{14,9},{15,8},{24,31... | collective-permute-start | bytes 49160 | tf_op jit(solution)/shard_map/ppermute | solution.py:594
  29.7 0.0 collective-permute-done.5.refs_5_
  29.8 5.3 %collective-permute-done.2.refs_1_ = f32[8,512]{1,0:T(8,128)S(1)} collective-permute-done((f32[8,512]{1,0:T(8,128)S(1)}, f32[8,512]{1,0:T(8,128)S(1)}, u32[]{:S(2)}, u32[]{:S(2)}) %collective-permute-start.2) | collective-permute-done | bytes 16416 | tf_op jit(solution)/shard_map/ppermute | solution.py:594
  35.0 3.9 %collective-permute-done.6.refs_7_ = f32[2,128,256]{2,1,0:T(8,128)S(1)} collective-permute-done((f32[2,128,256]{2,1,0:T(8,128)S(1)}, f32[2,128,256]{2,1,0:T(8,128)S(1)}, u32[]{:S(2)}, u32[]{:S(2)}) %collective-permute-start.6) | collective-permute-done | bytes 262176 | tf_op jit(solution)/shard_map/ppermute | solution.py:567
  38.9 0.0 collective-permute-done.7.refs_8_
  38.9 0.0 collective-permute-done.8.refs_9_
  38.9 0.1 collect.1
  39.0 0.1 collective-permute-start.9
  39.1 0.5 collective-permute-start.10
  39.6 2.1 %collective-permute-start.11 = (f32[520,256]{1,0:T(8,128)S(1)}, f32[520,256]{1,0:T(8,128)S(1)}, u32[]{:S(2)}, u32[]{:S(2)}) collective-permute-start(f32[520,256]{1,0:T(8,128)S(1)} %get-tuple-element.60.refs_2_.refs_1_.refs_0_), channel_id=1, source_target_pairs={{1,2},{2,1},{3,4},{4,3},{5,6},{6,5},{7,15},{8,16},{9,10},{10,9},{1... | collective-permute-start | bytes 1597448 | tf_op jit(solution)/shard_map/ppermute | solution.py:620
  41.7 0.0 collective-permute-done.9.refs_4_.refs_2_.refs_1_
  41.7 4.8 %collective-permute-start.12 = (f32[4,128,256]{2,1,0:T(8,128)S(1)}, f32[4,128,256]{2,1,0:T(8,128)S(1)}, u32[]{:S(2)}, u32[]{:S(2)}) collective-permute-start(f32[4,128,256]{2,1,0:T(8,128)S(1)} %collective-permute-done.9.refs_4_.refs_2_.refs_1_), channel_id=1, source_target_pairs={{1,2},{2,1},{3,4},{4,3},{5,6},{6,5},{7,15},{8,16},{9,10},{10,9},{1... | collective-permute-start | bytes 1572872 | tf_op jit(solution)/shard_map/ppermute | solution.py:622
  46.5 0.0 collective-permute-done.10.refs_3_
  46.6 3.4 %prepare.1 = (bf16[1024,512]{1,0:T(8,128)(2,1)S(1)}, bf16[1024,512]{1,0:T(8,128)(2,1)S(1)}, bf16[256,1024]{1,0:T(8,128)(2,1)S(1)}, bf16[256,1024]{1,0:T(8,128)(2...) custom-call(f32[8,512]{1,0:T(8,128)S(1)} %get-tuple-element.59.refs_0_, ...), custom_call_target="tpu_custom_call" | custom-call | flops 1073741824 | tf_op jit(solution)/shard_map/prepare/pallas_call | solution.py:515
  50.0 1.7 %collective-permute-done.11.refs_6_ = f32[520,256]{1,0:T(8,128)S(1)} collective-permute-done((f32[520,256]{1,0:T(8,128)S(1)}, f32[520,256]{1,0:T(8,128)S(1)}, u32[]{:S(2)}, u32[]{:S(2)}) %collective-permute-start.11) | collective-permute-done | bytes 532512 | tf_op jit(solution)/shard_map/ppermute | solution.py:620
  51.7 1.8 %middle.1 = (bf16[512,512]{1,0:T(8,128)(2,1)S(1)}, bf16[512,512]{1,0:T(8,128)(2,1)S(1)}, f32[512,512]{1,0:T(8,128)S(1)}, f32[256,512]{1,0:T(8,128)S(1)}, f32[8,256]{1,0:T(8,128)S(1)}) custom-call(f32[8,512]{1,0:T(8,128)S(1)} %get-tuple-element.59.refs_0_, bf16[1024,512]{1,0:T(8,128)(2,1)S(1)} %get-tuple-element.62.refs_1_.refs_3_, ...), custom_call_target="tpu_custom_call" | custom-call | flops 1342177280 | tf_op jit(solution)/shard_map/middle/pallas_call | solution.py:515
  53.5 3.8 %collective-permute-done.12.refs_15_ = f32[4,128,256]{2,1,0:T(8,128)S(1)} collective-permute-done((f32[4,128,256]{2,1,0:T(8,128)S(1)}, f32[4,128,256]{2,1,0:T(8,128)S(1)}, u32[]{:S(2)}, u32[]{:S(2)}) %collective-permute-start.12) | collective-permute-done | bytes 524320 | tf_op jit(solution)/shard_map/ppermute | solution.py:622
  57.3 9.5 %region.1 = (bf16[512,512]{1,0:T(8,128)(2,1)S(1)}, bf16[512,512]{1,0:T(8,128)(2,1)S(1)}, bf16[512,256]{1,0:T(8,128)(2,1)S(1)}, bf16[512,256]{1,0:T(8,128)(2,1)S(...) custom-call(f32[8,512]{1,0:T(8,128)S(1)} %get-tuple-element.59.refs_0_, ...), custom_call_target="tpu_custom_call" | custom-call | tf_op jit(solution)/shard_map/region/pallas_call | solution.py:515
  66.8 1.0 %collective-permute-start.13 = (f32[128,256]{1,0:T(8,128)S(1)}, f32[128,256]{1,0:T(8,128)S(1)}, u32[]{:S(2)}, u32[]{:S(2)}) collective-permute-start(f32[128,256]{1,0:T(8,128)S(1)} %get-tuple-element.74), channel_id=1, source_target_pairs={{0,7},{1,6},{2,5},{3,4},{4,3},{5,2},{6,1},{7,0},{8,15},{9,14},{10,... | collective-permute-start | bytes 393224 | tf_op jit(solution)/shard_map/ppermute | solution.py:656
  67.8 2.0 %collective-permute-start.14 = (f32[128,256]{1,0:T(8,128)S(1)}, f32[128,256]{1,0:T(8,128)S(1)}, u32[]{:S(2)}, u32[]{:S(2)}) collective-permute-start(f32[128,256]{1,0:T(8,128)S(1)} %get-tuple-element.75), channel_id=1, source_target_pairs={{0,6},{1,7},{2,4},{3,5},{4,2},{5,3},{6,0},{7,1},{8,14},{9,15},{10,... | collective-permute-start | bytes 393224 | tf_op jit(solution)/shard_map/ppermute | solution.py:656
  69.8 0.8 others.1
  70.6 0.1 collective-permute-start.15
  70.7 3.2 %collective-permute-start.16 = (f32[128,256]{1,0:T(8,128)S(1)}, f32[128,256]{1,0:T(8,128)S(1)}, u32[]{:S(2)}, u32[]{:S(2)}) collective-permute-start(f32[128,256]{1,0:T(8,128)S(1)} %get-tuple-element.82), channel_id=1, source_target_pairs={{0,4},{1,5},{2,6},{3,7},{4,0},{5,1},{6,2},{7,3},{8,12},{9,13},{10,... | collective-permute-start | bytes 393224 | tf_op jit(solution)/shard_map/ppermute | solution.py:656
  73.9 0.2 collective-permute-start.17
  74.1 0.4 collective-permute-done.13.refs_0_
  74.5 8.5 %collective-permute-start.18 = (f32[128,256]{1,0:T(8,128)S(1)}, f32[128,256]{1,0:T(8,128)S(1)}, u32[]{:S(2)}, u32[]{:S(2)}) collective-permute-start(f32[128,256]{1,0:T(8,128)S(1)} %get-tuple-element.84), channel_id=1, source_target_pairs={{0,2},{1,3},{2,0},{3,1},{4,6},{5,7},{6,4},{7,5},{8,10},{9,11},{10,... | collective-permute-start | bytes 393224 | tf_op jit(solution)/shard_map/ppermute | solution.py:656
  83.1 0.0 collective-permute-done.14.refs_1_
  83.1 0.5 collective-permute-start.19
  83.6 4.5 %collective-permute-done.15.refs_2_ = f32[128,256]{1,0:T(8,128)S(1)} collective-permute-done((f32[128,256]{1,0:T(8,128)S(1)}, f32[128,256]{1,0:T(8,128)S(1)}, u32[]{:S(2)}, u32[]{:S(2)}) %collective-permute-start.15) | collective-permute-done | bytes 131104 | tf_op jit(solution)/shard_map/ppermute | solution.py:656
  88.1 3.2 %collective-permute-done.16.refs_3_ = f32[128,256]{1,0:T(8,128)S(1)} collective-permute-done((f32[128,256]{1,0:T(8,128)S(1)}, f32[128,256]{1,0:T(8,128)S(1)}, u32[]{:S(2)}, u32[]{:S(2)}) %collective-permute-start.16) | collective-permute-done | bytes 131104 | tf_op jit(solution)/shard_map/ppermute | solution.py:656
  91.3 0.0 collective-permute-done.17.refs_4_
  91.4 1.6 %collective-permute-done.18.refs_5_ = f32[128,256]{1,0:T(8,128)S(1)} collective-permute-done((f32[128,256]{1,0:T(8,128)S(1)}, f32[128,256]{1,0:T(8,128)S(1)}, u32[]{:S(2)}, u32[]{:S(2)}) %collective-permute-start.18) | collective-permute-done | bytes 131104 | tf_op jit(solution)/shard_map/ppermute | solution.py:656
  92.9 0.0 collective-permute-done.19.refs_6_
  92.9 1.1 %unpack.1 = f32[128,8,256]{2,1,0:T(8,128)} custom-call(f32[128,256]{1,0:T(8,128)S(1)} %collective-permute-done.13.refs_0_, f32[128,256]{1,0:T(8,128)S(1)} %collective-permute-done.14.refs_1_, f32[128,256]{1,0:T(8,128)S(1)} %collective-permute-done.15.refs_2_, f32[128,256]{1,0:T(8,128)S(1)} %collective-permute-done.16.refs_3_, ...), custom_call_target="tpu_custom_call" | custom-call | tf_op jit(solution)/shard_map/unpack/pallas_call | solution.py:515
  (3 shorter events, 0.0 us)
Async XLA Ops:
  0.0 1.2 %copy-start = (f32[128,8,256]{2,1,0:T(8,128)S(1)}, f32[128,8,256]{2,1,0:T(8,128)}, u32[]{:S(2)}) copy-start(f32[128,8,256]{2,1,0:T(8,128)} %refs_0_.5) | copy-start | bytes 3145732
  1.2 0.8 copy-start.1
  2.3 15.0 %collective-permute-start = (f32[264,256]{1,0:T(8,128)S(1)}, f32[264,256]{1,0:T(8,128)S(1)}, u32[]{:S(2)}, u32[]{:S(2)}) collective-permute-start(f32[264,256]{1,0:T(8,128)S(1)} %get-tuple-element.48), channel_id=1, source_target_pairs={{0,8},{16,24},{8,0},{24,16},{1,9},{17,25},{9,1},{25,17},{2,10},{18... | collective-permute-start | bytes 811016 | tf_op jit(solution)/shard_map/ppermute | solution.py:551
  2.4 5.0 %copy-start.2 = (f32[128]{0:T(128)S(1)}, f32[128]{0:T(128)}, u32[]{:S(2)}) copy-start(f32[128]{0:T(128)} %param.9) | copy-start | bytes 1540
  2.4 14.9 %collective-permute-start.1 = (f32[264,256]{1,0:T(8,128)S(1)}, f32[264,256]{1,0:T(8,128)S(1)}, u32[]{:S(2)}, u32[]{:S(2)}) collective-permute-start(f32[264,256]{1,0:T(8,128)S(1)} %get-tuple-element.49), channel_id=1, source_target_pairs={{8,16},{16,8},{9,17},{17,9},{10,18},{18,10},{11,19},{19,11},{12,20... | collective-permute-start | bytes 811016 | tf_op jit(solution)/shard_map/ppermute | solution.py:551
  9.0 11.9 %collective-permute-start.3 = (f32[2,128,256]{2,1,0:T(8,128)S(1)}, f32[2,128,256]{2,1,0:T(8,128)S(1)}, u32[]{:S(2)}, u32[]{:S(2)}) collective-permute-start(f32[2,128,256]{2,1,0:T(8,128)S(1)} %get-tuple-element.53), channel_id=1, source_target_pairs={{4,2},{5,3},{2,4},{3,5},{12,10},{13,11},{10,12},{11,13},{20,18},{2... | collective-permute-start | bytes 786440 | tf_op jit(solution)/shard_map/ppermute | solution.py:567
  9.6 18.2 %collective-permute-start.4 = (f32[2,128,256]{2,1,0:T(8,128)S(1)}, f32[2,128,256]{2,1,0:T(8,128)S(1)}, u32[]{:S(2)}, u32[]{:S(2)}) collective-permute-start(f32[2,128,256]{2,1,0:T(8,128)S(1)} %get-tuple-element.54), channel_id=1, source_target_pairs={{6,2},{7,3},{0,4},{1,5},{14,10},{15,11},{8,12},{9,13},{22,18},{23,... | collective-permute-start | bytes 786440 | tf_op jit(solution)/shard_map/ppermute | solution.py:567
  15.8 13.9 %collective-permute-start.5 = (f32[2,128,256]{2,1,0:T(8,128)S(1)}, f32[2,128,256]{2,1,0:T(8,128)S(1)}, u32[]{:S(2)}, u32[]{:S(2)}) collective-permute-start(f32[2,128,256]{2,1,0:T(8,128)S(1)} %get-tuple-element.55), channel_id=1, source_target_pairs={{0,2},{1,3},{6,4},{7,5},{8,10},{9,11},{14,12},{15,13},{16,18},{17,... | collective-permute-start | bytes 786440 | tf_op jit(solution)/shard_map/ppermute | solution.py:567
  18.3 20.7 %collective-permute-start.6 = (f32[2,128,256]{2,1,0:T(8,128)S(1)}, f32[2,128,256]{2,1,0:T(8,128)S(1)}, u32[]{:S(2)}, u32[]{:S(2)}) collective-permute-start(f32[2,128,256]{2,1,0:T(8,128)S(1)} %get-tuple-element.56), channel_id=1, source_target_pairs={{2,0},{3,1},{4,6},{5,7},{10,8},{11,9},{12,14},{13,15},{18,16},{19,... | collective-permute-start | bytes 786440 | tf_op jit(solution)/shard_map/ppermute | solution.py:567
  19.6 19.4 %collective-permute-start.7 = (f32[2,128,256]{2,1,0:T(8,128)S(1)}, f32[2,128,256]{2,1,0:T(8,128)S(1)}, u32[]{:S(2)}, u32[]{:S(2)}) collective-permute-start(f32[2,128,256]{2,1,0:T(8,128)S(1)} %get-tuple-element.57), channel_id=1, source_target_pairs={{4,0},{5,1},{2,6},{3,7},{12,8},{13,9},{10,14},{11,15},{20,16},{21,... | collective-permute-start | bytes 786440 | tf_op jit(solution)/shard_map/ppermute | solution.py:567
  20.9 6.2 %copy-start.5 = (s32[1,512]{1,0:T(1,128)S(1)}, s32[1,512]{1,0:T(1,128)}, u32[]{:S(2)}) copy-start(s32[1,512]{1,0:T(1,128)} %param.10) | copy-start | bytes 6148
  20.9 18.0 %collective-permute-start.8 = (f32[2,128,256]{2,1,0:T(8,128)S(1)}, f32[2,128,256]{2,1,0:T(8,128)S(1)}, u32[]{:S(2)}, u32[]{:S(2)}) collective-permute-start(f32[2,128,256]{2,1,0:T(8,128)S(1)} %get-tuple-element.58), channel_id=1, source_target_pairs={{6,0},{7,1},{0,6},{1,7},{14,8},{15,9},{8,14},{9,15},{22,16},{23,17... | collective-permute-start | bytes 786440 | tf_op jit(solution)/shard_map/ppermute | solution.py:567
  27.1 0.7 copy-start.3
  27.1 0.7 copy-start.4
  27.8 7.2 %collective-permute-start.2 = (f32[8,512]{1,0:T(8,128)S(1)}, f32[8,512]{1,0:T(8,128)S(1)}, u32[]{:S(2)}, u32[]{:S(2)}) collective-permute-start(f32[8,512]{1,0:T(8,128)S(1)} %concatenate.3.refs_0_), channel_id=1, source_target_pairs={{8,15},{9,14},{10,13},{11,12},{12,11},{13,10},{14,9},{15,8},{24,31... | collective-permute-start | bytes 49160 | tf_op jit(solution)/shard_map/ppermute | solution.py:594
  39.0 2.7 %collective-permute-start.9 = (f32[4,128,256]{2,1,0:T(8,128)S(1)}, f32[4,128,256]{2,1,0:T(8,128)S(1)}, u32[]{:S(2)}, u32[]{:S(2)}) collective-permute-start(f32[4,128,256]{2,1,0:T(8,128)S(1)} %get-tuple-element.61.refs_1_), channel_id=1, source_target_pairs={{0,1},{1,0},{2,3},{3,2},{4,5},{5,4},{6,7},{7,6},{8,9},{9,8},{10,11... | collective-permute-start | bytes 1572872 | tf_op jit(solution)/shard_map/ppermute | solution.py:619
  39.1 7.4 %collective-permute-start.10 = (f32[520,256]{1,0:T(8,128)S(1)}, f32[520,256]{1,0:T(8,128)S(1)}, u32[]{:S(2)}, u32[]{:S(2)}) collective-permute-start(f32[520,256]{1,0:T(8,128)S(1)} %get-tuple-element.60.refs_2_.refs_1_.refs_0_), channel_id=1, source_target_pairs={{0,1},{1,0},{2,3},{3,2},{4,5},{5,4},{6,7},{7,6},{8,9},{9,8},{10,11... | collective-permute-start | bytes 1597448 | tf_op jit(solution)/shard_map/ppermute | solution.py:621
  39.6 12.0 %collective-permute-start.11 = (f32[520,256]{1,0:T(8,128)S(1)}, f32[520,256]{1,0:T(8,128)S(1)}, u32[]{:S(2)}, u32[]{:S(2)}) collective-permute-start(f32[520,256]{1,0:T(8,128)S(1)} %get-tuple-element.60.refs_2_.refs_1_.refs_0_), channel_id=1, source_target_pairs={{1,2},{2,1},{3,4},{4,3},{5,6},{6,5},{7,15},{8,16},{9,10},{10,9},{1... | collective-permute-start | bytes 1597448 | tf_op jit(solution)/shard_map/ppermute | solution.py:620
  41.7 15.5 %collective-permute-start.12 = (f32[4,128,256]{2,1,0:T(8,128)S(1)}, f32[4,128,256]{2,1,0:T(8,128)S(1)}, u32[]{:S(2)}, u32[]{:S(2)}) collective-permute-start(f32[4,128,256]{2,1,0:T(8,128)S(1)} %collective-permute-done.9.refs_4_.refs_2_.refs_1_), channel_id=1, source_target_pairs={{1,2},{2,1},{3,4},{4,3},{5,6},{6,5},{7,15},{8,16},{9,10},{10,9},{1... | collective-permute-start | bytes 1572872 | tf_op jit(solution)/shard_map/ppermute | solution.py:622
  66.8 7.8 %collective-permute-start.13 = (f32[128,256]{1,0:T(8,128)S(1)}, f32[128,256]{1,0:T(8,128)S(1)}, u32[]{:S(2)}, u32[]{:S(2)}) collective-permute-start(f32[128,256]{1,0:T(8,128)S(1)} %get-tuple-element.74), channel_id=1, source_target_pairs={{0,7},{1,6},{2,5},{3,4},{4,3},{5,2},{6,1},{7,0},{8,15},{9,14},{10,... | collective-permute-start | bytes 393224 | tf_op jit(solution)/shard_map/ppermute | solution.py:656
  67.8 15.3 %collective-permute-start.14 = (f32[128,256]{1,0:T(8,128)S(1)}, f32[128,256]{1,0:T(8,128)S(1)}, u32[]{:S(2)}, u32[]{:S(2)}) collective-permute-start(f32[128,256]{1,0:T(8,128)S(1)} %get-tuple-element.75), channel_id=1, source_target_pairs={{0,6},{1,7},{2,4},{3,5},{4,2},{5,3},{6,0},{7,1},{8,14},{9,15},{10,... | collective-permute-start | bytes 393224 | tf_op jit(solution)/shard_map/ppermute | solution.py:656
  70.6 17.5 %collective-permute-start.15 = (f32[128,256]{1,0:T(8,128)S(1)}, f32[128,256]{1,0:T(8,128)S(1)}, u32[]{:S(2)}, u32[]{:S(2)}) collective-permute-start(f32[128,256]{1,0:T(8,128)S(1)} %get-tuple-element.81), channel_id=1, source_target_pairs={{0,5},{1,4},{2,7},{3,6},{4,1},{5,0},{6,3},{7,2},{8,13},{9,12},{10,... | collective-permute-start | bytes 393224 | tf_op jit(solution)/shard_map/ppermute | solution.py:656
  70.7 20.6 %collective-permute-start.16 = (f32[128,256]{1,0:T(8,128)S(1)}, f32[128,256]{1,0:T(8,128)S(1)}, u32[]{:S(2)}, u32[]{:S(2)}) collective-permute-start(f32[128,256]{1,0:T(8,128)S(1)} %get-tuple-element.82), channel_id=1, source_target_pairs={{0,4},{1,5},{2,6},{3,7},{4,0},{5,1},{6,2},{7,3},{8,12},{9,13},{10,... | collective-permute-start | bytes 393224 | tf_op jit(solution)/shard_map/ppermute | solution.py:656
  73.9 17.4 %collective-permute-start.17 = (f32[128,256]{1,0:T(8,128)S(1)}, f32[128,256]{1,0:T(8,128)S(1)}, u32[]{:S(2)}, u32[]{:S(2)}) collective-permute-start(f32[128,256]{1,0:T(8,128)S(1)} %get-tuple-element.83), channel_id=1, source_target_pairs={{0,3},{1,2},{2,1},{3,0},{4,7},{5,6},{6,5},{7,4},{8,11},{9,10},{10,... | collective-permute-start | bytes 393224 | tf_op jit(solution)/shard_map/ppermute | solution.py:656
  74.5 18.4 %collective-permute-start.18 = (f32[128,256]{1,0:T(8,128)S(1)}, f32[128,256]{1,0:T(8,128)S(1)}, u32[]{:S(2)}, u32[]{:S(2)}) collective-permute-start(f32[128,256]{1,0:T(8,128)S(1)} %get-tuple-element.84), channel_id=1, source_target_pairs={{0,2},{1,3},{2,0},{3,1},{4,6},{5,7},{6,4},{7,5},{8,10},{9,11},{10,... | collective-permute-start | bytes 393224 | tf_op jit(solution)/shard_map/ppermute | solution.py:656
  83.1 9.8 %collective-permute-start.19 = (f32[128,256]{1,0:T(8,128)S(1)}, f32[128,256]{1,0:T(8,128)S(1)}, u32[]{:S(2)}, u32[]{:S(2)}) collective-permute-start(f32[128,256]{1,0:T(8,128)S(1)} %get-tuple-element.85), channel_id=1, source_target_pairs={{0,1},{1,0},{2,3},{3,2},{4,5},{5,4},{6,7},{7,6},{8,9},{9,8},{10,11... | collective-permute-start | bytes 393224 | tf_op jit(solution)/shard_map/ppermute | solution.py:656

commit v24 on v23

--- a/solution.py
+++ b/solution.py
@@ -588,8 +588,9 @@
     got_outer = [outer[0]] + [
         between(outer[s], [(s, 0), (chips - 1 - s, chips - 1)]) for s in range(1, chips)
     ]
-    order = [(targets[s], s) for s in range(chips)]
-    pieces_in = got_inner + got_outer
+    turns = [0, chips - 1, *range(1, chips - 1)]
+    order = [(targets[s], k) for k, s in enumerate(turns)]
+    pieces_in = [got_inner[s] for s in turns] + got_outer
     mine, _ = lax.optimization_barrier((mine, outer[0]))
     other = lax.ppermute(
         mine, axes,

time: 94.7 us -> 94.8 us (level)
  transfers between devices with their start and end apart: 20 -> 20, of which waited for: 8 -> 9; matrix products, arithmetic and copies ran while one was open for 0% -> 0% of each run, Pallas kernels for 9% -> 9%
where the time goes in v24:
time: 94.8 us; the launch traced here: 94.3 us
  starting transfers between devices  46.9 us (49%)
  waiting for transfers between devices  24.1 us (25%)
  Pallas kernels  19.5 us (21%)
  local copies, waits for them, and re-layouts  2.71 us (3%)
  between operations  1.11 us (1%)
    pallas_call x9, Pallas kernels, call(): pl.pallas_call(lambda *refs: kernel(position(), *refs), out_shape=out_sha...  19.5 us
    ppermute x6, starting transfers between devices, between(): lax.ppermute(message, 'member', [(2 * a + core, 2 * b + core) for a, b in...  16.3 us
    ppermute x7, starting transfers between devices, swapped(): lax.ppermute(analysed[x], 'member', [(i, i ^ x) for i in range(lanes)])  16.2 us
    ppermute x7, waiting for transfers between devices, swapped(): lax.ppermute(analysed[x], 'member', [(i, i ^ x) for i in range(lanes)])  9.24 us
    ppermute x1, waiting for transfers between devices, per_device(): lax.ppermute(mine, axes, [(p * lanes + i, p * lanes + lanes - 1 - i) for...  5.07 us
    ppermute x2, starting transfers between devices, swap(): lax.ppermute(message, 'patch', [(p, p + 1) for p in lower] + [(p + 1, p)...  5.06 us
    ppermute x1, starting transfers between devices, per_device(): got_rest = lax.ppermute(far_own, axes, borders)  4.81 us
    ppermute x6, waiting for transfers between devices, between(): lax.ppermute(message, 'member', [(2 * a + core, 2 * b + core) for a, b in...  4.1 us
  transfers between devices with their start and end apart: 20, of which 9 were waited for; matrix products, arithmetic and copies ran while one was open for 0% of the time, Pallas kernels for 9%

profile of v24, /device:TPU:2, one launch (start us, length us, event | category | flops | bytes accessed | tf_op | source)
XLA Modules:
  0.0 94.3 jit_solution(15505544217528725132)
XLA Ops:
  0.0 0.0 copy-start
  0.0 1.2 %copy-done = f32[128,8,256]{2,1,0:T(8,128)S(1)} copy-done((f32[128,8,256]{2,1,0:T(8,128)S(1)}, f32[128,8,256]{2,1,0:T(8,128)}, u32[]{:S(2)}) %copy-start) | copy-done | bytes 1048600
  1.2 0.0 copy-start.1
  1.2 0.8 copy-done.1
  2.0 0.3 pack.1
  2.3 0.1 collective-permute-start
  2.4 0.0 copy-start.2
  2.4 5.0 %collective-permute-start.1 = (f32[264,256]{1,0:T(8,128)S(1)}, f32[264,256]{1,0:T(8,128)S(1)}, u32[]{:S(2)}, u32[]{:S(2)}) collective-permute-start(f32[264,256]{1,0:T(8,128)S(1)} %get-tuple-element.49), channel_id=1, source_target_pairs={{8,16},{16,8},{9,17},{17,9},{10,18},{18,10},{11,19},{19,11},{12,20... | collective-permute-start | bytes 811016 | tf_op jit(solution)/shard_map/ppermute | solution.py:551
  7.4 0.0 copy-done.2
  7.4 1.6 %inner.1 = (f32[4,128,256]{2,1,0:T(8,128)S(1)}, f32[128,128]{1,0:T(8,128)S(1)}, f32[2,128,256]{2,1,0:T(8,128)S(1)}, f32[2,128,256]{2,1,0:T(8,128)S(1)}, f32[2,12...) custom-call(f32[128,8,256]{2,1,0:T(8,128)S(1)} %copy-done, f32[4,8,256]{2,1,0:T(8,128)S(1)} %copy-done.1, f32[1,128]{1,0:T(1,128)S(1)} %bitcast.2), custom_call_target="tpu_custom_call" | custom-call | tf_op jit(solution)/shard_map/inner/pallas_call | solution.py:515
  9.0 3.5 %collective-permute-start.3 = (f32[2,128,256]{2,1,0:T(8,128)S(1)}, f32[2,128,256]{2,1,0:T(8,128)S(1)}, u32[]{:S(2)}, u32[]{:S(2)}) collective-permute-start(f32[2,128,256]{2,1,0:T(8,128)S(1)} %get-tuple-element.53), channel_id=1, source_target_pairs={{0,2},{1,3},{6,4},{7,5},{8,10},{9,11},{14,12},{15,13},{16,18},{17,... | collective-permute-start | bytes 786440 | tf_op jit(solution)/shard_map/ppermute | solution.py:567
  12.5 0.7 collective-permute-start.4
  13.2 4.0 %collective-permute-start.5 = (f32[2,128,256]{2,1,0:T(8,128)S(1)}, f32[2,128,256]{2,1,0:T(8,128)S(1)}, u32[]{:S(2)}, u32[]{:S(2)}) collective-permute-start(f32[2,128,256]{2,1,0:T(8,128)S(1)} %get-tuple-element.55), channel_id=1, source_target_pairs={{6,2},{7,3},{0,4},{1,5},{14,10},{15,11},{8,12},{9,13},{22,18},{23,... | collective-permute-start | bytes 786440 | tf_op jit(solution)/shard_map/ppermute | solution.py:567
  17.1 0.0 collective-permute-done.refs_4_
  17.2 0.2 collective-permute-done.1.refs_5_
  17.3 0.9 edge.1
  18.3 1.3 %collective-permute-start.6 = (f32[2,128,256]{2,1,0:T(8,128)S(1)}, f32[2,128,256]{2,1,0:T(8,128)S(1)}, u32[]{:S(2)}, u32[]{:S(2)}) collective-permute-start(f32[2,128,256]{2,1,0:T(8,128)S(1)} %get-tuple-element.56), channel_id=1, source_target_pairs={{2,0},{3,1},{4,6},{5,7},{10,8},{11,9},{12,14},{13,15},{18,16},{19,... | collective-permute-start | bytes 786440 | tf_op jit(solution)/shard_map/ppermute | solution.py:567
  19.6 1.3 %collective-permute-start.7 = (f32[2,128,256]{2,1,0:T(8,128)S(1)}, f32[2,128,256]{2,1,0:T(8,128)S(1)}, u32[]{:S(2)}, u32[]{:S(2)}) collective-permute-start(f32[2,128,256]{2,1,0:T(8,128)S(1)} %get-tuple-element.57), channel_id=1, source_target_pairs={{4,0},{5,1},{2,6},{3,7},{12,8},{13,9},{10,14},{11,15},{20,16},{21,... | collective-permute-start | bytes 786440 | tf_op jit(solution)/shard_map/ppermute | solution.py:567
  20.9 0.0 collective-permute-done.3.refs_3_
  20.9 0.0 copy-start.5
  20.9 5.5 %collective-permute-start.8 = (f32[2,128,256]{2,1,0:T(8,128)S(1)}, f32[2,128,256]{2,1,0:T(8,128)S(1)}, u32[]{:S(2)}, u32[]{:S(2)}) collective-permute-start(f32[2,128,256]{2,1,0:T(8,128)S(1)} %get-tuple-element.58), channel_id=1, source_target_pairs={{6,0},{7,1},{0,6},{1,7},{14,8},{15,9},{8,14},{9,15},{22,16},{23,17... | collective-permute-start | bytes 786440 | tf_op jit(solution)/shard_map/ppermute | solution.py:567
  27.0 0.0 copy-done.5
  27.1 0.0 copy-start.3
  27.1 0.0 copy-start.4
  27.1 0.6 copy-done.3
  27.8 0.0 copy-done.4
  27.8 0.0 collective-permute-done.4.refs_4_
  27.8 1.9 %collective-permute-start.2 = (f32[8,512]{1,0:T(8,128)S(1)}, f32[8,512]{1,0:T(8,128)S(1)}, u32[]{:S(2)}, u32[]{:S(2)}) collective-permute-start(f32[8,512]{1,0:T(8,128)S(1)} %concatenate.3.refs_0_), channel_id=1, source_target_pairs={{8,15},{9,14},{10,13},{11,12},{12,11},{13,10},{14,9},{15,8},{24,31... | collective-permute-start | bytes 49160 | tf_op jit(solution)/shard_map/ppermute | solution.py:595
  29.7 0.0 collective-permute-done.5.refs_5_
  29.8 5.1 %collective-permute-done.2.refs_1_ = f32[8,512]{1,0:T(8,128)S(1)} collective-permute-done((f32[8,512]{1,0:T(8,128)S(1)}, f32[8,512]{1,0:T(8,128)S(1)}, u32[]{:S(2)}, u32[]{:S(2)}) %collective-permute-start.2) | collective-permute-done | bytes 16416 | tf_op jit(solution)/shard_map/ppermute | solution.py:595
  34.8 4.1 %collective-permute-done.6.refs_7_ = f32[2,128,256]{2,1,0:T(8,128)S(1)} collective-permute-done((f32[2,128,256]{2,1,0:T(8,128)S(1)}, f32[2,128,256]{2,1,0:T(8,128)S(1)}, u32[]{:S(2)}, u32[]{:S(2)}) %collective-permute-start.6) | collective-permute-done | bytes 262176 | tf_op jit(solution)/shard_map/ppermute | solution.py:567
  38.9 0.0 collective-permute-done.7.refs_8_
  38.9 0.0 collective-permute-done.8.refs_9_
  38.9 0.1 collect.1
  39.0 0.1 collective-permute-start.9
  39.1 0.5 collective-permute-start.10
  39.6 2.1 %collective-permute-start.11 = (f32[520,256]{1,0:T(8,128)S(1)}, f32[520,256]{1,0:T(8,128)S(1)}, u32[]{:S(2)}, u32[]{:S(2)}) collective-permute-start(f32[520,256]{1,0:T(8,128)S(1)} %get-tuple-element.60.refs_2_.refs_1_.refs_0_), channel_id=1, source_target_pairs={{1,2},{2,1},{3,4},{4,3},{5,6},{6,5},{7,15},{8,16},{9,10},{10,9},{1... | collective-permute-start | bytes 1597448 | tf_op jit(solution)/shard_map/ppermute | solution.py:621
  41.7 0.0 collective-permute-done.9.refs_4_.refs_2_.refs_1_
  41.7 4.8 %collective-permute-start.12 = (f32[4,128,256]{2,1,0:T(8,128)S(1)}, f32[4,128,256]{2,1,0:T(8,128)S(1)}, u32[]{:S(2)}, u32[]{:S(2)}) collective-permute-start(f32[4,128,256]{2,1,0:T(8,128)S(1)} %collective-permute-done.9.refs_4_.refs_2_.refs_1_), channel_id=1, source_target_pairs={{1,2},{2,1},{3,4},{4,3},{5,6},{6,5},{7,15},{8,16},{9,10},{10,9},{1... | collective-permute-start | bytes 1572872 | tf_op jit(solution)/shard_map/ppermute | solution.py:623
  46.5 0.0 collective-permute-done.10.refs_3_
  46.6 3.4 %prepare.1 = (bf16[1024,512]{1,0:T(8,128)(2,1)S(1)}, bf16[1024,512]{1,0:T(8,128)(2,1)S(1)}, bf16[256,1024]{1,0:T(8,128)(2,1)S(1)}, bf16[256,1024]{1,0:T(8,128)(2...) custom-call(f32[8,512]{1,0:T(8,128)S(1)} %get-tuple-element.59.refs_0_, ...), custom_call_target="tpu_custom_call" | custom-call | flops 1073741824 | tf_op jit(solution)/shard_map/prepare/pallas_call | solution.py:515
  50.0 1.7 %collective-permute-done.11.refs_6_ = f32[520,256]{1,0:T(8,128)S(1)} collective-permute-done((f32[520,256]{1,0:T(8,128)S(1)}, f32[520,256]{1,0:T(8,128)S(1)}, u32[]{:S(2)}, u32[]{:S(2)}) %collective-permute-start.11) | collective-permute-done | bytes 532512 | tf_op jit(solution)/shard_map/ppermute | solution.py:621
  51.7 1.8 %middle.1 = (bf16[512,512]{1,0:T(8,128)(2,1)S(1)}, bf16[512,512]{1,0:T(8,128)(2,1)S(1)}, f32[512,512]{1,0:T(8,128)S(1)}, f32[256,512]{1,0:T(8,128)S(1)}, f32[8,256]{1,0:T(8,128)S(1)}) custom-call(f32[8,512]{1,0:T(8,128)S(1)} %get-tuple-element.59.refs_0_, bf16[1024,512]{1,0:T(8,128)(2,1)S(1)} %get-tuple-element.62.refs_1_.refs_3_, ...), custom_call_target="tpu_custom_call" | custom-call | flops 1342177280 | tf_op jit(solution)/shard_map/middle/pallas_call | solution.py:515
  53.5 3.8 %collective-permute-done.12.refs_15_ = f32[4,128,256]{2,1,0:T(8,128)S(1)} collective-permute-done((f32[4,128,256]{2,1,0:T(8,128)S(1)}, f32[4,128,256]{2,1,0:T(8,128)S(1)}, u32[]{:S(2)}, u32[]{:S(2)}) %collective-permute-start.12) | collective-permute-done | bytes 524320 | tf_op jit(solution)/shard_map/ppermute | solution.py:623
  57.3 9.5 %region.1 = (bf16[512,512]{1,0:T(8,128)(2,1)S(1)}, bf16[512,512]{1,0:T(8,128)(2,1)S(1)}, bf16[512,256]{1,0:T(8,128)(2,1)S(1)}, bf16[512,256]{1,0:T(8,128)(2,1)S(...) custom-call(f32[8,512]{1,0:T(8,128)S(1)} %get-tuple-element.59.refs_0_, ...), custom_call_target="tpu_custom_call" | custom-call | tf_op jit(solution)/shard_map/region/pallas_call | solution.py:515
  66.8 2.2 %collective-permute-start.13 = (f32[128,256]{1,0:T(8,128)S(1)}, f32[128,256]{1,0:T(8,128)S(1)}, u32[]{:S(2)}, u32[]{:S(2)}) collective-permute-start(f32[128,256]{1,0:T(8,128)S(1)} %get-tuple-element.74), channel_id=1, source_target_pairs={{0,7},{1,6},{2,5},{3,4},{4,3},{5,2},{6,1},{7,0},{8,15},{9,14},{10,... | collective-permute-start | bytes 393224 | tf_op jit(solution)/shard_map/ppermute | solution.py:657
  69.0 0.8 collective-permute-start.14
  69.8 0.8 others.1
  70.6 0.1 collective-permute-start.15
  70.7 3.2 %collective-permute-start.16 = (f32[128,256]{1,0:T(8,128)S(1)}, f32[128,256]{1,0:T(8,128)S(1)}, u32[]{:S(2)}, u32[]{:S(2)}) collective-permute-start(f32[128,256]{1,0:T(8,128)S(1)} %get-tuple-element.82), channel_id=1, source_target_pairs={{0,4},{1,5},{2,6},{3,7},{4,0},{5,1},{6,2},{7,3},{8,12},{9,13},{10,... | collective-permute-start | bytes 393224 | tf_op jit(solution)/shard_map/ppermute | solution.py:657
  73.9 0.1 collective-permute-start.17
  74.0 0.2 collective-permute-done.13.refs_0_
  74.3 9.8 %collective-permute-start.18 = (f32[128,256]{1,0:T(8,128)S(1)}, f32[128,256]{1,0:T(8,128)S(1)}, u32[]{:S(2)}, u32[]{:S(2)}) collective-permute-start(f32[128,256]{1,0:T(8,128)S(1)} %get-tuple-element.84), channel_id=1, source_target_pairs={{0,2},{1,3},{2,0},{3,1},{4,6},{5,7},{6,4},{7,5},{8,10},{9,11},{10,... | collective-permute-start | bytes 393224 | tf_op jit(solution)/shard_map/ppermute | solution.py:657
  84.0 0.0 collective-permute-done.14.refs_1_
  84.0 0.0 collective-permute-start.19
  84.0 5.2 %collective-permute-done.15.refs_2_ = f32[128,256]{1,0:T(8,128)S(1)} collective-permute-done((f32[128,256]{1,0:T(8,128)S(1)}, f32[128,256]{1,0:T(8,128)S(1)}, u32[]{:S(2)}, u32[]{:S(2)}) %collective-permute-start.15) | collective-permute-done | bytes 131104 | tf_op jit(solution)/shard_map/ppermute | solution.py:657
  89.2 2.4 %collective-permute-done.16.refs_3_ = f32[128,256]{1,0:T(8,128)S(1)} collective-permute-done((f32[128,256]{1,0:T(8,128)S(1)}, f32[128,256]{1,0:T(8,128)S(1)}, u32[]{:S(2)}, u32[]{:S(2)}) %collective-permute-start.16) | collective-permute-done | bytes 131104 | tf_op jit(solution)/shard_map/ppermute | solution.py:657
  91.6 0.0 collective-permute-done.17.refs_4_
  91.6 1.4 %collective-permute-done.18.refs_5_ = f32[128,256]{1,0:T(8,128)S(1)} collective-permute-done((f32[128,256]{1,0:T(8,128)S(1)}, f32[128,256]{1,0:T(8,128)S(1)}, u32[]{:S(2)}, u32[]{:S(2)}) %collective-permute-start.18) | collective-permute-done | bytes 131104 | tf_op jit(solution)/shard_map/ppermute | solution.py:657
  93.1 0.0 collective-permute-done.19.refs_6_
  93.1 1.1 %unpack.1 = f32[128,8,256]{2,1,0:T(8,128)} custom-call(f32[128,256]{1,0:T(8,128)S(1)} %collective-permute-done.13.refs_0_, f32[128,256]{1,0:T(8,128)S(1)} %collective-permute-done.14.refs_1_, f32[128,256]{1,0:T(8,128)S(1)} %collective-permute-done.15.refs_2_, f32[128,256]{1,0:T(8,128)S(1)} %collective-permute-done.16.refs_3_, ...), custom_call_target="tpu_custom_call" | custom-call | tf_op jit(solution)/shard_map/unpack/pallas_call | solution.py:515
  (3 shorter events, 0.0 us)
Async XLA Ops:
  0.0 1.2 %copy-start = (f32[128,8,256]{2,1,0:T(8,128)S(1)}, f32[128,8,256]{2,1,0:T(8,128)}, u32[]{:S(2)}) copy-start(f32[128,8,256]{2,1,0:T(8,128)} %refs_0_.5) | copy-start | bytes 3145732
  1.2 0.8 copy-start.1
  2.3 14.9 %collective-permute-start = (f32[264,256]{1,0:T(8,128)S(1)}, f32[264,256]{1,0:T(8,128)S(1)}, u32[]{:S(2)}, u32[]{:S(2)}) collective-permute-start(f32[264,256]{1,0:T(8,128)S(1)} %get-tuple-element.48), channel_id=1, source_target_pairs={{0,8},{16,24},{8,0},{24,16},{1,9},{17,25},{9,1},{25,17},{2,10},{18... | collective-permute-start | bytes 811016 | tf_op jit(solution)/shard_map/ppermute | solution.py:551
  2.4 5.0 %copy-start.2 = (f32[128]{0:T(128)S(1)}, f32[128]{0:T(128)}, u32[]{:S(2)}) copy-start(f32[128]{0:T(128)} %param.9) | copy-start | bytes 1540
  2.4 14.9 %collective-permute-start.1 = (f32[264,256]{1,0:T(8,128)S(1)}, f32[264,256]{1,0:T(8,128)S(1)}, u32[]{:S(2)}, u32[]{:S(2)}) collective-permute-start(f32[264,256]{1,0:T(8,128)S(1)} %get-tuple-element.49), channel_id=1, source_target_pairs={{8,16},{16,8},{9,17},{17,9},{10,18},{18,10},{11,19},{19,11},{12,20... | collective-permute-start | bytes 811016 | tf_op jit(solution)/shard_map/ppermute | solution.py:551
  9.0 11.9 %collective-permute-start.3 = (f32[2,128,256]{2,1,0:T(8,128)S(1)}, f32[2,128,256]{2,1,0:T(8,128)S(1)}, u32[]{:S(2)}, u32[]{:S(2)}) collective-permute-start(f32[2,128,256]{2,1,0:T(8,128)S(1)} %get-tuple-element.53), channel_id=1, source_target_pairs={{0,2},{1,3},{6,4},{7,5},{8,10},{9,11},{14,12},{15,13},{16,18},{17,... | collective-permute-start | bytes 786440 | tf_op jit(solution)/shard_map/ppermute | solution.py:567
  12.5 15.3 %collective-permute-start.4 = (f32[2,128,256]{2,1,0:T(8,128)S(1)}, f32[2,128,256]{2,1,0:T(8,128)S(1)}, u32[]{:S(2)}, u32[]{:S(2)}) collective-permute-start(f32[2,128,256]{2,1,0:T(8,128)S(1)} %get-tuple-element.54), channel_id=1, source_target_pairs={{4,2},{5,3},{2,4},{3,5},{12,10},{13,11},{10,12},{11,13},{20,18},{2... | collective-permute-start | bytes 786440 | tf_op jit(solution)/shard_map/ppermute | solution.py:567
  13.2 16.6 %collective-permute-start.5 = (f32[2,128,256]{2,1,0:T(8,128)S(1)}, f32[2,128,256]{2,1,0:T(8,128)S(1)}, u32[]{:S(2)}, u32[]{:S(2)}) collective-permute-start(f32[2,128,256]{2,1,0:T(8,128)S(1)} %get-tuple-element.55), channel_id=1, source_target_pairs={{6,2},{7,3},{0,4},{1,5},{14,10},{15,11},{8,12},{9,13},{22,18},{23,... | collective-permute-start | bytes 786440 | tf_op jit(solution)/shard_map/ppermute | solution.py:567
  18.3 20.7 %collective-permute-start.6 = (f32[2,128,256]{2,1,0:T(8,128)S(1)}, f32[2,128,256]{2,1,0:T(8,128)S(1)}, u32[]{:S(2)}, u32[]{:S(2)}) collective-permute-start(f32[2,128,256]{2,1,0:T(8,128)S(1)} %get-tuple-element.56), channel_id=1, source_target_pairs={{2,0},{3,1},{4,6},{5,7},{10,8},{11,9},{12,14},{13,15},{18,16},{19,... | collective-permute-start | bytes 786440 | tf_op jit(solution)/shard_map/ppermute | solution.py:567
  19.6 19.4 %collective-permute-start.7 = (f32[2,128,256]{2,1,0:T(8,128)S(1)}, f32[2,128,256]{2,1,0:T(8,128)S(1)}, u32[]{:S(2)}, u32[]{:S(2)}) collective-permute-start(f32[2,128,256]{2,1,0:T(8,128)S(1)} %get-tuple-element.57), channel_id=1, source_target_pairs={{4,0},{5,1},{2,6},{3,7},{12,8},{13,9},{10,14},{11,15},{20,16},{21,... | collective-permute-start | bytes 786440 | tf_op jit(solution)/shard_map/ppermute | solution.py:567
  20.9 6.2 %copy-start.5 = (s32[1,512]{1,0:T(1,128)S(1)}, s32[1,512]{1,0:T(1,128)}, u32[]{:S(2)}) copy-start(s32[1,512]{1,0:T(1,128)} %param.10) | copy-start | bytes 6148
  20.9 18.0 %collective-permute-start.8 = (f32[2,128,256]{2,1,0:T(8,128)S(1)}, f32[2,128,256]{2,1,0:T(8,128)S(1)}, u32[]{:S(2)}, u32[]{:S(2)}) collective-permute-start(f32[2,128,256]{2,1,0:T(8,128)S(1)} %get-tuple-element.58), channel_id=1, source_target_pairs={{6,0},{7,1},{0,6},{1,7},{14,8},{15,9},{8,14},{9,15},{22,16},{23,17... | collective-permute-start | bytes 786440 | tf_op jit(solution)/shard_map/ppermute | solution.py:567
  27.1 0.7 copy-start.3
  27.1 0.7 copy-start.4
  27.8 7.0 %collective-permute-start.2 = (f32[8,512]{1,0:T(8,128)S(1)}, f32[8,512]{1,0:T(8,128)S(1)}, u32[]{:S(2)}, u32[]{:S(2)}) collective-permute-start(f32[8,512]{1,0:T(8,128)S(1)} %concatenate.3.refs_0_), channel_id=1, source_target_pairs={{8,15},{9,14},{10,13},{11,12},{12,11},{13,10},{14,9},{15,8},{24,31... | collective-permute-start | bytes 49160 | tf_op jit(solution)/shard_map/ppermute | solution.py:595
  39.0 2.7 %collective-permute-start.9 = (f32[4,128,256]{2,1,0:T(8,128)S(1)}, f32[4,128,256]{2,1,0:T(8,128)S(1)}, u32[]{:S(2)}, u32[]{:S(2)}) collective-permute-start(f32[4,128,256]{2,1,0:T(8,128)S(1)} %get-tuple-element.61.refs_1_), channel_id=1, source_target_pairs={{0,1},{1,0},{2,3},{3,2},{4,5},{5,4},{6,7},{7,6},{8,9},{9,8},{10,11... | collective-permute-start | bytes 1572872 | tf_op jit(solution)/shard_map/ppermute | solution.py:620
  39.1 7.4 %collective-permute-start.10 = (f32[520,256]{1,0:T(8,128)S(1)}, f32[520,256]{1,0:T(8,128)S(1)}, u32[]{:S(2)}, u32[]{:S(2)}) collective-permute-start(f32[520,256]{1,0:T(8,128)S(1)} %get-tuple-element.60.refs_2_.refs_1_.refs_0_), channel_id=1, source_target_pairs={{0,1},{1,0},{2,3},{3,2},{4,5},{5,4},{6,7},{7,6},{8,9},{9,8},{10,11... | collective-permute-start | bytes 1597448 | tf_op jit(solution)/shard_map/ppermute | solution.py:622
  39.6 12.0 %collective-permute-start.11 = (f32[520,256]{1,0:T(8,128)S(1)}, f32[520,256]{1,0:T(8,128)S(1)}, u32[]{:S(2)}, u32[]{:S(2)}) collective-permute-start(f32[520,256]{1,0:T(8,128)S(1)} %get-tuple-element.60.refs_2_.refs_1_.refs_0_), channel_id=1, source_target_pairs={{1,2},{2,1},{3,4},{4,3},{5,6},{6,5},{7,15},{8,16},{9,10},{10,9},{1... | collective-permute-start | bytes 1597448 | tf_op jit(solution)/shard_map/ppermute | solution.py:621
  41.7 15.5 %collective-permute-start.12 = (f32[4,128,256]{2,1,0:T(8,128)S(1)}, f32[4,128,256]{2,1,0:T(8,128)S(1)}, u32[]{:S(2)}, u32[]{:S(2)}) collective-permute-start(f32[4,128,256]{2,1,0:T(8,128)S(1)} %collective-permute-done.9.refs_4_.refs_2_.refs_1_), channel_id=1, source_target_pairs={{1,2},{2,1},{3,4},{4,3},{5,6},{6,5},{7,15},{8,16},{9,10},{10,9},{1... | collective-permute-start | bytes 1572872 | tf_op jit(solution)/shard_map/ppermute | solution.py:623
  66.8 7.5 %collective-permute-start.13 = (f32[128,256]{1,0:T(8,128)S(1)}, f32[128,256]{1,0:T(8,128)S(1)}, u32[]{:S(2)}, u32[]{:S(2)}) collective-permute-start(f32[128,256]{1,0:T(8,128)S(1)} %get-tuple-element.74), channel_id=1, source_target_pairs={{0,7},{1,6},{2,5},{3,4},{4,3},{5,2},{6,1},{7,0},{8,15},{9,14},{10,... | collective-permute-start | bytes 393224 | tf_op jit(solution)/shard_map/ppermute | solution.py:657
  69.0 15.0 %collective-permute-start.14 = (f32[128,256]{1,0:T(8,128)S(1)}, f32[128,256]{1,0:T(8,128)S(1)}, u32[]{:S(2)}, u32[]{:S(2)}) collective-permute-start(f32[128,256]{1,0:T(8,128)S(1)} %get-tuple-element.75), channel_id=1, source_target_pairs={{0,6},{1,7},{2,4},{3,5},{4,2},{5,3},{6,0},{7,1},{8,14},{9,15},{10,... | collective-permute-start | bytes 393224 | tf_op jit(solution)/shard_map/ppermute | solution.py:657
  70.6 18.5 %collective-permute-start.15 = (f32[128,256]{1,0:T(8,128)S(1)}, f32[128,256]{1,0:T(8,128)S(1)}, u32[]{:S(2)}, u32[]{:S(2)}) collective-permute-start(f32[128,256]{1,0:T(8,128)S(1)} %get-tuple-element.81), channel_id=1, source_target_pairs={{0,5},{1,4},{2,7},{3,6},{4,1},{5,0},{6,3},{7,2},{8,13},{9,12},{10,... | collective-permute-start | bytes 393224 | tf_op jit(solution)/shard_map/ppermute | solution.py:657
  70.7 20.9 %collective-permute-start.16 = (f32[128,256]{1,0:T(8,128)S(1)}, f32[128,256]{1,0:T(8,128)S(1)}, u32[]{:S(2)}, u32[]{:S(2)}) collective-permute-start(f32[128,256]{1,0:T(8,128)S(1)} %get-tuple-element.82), channel_id=1, source_target_pairs={{0,4},{1,5},{2,6},{3,7},{4,0},{5,1},{6,2},{7,3},{8,12},{9,13},{10,... | collective-permute-start | bytes 393224 | tf_op jit(solution)/shard_map/ppermute | solution.py:657
  73.9 17.7 %collective-permute-start.17 = (f32[128,256]{1,0:T(8,128)S(1)}, f32[128,256]{1,0:T(8,128)S(1)}, u32[]{:S(2)}, u32[]{:S(2)}) collective-permute-start(f32[128,256]{1,0:T(8,128)S(1)} %get-tuple-element.83), channel_id=1, source_target_pairs={{0,3},{1,2},{2,1},{3,0},{4,7},{5,6},{6,5},{7,4},{8,11},{9,10},{10,... | collective-permute-start | bytes 393224 | tf_op jit(solution)/shard_map/ppermute | solution.py:657
  74.3 18.8 %collective-permute-start.18 = (f32[128,256]{1,0:T(8,128)S(1)}, f32[128,256]{1,0:T(8,128)S(1)}, u32[]{:S(2)}, u32[]{:S(2)}) collective-permute-start(f32[128,256]{1,0:T(8,128)S(1)} %get-tuple-element.84), channel_id=1, source_target_pairs={{0,2},{1,3},{2,0},{3,1},{4,6},{5,7},{6,4},{7,5},{8,10},{9,11},{10,... | collective-permute-start | bytes 393224 | tf_op jit(solution)/shard_map/ppermute | solution.py:657
  84.0 9.0 %collective-permute-start.19 = (f32[128,256]{1,0:T(8,128)S(1)}, f32[128,256]{1,0:T(8,128)S(1)}, u32[]{:S(2)}, u32[]{:S(2)}) collective-permute-start(f32[128,256]{1,0:T(8,128)S(1)} %get-tuple-element.85), channel_id=1, source_target_pairs={{0,1},{1,0},{2,3},{3,2},{4,5},{5,4},{6,7},{7,6},{8,9},{9,8},{10,11... | collective-permute-start | bytes 393224 | tf_op jit(solution)/shard_map/ppermute | solution.py:657

commit v25 on v24

--- a/solution.py
+++ b/solution.py
@@ -637,7 +637,7 @@
         [observed, *prepared[:4], prepared[6], got_half],
         flops=10 * halves * slots * slots, limit=20,
     )
-    order = sorted(range(lanes), key=lambda x: (x.bit_length() != lanes.bit_length() - 1, -x))
+    order = sorted(range(lanes), key=lambda x: (-x.bit_length(), x))
     row = array(step, width)
     *shared, first, second = call(
         functools.partial(region_kernel, order[:2]), "region",

time: 94.8 us -> 94.1 us (level)
  starting transfers between devices: 46.9 us -> 37.1 us
  waiting for transfers between devices: 24.1 us -> 32.9 us
    ppermute x7, starting transfers between devices: 16.2 us -> 6.38 us  [swapped(): lax.ppermute(analysed[x], 'member', [(i, i ^ x) for i in range(lanes)])]
    ppermute x7, waiting for transfers between devices: 9.24 us -> 18 us  [swapped(): lax.ppermute(analysed[x], 'member', [(i, i ^ x) for i in range(lanes)])]
where the time goes in v25:
time: 94.1 us; the launch traced here: 93.3 us
  starting transfers between devices  37.1 us (39%)
  waiting for transfers between devices  32.9 us (35%)
  Pallas kernels  19.5 us (21%)
  local copies, waits for them, and re-layouts  2.71 us (3%)
  between operations  1.11 us (1%)
    pallas_call x9, Pallas kernels, call(): pl.pallas_call(lambda *refs: kernel(position(), *refs), out_shape=out_sha...  19.5 us
    ppermute x7, waiting for transfers between devices, swapped(): lax.ppermute(analysed[x], 'member', [(i, i ^ x) for i in range(lanes)])  18 us
    ppermute x6, starting transfers between devices, between(): lax.ppermute(message, 'member', [(2 * a + core, 2 * b + core) for a, b in...  16.3 us
    ppermute x7, starting transfers between devices, swapped(): lax.ppermute(analysed[x], 'member', [(i, i ^ x) for i in range(lanes)])  6.38 us
    ppermute x1, waiting for transfers between devices, per_device(): lax.ppermute(mine, axes, [(p * lanes + i, p * lanes + lanes - 1 - i) for...  5.07 us
    ppermute x2, starting transfers between devices, swap(): lax.ppermute(message, 'patch', [(p, p + 1) for p in lower] + [(p + 1, p)...  5.06 us
    ppermute x1, starting transfers between devices, per_device(): got_rest = lax.ppermute(far_own, axes, borders)  4.81 us
    ppermute x6, waiting for transfers between devices, between(): lax.ppermute(message, 'member', [(2 * a + core, 2 * b + core) for a, b in...  4.1 us
  transfers between devices with their start and end apart: 20, of which 9 were waited for; matrix products, arithmetic and copies ran while one was open for 0% of the time, Pallas kernels for 9%

profile of v25, /device:TPU:2, one launch (start us, length us, event | category | flops | bytes accessed | tf_op | source)
XLA Modules:
  0.0 93.3 jit_solution(17810050921462434880)
XLA Ops:
  0.0 0.0 copy-start
  0.0 1.2 %copy-done = f32[128,8,256]{2,1,0:T(8,128)S(1)} copy-done((f32[128,8,256]{2,1,0:T(8,128)S(1)}, f32[128,8,256]{2,1,0:T(8,128)}, u32[]{:S(2)}) %copy-start) | copy-done | bytes 1048600
  1.2 0.0 copy-start.1
  1.2 0.8 copy-done.1
  2.0 0.3 pack.1
  2.3 0.1 collective-permute-start
  2.4 0.0 copy-start.2
  2.4 5.0 %collective-permute-start.1 = (f32[264,256]{1,0:T(8,128)S(1)}, f32[264,256]{1,0:T(8,128)S(1)}, u32[]{:S(2)}, u32[]{:S(2)}) collective-permute-start(f32[264,256]{1,0:T(8,128)S(1)} %get-tuple-element.49), channel_id=1, source_target_pairs={{8,16},{16,8},{9,17},{17,9},{10,18},{18,10},{11,19},{19,11},{12,20... | collective-permute-start | bytes 811016 | tf_op jit(solution)/shard_map/ppermute | solution.py:551
  7.4 0.0 copy-done.2
  7.4 1.6 %inner.1 = (f32[4,128,256]{2,1,0:T(8,128)S(1)}, f32[128,128]{1,0:T(8,128)S(1)}, f32[2,128,256]{2,1,0:T(8,128)S(1)}, f32[2,128,256]{2,1,0:T(8,128)S(1)}, f32[2,12...) custom-call(f32[128,8,256]{2,1,0:T(8,128)S(1)} %copy-done, f32[4,8,256]{2,1,0:T(8,128)S(1)} %copy-done.1, f32[1,128]{1,0:T(1,128)S(1)} %bitcast.2), custom_call_target="tpu_custom_call" | custom-call | tf_op jit(solution)/shard_map/inner/pallas_call | solution.py:515
  9.0 3.5 %collective-permute-start.3 = (f32[2,128,256]{2,1,0:T(8,128)S(1)}, f32[2,128,256]{2,1,0:T(8,128)S(1)}, u32[]{:S(2)}, u32[]{:S(2)}) collective-permute-start(f32[2,128,256]{2,1,0:T(8,128)S(1)} %get-tuple-element.53), channel_id=1, source_target_pairs={{0,2},{1,3},{6,4},{7,5},{8,10},{9,11},{14,12},{15,13},{16,18},{17,... | collective-permute-start | bytes 786440 | tf_op jit(solution)/shard_map/ppermute | solution.py:567
  12.5 0.7 collective-permute-start.4
  13.2 4.0 %collective-permute-start.5 = (f32[2,128,256]{2,1,0:T(8,128)S(1)}, f32[2,128,256]{2,1,0:T(8,128)S(1)}, u32[]{:S(2)}, u32[]{:S(2)}) collective-permute-start(f32[2,128,256]{2,1,0:T(8,128)S(1)} %get-tuple-element.55), channel_id=1, source_target_pairs={{6,2},{7,3},{0,4},{1,5},{14,10},{15,11},{8,12},{9,13},{22,18},{23,... | collective-permute-start | bytes 786440 | tf_op jit(solution)/shard_map/ppermute | solution.py:567
  17.1 0.0 collective-permute-done.refs_4_
  17.2 0.2 collective-permute-done.1.refs_5_
  17.3 0.9 edge.1
  18.3 1.3 %collective-permute-start.6 = (f32[2,128,256]{2,1,0:T(8,128)S(1)}, f32[2,128,256]{2,1,0:T(8,128)S(1)}, u32[]{:S(2)}, u32[]{:S(2)}) collective-permute-start(f32[2,128,256]{2,1,0:T(8,128)S(1)} %get-tuple-element.56), channel_id=1, source_target_pairs={{2,0},{3,1},{4,6},{5,7},{10,8},{11,9},{12,14},{13,15},{18,16},{19,... | collective-permute-start | bytes 786440 | tf_op jit(solution)/shard_map/ppermute | solution.py:567
  19.6 1.3 %collective-permute-start.7 = (f32[2,128,256]{2,1,0:T(8,128)S(1)}, f32[2,128,256]{2,1,0:T(8,128)S(1)}, u32[]{:S(2)}, u32[]{:S(2)}) collective-permute-start(f32[2,128,256]{2,1,0:T(8,128)S(1)} %get-tuple-element.57), channel_id=1, source_target_pairs={{4,0},{5,1},{2,6},{3,7},{12,8},{13,9},{10,14},{11,15},{20,16},{21,... | collective-permute-start | bytes 786440 | tf_op jit(solution)/shard_map/ppermute | solution.py:567
  20.9 0.0 collective-permute-done.3.refs_3_
  20.9 0.0 copy-start.5
  20.9 5.5 %collective-permute-start.8 = (f32[2,128,256]{2,1,0:T(8,128)S(1)}, f32[2,128,256]{2,1,0:T(8,128)S(1)}, u32[]{:S(2)}, u32[]{:S(2)}) collective-permute-start(f32[2,128,256]{2,1,0:T(8,128)S(1)} %get-tuple-element.58), channel_id=1, source_target_pairs={{6,0},{7,1},{0,6},{1,7},{14,8},{15,9},{8,14},{9,15},{22,16},{23,17... | collective-permute-start | bytes 786440 | tf_op jit(solution)/shard_map/ppermute | solution.py:567
  27.0 0.0 copy-done.5
  27.1 0.0 copy-start.3
  27.1 0.0 copy-start.4
  27.1 0.6 copy-done.3
  27.8 0.0 copy-done.4
  27.8 0.0 collective-permute-done.4.refs_4_
  27.8 1.9 %collective-permute-start.2 = (f32[8,512]{1,0:T(8,128)S(1)}, f32[8,512]{1,0:T(8,128)S(1)}, u32[]{:S(2)}, u32[]{:S(2)}) collective-permute-start(f32[8,512]{1,0:T(8,128)S(1)} %concatenate.3.refs_0_), channel_id=1, source_target_pairs={{8,15},{9,14},{10,13},{11,12},{12,11},{13,10},{14,9},{15,8},{24,31... | collective-permute-start | bytes 49160 | tf_op jit(solution)/shard_map/ppermute | solution.py:595
  29.7 0.0 collective-permute-done.5.refs_5_
  29.8 5.1 %collective-permute-done.2.refs_1_ = f32[8,512]{1,0:T(8,128)S(1)} collective-permute-done((f32[8,512]{1,0:T(8,128)S(1)}, f32[8,512]{1,0:T(8,128)S(1)}, u32[]{:S(2)}, u32[]{:S(2)}) %collective-permute-start.2) | collective-permute-done | bytes 16416 | tf_op jit(solution)/shard_map/ppermute | solution.py:595
  34.8 4.1 %collective-permute-done.6.refs_7_ = f32[2,128,256]{2,1,0:T(8,128)S(1)} collective-permute-done((f32[2,128,256]{2,1,0:T(8,128)S(1)}, f32[2,128,256]{2,1,0:T(8,128)S(1)}, u32[]{:S(2)}, u32[]{:S(2)}) %collective-permute-start.6) | collective-permute-done | bytes 262176 | tf_op jit(solution)/shard_map/ppermute | solution.py:567
  38.9 0.0 collective-permute-done.7.refs_8_
  38.9 0.0 collective-permute-done.8.refs_9_
  38.9 0.1 collect.1
  39.0 0.1 collective-permute-start.9
  39.1 0.5 collective-permute-start.10
  39.6 2.1 %collective-permute-start.11 = (f32[520,256]{1,0:T(8,128)S(1)}, f32[520,256]{1,0:T(8,128)S(1)}, u32[]{:S(2)}, u32[]{:S(2)}) collective-permute-start(f32[520,256]{1,0:T(8,128)S(1)} %get-tuple-element.60.refs_2_.refs_1_.refs_0_), channel_id=1, source_target_pairs={{1,2},{2,1},{3,4},{4,3},{5,6},{6,5},{7,15},{8,16},{9,10},{10,9},{1... | collective-permute-start | bytes 1597448 | tf_op jit(solution)/shard_map/ppermute | solution.py:621
  41.7 0.0 collective-permute-done.9.refs_4_.refs_2_.refs_1_
  41.7 4.8 %collective-permute-start.12 = (f32[4,128,256]{2,1,0:T(8,128)S(1)}, f32[4,128,256]{2,1,0:T(8,128)S(1)}, u32[]{:S(2)}, u32[]{:S(2)}) collective-permute-start(f32[4,128,256]{2,1,0:T(8,128)S(1)} %collective-permute-done.9.refs_4_.refs_2_.refs_1_), channel_id=1, source_target_pairs={{1,2},{2,1},{3,4},{4,3},{5,6},{6,5},{7,15},{8,16},{9,10},{10,9},{1... | collective-permute-start | bytes 1572872 | tf_op jit(solution)/shard_map/ppermute | solution.py:623
  46.5 0.0 collective-permute-done.10.refs_3_
  46.6 3.4 %prepare.1 = (bf16[1024,512]{1,0:T(8,128)(2,1)S(1)}, bf16[1024,512]{1,0:T(8,128)(2,1)S(1)}, bf16[256,1024]{1,0:T(8,128)(2,1)S(1)}, bf16[256,1024]{1,0:T(8,128)(2...) custom-call(f32[8,512]{1,0:T(8,128)S(1)} %get-tuple-element.59.refs_0_, ...), custom_call_target="tpu_custom_call" | custom-call | flops 1073741824 | tf_op jit(solution)/shard_map/prepare/pallas_call | solution.py:515
  50.0 1.7 %collective-permute-done.11.refs_6_ = f32[520,256]{1,0:T(8,128)S(1)} collective-permute-done((f32[520,256]{1,0:T(8,128)S(1)}, f32[520,256]{1,0:T(8,128)S(1)}, u32[]{:S(2)}, u32[]{:S(2)}) %collective-permute-start.11) | collective-permute-done | bytes 532512 | tf_op jit(solution)/shard_map/ppermute | solution.py:621
  51.7 1.8 %middle.1 = (bf16[512,512]{1,0:T(8,128)(2,1)S(1)}, bf16[512,512]{1,0:T(8,128)(2,1)S(1)}, f32[512,512]{1,0:T(8,128)S(1)}, f32[256,512]{1,0:T(8,128)S(1)}, f32[8,256]{1,0:T(8,128)S(1)}) custom-call(f32[8,512]{1,0:T(8,128)S(1)} %get-tuple-element.59.refs_0_, bf16[1024,512]{1,0:T(8,128)(2,1)S(1)} %get-tuple-element.62.refs_1_.refs_3_, ...), custom_call_target="tpu_custom_call" | custom-call | flops 1342177280 | tf_op jit(solution)/shard_map/middle/pallas_call | solution.py:515
  53.5 3.8 %collective-permute-done.12.refs_15_ = f32[4,128,256]{2,1,0:T(8,128)S(1)} collective-permute-done((f32[4,128,256]{2,1,0:T(8,128)S(1)}, f32[4,128,256]{2,1,0:T(8,128)S(1)}, u32[]{:S(2)}, u32[]{:S(2)}) %collective-permute-start.12) | collective-permute-done | bytes 524320 | tf_op jit(solution)/shard_map/ppermute | solution.py:623
  57.3 9.5 %region.1 = (bf16[512,512]{1,0:T(8,128)(2,1)S(1)}, bf16[512,512]{1,0:T(8,128)(2,1)S(1)}, bf16[512,256]{1,0:T(8,128)(2,1)S(1)}, bf16[512,256]{1,0:T(8,128)(2,1)S(...) custom-call(f32[8,512]{1,0:T(8,128)S(1)} %get-tuple-element.59.refs_0_, ...), custom_call_target="tpu_custom_call" | custom-call | tf_op jit(solution)/shard_map/region/pallas_call | solution.py:515
  66.8 0.1 collective-permute-start.13
  66.9 1.8 %collective-permute-start.14 = (f32[128,256]{1,0:T(8,128)S(1)}, f32[128,256]{1,0:T(8,128)S(1)}, u32[]{:S(2)}, u32[]{:S(2)}) collective-permute-start(f32[128,256]{1,0:T(8,128)S(1)} %get-tuple-element.75), channel_id=1, source_target_pairs={{0,5},{1,4},{2,7},{3,6},{4,1},{5,0},{6,3},{7,2},{8,13},{9,12},{10,... | collective-permute-start | bytes 393224 | tf_op jit(solution)/shard_map/ppermute | solution.py:657
  68.6 0.8 others.1
  69.5 2.5 %collective-permute-start.15 = (f32[128,256]{1,0:T(8,128)S(1)}, f32[128,256]{1,0:T(8,128)S(1)}, u32[]{:S(2)}, u32[]{:S(2)}) collective-permute-start(f32[128,256]{1,0:T(8,128)S(1)} %get-tuple-element.81), channel_id=1, source_target_pairs={{0,6},{1,7},{2,4},{3,5},{4,2},{5,3},{6,0},{7,1},{8,14},{9,15},{10,... | collective-permute-start | bytes 393224 | tf_op jit(solution)/shard_map/ppermute | solution.py:657
  71.9 2.0 %collective-permute-start.16 = (f32[128,256]{1,0:T(8,128)S(1)}, f32[128,256]{1,0:T(8,128)S(1)}, u32[]{:S(2)}, u32[]{:S(2)}) collective-permute-start(f32[128,256]{1,0:T(8,128)S(1)} %get-tuple-element.82), channel_id=1, source_target_pairs={{0,7},{1,6},{2,5},{3,4},{4,3},{5,2},{6,1},{7,0},{8,15},{9,14},{10,... | collective-permute-start | bytes 393224 | tf_op jit(solution)/shard_map/ppermute | solution.py:657
  73.9 0.0 collective-permute-start.17
  73.9 9.9 %collective-permute-done.13.refs_0_ = f32[128,256]{1,0:T(8,128)S(1)} collective-permute-done((f32[128,256]{1,0:T(8,128)S(1)}, f32[128,256]{1,0:T(8,128)S(1)}, u32[]{:S(2)}, u32[]{:S(2)}) %collective-permute-start.13) | collective-permute-done | bytes 131104 | tf_op jit(solution)/shard_map/ppermute | solution.py:657
  83.9 0.0 collective-permute-start.18
  83.9 2.6 %collective-permute-done.14.refs_1_ = f32[128,256]{1,0:T(8,128)S(1)} collective-permute-done((f32[128,256]{1,0:T(8,128)S(1)}, f32[128,256]{1,0:T(8,128)S(1)}, u32[]{:S(2)}, u32[]{:S(2)}) %collective-permute-start.14) | collective-permute-done | bytes 131104 | tf_op jit(solution)/shard_map/ppermute | solution.py:657
  86.5 0.1 collective-permute-start.19
  86.5 0.0 collective-permute-done.15.refs_2_
  86.5 0.0 collective-permute-done.16.refs_3_
  86.5 2.8 %collective-permute-done.17.refs_4_ = f32[128,256]{1,0:T(8,128)S(1)} collective-permute-done((f32[128,256]{1,0:T(8,128)S(1)}, f32[128,256]{1,0:T(8,128)S(1)}, u32[]{:S(2)}, u32[]{:S(2)}) %collective-permute-start.17) | collective-permute-done | bytes 131104 | tf_op jit(solution)/shard_map/ppermute | solution.py:657
  89.4 2.6 %collective-permute-done.18.refs_5_ = f32[128,256]{1,0:T(8,128)S(1)} collective-permute-done((f32[128,256]{1,0:T(8,128)S(1)}, f32[128,256]{1,0:T(8,128)S(1)}, u32[]{:S(2)}, u32[]{:S(2)}) %collective-permute-start.18) | collective-permute-done | bytes 131104 | tf_op jit(solution)/shard_map/ppermute | solution.py:657
  92.0 0.0 collective-permute-done.19.refs_6_
  92.0 1.1 %unpack.1 = f32[128,8,256]{2,1,0:T(8,128)} custom-call(f32[128,256]{1,0:T(8,128)S(1)} %collective-permute-done.13.refs_0_, f32[128,256]{1,0:T(8,128)S(1)} %collective-permute-done.14.refs_1_, f32[128,256]{1,0:T(8,128)S(1)} %collective-permute-done.15.refs_2_, f32[128,256]{1,0:T(8,128)S(1)} %collective-permute-done.16.refs_3_, ...), custom_call_target="tpu_custom_call" | custom-call | tf_op jit(solution)/shard_map/unpack/pallas_call | solution.py:515
  (3 shorter events, 0.0 us)
Async XLA Ops:
  0.0 1.2 %copy-start = (f32[128,8,256]{2,1,0:T(8,128)S(1)}, f32[128,8,256]{2,1,0:T(8,128)}, u32[]{:S(2)}) copy-start(f32[128,8,256]{2,1,0:T(8,128)} %refs_0_.5) | copy-start | bytes 3145732
  1.2 0.8 copy-start.1
  2.3 14.9 %collective-permute-start = (f32[264,256]{1,0:T(8,128)S(1)}, f32[264,256]{1,0:T(8,128)S(1)}, u32[]{:S(2)}, u32[]{:S(2)}) collective-permute-start(f32[264,256]{1,0:T(8,128)S(1)} %get-tuple-element.48), channel_id=1, source_target_pairs={{0,8},{16,24},{8,0},{24,16},{1,9},{17,25},{9,1},{25,17},{2,10},{18... | collective-permute-start | bytes 811016 | tf_op jit(solution)/shard_map/ppermute | solution.py:551
  2.4 5.0 %copy-start.2 = (f32[128]{0:T(128)S(1)}, f32[128]{0:T(128)}, u32[]{:S(2)}) copy-start(f32[128]{0:T(128)} %param.9) | copy-start | bytes 1540
  2.4 14.9 %collective-permute-start.1 = (f32[264,256]{1,0:T(8,128)S(1)}, f32[264,256]{1,0:T(8,128)S(1)}, u32[]{:S(2)}, u32[]{:S(2)}) collective-permute-start(f32[264,256]{1,0:T(8,128)S(1)} %get-tuple-element.49), channel_id=1, source_target_pairs={{8,16},{16,8},{9,17},{17,9},{10,18},{18,10},{11,19},{19,11},{12,20... | collective-permute-start | bytes 811016 | tf_op jit(solution)/shard_map/ppermute | solution.py:551
  9.0 11.9 %collective-permute-start.3 = (f32[2,128,256]{2,1,0:T(8,128)S(1)}, f32[2,128,256]{2,1,0:T(8,128)S(1)}, u32[]{:S(2)}, u32[]{:S(2)}) collective-permute-start(f32[2,128,256]{2,1,0:T(8,128)S(1)} %get-tuple-element.53), channel_id=1, source_target_pairs={{0,2},{1,3},{6,4},{7,5},{8,10},{9,11},{14,12},{15,13},{16,18},{17,... | collective-permute-start | bytes 786440 | tf_op jit(solution)/shard_map/ppermute | solution.py:567
  12.5 15.3 %collective-permute-start.4 = (f32[2,128,256]{2,1,0:T(8,128)S(1)}, f32[2,128,256]{2,1,0:T(8,128)S(1)}, u32[]{:S(2)}, u32[]{:S(2)}) collective-permute-start(f32[2,128,256]{2,1,0:T(8,128)S(1)} %get-tuple-element.54), channel_id=1, source_target_pairs={{4,2},{5,3},{2,4},{3,5},{12,10},{13,11},{10,12},{11,13},{20,18},{2... | collective-permute-start | bytes 786440 | tf_op jit(solution)/shard_map/ppermute | solution.py:567
  13.2 16.6 %collective-permute-start.5 = (f32[2,128,256]{2,1,0:T(8,128)S(1)}, f32[2,128,256]{2,1,0:T(8,128)S(1)}, u32[]{:S(2)}, u32[]{:S(2)}) collective-permute-start(f32[2,128,256]{2,1,0:T(8,128)S(1)} %get-tuple-element.55), channel_id=1, source_target_pairs={{6,2},{7,3},{0,4},{1,5},{14,10},{15,11},{8,12},{9,13},{22,18},{23,... | collective-permute-start | bytes 786440 | tf_op jit(solution)/shard_map/ppermute | solution.py:567
  18.3 20.7 %collective-permute-start.6 = (f32[2,128,256]{2,1,0:T(8,128)S(1)}, f32[2,128,256]{2,1,0:T(8,128)S(1)}, u32[]{:S(2)}, u32[]{:S(2)}) collective-permute-start(f32[2,128,256]{2,1,0:T(8,128)S(1)} %get-tuple-element.56), channel_id=1, source_target_pairs={{2,0},{3,1},{4,6},{5,7},{10,8},{11,9},{12,14},{13,15},{18,16},{19,... | collective-permute-start | bytes 786440 | tf_op jit(solution)/shard_map/ppermute | solution.py:567
  19.6 19.4 %collective-permute-start.7 = (f32[2,128,256]{2,1,0:T(8,128)S(1)}, f32[2,128,256]{2,1,0:T(8,128)S(1)}, u32[]{:S(2)}, u32[]{:S(2)}) collective-permute-start(f32[2,128,256]{2,1,0:T(8,128)S(1)} %get-tuple-element.57), channel_id=1, source_target_pairs={{4,0},{5,1},{2,6},{3,7},{12,8},{13,9},{10,14},{11,15},{20,16},{21,... | collective-permute-start | bytes 786440 | tf_op jit(solution)/shard_map/ppermute | solution.py:567
  20.9 6.2 %copy-start.5 = (s32[1,512]{1,0:T(1,128)S(1)}, s32[1,512]{1,0:T(1,128)}, u32[]{:S(2)}) copy-start(s32[1,512]{1,0:T(1,128)} %param.10) | copy-start | bytes 6148
  20.9 18.0 %collective-permute-start.8 = (f32[2,128,256]{2,1,0:T(8,128)S(1)}, f32[2,128,256]{2,1,0:T(8,128)S(1)}, u32[]{:S(2)}, u32[]{:S(2)}) collective-permute-start(f32[2,128,256]{2,1,0:T(8,128)S(1)} %get-tuple-element.58), channel_id=1, source_target_pairs={{6,0},{7,1},{0,6},{1,7},{14,8},{15,9},{8,14},{9,15},{22,16},{23,17... | collective-permute-start | bytes 786440 | tf_op jit(solution)/shard_map/ppermute | solution.py:567
  27.1 0.7 copy-start.3
  27.1 0.7 copy-start.4
  27.8 7.0 %collective-permute-start.2 = (f32[8,512]{1,0:T(8,128)S(1)}, f32[8,512]{1,0:T(8,128)S(1)}, u32[]{:S(2)}, u32[]{:S(2)}) collective-permute-start(f32[8,512]{1,0:T(8,128)S(1)} %concatenate.3.refs_0_), channel_id=1, source_target_pairs={{8,15},{9,14},{10,13},{11,12},{12,11},{13,10},{14,9},{15,8},{24,31... | collective-permute-start | bytes 49160 | tf_op jit(solution)/shard_map/ppermute | solution.py:595
  39.0 2.7 %collective-permute-start.9 = (f32[4,128,256]{2,1,0:T(8,128)S(1)}, f32[4,128,256]{2,1,0:T(8,128)S(1)}, u32[]{:S(2)}, u32[]{:S(2)}) collective-permute-start(f32[4,128,256]{2,1,0:T(8,128)S(1)} %get-tuple-element.61.refs_1_), channel_id=1, source_target_pairs={{0,1},{1,0},{2,3},{3,2},{4,5},{5,4},{6,7},{7,6},{8,9},{9,8},{10,11... | collective-permute-start | bytes 1572872 | tf_op jit(solution)/shard_map/ppermute | solution.py:620
  39.1 7.4 %collective-permute-start.10 = (f32[520,256]{1,0:T(8,128)S(1)}, f32[520,256]{1,0:T(8,128)S(1)}, u32[]{:S(2)}, u32[]{:S(2)}) collective-permute-start(f32[520,256]{1,0:T(8,128)S(1)} %get-tuple-element.60.refs_2_.refs_1_.refs_0_), channel_id=1, source_target_pairs={{0,1},{1,0},{2,3},{3,2},{4,5},{5,4},{6,7},{7,6},{8,9},{9,8},{10,11... | collective-permute-start | bytes 1597448 | tf_op jit(solution)/shard_map/ppermute | solution.py:622
  39.6 12.0 %collective-permute-start.11 = (f32[520,256]{1,0:T(8,128)S(1)}, f32[520,256]{1,0:T(8,128)S(1)}, u32[]{:S(2)}, u32[]{:S(2)}) collective-permute-start(f32[520,256]{1,0:T(8,128)S(1)} %get-tuple-element.60.refs_2_.refs_1_.refs_0_), channel_id=1, source_target_pairs={{1,2},{2,1},{3,4},{4,3},{5,6},{6,5},{7,15},{8,16},{9,10},{10,9},{1... | collective-permute-start | bytes 1597448 | tf_op jit(solution)/shard_map/ppermute | solution.py:621
  41.7 15.5 %collective-permute-start.12 = (f32[4,128,256]{2,1,0:T(8,128)S(1)}, f32[4,128,256]{2,1,0:T(8,128)S(1)}, u32[]{:S(2)}, u32[]{:S(2)}) collective-permute-start(f32[4,128,256]{2,1,0:T(8,128)S(1)} %collective-permute-done.9.refs_4_.refs_2_.refs_1_), channel_id=1, source_target_pairs={{1,2},{2,1},{3,4},{4,3},{5,6},{6,5},{7,15},{8,16},{9,10},{10,9},{1... | collective-permute-start | bytes 1572872 | tf_op jit(solution)/shard_map/ppermute | solution.py:623
  66.8 17.1 %collective-permute-start.13 = (f32[128,256]{1,0:T(8,128)S(1)}, f32[128,256]{1,0:T(8,128)S(1)}, u32[]{:S(2)}, u32[]{:S(2)}) collective-permute-start(f32[128,256]{1,0:T(8,128)S(1)} %get-tuple-element.74), channel_id=1, source_target_pairs={{0,4},{1,5},{2,6},{3,7},{4,0},{5,1},{6,2},{7,3},{8,12},{9,13},{10,... | collective-permute-start | bytes 393224 | tf_op jit(solution)/shard_map/ppermute | solution.py:657
  66.9 19.6 %collective-permute-start.14 = (f32[128,256]{1,0:T(8,128)S(1)}, f32[128,256]{1,0:T(8,128)S(1)}, u32[]{:S(2)}, u32[]{:S(2)}) collective-permute-start(f32[128,256]{1,0:T(8,128)S(1)} %get-tuple-element.75), channel_id=1, source_target_pairs={{0,5},{1,4},{2,7},{3,6},{4,1},{5,0},{6,3},{7,2},{8,13},{9,12},{10,... | collective-permute-start | bytes 393224 | tf_op jit(solution)/shard_map/ppermute | solution.py:657
  69.5 17.1 %collective-permute-start.15 = (f32[128,256]{1,0:T(8,128)S(1)}, f32[128,256]{1,0:T(8,128)S(1)}, u32[]{:S(2)}, u32[]{:S(2)}) collective-permute-start(f32[128,256]{1,0:T(8,128)S(1)} %get-tuple-element.81), channel_id=1, source_target_pairs={{0,6},{1,7},{2,4},{3,5},{4,2},{5,3},{6,0},{7,1},{8,14},{9,15},{10,... | collective-permute-start | bytes 393224 | tf_op jit(solution)/shard_map/ppermute | solution.py:657
  71.9 14.6 %collective-permute-start.16 = (f32[128,256]{1,0:T(8,128)S(1)}, f32[128,256]{1,0:T(8,128)S(1)}, u32[]{:S(2)}, u32[]{:S(2)}) collective-permute-start(f32[128,256]{1,0:T(8,128)S(1)} %get-tuple-element.82), channel_id=1, source_target_pairs={{0,7},{1,6},{2,5},{3,4},{4,3},{5,2},{6,1},{7,0},{8,15},{9,14},{10,... | collective-permute-start | bytes 393224 | tf_op jit(solution)/shard_map/ppermute | solution.py:657
  73.9 15.4 %collective-permute-start.17 = (f32[128,256]{1,0:T(8,128)S(1)}, f32[128,256]{1,0:T(8,128)S(1)}, u32[]{:S(2)}, u32[]{:S(2)}) collective-permute-start(f32[128,256]{1,0:T(8,128)S(1)} %get-tuple-element.83), channel_id=1, source_target_pairs={{0,2},{1,3},{2,0},{3,1},{4,6},{5,7},{6,4},{7,5},{8,10},{9,11},{10,... | collective-permute-start | bytes 393224 | tf_op jit(solution)/shard_map/ppermute | solution.py:657
  83.9 8.1 %collective-permute-start.18 = (f32[128,256]{1,0:T(8,128)S(1)}, f32[128,256]{1,0:T(8,128)S(1)}, u32[]{:S(2)}, u32[]{:S(2)}) collective-permute-start(f32[128,256]{1,0:T(8,128)S(1)} %get-tuple-element.84), channel_id=1, source_target_pairs={{0,3},{1,2},{2,1},{3,0},{4,7},{5,6},{6,5},{7,4},{8,11},{9,10},{10,... | collective-permute-start | bytes 393224 | tf_op jit(solution)/shard_map/ppermute | solution.py:657
  86.5 5.5 %collective-permute-start.19 = (f32[128,256]{1,0:T(8,128)S(1)}, f32[128,256]{1,0:T(8,128)S(1)}, u32[]{:S(2)}, u32[]{:S(2)}) collective-permute-start(f32[128,256]{1,0:T(8,128)S(1)} %get-tuple-element.85), channel_id=1, source_target_pairs={{0,1},{1,0},{2,3},{3,2},{4,5},{5,4},{6,7},{7,6},{8,9},{9,8},{10,11... | collective-permute-start | bytes 393224 | tf_op jit(solution)/shard_map/ppermute | solution.py:657
